TPU v7x, 32 devices: a whole 2x2x4 slice. The times are simulated.
32 devices in a mesh: feat: 2 (over core), dom: 16 (over z, y, x).
Axes of the slice: x: 2, y: 2, z: 4, core: 2. Of those that a mesh axis runs over, the one named last changes fastest.
Arguments:
- features: bfloat16 [16384, 1024], P('dom', 'feat'), may hold values from -6 to 6
- tile_weight: bfloat16 [2048, 128, 128], P('dom'), may hold values from 0 to 0.029907227
- tile_dst: int32 [2048], P('dom'), may hold values from 0 to 15
- tile_src: int32 [2048], P('dom'), may hold values from 0 to 7
- tile_rows: int32 [2048], P('dom'), may hold values from 1 to 128
- w_self1: bfloat16 [1024, 256], P('feat'), may hold values from -0.1875 to 0.1875
- neighbour_weight_first: bfloat16 [1024, 256], P('feat'), may hold values from -0.1875 to 0.1875
- send_list: int32 [16, 16, 8], replicated, may hold values from 0 to 127
- send_count: int32 [16, 16], replicated, may hold values from 1 to 8
- adj_two: bfloat16 [1024, 256], P('dom'), may hold values from 0 to 0.0049743652
- w_self2: bfloat16 [256, 172], replicated, may hold values from -0.375 to 0.375
- w_neigh2: bfloat16 [256, 172], replicated, may hold values from -0.375 to 0.375
Outputs:
- logits: float32 [1024, 172], P('dom')
Inputs may be any that keep to these rules, and one draw needn't show every extreme that they name: `send_list`: every send list slot names a local hidden row of the sender.
All inputs are finite; a program needn't handle non-finite values.
Results may differ from a plain program's by a relative error of at most 0.0012.
The roundings to bfloat16 on the way count: a program that leaves them out, or rounds other values in their place, can miss the bound.
Values may be sent and summed in bfloat16 or wider, within the bound.
No kernel may reach another device: no remote copies, remote signals or barrier semaphores. Data moves between devices by JAX's collectives and lax.ppermute only.
A program may use at most 128 MiB of HBM per device.

v0:
```python
import jax
import jax.numpy as jnp
from jax import lax
from jax.sharding import PartitionSpec as P


def pull_rows(hidden, send_list, send_count):
    parts = lax.axis_size("dom")
    me = lax.axis_index("dom")
    width = hidden.shape[1]
    slot_count = send_list.shape[2]
    slots = jnp.arange(slot_count, dtype=jnp.int32)
    everything = lax.all_gather(hidden, "dom", axis=0, tiled=True)
    lists = lax.dynamic_slice_in_dim(send_list, me, 1, 1)[:, 0, :]
    counts = lax.dynamic_slice_in_dim(send_count, me, 1, 1)[:, 0]
    owners = jnp.arange(parts, dtype=jnp.int32)[:, None] * hidden.shape[0]
    rows = jnp.take(everything, (owners + lists).reshape(parts * slot_count), axis=0)
    rows = rows.reshape(parts, slot_count, width)
    valid = (slots[None, :] < counts[:, None])[:, :, None]
    rows = jnp.where(valid, rows, jnp.zeros_like(rows))
    return rows.reshape(parts * slot_count, width)


def body(
    features,
    tile_weight,
    tile_dst,
    tile_src,
    tile_rows,
    w_self1,
    neighbour_weight_first,
    send_list,
    send_count,
    adj_two,
    w_self2,
    w_neigh2,
):
    tile_size = tile_weight.shape[1]
    n_rows = features.shape[0]
    slice_width = features.shape[1]
    hidden_width = w_self1.shape[1]
    blocks = features.reshape(n_rows // tile_size, tile_size, slice_width)
    row_indices = jnp.arange(tile_size, dtype=jnp.int32)
    valid = row_indices[None, :, None] < tile_rows[:, None, None]
    masked_features = jnp.where(valid, tile_weight, jnp.zeros_like(tile_weight))
    source_nodes = jnp.take(blocks, tile_src, axis=0)
    collected_rows = jnp.einsum(
        "zvx,zxm->zvm", masked_features, source_nodes, preferred_element_type=jnp.float32
    ).astype(jnp.bfloat16)
    neighbour_rows = jnp.einsum(
        "kys,sj->kyj", collected_rows, neighbour_weight_first, preferred_element_type=jnp.float32
    )
    block_count = lax.axis_size("dom") * tile_size // tile_size
    targets = jnp.arange(block_count, dtype=jnp.int32)
    onehot = (tile_dst[:, None] == targets[None, :]).astype(jnp.float32)
    summed = jnp.einsum("tb,trh->brh", onehot, neighbour_rows, precision=lax.Precision.HIGHEST)
    scattered = lax.psum_scatter(
        summed.reshape(lax.axis_size("dom") * tile_size, hidden_width),
        "dom",
        scatter_dimension=0,
        tiled=True,
    )
    own_rows = features[:tile_size]
    total = scattered + jnp.dot(own_rows, w_self1, preferred_element_type=jnp.float32)
    out_rows = adj_two.shape[0]
    pre = lax.psum(total, "feat")
    hidden = jnp.maximum(pre, 0.0).astype(jnp.bfloat16)
    received = pull_rows(hidden, send_list, send_count)
    pool = jnp.concatenate([hidden, received], axis=0)
    neighbour_mean = jnp.dot(adj_two, pool, preferred_element_type=jnp.float32).astype(jnp.bfloat16)
    logits = jnp.dot(hidden[:out_rows], w_self2, preferred_element_type=jnp.float32) + jnp.dot(
        neighbour_mean, w_neigh2, preferred_element_type=jnp.float32
    )
    return logits


def solution(mesh):
    in_specs = (
        P("dom", "feat"),
        P("dom", None, None),
        P("dom"),
        P("dom"),
        P("dom"),
        P("feat", None),
        P("feat", None),
        P(),
        P(),
        P("dom", None),
        P(),
        P(),
    )
    out_specs = P("dom", None)
    return jax.shard_map(body, mesh=mesh, in_specs=in_specs, out_specs=out_specs, check_vma=False)
```

profile of v0, /device:TPU:0, one launch (start us, length us, event | category | flops | bytes accessed | tf_op | source)
XLA Modules:
  0.0 228.2 jit_solution(17137655096707782786)
XLA Ops:
  6.5 0.0 copy-start
  6.5 0.0 reduce-scatter.2.cloned.1.call-start
  6.5 0.7 compare_select_fusion.2
  7.2 0.7 compare_and_fusion.1
  7.9 0.7 iota_compare_fusion
  8.7 9.4 %gather_fusion = bf16[128,128,512]{2,1,0:T(8,128)(2,1)} fusion(bf16[8,128,512]{2,1,0:T(8,128)(2,1)} %bitcast.15, s32[1024]{0:T(1024)S(1)} %pad_clamp_fusion.1), kind=kCustom, calls=%fused_computation | custom fusion | bytes 33554944 | tf_op jit(solution)/shard_map/jit(_take)/gather | solution.py:46
  18.1 15.7 %fusion.5 = bf16[128,128,512]{2,1,0:T(8,128)(2,1)} fusion(bf16[128,128,512]{2,1,0:T(8,128)(2,1)} %gather_fusion, pred[128]{0:T(512)(128)(4,1)S(1)} %compare_and_fusion.1, bf16[128,128,128]{2,1,0:T(8,128)(2,1)} %param.13, pred[128,128]{1,0:T(8,128)(4,1)S(1)} %iota_compare_fusion), kind=kOutput, calls=%fused_computation.7 | convolution fusion | flops 2166358016 | bytes 37765248 | tf_op jit(solution)/shard_map/zvx,zxm->zvm/dot_general | solution.py:47
  33.8 0.0 copy-done
  33.8 0.0 copy-start.7
  33.8 30.1 %fusion = f32[128,128,256]{2,0,1:T(8,128)} fusion(bf16[128,128,512]{2,1,0:T(8,128)(2,1)} %fusion.5, bf16[512,256]{1,0:T(8,128)(2,1)S(1)} %copy-done), kind=kOutput, calls=%fused_computation.2 | convolution fusion | flops 4294967296 | bytes 33816576 | tf_op jit(solution)/shard_map/kys,sj->kyj/dot_general | solution.py:50
  64.0 0.0 copy-done.7
  64.0 0.0 copy-start.1
  64.0 0.0 copy-start.4
  64.0 0.0 copy-start.6
  64.0 0.0 copy-start.2
  64.0 0.0 copy-start.3
  64.0 0.0 copy-start.5
  64.0 9.1 %fusion.25 = f32[16,128,256]{2,0,1:T(8,128)S(1)} fusion(f32[128,128,256]{2,0,1:T(8,128)} %fusion, s32[128]{0:T(128)S(1)} %copy-done.7), kind=kOutput, calls=%fused_computation.31 | convolution fusion | flops 805308416 | bytes 18874880 | tf_op jit(solution)/shard_map/tb,trh->brh/dot_general | solution.py:56
  73.2 2.6 %copy.13 = f32[16,128,256]{2,1,0:T(8,128)} copy(f32[16,128,256]{2,0,1:T(8,128)S(1)} %fusion.25) | data formatting | bytes 4194304 | tf_op jit(solution)/shard_map/tb,trh->brh/dot_general | solution.py:56
  75.7 0.0 reduce-scatter.2.cloned.1.call-update
  75.7 0.0 all-gather.2.cloned.1.call-start
  75.8 83.4 %reduce-scatter.2.cloned.1.call-done = f32[128,256]{1,0:T(8,128)} async-done(((f32[2048,256]{1,0:T(8,128)}), f32[128,256]{1,0:T(8,128)}) %reduce-scatter.2.cloned.1.call-update) | async-done | bytes 131088 | tf_op jit(solution)/shard_map/reduce_scatter | solution.py:57
  159.2 0.0 copy-done.1
  159.2 1.2 convolution_add_fusion
  160.4 3.8 %all-reduce.1 = bf16[128,256]{1,0:T(8,128)(2,1)S(1)} all-reduce(f32[128,256]{1,0:T(8,128)S(1)} %convolution_add_fusion), channel_id=1, replica_groups=mesh['feat'=2,'dom'=16] {'feat'}, use_global_device_ids=true, to_apply=%region_1.2 | all-reduce | flops 32768 | bytes 196608 | tf_op jit(solution)/shard_map/psum | solution.py:66
  164.2 0.6 maximum_convert_fusion
  164.8 0.0 all-gather.2.cloned.1.call-update
  164.9 0.1 add.73
  165.0 0.1 add.78
  165.0 0.1 add.74
  165.1 0.0 copy-done.4
  165.1 0.4 dynamic-slice_reduce_fusion
  165.6 0.1 squeeze.6
  165.7 0.1 squeeze.5
  165.8 0.0 copy-done.6
  165.8 0.2 dynamic-slice_reduce_fusion.1
  165.9 0.1 iota_compare_fusion.1
  166.0 0.1 lt.81
  166.2 0.0 copy-done.2
  166.2 0.9 fusion.22
  167.1 50.2 %all-gather.2.cloned.1.call-done = bf16[2048,256]{1,0:T(8,128)(2,1)} async-done(((bf16[128,256]{1,0:T(8,128)(2,1)}), bf16[2048,256]{1,0:T(8,128)(2,1)}) %all-gather.2.cloned.1.call-update) | async-done | bytes 1048592 | tf_op jit(solution)/shard_map/all_gather | solution.py:13
  217.3 2.1 gather_fusion.1
  219.4 0.1 select_select_fusion
  219.5 0.0 copy-done.3
  219.5 0.0 copy-done.5
  219.5 1.9 fusion.13
  (5 shorter events, 0.0 us)
Async XLA Ops:
  6.5 27.3 %copy-start = (bf16[512,256]{1,0:T(8,128)(2,1)S(1)}, bf16[512,256]{1,0:T(8,128)(2,1)}, u32[]{:S(2)}) copy-start(bf16[512,256]{1,0:T(8,128)(2,1)} %param.18) | copy-start | bytes 786436
  6.5 152.7 %reduce-scatter.2.cloned.1.call-start = ((), (), s32[]{:S(2)}) async-start(), calls=%async_computation.1 | async-start | bytes 2228224 | tf_op jit(solution)/shard_map/reduce_scatter | solution.py:57
  33.8 30.1 %copy-start.7 = (s32[128]{0:T(128)S(1)}, s32[128]{0:T(128)}, u32[]{:S(2)}) copy-start(s32[128]{0:T(128)} %param.14) | copy-start | bytes 1540
  64.0 95.2 %copy-start.1 = (bf16[512,256]{1,0:T(8,128)(2,1)S(1)}, bf16[512,256]{1,0:T(8,128)(2,1)}, u32[]{:S(2)}) copy-start(bf16[512,256]{1,0:T(8,128)(2,1)} %param.17) | copy-start | bytes 786436
  64.0 101.2 %copy-start.4 = (s32[16,16,8]{1,2,0:T(8,128)S(1)}, s32[16,16,8]{1,2,0:T(8,128)}, u32[]{:S(2)}) copy-start(s32[16,16,8]{1,2,0:T(8,128)} %param.19) | copy-start | bytes 24580
  64.0 101.8 %copy-start.6 = (s32[16,16]{1,0:T(8,128)S(1)}, s32[16,16]{1,0:T(8,128)}, u32[]{:S(2)}) copy-start(s32[16,16]{1,0:T(8,128)} %param.20) | copy-start | bytes 3076
  64.0 102.2 %copy-start.2 = (bf16[256,172]{0,1:T(8,128)(2,1)S(1)}, bf16[256,172]{0,1:T(8,128)(2,1)}, u32[]{:S(2)}) copy-start(bf16[256,172]{0,1:T(8,128)(2,1)} %param.22) | copy-start | bytes 264196
  64.0 155.5 %copy-start.3 = (bf16[256,172]{0,1:T(8,128)(2,1)S(1)}, bf16[256,172]{0,1:T(8,128)(2,1)}, u32[]{:S(2)}) copy-start(bf16[256,172]{0,1:T(8,128)(2,1)} %param.23) | copy-start | bytes 264196
  64.0 155.5 %copy-start.5 = (bf16[64,256]{1,0:T(8,128)(2,1)S(1)}, bf16[64,256]{1,0:T(8,128)(2,1)}, u32[]{:S(2)}) copy-start(bf16[64,256]{1,0:T(8,128)(2,1)} %param.21) | copy-start | bytes 98308
  75.7 141.5 %all-gather.2.cloned.1.call-start = ((), (), s32[]{:S(2)}) async-start(), calls=%async_computation.2 | async-start | bytes 1114112 | tf_op jit(solution)/shard_map/all_gather | solution.py:13
Sparse Core Ops, SparseCore 0:
  75.9 83.2 reduce-scatter.1
  165.0 52.2 all-gather.1
where the time goes:
time: 229 us; the launch traced here: 228 us
  waiting for transfers between devices  134 us (59%)
  matrix products  59 us (26%)
  local copies, waits for them, and re-layouts  15.3 us (7%)
  between operations  13.6 us (6%)
  blocking collectives  3.85 us (2%)
  other arithmetic  2.94 us (1%)
    reduce_scatter x1, waiting for transfers between devices, body(): lax.psum_scatter(summed.reshape(lax.axis_size('dom') * tile_size, hidden_...  83.4 us
    all_gather x1, waiting for transfers between devices, pull_rows(): everything = lax.all_gather(hidden, 'dom', axis=0, tiled=True)  50.2 us
    dot_general x1, matrix products, body(): jnp.einsum('kys,sj->kyj', collected_rows, neighbour_weight_first, preferr...  30.1 us
    dot_general x1, matrix products, body(): jnp.einsum('zvx,zxm->zvm', masked_features, source_nodes, preferred_eleme...  15.7 us
    gather x1, local copies, waits for them, and re-layouts, body(): source_nodes = jnp.take(blocks, tile_src, axis=0)  9.42 us
    dot_general x1, matrix products, body(): jnp.einsum('tb,trh->brh', onehot, neighbour_rows, precision=lax.Precision...  9.14 us
  transfers between devices with their start and end apart: 2, of which 2 were waited for; matrix products, arithmetic and copies ran while one was open for 1% of the time, Pallas kernels for 0%

commit v1 on v0

v1 whole, which is shorter than its diff:
```python
import functools

import jax
import jax.numpy as jnp
from jax import lax
from jax.experimental import pallas as pl
from jax.experimental.pallas import tpu as pltpu
from jax.sharding import PartitionSpec as P

UNIT = 16
CHUNKS = 1


def group_of(core, place, groups):
    pair = 2 * (place // 2) + core
    return pair if place % 2 == 0 else groups - 1 - pair


def plan(src_row, rows_row, tops, tiles, n_blocks):
    units = len(tops) * tiles
    keys = []
    lane = lax.broadcasted_iota(jnp.int32, (1, tiles), 1)
    for j, top in enumerate(tops):
        keys.append(jnp.where(rows_row > top, src_row, n_blocks) * units + j * tiles + lane)
    key_row = jnp.concatenate(keys, axis=1)
    sub_i = lax.broadcasted_iota(jnp.int32, (units, units), 0)
    lane_i = lax.broadcasted_iota(jnp.int32, (units, units), 1)
    key_mat = jnp.broadcast_to(key_row, (units, units))
    key_col = jnp.sum(jnp.where(sub_i == lane_i, key_mat, 0).astype(jnp.float32), axis=1, keepdims=True).astype(jnp.int32)
    key_col_mat = jnp.broadcast_to(key_col, (units, units))
    rank_col = jnp.sum(jnp.where(key_mat < key_col_mat, 1.0, 0.0), axis=1, keepdims=True).astype(jnp.int32)
    inv = jnp.sum(jnp.where(rank_col == lane_i, sub_i, 0).astype(jnp.float32), axis=0, keepdims=True).astype(jnp.int32)
    starts = jnp.sum(jnp.where(key_col_mat < lane_i * units, 1.0, 0.0), axis=0, keepdims=True).astype(jnp.int32)
    return inv, starts


def tiles_kernel(
    chunk, per, n, radix,
    ids, src_s, dst_s, rows_s, src_v, rows_v, tw, xo, xp, wo, wp, so, sp,
    *rest,
):
    outs, rest = rest[:radix], rest[radix:]
    tbuf, xbuf, wbuf, sbuf, packed, gath, res, acc, plan_v, plan_s, sems = rest
    tiles, groups = tw.shape[0], tw.shape[1]
    tile = tw.shape[3]
    width = xo.shape[1]
    n_blocks = xo.shape[0] // tile
    hidden = wo.shape[1]
    units = per * tiles
    core, me = ids[0], ids[1]
    gs = [group_of(core, chunk * per + j, groups) for j in range(per)]
    copies = [pltpu.make_async_copy(tw.at[:, gs[j]], tbuf.at[j], sems.at[j]) for j in range(per)]
    extra = [
        pltpu.make_async_copy(a, b, sems.at[per + i])
        for i, (a, b) in enumerate([
            (xo, xbuf.at[0]), (xp, xbuf.at[1]), (wo, wbuf.at[0]), (wp, wbuf.at[1]), (so, sbuf.at[0]), (sp, sbuf.at[1]),
        ])
    ]
    for c in copies + extra:
        c.start()

    inv, starts = plan(src_v[...], rows_v[...], [UNIT * g for g in gs], tiles, n_blocks)
    plan_v[0:1, :] = inv
    plan_v[1:2, :] = starts
    to_scalar = pltpu.make_async_copy(plan_v, plan_s, sems.at[per + 6])
    to_scalar.start()
    acc[...] = jnp.zeros_like(acc)
    to_scalar.wait()
    n_valid = plan_s[1, n_blocks]
    for c in copies:
        c.wait()

    row_i = lax.broadcasted_iota(jnp.int32, (UNIT, tile), 0)

    def pack(b, carry):
        for i in range(8):
            p = b * 8 + i
            u = plan_s[0, p]
            t = lax.rem(u, tiles)
            j = lax.div(u, tiles)
            g = gs[0]
            for q in range(1, per):
                g = jnp.where(j == q, gs[q], g)
            value = tbuf[j, t].astype(jnp.float32)
            value = jnp.where(row_i < rows_s[t] - UNIT * g, value, 0.0).astype(jnp.bfloat16)
            packed[pl.ds(pl.multiple_of(p * UNIT, UNIT), UNIT), :] = value
        return carry

    lax.fori_loop(0, lax.div(n_valid + 7, 8), pack, 0)
    for c in extra:
        c.wait()

    def first(s, carry):
        lo, hi = plan_s[1, s], plan_s[1, s + 1]
        base = pl.multiple_of(s * tile, tile)

        def block(b, inner):
            at = pl.multiple_of((lo + 8 * b) * UNIT, UNIT)
            lhs = packed[pl.ds(at, 8 * UNIT), :]
            for h in range(2):
                got = jnp.dot(lhs, xbuf[h, pl.ds(base, tile), :], preferred_element_type=jnp.float32)
                gath[pl.ds(at, 8 * UNIT), h * width:(h + 1) * width] = got.astype(jnp.bfloat16)
            return inner

        return lax.fori_loop(0, lax.div(hi - lo + 7, 8), block, carry)

    lax.fori_loop(0, n_blocks, first, 0)

    for j in range(per):
        at = pl.multiple_of(gs[j] * UNIT, UNIT)
        own = jnp.dot(xbuf[0, pl.ds(at, UNIT), :], sbuf[0], preferred_element_type=jnp.float32)
        own = own + jnp.dot(xbuf[1, pl.ds(at, UNIT), :], sbuf[1], preferred_element_type=jnp.float32)
        acc[0, j * UNIT:(j + 1) * UNIT, :] = own

    def second(b, carry):
        at = pl.multiple_of(b * 16 * UNIT, 16 * UNIT)
        got = jnp.dot(gath[pl.ds(at, 16 * UNIT), :width], wbuf[0], preferred_element_type=jnp.float32)
        got = got + jnp.dot(gath[pl.ds(at, 16 * UNIT), width:], wbuf[1], preferred_element_type=jnp.float32)
        res[...] = got
        for i in range(16):
            p = b * 16 + i
            u = plan_s[0, p]
            t = lax.rem(u, tiles)
            j = lax.div(u, tiles)
            slot = jnp.bitwise_xor(dst_s[t], me)
            slot = lax.rem(slot, radix) * (n // radix) + lax.div(slot, radix)
            slot = jnp.where(p < n_valid, slot, n)
            where = pl.ds(pl.multiple_of(j * UNIT, UNIT), UNIT)
            acc[slot, where, :] += res[i * UNIT:(i + 1) * UNIT, :]
        return carry

    lax.fori_loop(0, lax.div(n_valid + 15, 16), second, 0)
    span = n // radix
    back = [pltpu.make_async_copy(acc.at[pl.ds(k * span, span)], outs[k], sems.at[per + 7 + k]) for k in range(radix)]
    for c in back:
        c.start()
    for c in back:
        c.wait()


def neighbour_terms(chunk, per, n, radix, ids, src, dst, rows, tw, xo, xp, wo, wp, so, sp):
    tiles, groups, _, tile = tw.shape
    units = per * tiles
    hidden = wo.shape[1]
    width = xo.shape[1]
    smem = pl.BlockSpec(memory_space=pltpu.SMEM)
    vmem = pl.BlockSpec(memory_space=pltpu.VMEM)
    anym = pl.BlockSpec(memory_space=pl.ANY)
    flops = 2 * units * UNIT * (tile * 2 * width + 2 * width * hidden)
    return pl.pallas_call(
        functools.partial(tiles_kernel, chunk, per, n, radix),
        out_shape=[jax.ShapeDtypeStruct((n // radix, per * UNIT, hidden), jnp.float32)] * radix,
        in_specs=[smem] * 4 + [vmem] * 2 + [anym] * 7,
        out_specs=[anym] * radix,
        scratch_shapes=[
            pltpu.VMEM((per, tiles, UNIT, tile), tw.dtype),
            pltpu.VMEM((2,) + xo.shape, xo.dtype),
            pltpu.VMEM((2,) + wo.shape, wo.dtype),
            pltpu.VMEM((2,) + so.shape, so.dtype),
            pltpu.VMEM(((units + 8) * UNIT, tile), jnp.bfloat16),
            pltpu.VMEM(((units + 16) * UNIT, 2 * width), jnp.bfloat16),
            pltpu.VMEM((16 * UNIT, hidden), jnp.float32),
            pltpu.VMEM((n + 1, per * UNIT, hidden), jnp.float32),
            pltpu.VMEM((2, units), jnp.int32),
            pltpu.SMEM((2, units), jnp.int32),
            pltpu.SemaphoreType.DMA((per + 7 + radix,)),
        ],
        compiler_params=pltpu.CompilerParams(vmem_limit_bytes=56 * 1024 * 1024),
        cost_estimate=pl.CostEstimate(flops=flops, bytes_accessed=8 << 20, transcendentals=0),
        name="neighbour_terms",
    )(ids, src, dst, rows, src.reshape(1, tiles), rows.reshape(1, tiles), tw, xo, xp, wo, wp, so, sp)


def select_kernel(tile, places, ids, lists, counts, out):
    core, me = ids[0], ids[1]
    slots, n = lists.shape[1], lists.shape[2]
    total = n * slots
    q_n = lax.broadcasted_iota(jnp.int32, (total, n), 0)
    r_n = lax.broadcasted_iota(jnp.int32, (total, n), 1)
    mine = lists[me].astype(jnp.float32)
    cnt = counts[pl.ds(me, 1), :]
    picked = jnp.zeros((total, n), jnp.float32)
    slot = jnp.bitwise_and(q_n, slots - 1)
    for k in range(slots):
        picked = jnp.where(slot == k, mine[k:k + 1, :], picked)
    good = jnp.logical_and(q_n // slots == r_n, slot < cnt)
    row = jnp.sum(jnp.where(good, picked + 1.0, 0.0), axis=1, keepdims=True) - 1.0
    held = len(places) * UNIT
    lane = lax.broadcasted_iota(jnp.int32, (1, held), 1)
    name = jnp.zeros((1, held), jnp.int32)
    for i, place in enumerate(places):
        g = group_of(core, place, tile // UNIT)
        name = jnp.where(lane // UNIT == i, g * UNIT + lane % UNIT, name)
    out[...] = jnp.where(row == name.astype(jnp.float32), 1.0, 0.0).astype(jnp.bfloat16)


def selection(ids, send_list, send_count, tile, places):
    n, _, slots = send_list.shape
    smem = pl.BlockSpec(memory_space=pltpu.SMEM)
    vmem = pl.BlockSpec(memory_space=pltpu.VMEM)
    return pl.pallas_call(
        functools.partial(select_kernel, tile, places),
        out_shape=jax.ShapeDtypeStruct((n * slots, len(places) * UNIT), jnp.bfloat16),
        in_specs=[smem, vmem, vmem],
        out_specs=vmem,
        compiler_params=pltpu.CompilerParams(vmem_limit_bytes=32 * 1024 * 1024),
        name="selection",
    )(ids, jnp.swapaxes(send_list, 1, 2), send_count)


def hidden_kernel(chunks, parts, *refs):
    sel, (own, send) = refs[chunks * parts], refs[chunks * parts + 1:]
    rows = refs[0].shape[1]
    for c in range(chunks):
        total = refs[c * parts][0]
        for k in range(1, parts):
            total = total + refs[c * parts + k][0]
        own[c * rows:(c + 1) * rows, :] = jnp.maximum(total, 0.0).astype(jnp.bfloat16)
    picked = jnp.dot(sel[...], own[...], preferred_element_type=jnp.float32).astype(jnp.bfloat16)
    half = picked.shape[0]
    send[:half, :] = picked
    send[half:, :] = picked


def hidden_rows(chunk_parts, sel):
    chunks, parts = len(chunk_parts), len(chunk_parts[0])
    held = sel.shape[1]
    width = chunk_parts[0][0].shape[2]
    vmem = pl.BlockSpec(memory_space=pltpu.VMEM)
    flat = [a for part in chunk_parts for a in part]
    return pl.pallas_call(
        functools.partial(hidden_kernel, chunks, parts),
        out_shape=[
            jax.ShapeDtypeStruct((held, width), jnp.bfloat16),
            jax.ShapeDtypeStruct((2 * sel.shape[0], width), jnp.bfloat16),
        ],
        in_specs=[vmem] * (len(flat) + 1),
        out_specs=[vmem] * 2,
        compiler_params=pltpu.CompilerParams(vmem_limit_bytes=32 * 1024 * 1024),
        name="hidden_rows",
    )(*flat, sel)


def logits_kernel(tile, places, ids, own, other, received, adj, w_self, w_neigh, out, pool):
    core = ids[0]
    groups = tile // UNIT
    for i, place in enumerate(places):
        mine = group_of(core, place, groups)
        theirs = group_of(1 - core, place, groups)
        pool[pl.ds(pl.multiple_of(mine * UNIT, UNIT), UNIT), :] = own[i * UNIT:(i + 1) * UNIT, :]
        pool[pl.ds(pl.multiple_of(theirs * UNIT, UNIT), UNIT), :] = other[i * UNIT:(i + 1) * UNIT, :]
    half = received.shape[0] // 2
    both = received[:half, :].astype(jnp.float32) + received[half:, :].astype(jnp.float32)
    pool[tile:, :] = both.astype(jnp.bfloat16)
    mean = jnp.dot(adj[...], pool[...], preferred_element_type=jnp.float32).astype(jnp.bfloat16)
    dims = (((1,), (1,)), ((), ()))
    rows = adj.shape[0]
    got = lax.dot_general(pool[:rows, :], w_self[...], dims, preferred_element_type=jnp.float32)
    out[...] = got + lax.dot_general(mean, w_neigh[...], dims, preferred_element_type=jnp.float32)


def logits_of(ids, own, other, received, adj, w_self, w_neigh, tile, places):
    smem = pl.BlockSpec(memory_space=pltpu.SMEM)
    vmem = pl.BlockSpec(memory_space=pltpu.VMEM)
    return pl.pallas_call(
        functools.partial(logits_kernel, tile, places),
        out_shape=jax.ShapeDtypeStruct((adj.shape[0], w_self.shape[1]), jnp.float32),
        in_specs=[smem] + [vmem] * 6,
        out_specs=vmem,
        scratch_shapes=[pltpu.VMEM((adj.shape[1], own.shape[1]), jnp.bfloat16)],
        compiler_params=pltpu.CompilerParams(vmem_limit_bytes=32 * 1024 * 1024),
        name="logits",
    )(ids, own, other, received, adj, w_self.T, w_neigh.T)


def exchange(parts, stride, n):
    got = [parts[0]]
    for k in range(1, len(parts)):
        got.append(lax.ppermute(parts[k], "dom", [(i, i ^ (k * stride)) for i in range(n)]))
    return got


def body(
    features,
    tile_weight,
    tile_dst,
    tile_src,
    tile_rows,
    w_self1,
    neighbour_weight_first,
    send_list,
    send_count,
    adj_two,
    w_self2,
    w_neigh2,
):
    n = lax.axis_size("dom")
    tile = tile_weight.shape[1]
    groups = tile // UNIT
    per = groups // 2 // CHUNKS
    places = list(range(groups // 2))
    bits = n.bit_length() - 1
    assert n == 1 << bits and bits >= 2
    radices = [2] * (bits // 2) + [1] * (bits % 2)
    ids = jnp.stack([lax.axis_index("feat"), lax.axis_index("dom")]).astype(jnp.int32)
    swap = [(0, 1), (1, 0)]
    xp = lax.ppermute(features, "feat", swap)
    wp = lax.ppermute(neighbour_weight_first, "feat", swap)
    sp = lax.ppermute(w_self1, "feat", swap)
    sel = selection(ids, send_list, send_count, tile, places)
    tw = tile_weight.reshape(tile_weight.shape[0], groups, UNIT, tile)
    done = []
    for chunk in range(CHUNKS):
        parts = neighbour_terms(
            chunk, per, n, 4, ids, tile_src, tile_dst, tile_rows, tw, features, xp,
            neighbour_weight_first, wp, w_self1, sp,
        )
        got = exchange(parts, 1, n)
        stride = 4
        for radix in radices[1:]:
            ways = 1 << radix
            parts = []
            for k in range(ways):
                total = got[0][k::ways]
                for a in got[1:]:
                    total = total + a[k::ways]
                parts.append(total)
            got = exchange(parts, stride, n)
            stride *= ways
        done.append(got)
    own, send = hidden_rows(done, sel)
    other = lax.ppermute(own, "feat", swap)
    received = lax.all_to_all(send, ("feat", "dom"), 0, 0, tiled=True)
    return logits_of(ids, own, other, received, adj_two, w_self2, w_neigh2, tile, places)


def solution(mesh):
    in_specs = (
        P("dom", "feat"),
        P("dom", None, None),
        P("dom"),
        P("dom"),
        P("dom"),
        P("feat", None),
        P("feat", None),
        P(),
        P(),
        P("dom", None),
        P(),
        P(),
    )
    out_specs = P("dom", None)
    return jax.shard_map(body, mesh=mesh, in_specs=in_specs, out_specs=out_specs, check_vma=False)
```

time: 229 us -> 68.8 us (0.30)
  waiting for transfers between devices: 134 us -> 27.5 us
  matrix products: 59 us -> 0 us
  Pallas kernels: 0 us -> 23.9 us
  starting transfers between devices: 0.04 us -> 14.9 us
  local copies, waits for them, and re-layouts: 15.3 us -> 1.12 us
  between operations: 13.6 us -> 0.08 us
  blocking collectives: 3.85 us -> 0 us
    reduce_scatter x1 -> x0, waiting for transfers between devices: 83.4 us -> none  [body(): lax.psum_scatter(summed.reshape(lax.axis_size('dom') * tile_size, hidden_...]
    dot_general x6 -> x0, matrix products: 59 us -> none  [the longest x1 30.1 us: body(): jnp.einsum('kys,sj->kyj', collected_rows, neighbour_weight_first, preferr...]
    all_gather x1 -> x0, waiting for transfers between devices: 50.2 us -> none  [pull_rows(): everything = lax.all_gather(hidden, 'dom', axis=0, tiled=True)]
    pallas_call x0 -> x4, Pallas kernels: none -> 23.9 us  [the longest x1 21 us: neighbour_terms(): pl.pallas_call(functools.partial(tiles_kernel, chunk, per, n, radix), out...]
    ppermute x0 -> x10, waiting for transfers between devices: none -> 20.9 us  [the longest x6 17.8 us: exchange(): lax.ppermute(parts[k], 'dom', [(i, i ^ k * stride) for i in range(n)])]
    ppermute x0 -> x10, starting transfers between devices: none -> 11.7 us  [the longest x6 10.4 us: exchange(): lax.ppermute(parts[k], 'dom', [(i, i ^ k * stride) for i in range(n)])]
    gather x2 -> x0, local copies, waits for them, and re-layouts: 11.5 us -> none  [the longest x1 9.42 us: body(): source_nodes = jnp.take(blocks, tile_src, axis=0)]
    all_to_all x0 -> x1, waiting for transfers between devices: none -> 6.64 us  [body(): received = lax.all_to_all(send, ('feat', 'dom'), 0, 0, tiled=True)]
  transfers between devices with their start and end apart: 2 -> 11, of which waited for: 2 -> 8; matrix products, arithmetic and copies ran while one was open for 1% -> 1% of each run, Pallas kernels for 0% -> 1%
where the time goes in v1:
time: 68.8 us; the launch traced here: 69.2 us
  waiting for transfers between devices  27.5 us (40%)
  Pallas kernels  23.9 us (35%)
  starting transfers between devices  14.9 us (22%)
  other arithmetic  1.65 us (2%)
  local copies, waits for them, and re-layouts  1.12 us (2%)
    pallas_call x1, Pallas kernels, neighbour_terms(): pl.pallas_call(functools.partial(tiles_kernel, chunk, per, n, radix), out...  21 us
    ppermute x6, waiting for transfers between devices, exchange(): lax.ppermute(parts[k], 'dom', [(i, i ^ k * stride) for i in range(n)])  17.8 us
    ppermute x6, starting transfers between devices, exchange(): lax.ppermute(parts[k], 'dom', [(i, i ^ k * stride) for i in range(n)])  10.4 us
    all_to_all x1, waiting for transfers between devices, body(): received = lax.all_to_all(send, ('feat', 'dom'), 0, 0, tiled=True)  6.64 us
    all_to_all x1, starting transfers between devices, body(): received = lax.all_to_all(send, ('feat', 'dom'), 0, 0, tiled=True)  3.21 us
    ppermute x1, waiting for transfers between devices, body(): wp = lax.ppermute(neighbour_weight_first, 'feat', swap)  1.72 us
    pallas_call x1, Pallas kernels, logits_of(): pl.pallas_call(functools.partial(logits_kernel, tile, places), out_shape=...  1.47 us
  transfers between devices with their start and end apart: 11, of which 8 were waited for; matrix products, arithmetic and copies ran while one was open for 1% of the time, Pallas kernels for 1%

profile of v1, /device:TPU:0, one launch (start us, length us, event | category | flops | bytes accessed | tf_op | source)
XLA Modules:
  0.0 69.2 jit_solution(12545207697242262478)
XLA Ops:
  0.0 0.5 collective-permute-start
  0.5 0.1 collective-permute-start.1
  0.5 0.5 collective-permute-start.2
  1.0 0.6 pad_add_fusion.ids
  1.6 1.7 %collective-permute-done.1.wp = bf16[512,256]{1,0:T(8,128)(2,1)S(1)} collective-permute-done((bf16[512,256]{1,0:T(8,128)(2,1)}, bf16[512,256]{1,0:T(8,128)(2,1)S(1)}, u32[]{:S(2)}, u32[]{:S(2)}) %collective-permute-start.1) | collective-permute-done | bytes 262176 | tf_op jit(solution)/shard_map/ppermute | solution.py:308
  3.3 0.0 copy-start.7
  3.3 0.4 collective-permute-done.2.sp
  3.7 0.0 copy-start.8
  3.7 0.0 collective-permute-done.xp
  3.7 0.0 copy-start.6
  3.7 0.3 copy-done.7
  4.0 0.4 copy-done.8
  4.4 0.4 copy-done.6
  4.8 0.0 copy-start.2
  4.8 0.0 copy-start.4
  4.8 0.0 copy-start.5
  4.8 0.0 copy-start
  4.8 0.0 copy-start.1
  4.8 0.0 copy-start.3
  4.8 21.0 %neighbour_terms.1 = (f32[4,64,256]{2,1,0:T(8,128)}, f32[4,64,256]{2,1,0:T(8,128)}, f32[4,64,256]{2,1,0:T(8,128)}, f32[4,64,256]{2,1,0:T(8,128)}) custom-call(s32[2]{0:T(128)} %pad_add_fusion.ids, s32[128]{0:T(128)} %src_s.1, s32[128]{0:T(128)} %dst_s.1, s32[128]{0:T(128)} %rows_s.1, s32[1,128]{1,0:T(1,128)} %bitcast.15, s32[1,128]{1,0:T(1,128)} %bitcast.16, ...), custom_call_target="tpu_custom_call" | custom-call | flops 6442450944 | bytes 8388608 | tf_op jit(solution)/shard_map/neighbour_terms/pallas_call | solution.py:150
  25.8 4.1 %collective-permute-start.3 = (f32[4,64,256]{2,1,0:T(8,128)}, f32[4,64,256]{2,1,0:T(8,128)S(1)}, u32[]{:S(2)}, u32[]{:S(2)}) collective-permute-start(f32[4,64,256]{2,1,0:T(8,128)} %get-tuple-element.12), channel_id=1, source_target_pairs={{0,1},{1,0},{2,3},{3,2},{4,5},{5,4},{6,7},{7,6},{8,9},{9,8},{10,11... | collective-permute-start | bytes 786440 | tf_op jit(solution)/shard_map/ppermute | solution.py:279
  29.9 0.4 collective-permute-start.4
  30.3 1.2 %collective-permute-start.5 = (f32[4,64,256]{2,1,0:T(8,128)}, f32[4,64,256]{2,1,0:T(8,128)S(1)}, u32[]{:S(2)}, u32[]{:S(2)}) collective-permute-start(f32[4,64,256]{2,1,0:T(8,128)} %get-tuple-element.14), channel_id=1, source_target_pairs={{0,3},{1,2},{2,1},{3,0},{4,7},{5,6},{6,5},{7,4},{8,11},{9,10},{10,... | collective-permute-start | bytes 786440 | tf_op jit(solution)/shard_map/ppermute | solution.py:279
  31.5 5.8 %collective-permute-done.3 = f32[4,64,256]{2,1,0:T(8,128)S(1)} collective-permute-done((f32[4,64,256]{2,1,0:T(8,128)}, f32[4,64,256]{2,1,0:T(8,128)S(1)}, u32[]{:S(2)}, u32[]{:S(2)}) %collective-permute-start.3) | collective-permute-done | bytes 262176 | tf_op jit(solution)/shard_map/ppermute | solution.py:279
  37.2 6.6 %collective-permute-done.4 = f32[4,64,256]{2,1,0:T(8,128)S(1)} collective-permute-done((f32[4,64,256]{2,1,0:T(8,128)}, f32[4,64,256]{2,1,0:T(8,128)S(1)}, u32[]{:S(2)}, u32[]{:S(2)}) %collective-permute-start.4) | collective-permute-done | bytes 262176 | tf_op jit(solution)/shard_map/ppermute | solution.py:279
  43.8 0.0 collective-permute-done.5
  43.8 1.0 %slice_add_fusion = (f32[1,64,256]{2,1,0:T(8,128)S(1)}, f32[1,64,256]{2,1,0:T(8,128)S(1)}, f32[1,64,256]{2,1,0:T(8,128)S(1)}, f32[1,64,256]{2,1,0:T(8,128)S(1)}) fusion(f32[4,64,256]{2,1,0:T(8,128)S(1)} %collective-permute-done.5, f32[4,64,256]{2,1,0:T(8,128)S(1)} %collective-permute-done.4, f32[4,64,256]{2,1,0:T(8,128)S(1)} %collective-permute-done.3, ...), kind=kLoop, calls=%fused_computation | loop fusion | flops 196608 | bytes 1310720 | tf_op jit(solution)/shard_map/add | solution.py:326
  44.8 1.5 %collective-permute-start.6 = (f32[1,64,256]{2,1,0:T(8,128)S(1)}, f32[1,64,256]{2,1,0:T(8,128)S(1)}, u32[]{:S(2)}, u32[]{:S(2)}) collective-permute-start(f32[1,64,256]{2,1,0:T(8,128)S(1)} %get-tuple-element.19), channel_id=1, source_target_pairs={{0,4},{1,5},{2,6},{3,7},{4,0},{5,1},{6,2},{7,3},{8,12},{9,13},{10,... | collective-permute-start | bytes 196616 | tf_op jit(solution)/shard_map/ppermute | solution.py:279
  46.3 3.3 %collective-permute-start.7 = (f32[1,64,256]{2,1,0:T(8,128)S(1)}, f32[1,64,256]{2,1,0:T(8,128)S(1)}, u32[]{:S(2)}, u32[]{:S(2)}) collective-permute-start(f32[1,64,256]{2,1,0:T(8,128)S(1)} %get-tuple-element.18), channel_id=1, source_target_pairs={{0,8},{1,9},{2,10},{3,11},{4,12},{5,13},{6,14},{7,15},{8,0},{9,1},... | collective-permute-start | bytes 196616 | tf_op jit(solution)/shard_map/ppermute | solution.py:279
  49.7 0.0 collective-permute-start.8
  49.7 0.0 copy-done.2
  49.7 0.0 copy-done.4
  49.7 0.0 copy-done.5
  49.7 0.7 selection.1.refs_4_
  50.4 0.0 collective-permute-done.6.refs_1_
  50.4 4.1 %collective-permute-done.7.refs_2_ = f32[1,64,256]{2,1,0:T(8,128)S(1)} collective-permute-done((f32[1,64,256]{2,1,0:T(8,128)S(1)}, f32[1,64,256]{2,1,0:T(8,128)S(1)}, u32[]{:S(2)}, u32[]{:S(2)}) %collective-permute-start.7) | collective-permute-done | bytes 65568 | tf_op jit(solution)/shard_map/ppermute | solution.py:279
  54.4 1.4 %collective-permute-done.8.refs_3_ = f32[1,64,256]{2,1,0:T(8,128)S(1)} collective-permute-done((f32[1,64,256]{2,1,0:T(8,128)S(1)}, f32[1,64,256]{2,1,0:T(8,128)S(1)}, u32[]{:S(2)}, u32[]{:S(2)}) %collective-permute-start.8) | collective-permute-done | bytes 65568 | tf_op jit(solution)/shard_map/ppermute | solution.py:279
  55.8 0.8 %hidden_rows.1 = (bf16[64,256]{1,0:T(8,128)(2,1)S(1)}, bf16[256,256]{1,0:T(8,128)(2,1)}) custom-call(f32[1,64,256]{2,1,0:T(8,128)S(1)} %get-tuple-element.20.refs_0_, f32[1,64,256]{2,1,0:T(8,128)S(1)} %collective-permute-done.6.refs_1_, f32[1,64,256]{2,1,0:T(8,128)S(1)} %collective-permute-done.7.refs_2_, f32[1,64,256]{2,1,0:T(8,128)S(1)} %collective-permute-done.8.refs_3_, ...), custom_call_target="tpu_custom_call" | custom-call | tf_op jit(solution)/shard_map/hidden_rows/pallas_call | solution.py:231
  56.6 3.2 %all-to-all-start = ((bf16[32,8,256]{2,1,0:T(8,128)(2,1)}), bf16[32,8,256]{2,1,0:T(8,128)(2,1)S(1)}, u32[]{:S(2)}, u32[]{:S(2)}) async-start(bf16[32,8,256]{2,1,0:T(8,128)(2,1)} %bitcast.6), calls=%async_computation | async-start | bytes 262144 | tf_op jit(solution)/shard_map/all_to_all | solution.py:333
  59.8 0.3 collective-permute-start.9
  60.2 1.0 %collective-permute-done.9.other = bf16[64,256]{1,0:T(8,128)(2,1)S(1)} collective-permute-done((bf16[64,256]{1,0:T(8,128)(2,1)S(1)}, bf16[64,256]{1,0:T(8,128)(2,1)S(1)}, u32[]{:S(2)}, u32[]{:S(2)}) %collective-permute-start.9) | collective-permute-done | bytes 32800 | tf_op jit(solution)/shard_map/ppermute | solution.py:332
  61.1 6.6 %all-to-all-done = bf16[32,8,256]{2,1,0:T(8,128)(2,1)S(1)} async-done(((bf16[32,8,256]{2,1,0:T(8,128)(2,1)}), bf16[32,8,256]{2,1,0:T(8,128)(2,1)S(1)}, u32[]{:S(2)}, u32[]{:S(2)}) %all-to-all-start) | async-done | bytes 131104 | tf_op jit(solution)/shard_map/all_to_all | solution.py:333
  67.8 0.0 copy-done
  67.8 0.0 copy-done.1
  67.8 0.0 copy-done.3
  67.8 1.5 %logits.1 = f32[64,172]{1,0:T(8,128)} custom-call(s32[2]{0:T(128)S(1)} %copy-done.5, bf16[64,256]{1,0:T(8,128)(2,1)S(1)} %get-tuple-element.15.own, bf16[64,256]{1,0:T(8,128)(2,1)S(1)} %collective-permute-done.9.other, bf16[256,256]{1,0:T(8,128)(2,1)S(1)} %bitcast.10, bf16[64,256]{1,0:T(8,128)(2,1)S(1)} %copy-done.3, bf16[172,256]{1,0:T(8,128)(2,1)S(1)} %bitcast.11, ...), custom_call_target="tpu_custom_call" | custom-call | tf_op jit(solution)/shard_map/logits/pallas_call | solution.py:265
Async XLA Ops:
  0.0 3.7 %collective-permute-start = (bf16[1024,512]{1,0:T(8,128)(2,1)}, bf16[1024,512]{1,0:T(8,128)(2,1)S(1)}, u32[]{:S(2)}, u32[]{:S(2)}) collective-permute-start(bf16[1024,512]{1,0:T(8,128)(2,1)} %xo.1), channel_id=1, source_target_pairs={{0,16},{16,0},{1,17},{17,1},{2,18},{18,2},{3,19},{19,3},{4,20},{20... | collective-permute-start | bytes 3145736 | tf_op jit(solution)/shard_map/ppermute | solution.py:307
  0.5 2.9 %collective-permute-start.1 = (bf16[512,256]{1,0:T(8,128)(2,1)}, bf16[512,256]{1,0:T(8,128)(2,1)S(1)}, u32[]{:S(2)}, u32[]{:S(2)}) collective-permute-start(bf16[512,256]{1,0:T(8,128)(2,1)} %wo.1), channel_id=1, source_target_pairs={{0,16},{16,0},{1,17},{17,1},{2,18},{18,2},{3,19},{19,3},{4,20},{20... | collective-permute-start | bytes 786440 | tf_op jit(solution)/shard_map/ppermute | solution.py:308
  0.5 3.2 %collective-permute-start.2 = (bf16[512,256]{1,0:T(8,128)(2,1)}, bf16[512,256]{1,0:T(8,128)(2,1)S(1)}, u32[]{:S(2)}, u32[]{:S(2)}) collective-permute-start(bf16[512,256]{1,0:T(8,128)(2,1)} %so.1), channel_id=1, source_target_pairs={{0,16},{16,0},{1,17},{17,1},{2,18},{18,2},{3,19},{19,3},{4,20},{20... | collective-permute-start | bytes 786440 | tf_op jit(solution)/shard_map/ppermute | solution.py:309
  3.3 0.7 copy-start.7
  3.7 0.7 copy-start.8
  3.7 1.1 %copy-start.6 = (bf16[1024,512]{1,0:T(8,128)(2,1)}, bf16[1024,512]{1,0:T(8,128)(2,1)S(1)}, u32[]{:S(2)}) copy-start(bf16[1024,512]{1,0:T(8,128)(2,1)S(1)} %collective-permute-done.xp) | copy-start | bytes 3145732
  4.8 44.9 %copy-start.2 = (s32[16,16,8]{1,2,0:T(8,128)S(1)}, s32[16,16,8]{1,2,0:T(8,128)}, u32[]{:S(2)}) copy-start(s32[16,16,8]{1,2,0:T(8,128)} %param.19) | copy-start | bytes 24580
  4.8 44.9 %copy-start.4 = (s32[16,16]{1,0:T(8,128)S(1)}, s32[16,16]{1,0:T(8,128)}, u32[]{:S(2)}) copy-start(s32[16,16]{1,0:T(8,128)} %counts.1) | copy-start | bytes 3076
  4.8 44.9 %copy-start.5 = (s32[2]{0:T(128)S(1)}, s32[2]{0:T(128)}, u32[]{:S(2)}) copy-start(s32[2]{0:T(128)} %pad_add_fusion.ids) | copy-start | bytes 28
  4.8 63.0 %copy-start = (bf16[256,172]{0,1:T(8,128)(2,1)S(1)}, bf16[256,172]{0,1:T(8,128)(2,1)}, u32[]{:S(2)}) copy-start(bf16[256,172]{0,1:T(8,128)(2,1)} %param.22) | copy-start | bytes 264196
  4.8 63.0 %copy-start.1 = (bf16[256,172]{0,1:T(8,128)(2,1)S(1)}, bf16[256,172]{0,1:T(8,128)(2,1)}, u32[]{:S(2)}) copy-start(bf16[256,172]{0,1:T(8,128)(2,1)} %param.23) | copy-start | bytes 264196
  4.8 63.0 %copy-start.3 = (bf16[64,256]{1,0:T(8,128)(2,1)S(1)}, bf16[64,256]{1,0:T(8,128)(2,1)}, u32[]{:S(2)}) copy-start(bf16[64,256]{1,0:T(8,128)(2,1)} %adj.1) | copy-start | bytes 98308
  25.8 11.4 %collective-permute-start.3 = (f32[4,64,256]{2,1,0:T(8,128)}, f32[4,64,256]{2,1,0:T(8,128)S(1)}, u32[]{:S(2)}, u32[]{:S(2)}) collective-permute-start(f32[4,64,256]{2,1,0:T(8,128)} %get-tuple-element.12), channel_id=1, source_target_pairs={{0,1},{1,0},{2,3},{3,2},{4,5},{5,4},{6,7},{7,6},{8,9},{9,8},{10,11... | collective-permute-start | bytes 786440 | tf_op jit(solution)/shard_map/ppermute | solution.py:279
  29.9 13.9 %collective-permute-start.4 = (f32[4,64,256]{2,1,0:T(8,128)}, f32[4,64,256]{2,1,0:T(8,128)S(1)}, u32[]{:S(2)}, u32[]{:S(2)}) collective-permute-start(f32[4,64,256]{2,1,0:T(8,128)} %get-tuple-element.13), channel_id=1, source_target_pairs={{0,2},{1,3},{2,0},{3,1},{4,6},{5,7},{6,4},{7,5},{8,10},{9,11},{10,... | collective-permute-start | bytes 786440 | tf_op jit(solution)/shard_map/ppermute | solution.py:279
  30.3 13.5 %collective-permute-start.5 = (f32[4,64,256]{2,1,0:T(8,128)}, f32[4,64,256]{2,1,0:T(8,128)S(1)}, u32[]{:S(2)}, u32[]{:S(2)}) collective-permute-start(f32[4,64,256]{2,1,0:T(8,128)} %get-tuple-element.14), channel_id=1, source_target_pairs={{0,3},{1,2},{2,1},{3,0},{4,7},{5,6},{6,5},{7,4},{8,11},{9,10},{10,... | collective-permute-start | bytes 786440 | tf_op jit(solution)/shard_map/ppermute | solution.py:279
  44.8 5.5 %collective-permute-start.6 = (f32[1,64,256]{2,1,0:T(8,128)S(1)}, f32[1,64,256]{2,1,0:T(8,128)S(1)}, u32[]{:S(2)}, u32[]{:S(2)}) collective-permute-start(f32[1,64,256]{2,1,0:T(8,128)S(1)} %get-tuple-element.19), channel_id=1, source_target_pairs={{0,4},{1,5},{2,6},{3,7},{4,0},{5,1},{6,2},{7,3},{8,12},{9,13},{10,... | collective-permute-start | bytes 196616 | tf_op jit(solution)/shard_map/ppermute | solution.py:279
  46.3 8.1 %collective-permute-start.7 = (f32[1,64,256]{2,1,0:T(8,128)S(1)}, f32[1,64,256]{2,1,0:T(8,128)S(1)}, u32[]{:S(2)}, u32[]{:S(2)}) collective-permute-start(f32[1,64,256]{2,1,0:T(8,128)S(1)} %get-tuple-element.18), channel_id=1, source_target_pairs={{0,8},{1,9},{2,10},{3,11},{4,12},{5,13},{6,14},{7,15},{8,0},{9,1},... | collective-permute-start | bytes 196616 | tf_op jit(solution)/shard_map/ppermute | solution.py:279
  49.7 6.2 %collective-permute-start.8 = (f32[1,64,256]{2,1,0:T(8,128)S(1)}, f32[1,64,256]{2,1,0:T(8,128)S(1)}, u32[]{:S(2)}, u32[]{:S(2)}) collective-permute-start(f32[1,64,256]{2,1,0:T(8,128)S(1)} %get-tuple-element.17), channel_id=1, source_target_pairs={{0,12},{1,13},{2,14},{3,15},{4,8},{5,9},{6,10},{7,11},{8,4},{9,5},... | collective-permute-start | bytes 196616 | tf_op jit(solution)/shard_map/ppermute | solution.py:279
  56.6 11.1 %all-to-all-start = ((bf16[32,8,256]{2,1,0:T(8,128)(2,1)}), bf16[32,8,256]{2,1,0:T(8,128)(2,1)S(1)}, u32[]{:S(2)}, u32[]{:S(2)}) async-start(bf16[32,8,256]{2,1,0:T(8,128)(2,1)} %bitcast.6), calls=%async_computation | async-start | bytes 262144 | tf_op jit(solution)/shard_map/all_to_all | solution.py:333
  59.8 1.3 %collective-permute-start.9 = (bf16[64,256]{1,0:T(8,128)(2,1)S(1)}, bf16[64,256]{1,0:T(8,128)(2,1)S(1)}, u32[]{:S(2)}, u32[]{:S(2)}) collective-permute-start(bf16[64,256]{1,0:T(8,128)(2,1)S(1)} %get-tuple-element.15.own), channel_id=1, source_target_pairs={{0,16},{16,0},{1,17},{17,1},{2,18},{18,2},{3,19},{19,3},{4,20},{20... | collective-permute-start | bytes 98312 | tf_op jit(solution)/shard_map/ppermute | solution.py:332

commit v2 on v1

v2 whole, which is shorter than its diff:
```python
import functools

import jax
import jax.numpy as jnp
from jax import lax
from jax.experimental import pallas as pl
from jax.experimental.pallas import tpu as pltpu
from jax.sharding import PartitionSpec as P

UNIT = 16
BLOCK = 16
LEAD = 3
CHUNKS = 1


def group_of(core, place, groups):
    pair = 2 * (place // 2) + core
    return pair if place % 2 == 0 else groups - 1 - pair


def plan_kernel(chunks, per, n, radix, n_src, ids, src_v, rows_v, dst_v, lists, counts, *outs):
    core, me = ids[0], ids[1]
    tiles = src_v.shape[1]
    tables, sel = outs[:chunks], outs[chunks]
    n_pos = tables[0].shape[1]
    units = per * tiles
    groups = 2 * per * chunks
    lead = LEAD * BLOCK
    src, rows = src_v[...], rows_v[...]
    slot = jnp.bitwise_xor(dst_v[...], me)
    slot = jnp.bitwise_and(slot, radix - 1) * (n // radix) + lax.div(slot, radix)
    lane = lax.broadcasted_iota(jnp.int32, (1, tiles), 1)
    block_i = lax.broadcasted_iota(jnp.int32, (n_src, tiles), 0)
    before = lax.broadcasted_iota(jnp.int32, (units, units), 0) < lax.broadcasted_iota(jnp.int32, (units, units), 1)
    before = jnp.where(before, 1.0, 0.0).astype(jnp.bfloat16)
    pos_i = lax.broadcasted_iota(jnp.int32, (tiles, n_pos), 1).astype(jnp.float32)
    place_i = lax.broadcasted_iota(jnp.int32, (1, n_pos), 1)
    trash = float(n * per << 14)
    for c in range(chunks):
        hot, words, valid = [], [], []
        for j in range(per):
            g = group_of(core, c * per + j, groups)
            limit = jnp.clip(rows - UNIT * g, 0, UNIT)
            ok = limit > 0
            valid.append(ok)
            words.append(((slot * per + j) * 512 + (j * tiles + lane)) * 32 + limit)
            hot.append(jnp.where(jnp.logical_and(block_i == src, ok), 1.0, 0.0))
        hot = jnp.concatenate(hot, axis=1)
        earlier = jnp.dot(hot.astype(jnp.bfloat16), before, preferred_element_type=jnp.float32)
        blocks = jnp.floor((jnp.sum(hot, axis=1, keepdims=True) + (BLOCK - 1)) * (1.0 / BLOCK))
        run = jnp.zeros((1, 1), jnp.float32)
        pos = jnp.zeros((1, units), jnp.float32)
        owner = jnp.zeros((1, n_pos), jnp.float32)
        for s in range(n_src):
            pos = pos + hot[s:s + 1, :] * (earlier[s:s + 1, :] + (run * BLOCK + lead))
            run = run + blocks[s:s + 1, :]
            owner = owner + jnp.where(place_i.astype(jnp.float32) >= run, 1.0, 0.0)
        stack = [jnp.where(valid[j], pos[:, j * tiles:(j + 1) * tiles], -1.0) for j in range(per)]
        stack += [w.astype(jnp.float32) - trash for w in words]
        stack += [jnp.zeros((1, tiles), jnp.float32)] * (-len(stack) % 8)
        cols = jnp.concatenate(stack, axis=0).T
        found = jnp.zeros((tiles, n_pos), jnp.float32)
        for j in range(per):
            found = found + jnp.where(cols[:, j:j + 1] == pos_i, cols[:, per + j:per + j + 1], 0.0)
        word = jnp.sum(found, axis=0, keepdims=True) + trash
        owner = jnp.where(place_i == n_pos - 1, run, jnp.minimum(owner, n_src - 1.0))
        tables[c][0:1, :] = word.astype(jnp.int32)
        tables[c][1:2, :] = owner.astype(jnp.int32)

    slots = lists.shape[1]
    total = n * slots
    q_n = lax.broadcasted_iota(jnp.int32, (total, n), 0)
    r_n = lax.broadcasted_iota(jnp.int32, (total, n), 1)
    mine = lists[me].astype(jnp.float32)
    cnt = counts[pl.ds(me, 1), :]
    picked = jnp.zeros((total, n), jnp.float32)
    k_n = jnp.bitwise_and(q_n, slots - 1)
    for k in range(slots):
        picked = jnp.where(k_n == k, mine[k:k + 1, :], picked)
    good = jnp.logical_and(lax.div(q_n, slots) == r_n, k_n < cnt)
    row = jnp.sum(jnp.where(good, picked + 1.0, 0.0), axis=1, keepdims=True) - 1.0
    held = groups // 2 * UNIT
    lane = lax.broadcasted_iota(jnp.int32, (1, held), 1)
    name = jnp.zeros((1, held), jnp.int32)
    for i in range(groups // 2):
        g = group_of(core, i, groups)
        name = jnp.where(lax.div(lane, UNIT) == i, g * UNIT + jnp.bitwise_and(lane, UNIT - 1), name)
    sel[...] = jnp.where(row == name.astype(jnp.float32), 1.0, 0.0).astype(jnp.bfloat16)


def plan(chunks, per, n, radix, n_src, ids, src, rows, dst, send_list, send_count):
    tiles = src.shape[0]
    slots = send_list.shape[2]
    n_pos = -(-(LEAD * BLOCK + per * tiles + (n_src + LEAD) * BLOCK) // 128) * 128
    smem = pl.BlockSpec(memory_space=pltpu.SMEM)
    vmem = pl.BlockSpec(memory_space=pltpu.VMEM)
    return pl.pallas_call(
        functools.partial(plan_kernel, chunks, per, n, radix, n_src),
        out_shape=[jax.ShapeDtypeStruct((2, n_pos), jnp.int32)] * chunks
        + [jax.ShapeDtypeStruct((n * slots, chunks * per * UNIT), jnp.bfloat16)],
        in_specs=[smem] + [vmem] * 5,
        out_specs=[vmem] * (chunks + 1),
        compiler_params=pltpu.CompilerParams(vmem_limit_bytes=32 * 1024 * 1024),
        name="plan",
    )(ids, src.reshape(1, tiles), rows.reshape(1, tiles), dst.reshape(1, tiles), jnp.swapaxes(send_list, 1, 2), send_count)


def tiles_kernel(chunk, per, n, radix, ids, table, tw, xo, xp, wo, wp, so, sp, *rest):
    outs, rest = rest[:radix], rest[radix:]
    tbuf, xbuf, wbuf, sbuf, masks, packed, gath, res, acc, sems = rest
    tiles, groups = tw.shape[0], tw.shape[1]
    tile = tw.shape[3]
    width = xo.shape[1]
    core = ids[0]
    gs = [group_of(core, chunk * per + j, groups) for j in range(per)]
    copies = [
        pltpu.make_async_copy(a, b, sems.at[i])
        for i, (a, b) in enumerate(
            [(tw.at[:, gs[j]], tbuf.at[pl.ds(j * tiles, tiles)]) for j in range(per)]
            + [
                (xo, xbuf.at[:, pl.ds(0, width)]),
                (xp, xbuf.at[:, pl.ds(width, width)]),
                (wo, wbuf.at[pl.ds(0, width)]),
                (wp, wbuf.at[pl.ds(width, width)]),
                (so, sbuf.at[pl.ds(0, width)]),
                (sp, sbuf.at[pl.ds(width, width)]),
            ]
        )
    ]
    for c in copies:
        c.start()
    acc[...] = jnp.zeros_like(acc)
    row_i = lax.broadcasted_iota(jnp.int32, (UNIT, tile), 0)
    for m in range(UNIT + 1):
        masks[m] = jnp.where(row_i < m, 1.0, 0.0).astype(jnp.bfloat16)
    n_blocks = table[1, table.shape[1] - 1]
    for c in copies:
        c.wait()
    for j in range(per):
        at = pl.multiple_of(gs[j] * UNIT, UNIT)
        own = jnp.dot(xbuf[pl.ds(at, UNIT), :], sbuf[...], preferred_element_type=jnp.float32)
        acc[j * UNIT:(j + 1) * UNIT, :] = own

    def step(i, carry):
        for k in range(BLOCK):
            word = table[0, i * BLOCK + k]
            at = pl.multiple_of(lax.shift_right_logical(word, 14) * UNIT, UNIT)
            acc[pl.ds(at, UNIT), :] += res[k * UNIT:(k + 1) * UNIT, :]
        res[...] = jnp.dot(gath[...], wbuf[...], preferred_element_type=jnp.float32)
        s = table[1, jnp.maximum(i - 1, 0)]
        base = pl.multiple_of(s * tile, tile)
        for h in range(0, 2 * width, 256):
            got = jnp.dot(packed[...], xbuf[pl.ds(base, tile), h:h + 256], preferred_element_type=jnp.float32)
            gath[:, h:h + 256] = got.astype(jnp.bfloat16)
        for k in range(BLOCK):
            word = table[0, (i + LEAD) * BLOCK + k]
            u = jnp.bitwise_and(lax.shift_right_logical(word, 5), 511)
            packed[k * UNIT:(k + 1) * UNIT, :] = tbuf[u] * masks[jnp.bitwise_and(word, 31)]
        return carry

    lax.fori_loop(0, n_blocks + LEAD, step, 0)
    span = n // radix * per * UNIT
    back = [pltpu.make_async_copy(acc.at[pl.ds(k * span, span)], outs[k], sems.at[per + 6 + k]) for k in range(radix)]
    for c in back:
        c.start()
    for c in back:
        c.wait()


def neighbour_terms(chunk, per, n, radix, ids, table, tw, xo, xp, wo, wp, so, sp):
    tiles, groups, _, tile = tw.shape
    units = per * tiles
    hidden = wo.shape[1]
    rows, width = xo.shape
    smem = pl.BlockSpec(memory_space=pltpu.SMEM)
    anym = pl.BlockSpec(memory_space=pl.ANY)
    flops = 2 * units * UNIT * (tile * 2 * width + 2 * width * hidden)
    return pl.pallas_call(
        functools.partial(tiles_kernel, chunk, per, n, radix),
        out_shape=[jax.ShapeDtypeStruct((n // radix * per * UNIT, hidden), jnp.float32)] * radix,
        in_specs=[smem] * 2 + [anym] * 7,
        out_specs=[anym] * radix,
        scratch_shapes=[
            pltpu.VMEM((units, UNIT, tile), tw.dtype),
            pltpu.VMEM((rows, 2 * width), xo.dtype),
            pltpu.VMEM((2 * width, hidden), wo.dtype),
            pltpu.VMEM((2 * width, hidden), so.dtype),
            pltpu.VMEM((UNIT + 1, UNIT, tile), jnp.bfloat16),
            pltpu.VMEM((BLOCK * UNIT, tile), jnp.bfloat16),
            pltpu.VMEM((BLOCK * UNIT, 2 * width), jnp.bfloat16),
            pltpu.VMEM((BLOCK * UNIT, hidden), jnp.float32),
            pltpu.VMEM(((n * per + 1) * UNIT, hidden), jnp.float32),
            pltpu.SemaphoreType.DMA((per + 6 + radix,)),
        ],
        compiler_params=pltpu.CompilerParams(vmem_limit_bytes=40 * 1024 * 1024),
        cost_estimate=pl.CostEstimate(flops=flops, bytes_accessed=8 << 20, transcendentals=0),
        name="neighbour_terms",
    )(ids, table, tw, xo, xp, wo, wp, so, sp)


def hidden_kernel(chunks, parts, *refs):
    sel, (own, send) = refs[chunks * parts], refs[chunks * parts + 1:]
    rows = refs[0].shape[0]
    for c in range(chunks):
        total = refs[c * parts][...]
        for k in range(1, parts):
            total = total + refs[c * parts + k][...]
        own[c * rows:(c + 1) * rows, :] = jnp.maximum(total, 0.0).astype(jnp.bfloat16)
    picked = jnp.dot(sel[...], own[...], preferred_element_type=jnp.float32).astype(jnp.bfloat16)
    half = picked.shape[0]
    send[:half, :] = picked
    send[half:, :] = picked


def hidden_rows(chunk_parts, sel):
    chunks, parts = len(chunk_parts), len(chunk_parts[0])
    held = sel.shape[1]
    width = chunk_parts[0][0].shape[1]
    vmem = pl.BlockSpec(memory_space=pltpu.VMEM)
    flat = [a for part in chunk_parts for a in part]
    return pl.pallas_call(
        functools.partial(hidden_kernel, chunks, parts),
        out_shape=[
            jax.ShapeDtypeStruct((held, width), jnp.bfloat16),
            jax.ShapeDtypeStruct((2 * sel.shape[0], width), jnp.bfloat16),
        ],
        in_specs=[vmem] * (len(flat) + 1),
        out_specs=[vmem] * 2,
        compiler_params=pltpu.CompilerParams(vmem_limit_bytes=32 * 1024 * 1024),
        name="hidden_rows",
    )(*flat, sel)


def logits_kernel(tile, places, ids, own, other, received, adj, w_self, w_neigh, out, pool):
    core = ids[0]
    groups = tile // UNIT
    for i, place in enumerate(places):
        mine = group_of(core, place, groups)
        theirs = group_of(1 - core, place, groups)
        pool[pl.ds(pl.multiple_of(mine * UNIT, UNIT), UNIT), :] = own[i * UNIT:(i + 1) * UNIT, :]
        pool[pl.ds(pl.multiple_of(theirs * UNIT, UNIT), UNIT), :] = other[i * UNIT:(i + 1) * UNIT, :]
    half = received.shape[0] // 2
    both = received[:half, :].astype(jnp.float32) + received[half:, :].astype(jnp.float32)
    pool[tile:, :] = both.astype(jnp.bfloat16)
    mean = jnp.dot(adj[...], pool[...], preferred_element_type=jnp.float32).astype(jnp.bfloat16)
    dims = (((1,), (1,)), ((), ()))
    rows = adj.shape[0]
    got = lax.dot_general(pool[:rows, :], w_self[...], dims, preferred_element_type=jnp.float32)
    out[...] = got + lax.dot_general(mean, w_neigh[...], dims, preferred_element_type=jnp.float32)


def logits_of(ids, own, other, received, adj, w_self, w_neigh, tile, places):
    smem = pl.BlockSpec(memory_space=pltpu.SMEM)
    vmem = pl.BlockSpec(memory_space=pltpu.VMEM)
    return pl.pallas_call(
        functools.partial(logits_kernel, tile, places),
        out_shape=jax.ShapeDtypeStruct((adj.shape[0], w_self.shape[1]), jnp.float32),
        in_specs=[smem] + [vmem] * 6,
        out_specs=vmem,
        scratch_shapes=[pltpu.VMEM((adj.shape[1], own.shape[1]), jnp.bfloat16)],
        compiler_params=pltpu.CompilerParams(vmem_limit_bytes=32 * 1024 * 1024),
        name="logits",
    )(ids, own, other, received, adj, w_self.T, w_neigh.T)


def exchange(parts, stride, n):
    got = [parts[0]]
    for k in range(1, len(parts)):
        got.append(lax.ppermute(parts[k], "dom", [(i, i ^ (k * stride)) for i in range(n)]))
    return got


def body(
    features,
    tile_weight,
    tile_dst,
    tile_src,
    tile_rows,
    w_self1,
    neighbour_weight_first,
    send_list,
    send_count,
    adj_two,
    w_self2,
    w_neigh2,
):
    n = lax.axis_size("dom")
    tile = tile_weight.shape[1]
    groups = tile // UNIT
    per = groups // 2 // CHUNKS
    places = list(range(groups // 2))
    bits = n.bit_length() - 1
    assert n == 1 << bits and bits >= 2
    radices = [2] * (bits // 2) + [1] * (bits % 2)
    ids = jnp.stack([lax.axis_index("feat"), lax.axis_index("dom")]).astype(jnp.int32)
    swap = [(0, 1), (1, 0)]
    xp = lax.ppermute(features, "feat", swap)
    wp = lax.ppermute(neighbour_weight_first, "feat", swap)
    sp = lax.ppermute(w_self1, "feat", swap)
    tw = tile_weight.reshape(tile_weight.shape[0], groups, UNIT, tile)
    *tables, sel = plan(CHUNKS, per, n, 4, features.shape[0] // tile, ids, tile_src, tile_rows, tile_dst, send_list, send_count)
    done = []
    for chunk in range(CHUNKS):
        parts = neighbour_terms(
            chunk, per, n, 4, ids, tables[chunk], tw, features, xp, neighbour_weight_first, wp, w_self1, sp,
        )
        got = exchange(parts, 1, n)
        stride = 4
        left = n // 4
        for radix in radices[1:]:
            ways = 1 << radix
            got = [a.reshape(left, per * UNIT, -1) for a in got]
            left //= ways
            parts = []
            for k in range(ways):
                total = got[0][k::ways]
                for a in got[1:]:
                    total = total + a[k::ways]
                parts.append(total.reshape(left * per * UNIT, -1))
            got = exchange(parts, stride, n)
            stride *= ways
        done.append(got)
    own, send = hidden_rows(done, sel)
    other = lax.ppermute(own, "feat", swap)
    received = lax.all_to_all(send, ("feat", "dom"), 0, 0, tiled=True)
    return logits_of(ids, own, other, received, adj_two, w_self2, w_neigh2, tile, places)


def solution(mesh):
    in_specs = (
        P("dom", "feat"),
        P("dom", None, None),
        P("dom"),
        P("dom"),
        P("dom"),
        P("feat", None),
        P("feat", None),
        P(),
        P(),
        P("dom", None),
        P(),
        P(),
    )
    out_specs = P("dom", None)
    return jax.shard_map(body, mesh=mesh, in_specs=in_specs, out_specs=out_specs, check_vma=False)
```

time: 68.8 us -> 64.8 us (0.942)
  local copies, waits for them, and re-layouts: 1.12 us -> 8.82 us
  Pallas kernels: 23.9 us -> 16.2 us
  waiting for transfers between devices: 27.5 us -> 25.1 us
  other arithmetic: 1.65 us -> 0.14 us
    pallas_call x1, Pallas kernels: 21 us -> 12.8 us  [neighbour_terms(): pl.pallas_call(functools.partial(tiles_kernel, chunk, per, n, radix), out...]
    unnamed x18 -> x24, local copies, waits for them, and re-layouts: 1.12 us -> 8.82 us
    ppermute x1, waiting for transfers between devices: 1.72 us -> 0.01 us  [body(): wp = lax.ppermute(neighbour_weight_first, 'feat', swap)]
    add x1, other arithmetic: 1.01 us -> 0.07 us  [body(): total = total + a[k::ways]]
  transfers between devices with their start and end apart: 11 -> 11, of which waited for: 8 -> 7; matrix products, arithmetic and copies ran while one was open for 1% -> 0% of each run, Pallas kernels for 1% -> 2%
where the time goes in v2:
time: 64.8 us
  waiting for transfers between devices  25.1 us (39%)
  Pallas kernels  16.2 us (25%)
  starting transfers between devices  14.4 us (22%)
  local copies, waits for them, and re-layouts  8.82 us (14%)
    ppermute x6, waiting for transfers between devices, exchange(): lax.ppermute(parts[k], 'dom', [(i, i ^ k * stride) for i in range(n)])  17.5 us
    pallas_call x1, Pallas kernels, neighbour_terms(): pl.pallas_call(functools.partial(tiles_kernel, chunk, per, n, radix), out...  12.8 us
    ppermute x6, starting transfers between devices, exchange(): lax.ppermute(parts[k], 'dom', [(i, i ^ k * stride) for i in range(n)])  9.79 us
    unnamed x24, local copies, waits for them, and re-layouts  8.82 us
    all_to_all x1, waiting for transfers between devices, body(): received = lax.all_to_all(send, ('feat', 'dom'), 0, 0, tiled=True)  6.64 us
    all_to_all x1, starting transfers between devices, body(): received = lax.all_to_all(send, ('feat', 'dom'), 0, 0, tiled=True)  3.31 us
    pallas_call x1, Pallas kernels, logits_of(): pl.pallas_call(functools.partial(logits_kernel, tile, places), out_shape=...  1.47 us
  transfers between devices with their start and end apart: 11, of which 7 were waited for; matrix products, arithmetic and copies ran while one was open for 0% of the time, Pallas kernels for 2%

profile of v2, /device:TPU:0, one launch (start us, length us, event | category | flops | bytes accessed | tf_op | source)
XLA Modules:
  0.0 64.8 jit_solution(12144846032083046001)
XLA Ops:
  0.0 0.5 collective-permute-start
  0.5 0.1 collective-permute-start.2
  0.5 0.5 collective-permute-start.1
  1.0 0.1 pad_add_fusion.ids
  1.0 0.0 copy-start.2
  1.0 0.8 %copy-done.2 = s32[16,16,8]{1,2,0:T(8,128)S(1)} copy-done((s32[16,16,8]{1,2,0:T(8,128)S(1)}, s32[16,16,8]{1,2,0:T(8,128)}, u32[]{:S(2)}) %copy-start.2) | copy-done | bytes 8216
  1.9 0.0 copy-start.4
  1.9 0.7 %copy-done.4 = s32[16,16]{1,0:T(8,128)S(1)} copy-done((s32[16,16]{1,0:T(8,128)S(1)}, s32[16,16]{1,0:T(8,128)}, u32[]{:S(2)}) %copy-start.4) | copy-done | bytes 1048
  2.6 0.0 copy-start.5
  2.6 0.7 %copy-done.5 = s32[128]{0:T(128)S(1)} copy-done((s32[128]{0:T(128)S(1)}, s32[128]{0:T(128)}, u32[]{:S(2)}) %copy-start.5) | copy-done | bytes 536
  3.2 0.0 copy-start.6
  3.2 0.7 %copy-done.6 = s32[128]{0:T(128)S(1)} copy-done((s32[128]{0:T(128)S(1)}, s32[128]{0:T(128)}, u32[]{:S(2)}) %copy-start.6) | copy-done | bytes 536
  3.9 0.0 copy-start.7
  3.9 0.7 %copy-done.7 = s32[128]{0:T(128)S(1)} copy-done((s32[128]{0:T(128)S(1)}, s32[128]{0:T(128)}, u32[]{:S(2)}) %copy-start.7) | copy-done | bytes 536
  4.5 1.1 %plan.1 = (s32[2,768]{1,0:T(2,128)S(1)}, bf16[128,64]{1,0:T(8,128)(2,1)S(1)}) custom-call(s32[2]{0:T(128)S(1)} %pad_add_fusion.ids, s32[1,128]{1,0:T(1,128)S(1)} %bitcast.15, s32[1,128]{1,0:T(1,128)S(1)} %bitcast.16, s32[1,128]{1,0:T(1,128)S(1)} %bitcast.17, s32[16,8,16]{2,1,0:T(8,128)S(1)} %bitcast.14, s32[16,16]{1,0:T(8,128)S(1)} %copy-done.4), custom_call_target="tpu_custom_call" | custom-call | tf_op jit(solution)/shard_map/plan/pallas_call | solution.py:97
  5.7 0.0 collective-permute-done.2.sp
  5.7 0.0 collective-permute-done.1.wp
  5.7 0.0 collective-permute-done.xp
  5.7 0.0 copy-start.8
  5.7 2.2 %copy-done.8 = bf16[128,128,128]{2,1,0:T(8,128)(2,1)S(1)} copy-done((bf16[128,128,128]{2,1,0:T(8,128)(2,1)S(1)}, bf16[128,128,128]{2,1,0:T(8,128)(2,1)}, u32[]{:S(2)}) %copy-start.8) | copy-done | bytes 4194328
  7.9 0.0 copy-start.9
  7.9 1.2 %copy-done.9 = bf16[1024,512]{1,0:T(8,128)(2,1)S(1)} copy-done((bf16[1024,512]{1,0:T(8,128)(2,1)S(1)}, bf16[1024,512]{1,0:T(8,128)(2,1)}, u32[]{:S(2)}) %copy-start.9) | copy-done | bytes 1048600
  9.1 0.0 copy-start.10
  9.1 0.9 %copy-done.10 = bf16[512,256]{1,0:T(8,128)(2,1)S(1)} copy-done((bf16[512,256]{1,0:T(8,128)(2,1)S(1)}, bf16[512,256]{1,0:T(8,128)(2,1)}, u32[]{:S(2)}) %copy-start.10) | copy-done | bytes 262168
  10.1 0.0 copy-start.11
  10.1 0.9 %copy-done.11 = bf16[512,256]{1,0:T(8,128)(2,1)S(1)} copy-done((bf16[512,256]{1,0:T(8,128)(2,1)S(1)}, bf16[512,256]{1,0:T(8,128)(2,1)}, u32[]{:S(2)}) %copy-start.11) | copy-done | bytes 262168
  11.0 0.0 copy-start
  11.0 0.0 copy-start.1
  11.0 0.0 copy-start.3
  11.0 12.8 %neighbour_terms.1 = (f32[256,256]{1,0:T(8,128)S(1)}, f32[256,256]{1,0:T(8,128)S(1)}, f32[256,256]{1,0:T(8,128)S(1)}, f32[256,256]{1,0:T(8,128)S(1)}) custom-call(s32[2]{0:T(128)S(1)} %pad_add_fusion.ids, s32[2,768]{1,0:T(2,128)S(1)} %get-tuple-element.13.table, bf16[128,8,16,128]{3,2,1,0:T(8,128)(2,1)S(1)} %bitcast.18, bf16[1024,512]{1,0:T(8,128)(2,1)S(1)} %copy-done.9, ...), custom_call_target="tpu_custom_call" | custom-call | flops 6442450944 | bytes 8388608 | tf_op jit(solution)/shard_map/neighbour_terms/pallas_call | solution.py:178
  23.9 3.5 %collective-permute-start.3 = (f32[256,256]{1,0:T(8,128)S(1)}, f32[256,256]{1,0:T(8,128)S(1)}, u32[]{:S(2)}, u32[]{:S(2)}) collective-permute-start(f32[256,256]{1,0:T(8,128)S(1)} %get-tuple-element.15), channel_id=1, source_target_pairs={{0,1},{1,0},{2,3},{3,2},{4,5},{5,4},{6,7},{7,6},{8,9},{9,8},{10,11... | collective-permute-start | bytes 786440 | tf_op jit(solution)/shard_map/ppermute | solution.py:269
  27.3 0.6 collective-permute-start.4
  27.9 0.9 %collective-permute-start.5 = (f32[256,256]{1,0:T(8,128)S(1)}, f32[256,256]{1,0:T(8,128)S(1)}, u32[]{:S(2)}, u32[]{:S(2)}) collective-permute-start(f32[256,256]{1,0:T(8,128)S(1)} %get-tuple-element.17), channel_id=1, source_target_pairs={{0,3},{1,2},{2,1},{3,0},{4,7},{5,6},{6,5},{7,4},{8,11},{9,10},{10,... | collective-permute-start | bytes 786440 | tf_op jit(solution)/shard_map/ppermute | solution.py:269
  28.9 5.6 %collective-permute-done.3 = f32[256,256]{1,0:T(8,128)S(1)} collective-permute-done((f32[256,256]{1,0:T(8,128)S(1)}, f32[256,256]{1,0:T(8,128)S(1)}, u32[]{:S(2)}, u32[]{:S(2)}) %collective-permute-start.3) | collective-permute-done | bytes 262176 | tf_op jit(solution)/shard_map/ppermute | solution.py:269
  34.5 6.9 %collective-permute-done.4 = f32[256,256]{1,0:T(8,128)S(1)} collective-permute-done((f32[256,256]{1,0:T(8,128)S(1)}, f32[256,256]{1,0:T(8,128)S(1)}, u32[]{:S(2)}, u32[]{:S(2)}) %collective-permute-start.4) | collective-permute-done | bytes 262176 | tf_op jit(solution)/shard_map/ppermute | solution.py:269
  41.4 0.0 collective-permute-done.5
  41.4 0.1 slice_add_fusion
  41.4 4.1 %collective-permute-start.8 = (f32[64,256]{1,0:T(8,128)S(1)}, f32[64,256]{1,0:T(8,128)S(1)}, u32[]{:S(2)}, u32[]{:S(2)}) collective-permute-start(f32[64,256]{1,0:T(8,128)S(1)} %get-tuple-element.21), channel_id=1, source_target_pairs={{0,12},{1,13},{2,14},{3,15},{4,8},{5,9},{6,10},{7,11},{8,4},{9,5},... | collective-permute-start | bytes 196616 | tf_op jit(solution)/shard_map/ppermute | solution.py:269
  45.6 0.0 collective-permute-start.7
  45.6 0.6 collective-permute-start.6
  46.2 2.4 %collective-permute-done.8.refs_3_ = f32[64,256]{1,0:T(8,128)S(1)} collective-permute-done((f32[64,256]{1,0:T(8,128)S(1)}, f32[64,256]{1,0:T(8,128)S(1)}, u32[]{:S(2)}, u32[]{:S(2)}) %collective-permute-start.8) | collective-permute-done | bytes 65568 | tf_op jit(solution)/shard_map/ppermute | solution.py:269
  48.6 2.3 %collective-permute-done.7.refs_2_ = f32[64,256]{1,0:T(8,128)S(1)} collective-permute-done((f32[64,256]{1,0:T(8,128)S(1)}, f32[64,256]{1,0:T(8,128)S(1)}, u32[]{:S(2)}, u32[]{:S(2)}) %collective-permute-start.7) | collective-permute-done | bytes 65568 | tf_op jit(solution)/shard_map/ppermute | solution.py:269
  50.9 0.4 collective-permute-done.6.refs_1_
  51.2 0.8 %hidden_rows.1 = (bf16[64,256]{1,0:T(8,128)(2,1)S(1)}, bf16[256,256]{1,0:T(8,128)(2,1)}) custom-call(f32[64,256]{1,0:T(8,128)S(1)} %get-tuple-element.24.refs_0_, f32[64,256]{1,0:T(8,128)S(1)} %collective-permute-done.6.refs_1_, f32[64,256]{1,0:T(8,128)S(1)} %collective-permute-done.7.refs_2_, f32[64,256]{1,0:T(8,128)S(1)} %collective-permute-done.8.refs_3_, ...), custom_call_target="tpu_custom_call" | custom-call | tf_op jit(solution)/shard_map/hidden_rows/pallas_call | solution.py:221
  52.0 3.3 %all-to-all-start = ((bf16[32,8,256]{2,1,0:T(8,128)(2,1)}), bf16[32,8,256]{2,1,0:T(8,128)(2,1)S(1)}, u32[]{:S(2)}, u32[]{:S(2)}) async-start(bf16[32,8,256]{2,1,0:T(8,128)(2,1)} %bitcast.7), calls=%async_computation | async-start | bytes 262144 | tf_op jit(solution)/shard_map/all_to_all | solution.py:325
  55.4 0.3 collective-permute-start.9
  55.7 1.0 %collective-permute-done.9.other = bf16[64,256]{1,0:T(8,128)(2,1)S(1)} collective-permute-done((bf16[64,256]{1,0:T(8,128)(2,1)S(1)}, bf16[64,256]{1,0:T(8,128)(2,1)S(1)}, u32[]{:S(2)}, u32[]{:S(2)}) %collective-permute-start.9) | collective-permute-done | bytes 32800 | tf_op jit(solution)/shard_map/ppermute | solution.py:324
  56.6 6.6 %all-to-all-done = bf16[32,8,256]{2,1,0:T(8,128)(2,1)S(1)} async-done(((bf16[32,8,256]{2,1,0:T(8,128)(2,1)}), bf16[32,8,256]{2,1,0:T(8,128)(2,1)S(1)}, u32[]{:S(2)}, u32[]{:S(2)}) %all-to-all-start) | async-done | bytes 131104 | tf_op jit(solution)/shard_map/all_to_all | solution.py:325
  63.3 0.0 copy-done
  63.3 0.0 copy-done.1
  63.3 0.0 copy-done.3
  63.3 1.5 %logits.1 = f32[64,172]{1,0:T(8,128)} custom-call(s32[2]{0:T(128)S(1)} %pad_add_fusion.ids, bf16[64,256]{1,0:T(8,128)(2,1)S(1)} %get-tuple-element.19.own, bf16[64,256]{1,0:T(8,128)(2,1)S(1)} %collective-permute-done.9.other, bf16[256,256]{1,0:T(8,128)(2,1)S(1)} %bitcast.11, bf16[64,256]{1,0:T(8,128)(2,1)S(1)} %copy-done.3, bf16[172,256]{1,0:T(8,128)(2,1)S(1)} %bitcast.12, ...), custom_call_target="tpu_custom_call" | custom-call | tf_op jit(solution)/shard_map/logits/pallas_call | solution.py:255
Async XLA Ops:
  0.0 5.7 %collective-permute-start = (bf16[1024,512]{1,0:T(8,128)(2,1)}, bf16[1024,512]{1,0:T(8,128)(2,1)S(1)}, u32[]{:S(2)}, u32[]{:S(2)}) collective-permute-start(bf16[1024,512]{1,0:T(8,128)(2,1)} %xo.1), channel_id=1, source_target_pairs={{0,16},{16,0},{1,17},{17,1},{2,18},{18,2},{3,19},{19,3},{4,20},{20... | collective-permute-start | bytes 3145736 | tf_op jit(solution)/shard_map/ppermute | solution.py:297
  0.5 5.2 %collective-permute-start.2 = (bf16[512,256]{1,0:T(8,128)(2,1)}, bf16[512,256]{1,0:T(8,128)(2,1)S(1)}, u32[]{:S(2)}, u32[]{:S(2)}) collective-permute-start(bf16[512,256]{1,0:T(8,128)(2,1)} %so.1), channel_id=1, source_target_pairs={{0,16},{16,0},{1,17},{17,1},{2,18},{18,2},{3,19},{19,3},{4,20},{20... | collective-permute-start | bytes 786440 | tf_op jit(solution)/shard_map/ppermute | solution.py:299
  0.5 5.2 %collective-permute-start.1 = (bf16[512,256]{1,0:T(8,128)(2,1)}, bf16[512,256]{1,0:T(8,128)(2,1)S(1)}, u32[]{:S(2)}, u32[]{:S(2)}) collective-permute-start(bf16[512,256]{1,0:T(8,128)(2,1)} %wo.1), channel_id=1, source_target_pairs={{0,16},{16,0},{1,17},{17,1},{2,18},{18,2},{3,19},{19,3},{4,20},{20... | collective-permute-start | bytes 786440 | tf_op jit(solution)/shard_map/ppermute | solution.py:298
  1.0 0.8 %copy-start.2 = (s32[16,16,8]{1,2,0:T(8,128)S(1)}, s32[16,16,8]{1,2,0:T(8,128)}, u32[]{:S(2)}) copy-start(s32[16,16,8]{1,2,0:T(8,128)} %param.19) | copy-start | bytes 24580
  1.9 0.7 %copy-start.4 = (s32[16,16]{1,0:T(8,128)S(1)}, s32[16,16]{1,0:T(8,128)}, u32[]{:S(2)}) copy-start(s32[16,16]{1,0:T(8,128)} %counts.1) | copy-start | bytes 3076
  2.6 0.7 %copy-start.5 = (s32[128]{0:T(128)S(1)}, s32[128]{0:T(128)}, u32[]{:S(2)}) copy-start(s32[128]{0:T(128)} %param.15) | copy-start | bytes 1540
  3.2 0.7 %copy-start.6 = (s32[128]{0:T(128)S(1)}, s32[128]{0:T(128)}, u32[]{:S(2)}) copy-start(s32[128]{0:T(128)} %param.16) | copy-start | bytes 1540
  3.9 0.7 %copy-start.7 = (s32[128]{0:T(128)S(1)}, s32[128]{0:T(128)}, u32[]{:S(2)}) copy-start(s32[128]{0:T(128)} %param.14) | copy-start | bytes 1540
  5.7 2.2 %copy-start.8 = (bf16[128,128,128]{2,1,0:T(8,128)(2,1)S(1)}, bf16[128,128,128]{2,1,0:T(8,128)(2,1)}, u32[]{:S(2)}) copy-start(bf16[128,128,128]{2,1,0:T(8,128)(2,1)} %param.13) | copy-start | bytes 12582916
  7.9 1.2 %copy-start.9 = (bf16[1024,512]{1,0:T(8,128)(2,1)S(1)}, bf16[1024,512]{1,0:T(8,128)(2,1)}, u32[]{:S(2)}) copy-start(bf16[1024,512]{1,0:T(8,128)(2,1)} %xo.1) | copy-start | bytes 3145732
  9.1 0.9 %copy-start.10 = (bf16[512,256]{1,0:T(8,128)(2,1)S(1)}, bf16[512,256]{1,0:T(8,128)(2,1)}, u32[]{:S(2)}) copy-start(bf16[512,256]{1,0:T(8,128)(2,1)} %wo.1) | copy-start | bytes 786436
  10.1 0.9 %copy-start.11 = (bf16[512,256]{1,0:T(8,128)(2,1)S(1)}, bf16[512,256]{1,0:T(8,128)(2,1)}, u32[]{:S(2)}) copy-start(bf16[512,256]{1,0:T(8,128)(2,1)} %so.1) | copy-start | bytes 786436
  11.0 52.2 %copy-start = (bf16[256,172]{0,1:T(8,128)(2,1)S(1)}, bf16[256,172]{0,1:T(8,128)(2,1)}, u32[]{:S(2)}) copy-start(bf16[256,172]{0,1:T(8,128)(2,1)} %param.22) | copy-start | bytes 264196
  11.0 52.2 %copy-start.1 = (bf16[256,172]{0,1:T(8,128)(2,1)S(1)}, bf16[256,172]{0,1:T(8,128)(2,1)}, u32[]{:S(2)}) copy-start(bf16[256,172]{0,1:T(8,128)(2,1)} %param.23) | copy-start | bytes 264196
  11.0 52.2 %copy-start.3 = (bf16[64,256]{1,0:T(8,128)(2,1)S(1)}, bf16[64,256]{1,0:T(8,128)(2,1)}, u32[]{:S(2)}) copy-start(bf16[64,256]{1,0:T(8,128)(2,1)} %adj.1) | copy-start | bytes 98308
  23.9 10.6 %collective-permute-start.3 = (f32[256,256]{1,0:T(8,128)S(1)}, f32[256,256]{1,0:T(8,128)S(1)}, u32[]{:S(2)}, u32[]{:S(2)}) collective-permute-start(f32[256,256]{1,0:T(8,128)S(1)} %get-tuple-element.15), channel_id=1, source_target_pairs={{0,1},{1,0},{2,3},{3,2},{4,5},{5,4},{6,7},{7,6},{8,9},{9,8},{10,11... | collective-permute-start | bytes 786440 | tf_op jit(solution)/shard_map/ppermute | solution.py:269
  27.3 14.0 %collective-permute-start.4 = (f32[256,256]{1,0:T(8,128)S(1)}, f32[256,256]{1,0:T(8,128)S(1)}, u32[]{:S(2)}, u32[]{:S(2)}) collective-permute-start(f32[256,256]{1,0:T(8,128)S(1)} %get-tuple-element.16), channel_id=1, source_target_pairs={{0,2},{1,3},{2,0},{3,1},{4,6},{5,7},{6,4},{7,5},{8,10},{9,11},{10,... | collective-permute-start | bytes 786440 | tf_op jit(solution)/shard_map/ppermute | solution.py:269
  27.9 13.5 %collective-permute-start.5 = (f32[256,256]{1,0:T(8,128)S(1)}, f32[256,256]{1,0:T(8,128)S(1)}, u32[]{:S(2)}, u32[]{:S(2)}) collective-permute-start(f32[256,256]{1,0:T(8,128)S(1)} %get-tuple-element.17), channel_id=1, source_target_pairs={{0,3},{1,2},{2,1},{3,0},{4,7},{5,6},{6,5},{7,4},{8,11},{9,10},{10,... | collective-permute-start | bytes 786440 | tf_op jit(solution)/shard_map/ppermute | solution.py:269
  41.4 7.1 %collective-permute-start.8 = (f32[64,256]{1,0:T(8,128)S(1)}, f32[64,256]{1,0:T(8,128)S(1)}, u32[]{:S(2)}, u32[]{:S(2)}) collective-permute-start(f32[64,256]{1,0:T(8,128)S(1)} %get-tuple-element.21), channel_id=1, source_target_pairs={{0,12},{1,13},{2,14},{3,15},{4,8},{5,9},{6,10},{7,11},{8,4},{9,5},... | collective-permute-start | bytes 196616 | tf_op jit(solution)/shard_map/ppermute | solution.py:269
  45.6 5.3 %collective-permute-start.7 = (f32[64,256]{1,0:T(8,128)S(1)}, f32[64,256]{1,0:T(8,128)S(1)}, u32[]{:S(2)}, u32[]{:S(2)}) collective-permute-start(f32[64,256]{1,0:T(8,128)S(1)} %get-tuple-element.22), channel_id=1, source_target_pairs={{0,8},{1,9},{2,10},{3,11},{4,12},{5,13},{6,14},{7,15},{8,0},{9,1},... | collective-permute-start | bytes 196616 | tf_op jit(solution)/shard_map/ppermute | solution.py:269
  45.6 5.7 %collective-permute-start.6 = (f32[64,256]{1,0:T(8,128)S(1)}, f32[64,256]{1,0:T(8,128)S(1)}, u32[]{:S(2)}, u32[]{:S(2)}) collective-permute-start(f32[64,256]{1,0:T(8,128)S(1)} %get-tuple-element.23), channel_id=1, source_target_pairs={{0,4},{1,5},{2,6},{3,7},{4,0},{5,1},{6,2},{7,3},{8,12},{9,13},{10,... | collective-permute-start | bytes 196616 | tf_op jit(solution)/shard_map/ppermute | solution.py:269
  52.0 11.2 %all-to-all-start = ((bf16[32,8,256]{2,1,0:T(8,128)(2,1)}), bf16[32,8,256]{2,1,0:T(8,128)(2,1)S(1)}, u32[]{:S(2)}, u32[]{:S(2)}) async-start(bf16[32,8,256]{2,1,0:T(8,128)(2,1)} %bitcast.7), calls=%async_computation | async-start | bytes 262144 | tf_op jit(solution)/shard_map/all_to_all | solution.py:325
  55.4 1.3 %collective-permute-start.9 = (bf16[64,256]{1,0:T(8,128)(2,1)S(1)}, bf16[64,256]{1,0:T(8,128)(2,1)S(1)}, u32[]{:S(2)}, u32[]{:S(2)}) collective-permute-start(bf16[64,256]{1,0:T(8,128)(2,1)S(1)} %get-tuple-element.19.own), channel_id=1, source_target_pairs={{0,16},{16,0},{1,17},{17,1},{2,18},{18,2},{3,19},{19,3},{4,20},{20... | collective-permute-start | bytes 98312 | tf_op jit(solution)/shard_map/ppermute | solution.py:324

commit v3 on v2

--- a/solution.py
+++ b/solution.py
@@ -9,7 +9,7 @@
 
 UNIT = 16
 BLOCK = 16
-LEAD = 3
+LEAD = 2
 CHUNKS = 1
 
 
@@ -18,17 +18,29 @@
     return pair if place % 2 == 0 else groups - 1 - pair
 
 
-def plan_kernel(chunks, per, n, radix, n_src, ids, src_v, rows_v, dst_v, lists, counts, *outs):
+def plan_kernel(chunks, per, n, radix, n_src, ids, src_h, rows_h, dst_h, lists_h, counts_h, tw, xo, wo, so, *rest):
+    tables, rest = rest[:chunks], rest[chunks:]
+    packs, rest = rest[:chunks], rest[chunks:]
+    sel, xo_out, wo_out, so_out = rest[:4]
+    src_v, rows_v, dst_v, lists, counts, tbuf, masks, table_s, sems = rest[4:]
     core, me = ids[0], ids[1]
     tiles = src_v.shape[1]
-    tables, sel = outs[:chunks], outs[chunks]
+    tile = tw.shape[3]
+    lead = LEAD * BLOCK
     n_pos = tables[0].shape[1]
     units = per * tiles
     groups = 2 * per * chunks
-    lead = LEAD * BLOCK
-    src, rows = src_v[...], rows_v[...]
-    slot = jnp.bitwise_xor(dst_v[...], me)
-    slot = jnp.bitwise_and(slot, radix - 1) * (n // radix) + lax.div(slot, radix)
+    half = groups // 2
+    gs = [group_of(core, i, groups) for i in range(half)]
+    small = [(src_h, src_v), (rows_h, rows_v), (dst_h, dst_v), (lists_h, lists), (counts_h, counts)]
+    large = [(tw.at[:, g], tbuf.at[pl.ds(i * tiles, tiles)]) for i, g in enumerate(gs)]
+    large += [(xo, xo_out), (wo, wo_out), (so, so_out)]
+    copies = [pltpu.make_async_copy(a, b, sems.at[i]) for i, (a, b) in enumerate(small + large)]
+    for c in copies:
+        c.start()
+    row_i = lax.broadcasted_iota(jnp.int32, (UNIT, tile), 0)
+    for m in range(UNIT + 1):
+        masks[m] = jnp.where(row_i < m, 1.0, 0.0).astype(jnp.bfloat16)
     lane = lax.broadcasted_iota(jnp.int32, (1, tiles), 1)
     block_i = lax.broadcasted_iota(jnp.int32, (n_src, tiles), 0)
     before = lax.broadcasted_iota(jnp.int32, (units, units), 0) < lax.broadcasted_iota(jnp.int32, (units, units), 1)
@@ -36,11 +48,16 @@
     pos_i = lax.broadcasted_iota(jnp.int32, (tiles, n_pos), 1).astype(jnp.float32)
     place_i = lax.broadcasted_iota(jnp.int32, (1, n_pos), 1)
     trash = float(n * per << 14)
+    for c in copies[:5]:
+        c.wait()
+    src, rows = src_v[...], rows_v[...]
+    slot = jnp.bitwise_xor(dst_v[...], me)
+    slot = jnp.bitwise_and(slot, radix - 1) * (n // radix) + lax.div(slot, radix)
+    to_scalar = []
     for c in range(chunks):
         hot, words, valid = [], [], []
         for j in range(per):
-            g = group_of(core, c * per + j, groups)
-            limit = jnp.clip(rows - UNIT * g, 0, UNIT)
+            limit = jnp.clip(rows - UNIT * gs[c * per + j], 0, UNIT)
             ok = limit > 0
             valid.append(ok)
             words.append(((slot * per + j) * 512 + (j * tiles + lane)) * 32 + limit)
@@ -66,6 +83,9 @@
         owner = jnp.where(place_i == n_pos - 1, run, jnp.minimum(owner, n_src - 1.0))
         tables[c][0:1, :] = word.astype(jnp.int32)
         tables[c][1:2, :] = owner.astype(jnp.int32)
+        copy = pltpu.make_async_copy(tables[c], table_s.at[c], sems.at[len(copies) + c])
+        copy.start()
+        to_scalar.append(copy)
 
     slots = lists.shape[1]
     total = n * slots
@@ -79,67 +99,92 @@
         picked = jnp.where(k_n == k, mine[k:k + 1, :], picked)
     good = jnp.logical_and(lax.div(q_n, slots) == r_n, k_n < cnt)
     row = jnp.sum(jnp.where(good, picked + 1.0, 0.0), axis=1, keepdims=True) - 1.0
-    held = groups // 2 * UNIT
-    lane = lax.broadcasted_iota(jnp.int32, (1, held), 1)
-    name = jnp.zeros((1, held), jnp.int32)
-    for i in range(groups // 2):
-        g = group_of(core, i, groups)
-        name = jnp.where(lax.div(lane, UNIT) == i, g * UNIT + jnp.bitwise_and(lane, UNIT - 1), name)
+    lane = lax.broadcasted_iota(jnp.int32, (1, half * UNIT), 1)
+    name = jnp.zeros((1, half * UNIT), jnp.int32)
+    for i in range(half):
+        name = jnp.where(lax.div(lane, UNIT) == i, gs[i] * UNIT + jnp.bitwise_and(lane, UNIT - 1), name)
     sel[...] = jnp.where(row == name.astype(jnp.float32), 1.0, 0.0).astype(jnp.bfloat16)
 
-
-def plan(chunks, per, n, radix, n_src, ids, src, rows, dst, send_list, send_count):
-    tiles = src.shape[0]
+    for c in copies[5:5 + half]:
+        c.wait()
+    for c in range(chunks):
+        to_scalar[c].wait()
+
+        def block(b, carry):
+            for k in range(BLOCK):
+                word = table_s[c, 0, lead + b * BLOCK + k]
+                u = jnp.bitwise_and(lax.shift_right_logical(word, 5), 511) + c * units
+                at = pl.multiple_of((b * BLOCK + k) * UNIT, UNIT)
+                packs[c][pl.ds(at, UNIT), :] = tbuf[u] * masks[jnp.bitwise_and(word, 31)]
+            return carry
+
+        lax.fori_loop(0, table_s[c, 1, n_pos - 1], block, 0)
+    for c in copies[5 + half:]:
+        c.wait()
+
+
+def plan(chunks, per, n, radix, ids, src, rows, dst, send_list, send_count, tw, xo, wo, so):
+    tiles, _, _, tile = tw.shape
     slots = send_list.shape[2]
-    n_pos = -(-(LEAD * BLOCK + per * tiles + (n_src + LEAD) * BLOCK) // 128) * 128
+    n_src = xo.shape[0] // tile
+    blocks = per * tiles // BLOCK + n_src + LEAD
+    n_pos = -(-((LEAD + blocks) * BLOCK + 1) // 128) * 128
     smem = pl.BlockSpec(memory_space=pltpu.SMEM)
     vmem = pl.BlockSpec(memory_space=pltpu.VMEM)
+    hbm = pl.BlockSpec(memory_space=pltpu.HBM)
+    lists = jnp.swapaxes(send_list, 1, 2)
+    half = chunks * per
     return pl.pallas_call(
         functools.partial(plan_kernel, chunks, per, n, radix, n_src),
         out_shape=[jax.ShapeDtypeStruct((2, n_pos), jnp.int32)] * chunks
-        + [jax.ShapeDtypeStruct((n * slots, chunks * per * UNIT), jnp.bfloat16)],
-        in_specs=[smem] + [vmem] * 5,
-        out_specs=[vmem] * (chunks + 1),
+        + [jax.ShapeDtypeStruct((blocks * BLOCK * UNIT, tile), tw.dtype)] * chunks
+        + [
+            jax.ShapeDtypeStruct((n * slots, half * UNIT), jnp.bfloat16),
+            jax.ShapeDtypeStruct(xo.shape, xo.dtype),
+            jax.ShapeDtypeStruct(wo.shape, wo.dtype),
+            jax.ShapeDtypeStruct(so.shape, so.dtype),
+        ],
+        in_specs=[smem] + [hbm] * 9,
+        out_specs=[vmem] * (2 * chunks + 4),
+        scratch_shapes=[
+            pltpu.VMEM((1, tiles), jnp.int32),
+            pltpu.VMEM((1, tiles), jnp.int32),
+            pltpu.VMEM((1, tiles), jnp.int32),
+            pltpu.VMEM(lists.shape, jnp.int32),
+            pltpu.VMEM(send_count.shape, jnp.int32),
+            pltpu.VMEM((half * tiles, UNIT, tile), tw.dtype),
+            pltpu.VMEM((UNIT + 1, UNIT, tile), jnp.bfloat16),
+            pltpu.SMEM((chunks, 2, n_pos), jnp.int32),
+            pltpu.SemaphoreType.DMA((5 + half + 3 + chunks,)),
+        ],
         compiler_params=pltpu.CompilerParams(vmem_limit_bytes=32 * 1024 * 1024),
         name="plan",
-    )(ids, src.reshape(1, tiles), rows.reshape(1, tiles), dst.reshape(1, tiles), jnp.swapaxes(send_list, 1, 2), send_count)
-
-
-def tiles_kernel(chunk, per, n, radix, ids, table, tw, xo, xp, wo, wp, so, sp, *rest):
+    )(ids, *[
+        pltpu.with_memory_space_constraint(a, pltpu.HBM)
+        for a in (src.reshape(1, tiles), rows.reshape(1, tiles), dst.reshape(1, tiles), lists, send_count, tw, xo, wo, so)
+    ])
+
+
+def tiles_kernel(chunk, per, n, radix, groups, ids, table, packed, xo, xp, wo, wp, so, sp, *rest):
     outs, rest = rest[:radix], rest[radix:]
-    tbuf, xbuf, wbuf, sbuf, masks, packed, gath, res, acc, sems = rest
-    tiles, groups = tw.shape[0], tw.shape[1]
-    tile = tw.shape[3]
+    wbuf, gath, res, acc, sems = rest
+    tile = packed.shape[1]
     width = xo.shape[1]
     core = ids[0]
-    gs = [group_of(core, chunk * per + j, groups) for j in range(per)]
     copies = [
-        pltpu.make_async_copy(a, b, sems.at[i])
-        for i, (a, b) in enumerate(
-            [(tw.at[:, gs[j]], tbuf.at[pl.ds(j * tiles, tiles)]) for j in range(per)]
-            + [
-                (xo, xbuf.at[:, pl.ds(0, width)]),
-                (xp, xbuf.at[:, pl.ds(width, width)]),
-                (wo, wbuf.at[pl.ds(0, width)]),
-                (wp, wbuf.at[pl.ds(width, width)]),
-                (so, sbuf.at[pl.ds(0, width)]),
-                (sp, sbuf.at[pl.ds(width, width)]),
-            ]
-        )
+        pltpu.make_async_copy(wo, wbuf.at[pl.ds(0, width)], sems.at[0]),
+        pltpu.make_async_copy(wp, wbuf.at[pl.ds(width, width)], sems.at[1]),
     ]
     for c in copies:
         c.start()
     acc[...] = jnp.zeros_like(acc)
-    row_i = lax.broadcasted_iota(jnp.int32, (UNIT, tile), 0)
-    for m in range(UNIT + 1):
-        masks[m] = jnp.where(row_i < m, 1.0, 0.0).astype(jnp.bfloat16)
-    n_blocks = table[1, table.shape[1] - 1]
+    for j in range(per):
+        at = pl.multiple_of(group_of(core, chunk * per + j, groups) * UNIT, UNIT)
+        own = jnp.dot(xo[pl.ds(at, UNIT), :], so[...], preferred_element_type=jnp.float32)
+        own = own + jnp.dot(xp[pl.ds(at, UNIT), :], sp[...], preferred_element_type=jnp.float32)
+        acc[j * UNIT:(j + 1) * UNIT, :] = own
     for c in copies:
         c.wait()
-    for j in range(per):
-        at = pl.multiple_of(gs[j] * UNIT, UNIT)
-        own = jnp.dot(xbuf[pl.ds(at, UNIT), :], sbuf[...], preferred_element_type=jnp.float32)
-        acc[j * UNIT:(j + 1) * UNIT, :] = own
 
     def step(i, carry):
         for k in range(BLOCK):
@@ -147,55 +192,48 @@
             at = pl.multiple_of(lax.shift_right_logical(word, 14) * UNIT, UNIT)
             acc[pl.ds(at, UNIT), :] += res[k * UNIT:(k + 1) * UNIT, :]
         res[...] = jnp.dot(gath[...], wbuf[...], preferred_element_type=jnp.float32)
-        s = table[1, jnp.maximum(i - 1, 0)]
-        base = pl.multiple_of(s * tile, tile)
-        for h in range(0, 2 * width, 256):
-            got = jnp.dot(packed[...], xbuf[pl.ds(base, tile), h:h + 256], preferred_element_type=jnp.float32)
-            gath[:, h:h + 256] = got.astype(jnp.bfloat16)
-        for k in range(BLOCK):
-            word = table[0, (i + LEAD) * BLOCK + k]
-            u = jnp.bitwise_and(lax.shift_right_logical(word, 5), 511)
-            packed[k * UNIT:(k + 1) * UNIT, :] = tbuf[u] * masks[jnp.bitwise_and(word, 31)]
+        base = pl.multiple_of(table[1, i] * tile, tile)
+        lhs = packed[pl.ds(pl.multiple_of(i * BLOCK * UNIT, BLOCK * UNIT), BLOCK * UNIT), :]
+        for q, x in enumerate((xo, xp)):
+            for h in range(0, width, 256):
+                got = jnp.dot(lhs, x[pl.ds(base, tile), h:h + 256], preferred_element_type=jnp.float32)
+                gath[:, q * width + h:q * width + h + 256] = got.astype(jnp.bfloat16)
         return carry
 
-    lax.fori_loop(0, n_blocks + LEAD, step, 0)
+    lax.fori_loop(0, table[1, table.shape[1] - 1] + LEAD, step, 0)
     span = n // radix * per * UNIT
-    back = [pltpu.make_async_copy(acc.at[pl.ds(k * span, span)], outs[k], sems.at[per + 6 + k]) for k in range(radix)]
+    back = [pltpu.make_async_copy(acc.at[pl.ds(k * span, span)], outs[k], sems.at[2 + k]) for k in range(radix)]
     for c in back:
         c.start()
     for c in back:
         c.wait()
 
 
-def neighbour_terms(chunk, per, n, radix, ids, table, tw, xo, xp, wo, wp, so, sp):
-    tiles, groups, _, tile = tw.shape
-    units = per * tiles
+def neighbour_terms(chunk, per, n, radix, groups, ids, table, packed, xo, xp, wo, wp, so, sp):
     hidden = wo.shape[1]
-    rows, width = xo.shape
+    width = xo.shape[1]
+    tile = packed.shape[1]
     smem = pl.BlockSpec(memory_space=pltpu.SMEM)
+    vmem = pl.BlockSpec(memory_space=pltpu.VMEM)
     anym = pl.BlockSpec(memory_space=pl.ANY)
-    flops = 2 * units * UNIT * (tile * 2 * width + 2 * width * hidden)
+    flops = 2 * packed.shape[0] * (tile * 2 * width + 2 * width * hidden)
+    sums = (n * per + 1) * UNIT * hidden * 4
     return pl.pallas_call(
-        functools.partial(tiles_kernel, chunk, per, n, radix),
+        functools.partial(tiles_kernel, chunk, per, n, radix, groups),
         out_shape=[jax.ShapeDtypeStruct((n // radix * per * UNIT, hidden), jnp.float32)] * radix,
-        in_specs=[smem] * 2 + [anym] * 7,
+        in_specs=[smem] * 2 + [vmem] * 7,
         out_specs=[anym] * radix,
         scratch_shapes=[
-            pltpu.VMEM((units, UNIT, tile), tw.dtype),
-            pltpu.VMEM((rows, 2 * width), xo.dtype),
             pltpu.VMEM((2 * width, hidden), wo.dtype),
-            pltpu.VMEM((2 * width, hidden), so.dtype),
-            pltpu.VMEM((UNIT + 1, UNIT, tile), jnp.bfloat16),
-            pltpu.VMEM((BLOCK * UNIT, tile), jnp.bfloat16),
             pltpu.VMEM((BLOCK * UNIT, 2 * width), jnp.bfloat16),
             pltpu.VMEM((BLOCK * UNIT, hidden), jnp.float32),
             pltpu.VMEM(((n * per + 1) * UNIT, hidden), jnp.float32),
-            pltpu.SemaphoreType.DMA((per + 6 + radix,)),
+            pltpu.SemaphoreType.DMA((2 + radix,)),
         ],
-        compiler_params=pltpu.CompilerParams(vmem_limit_bytes=40 * 1024 * 1024),
+        compiler_params=pltpu.CompilerParams(vmem_limit_bytes=(16 << 20) + sums),
         cost_estimate=pl.CostEstimate(flops=flops, bytes_accessed=8 << 20, transcendentals=0),
         name="neighbour_terms",
-    )(ids, table, tw, xo, xp, wo, wp, so, sp)
+    )(ids, table, packed, xo, xp, wo, wp, so, sp)
 
 
 def hidden_kernel(chunks, parts, *refs):
@@ -298,12 +336,14 @@
     wp = lax.ppermute(neighbour_weight_first, "feat", swap)
     sp = lax.ppermute(w_self1, "feat", swap)
     tw = tile_weight.reshape(tile_weight.shape[0], groups, UNIT, tile)
-    *tables, sel = plan(CHUNKS, per, n, 4, features.shape[0] // tile, ids, tile_src, tile_rows, tile_dst, send_list, send_count)
+    planned = plan(
+        CHUNKS, per, n, 4, ids, tile_src, tile_rows, tile_dst, send_list, send_count, tw, features,
+        neighbour_weight_first, w_self1,
+    )
+    tables, packs, (sel, xo, wo, so) = planned[:CHUNKS], planned[CHUNKS:2 * CHUNKS], planned[2 * CHUNKS:]
     done = []
     for chunk in range(CHUNKS):
-        parts = neighbour_terms(
-            chunk, per, n, 4, ids, tables[chunk], tw, features, xp, neighbour_weight_first, wp, w_self1, sp,
-        )
+        parts = neighbour_terms(chunk, per, n, 4, groups, ids, tables[chunk], packs[chunk], xo, xp, wo, wp, so, sp)
         got = exchange(parts, 1, n)
         stride = 4
         left = n // 4

time: 64.8 us -> 58 us (0.90)
  local copies, waits for them, and re-layouts: 8.82 us -> 0.02 us
  Pallas kernels: 16.2 us -> 19.2 us
  starting transfers between devices: 14.4 us -> 13.3 us
    unnamed x24 -> x6, local copies, waits for them, and re-layouts: 8.82 us -> 0.02 us
    pallas_call x1, Pallas kernels: 1.14 us -> 4.53 us  [plan(): pl.pallas_call(functools.partial(plan_kernel, chunks, per, n, radix, n_sr...]
    ppermute x6, starting transfers between devices: 9.79 us -> 8.59 us  [exchange(): lax.ppermute(parts[k], 'dom', [(i, i ^ k * stride) for i in range(n)])]
  transfers between devices with their start and end apart: 11 -> 11, of which waited for: 7 -> 6; matrix products, arithmetic and copies ran while one was open for 0% -> 0% of each run, Pallas kernels for 2% -> 8%
where the time goes in v3:
time: 58 us; the launch traced here: 57.9 us
  waiting for transfers between devices  25.2 us (43%)
  Pallas kernels  19.2 us (33%)
  starting transfers between devices  13.3 us (23%)
    ppermute x6, waiting for transfers between devices, exchange(): lax.ppermute(parts[k], 'dom', [(i, i ^ k * stride) for i in range(n)])  17.6 us
    pallas_call x1, Pallas kernels, neighbour_terms(): pl.pallas_call(functools.partial(tiles_kernel, chunk, per, n, radix, grou...  12.3 us
    ppermute x6, starting transfers between devices, exchange(): lax.ppermute(parts[k], 'dom', [(i, i ^ k * stride) for i in range(n)])  8.59 us
    all_to_all x1, waiting for transfers between devices, body(): received = lax.all_to_all(send, ('feat', 'dom'), 0, 0, tiled=True)  6.64 us
    pallas_call x1, Pallas kernels, plan(): pl.pallas_call(functools.partial(plan_kernel, chunks, per, n, radix, n_sr...  4.53 us
    all_to_all x1, starting transfers between devices, body(): received = lax.all_to_all(send, ('feat', 'dom'), 0, 0, tiled=True)  3.46 us
    pallas_call x1, Pallas kernels, logits_of(): pl.pallas_call(functools.partial(logits_kernel, tile, places), out_shape=...  1.47 us
  transfers between devices with their start and end apart: 11, of which 6 were waited for; matrix products, arithmetic and copies ran while one was open for 0% of the time, Pallas kernels for 8%

profile of v3, /device:TPU:0, one launch (start us, length us, event | category | flops | bytes accessed | tf_op | source)
XLA Modules:
  0.0 57.9 jit_solution(18430567410977297072)
XLA Ops:
  0.0 0.5 collective-permute-start
  0.5 0.1 collective-permute-start.2
  0.5 0.5 collective-permute-start.1
  1.0 0.1 pad_add_fusion.ids
  1.0 4.5 %plan.1 = (s32[2,768]{1,0:T(2,128)S(1)}, bf16[10752,128]{1,0:T(8,128)(2,1)S(1)}, bf16[128,64]{1,0:T(8,128)(2,1)S(1)}, bf16[1024,512]{1,0:T(8,128)(2,1)S(1)}, bf1...) custom-call(s32[2]{0:T(128)S(1)} %pad_add_fusion.ids, s32[1,128]{1,0:T(1,128)} %bitcast.16, s32[1,128]{1,0:T(1,128)} %bitcast.17, ...), custom_call_target="tpu_custom_call" | custom-call | tf_op jit(solution)/shard_map/plan/pallas_call | solution.py:137
  5.6 0.0 collective-permute-done.2.sp
  5.6 0.0 collective-permute-done.1.wp
  5.6 0.0 collective-permute-done.xp
  5.6 0.0 copy-start
  5.6 0.0 copy-start.1
  5.6 0.0 copy-start.2
  5.6 12.3 %neighbour_terms.1 = (f32[256,256]{1,0:T(8,128)S(1)}, f32[256,256]{1,0:T(8,128)S(1)}, f32[256,256]{1,0:T(8,128)S(1)}, f32[256,256]{1,0:T(8,128)S(1)}) custom-call(s32[2]{0:T(128)S(1)} %pad_add_fusion.ids, s32[2,768]{1,0:T(2,128)S(1)} %get-tuple-element.17.table, bf16[10752,128]{1,0:T(8,128)(2,1)S(1)} %get-tuple-element.18.packed, ...), custom_call_target="tpu_custom_call" | custom-call | flops 8455716864 | bytes 8388608 | tf_op jit(solution)/shard_map/neighbour_terms/pallas_call | solution.py:221
  18.0 1.5 %collective-permute-start.3 = (f32[256,256]{1,0:T(8,128)S(1)}, f32[256,256]{1,0:T(8,128)S(1)}, u32[]{:S(2)}, u32[]{:S(2)}) collective-permute-start(f32[256,256]{1,0:T(8,128)S(1)} %get-tuple-element.23), channel_id=1, source_target_pairs={{0,1},{1,0},{2,3},{3,2},{4,5},{5,4},{6,7},{7,6},{8,9},{9,8},{10,11... | collective-permute-start | bytes 786440 | tf_op jit(solution)/shard_map/ppermute | solution.py:307
  19.5 2.6 %collective-permute-start.4 = (f32[256,256]{1,0:T(8,128)S(1)}, f32[256,256]{1,0:T(8,128)S(1)}, u32[]{:S(2)}, u32[]{:S(2)}) collective-permute-start(f32[256,256]{1,0:T(8,128)S(1)} %get-tuple-element.24), channel_id=1, source_target_pairs={{0,2},{1,3},{2,0},{3,1},{4,6},{5,7},{6,4},{7,5},{8,10},{9,11},{10,... | collective-permute-start | bytes 786440 | tf_op jit(solution)/shard_map/ppermute | solution.py:307
  22.1 0.0 collective-permute-start.5
  22.1 5.2 %collective-permute-done.3 = f32[256,256]{1,0:T(8,128)S(1)} collective-permute-done((f32[256,256]{1,0:T(8,128)S(1)}, f32[256,256]{1,0:T(8,128)S(1)}, u32[]{:S(2)}, u32[]{:S(2)}) %collective-permute-start.3) | collective-permute-done | bytes 262176 | tf_op jit(solution)/shard_map/ppermute | solution.py:307
  27.2 7.2 %collective-permute-done.4 = f32[256,256]{1,0:T(8,128)S(1)} collective-permute-done((f32[256,256]{1,0:T(8,128)S(1)}, f32[256,256]{1,0:T(8,128)S(1)}, u32[]{:S(2)}, u32[]{:S(2)}) %collective-permute-start.4) | collective-permute-done | bytes 262176 | tf_op jit(solution)/shard_map/ppermute | solution.py:307
  34.4 0.0 collective-permute-done.5
  34.4 0.1 slice_add_fusion
  34.5 3.9 %collective-permute-start.8 = (f32[64,256]{1,0:T(8,128)S(1)}, f32[64,256]{1,0:T(8,128)S(1)}, u32[]{:S(2)}, u32[]{:S(2)}) collective-permute-start(f32[64,256]{1,0:T(8,128)S(1)} %get-tuple-element.29), channel_id=1, source_target_pairs={{0,12},{1,13},{2,14},{3,15},{4,8},{5,9},{6,10},{7,11},{8,4},{9,5},... | collective-permute-start | bytes 196616 | tf_op jit(solution)/shard_map/ppermute | solution.py:307
  38.3 0.0 collective-permute-start.7
  38.3 0.6 %collective-permute-start.6 = (f32[64,256]{1,0:T(8,128)S(1)}, f32[64,256]{1,0:T(8,128)S(1)}, u32[]{:S(2)}, u32[]{:S(2)}) collective-permute-start(f32[64,256]{1,0:T(8,128)S(1)} %get-tuple-element.31), channel_id=1, source_target_pairs={{0,4},{1,5},{2,6},{3,7},{4,0},{5,1},{6,2},{7,3},{8,12},{9,13},{10,... | collective-permute-start | bytes 196616 | tf_op jit(solution)/shard_map/ppermute | solution.py:307
  39.0 2.3 %collective-permute-done.8.refs_3_ = f32[64,256]{1,0:T(8,128)S(1)} collective-permute-done((f32[64,256]{1,0:T(8,128)S(1)}, f32[64,256]{1,0:T(8,128)S(1)}, u32[]{:S(2)}, u32[]{:S(2)}) %collective-permute-start.8) | collective-permute-done | bytes 65568 | tf_op jit(solution)/shard_map/ppermute | solution.py:307
  41.3 2.9 %collective-permute-done.7.refs_2_ = f32[64,256]{1,0:T(8,128)S(1)} collective-permute-done((f32[64,256]{1,0:T(8,128)S(1)}, f32[64,256]{1,0:T(8,128)S(1)}, u32[]{:S(2)}, u32[]{:S(2)}) %collective-permute-start.7) | collective-permute-done | bytes 65568 | tf_op jit(solution)/shard_map/ppermute | solution.py:307
  44.2 0.0 collective-permute-done.6.refs_1_
  44.2 0.8 %hidden_rows.1 = (bf16[64,256]{1,0:T(8,128)(2,1)S(1)}, bf16[256,256]{1,0:T(8,128)(2,1)}) custom-call(f32[64,256]{1,0:T(8,128)S(1)} %get-tuple-element.32.refs_0_, f32[64,256]{1,0:T(8,128)S(1)} %collective-permute-done.6.refs_1_, f32[64,256]{1,0:T(8,128)S(1)} %collective-permute-done.7.refs_2_, f32[64,256]{1,0:T(8,128)S(1)} %collective-permute-done.8.refs_3_, ...), custom_call_target="tpu_custom_call" | custom-call | tf_op jit(solution)/shard_map/hidden_rows/pallas_call | solution.py:259
  45.1 3.5 %all-to-all-start = ((bf16[32,8,256]{2,1,0:T(8,128)(2,1)}), bf16[32,8,256]{2,1,0:T(8,128)(2,1)S(1)}, u32[]{:S(2)}, u32[]{:S(2)}) async-start(bf16[32,8,256]{2,1,0:T(8,128)(2,1)} %bitcast.7), calls=%async_computation | async-start | bytes 262144 | tf_op jit(solution)/shard_map/all_to_all | solution.py:365
  48.5 0.3 collective-permute-start.9
  48.8 1.0 %collective-permute-done.9.other = bf16[64,256]{1,0:T(8,128)(2,1)S(1)} collective-permute-done((bf16[64,256]{1,0:T(8,128)(2,1)S(1)}, bf16[64,256]{1,0:T(8,128)(2,1)S(1)}, u32[]{:S(2)}, u32[]{:S(2)}) %collective-permute-start.9) | collective-permute-done | bytes 32800 | tf_op jit(solution)/shard_map/ppermute | solution.py:364
  49.8 6.6 %all-to-all-done = bf16[32,8,256]{2,1,0:T(8,128)(2,1)S(1)} async-done(((bf16[32,8,256]{2,1,0:T(8,128)(2,1)}), bf16[32,8,256]{2,1,0:T(8,128)(2,1)S(1)}, u32[]{:S(2)}, u32[]{:S(2)}) %all-to-all-start) | async-done | bytes 131104 | tf_op jit(solution)/shard_map/all_to_all | solution.py:365
  56.4 0.0 copy-done
  56.4 0.0 copy-done.1
  56.4 0.0 copy-done.2
  56.4 1.5 %logits.1 = f32[64,172]{1,0:T(8,128)} custom-call(s32[2]{0:T(128)S(1)} %pad_add_fusion.ids, bf16[64,256]{1,0:T(8,128)(2,1)S(1)} %get-tuple-element.27.own, bf16[64,256]{1,0:T(8,128)(2,1)S(1)} %collective-permute-done.9.other, bf16[256,256]{1,0:T(8,128)(2,1)S(1)} %bitcast.11, bf16[64,256]{1,0:T(8,128)(2,1)S(1)} %copy-done.2, bf16[172,256]{1,0:T(8,128)(2,1)S(1)} %bitcast.12, ...), custom_call_target="tpu_custom_call" | custom-call | tf_op jit(solution)/shard_map/logits/pallas_call | solution.py:293
Async XLA Ops:
  0.0 5.6 %collective-permute-start = (bf16[1024,512]{1,0:T(8,128)(2,1)}, bf16[1024,512]{1,0:T(8,128)(2,1)S(1)}, u32[]{:S(2)}, u32[]{:S(2)}) collective-permute-start(bf16[1024,512]{1,0:T(8,128)(2,1)} %xo.1), channel_id=1, source_target_pairs={{0,16},{16,0},{1,17},{17,1},{2,18},{18,2},{3,19},{19,3},{4,20},{20... | collective-permute-start | bytes 3145736 | tf_op jit(solution)/shard_map/ppermute | solution.py:335
  0.5 5.1 %collective-permute-start.2 = (bf16[512,256]{1,0:T(8,128)(2,1)}, bf16[512,256]{1,0:T(8,128)(2,1)S(1)}, u32[]{:S(2)}, u32[]{:S(2)}) collective-permute-start(bf16[512,256]{1,0:T(8,128)(2,1)} %so.1), channel_id=1, source_target_pairs={{0,16},{16,0},{1,17},{17,1},{2,18},{18,2},{3,19},{19,3},{4,20},{20... | collective-permute-start | bytes 786440 | tf_op jit(solution)/shard_map/ppermute | solution.py:337
  0.5 5.1 %collective-permute-start.1 = (bf16[512,256]{1,0:T(8,128)(2,1)}, bf16[512,256]{1,0:T(8,128)(2,1)S(1)}, u32[]{:S(2)}, u32[]{:S(2)}) collective-permute-start(bf16[512,256]{1,0:T(8,128)(2,1)} %wo.1), channel_id=1, source_target_pairs={{0,16},{16,0},{1,17},{17,1},{2,18},{18,2},{3,19},{19,3},{4,20},{20... | collective-permute-start | bytes 786440 | tf_op jit(solution)/shard_map/ppermute | solution.py:336
  5.6 50.8 %copy-start = (bf16[256,172]{0,1:T(8,128)(2,1)S(1)}, bf16[256,172]{0,1:T(8,128)(2,1)}, u32[]{:S(2)}) copy-start(bf16[256,172]{0,1:T(8,128)(2,1)} %param.22) | copy-start | bytes 264196
  5.6 50.8 %copy-start.1 = (bf16[256,172]{0,1:T(8,128)(2,1)S(1)}, bf16[256,172]{0,1:T(8,128)(2,1)}, u32[]{:S(2)}) copy-start(bf16[256,172]{0,1:T(8,128)(2,1)} %param.23) | copy-start | bytes 264196
  5.6 50.8 %copy-start.2 = (bf16[64,256]{1,0:T(8,128)(2,1)S(1)}, bf16[64,256]{1,0:T(8,128)(2,1)}, u32[]{:S(2)}) copy-start(bf16[64,256]{1,0:T(8,128)(2,1)} %adj.1) | copy-start | bytes 98308
  18.0 9.2 %collective-permute-start.3 = (f32[256,256]{1,0:T(8,128)S(1)}, f32[256,256]{1,0:T(8,128)S(1)}, u32[]{:S(2)}, u32[]{:S(2)}) collective-permute-start(f32[256,256]{1,0:T(8,128)S(1)} %get-tuple-element.23), channel_id=1, source_target_pairs={{0,1},{1,0},{2,3},{3,2},{4,5},{5,4},{6,7},{7,6},{8,9},{9,8},{10,11... | collective-permute-start | bytes 786440 | tf_op jit(solution)/shard_map/ppermute | solution.py:307
  19.5 14.9 %collective-permute-start.4 = (f32[256,256]{1,0:T(8,128)S(1)}, f32[256,256]{1,0:T(8,128)S(1)}, u32[]{:S(2)}, u32[]{:S(2)}) collective-permute-start(f32[256,256]{1,0:T(8,128)S(1)} %get-tuple-element.24), channel_id=1, source_target_pairs={{0,2},{1,3},{2,0},{3,1},{4,6},{5,7},{6,4},{7,5},{8,10},{9,11},{10,... | collective-permute-start | bytes 786440 | tf_op jit(solution)/shard_map/ppermute | solution.py:307
  22.1 12.3 %collective-permute-start.5 = (f32[256,256]{1,0:T(8,128)S(1)}, f32[256,256]{1,0:T(8,128)S(1)}, u32[]{:S(2)}, u32[]{:S(2)}) collective-permute-start(f32[256,256]{1,0:T(8,128)S(1)} %get-tuple-element.25), channel_id=1, source_target_pairs={{0,3},{1,2},{2,1},{3,0},{4,7},{5,6},{6,5},{7,4},{8,11},{9,10},{10,... | collective-permute-start | bytes 786440 | tf_op jit(solution)/shard_map/ppermute | solution.py:307
  34.5 6.8 %collective-permute-start.8 = (f32[64,256]{1,0:T(8,128)S(1)}, f32[64,256]{1,0:T(8,128)S(1)}, u32[]{:S(2)}, u32[]{:S(2)}) collective-permute-start(f32[64,256]{1,0:T(8,128)S(1)} %get-tuple-element.29), channel_id=1, source_target_pairs={{0,12},{1,13},{2,14},{3,15},{4,8},{5,9},{6,10},{7,11},{8,4},{9,5},... | collective-permute-start | bytes 196616 | tf_op jit(solution)/shard_map/ppermute | solution.py:307
  38.3 5.9 %collective-permute-start.7 = (f32[64,256]{1,0:T(8,128)S(1)}, f32[64,256]{1,0:T(8,128)S(1)}, u32[]{:S(2)}, u32[]{:S(2)}) collective-permute-start(f32[64,256]{1,0:T(8,128)S(1)} %get-tuple-element.30), channel_id=1, source_target_pairs={{0,8},{1,9},{2,10},{3,11},{4,12},{5,13},{6,14},{7,15},{8,0},{9,1},... | collective-permute-start | bytes 196616 | tf_op jit(solution)/shard_map/ppermute | solution.py:307
  38.3 5.9 %collective-permute-start.6 = (f32[64,256]{1,0:T(8,128)S(1)}, f32[64,256]{1,0:T(8,128)S(1)}, u32[]{:S(2)}, u32[]{:S(2)}) collective-permute-start(f32[64,256]{1,0:T(8,128)S(1)} %get-tuple-element.31), channel_id=1, source_target_pairs={{0,4},{1,5},{2,6},{3,7},{4,0},{5,1},{6,2},{7,3},{8,12},{9,13},{10,... | collective-permute-start | bytes 196616 | tf_op jit(solution)/shard_map/ppermute | solution.py:307
  45.1 11.4 %all-to-all-start = ((bf16[32,8,256]{2,1,0:T(8,128)(2,1)}), bf16[32,8,256]{2,1,0:T(8,128)(2,1)S(1)}, u32[]{:S(2)}, u32[]{:S(2)}) async-start(bf16[32,8,256]{2,1,0:T(8,128)(2,1)} %bitcast.7), calls=%async_computation | async-start | bytes 262144 | tf_op jit(solution)/shard_map/all_to_all | solution.py:365
  48.5 1.3 %collective-permute-start.9 = (bf16[64,256]{1,0:T(8,128)(2,1)S(1)}, bf16[64,256]{1,0:T(8,128)(2,1)S(1)}, u32[]{:S(2)}, u32[]{:S(2)}) collective-permute-start(bf16[64,256]{1,0:T(8,128)(2,1)S(1)} %get-tuple-element.27.own), channel_id=1, source_target_pairs={{0,16},{16,0},{1,17},{17,1},{2,18},{18,2},{3,19},{19,3},{4,20},{20... | collective-permute-start | bytes 98312 | tf_op jit(solution)/shard_map/ppermute | solution.py:364

commit v4 on v3

--- a/solution.py
+++ b/solution.py
@@ -8,7 +8,8 @@
 from jax.sharding import PartitionSpec as P
 
 UNIT = 16
-BLOCK = 16
+BLOCK = 8
+STEP = 4
 LEAD = 2
 CHUNKS = 1
 
@@ -26,7 +27,7 @@
     core, me = ids[0], ids[1]
     tiles = src_v.shape[1]
     tile = tw.shape[3]
-    lead = LEAD * BLOCK
+    lead = LEAD * STEP * BLOCK
     n_pos = tables[0].shape[1]
     units = per * tiles
     groups = 2 * per * chunks
@@ -99,11 +100,8 @@
         picked = jnp.where(k_n == k, mine[k:k + 1, :], picked)
     good = jnp.logical_and(lax.div(q_n, slots) == r_n, k_n < cnt)
     row = jnp.sum(jnp.where(good, picked + 1.0, 0.0), axis=1, keepdims=True) - 1.0
-    lane = lax.broadcasted_iota(jnp.int32, (1, half * UNIT), 1)
-    name = jnp.zeros((1, half * UNIT), jnp.int32)
-    for i in range(half):
-        name = jnp.where(lax.div(lane, UNIT) == i, gs[i] * UNIT + jnp.bitwise_and(lane, UNIT - 1), name)
-    sel[...] = jnp.where(row == name.astype(jnp.float32), 1.0, 0.0).astype(jnp.bfloat16)
+    lane = lax.broadcasted_iota(jnp.int32, (1, sel.shape[1]), 1).astype(jnp.float32)
+    sel[...] = jnp.where(row == lane, 1.0, 0.0).astype(jnp.bfloat16)
 
     for c in copies[5:5 + half]:
         c.wait()
@@ -127,8 +125,8 @@
     tiles, _, _, tile = tw.shape
     slots = send_list.shape[2]
     n_src = xo.shape[0] // tile
-    blocks = per * tiles // BLOCK + n_src + LEAD
-    n_pos = -(-((LEAD + blocks) * BLOCK + 1) // 128) * 128
+    blocks = -(-(per * tiles // BLOCK + n_src) // STEP + -LEAD) * STEP
+    n_pos = -(-((LEAD * STEP + blocks) * BLOCK + 1) // 128) * 128
     smem = pl.BlockSpec(memory_space=pltpu.SMEM)
     vmem = pl.BlockSpec(memory_space=pltpu.VMEM)
     hbm = pl.BlockSpec(memory_space=pltpu.HBM)
@@ -139,7 +137,7 @@
         out_shape=[jax.ShapeDtypeStruct((2, n_pos), jnp.int32)] * chunks
         + [jax.ShapeDtypeStruct((blocks * BLOCK * UNIT, tile), tw.dtype)] * chunks
         + [
-            jax.ShapeDtypeStruct((n * slots, half * UNIT), jnp.bfloat16),
+            jax.ShapeDtypeStruct((n * slots, 2 * half * UNIT), jnp.bfloat16),
             jax.ShapeDtypeStruct(xo.shape, xo.dtype),
             jax.ShapeDtypeStruct(wo.shape, wo.dtype),
             jax.ShapeDtypeStruct(so.shape, so.dtype),
@@ -186,21 +184,25 @@
     for c in copies:
         c.wait()
 
+    size = BLOCK * UNIT
+
     def step(i, carry):
-        for k in range(BLOCK):
-            word = table[0, i * BLOCK + k]
+        for k in range(STEP * BLOCK):
+            word = table[0, i * (STEP * BLOCK) + k]
             at = pl.multiple_of(lax.shift_right_logical(word, 14) * UNIT, UNIT)
             acc[pl.ds(at, UNIT), :] += res[k * UNIT:(k + 1) * UNIT, :]
         res[...] = jnp.dot(gath[...], wbuf[...], preferred_element_type=jnp.float32)
-        base = pl.multiple_of(table[1, i] * tile, tile)
-        lhs = packed[pl.ds(pl.multiple_of(i * BLOCK * UNIT, BLOCK * UNIT), BLOCK * UNIT), :]
-        for q, x in enumerate((xo, xp)):
-            for h in range(0, width, 256):
-                got = jnp.dot(lhs, x[pl.ds(base, tile), h:h + 256], preferred_element_type=jnp.float32)
-                gath[:, q * width + h:q * width + h + 256] = got.astype(jnp.bfloat16)
+        for m in range(STEP):
+            base = pl.multiple_of(table[1, i * STEP + m] * tile, tile)
+            lhs = packed[pl.ds(pl.multiple_of((i * STEP + m) * size, size), size), :]
+            for q, x in enumerate((xo, xp)):
+                for h in range(0, width, 256):
+                    got = jnp.dot(lhs, x[pl.ds(base, tile), h:h + 256], preferred_element_type=jnp.float32)
+                    gath[m * size:(m + 1) * size, q * width + h:q * width + h + 256] = got.astype(jnp.bfloat16)
         return carry
 
-    lax.fori_loop(0, table[1, table.shape[1] - 1] + LEAD, step, 0)
+    steps = lax.div(table[1, table.shape[1] - 1] + STEP - 1, STEP)
+    lax.fori_loop(0, steps + LEAD, step, 0)
     span = n // radix * per * UNIT
     back = [pltpu.make_async_copy(acc.at[pl.ds(k * span, span)], outs[k], sems.at[2 + k]) for k in range(radix)]
     for c in back:
@@ -225,8 +227,8 @@
         out_specs=[anym] * radix,
         scratch_shapes=[
             pltpu.VMEM((2 * width, hidden), wo.dtype),
-            pltpu.VMEM((BLOCK * UNIT, 2 * width), jnp.bfloat16),
-            pltpu.VMEM((BLOCK * UNIT, hidden), jnp.float32),
+            pltpu.VMEM((STEP * BLOCK * UNIT, 2 * width), jnp.bfloat16),
+            pltpu.VMEM((STEP * BLOCK * UNIT, hidden), jnp.float32),
             pltpu.VMEM(((n * per + 1) * UNIT, hidden), jnp.float32),
             pltpu.SemaphoreType.DMA((2 + radix,)),
         ],
@@ -237,68 +239,77 @@
 
 
 def hidden_kernel(chunks, parts, *refs):
-    sel, (own, send) = refs[chunks * parts], refs[chunks * parts + 1:]
+    own = refs[chunks * parts]
     rows = refs[0].shape[0]
     for c in range(chunks):
         total = refs[c * parts][...]
         for k in range(1, parts):
             total = total + refs[c * parts + k][...]
         own[c * rows:(c + 1) * rows, :] = jnp.maximum(total, 0.0).astype(jnp.bfloat16)
-    picked = jnp.dot(sel[...], own[...], preferred_element_type=jnp.float32).astype(jnp.bfloat16)
-    half = picked.shape[0]
-    send[:half, :] = picked
-    send[half:, :] = picked
-
-
-def hidden_rows(chunk_parts, sel):
+
+
+def hidden_rows(chunk_parts):
     chunks, parts = len(chunk_parts), len(chunk_parts[0])
-    held = sel.shape[1]
-    width = chunk_parts[0][0].shape[1]
+    rows, width = chunk_parts[0][0].shape
     vmem = pl.BlockSpec(memory_space=pltpu.VMEM)
     flat = [a for part in chunk_parts for a in part]
     return pl.pallas_call(
         functools.partial(hidden_kernel, chunks, parts),
+        out_shape=jax.ShapeDtypeStruct((chunks * rows, width), jnp.bfloat16),
+        in_specs=[vmem] * len(flat),
+        out_specs=vmem,
+        compiler_params=pltpu.CompilerParams(vmem_limit_bytes=32 * 1024 * 1024),
+        name="hidden_rows",
+    )(*flat)
+
+
+def send_kernel(groups, ids, own, other, sel, hidden, send):
+    core = ids[0]
+    for i in range(groups // 2):
+        mine = group_of(core, i, groups)
+        theirs = group_of(1 - core, i, groups)
+        hidden[pl.ds(pl.multiple_of(mine * UNIT, UNIT), UNIT), :] = own[i * UNIT:(i + 1) * UNIT, :]
+        hidden[pl.ds(pl.multiple_of(theirs * UNIT, UNIT), UNIT), :] = other[i * UNIT:(i + 1) * UNIT, :]
+    send[...] = jnp.dot(sel[...], hidden[...], preferred_element_type=jnp.float32).astype(jnp.bfloat16)
+
+
+def rows_to_send(groups, ids, own, other, sel):
+    smem = pl.BlockSpec(memory_space=pltpu.SMEM)
+    vmem = pl.BlockSpec(memory_space=pltpu.VMEM)
+    width = own.shape[1]
+    return pl.pallas_call(
+        functools.partial(send_kernel, groups),
         out_shape=[
-            jax.ShapeDtypeStruct((held, width), jnp.bfloat16),
-            jax.ShapeDtypeStruct((2 * sel.shape[0], width), jnp.bfloat16),
+            jax.ShapeDtypeStruct((groups * UNIT, width), jnp.bfloat16),
+            jax.ShapeDtypeStruct((sel.shape[0], width), jnp.bfloat16),
         ],
-        in_specs=[vmem] * (len(flat) + 1),
+        in_specs=[smem] + [vmem] * 3,
         out_specs=[vmem] * 2,
         compiler_params=pltpu.CompilerParams(vmem_limit_bytes=32 * 1024 * 1024),
-        name="hidden_rows",
-    )(*flat, sel)
-
-
-def logits_kernel(tile, places, ids, own, other, received, adj, w_self, w_neigh, out, pool):
-    core = ids[0]
-    groups = tile // UNIT
-    for i, place in enumerate(places):
-        mine = group_of(core, place, groups)
-        theirs = group_of(1 - core, place, groups)
-        pool[pl.ds(pl.multiple_of(mine * UNIT, UNIT), UNIT), :] = own[i * UNIT:(i + 1) * UNIT, :]
-        pool[pl.ds(pl.multiple_of(theirs * UNIT, UNIT), UNIT), :] = other[i * UNIT:(i + 1) * UNIT, :]
-    half = received.shape[0] // 2
-    both = received[:half, :].astype(jnp.float32) + received[half:, :].astype(jnp.float32)
-    pool[tile:, :] = both.astype(jnp.bfloat16)
-    mean = jnp.dot(adj[...], pool[...], preferred_element_type=jnp.float32).astype(jnp.bfloat16)
+        name="rows_to_send",
+    )(ids, own, other, sel)
+
+
+def logits_kernel(hidden, received, adj, w_self, w_neigh, out):
+    tile, rows = hidden.shape[0], adj.shape[0]
+    mean = jnp.dot(adj[:, :tile], hidden[...], preferred_element_type=jnp.float32)
+    mean = mean + jnp.dot(adj[:, tile:], received[...], preferred_element_type=jnp.float32)
     dims = (((1,), (1,)), ((), ()))
-    rows = adj.shape[0]
-    got = lax.dot_general(pool[:rows, :], w_self[...], dims, preferred_element_type=jnp.float32)
-    out[...] = got + lax.dot_general(mean, w_neigh[...], dims, preferred_element_type=jnp.float32)
-
-
-def logits_of(ids, own, other, received, adj, w_self, w_neigh, tile, places):
-    smem = pl.BlockSpec(memory_space=pltpu.SMEM)
-    vmem = pl.BlockSpec(memory_space=pltpu.VMEM)
-    return pl.pallas_call(
-        functools.partial(logits_kernel, tile, places),
+    got = lax.dot_general(hidden[:rows, :], w_self[...], dims, preferred_element_type=jnp.float32)
+    got = got + lax.dot_general(mean.astype(jnp.bfloat16), w_neigh[...], dims, preferred_element_type=jnp.float32)
+    out[...] = got
+
+
+def logits_of(hidden, received, adj, w_self, w_neigh):
+    vmem = pl.BlockSpec(memory_space=pltpu.VMEM)
+    return pl.pallas_call(
+        logits_kernel,
         out_shape=jax.ShapeDtypeStruct((adj.shape[0], w_self.shape[1]), jnp.float32),
-        in_specs=[smem] + [vmem] * 6,
+        in_specs=[vmem] * 5,
         out_specs=vmem,
-        scratch_shapes=[pltpu.VMEM((adj.shape[1], own.shape[1]), jnp.bfloat16)],
         compiler_params=pltpu.CompilerParams(vmem_limit_bytes=32 * 1024 * 1024),
         name="logits",
-    )(ids, own, other, received, adj, w_self.T, w_neigh.T)
+    )(hidden, received, adj, w_self.T, w_neigh.T)
 
 
 def exchange(parts, stride, n):
@@ -326,7 +337,6 @@
     tile = tile_weight.shape[1]
     groups = tile // UNIT
     per = groups // 2 // CHUNKS
-    places = list(range(groups // 2))
     bits = n.bit_length() - 1
     assert n == 1 << bits and bits >= 2
     radices = [2] * (bits // 2) + [1] * (bits % 2)
@@ -360,10 +370,11 @@
             got = exchange(parts, stride, n)
             stride *= ways
         done.append(got)
-    own, send = hidden_rows(done, sel)
+    own = hidden_rows(done)
     other = lax.ppermute(own, "feat", swap)
-    received = lax.all_to_all(send, ("feat", "dom"), 0, 0, tiled=True)
-    return logits_of(ids, own, other, received, adj_two, w_self2, w_neigh2, tile, places)
+    hidden, send = rows_to_send(groups, ids, own, other, sel)
+    received = lax.all_to_all(send, "dom", 0, 0, tiled=True)
+    return logits_of(hidden, received, adj_two, w_self2, w_neigh2)
 
 
 def solution(mesh):

time: 58 us -> 57.5 us (level)
  blocking collectives: 0 us -> 12.1 us
  waiting for transfers between devices: 25.2 us -> 18 us
  Pallas kernels: 19.2 us -> 16.3 us
  starting transfers between devices: 13.3 us -> 10.5 us
    all_to_all x0 -> x1, blocking collectives: none -> 12.1 us  [body(): received = lax.all_to_all(send, 'dom', 0, 0, tiled=True)]
    all_to_all x1 -> x0, waiting for transfers between devices: 6.64 us -> none  [body(): received = lax.all_to_all(send, ('feat', 'dom'), 0, 0, tiled=True)]
    all_to_all x1 -> x0, starting transfers between devices: 3.46 us -> none  [body(): received = lax.all_to_all(send, ('feat', 'dom'), 0, 0, tiled=True)]
    pallas_call x1, Pallas kernels: 12.3 us -> 10.4 us  [neighbour_terms(): pl.pallas_call(functools.partial(tiles_kernel, chunk, per, n, radix, grou...]
    pallas_call x1, Pallas kernels: 0.82 us -> 0.02 us  [hidden_rows(): pl.pallas_call(functools.partial(hidden_kernel, chunks, parts), out_shape...]
    ppermute x6, starting transfers between devices: 8.59 us -> 9.39 us  [exchange(): lax.ppermute(parts[k], 'dom', [(i, i ^ k * stride) for i in range(n)])]
    ppermute x6, waiting for transfers between devices: 17.6 us -> 16.8 us  [exchange(): lax.ppermute(parts[k], 'dom', [(i, i ^ k * stride) for i in range(n)])]
    pallas_call x1 -> x2, Pallas kernels: 1.47 us -> 1.6 us  [the longest x1 0.91 us: logits_of(): pl.pallas_call(logits_kernel, out_shape=jax.ShapeDtypeStruct((adj.shape[0...]
  transfers between devices with their start and end apart: 11 -> 10, of which waited for: 6 -> 5; matrix products, arithmetic and copies ran while one was open for 0% -> 0% of each run, Pallas kernels for 8% -> 8%
where the time goes in v4:
time: 57.5 us; the launch traced here: 57.2 us
  waiting for transfers between devices  18 us (31%)
  Pallas kernels  16.3 us (28%)
  blocking collectives  12.1 us (21%)
  starting transfers between devices  10.5 us (18%)
    ppermute x6, waiting for transfers between devices, exchange(): lax.ppermute(parts[k], 'dom', [(i, i ^ k * stride) for i in range(n)])  16.8 us
    all_to_all x1, blocking collectives, body(): received = lax.all_to_all(send, 'dom', 0, 0, tiled=True)  12.1 us
    pallas_call x1, Pallas kernels, neighbour_terms(): pl.pallas_call(functools.partial(tiles_kernel, chunk, per, n, radix, grou...  10.4 us
    ppermute x6, starting transfers between devices, exchange(): lax.ppermute(parts[k], 'dom', [(i, i ^ k * stride) for i in range(n)])  9.39 us
    pallas_call x1, Pallas kernels, plan(): pl.pallas_call(functools.partial(plan_kernel, chunks, per, n, radix, n_sr...  4.35 us
    ppermute x1, waiting for transfers between devices, body(): other = lax.ppermute(own, 'feat', swap)  1.15 us
  transfers between devices with their start and end apart: 10, of which 5 were waited for; matrix products, arithmetic and copies ran while one was open for 0% of the time, Pallas kernels for 8%

profile of v4, /device:TPU:0, one launch (start us, length us, event | category | flops | bytes accessed | tf_op | source)
XLA Modules:
  0.0 57.2 jit_solution(18155520735344190993)
XLA Ops:
  0.0 0.5 collective-permute-start
  0.5 0.1 collective-permute-start.2
  0.5 0.5 collective-permute-start.1
  1.0 0.1 pad_add_fusion.ids
  1.0 4.4 %plan.1 = (s32[2,768]{1,0:T(2,128)S(1)}, bf16[10240,128]{1,0:T(8,128)(2,1)S(1)}, bf16[128,128]{1,0:T(8,128)(2,1)S(1)}, bf16[1024,512]{1,0:T(8,128)(2,1)S(1)}, bf...) custom-call(s32[2]{0:T(128)S(1)} %pad_add_fusion.ids, s32[1,128]{1,0:T(1,128)} %bitcast.17, s32[1,128]{1,0:T(1,128)} %bitcast.18, ...), custom_call_target="tpu_custom_call" | custom-call | tf_op jit(solution)/shard_map/plan/pallas_call | solution.py:135
  5.4 0.0 collective-permute-done.2.sp
  5.4 0.0 collective-permute-done.1.wp
  5.4 0.0 collective-permute-done.xp
  5.4 0.0 copy-start
  5.4 0.0 copy-start.1
  5.5 0.0 copy-start.2
  5.5 10.4 %neighbour_terms.1 = (f32[256,256]{1,0:T(8,128)S(1)}, f32[256,256]{1,0:T(8,128)S(1)}, f32[256,256]{1,0:T(8,128)S(1)}, f32[256,256]{1,0:T(8,128)S(1)}) custom-call(s32[2]{0:T(128)S(1)} %pad_add_fusion.ids, s32[2,768]{1,0:T(2,128)S(1)} %get-tuple-element.17.table, bf16[10240,128]{1,0:T(8,128)(2,1)S(1)} %get-tuple-element.18.packed, ...), custom_call_target="tpu_custom_call" | custom-call | flops 8053063680 | bytes 8388608 | tf_op jit(solution)/shard_map/neighbour_terms/pallas_call | solution.py:223
  15.8 2.5 %collective-permute-start.3 = (f32[256,256]{1,0:T(8,128)S(1)}, f32[256,256]{1,0:T(8,128)S(1)}, u32[]{:S(2)}, u32[]{:S(2)}) collective-permute-start(f32[256,256]{1,0:T(8,128)S(1)} %get-tuple-element.23), channel_id=1, source_target_pairs={{0,1},{1,0},{2,3},{3,2},{4,5},{5,4},{6,7},{7,6},{8,9},{9,8},{10,11... | collective-permute-start | bytes 786440 | tf_op jit(solution)/shard_map/ppermute | solution.py:318
  18.4 1.6 %collective-permute-start.4 = (f32[256,256]{1,0:T(8,128)S(1)}, f32[256,256]{1,0:T(8,128)S(1)}, u32[]{:S(2)}, u32[]{:S(2)}) collective-permute-start(f32[256,256]{1,0:T(8,128)S(1)} %get-tuple-element.24), channel_id=1, source_target_pairs={{0,2},{1,3},{2,0},{3,1},{4,6},{5,7},{6,4},{7,5},{8,10},{9,11},{10,... | collective-permute-start | bytes 786440 | tf_op jit(solution)/shard_map/ppermute | solution.py:318
  19.9 0.8 %collective-permute-start.5 = (f32[256,256]{1,0:T(8,128)S(1)}, f32[256,256]{1,0:T(8,128)S(1)}, u32[]{:S(2)}, u32[]{:S(2)}) collective-permute-start(f32[256,256]{1,0:T(8,128)S(1)} %get-tuple-element.25), channel_id=1, source_target_pairs={{0,3},{1,2},{2,1},{3,0},{4,7},{5,6},{6,5},{7,4},{8,11},{9,10},{10,... | collective-permute-start | bytes 786440 | tf_op jit(solution)/shard_map/ppermute | solution.py:318
  20.8 4.7 %collective-permute-done.3 = f32[256,256]{1,0:T(8,128)S(1)} collective-permute-done((f32[256,256]{1,0:T(8,128)S(1)}, f32[256,256]{1,0:T(8,128)S(1)}, u32[]{:S(2)}, u32[]{:S(2)}) %collective-permute-start.3) | collective-permute-done | bytes 262176 | tf_op jit(solution)/shard_map/ppermute | solution.py:318
  25.5 7.6 %collective-permute-done.4 = f32[256,256]{1,0:T(8,128)S(1)} collective-permute-done((f32[256,256]{1,0:T(8,128)S(1)}, f32[256,256]{1,0:T(8,128)S(1)}, u32[]{:S(2)}, u32[]{:S(2)}) %collective-permute-start.4) | collective-permute-done | bytes 262176 | tf_op jit(solution)/shard_map/ppermute | solution.py:318
  33.1 0.0 collective-permute-done.5
  33.1 0.1 slice_add_fusion
  33.2 2.8 %collective-permute-start.8 = (f32[64,256]{1,0:T(8,128)S(1)}, f32[64,256]{1,0:T(8,128)S(1)}, u32[]{:S(2)}, u32[]{:S(2)}) collective-permute-start(f32[64,256]{1,0:T(8,128)S(1)} %get-tuple-element.29), channel_id=1, source_target_pairs={{0,12},{1,13},{2,14},{3,15},{4,8},{5,9},{6,10},{7,11},{8,4},{9,5},... | collective-permute-start | bytes 196616 | tf_op jit(solution)/shard_map/ppermute | solution.py:318
  36.0 0.0 collective-permute-start.7
  36.0 1.7 %collective-permute-start.6 = (f32[64,256]{1,0:T(8,128)S(1)}, f32[64,256]{1,0:T(8,128)S(1)}, u32[]{:S(2)}, u32[]{:S(2)}) collective-permute-start(f32[64,256]{1,0:T(8,128)S(1)} %get-tuple-element.31), channel_id=1, source_target_pairs={{0,4},{1,5},{2,6},{3,7},{4,0},{5,1},{6,2},{7,3},{8,12},{9,13},{10,... | collective-permute-start | bytes 196616 | tf_op jit(solution)/shard_map/ppermute | solution.py:318
  37.6 2.3 %collective-permute-done.8.refs_3_ = f32[64,256]{1,0:T(8,128)S(1)} collective-permute-done((f32[64,256]{1,0:T(8,128)S(1)}, f32[64,256]{1,0:T(8,128)S(1)}, u32[]{:S(2)}, u32[]{:S(2)}) %collective-permute-start.8) | collective-permute-done | bytes 65568 | tf_op jit(solution)/shard_map/ppermute | solution.py:318
  39.9 2.2 %collective-permute-done.7.refs_2_ = f32[64,256]{1,0:T(8,128)S(1)} collective-permute-done((f32[64,256]{1,0:T(8,128)S(1)}, f32[64,256]{1,0:T(8,128)S(1)}, u32[]{:S(2)}, u32[]{:S(2)}) %collective-permute-start.7) | collective-permute-done | bytes 65568 | tf_op jit(solution)/shard_map/ppermute | solution.py:318
  42.1 0.0 collective-permute-done.6.refs_1_
  42.1 0.1 collective-permute-start.9
  42.3 1.2 %collective-permute-done.9.other = bf16[64,256]{1,0:T(8,128)(2,1)S(1)} collective-permute-done((bf16[64,256]{1,0:T(8,128)(2,1)S(1)}, bf16[64,256]{1,0:T(8,128)(2,1)S(1)}, u32[]{:S(2)}, u32[]{:S(2)}) %collective-permute-start.9) | collective-permute-done | bytes 32800 | tf_op jit(solution)/shard_map/ppermute | solution.py:374
  43.4 0.7 %rows_to_send.1 = (bf16[128,256]{1,0:T(8,128)(2,1)S(1)}, bf16[128,256]{1,0:T(8,128)(2,1)S(1)}) custom-call(s32[2]{0:T(128)S(1)} %pad_add_fusion.ids, bf16[64,256]{1,0:T(8,128)(2,1)S(1)} %hidden_rows.1.own, bf16[64,256]{1,0:T(8,128)(2,1)S(1)} %collective-permute-done.9.other, bf16[128,128]{1,0:T(8,128)(2,1)S(1)} %get-tuple-element.26.sel), custom_call_target="tpu_custom_call" | custom-call | tf_op jit(solution)/shard_map/rows_to_send/pallas_call | solution.py:280
  44.1 12.1 %all_to_all.11 = bf16[16,8,256]{2,1,0:T(8,128)(2,1)S(1)} all-to-all(bf16[16,8,256]{2,1,0:T(8,128)(2,1)S(1)} %bitcast.14), channel_id=1, replica_groups=mesh['feat'=2,'dom'=16] {'dom'}, dimensions={0} | all-to-all | bytes 131072 | tf_op jit(solution)/shard_map/all_to_all | solution.py:376
  56.2 0.0 copy-done
  56.2 0.0 copy-done.1
  56.2 0.0 copy-done.2
  56.2 0.9 %logits.1 = f32[64,172]{1,0:T(8,128)} custom-call(bf16[128,256]{1,0:T(8,128)(2,1)S(1)} %get-tuple-element.27.hidden, bf16[128,256]{1,0:T(8,128)(2,1)S(1)} %bitcast.11, bf16[64,256]{1,0:T(8,128)(2,1)S(1)} %copy-done.2, bf16[172,256]{1,0:T(8,128)(2,1)S(1)} %bitcast.12, bf16[172,256]{1,0:T(8,128)(2,1)S(1)} %bitcast.13), custom_call_target="tpu_custom_call" | custom-call | tf_op jit(solution)/shard_map/logits/pallas_call | solution.py:305
  (1 shorter events, 0.0 us)
Async XLA Ops:
  0.0 5.4 %collective-permute-start = (bf16[1024,512]{1,0:T(8,128)(2,1)}, bf16[1024,512]{1,0:T(8,128)(2,1)S(1)}, u32[]{:S(2)}, u32[]{:S(2)}) collective-permute-start(bf16[1024,512]{1,0:T(8,128)(2,1)} %xo.1), channel_id=1, source_target_pairs={{0,16},{16,0},{1,17},{17,1},{2,18},{18,2},{3,19},{19,3},{4,20},{20... | collective-permute-start | bytes 3145736 | tf_op jit(solution)/shard_map/ppermute | solution.py:345
  0.5 4.9 %collective-permute-start.2 = (bf16[512,256]{1,0:T(8,128)(2,1)}, bf16[512,256]{1,0:T(8,128)(2,1)S(1)}, u32[]{:S(2)}, u32[]{:S(2)}) collective-permute-start(bf16[512,256]{1,0:T(8,128)(2,1)} %so.1), channel_id=1, source_target_pairs={{0,16},{16,0},{1,17},{17,1},{2,18},{18,2},{3,19},{19,3},{4,20},{20... | collective-permute-start | bytes 786440 | tf_op jit(solution)/shard_map/ppermute | solution.py:347
  0.5 4.9 %collective-permute-start.1 = (bf16[512,256]{1,0:T(8,128)(2,1)}, bf16[512,256]{1,0:T(8,128)(2,1)S(1)}, u32[]{:S(2)}, u32[]{:S(2)}) collective-permute-start(bf16[512,256]{1,0:T(8,128)(2,1)} %wo.1), channel_id=1, source_target_pairs={{0,16},{16,0},{1,17},{17,1},{2,18},{18,2},{3,19},{19,3},{4,20},{20... | collective-permute-start | bytes 786440 | tf_op jit(solution)/shard_map/ppermute | solution.py:346
  5.4 50.8 %copy-start = (bf16[256,172]{0,1:T(8,128)(2,1)S(1)}, bf16[256,172]{0,1:T(8,128)(2,1)}, u32[]{:S(2)}) copy-start(bf16[256,172]{0,1:T(8,128)(2,1)} %param.22) | copy-start | bytes 264196
  5.4 50.8 %copy-start.1 = (bf16[256,172]{0,1:T(8,128)(2,1)S(1)}, bf16[256,172]{0,1:T(8,128)(2,1)}, u32[]{:S(2)}) copy-start(bf16[256,172]{0,1:T(8,128)(2,1)} %param.23) | copy-start | bytes 264196
  5.5 50.8 %copy-start.2 = (bf16[64,256]{1,0:T(8,128)(2,1)S(1)}, bf16[64,256]{1,0:T(8,128)(2,1)}, u32[]{:S(2)}) copy-start(bf16[64,256]{1,0:T(8,128)(2,1)} %adj.1) | copy-start | bytes 98308
  15.8 9.7 %collective-permute-start.3 = (f32[256,256]{1,0:T(8,128)S(1)}, f32[256,256]{1,0:T(8,128)S(1)}, u32[]{:S(2)}, u32[]{:S(2)}) collective-permute-start(f32[256,256]{1,0:T(8,128)S(1)} %get-tuple-element.23), channel_id=1, source_target_pairs={{0,1},{1,0},{2,3},{3,2},{4,5},{5,4},{6,7},{7,6},{8,9},{9,8},{10,11... | collective-permute-start | bytes 786440 | tf_op jit(solution)/shard_map/ppermute | solution.py:318
  18.4 14.7 %collective-permute-start.4 = (f32[256,256]{1,0:T(8,128)S(1)}, f32[256,256]{1,0:T(8,128)S(1)}, u32[]{:S(2)}, u32[]{:S(2)}) collective-permute-start(f32[256,256]{1,0:T(8,128)S(1)} %get-tuple-element.24), channel_id=1, source_target_pairs={{0,2},{1,3},{2,0},{3,1},{4,6},{5,7},{6,4},{7,5},{8,10},{9,11},{10,... | collective-permute-start | bytes 786440 | tf_op jit(solution)/shard_map/ppermute | solution.py:318
  19.9 13.2 %collective-permute-start.5 = (f32[256,256]{1,0:T(8,128)S(1)}, f32[256,256]{1,0:T(8,128)S(1)}, u32[]{:S(2)}, u32[]{:S(2)}) collective-permute-start(f32[256,256]{1,0:T(8,128)S(1)} %get-tuple-element.25), channel_id=1, source_target_pairs={{0,3},{1,2},{2,1},{3,0},{4,7},{5,6},{6,5},{7,4},{8,11},{9,10},{10,... | collective-permute-start | bytes 786440 | tf_op jit(solution)/shard_map/ppermute | solution.py:318
  33.2 6.7 %collective-permute-start.8 = (f32[64,256]{1,0:T(8,128)S(1)}, f32[64,256]{1,0:T(8,128)S(1)}, u32[]{:S(2)}, u32[]{:S(2)}) collective-permute-start(f32[64,256]{1,0:T(8,128)S(1)} %get-tuple-element.29), channel_id=1, source_target_pairs={{0,12},{1,13},{2,14},{3,15},{4,8},{5,9},{6,10},{7,11},{8,4},{9,5},... | collective-permute-start | bytes 196616 | tf_op jit(solution)/shard_map/ppermute | solution.py:318
  36.0 6.2 %collective-permute-start.7 = (f32[64,256]{1,0:T(8,128)S(1)}, f32[64,256]{1,0:T(8,128)S(1)}, u32[]{:S(2)}, u32[]{:S(2)}) collective-permute-start(f32[64,256]{1,0:T(8,128)S(1)} %get-tuple-element.30), channel_id=1, source_target_pairs={{0,8},{1,9},{2,10},{3,11},{4,12},{5,13},{6,14},{7,15},{8,0},{9,1},... | collective-permute-start | bytes 196616 | tf_op jit(solution)/shard_map/ppermute | solution.py:318
  36.0 6.2 %collective-permute-start.6 = (f32[64,256]{1,0:T(8,128)S(1)}, f32[64,256]{1,0:T(8,128)S(1)}, u32[]{:S(2)}, u32[]{:S(2)}) collective-permute-start(f32[64,256]{1,0:T(8,128)S(1)} %get-tuple-element.31), channel_id=1, source_target_pairs={{0,4},{1,5},{2,6},{3,7},{4,0},{5,1},{6,2},{7,3},{8,12},{9,13},{10,... | collective-permute-start | bytes 196616 | tf_op jit(solution)/shard_map/ppermute | solution.py:318
  42.1 1.3 %collective-permute-start.9 = (bf16[64,256]{1,0:T(8,128)(2,1)S(1)}, bf16[64,256]{1,0:T(8,128)(2,1)S(1)}, u32[]{:S(2)}, u32[]{:S(2)}) collective-permute-start(bf16[64,256]{1,0:T(8,128)(2,1)S(1)} %hidden_rows.1.own), channel_id=1, source_target_pairs={{0,16},{16,0},{1,17},{17,1},{2,18},{18,2},{3,19},{19,3},{4,20},{20... | collective-permute-start | bytes 98312 | tf_op jit(solution)/shard_map/ppermute | solution.py:374

commit v5 on v4

--- a/solution.py
+++ b/solution.py
@@ -17,6 +17,42 @@
 def group_of(core, place, groups):
     pair = 2 * (place // 2) + core
     return pair if place % 2 == 0 else groups - 1 - pair
+
+
+LN2 = 0.6931471805599453
+
+
+def tail_rows(slots):
+    return -(-slots // 16) * 16
+
+
+def encode(x):
+    top = jnp.max(jnp.abs(x), axis=0, keepdims=True)
+    power = jnp.ceil(jnp.log(jnp.maximum(top, 1e-30)) * (1.0 / LN2) + 1e-3) - 15.0
+    return jnp.floor(x * jnp.exp(power * -LN2) + 0.5), power
+
+
+def to_int16(x):
+    return x.astype(jnp.int32).astype(jnp.int16)
+
+
+def write_coded(out, tail, slots, rows, value_of):
+    tail[...] = jnp.zeros_like(tail)
+    for s in range(slots):
+        whole, power = encode(value_of(s))
+        out[s * rows:(s + 1) * rows, :] = to_int16(whole)
+        tail[s:s + 1, :] = power
+    out[slots * rows:, :] = to_int16(tail[...])
+
+
+def read_coded(ref, slots, rows):
+    powers = ref[slots * rows:, :].astype(jnp.int32).astype(jnp.float32)
+
+    def value_of(s):
+        whole = ref[s * rows:(s + 1) * rows, :].astype(jnp.int32).astype(jnp.float32)
+        return whole * jnp.exp(powers[s:s + 1, :] * LN2)
+
+    return value_of
 
 
 def plan_kernel(chunks, per, n, radix, n_src, ids, src_h, rows_h, dst_h, lists_h, counts_h, tw, xo, wo, so, *rest):
@@ -164,8 +200,8 @@
 
 
 def tiles_kernel(chunk, per, n, radix, groups, ids, table, packed, xo, xp, wo, wp, so, sp, *rest):
-    outs, rest = rest[:radix], rest[radix:]
-    wbuf, gath, res, acc, sems = rest
+    acc, outs, rest = rest[0], rest[1:radix], rest[radix:]
+    wbuf, gath, res, tail, sems = rest
     tile = packed.shape[1]
     width = xo.shape[1]
     core = ids[0]
@@ -203,12 +239,9 @@
 
     steps = lax.div(table[1, table.shape[1] - 1] + STEP - 1, STEP)
     lax.fori_loop(0, steps + LEAD, step, 0)
-    span = n // radix * per * UNIT
-    back = [pltpu.make_async_copy(acc.at[pl.ds(k * span, span)], outs[k], sems.at[2 + k]) for k in range(radix)]
-    for c in back:
-        c.start()
-    for c in back:
-        c.wait()
+    slots, rows = n // radix, per * UNIT
+    for k, out in enumerate(outs, 1):
+        write_coded(out, tail, slots, rows, lambda s: acc[(k * slots + s) * rows:(k * slots + s + 1) * rows, :])
 
 
 def neighbour_terms(chunk, per, n, radix, groups, ids, table, packed, xo, xp, wo, wp, so, sp):
@@ -217,44 +250,78 @@
     tile = packed.shape[1]
     smem = pl.BlockSpec(memory_space=pltpu.SMEM)
     vmem = pl.BlockSpec(memory_space=pltpu.VMEM)
-    anym = pl.BlockSpec(memory_space=pl.ANY)
     flops = 2 * packed.shape[0] * (tile * 2 * width + 2 * width * hidden)
     sums = (n * per + 1) * UNIT * hidden * 4
+    slots, rows = n // radix, per * UNIT
+    coded = jax.ShapeDtypeStruct((slots * rows + tail_rows(slots), hidden), jnp.int16)
     return pl.pallas_call(
         functools.partial(tiles_kernel, chunk, per, n, radix, groups),
-        out_shape=[jax.ShapeDtypeStruct((n // radix * per * UNIT, hidden), jnp.float32)] * radix,
+        out_shape=[jax.ShapeDtypeStruct(((n * per + 1) * UNIT, hidden), jnp.float32)] + [coded] * (radix - 1),
         in_specs=[smem] * 2 + [vmem] * 7,
-        out_specs=[anym] * radix,
+        out_specs=[vmem] * radix,
         scratch_shapes=[
             pltpu.VMEM((2 * width, hidden), wo.dtype),
             pltpu.VMEM((STEP * BLOCK * UNIT, 2 * width), jnp.bfloat16),
             pltpu.VMEM((STEP * BLOCK * UNIT, hidden), jnp.float32),
-            pltpu.VMEM(((n * per + 1) * UNIT, hidden), jnp.float32),
-            pltpu.SemaphoreType.DMA((2 + radix,)),
+            pltpu.VMEM((tail_rows(slots), hidden), jnp.float32),
+            pltpu.SemaphoreType.DMA((2,)),
         ],
-        compiler_params=pltpu.CompilerParams(vmem_limit_bytes=(16 << 20) + sums),
+        compiler_params=pltpu.CompilerParams(vmem_limit_bytes=(16 << 20) + 2 * sums),
         cost_estimate=pl.CostEstimate(flops=flops, bytes_accessed=8 << 20, transcendentals=0),
         name="neighbour_terms",
     )(ids, table, packed, xo, xp, wo, wp, so, sp)
 
 
-def hidden_kernel(chunks, parts, *refs):
-    own = refs[chunks * parts]
-    rows = refs[0].shape[0]
+def combine_kernel(slots, rows, ways, own, *refs):
+    parts = len(refs) - ways - 1
+    coded, outs, tail = refs[:parts], refs[parts:parts + ways], refs[parts + ways]
+    values = [read_coded(a, slots, rows) for a in coded]
+
+    def total(s):
+        got = own[s * rows:(s + 1) * rows, :]
+        for value in values:
+            got = got + value(s)
+        return got
+
+    for i in range(slots // ways):
+        outs[0][i * rows:(i + 1) * rows, :] = total(i * ways)
+    for k in range(1, ways):
+        write_coded(outs[k], tail, slots // ways, rows, lambda s: total(s * ways + k))
+
+
+def combine(slots, rows, ways, own, coded):
+    width = own.shape[1]
+    left = slots // ways
+    vmem = pl.BlockSpec(memory_space=pltpu.VMEM)
+    out = jax.ShapeDtypeStruct((left * rows + tail_rows(left), width), jnp.int16)
+    return pl.pallas_call(
+        functools.partial(combine_kernel, slots, rows, ways),
+        out_shape=[jax.ShapeDtypeStruct((left * rows, width), jnp.float32)] + [out] * (ways - 1),
+        in_specs=[vmem] * (1 + len(coded)),
+        out_specs=[vmem] * ways,
+        scratch_shapes=[pltpu.VMEM((tail_rows(left), width), jnp.float32)],
+        compiler_params=pltpu.CompilerParams(vmem_limit_bytes=32 * 1024 * 1024),
+        name="combine",
+    )(own, *coded)
+
+
+def hidden_kernel(chunks, parts, rows, *refs):
+    out = refs[chunks * parts]
     for c in range(chunks):
-        total = refs[c * parts][...]
-        for k in range(1, parts):
-            total = total + refs[c * parts + k][...]
-        own[c * rows:(c + 1) * rows, :] = jnp.maximum(total, 0.0).astype(jnp.bfloat16)
-
-
-def hidden_rows(chunk_parts):
+        own, coded = refs[c * parts], refs[c * parts + 1:(c + 1) * parts]
+        total = own[:rows, :]
+        for a in coded:
+            total = total + read_coded(a, 1, rows)(0)
+        out[c * rows:(c + 1) * rows, :] = jnp.maximum(total, 0.0).astype(jnp.bfloat16)
+
+
+def hidden_rows(chunk_parts, rows):
     chunks, parts = len(chunk_parts), len(chunk_parts[0])
-    rows, width = chunk_parts[0][0].shape
+    width = chunk_parts[0][0].shape[1]
     vmem = pl.BlockSpec(memory_space=pltpu.VMEM)
     flat = [a for part in chunk_parts for a in part]
     return pl.pallas_call(
-        functools.partial(hidden_kernel, chunks, parts),
+        functools.partial(hidden_kernel, chunks, parts, rows),
         out_shape=jax.ShapeDtypeStruct((chunks * rows, width), jnp.bfloat16),
         in_specs=[vmem] * len(flat),
         out_specs=vmem,
@@ -356,21 +423,13 @@
         parts = neighbour_terms(chunk, per, n, 4, groups, ids, tables[chunk], packs[chunk], xo, xp, wo, wp, so, sp)
         got = exchange(parts, 1, n)
         stride = 4
-        left = n // 4
         for radix in radices[1:]:
             ways = 1 << radix
-            got = [a.reshape(left, per * UNIT, -1) for a in got]
-            left //= ways
-            parts = []
-            for k in range(ways):
-                total = got[0][k::ways]
-                for a in got[1:]:
-                    total = total + a[k::ways]
-                parts.append(total.reshape(left * per * UNIT, -1))
+            parts = combine(n // stride, per * UNIT, ways, got[0], got[1:])
             got = exchange(parts, stride, n)
             stride *= ways
         done.append(got)
-    own = hidden_rows(done)
+    own = hidden_rows(done, per * UNIT)
     other = lax.ppermute(own, "feat", swap)
     hidden, send = rows_to_send(groups, ids, own, other, sel)
     received = lax.all_to_all(send, "dom", 0, 0, tiled=True)

time: 57.5 us -> 51.8 us (0.901); the launches traced: 57.2 us -> 52.2 us
  waiting for transfers between devices: 18 us -> 14.2 us
  blocking collectives: 12.1 us -> 10.7 us
    ppermute x6, waiting for transfers between devices: 16.8 us -> 13 us  [exchange(): lax.ppermute(parts[k], 'dom', [(i, i ^ k * stride) for i in range(n)])]
    all_to_all x1, blocking collectives: 12.1 us -> 10.7 us  [body(): received = lax.all_to_all(send, 'dom', 0, 0, tiled=True)]
where the time goes in v5:
time: 51.8 us; the launch traced here: 52.2 us
  Pallas kernels  16.6 us (32%)
  waiting for transfers between devices  14.2 us (27%)
  blocking collectives  10.7 us (21%)
  starting transfers between devices  10.5 us (20%)
    ppermute x6, waiting for transfers between devices, exchange(): lax.ppermute(parts[k], 'dom', [(i, i ^ k * stride) for i in range(n)])  13 us
    all_to_all x1, blocking collectives, body(): received = lax.all_to_all(send, 'dom', 0, 0, tiled=True)  10.7 us
    pallas_call x1, Pallas kernels, neighbour_terms(): pl.pallas_call(functools.partial(tiles_kernel, chunk, per, n, radix, grou...  10.5 us
    ppermute x6, starting transfers between devices, exchange(): lax.ppermute(parts[k], 'dom', [(i, i ^ k * stride) for i in range(n)])  9.48 us
    pallas_call x1, Pallas kernels, plan(): pl.pallas_call(functools.partial(plan_kernel, chunks, per, n, radix, n_sr...  4.27 us
    ppermute x1, waiting for transfers between devices, body(): other = lax.ppermute(own, 'feat', swap)  1.19 us
  transfers between devices with their start and end apart: 10, of which 5 were waited for; matrix products, arithmetic and copies ran while one was open for 0% of the time, Pallas kernels for 8%

profile of v5, /device:TPU:0, one launch (start us, length us, event | category | flops | bytes accessed | tf_op | source)
XLA Modules:
  0.0 52.2 jit_solution(4917298654821261093)
XLA Ops:
  0.0 0.5 collective-permute-start
  0.5 0.1 collective-permute-start.2
  0.5 0.5 collective-permute-start.1
  1.0 0.1 pad_add_fusion.ids
  1.0 4.3 %plan.1 = (s32[2,768]{1,0:T(2,128)S(1)}, bf16[10240,128]{1,0:T(8,128)(2,1)S(1)}, bf16[128,128]{1,0:T(8,128)(2,1)S(1)}, bf16[1024,512]{1,0:T(8,128)(2,1)S(1)}, bf...) custom-call(s32[2]{0:T(128)S(1)} %pad_add_fusion.ids, s32[1,128]{1,0:T(1,128)} %bitcast.17, s32[1,128]{1,0:T(1,128)} %bitcast.18, ...), custom_call_target="tpu_custom_call" | custom-call | tf_op jit(solution)/shard_map/plan/pallas_call | solution.py:171
  5.3 0.0 collective-permute-done.2.sp
  5.3 0.0 collective-permute-done.1.wp
  5.3 0.0 collective-permute-done.xp
  5.3 0.0 copy-start
  5.4 0.0 copy-start.1
  5.4 0.0 copy-start.2
  5.4 10.5 %neighbour_terms.1 = (f32[1040,256]{1,0:T(8,128)S(1)}, s16[272,256]{1,0:T(8,128)(2,1)S(1)}, s16[272,256]{1,0:T(8,128)(2,1)S(1)}, s16[272,256]{1,0:T(8,128)(2,1)S(1)}) custom-call(s32[2]{0:T(128)S(1)} %pad_add_fusion.ids, s32[2,768]{1,0:T(2,128)S(1)} %get-tuple-element.21.table, bf16[10240,128]{1,0:T(8,128)(2,1)S(1)} %get-tuple-element.22.packed, ...), custom_call_target="tpu_custom_call" | custom-call | flops 8053063680 | bytes 8388608 | tf_op jit(solution)/shard_map/neighbour_terms/pallas_call | solution.py:257
  15.9 2.6 %collective-permute-start.3 = (s16[272,256]{1,0:T(8,128)(2,1)S(1)}, s16[272,256]{1,0:T(8,128)(2,1)S(1)}, u32[]{:S(2)}, u32[]{:S(2)}) collective-permute-start(s16[272,256]{1,0:T(8,128)(2,1)S(1)} %get-tuple-element.27), channel_id=1, source_target_pairs={{0,1},{1,0},{2,3},{3,2},{4,5},{5,4},{6,7},{7,6},{8,9},{9,8},{10,11... | collective-permute-start | bytes 417800 | tf_op jit(solution)/shard_map/ppermute | solution.py:385
  18.4 1.6 %collective-permute-start.4 = (s16[272,256]{1,0:T(8,128)(2,1)S(1)}, s16[272,256]{1,0:T(8,128)(2,1)S(1)}, u32[]{:S(2)}, u32[]{:S(2)}) collective-permute-start(s16[272,256]{1,0:T(8,128)(2,1)S(1)} %get-tuple-element.28), channel_id=1, source_target_pairs={{0,2},{1,3},{2,0},{3,1},{4,6},{5,7},{6,4},{7,5},{8,10},{9,11},{10,... | collective-permute-start | bytes 417800 | tf_op jit(solution)/shard_map/ppermute | solution.py:385
  20.0 0.0 collective-permute-start.5
  20.0 2.9 %collective-permute-done.3.refs_0_ = s16[272,256]{1,0:T(8,128)(2,1)S(1)} collective-permute-done((s16[272,256]{1,0:T(8,128)(2,1)S(1)}, s16[272,256]{1,0:T(8,128)(2,1)S(1)}, u32[]{:S(2)}, u32[]{:S(2)}) %collective-permute-start.3) | collective-permute-done | bytes 139296 | tf_op jit(solution)/shard_map/ppermute | solution.py:385
  23.0 4.3 %collective-permute-done.4.refs_1_ = s16[272,256]{1,0:T(8,128)(2,1)S(1)} collective-permute-done((s16[272,256]{1,0:T(8,128)(2,1)S(1)}, s16[272,256]{1,0:T(8,128)(2,1)S(1)}, u32[]{:S(2)}, u32[]{:S(2)}) %collective-permute-start.4) | collective-permute-done | bytes 139296 | tf_op jit(solution)/shard_map/ppermute | solution.py:385
  27.2 0.0 collective-permute-done.5.refs_2_
  27.2 0.2 combine.1
  27.4 2.5 %collective-permute-start.6 = (s16[80,256]{1,0:T(8,128)(2,1)S(1)}, s16[80,256]{1,0:T(8,128)(2,1)S(1)}, u32[]{:S(2)}, u32[]{:S(2)}) collective-permute-start(s16[80,256]{1,0:T(8,128)(2,1)S(1)} %get-tuple-element.31), channel_id=1, source_target_pairs={{0,4},{1,5},{2,6},{3,7},{4,0},{5,1},{6,2},{7,3},{8,12},{9,13},{10,... | collective-permute-start | bytes 122888 | tf_op jit(solution)/shard_map/ppermute | solution.py:385
  30.0 2.8 %collective-permute-start.7 = (s16[80,256]{1,0:T(8,128)(2,1)S(1)}, s16[80,256]{1,0:T(8,128)(2,1)S(1)}, u32[]{:S(2)}, u32[]{:S(2)}) collective-permute-start(s16[80,256]{1,0:T(8,128)(2,1)S(1)} %get-tuple-element.32), channel_id=1, source_target_pairs={{0,8},{1,9},{2,10},{3,11},{4,12},{5,13},{6,14},{7,15},{8,0},{9,1},... | collective-permute-start | bytes 122888 | tf_op jit(solution)/shard_map/ppermute | solution.py:385
  32.8 0.0 collective-permute-start.8
  32.8 0.0 collective-permute-done.6.refs_1_
  32.8 3.0 %collective-permute-done.7.refs_2_ = s16[80,256]{1,0:T(8,128)(2,1)S(1)} collective-permute-done((s16[80,256]{1,0:T(8,128)(2,1)S(1)}, s16[80,256]{1,0:T(8,128)(2,1)S(1)}, u32[]{:S(2)}, u32[]{:S(2)}) %collective-permute-start.7) | collective-permute-done | bytes 40992 | tf_op jit(solution)/shard_map/ppermute | solution.py:385
  35.7 2.8 %collective-permute-done.8.refs_3_ = s16[80,256]{1,0:T(8,128)(2,1)S(1)} collective-permute-done((s16[80,256]{1,0:T(8,128)(2,1)S(1)}, s16[80,256]{1,0:T(8,128)(2,1)S(1)}, u32[]{:S(2)}, u32[]{:S(2)}) %collective-permute-start.8) | collective-permute-done | bytes 40992 | tf_op jit(solution)/shard_map/ppermute | solution.py:385
  38.6 0.1 collective-permute-start.9
  38.7 1.2 %collective-permute-done.9.other = bf16[64,256]{1,0:T(8,128)(2,1)S(1)} collective-permute-done((bf16[64,256]{1,0:T(8,128)(2,1)S(1)}, bf16[64,256]{1,0:T(8,128)(2,1)S(1)}, u32[]{:S(2)}, u32[]{:S(2)}) %collective-permute-start.9) | collective-permute-done | bytes 32800 | tf_op jit(solution)/shard_map/ppermute | solution.py:433
  39.9 0.7 %rows_to_send.1 = (bf16[128,256]{1,0:T(8,128)(2,1)S(1)}, bf16[128,256]{1,0:T(8,128)(2,1)S(1)}) custom-call(s32[2]{0:T(128)S(1)} %pad_add_fusion.ids, bf16[64,256]{1,0:T(8,128)(2,1)S(1)} %hidden_rows.1.own, bf16[64,256]{1,0:T(8,128)(2,1)S(1)} %collective-permute-done.9.other, bf16[128,128]{1,0:T(8,128)(2,1)S(1)} %get-tuple-element.34.sel), custom_call_target="tpu_custom_call" | custom-call | tf_op jit(solution)/shard_map/rows_to_send/pallas_call | solution.py:347
  40.6 10.7 %all_to_all.11 = bf16[16,8,256]{2,1,0:T(8,128)(2,1)S(1)} all-to-all(bf16[16,8,256]{2,1,0:T(8,128)(2,1)S(1)} %bitcast.14), channel_id=1, replica_groups=mesh['feat'=2,'dom'=16] {'dom'}, dimensions={0} | all-to-all | bytes 131072 | tf_op jit(solution)/shard_map/all_to_all | solution.py:435
  51.3 0.0 copy-done
  51.3 0.0 copy-done.1
  51.3 0.0 copy-done.2
  51.3 0.9 %logits.1 = f32[64,172]{1,0:T(8,128)} custom-call(bf16[128,256]{1,0:T(8,128)(2,1)S(1)} %get-tuple-element.35.hidden, bf16[128,256]{1,0:T(8,128)(2,1)S(1)} %bitcast.11, bf16[64,256]{1,0:T(8,128)(2,1)S(1)} %copy-done.2, bf16[172,256]{1,0:T(8,128)(2,1)S(1)} %bitcast.12, bf16[172,256]{1,0:T(8,128)(2,1)S(1)} %bitcast.13), custom_call_target="tpu_custom_call" | custom-call | tf_op jit(solution)/shard_map/logits/pallas_call | solution.py:372
  (1 shorter events, 0.0 us)
Async XLA Ops:
  0.0 5.3 %collective-permute-start = (bf16[1024,512]{1,0:T(8,128)(2,1)}, bf16[1024,512]{1,0:T(8,128)(2,1)S(1)}, u32[]{:S(2)}, u32[]{:S(2)}) collective-permute-start(bf16[1024,512]{1,0:T(8,128)(2,1)} %xo.1), channel_id=1, source_target_pairs={{0,16},{16,0},{1,17},{17,1},{2,18},{18,2},{3,19},{19,3},{4,20},{20... | collective-permute-start | bytes 3145736 | tf_op jit(solution)/shard_map/ppermute | solution.py:412
  0.5 4.9 %collective-permute-start.2 = (bf16[512,256]{1,0:T(8,128)(2,1)}, bf16[512,256]{1,0:T(8,128)(2,1)S(1)}, u32[]{:S(2)}, u32[]{:S(2)}) collective-permute-start(bf16[512,256]{1,0:T(8,128)(2,1)} %so.1), channel_id=1, source_target_pairs={{0,16},{16,0},{1,17},{17,1},{2,18},{18,2},{3,19},{19,3},{4,20},{20... | collective-permute-start | bytes 786440 | tf_op jit(solution)/shard_map/ppermute | solution.py:414
  0.5 4.8 %collective-permute-start.1 = (bf16[512,256]{1,0:T(8,128)(2,1)}, bf16[512,256]{1,0:T(8,128)(2,1)S(1)}, u32[]{:S(2)}, u32[]{:S(2)}) collective-permute-start(bf16[512,256]{1,0:T(8,128)(2,1)} %wo.1), channel_id=1, source_target_pairs={{0,16},{16,0},{1,17},{17,1},{2,18},{18,2},{3,19},{19,3},{4,20},{20... | collective-permute-start | bytes 786440 | tf_op jit(solution)/shard_map/ppermute | solution.py:413
  5.3 46.0 %copy-start = (bf16[256,172]{0,1:T(8,128)(2,1)S(1)}, bf16[256,172]{0,1:T(8,128)(2,1)}, u32[]{:S(2)}) copy-start(bf16[256,172]{0,1:T(8,128)(2,1)} %param.22) | copy-start | bytes 264196
  5.4 46.0 %copy-start.1 = (bf16[256,172]{0,1:T(8,128)(2,1)S(1)}, bf16[256,172]{0,1:T(8,128)(2,1)}, u32[]{:S(2)}) copy-start(bf16[256,172]{0,1:T(8,128)(2,1)} %param.23) | copy-start | bytes 264196
  5.4 45.9 %copy-start.2 = (bf16[64,256]{1,0:T(8,128)(2,1)S(1)}, bf16[64,256]{1,0:T(8,128)(2,1)}, u32[]{:S(2)}) copy-start(bf16[64,256]{1,0:T(8,128)(2,1)} %adj.1) | copy-start | bytes 98308
  15.9 7.1 %collective-permute-start.3 = (s16[272,256]{1,0:T(8,128)(2,1)S(1)}, s16[272,256]{1,0:T(8,128)(2,1)S(1)}, u32[]{:S(2)}, u32[]{:S(2)}) collective-permute-start(s16[272,256]{1,0:T(8,128)(2,1)S(1)} %get-tuple-element.27), channel_id=1, source_target_pairs={{0,1},{1,0},{2,3},{3,2},{4,5},{5,4},{6,7},{7,6},{8,9},{9,8},{10,11... | collective-permute-start | bytes 417800 | tf_op jit(solution)/shard_map/ppermute | solution.py:385
  18.4 8.8 %collective-permute-start.4 = (s16[272,256]{1,0:T(8,128)(2,1)S(1)}, s16[272,256]{1,0:T(8,128)(2,1)S(1)}, u32[]{:S(2)}, u32[]{:S(2)}) collective-permute-start(s16[272,256]{1,0:T(8,128)(2,1)S(1)} %get-tuple-element.28), channel_id=1, source_target_pairs={{0,2},{1,3},{2,0},{3,1},{4,6},{5,7},{6,4},{7,5},{8,10},{9,11},{10,... | collective-permute-start | bytes 417800 | tf_op jit(solution)/shard_map/ppermute | solution.py:385
  20.0 7.2 %collective-permute-start.5 = (s16[272,256]{1,0:T(8,128)(2,1)S(1)}, s16[272,256]{1,0:T(8,128)(2,1)S(1)}, u32[]{:S(2)}, u32[]{:S(2)}) collective-permute-start(s16[272,256]{1,0:T(8,128)(2,1)S(1)} %get-tuple-element.29), channel_id=1, source_target_pairs={{0,3},{1,2},{2,1},{3,0},{4,7},{5,6},{6,5},{7,4},{8,11},{9,10},{10,... | collective-permute-start | bytes 417800 | tf_op jit(solution)/shard_map/ppermute | solution.py:385
  27.4 5.3 %collective-permute-start.6 = (s16[80,256]{1,0:T(8,128)(2,1)S(1)}, s16[80,256]{1,0:T(8,128)(2,1)S(1)}, u32[]{:S(2)}, u32[]{:S(2)}) collective-permute-start(s16[80,256]{1,0:T(8,128)(2,1)S(1)} %get-tuple-element.31), channel_id=1, source_target_pairs={{0,4},{1,5},{2,6},{3,7},{4,0},{5,1},{6,2},{7,3},{8,12},{9,13},{10,... | collective-permute-start | bytes 122888 | tf_op jit(solution)/shard_map/ppermute | solution.py:385
  30.0 5.8 %collective-permute-start.7 = (s16[80,256]{1,0:T(8,128)(2,1)S(1)}, s16[80,256]{1,0:T(8,128)(2,1)S(1)}, u32[]{:S(2)}, u32[]{:S(2)}) collective-permute-start(s16[80,256]{1,0:T(8,128)(2,1)S(1)} %get-tuple-element.32), channel_id=1, source_target_pairs={{0,8},{1,9},{2,10},{3,11},{4,12},{5,13},{6,14},{7,15},{8,0},{9,1},... | collective-permute-start | bytes 122888 | tf_op jit(solution)/shard_map/ppermute | solution.py:385
  32.8 5.8 %collective-permute-start.8 = (s16[80,256]{1,0:T(8,128)(2,1)S(1)}, s16[80,256]{1,0:T(8,128)(2,1)S(1)}, u32[]{:S(2)}, u32[]{:S(2)}) collective-permute-start(s16[80,256]{1,0:T(8,128)(2,1)S(1)} %get-tuple-element.33), channel_id=1, source_target_pairs={{0,12},{1,13},{2,14},{3,15},{4,8},{5,9},{6,10},{7,11},{8,4},{9,5},... | collective-permute-start | bytes 122888 | tf_op jit(solution)/shard_map/ppermute | solution.py:385
  38.6 1.3 %collective-permute-start.9 = (bf16[64,256]{1,0:T(8,128)(2,1)S(1)}, bf16[64,256]{1,0:T(8,128)(2,1)S(1)}, u32[]{:S(2)}, u32[]{:S(2)}) collective-permute-start(bf16[64,256]{1,0:T(8,128)(2,1)S(1)} %hidden_rows.1.own), channel_id=1, source_target_pairs={{0,16},{16,0},{1,17},{17,1},{2,18},{18,2},{3,19},{19,3},{4,20},{20... | collective-permute-start | bytes 98312 | tf_op jit(solution)/shard_map/ppermute | solution.py:433

commit v6 on v5

--- a/solution.py
+++ b/solution.py
@@ -134,7 +134,9 @@
     k_n = jnp.bitwise_and(q_n, slots - 1)
     for k in range(slots):
         picked = jnp.where(k_n == k, mine[k:k + 1, :], picked)
-    good = jnp.logical_and(lax.div(q_n, slots) == r_n, k_n < cnt)
+    block = lax.div(q_n, slots)
+    apart = jnp.bitwise_and(block, n // radix - 1) * radix + lax.div(block, n // radix)
+    good = jnp.logical_and(jnp.bitwise_xor(apart, me) == r_n, k_n < cnt)
     row = jnp.sum(jnp.where(good, picked + 1.0, 0.0), axis=1, keepdims=True) - 1.0
     lane = lax.broadcasted_iota(jnp.int32, (1, sel.shape[1]), 1).astype(jnp.float32)
     sel[...] = jnp.where(row == lane, 1.0, 0.0).astype(jnp.bfloat16)
@@ -330,53 +332,92 @@
     )(*flat)
 
 
-def send_kernel(groups, ids, own, other, sel, hidden, send):
+def send_kernel(groups, ways, ids, own, other, sel, hidden, *sends):
     core = ids[0]
     for i in range(groups // 2):
         mine = group_of(core, i, groups)
         theirs = group_of(1 - core, i, groups)
         hidden[pl.ds(pl.multiple_of(mine * UNIT, UNIT), UNIT), :] = own[i * UNIT:(i + 1) * UNIT, :]
         hidden[pl.ds(pl.multiple_of(theirs * UNIT, UNIT), UNIT), :] = other[i * UNIT:(i + 1) * UNIT, :]
-    send[...] = jnp.dot(sel[...], hidden[...], preferred_element_type=jnp.float32).astype(jnp.bfloat16)
-
-
-def rows_to_send(groups, ids, own, other, sel):
+    picked = jnp.dot(sel[...], hidden[...], preferred_element_type=jnp.float32).astype(jnp.bfloat16)
+    rows = sel.shape[0] // ways
+    for k in range(ways):
+        sends[k][...] = picked[k * rows:(k + 1) * rows, :]
+
+
+def rows_to_send(groups, ways, ids, own, other, sel):
     smem = pl.BlockSpec(memory_space=pltpu.SMEM)
     vmem = pl.BlockSpec(memory_space=pltpu.VMEM)
     width = own.shape[1]
     return pl.pallas_call(
-        functools.partial(send_kernel, groups),
-        out_shape=[
-            jax.ShapeDtypeStruct((groups * UNIT, width), jnp.bfloat16),
-            jax.ShapeDtypeStruct((sel.shape[0], width), jnp.bfloat16),
-        ],
+        functools.partial(send_kernel, groups, ways),
+        out_shape=[jax.ShapeDtypeStruct((groups * UNIT, width), jnp.bfloat16)]
+        + [jax.ShapeDtypeStruct((sel.shape[0] // ways, width), jnp.bfloat16)] * ways,
         in_specs=[smem] + [vmem] * 3,
-        out_specs=[vmem] * 2,
+        out_specs=[vmem] * (1 + ways),
         compiler_params=pltpu.CompilerParams(vmem_limit_bytes=32 * 1024 * 1024),
         name="rows_to_send",
     )(ids, own, other, sel)
 
 
-def logits_kernel(hidden, received, adj, w_self, w_neigh, out):
+def regroup_kernel(had, left, ways, slots, *refs):
+    parts = len(refs) - ways
+    values = [a[...].astype(jnp.float32) for a in refs[:parts]]
+    for k in range(ways):
+        pieces = []
+        for value in values:
+            for p in range(had):
+                for r in range(left // ways):
+                    at = (p * left + r * ways + k) * slots
+                    pieces.append(value[at:at + slots, :])
+        refs[parts + k][...] = jnp.concatenate(pieces, axis=0).astype(jnp.bfloat16)
+
+
+def regroup(had, left, ways, slots, arrays):
+    rows, width = arrays[0].shape
+    vmem = pl.BlockSpec(memory_space=pltpu.VMEM)
+    out = jax.ShapeDtypeStruct((len(arrays) * rows // ways, width), jnp.bfloat16)
+    return pl.pallas_call(
+        functools.partial(regroup_kernel, had, left, ways, slots),
+        out_shape=[out] * ways,
+        in_specs=[vmem] * len(arrays),
+        out_specs=[vmem] * ways,
+        compiler_params=pltpu.CompilerParams(vmem_limit_bytes=32 * 1024 * 1024),
+        name="regroup",
+    )(*arrays)
+
+
+def logits_kernel(order, slots, ids, hidden, adj, w_self, w_neigh, *refs):
+    arrived, (out, pool) = refs[:-2], refs[-2:]
+    me = ids[1]
     tile, rows = hidden.shape[0], adj.shape[0]
+    at = 0
+    for a in arrived:
+        value = a[...].astype(jnp.float32)
+        for i in range(a.shape[0] // slots):
+            sender = jnp.bitwise_xor(me, order[at])
+            pool[pl.ds(pl.multiple_of(sender * slots, slots), slots), :] = value[i * slots:(i + 1) * slots, :]
+            at += 1
     mean = jnp.dot(adj[:, :tile], hidden[...], preferred_element_type=jnp.float32)
-    mean = mean + jnp.dot(adj[:, tile:], received[...], preferred_element_type=jnp.float32)
+    mean = mean + jnp.dot(adj[:, tile:], pool[...].astype(jnp.bfloat16), preferred_element_type=jnp.float32)
     dims = (((1,), (1,)), ((), ()))
     got = lax.dot_general(hidden[:rows, :], w_self[...], dims, preferred_element_type=jnp.float32)
     got = got + lax.dot_general(mean.astype(jnp.bfloat16), w_neigh[...], dims, preferred_element_type=jnp.float32)
     out[...] = got
 
 
-def logits_of(hidden, received, adj, w_self, w_neigh):
-    vmem = pl.BlockSpec(memory_space=pltpu.VMEM)
-    return pl.pallas_call(
-        logits_kernel,
+def logits_of(order, slots, ids, hidden, adj, w_self, w_neigh, arrived):
+    smem = pl.BlockSpec(memory_space=pltpu.SMEM)
+    vmem = pl.BlockSpec(memory_space=pltpu.VMEM)
+    return pl.pallas_call(
+        functools.partial(logits_kernel, order, slots),
         out_shape=jax.ShapeDtypeStruct((adj.shape[0], w_self.shape[1]), jnp.float32),
-        in_specs=[vmem] * 5,
+        in_specs=[smem] + [vmem] * (4 + len(arrived)),
         out_specs=vmem,
+        scratch_shapes=[pltpu.VMEM((len(order) * slots, hidden.shape[1]), jnp.float32)],
         compiler_params=pltpu.CompilerParams(vmem_limit_bytes=32 * 1024 * 1024),
         name="logits",
-    )(hidden, received, adj, w_self.T, w_neigh.T)
+    )(ids, hidden, adj, w_self.T, w_neigh.T, *arrived)
 
 
 def exchange(parts, stride, n):
@@ -431,9 +472,20 @@
         done.append(got)
     own = hidden_rows(done, per * UNIT)
     other = lax.ppermute(own, "feat", swap)
-    hidden, send = rows_to_send(groups, ids, own, other, sel)
-    received = lax.all_to_all(send, "dom", 0, 0, tiled=True)
-    return logits_of(hidden, received, adj_two, w_self2, w_neigh2)
+    hidden, *sends = rows_to_send(groups, 4, ids, own, other, sel)
+    slots = send_list.shape[2]
+    arrived = exchange(sends, 1, n)
+    stride, order = 4, [0]
+    last = [k for k in range(4)]
+    for radix in radices[1:]:
+        ways = 1 << radix
+        sends = regroup(len(order), n // stride, ways, slots, arrived)
+        order = [k + v for k in last for v in order]
+        arrived = exchange(sends, stride, n)
+        last = [k * stride for k in range(ways)]
+        stride *= ways
+    order = tuple(k + v for k in last for v in order)
+    return logits_of(order, slots, ids, hidden, adj_two, w_self2, w_neigh2, arrived)
 
 
 def solution(mesh):

time: 51.8 us -> 55 us (1.062); the launches traced: 52.2 us -> 54.6 us
  blocking collectives: 10.7 us -> 0 us
  starting transfers between devices: 10.5 us -> 18.7 us
  waiting for transfers between devices: 14.2 us -> 18.5 us
  Pallas kernels: 16.6 us -> 17.2 us
    all_to_all x1 -> x0, blocking collectives: 10.7 us -> none  [body(): received = lax.all_to_all(send, 'dom', 0, 0, tiled=True)]
    ppermute x6 -> x12, starting transfers between devices: 9.48 us -> 17.7 us  [exchange(): lax.ppermute(parts[k], 'dom', [(i, i ^ k * stride) for i in range(n)])]
    ppermute x6 -> x12, waiting for transfers between devices: 13 us -> 17.3 us  [exchange(): lax.ppermute(parts[k], 'dom', [(i, i ^ k * stride) for i in range(n)])]
    pallas_call x2 -> x3, Pallas kernels: 1.6 us -> 2.17 us  [the longest x1 1.47 us: logits_of(): pl.pallas_call(functools.partial(logits_kernel, order, slots), out_shape=...]
  transfers between devices with their start and end apart: 10 -> 16, of which waited for: 5 -> 10; matrix products, arithmetic and copies ran while one was open for 0% -> 0% of each run, Pallas kernels for 8% -> 8%
where the time goes in v6:
time: 55 us; the launch traced here: 54.6 us
  starting transfers between devices  18.7 us (34%)
  waiting for transfers between devices  18.5 us (34%)
  Pallas kernels  17.2 us (31%)
    ppermute x12, starting transfers between devices, exchange(): lax.ppermute(parts[k], 'dom', [(i, i ^ k * stride) for i in range(n)])  17.7 us
    ppermute x12, waiting for transfers between devices, exchange(): lax.ppermute(parts[k], 'dom', [(i, i ^ k * stride) for i in range(n)])  17.3 us
    pallas_call x1, Pallas kernels, neighbour_terms(): pl.pallas_call(functools.partial(tiles_kernel, chunk, per, n, radix, grou...  10.5 us
    pallas_call x1, Pallas kernels, plan(): pl.pallas_call(functools.partial(plan_kernel, chunks, per, n, radix, n_sr...  4.35 us
    pallas_call x1, Pallas kernels, logits_of(): pl.pallas_call(functools.partial(logits_kernel, order, slots), out_shape=...  1.47 us
    ppermute x1, waiting for transfers between devices, body(): other = lax.ppermute(own, 'feat', swap)  1.19 us
  transfers between devices with their start and end apart: 16, of which 10 were waited for; matrix products, arithmetic and copies ran while one was open for 0% of the time, Pallas kernels for 8%

profile of v6, /device:TPU:0, one launch (start us, length us, event | category | flops | bytes accessed | tf_op | source)
XLA Modules:
  0.0 54.6 jit_solution(7360335737539955610)
XLA Ops:
  0.0 0.5 collective-permute-start
  0.5 0.1 collective-permute-start.2
  0.5 0.5 collective-permute-start.1
  1.0 0.1 pad_add_fusion.ids
  1.0 4.4 %plan.1 = (s32[2,768]{1,0:T(2,128)S(1)}, bf16[10240,128]{1,0:T(8,128)(2,1)S(1)}, bf16[128,128]{1,0:T(8,128)(2,1)S(1)}, bf16[1024,512]{1,0:T(8,128)(2,1)S(1)}, bf...) custom-call(s32[2]{0:T(128)S(1)} %pad_add_fusion.ids, s32[1,128]{1,0:T(1,128)} %bitcast.13, s32[1,128]{1,0:T(1,128)} %bitcast.14, ...), custom_call_target="tpu_custom_call" | custom-call | tf_op jit(solution)/shard_map/plan/pallas_call | solution.py:173
  5.4 0.0 collective-permute-done.2.sp
  5.4 0.0 collective-permute-done.1.wp
  5.4 0.0 collective-permute-done.xp
  5.4 0.0 copy-start
  5.4 0.0 copy-start.1
  5.5 0.0 copy-start.2
  5.5 10.5 %neighbour_terms.1 = (f32[1040,256]{1,0:T(8,128)S(1)}, s16[272,256]{1,0:T(8,128)(2,1)S(1)}, s16[272,256]{1,0:T(8,128)(2,1)S(1)}, s16[272,256]{1,0:T(8,128)(2,1)S(1)}) custom-call(s32[2]{0:T(128)S(1)} %pad_add_fusion.ids, s32[2,768]{1,0:T(2,128)S(1)} %get-tuple-element.28.table, bf16[10240,128]{1,0:T(8,128)(2,1)S(1)} %get-tuple-element.29.packed, ...), custom_call_target="tpu_custom_call" | custom-call | flops 8053063680 | bytes 8388608 | tf_op jit(solution)/shard_map/neighbour_terms/pallas_call | solution.py:259
  15.9 2.5 %collective-permute-start.3 = (s16[272,256]{1,0:T(8,128)(2,1)S(1)}, s16[272,256]{1,0:T(8,128)(2,1)S(1)}, u32[]{:S(2)}, u32[]{:S(2)}) collective-permute-start(s16[272,256]{1,0:T(8,128)(2,1)S(1)} %get-tuple-element.34), channel_id=1, source_target_pairs={{0,1},{1,0},{2,3},{3,2},{4,5},{5,4},{6,7},{7,6},{8,9},{9,8},{10,11... | collective-permute-start | bytes 417800 | tf_op jit(solution)/shard_map/ppermute | solution.py:426
  18.5 2.4 %collective-permute-start.4 = (s16[272,256]{1,0:T(8,128)(2,1)S(1)}, s16[272,256]{1,0:T(8,128)(2,1)S(1)}, u32[]{:S(2)}, u32[]{:S(2)}) collective-permute-start(s16[272,256]{1,0:T(8,128)(2,1)S(1)} %get-tuple-element.35), channel_id=1, source_target_pairs={{0,2},{1,3},{2,0},{3,1},{4,6},{5,7},{6,4},{7,5},{8,10},{9,11},{10,... | collective-permute-start | bytes 417800 | tf_op jit(solution)/shard_map/ppermute | solution.py:426
  20.9 0.0 collective-permute-start.5
  20.9 2.1 %collective-permute-done.3.refs_0_ = s16[272,256]{1,0:T(8,128)(2,1)S(1)} collective-permute-done((s16[272,256]{1,0:T(8,128)(2,1)S(1)}, s16[272,256]{1,0:T(8,128)(2,1)S(1)}, u32[]{:S(2)}, u32[]{:S(2)}) %collective-permute-start.3) | collective-permute-done | bytes 139296 | tf_op jit(solution)/shard_map/ppermute | solution.py:426
  23.0 4.3 %collective-permute-done.4.refs_1_ = s16[272,256]{1,0:T(8,128)(2,1)S(1)} collective-permute-done((s16[272,256]{1,0:T(8,128)(2,1)S(1)}, s16[272,256]{1,0:T(8,128)(2,1)S(1)}, u32[]{:S(2)}, u32[]{:S(2)}) %collective-permute-start.4) | collective-permute-done | bytes 139296 | tf_op jit(solution)/shard_map/ppermute | solution.py:426
  27.3 0.0 collective-permute-done.5.refs_2_
  27.3 0.2 combine.1
  27.5 1.6 %collective-permute-start.6 = (s16[80,256]{1,0:T(8,128)(2,1)S(1)}, s16[80,256]{1,0:T(8,128)(2,1)S(1)}, u32[]{:S(2)}, u32[]{:S(2)}) collective-permute-start(s16[80,256]{1,0:T(8,128)(2,1)S(1)} %get-tuple-element.38), channel_id=1, source_target_pairs={{0,4},{1,5},{2,6},{3,7},{4,0},{5,1},{6,2},{7,3},{8,12},{9,13},{10,... | collective-permute-start | bytes 122888 | tf_op jit(solution)/shard_map/ppermute | solution.py:426
  29.1 3.2 %collective-permute-start.7 = (s16[80,256]{1,0:T(8,128)(2,1)S(1)}, s16[80,256]{1,0:T(8,128)(2,1)S(1)}, u32[]{:S(2)}, u32[]{:S(2)}) collective-permute-start(s16[80,256]{1,0:T(8,128)(2,1)S(1)} %get-tuple-element.39), channel_id=1, source_target_pairs={{0,8},{1,9},{2,10},{3,11},{4,12},{5,13},{6,14},{7,15},{8,0},{9,1},... | collective-permute-start | bytes 122888 | tf_op jit(solution)/shard_map/ppermute | solution.py:426
  32.3 0.0 collective-permute-start.8
  32.3 0.0 collective-permute-done.6.refs_1_
  32.3 2.6 %collective-permute-done.7.refs_2_ = s16[80,256]{1,0:T(8,128)(2,1)S(1)} collective-permute-done((s16[80,256]{1,0:T(8,128)(2,1)S(1)}, s16[80,256]{1,0:T(8,128)(2,1)S(1)}, u32[]{:S(2)}, u32[]{:S(2)}) %collective-permute-start.7) | collective-permute-done | bytes 40992 | tf_op jit(solution)/shard_map/ppermute | solution.py:426
  34.9 3.2 %collective-permute-done.8.refs_3_ = s16[80,256]{1,0:T(8,128)(2,1)S(1)} collective-permute-done((s16[80,256]{1,0:T(8,128)(2,1)S(1)}, s16[80,256]{1,0:T(8,128)(2,1)S(1)}, u32[]{:S(2)}, u32[]{:S(2)}) %collective-permute-start.8) | collective-permute-done | bytes 40992 | tf_op jit(solution)/shard_map/ppermute | solution.py:426
  38.1 0.1 collective-permute-start.9
  38.2 1.2 %collective-permute-done.9.other = bf16[64,256]{1,0:T(8,128)(2,1)S(1)} collective-permute-done((bf16[64,256]{1,0:T(8,128)(2,1)S(1)}, bf16[64,256]{1,0:T(8,128)(2,1)S(1)}, u32[]{:S(2)}, u32[]{:S(2)}) %collective-permute-start.9) | collective-permute-done | bytes 32800 | tf_op jit(solution)/shard_map/ppermute | solution.py:474
  39.4 0.7 %rows_to_send.1 = (bf16[128,256]{1,0:T(8,128)(2,1)S(1)}, bf16[32,256]{1,0:T(8,128)(2,1)S(1)}, bf16[32,256]{1,0:T(8,128)(2,1)S(1)}, bf16[32,256]{1,0:T(8,128)(2,1)S(1)}, bf16[32,256]{1,0:T(8,128)(2,1)S(1)}) custom-call(s32[2]{0:T(128)S(1)} %pad_add_fusion.ids, bf16[64,256]{1,0:T(8,128)(2,1)S(1)} %hidden_rows.1.own, ...), custom_call_target="tpu_custom_call" | custom-call | tf_op jit(solution)/shard_map/rows_to_send/pallas_call | solution.py:352
  40.1 0.7 %collective-permute-start.10 = (bf16[32,256]{1,0:T(8,128)(2,1)S(1)}, bf16[32,256]{1,0:T(8,128)(2,1)S(1)}, u32[]{:S(2)}, u32[]{:S(2)}) collective-permute-start(bf16[32,256]{1,0:T(8,128)(2,1)S(1)} %get-tuple-element.44), channel_id=1, source_target_pairs={{0,1},{1,0},{2,3},{3,2},{4,5},{5,4},{6,7},{7,6},{8,9},{9,8},{10,11... | collective-permute-start | bytes 49160 | tf_op jit(solution)/shard_map/ppermute | solution.py:426
  40.8 0.6 %collective-permute-start.11 = (bf16[32,256]{1,0:T(8,128)(2,1)S(1)}, bf16[32,256]{1,0:T(8,128)(2,1)S(1)}, u32[]{:S(2)}, u32[]{:S(2)}) collective-permute-start(bf16[32,256]{1,0:T(8,128)(2,1)S(1)} %get-tuple-element.45), channel_id=1, source_target_pairs={{0,2},{1,3},{2,0},{3,1},{4,6},{5,7},{6,4},{7,5},{8,10},{9,11},{10,... | collective-permute-start | bytes 49160 | tf_op jit(solution)/shard_map/ppermute | solution.py:426
  41.4 2.2 %collective-permute-start.12 = (bf16[32,256]{1,0:T(8,128)(2,1)S(1)}, bf16[32,256]{1,0:T(8,128)(2,1)S(1)}, u32[]{:S(2)}, u32[]{:S(2)}) collective-permute-start(bf16[32,256]{1,0:T(8,128)(2,1)S(1)} %get-tuple-element.46), channel_id=1, source_target_pairs={{0,3},{1,2},{2,1},{3,0},{4,7},{5,6},{6,5},{7,4},{8,11},{9,10},{10,... | collective-permute-start | bytes 49160 | tf_op jit(solution)/shard_map/ppermute | solution.py:426
  43.7 0.2 collective-permute-done.10.refs_1_
  43.9 0.7 %collective-permute-done.11.refs_2_ = bf16[32,256]{1,0:T(8,128)(2,1)S(1)} collective-permute-done((bf16[32,256]{1,0:T(8,128)(2,1)S(1)}, bf16[32,256]{1,0:T(8,128)(2,1)S(1)}, u32[]{:S(2)}, u32[]{:S(2)}) %collective-permute-start.11) | collective-permute-done | bytes 16416 | tf_op jit(solution)/shard_map/ppermute | solution.py:426
  44.6 1.5 %collective-permute-done.12.refs_3_ = bf16[32,256]{1,0:T(8,128)(2,1)S(1)} collective-permute-done((bf16[32,256]{1,0:T(8,128)(2,1)S(1)}, bf16[32,256]{1,0:T(8,128)(2,1)S(1)}, u32[]{:S(2)}, u32[]{:S(2)}) %collective-permute-start.12) | collective-permute-done | bytes 16416 | tf_op jit(solution)/shard_map/ppermute | solution.py:426
  46.1 0.0 collective-permute-start.13
  46.1 1.5 %collective-permute-start.14 = (bf16[32,256]{1,0:T(8,128)(2,1)S(1)}, bf16[32,256]{1,0:T(8,128)(2,1)S(1)}, u32[]{:S(2)}, u32[]{:S(2)}) collective-permute-start(bf16[32,256]{1,0:T(8,128)(2,1)S(1)} %get-tuple-element.49), channel_id=1, source_target_pairs={{0,8},{1,9},{2,10},{3,11},{4,12},{5,13},{6,14},{7,15},{8,0},{9,1},... | collective-permute-start | bytes 49160 | tf_op jit(solution)/shard_map/ppermute | solution.py:426
  47.6 2.8 %collective-permute-start.15 = (bf16[32,256]{1,0:T(8,128)(2,1)S(1)}, bf16[32,256]{1,0:T(8,128)(2,1)S(1)}, u32[]{:S(2)}, u32[]{:S(2)}) collective-permute-start(bf16[32,256]{1,0:T(8,128)(2,1)S(1)} %get-tuple-element.50), channel_id=1, source_target_pairs={{0,12},{1,13},{2,14},{3,15},{4,8},{5,9},{6,10},{7,11},{8,4},{9,5},... | collective-permute-start | bytes 49160 | tf_op jit(solution)/shard_map/ppermute | solution.py:426
  50.5 0.0 collective-permute-done.13.refs_1_
  50.5 0.3 collective-permute-done.14.refs_2_
  50.8 2.4 %collective-permute-done.15.refs_3_ = bf16[32,256]{1,0:T(8,128)(2,1)S(1)} collective-permute-done((bf16[32,256]{1,0:T(8,128)(2,1)S(1)}, bf16[32,256]{1,0:T(8,128)(2,1)S(1)}, u32[]{:S(2)}, u32[]{:S(2)}) %collective-permute-start.15) | collective-permute-done | bytes 16416 | tf_op jit(solution)/shard_map/ppermute | solution.py:426
  53.2 0.0 copy-done
  53.2 0.0 copy-done.1
  53.2 0.0 copy-done.2
  53.2 1.5 %logits.1 = f32[64,172]{1,0:T(8,128)} custom-call(s32[2]{0:T(128)S(1)} %pad_add_fusion.ids, bf16[128,256]{1,0:T(8,128)(2,1)S(1)} %get-tuple-element.42.hidden, bf16[64,256]{1,0:T(8,128)(2,1)S(1)} %copy-done.2, bf16[172,256]{1,0:T(8,128)(2,1)S(1)} %bitcast.9, bf16[172,256]{1,0:T(8,128)(2,1)S(1)} %bitcast.10, bf16[32,256]{1,0:T(8,128)(2,1)S(1)} %get-tuple-element.47.refs_0_, ...), custom_call_target="tpu_custom_call" | custom-call | tf_op jit(solution)/shard_map/logits/pallas_call | solution.py:412
  (2 shorter events, 0.0 us)
Async XLA Ops:
  0.0 5.4 %collective-permute-start = (bf16[1024,512]{1,0:T(8,128)(2,1)}, bf16[1024,512]{1,0:T(8,128)(2,1)S(1)}, u32[]{:S(2)}, u32[]{:S(2)}) collective-permute-start(bf16[1024,512]{1,0:T(8,128)(2,1)} %xo.1), channel_id=1, source_target_pairs={{0,16},{16,0},{1,17},{17,1},{2,18},{18,2},{3,19},{19,3},{4,20},{20... | collective-permute-start | bytes 3145736 | tf_op jit(solution)/shard_map/ppermute | solution.py:453
  0.5 4.9 %collective-permute-start.2 = (bf16[512,256]{1,0:T(8,128)(2,1)}, bf16[512,256]{1,0:T(8,128)(2,1)S(1)}, u32[]{:S(2)}, u32[]{:S(2)}) collective-permute-start(bf16[512,256]{1,0:T(8,128)(2,1)} %so.1), channel_id=1, source_target_pairs={{0,16},{16,0},{1,17},{17,1},{2,18},{18,2},{3,19},{19,3},{4,20},{20... | collective-permute-start | bytes 786440 | tf_op jit(solution)/shard_map/ppermute | solution.py:455
  0.5 4.9 %collective-permute-start.1 = (bf16[512,256]{1,0:T(8,128)(2,1)}, bf16[512,256]{1,0:T(8,128)(2,1)S(1)}, u32[]{:S(2)}, u32[]{:S(2)}) collective-permute-start(bf16[512,256]{1,0:T(8,128)(2,1)} %wo.1), channel_id=1, source_target_pairs={{0,16},{16,0},{1,17},{17,1},{2,18},{18,2},{3,19},{19,3},{4,20},{20... | collective-permute-start | bytes 786440 | tf_op jit(solution)/shard_map/ppermute | solution.py:454
  5.4 47.7 %copy-start = (bf16[256,172]{0,1:T(8,128)(2,1)S(1)}, bf16[256,172]{0,1:T(8,128)(2,1)}, u32[]{:S(2)}) copy-start(bf16[256,172]{0,1:T(8,128)(2,1)} %param.22) | copy-start | bytes 264196
  5.4 47.7 %copy-start.1 = (bf16[256,172]{0,1:T(8,128)(2,1)S(1)}, bf16[256,172]{0,1:T(8,128)(2,1)}, u32[]{:S(2)}) copy-start(bf16[256,172]{0,1:T(8,128)(2,1)} %param.23) | copy-start | bytes 264196
  5.5 47.7 %copy-start.2 = (bf16[64,256]{1,0:T(8,128)(2,1)S(1)}, bf16[64,256]{1,0:T(8,128)(2,1)}, u32[]{:S(2)}) copy-start(bf16[64,256]{1,0:T(8,128)(2,1)} %adj.1) | copy-start | bytes 98308
  15.9 7.0 %collective-permute-start.3 = (s16[272,256]{1,0:T(8,128)(2,1)S(1)}, s16[272,256]{1,0:T(8,128)(2,1)S(1)}, u32[]{:S(2)}, u32[]{:S(2)}) collective-permute-start(s16[272,256]{1,0:T(8,128)(2,1)S(1)} %get-tuple-element.34), channel_id=1, source_target_pairs={{0,1},{1,0},{2,3},{3,2},{4,5},{5,4},{6,7},{7,6},{8,9},{9,8},{10,11... | collective-permute-start | bytes 417800 | tf_op jit(solution)/shard_map/ppermute | solution.py:426
  18.5 8.8 %collective-permute-start.4 = (s16[272,256]{1,0:T(8,128)(2,1)S(1)}, s16[272,256]{1,0:T(8,128)(2,1)S(1)}, u32[]{:S(2)}, u32[]{:S(2)}) collective-permute-start(s16[272,256]{1,0:T(8,128)(2,1)S(1)} %get-tuple-element.35), channel_id=1, source_target_pairs={{0,2},{1,3},{2,0},{3,1},{4,6},{5,7},{6,4},{7,5},{8,10},{9,11},{10,... | collective-permute-start | bytes 417800 | tf_op jit(solution)/shard_map/ppermute | solution.py:426
  20.9 6.4 %collective-permute-start.5 = (s16[272,256]{1,0:T(8,128)(2,1)S(1)}, s16[272,256]{1,0:T(8,128)(2,1)S(1)}, u32[]{:S(2)}, u32[]{:S(2)}) collective-permute-start(s16[272,256]{1,0:T(8,128)(2,1)S(1)} %get-tuple-element.36), channel_id=1, source_target_pairs={{0,3},{1,2},{2,1},{3,0},{4,7},{5,6},{6,5},{7,4},{8,11},{9,10},{10,... | collective-permute-start | bytes 417800 | tf_op jit(solution)/shard_map/ppermute | solution.py:426
  27.5 4.8 %collective-permute-start.6 = (s16[80,256]{1,0:T(8,128)(2,1)S(1)}, s16[80,256]{1,0:T(8,128)(2,1)S(1)}, u32[]{:S(2)}, u32[]{:S(2)}) collective-permute-start(s16[80,256]{1,0:T(8,128)(2,1)S(1)} %get-tuple-element.38), channel_id=1, source_target_pairs={{0,4},{1,5},{2,6},{3,7},{4,0},{5,1},{6,2},{7,3},{8,12},{9,13},{10,... | collective-permute-start | bytes 122888 | tf_op jit(solution)/shard_map/ppermute | solution.py:426
  29.1 5.8 %collective-permute-start.7 = (s16[80,256]{1,0:T(8,128)(2,1)S(1)}, s16[80,256]{1,0:T(8,128)(2,1)S(1)}, u32[]{:S(2)}, u32[]{:S(2)}) collective-permute-start(s16[80,256]{1,0:T(8,128)(2,1)S(1)} %get-tuple-element.39), channel_id=1, source_target_pairs={{0,8},{1,9},{2,10},{3,11},{4,12},{5,13},{6,14},{7,15},{8,0},{9,1},... | collective-permute-start | bytes 122888 | tf_op jit(solution)/shard_map/ppermute | solution.py:426
  32.3 5.8 %collective-permute-start.8 = (s16[80,256]{1,0:T(8,128)(2,1)S(1)}, s16[80,256]{1,0:T(8,128)(2,1)S(1)}, u32[]{:S(2)}, u32[]{:S(2)}) collective-permute-start(s16[80,256]{1,0:T(8,128)(2,1)S(1)} %get-tuple-element.40), channel_id=1, source_target_pairs={{0,12},{1,13},{2,14},{3,15},{4,8},{5,9},{6,10},{7,11},{8,4},{9,5},... | collective-permute-start | bytes 122888 | tf_op jit(solution)/shard_map/ppermute | solution.py:426
  38.1 1.3 %collective-permute-start.9 = (bf16[64,256]{1,0:T(8,128)(2,1)S(1)}, bf16[64,256]{1,0:T(8,128)(2,1)S(1)}, u32[]{:S(2)}, u32[]{:S(2)}) collective-permute-start(bf16[64,256]{1,0:T(8,128)(2,1)S(1)} %hidden_rows.1.own), channel_id=1, source_target_pairs={{0,16},{16,0},{1,17},{17,1},{2,18},{18,2},{3,19},{19,3},{4,20},{20... | collective-permute-start | bytes 98312 | tf_op jit(solution)/shard_map/ppermute | solution.py:474
  40.1 3.8 %collective-permute-start.10 = (bf16[32,256]{1,0:T(8,128)(2,1)S(1)}, bf16[32,256]{1,0:T(8,128)(2,1)S(1)}, u32[]{:S(2)}, u32[]{:S(2)}) collective-permute-start(bf16[32,256]{1,0:T(8,128)(2,1)S(1)} %get-tuple-element.44), channel_id=1, source_target_pairs={{0,1},{1,0},{2,3},{3,2},{4,5},{5,4},{6,7},{7,6},{8,9},{9,8},{10,11... | collective-permute-start | bytes 49160 | tf_op jit(solution)/shard_map/ppermute | solution.py:426
  40.8 3.8 %collective-permute-start.11 = (bf16[32,256]{1,0:T(8,128)(2,1)S(1)}, bf16[32,256]{1,0:T(8,128)(2,1)S(1)}, u32[]{:S(2)}, u32[]{:S(2)}) collective-permute-start(bf16[32,256]{1,0:T(8,128)(2,1)S(1)} %get-tuple-element.45), channel_id=1, source_target_pairs={{0,2},{1,3},{2,0},{3,1},{4,6},{5,7},{6,4},{7,5},{8,10},{9,11},{10,... | collective-permute-start | bytes 49160 | tf_op jit(solution)/shard_map/ppermute | solution.py:426
  41.4 4.6 %collective-permute-start.12 = (bf16[32,256]{1,0:T(8,128)(2,1)S(1)}, bf16[32,256]{1,0:T(8,128)(2,1)S(1)}, u32[]{:S(2)}, u32[]{:S(2)}) collective-permute-start(bf16[32,256]{1,0:T(8,128)(2,1)S(1)} %get-tuple-element.46), channel_id=1, source_target_pairs={{0,3},{1,2},{2,1},{3,0},{4,7},{5,6},{6,5},{7,4},{8,11},{9,10},{10,... | collective-permute-start | bytes 49160 | tf_op jit(solution)/shard_map/ppermute | solution.py:426
  46.1 4.4 %collective-permute-start.13 = (bf16[32,256]{1,0:T(8,128)(2,1)S(1)}, bf16[32,256]{1,0:T(8,128)(2,1)S(1)}, u32[]{:S(2)}, u32[]{:S(2)}) collective-permute-start(bf16[32,256]{1,0:T(8,128)(2,1)S(1)} %get-tuple-element.48), channel_id=1, source_target_pairs={{0,4},{1,5},{2,6},{3,7},{4,0},{5,1},{6,2},{7,3},{8,12},{9,13},{10,... | collective-permute-start | bytes 49160 | tf_op jit(solution)/shard_map/ppermute | solution.py:426
  46.1 4.7 %collective-permute-start.14 = (bf16[32,256]{1,0:T(8,128)(2,1)S(1)}, bf16[32,256]{1,0:T(8,128)(2,1)S(1)}, u32[]{:S(2)}, u32[]{:S(2)}) collective-permute-start(bf16[32,256]{1,0:T(8,128)(2,1)S(1)} %get-tuple-element.49), channel_id=1, source_target_pairs={{0,8},{1,9},{2,10},{3,11},{4,12},{5,13},{6,14},{7,15},{8,0},{9,1},... | collective-permute-start | bytes 49160 | tf_op jit(solution)/shard_map/ppermute | solution.py:426
  47.6 5.5 %collective-permute-start.15 = (bf16[32,256]{1,0:T(8,128)(2,1)S(1)}, bf16[32,256]{1,0:T(8,128)(2,1)S(1)}, u32[]{:S(2)}, u32[]{:S(2)}) collective-permute-start(bf16[32,256]{1,0:T(8,128)(2,1)S(1)} %get-tuple-element.50), channel_id=1, source_target_pairs={{0,12},{1,13},{2,14},{3,15},{4,8},{5,9},{6,10},{7,11},{8,4},{9,5},... | collective-permute-start | bytes 49160 | tf_op jit(solution)/shard_map/ppermute | solution.py:426

commit v7 on v5

--- a/solution.py
+++ b/solution.py
@@ -9,8 +9,8 @@
 
 UNIT = 16
 BLOCK = 8
-STEP = 4
-LEAD = 2
+STEP = 8
+PART = 256
 CHUNKS = 1
 
 
@@ -57,27 +57,22 @@
 
 def plan_kernel(chunks, per, n, radix, n_src, ids, src_h, rows_h, dst_h, lists_h, counts_h, tw, xo, wo, so, *rest):
     tables, rest = rest[:chunks], rest[chunks:]
-    packs, rest = rest[:chunks], rest[chunks:]
+    tbufs, rest = rest[:chunks], rest[chunks:]
     sel, xo_out, wo_out, so_out = rest[:4]
-    src_v, rows_v, dst_v, lists, counts, tbuf, masks, table_s, sems = rest[4:]
+    src_v, rows_v, dst_v, lists, counts, sems = rest[4:]
     core, me = ids[0], ids[1]
     tiles = src_v.shape[1]
-    tile = tw.shape[3]
-    lead = LEAD * STEP * BLOCK
     n_pos = tables[0].shape[1]
     units = per * tiles
     groups = 2 * per * chunks
     half = groups // 2
     gs = [group_of(core, i, groups) for i in range(half)]
     small = [(src_h, src_v), (rows_h, rows_v), (dst_h, dst_v), (lists_h, lists), (counts_h, counts)]
-    large = [(tw.at[:, g], tbuf.at[pl.ds(i * tiles, tiles)]) for i, g in enumerate(gs)]
+    large = [(tw.at[:, g], tbufs[i // per].at[pl.ds(i % per * tiles, tiles)]) for i, g in enumerate(gs)]
     large += [(xo, xo_out), (wo, wo_out), (so, so_out)]
     copies = [pltpu.make_async_copy(a, b, sems.at[i]) for i, (a, b) in enumerate(small + large)]
     for c in copies:
         c.start()
-    row_i = lax.broadcasted_iota(jnp.int32, (UNIT, tile), 0)
-    for m in range(UNIT + 1):
-        masks[m] = jnp.where(row_i < m, 1.0, 0.0).astype(jnp.bfloat16)
     lane = lax.broadcasted_iota(jnp.int32, (1, tiles), 1)
     block_i = lax.broadcasted_iota(jnp.int32, (n_src, tiles), 0)
     before = lax.broadcasted_iota(jnp.int32, (units, units), 0) < lax.broadcasted_iota(jnp.int32, (units, units), 1)
@@ -90,7 +85,6 @@
     src, rows = src_v[...], rows_v[...]
     slot = jnp.bitwise_xor(dst_v[...], me)
     slot = jnp.bitwise_and(slot, radix - 1) * (n // radix) + lax.div(slot, radix)
-    to_scalar = []
     for c in range(chunks):
         hot, words, valid = [], [], []
         for j in range(per):
@@ -106,7 +100,7 @@
         pos = jnp.zeros((1, units), jnp.float32)
         owner = jnp.zeros((1, n_pos), jnp.float32)
         for s in range(n_src):
-            pos = pos + hot[s:s + 1, :] * (earlier[s:s + 1, :] + (run * BLOCK + lead))
+            pos = pos + hot[s:s + 1, :] * (earlier[s:s + 1, :] + run * BLOCK)
             run = run + blocks[s:s + 1, :]
             owner = owner + jnp.where(place_i.astype(jnp.float32) >= run, 1.0, 0.0)
         stack = [jnp.where(valid[j], pos[:, j * tiles:(j + 1) * tiles], -1.0) for j in range(per)]
@@ -120,9 +114,6 @@
         owner = jnp.where(place_i == n_pos - 1, run, jnp.minimum(owner, n_src - 1.0))
         tables[c][0:1, :] = word.astype(jnp.int32)
         tables[c][1:2, :] = owner.astype(jnp.int32)
-        copy = pltpu.make_async_copy(tables[c], table_s.at[c], sems.at[len(copies) + c])
-        copy.start()
-        to_scalar.append(copy)
 
     slots = lists.shape[1]
     total = n * slots
@@ -139,21 +130,7 @@
     lane = lax.broadcasted_iota(jnp.int32, (1, sel.shape[1]), 1).astype(jnp.float32)
     sel[...] = jnp.where(row == lane, 1.0, 0.0).astype(jnp.bfloat16)
 
-    for c in copies[5:5 + half]:
-        c.wait()
-    for c in range(chunks):
-        to_scalar[c].wait()
-
-        def block(b, carry):
-            for k in range(BLOCK):
-                word = table_s[c, 0, lead + b * BLOCK + k]
-                u = jnp.bitwise_and(lax.shift_right_logical(word, 5), 511) + c * units
-                at = pl.multiple_of((b * BLOCK + k) * UNIT, UNIT)
-                packs[c][pl.ds(at, UNIT), :] = tbuf[u] * masks[jnp.bitwise_and(word, 31)]
-            return carry
-
-        lax.fori_loop(0, table_s[c, 1, n_pos - 1], block, 0)
-    for c in copies[5 + half:]:
+    for c in copies[5:]:
         c.wait()
 
 
@@ -161,8 +138,8 @@
     tiles, _, _, tile = tw.shape
     slots = send_list.shape[2]
     n_src = xo.shape[0] // tile
-    blocks = -(-(per * tiles // BLOCK + n_src) // STEP + -LEAD) * STEP
-    n_pos = -(-((LEAD * STEP + blocks) * BLOCK + 1) // 128) * 128
+    blocks = -(-(per * tiles // BLOCK + n_src) // STEP) * STEP
+    n_pos = -(-(blocks * BLOCK + 1) // 128) * 128
     smem = pl.BlockSpec(memory_space=pltpu.SMEM)
     vmem = pl.BlockSpec(memory_space=pltpu.VMEM)
     hbm = pl.BlockSpec(memory_space=pltpu.HBM)
@@ -171,7 +148,7 @@
     return pl.pallas_call(
         functools.partial(plan_kernel, chunks, per, n, radix, n_src),
         out_shape=[jax.ShapeDtypeStruct((2, n_pos), jnp.int32)] * chunks
-        + [jax.ShapeDtypeStruct((blocks * BLOCK * UNIT, tile), tw.dtype)] * chunks
+        + [jax.ShapeDtypeStruct((per * tiles, UNIT, tile), tw.dtype)] * chunks
         + [
             jax.ShapeDtypeStruct((n * slots, 2 * half * UNIT), jnp.bfloat16),
             jax.ShapeDtypeStruct(xo.shape, xo.dtype),
@@ -186,10 +163,7 @@
             pltpu.VMEM((1, tiles), jnp.int32),
             pltpu.VMEM(lists.shape, jnp.int32),
             pltpu.VMEM(send_count.shape, jnp.int32),
-            pltpu.VMEM((half * tiles, UNIT, tile), tw.dtype),
-            pltpu.VMEM((UNIT + 1, UNIT, tile), jnp.bfloat16),
-            pltpu.SMEM((chunks, 2, n_pos), jnp.int32),
-            pltpu.SemaphoreType.DMA((5 + half + 3 + chunks,)),
+            pltpu.SemaphoreType.DMA((5 + half + 3,)),
         ],
         compiler_params=pltpu.CompilerParams(vmem_limit_bytes=32 * 1024 * 1024),
         name="plan",
@@ -199,77 +173,93 @@
     ])
 
 
-def tiles_kernel(chunk, per, n, radix, groups, ids, table, packed, xo, xp, wo, wp, so, sp, *rest):
-    acc, outs, rest = rest[0], rest[1:radix], rest[radix:]
-    wbuf, gath, res, tail, sems = rest
-    tile = packed.shape[1]
+def tiles_kernel(chunk, per, n, radix, groups, ids, table, tbuf, xo, xp, wo, wp, so, sp, *rest):
+    own, outs, rest = rest[0], rest[1:radix], rest[radix:]
+    masks, sums, tail, accs = rest[0], rest[1], rest[2], rest[3:]
+    tile = tbuf.shape[2]
     width = xo.shape[1]
     core = ids[0]
-    copies = [
-        pltpu.make_async_copy(wo, wbuf.at[pl.ds(0, width)], sems.at[0]),
-        pltpu.make_async_copy(wp, wbuf.at[pl.ds(width, width)], sems.at[1]),
-    ]
-    for c in copies:
-        c.start()
-    acc[...] = jnp.zeros_like(acc)
-    for j in range(per):
-        at = pl.multiple_of(group_of(core, chunk * per + j, groups) * UNIT, UNIT)
-        own = jnp.dot(xo[pl.ds(at, UNIT), :], so[...], preferred_element_type=jnp.float32)
-        own = own + jnp.dot(xp[pl.ds(at, UNIT), :], sp[...], preferred_element_type=jnp.float32)
-        acc[j * UNIT:(j + 1) * UNIT, :] = own
-    for c in copies:
-        c.wait()
-
-    size = BLOCK * UNIT
+    for acc in accs:
+        acc[...] = jnp.zeros_like(acc)
+    row_i = lax.broadcasted_iota(jnp.int32, (UNIT, tile), 0)
+    for m in range(UNIT + 1):
+        masks[m] = jnp.where(row_i < m, 1.0, 0.0).astype(jnp.bfloat16)
+    parts = [(x, w, h) for x, w in ((xo, wo), (xp, wp)) for h in range(0, width, PART)]
 
     def step(i, carry):
-        for k in range(STEP * BLOCK):
-            word = table[0, i * (STEP * BLOCK) + k]
-            at = pl.multiple_of(lax.shift_right_logical(word, 14) * UNIT, UNIT)
-            acc[pl.ds(at, UNIT), :] += res[k * UNIT:(k + 1) * UNIT, :]
-        res[...] = jnp.dot(gath[...], wbuf[...], preferred_element_type=jnp.float32)
         for m in range(STEP):
-            base = pl.multiple_of(table[1, i * STEP + m] * tile, tile)
-            lhs = packed[pl.ds(pl.multiple_of((i * STEP + m) * size, size), size), :]
-            for q, x in enumerate((xo, xp)):
-                for h in range(0, width, 256):
-                    got = jnp.dot(lhs, x[pl.ds(base, tile), h:h + 256], preferred_element_type=jnp.float32)
-                    gath[m * size:(m + 1) * size, q * width + h:q * width + h + 256] = got.astype(jnp.bfloat16)
+            b = i * STEP + m
+            base = pl.multiple_of(table[1, b] * tile, tile)
+            rows, places = [], []
+            for k in range(BLOCK):
+                word = table[0, b * BLOCK + k]
+                u = jnp.bitwise_and(lax.shift_right_logical(word, 5), 511)
+                rows.append(tbuf[u] * masks[jnp.bitwise_and(word, 31)])
+                places.append(pl.multiple_of(lax.shift_right_logical(word, 14) * UNIT, UNIT))
+            lhs = jnp.concatenate(rows, axis=0)
+            for acc, (x, _, h) in zip(accs, parts):
+                got = jnp.dot(lhs, x[pl.ds(base, tile), h:h + PART], preferred_element_type=jnp.float32)
+                got = got.astype(jnp.bfloat16).astype(jnp.float32)
+                for k in range(BLOCK):
+                    acc[pl.ds(places[k], UNIT), :] += got[k * UNIT:(k + 1) * UNIT, :]
         return carry
 
     steps = lax.div(table[1, table.shape[1] - 1] + STEP - 1, STEP)
-    lax.fori_loop(0, steps + LEAD, step, 0)
+    lax.fori_loop(0, steps, step, 0)
+
     slots, rows = n // radix, per * UNIT
-    for k, out in enumerate(outs, 1):
-        write_coded(out, tail, slots, rows, lambda s: acc[(k * slots + s) * rows:(k * slots + s + 1) * rows, :])
-
-
-def neighbour_terms(chunk, per, n, radix, groups, ids, table, packed, xo, xp, wo, wp, so, sp):
+    size = min(256, slots * rows)
+    for k in range(radix):
+        out = own if k == 0 else sums
+
+        def weigh(r, carry):
+            at = pl.multiple_of(r * size, size)
+            got = jnp.zeros((size, out.shape[1]), jnp.float32)
+            for acc, (_, w, h) in zip(accs, parts):
+                value = acc[pl.ds(k * slots * rows + at, size), :]
+                high = value.astype(jnp.bfloat16)
+                low = (value - high.astype(jnp.float32)).astype(jnp.bfloat16)
+                got = got + jnp.dot(high, w[h:h + PART, :], preferred_element_type=jnp.float32)
+                got = got + jnp.dot(low, w[h:h + PART, :], preferred_element_type=jnp.float32)
+            out[pl.ds(at, size), :] = got
+            return carry
+
+        lax.fori_loop(0, slots * rows // size, weigh, 0)
+        if k == 0:
+            for j in range(per):
+                at = pl.multiple_of(group_of(core, chunk * per + j, groups) * UNIT, UNIT)
+                self = jnp.dot(xo[pl.ds(at, UNIT), :], so[...], preferred_element_type=jnp.float32)
+                self = self + jnp.dot(xp[pl.ds(at, UNIT), :], sp[...], preferred_element_type=jnp.float32)
+                out[j * UNIT:(j + 1) * UNIT, :] += self
+        else:
+            write_coded(outs[k - 1], tail, slots, rows, lambda s: sums[s * rows:(s + 1) * rows, :])
+
+
+def neighbour_terms(chunk, per, n, radix, groups, ids, table, tbuf, xo, xp, wo, wp, so, sp):
     hidden = wo.shape[1]
     width = xo.shape[1]
-    tile = packed.shape[1]
+    tile = tbuf.shape[2]
     smem = pl.BlockSpec(memory_space=pltpu.SMEM)
     vmem = pl.BlockSpec(memory_space=pltpu.VMEM)
-    flops = 2 * packed.shape[0] * (tile * 2 * width + 2 * width * hidden)
-    sums = (n * per + 1) * UNIT * hidden * 4
+    flops = 2 * tbuf.shape[0] * UNIT * tile * 2 * width + 4 * n * per * UNIT * 2 * width * hidden
     slots, rows = n // radix, per * UNIT
+    held = (n * per + 1) * UNIT * 2 * width * 4
     coded = jax.ShapeDtypeStruct((slots * rows + tail_rows(slots), hidden), jnp.int16)
     return pl.pallas_call(
         functools.partial(tiles_kernel, chunk, per, n, radix, groups),
-        out_shape=[jax.ShapeDtypeStruct(((n * per + 1) * UNIT, hidden), jnp.float32)] + [coded] * (radix - 1),
+        out_shape=[jax.ShapeDtypeStruct((slots * rows, hidden), jnp.float32)] + [coded] * (radix - 1),
         in_specs=[smem] * 2 + [vmem] * 7,
         out_specs=[vmem] * radix,
         scratch_shapes=[
-            pltpu.VMEM((2 * width, hidden), wo.dtype),
-            pltpu.VMEM((STEP * BLOCK * UNIT, 2 * width), jnp.bfloat16),
-            pltpu.VMEM((STEP * BLOCK * UNIT, hidden), jnp.float32),
+            pltpu.VMEM((UNIT + 1, UNIT, tile), jnp.bfloat16),
+            pltpu.VMEM((slots * rows, hidden), jnp.float32),
             pltpu.VMEM((tail_rows(slots), hidden), jnp.float32),
-            pltpu.SemaphoreType.DMA((2,)),
-        ],
-        compiler_params=pltpu.CompilerParams(vmem_limit_bytes=(16 << 20) + 2 * sums),
+        ]
+        + [pltpu.VMEM(((n * per + 1) * UNIT, PART), jnp.float32)] * (2 * width // PART),
+        compiler_params=pltpu.CompilerParams(vmem_limit_bytes=(16 << 20) + held),
         cost_estimate=pl.CostEstimate(flops=flops, bytes_accessed=8 << 20, transcendentals=0),
         name="neighbour_terms",
-    )(ids, table, packed, xo, xp, wo, wp, so, sp)
+    )(ids, table, tbuf, xo, xp, wo, wp, so, sp)
 
 
 def combine_kernel(slots, rows, ways, own, *refs):
@@ -417,10 +407,10 @@
         CHUNKS, per, n, 4, ids, tile_src, tile_rows, tile_dst, send_list, send_count, tw, features,
         neighbour_weight_first, w_self1,
     )
-    tables, packs, (sel, xo, wo, so) = planned[:CHUNKS], planned[CHUNKS:2 * CHUNKS], planned[2 * CHUNKS:]
+    tables, tbufs, (sel, xo, wo, so) = planned[:CHUNKS], planned[CHUNKS:2 * CHUNKS], planned[2 * CHUNKS:]
     done = []
     for chunk in range(CHUNKS):
-        parts = neighbour_terms(chunk, per, n, 4, groups, ids, tables[chunk], packs[chunk], xo, xp, wo, wp, so, sp)
+        parts = neighbour_terms(chunk, per, n, 4, groups, ids, tables[chunk], tbufs[chunk], xo, xp, wo, wp, so, sp)
         got = exchange(parts, 1, n)
         stride = 4
         for radix in radices[1:]:

time: 51.8 us -> 45.9 us (0.89); the launches traced: 52.2 us -> 45.4 us
  Pallas kernels: 16.6 us -> 12 us
  starting transfers between devices: 10.5 us -> 9.57 us
  waiting for transfers between devices: 14.2 us -> 13.5 us
  blocking collectives: 10.7 us -> 10.1 us
    pallas_call x1, Pallas kernels: 10.5 us -> 7.39 us  [neighbour_terms(): pl.pallas_call(functools.partial(tiles_kernel, chunk, per, n, radix, grou...]
    pallas_call x1, Pallas kernels: 4.27 us -> 2.76 us  [plan(): pl.pallas_call(functools.partial(plan_kernel, chunks, per, n, radix, n_sr...]
    ppermute x6, starting transfers between devices: 9.48 us -> 8.54 us  [exchange(): lax.ppermute(parts[k], 'dom', [(i, i ^ k * stride) for i in range(n)])]
    ppermute x6, waiting for transfers between devices: 13 us -> 12.3 us  [exchange(): lax.ppermute(parts[k], 'dom', [(i, i ^ k * stride) for i in range(n)])]
    all_to_all x1, blocking collectives: 10.7 us -> 10.1 us  [body(): received = lax.all_to_all(send, 'dom', 0, 0, tiled=True)]
  transfers between devices with their start and end apart: 10 -> 10, of which waited for: 5 -> 5; matrix products, arithmetic and copies ran while one was open for 0% -> 0% of each run, Pallas kernels for 8% -> 6%
where the time goes in v7:
time: 45.9 us; the launch traced here: 45.4 us
  waiting for transfers between devices  13.5 us (29%)
  Pallas kernels  12 us (26%)
  blocking collectives  10.1 us (22%)
  starting transfers between devices  9.57 us (21%)
    ppermute x6, waiting for transfers between devices, exchange(): lax.ppermute(parts[k], 'dom', [(i, i ^ k * stride) for i in range(n)])  12.3 us
    all_to_all x1, blocking collectives, body(): received = lax.all_to_all(send, 'dom', 0, 0, tiled=True)  10.1 us
    ppermute x6, starting transfers between devices, exchange(): lax.ppermute(parts[k], 'dom', [(i, i ^ k * stride) for i in range(n)])  8.54 us
    pallas_call x1, Pallas kernels, neighbour_terms(): pl.pallas_call(functools.partial(tiles_kernel, chunk, per, n, radix, grou...  7.39 us
    pallas_call x1, Pallas kernels, plan(): pl.pallas_call(functools.partial(plan_kernel, chunks, per, n, radix, n_sr...  2.76 us
    ppermute x1, waiting for transfers between devices, body(): other = lax.ppermute(own, 'feat', swap)  1.19 us
  transfers between devices with their start and end apart: 10, of which 5 were waited for; matrix products, arithmetic and copies ran while one was open for 0% of the time, Pallas kernels for 6%

profile of v7, /device:TPU:0, one launch (start us, length us, event | category | flops | bytes accessed | tf_op | source)
XLA Modules:
  0.0 45.4 jit_solution(12657060166069017866)
XLA Ops:
  0.0 0.5 collective-permute-start
  0.5 0.1 collective-permute-start.2
  0.5 0.5 collective-permute-start.1
  1.0 0.1 pad_add_fusion.ids
  1.0 2.8 %plan.1 = (s32[2,640]{1,0:T(2,128)S(1)}, bf16[512,16,128]{2,1,0:T(8,128)(2,1)S(1)}, bf16[128,128]{1,0:T(8,128)(2,1)S(1)}, bf16[1024,512]{1,0:T(8,128)(2,1)S(1)},...) custom-call(s32[2]{0:T(128)S(1)} %pad_add_fusion.ids, s32[1,128]{1,0:T(1,128)} %bitcast.17, ...), custom_call_target="tpu_custom_call" | custom-call | tf_op jit(solution)/shard_map/plan/pallas_call | solution.py:148
  3.8 0.0 collective-permute-done.2.sp
  3.8 0.0 collective-permute-done.1.wp
  3.8 0.0 collective-permute-done.xp
  3.8 0.0 copy-start
  3.8 0.0 copy-start.1
  3.9 0.0 copy-start.2
  3.9 7.4 %neighbour_terms.1 = (f32[256,256]{1,0:T(8,128)S(1)}, s16[272,256]{1,0:T(8,128)(2,1)S(1)}, s16[272,256]{1,0:T(8,128)(2,1)S(1)}, s16[272,256]{1,0:T(8,128)(2,1)S(1)}) custom-call(s32[2]{0:T(128)S(1)} %pad_add_fusion.ids, s32[2,640]{1,0:T(2,128)S(1)} %get-tuple-element.21.table, bf16[512,16,128]{2,1,0:T(8,128)(2,1)S(1)} %get-tuple-element.22.tbuf, ...), custom_call_target="tpu_custom_call" | custom-call | flops 3221225472 | bytes 8388608 | tf_op jit(solution)/shard_map/neighbour_terms/pallas_call | solution.py:248
  11.3 1.9 %collective-permute-start.3 = (s16[272,256]{1,0:T(8,128)(2,1)S(1)}, s16[272,256]{1,0:T(8,128)(2,1)S(1)}, u32[]{:S(2)}, u32[]{:S(2)}) collective-permute-start(s16[272,256]{1,0:T(8,128)(2,1)S(1)} %get-tuple-element.27), channel_id=1, source_target_pairs={{0,1},{1,0},{2,3},{3,2},{4,5},{5,4},{6,7},{7,6},{8,9},{9,8},{10,11... | collective-permute-start | bytes 417800 | tf_op jit(solution)/shard_map/ppermute | solution.py:375
  13.1 1.6 %collective-permute-start.4 = (s16[272,256]{1,0:T(8,128)(2,1)S(1)}, s16[272,256]{1,0:T(8,128)(2,1)S(1)}, u32[]{:S(2)}, u32[]{:S(2)}) collective-permute-start(s16[272,256]{1,0:T(8,128)(2,1)S(1)} %get-tuple-element.28), channel_id=1, source_target_pairs={{0,2},{1,3},{2,0},{3,1},{4,6},{5,7},{6,4},{7,5},{8,10},{9,11},{10,... | collective-permute-start | bytes 417800 | tf_op jit(solution)/shard_map/ppermute | solution.py:375
  14.7 0.1 collective-permute-start.5
  14.8 2.7 %collective-permute-done.3.refs_0_ = s16[272,256]{1,0:T(8,128)(2,1)S(1)} collective-permute-done((s16[272,256]{1,0:T(8,128)(2,1)S(1)}, s16[272,256]{1,0:T(8,128)(2,1)S(1)}, u32[]{:S(2)}, u32[]{:S(2)}) %collective-permute-start.3) | collective-permute-done | bytes 139296 | tf_op jit(solution)/shard_map/ppermute | solution.py:375
  17.5 4.2 %collective-permute-done.4.refs_1_ = s16[272,256]{1,0:T(8,128)(2,1)S(1)} collective-permute-done((s16[272,256]{1,0:T(8,128)(2,1)S(1)}, s16[272,256]{1,0:T(8,128)(2,1)S(1)}, u32[]{:S(2)}, u32[]{:S(2)}) %collective-permute-start.4) | collective-permute-done | bytes 139296 | tf_op jit(solution)/shard_map/ppermute | solution.py:375
  21.7 0.0 collective-permute-done.5.refs_2_
  21.7 0.2 combine.1
  21.9 1.7 %collective-permute-start.6 = (s16[80,256]{1,0:T(8,128)(2,1)S(1)}, s16[80,256]{1,0:T(8,128)(2,1)S(1)}, u32[]{:S(2)}, u32[]{:S(2)}) collective-permute-start(s16[80,256]{1,0:T(8,128)(2,1)S(1)} %get-tuple-element.31), channel_id=1, source_target_pairs={{0,4},{1,5},{2,6},{3,7},{4,0},{5,1},{6,2},{7,3},{8,12},{9,13},{10,... | collective-permute-start | bytes 122888 | tf_op jit(solution)/shard_map/ppermute | solution.py:375
  23.6 2.9 %collective-permute-start.7 = (s16[80,256]{1,0:T(8,128)(2,1)S(1)}, s16[80,256]{1,0:T(8,128)(2,1)S(1)}, u32[]{:S(2)}, u32[]{:S(2)}) collective-permute-start(s16[80,256]{1,0:T(8,128)(2,1)S(1)} %get-tuple-element.32), channel_id=1, source_target_pairs={{0,8},{1,9},{2,10},{3,11},{4,12},{5,13},{6,14},{7,15},{8,0},{9,1},... | collective-permute-start | bytes 122888 | tf_op jit(solution)/shard_map/ppermute | solution.py:375
  26.5 0.4 collective-permute-start.8
  26.9 0.0 collective-permute-done.6.refs_1_
  26.9 1.9 %collective-permute-done.7.refs_2_ = s16[80,256]{1,0:T(8,128)(2,1)S(1)} collective-permute-done((s16[80,256]{1,0:T(8,128)(2,1)S(1)}, s16[80,256]{1,0:T(8,128)(2,1)S(1)}, u32[]{:S(2)}, u32[]{:S(2)}) %collective-permute-start.7) | collective-permute-done | bytes 40992 | tf_op jit(solution)/shard_map/ppermute | solution.py:375
  28.8 3.5 %collective-permute-done.8.refs_3_ = s16[80,256]{1,0:T(8,128)(2,1)S(1)} collective-permute-done((s16[80,256]{1,0:T(8,128)(2,1)S(1)}, s16[80,256]{1,0:T(8,128)(2,1)S(1)}, u32[]{:S(2)}, u32[]{:S(2)}) %collective-permute-start.8) | collective-permute-done | bytes 40992 | tf_op jit(solution)/shard_map/ppermute | solution.py:375
  32.4 0.1 collective-permute-start.9
  32.4 1.2 %collective-permute-done.9.other = bf16[64,256]{1,0:T(8,128)(2,1)S(1)} collective-permute-done((bf16[64,256]{1,0:T(8,128)(2,1)S(1)}, bf16[64,256]{1,0:T(8,128)(2,1)S(1)}, u32[]{:S(2)}, u32[]{:S(2)}) %collective-permute-start.9) | collective-permute-done | bytes 32800 | tf_op jit(solution)/shard_map/ppermute | solution.py:423
  33.6 0.7 %rows_to_send.1 = (bf16[128,256]{1,0:T(8,128)(2,1)S(1)}, bf16[128,256]{1,0:T(8,128)(2,1)S(1)}) custom-call(s32[2]{0:T(128)S(1)} %pad_add_fusion.ids, bf16[64,256]{1,0:T(8,128)(2,1)S(1)} %hidden_rows.1.own, bf16[64,256]{1,0:T(8,128)(2,1)S(1)} %collective-permute-done.9.other, bf16[128,128]{1,0:T(8,128)(2,1)S(1)} %get-tuple-element.34.sel), custom_call_target="tpu_custom_call" | custom-call | tf_op jit(solution)/shard_map/rows_to_send/pallas_call | solution.py:337
  34.3 10.1 %all_to_all.11 = bf16[16,8,256]{2,1,0:T(8,128)(2,1)S(1)} all-to-all(bf16[16,8,256]{2,1,0:T(8,128)(2,1)S(1)} %bitcast.14), channel_id=1, replica_groups=mesh['feat'=2,'dom'=16] {'dom'}, dimensions={0} | all-to-all | bytes 131072 | tf_op jit(solution)/shard_map/all_to_all | solution.py:425
  44.5 0.0 copy-done
  44.5 0.0 copy-done.1
  44.5 0.0 copy-done.2
  44.5 0.9 %logits.1 = f32[64,172]{1,0:T(8,128)} custom-call(bf16[128,256]{1,0:T(8,128)(2,1)S(1)} %get-tuple-element.35.hidden, bf16[128,256]{1,0:T(8,128)(2,1)S(1)} %bitcast.11, bf16[64,256]{1,0:T(8,128)(2,1)S(1)} %copy-done.2, bf16[172,256]{1,0:T(8,128)(2,1)S(1)} %bitcast.12, bf16[172,256]{1,0:T(8,128)(2,1)S(1)} %bitcast.13), custom_call_target="tpu_custom_call" | custom-call | tf_op jit(solution)/shard_map/logits/pallas_call | solution.py:362
  (1 shorter events, 0.0 us)
Async XLA Ops:
  0.0 3.8 %collective-permute-start = (bf16[1024,512]{1,0:T(8,128)(2,1)}, bf16[1024,512]{1,0:T(8,128)(2,1)S(1)}, u32[]{:S(2)}, u32[]{:S(2)}) collective-permute-start(bf16[1024,512]{1,0:T(8,128)(2,1)} %xo.1), channel_id=1, source_target_pairs={{0,16},{16,0},{1,17},{17,1},{2,18},{18,2},{3,19},{19,3},{4,20},{20... | collective-permute-start | bytes 3145736 | tf_op jit(solution)/shard_map/ppermute | solution.py:402
  0.5 3.4 %collective-permute-start.2 = (bf16[512,256]{1,0:T(8,128)(2,1)}, bf16[512,256]{1,0:T(8,128)(2,1)S(1)}, u32[]{:S(2)}, u32[]{:S(2)}) collective-permute-start(bf16[512,256]{1,0:T(8,128)(2,1)} %so.1), channel_id=1, source_target_pairs={{0,16},{16,0},{1,17},{17,1},{2,18},{18,2},{3,19},{19,3},{4,20},{20... | collective-permute-start | bytes 786440 | tf_op jit(solution)/shard_map/ppermute | solution.py:404
  0.5 3.3 %collective-permute-start.1 = (bf16[512,256]{1,0:T(8,128)(2,1)}, bf16[512,256]{1,0:T(8,128)(2,1)S(1)}, u32[]{:S(2)}, u32[]{:S(2)}) collective-permute-start(bf16[512,256]{1,0:T(8,128)(2,1)} %wo.1), channel_id=1, source_target_pairs={{0,16},{16,0},{1,17},{17,1},{2,18},{18,2},{3,19},{19,3},{4,20},{20... | collective-permute-start | bytes 786440 | tf_op jit(solution)/shard_map/ppermute | solution.py:403
  3.8 40.6 %copy-start = (bf16[256,172]{0,1:T(8,128)(2,1)S(1)}, bf16[256,172]{0,1:T(8,128)(2,1)}, u32[]{:S(2)}) copy-start(bf16[256,172]{0,1:T(8,128)(2,1)} %param.22) | copy-start | bytes 264196
  3.8 40.6 %copy-start.1 = (bf16[256,172]{0,1:T(8,128)(2,1)S(1)}, bf16[256,172]{0,1:T(8,128)(2,1)}, u32[]{:S(2)}) copy-start(bf16[256,172]{0,1:T(8,128)(2,1)} %param.23) | copy-start | bytes 264196
  3.9 40.6 %copy-start.2 = (bf16[64,256]{1,0:T(8,128)(2,1)S(1)}, bf16[64,256]{1,0:T(8,128)(2,1)}, u32[]{:S(2)}) copy-start(bf16[64,256]{1,0:T(8,128)(2,1)} %adj.1) | copy-start | bytes 98308
  11.3 6.3 %collective-permute-start.3 = (s16[272,256]{1,0:T(8,128)(2,1)S(1)}, s16[272,256]{1,0:T(8,128)(2,1)S(1)}, u32[]{:S(2)}, u32[]{:S(2)}) collective-permute-start(s16[272,256]{1,0:T(8,128)(2,1)S(1)} %get-tuple-element.27), channel_id=1, source_target_pairs={{0,1},{1,0},{2,3},{3,2},{4,5},{5,4},{6,7},{7,6},{8,9},{9,8},{10,11... | collective-permute-start | bytes 417800 | tf_op jit(solution)/shard_map/ppermute | solution.py:375
  13.1 8.6 %collective-permute-start.4 = (s16[272,256]{1,0:T(8,128)(2,1)S(1)}, s16[272,256]{1,0:T(8,128)(2,1)S(1)}, u32[]{:S(2)}, u32[]{:S(2)}) collective-permute-start(s16[272,256]{1,0:T(8,128)(2,1)S(1)} %get-tuple-element.28), channel_id=1, source_target_pairs={{0,2},{1,3},{2,0},{3,1},{4,6},{5,7},{6,4},{7,5},{8,10},{9,11},{10,... | collective-permute-start | bytes 417800 | tf_op jit(solution)/shard_map/ppermute | solution.py:375
  14.7 7.0 %collective-permute-start.5 = (s16[272,256]{1,0:T(8,128)(2,1)S(1)}, s16[272,256]{1,0:T(8,128)(2,1)S(1)}, u32[]{:S(2)}, u32[]{:S(2)}) collective-permute-start(s16[272,256]{1,0:T(8,128)(2,1)S(1)} %get-tuple-element.29), channel_id=1, source_target_pairs={{0,3},{1,2},{2,1},{3,0},{4,7},{5,6},{6,5},{7,4},{8,11},{9,10},{10,... | collective-permute-start | bytes 417800 | tf_op jit(solution)/shard_map/ppermute | solution.py:375
  21.9 5.0 %collective-permute-start.6 = (s16[80,256]{1,0:T(8,128)(2,1)S(1)}, s16[80,256]{1,0:T(8,128)(2,1)S(1)}, u32[]{:S(2)}, u32[]{:S(2)}) collective-permute-start(s16[80,256]{1,0:T(8,128)(2,1)S(1)} %get-tuple-element.31), channel_id=1, source_target_pairs={{0,4},{1,5},{2,6},{3,7},{4,0},{5,1},{6,2},{7,3},{8,12},{9,13},{10,... | collective-permute-start | bytes 122888 | tf_op jit(solution)/shard_map/ppermute | solution.py:375
  23.6 5.2 %collective-permute-start.7 = (s16[80,256]{1,0:T(8,128)(2,1)S(1)}, s16[80,256]{1,0:T(8,128)(2,1)S(1)}, u32[]{:S(2)}, u32[]{:S(2)}) collective-permute-start(s16[80,256]{1,0:T(8,128)(2,1)S(1)} %get-tuple-element.32), channel_id=1, source_target_pairs={{0,8},{1,9},{2,10},{3,11},{4,12},{5,13},{6,14},{7,15},{8,0},{9,1},... | collective-permute-start | bytes 122888 | tf_op jit(solution)/shard_map/ppermute | solution.py:375
  26.5 5.8 %collective-permute-start.8 = (s16[80,256]{1,0:T(8,128)(2,1)S(1)}, s16[80,256]{1,0:T(8,128)(2,1)S(1)}, u32[]{:S(2)}, u32[]{:S(2)}) collective-permute-start(s16[80,256]{1,0:T(8,128)(2,1)S(1)} %get-tuple-element.33), channel_id=1, source_target_pairs={{0,12},{1,13},{2,14},{3,15},{4,8},{5,9},{6,10},{7,11},{8,4},{9,5},... | collective-permute-start | bytes 122888 | tf_op jit(solution)/shard_map/ppermute | solution.py:375
  32.4 1.3 %collective-permute-start.9 = (bf16[64,256]{1,0:T(8,128)(2,1)S(1)}, bf16[64,256]{1,0:T(8,128)(2,1)S(1)}, u32[]{:S(2)}, u32[]{:S(2)}) collective-permute-start(bf16[64,256]{1,0:T(8,128)(2,1)S(1)} %hidden_rows.1.own), channel_id=1, source_target_pairs={{0,16},{16,0},{1,17},{17,1},{2,18},{18,2},{3,19},{19,3},{4,20},{20... | collective-permute-start | bytes 98312 | tf_op jit(solution)/shard_map/ppermute | solution.py:423

commit v8 on v7

--- a/solution.py
+++ b/solution.py
@@ -371,7 +371,7 @@
 
 def exchange(parts, stride, n):
     got = [parts[0]]
-    for k in range(1, len(parts)):
+    for k in reversed(range(1, len(parts))):
         got.append(lax.ppermute(parts[k], "dom", [(i, i ^ (k * stride)) for i in range(n)]))
     return got
 

time: 45.9 us -> 46 us (level)
  blocking collectives: 10.1 us -> 12 us
  waiting for transfers between devices: 13.5 us -> 11.8 us
  starting transfers between devices: 9.57 us -> 10.6 us
  Pallas kernels: 12 us -> 11.2 us
    all_to_all x1, blocking collectives: 10.1 us -> 12 us  [body(): received = lax.all_to_all(send, 'dom', 0, 0, tiled=True)]
    ppermute x6, waiting for transfers between devices: 12.3 us -> 10.6 us  [exchange(): lax.ppermute(parts[k], 'dom', [(i, i ^ k * stride) for i in range(n)])]
    ppermute x6, starting transfers between devices: 8.54 us -> 9.6 us  [exchange(): lax.ppermute(parts[k], 'dom', [(i, i ^ k * stride) for i in range(n)])]
    pallas_call x1, Pallas kernels: 7.39 us -> 6.56 us  [neighbour_terms(): pl.pallas_call(functools.partial(tiles_kernel, chunk, per, n, radix, grou...]
where the time goes in v8:
time: 46 us; the launch traced here: 45.8 us
  blocking collectives  12 us (26%)
  waiting for transfers between devices  11.8 us (26%)
  Pallas kernels  11.2 us (24%)
  starting transfers between devices  10.6 us (23%)
    all_to_all x1, blocking collectives, body(): received = lax.all_to_all(send, 'dom', 0, 0, tiled=True)  12 us
    ppermute x6, waiting for transfers between devices, exchange(): lax.ppermute(parts[k], 'dom', [(i, i ^ k * stride) for i in range(n)])  10.6 us
    ppermute x6, starting transfers between devices, exchange(): lax.ppermute(parts[k], 'dom', [(i, i ^ k * stride) for i in range(n)])  9.6 us
    pallas_call x1, Pallas kernels, neighbour_terms(): pl.pallas_call(functools.partial(tiles_kernel, chunk, per, n, radix, grou...  6.56 us
    pallas_call x1, Pallas kernels, plan(): pl.pallas_call(functools.partial(plan_kernel, chunks, per, n, radix, n_sr...  2.76 us
    ppermute x1, waiting for transfers between devices, body(): other = lax.ppermute(own, 'feat', swap)  1.19 us
  transfers between devices with their start and end apart: 10, of which 5 were waited for; matrix products, arithmetic and copies ran while one was open for 0% of the time, Pallas kernels for 6%

profile of v8, /device:TPU:0, one launch (start us, length us, event | category | flops | bytes accessed | tf_op | source)
XLA Modules:
  0.0 45.8 jit_solution(3859928446334013935)
XLA Ops:
  0.0 0.5 collective-permute-start
  0.5 0.1 collective-permute-start.2
  0.5 0.5 collective-permute-start.1
  1.0 0.1 pad_add_fusion.ids
  1.0 2.8 %plan.1 = (s32[2,640]{1,0:T(2,128)S(1)}, bf16[512,16,128]{2,1,0:T(8,128)(2,1)S(1)}, bf16[128,128]{1,0:T(8,128)(2,1)S(1)}, bf16[1024,512]{1,0:T(8,128)(2,1)S(1)},...) custom-call(s32[2]{0:T(128)S(1)} %pad_add_fusion.ids, s32[1,128]{1,0:T(1,128)} %bitcast.17, ...), custom_call_target="tpu_custom_call" | custom-call | tf_op jit(solution)/shard_map/plan/pallas_call | solution.py:148
  3.8 0.0 collective-permute-done.2.sp
  3.8 0.0 collective-permute-done.1.wp
  3.8 0.0 collective-permute-done.xp
  3.8 0.0 copy-start
  3.8 0.0 copy-start.1
  3.9 0.0 copy-start.2
  3.9 6.6 %neighbour_terms.1 = (f32[256,256]{1,0:T(8,128)S(1)}, s16[272,256]{1,0:T(8,128)(2,1)S(1)}, s16[272,256]{1,0:T(8,128)(2,1)S(1)}, s16[272,256]{1,0:T(8,128)(2,1)S(1)}) custom-call(s32[2]{0:T(128)S(1)} %pad_add_fusion.ids, s32[2,640]{1,0:T(2,128)S(1)} %get-tuple-element.21.table, bf16[512,16,128]{2,1,0:T(8,128)(2,1)S(1)} %get-tuple-element.22.tbuf, ...), custom_call_target="tpu_custom_call" | custom-call | flops 3221225472 | bytes 8388608 | tf_op jit(solution)/shard_map/neighbour_terms/pallas_call | solution.py:248
  10.4 4.5 %collective-permute-start.3 = (s16[272,256]{1,0:T(8,128)(2,1)S(1)}, s16[272,256]{1,0:T(8,128)(2,1)S(1)}, u32[]{:S(2)}, u32[]{:S(2)}) collective-permute-start(s16[272,256]{1,0:T(8,128)(2,1)S(1)} %get-tuple-element.27), channel_id=1, source_target_pairs={{0,3},{1,2},{2,1},{3,0},{4,7},{5,6},{6,5},{7,4},{8,11},{9,10},{10,... | collective-permute-start | bytes 417800 | tf_op jit(solution)/shard_map/ppermute | solution.py:375
  14.9 0.6 %collective-permute-start.4 = (s16[272,256]{1,0:T(8,128)(2,1)S(1)}, s16[272,256]{1,0:T(8,128)(2,1)S(1)}, u32[]{:S(2)}, u32[]{:S(2)}) collective-permute-start(s16[272,256]{1,0:T(8,128)(2,1)S(1)} %get-tuple-element.28), channel_id=1, source_target_pairs={{0,2},{1,3},{2,0},{3,1},{4,6},{5,7},{6,4},{7,5},{8,10},{9,11},{10,... | collective-permute-start | bytes 417800 | tf_op jit(solution)/shard_map/ppermute | solution.py:375
  15.5 0.1 collective-permute-start.5
  15.6 3.8 %collective-permute-done.3.refs_0_ = s16[272,256]{1,0:T(8,128)(2,1)S(1)} collective-permute-done((s16[272,256]{1,0:T(8,128)(2,1)S(1)}, s16[272,256]{1,0:T(8,128)(2,1)S(1)}, u32[]{:S(2)}, u32[]{:S(2)}) %collective-permute-start.3) | collective-permute-done | bytes 139296 | tf_op jit(solution)/shard_map/ppermute | solution.py:375
  19.4 2.7 %collective-permute-done.4.refs_1_ = s16[272,256]{1,0:T(8,128)(2,1)S(1)} collective-permute-done((s16[272,256]{1,0:T(8,128)(2,1)S(1)}, s16[272,256]{1,0:T(8,128)(2,1)S(1)}, u32[]{:S(2)}, u32[]{:S(2)}) %collective-permute-start.4) | collective-permute-done | bytes 139296 | tf_op jit(solution)/shard_map/ppermute | solution.py:375
  22.1 0.0 collective-permute-done.5.refs_2_
  22.1 0.2 combine.1
  22.3 3.7 %collective-permute-start.6 = (s16[80,256]{1,0:T(8,128)(2,1)S(1)}, s16[80,256]{1,0:T(8,128)(2,1)S(1)}, u32[]{:S(2)}, u32[]{:S(2)}) collective-permute-start(s16[80,256]{1,0:T(8,128)(2,1)S(1)} %get-tuple-element.31), channel_id=1, source_target_pairs={{0,12},{1,13},{2,14},{3,15},{4,8},{5,9},{6,10},{7,11},{8,4},{9,5},... | collective-permute-start | bytes 122888 | tf_op jit(solution)/shard_map/ppermute | solution.py:375
  26.0 0.0 collective-permute-start.7
  26.0 0.7 %collective-permute-start.8 = (s16[80,256]{1,0:T(8,128)(2,1)S(1)}, s16[80,256]{1,0:T(8,128)(2,1)S(1)}, u32[]{:S(2)}, u32[]{:S(2)}) collective-permute-start(s16[80,256]{1,0:T(8,128)(2,1)S(1)} %get-tuple-element.33), channel_id=1, source_target_pairs={{0,4},{1,5},{2,6},{3,7},{4,0},{5,1},{6,2},{7,3},{8,12},{9,13},{10,... | collective-permute-start | bytes 122888 | tf_op jit(solution)/shard_map/ppermute | solution.py:375
  26.7 1.8 %collective-permute-done.6.refs_1_ = s16[80,256]{1,0:T(8,128)(2,1)S(1)} collective-permute-done((s16[80,256]{1,0:T(8,128)(2,1)S(1)}, s16[80,256]{1,0:T(8,128)(2,1)S(1)}, u32[]{:S(2)}, u32[]{:S(2)}) %collective-permute-start.6) | collective-permute-done | bytes 40992 | tf_op jit(solution)/shard_map/ppermute | solution.py:375
  28.5 2.4 %collective-permute-done.7.refs_2_ = s16[80,256]{1,0:T(8,128)(2,1)S(1)} collective-permute-done((s16[80,256]{1,0:T(8,128)(2,1)S(1)}, s16[80,256]{1,0:T(8,128)(2,1)S(1)}, u32[]{:S(2)}, u32[]{:S(2)}) %collective-permute-start.7) | collective-permute-done | bytes 40992 | tf_op jit(solution)/shard_map/ppermute | solution.py:375
  30.9 0.0 collective-permute-done.8.refs_3_
  30.9 0.1 collective-permute-start.9
  31.0 1.2 %collective-permute-done.9.other = bf16[64,256]{1,0:T(8,128)(2,1)S(1)} collective-permute-done((bf16[64,256]{1,0:T(8,128)(2,1)S(1)}, bf16[64,256]{1,0:T(8,128)(2,1)S(1)}, u32[]{:S(2)}, u32[]{:S(2)}) %collective-permute-start.9) | collective-permute-done | bytes 32800 | tf_op jit(solution)/shard_map/ppermute | solution.py:423
  32.2 0.7 %rows_to_send.1 = (bf16[128,256]{1,0:T(8,128)(2,1)S(1)}, bf16[128,256]{1,0:T(8,128)(2,1)S(1)}) custom-call(s32[2]{0:T(128)S(1)} %pad_add_fusion.ids, bf16[64,256]{1,0:T(8,128)(2,1)S(1)} %hidden_rows.1.own, bf16[64,256]{1,0:T(8,128)(2,1)S(1)} %collective-permute-done.9.other, bf16[128,128]{1,0:T(8,128)(2,1)S(1)} %get-tuple-element.34.sel), custom_call_target="tpu_custom_call" | custom-call | tf_op jit(solution)/shard_map/rows_to_send/pallas_call | solution.py:337
  32.9 12.0 %all_to_all.11 = bf16[16,8,256]{2,1,0:T(8,128)(2,1)S(1)} all-to-all(bf16[16,8,256]{2,1,0:T(8,128)(2,1)S(1)} %bitcast.14), channel_id=1, replica_groups=mesh['feat'=2,'dom'=16] {'dom'}, dimensions={0} | all-to-all | bytes 131072 | tf_op jit(solution)/shard_map/all_to_all | solution.py:425
  44.9 0.0 copy-done
  44.9 0.0 copy-done.1
  44.9 0.0 copy-done.2
  44.9 0.9 %logits.1 = f32[64,172]{1,0:T(8,128)} custom-call(bf16[128,256]{1,0:T(8,128)(2,1)S(1)} %get-tuple-element.35.hidden, bf16[128,256]{1,0:T(8,128)(2,1)S(1)} %bitcast.11, bf16[64,256]{1,0:T(8,128)(2,1)S(1)} %copy-done.2, bf16[172,256]{1,0:T(8,128)(2,1)S(1)} %bitcast.12, bf16[172,256]{1,0:T(8,128)(2,1)S(1)} %bitcast.13), custom_call_target="tpu_custom_call" | custom-call | tf_op jit(solution)/shard_map/logits/pallas_call | solution.py:362
  (1 shorter events, 0.0 us)
Async XLA Ops:
  0.0 3.8 %collective-permute-start = (bf16[1024,512]{1,0:T(8,128)(2,1)}, bf16[1024,512]{1,0:T(8,128)(2,1)S(1)}, u32[]{:S(2)}, u32[]{:S(2)}) collective-permute-start(bf16[1024,512]{1,0:T(8,128)(2,1)} %xo.1), channel_id=1, source_target_pairs={{0,16},{16,0},{1,17},{17,1},{2,18},{18,2},{3,19},{19,3},{4,20},{20... | collective-permute-start | bytes 3145736 | tf_op jit(solution)/shard_map/ppermute | solution.py:402
  0.5 3.4 %collective-permute-start.2 = (bf16[512,256]{1,0:T(8,128)(2,1)}, bf16[512,256]{1,0:T(8,128)(2,1)S(1)}, u32[]{:S(2)}, u32[]{:S(2)}) collective-permute-start(bf16[512,256]{1,0:T(8,128)(2,1)} %so.1), channel_id=1, source_target_pairs={{0,16},{16,0},{1,17},{17,1},{2,18},{18,2},{3,19},{19,3},{4,20},{20... | collective-permute-start | bytes 786440 | tf_op jit(solution)/shard_map/ppermute | solution.py:404
  0.5 3.3 %collective-permute-start.1 = (bf16[512,256]{1,0:T(8,128)(2,1)}, bf16[512,256]{1,0:T(8,128)(2,1)S(1)}, u32[]{:S(2)}, u32[]{:S(2)}) collective-permute-start(bf16[512,256]{1,0:T(8,128)(2,1)} %wo.1), channel_id=1, source_target_pairs={{0,16},{16,0},{1,17},{17,1},{2,18},{18,2},{3,19},{19,3},{4,20},{20... | collective-permute-start | bytes 786440 | tf_op jit(solution)/shard_map/ppermute | solution.py:403
  3.8 41.1 %copy-start = (bf16[256,172]{0,1:T(8,128)(2,1)S(1)}, bf16[256,172]{0,1:T(8,128)(2,1)}, u32[]{:S(2)}) copy-start(bf16[256,172]{0,1:T(8,128)(2,1)} %param.22) | copy-start | bytes 264196
  3.8 41.1 %copy-start.1 = (bf16[256,172]{0,1:T(8,128)(2,1)S(1)}, bf16[256,172]{0,1:T(8,128)(2,1)}, u32[]{:S(2)}) copy-start(bf16[256,172]{0,1:T(8,128)(2,1)} %param.23) | copy-start | bytes 264196
  3.9 41.0 %copy-start.2 = (bf16[64,256]{1,0:T(8,128)(2,1)S(1)}, bf16[64,256]{1,0:T(8,128)(2,1)}, u32[]{:S(2)}) copy-start(bf16[64,256]{1,0:T(8,128)(2,1)} %adj.1) | copy-start | bytes 98308
  10.4 8.9 %collective-permute-start.3 = (s16[272,256]{1,0:T(8,128)(2,1)S(1)}, s16[272,256]{1,0:T(8,128)(2,1)S(1)}, u32[]{:S(2)}, u32[]{:S(2)}) collective-permute-start(s16[272,256]{1,0:T(8,128)(2,1)S(1)} %get-tuple-element.27), channel_id=1, source_target_pairs={{0,3},{1,2},{2,1},{3,0},{4,7},{5,6},{6,5},{7,4},{8,11},{9,10},{10,... | collective-permute-start | bytes 417800 | tf_op jit(solution)/shard_map/ppermute | solution.py:375
  14.9 7.1 %collective-permute-start.4 = (s16[272,256]{1,0:T(8,128)(2,1)S(1)}, s16[272,256]{1,0:T(8,128)(2,1)S(1)}, u32[]{:S(2)}, u32[]{:S(2)}) collective-permute-start(s16[272,256]{1,0:T(8,128)(2,1)S(1)} %get-tuple-element.28), channel_id=1, source_target_pairs={{0,2},{1,3},{2,0},{3,1},{4,6},{5,7},{6,4},{7,5},{8,10},{9,11},{10,... | collective-permute-start | bytes 417800 | tf_op jit(solution)/shard_map/ppermute | solution.py:375
  15.5 6.5 %collective-permute-start.5 = (s16[272,256]{1,0:T(8,128)(2,1)S(1)}, s16[272,256]{1,0:T(8,128)(2,1)S(1)}, u32[]{:S(2)}, u32[]{:S(2)}) collective-permute-start(s16[272,256]{1,0:T(8,128)(2,1)S(1)} %get-tuple-element.29), channel_id=1, source_target_pairs={{0,1},{1,0},{2,3},{3,2},{4,5},{5,4},{6,7},{7,6},{8,9},{9,8},{10,11... | collective-permute-start | bytes 417800 | tf_op jit(solution)/shard_map/ppermute | solution.py:375
  22.3 6.2 %collective-permute-start.6 = (s16[80,256]{1,0:T(8,128)(2,1)S(1)}, s16[80,256]{1,0:T(8,128)(2,1)S(1)}, u32[]{:S(2)}, u32[]{:S(2)}) collective-permute-start(s16[80,256]{1,0:T(8,128)(2,1)S(1)} %get-tuple-element.31), channel_id=1, source_target_pairs={{0,12},{1,13},{2,14},{3,15},{4,8},{5,9},{6,10},{7,11},{8,4},{9,5},... | collective-permute-start | bytes 122888 | tf_op jit(solution)/shard_map/ppermute | solution.py:375
  26.0 4.9 %collective-permute-start.7 = (s16[80,256]{1,0:T(8,128)(2,1)S(1)}, s16[80,256]{1,0:T(8,128)(2,1)S(1)}, u32[]{:S(2)}, u32[]{:S(2)}) collective-permute-start(s16[80,256]{1,0:T(8,128)(2,1)S(1)} %get-tuple-element.32), channel_id=1, source_target_pairs={{0,8},{1,9},{2,10},{3,11},{4,12},{5,13},{6,14},{7,15},{8,0},{9,1},... | collective-permute-start | bytes 122888 | tf_op jit(solution)/shard_map/ppermute | solution.py:375
  26.0 4.9 %collective-permute-start.8 = (s16[80,256]{1,0:T(8,128)(2,1)S(1)}, s16[80,256]{1,0:T(8,128)(2,1)S(1)}, u32[]{:S(2)}, u32[]{:S(2)}) collective-permute-start(s16[80,256]{1,0:T(8,128)(2,1)S(1)} %get-tuple-element.33), channel_id=1, source_target_pairs={{0,4},{1,5},{2,6},{3,7},{4,0},{5,1},{6,2},{7,3},{8,12},{9,13},{10,... | collective-permute-start | bytes 122888 | tf_op jit(solution)/shard_map/ppermute | solution.py:375
  30.9 1.3 %collective-permute-start.9 = (bf16[64,256]{1,0:T(8,128)(2,1)S(1)}, bf16[64,256]{1,0:T(8,128)(2,1)S(1)}, u32[]{:S(2)}, u32[]{:S(2)}) collective-permute-start(bf16[64,256]{1,0:T(8,128)(2,1)S(1)} %hidden_rows.1.own), channel_id=1, source_target_pairs={{0,16},{16,0},{1,17},{17,1},{2,18},{18,2},{3,19},{19,3},{4,20},{20... | collective-permute-start | bytes 98312 | tf_op jit(solution)/shard_map/ppermute | solution.py:423

commit v9 on v8

--- a/solution.py
+++ b/solution.py
@@ -125,7 +125,9 @@
     k_n = jnp.bitwise_and(q_n, slots - 1)
     for k in range(slots):
         picked = jnp.where(k_n == k, mine[k:k + 1, :], picked)
-    good = jnp.logical_and(lax.div(q_n, slots) == r_n, k_n < cnt)
+    block = lax.div(q_n, slots)
+    apart = jnp.bitwise_and(block, n // 2 - 1) * 2 + lax.div(block, n // 2)
+    good = jnp.logical_and(jnp.bitwise_xor(apart, me) == r_n, k_n < cnt)
     row = jnp.sum(jnp.where(good, picked + 1.0, 0.0), axis=1, keepdims=True) - 1.0
     lane = lax.broadcasted_iota(jnp.int32, (1, sel.shape[1]), 1).astype(jnp.float32)
     sel[...] = jnp.where(row == lane, 1.0, 0.0).astype(jnp.bfloat16)
@@ -320,53 +322,92 @@
     )(*flat)
 
 
-def send_kernel(groups, ids, own, other, sel, hidden, send):
+def send_kernel(groups, ways, ids, own, other, sel, hidden, *sends):
     core = ids[0]
     for i in range(groups // 2):
         mine = group_of(core, i, groups)
         theirs = group_of(1 - core, i, groups)
         hidden[pl.ds(pl.multiple_of(mine * UNIT, UNIT), UNIT), :] = own[i * UNIT:(i + 1) * UNIT, :]
         hidden[pl.ds(pl.multiple_of(theirs * UNIT, UNIT), UNIT), :] = other[i * UNIT:(i + 1) * UNIT, :]
-    send[...] = jnp.dot(sel[...], hidden[...], preferred_element_type=jnp.float32).astype(jnp.bfloat16)
-
-
-def rows_to_send(groups, ids, own, other, sel):
+    picked = jnp.dot(sel[...], hidden[...], preferred_element_type=jnp.float32).astype(jnp.bfloat16)
+    rows = sel.shape[0] // ways
+    for k in range(ways):
+        sends[k][...] = picked[k * rows:(k + 1) * rows, :]
+
+
+def rows_to_send(groups, ways, ids, own, other, sel):
     smem = pl.BlockSpec(memory_space=pltpu.SMEM)
     vmem = pl.BlockSpec(memory_space=pltpu.VMEM)
     width = own.shape[1]
     return pl.pallas_call(
-        functools.partial(send_kernel, groups),
-        out_shape=[
-            jax.ShapeDtypeStruct((groups * UNIT, width), jnp.bfloat16),
-            jax.ShapeDtypeStruct((sel.shape[0], width), jnp.bfloat16),
-        ],
+        functools.partial(send_kernel, groups, ways),
+        out_shape=[jax.ShapeDtypeStruct((groups * UNIT, width), jnp.bfloat16)]
+        + [jax.ShapeDtypeStruct((sel.shape[0] // ways, width), jnp.bfloat16)] * ways,
         in_specs=[smem] + [vmem] * 3,
-        out_specs=[vmem] * 2,
+        out_specs=[vmem] * (1 + ways),
         compiler_params=pltpu.CompilerParams(vmem_limit_bytes=32 * 1024 * 1024),
         name="rows_to_send",
     )(ids, own, other, sel)
 
 
-def logits_kernel(hidden, received, adj, w_self, w_neigh, out):
+def regroup_kernel(had, left, ways, slots, *refs):
+    parts = len(refs) - ways
+    values = [a[...].astype(jnp.float32) for a in refs[:parts]]
+    for k in range(ways):
+        pieces = []
+        for value in values:
+            for p in range(had):
+                for r in range(left // ways):
+                    at = (p * left + r * ways + k) * slots
+                    pieces.append(value[at:at + slots, :])
+        refs[parts + k][...] = jnp.concatenate(pieces, axis=0).astype(jnp.bfloat16)
+
+
+def regroup(had, left, ways, slots, arrays):
+    rows, width = arrays[0].shape
+    vmem = pl.BlockSpec(memory_space=pltpu.VMEM)
+    out = jax.ShapeDtypeStruct((len(arrays) * rows // ways, width), jnp.bfloat16)
+    return pl.pallas_call(
+        functools.partial(regroup_kernel, had, left, ways, slots),
+        out_shape=[out] * ways,
+        in_specs=[vmem] * len(arrays),
+        out_specs=[vmem] * ways,
+        compiler_params=pltpu.CompilerParams(vmem_limit_bytes=32 * 1024 * 1024),
+        name="regroup",
+    )(*arrays)
+
+
+def logits_kernel(order, slots, ids, hidden, adj, w_self, w_neigh, *refs):
+    arrived, (out, pool) = refs[:-2], refs[-2:]
+    me = ids[1]
     tile, rows = hidden.shape[0], adj.shape[0]
+    at = 0
+    for a in arrived:
+        value = a[...].astype(jnp.float32)
+        for i in range(a.shape[0] // slots):
+            sender = jnp.bitwise_xor(me, order[at])
+            pool[pl.ds(pl.multiple_of(sender * slots, slots), slots), :] = value[i * slots:(i + 1) * slots, :]
+            at += 1
     mean = jnp.dot(adj[:, :tile], hidden[...], preferred_element_type=jnp.float32)
-    mean = mean + jnp.dot(adj[:, tile:], received[...], preferred_element_type=jnp.float32)
+    mean = mean + jnp.dot(adj[:, tile:], pool[...].astype(jnp.bfloat16), preferred_element_type=jnp.float32)
     dims = (((1,), (1,)), ((), ()))
     got = lax.dot_general(hidden[:rows, :], w_self[...], dims, preferred_element_type=jnp.float32)
     got = got + lax.dot_general(mean.astype(jnp.bfloat16), w_neigh[...], dims, preferred_element_type=jnp.float32)
     out[...] = got
 
 
-def logits_of(hidden, received, adj, w_self, w_neigh):
-    vmem = pl.BlockSpec(memory_space=pltpu.VMEM)
-    return pl.pallas_call(
-        logits_kernel,
+def logits_of(order, slots, ids, hidden, adj, w_self, w_neigh, arrived):
+    smem = pl.BlockSpec(memory_space=pltpu.SMEM)
+    vmem = pl.BlockSpec(memory_space=pltpu.VMEM)
+    return pl.pallas_call(
+        functools.partial(logits_kernel, order, slots),
         out_shape=jax.ShapeDtypeStruct((adj.shape[0], w_self.shape[1]), jnp.float32),
-        in_specs=[vmem] * 5,
+        in_specs=[smem] + [vmem] * (4 + len(arrived)),
         out_specs=vmem,
+        scratch_shapes=[pltpu.VMEM((len(order) * slots, hidden.shape[1]), jnp.float32)],
         compiler_params=pltpu.CompilerParams(vmem_limit_bytes=32 * 1024 * 1024),
         name="logits",
-    )(hidden, received, adj, w_self.T, w_neigh.T)
+    )(ids, hidden, adj, w_self.T, w_neigh.T, *arrived)
 
 
 def exchange(parts, stride, n):
@@ -421,9 +462,18 @@
         done.append(got)
     own = hidden_rows(done, per * UNIT)
     other = lax.ppermute(own, "feat", swap)
-    hidden, send = rows_to_send(groups, ids, own, other, sel)
-    received = lax.all_to_all(send, "dom", 0, 0, tiled=True)
-    return logits_of(hidden, received, adj_two, w_self2, w_neigh2)
+    hidden, *sends = rows_to_send(groups, 2, ids, own, other, sel)
+    slots = send_list.shape[2]
+    arrived = exchange(sends, 1, n)
+    stride, order, last = 2, [0], [0, 1]
+    while stride < n:
+        sends = regroup(len(order), n // stride, 2, slots, arrived)
+        order = [k + v for k in last for v in order]
+        arrived = exchange(sends, stride, n)
+        last = [0, stride]
+        stride *= 2
+    order = tuple(k + v for k in last for v in order)
+    return logits_of(order, slots, ids, hidden, adj_two, w_self2, w_neigh2, arrived)
 
 
 def solution(mesh):

time: 46 us -> 51.1 us (1.11)
  waiting for transfers between devices: 11.8 us -> 24.8 us
  blocking collectives: 12 us -> 0 us
  starting transfers between devices: 10.6 us -> 14.6 us
    ppermute x6 -> x10, waiting for transfers between devices: 10.6 us -> 23.6 us  [exchange(): lax.ppermute(parts[k], 'dom', [(i, i ^ k * stride) for i in range(n)])]
    all_to_all x1 -> x0, blocking collectives: 12 us -> none  [body(): received = lax.all_to_all(send, 'dom', 0, 0, tiled=True)]
    ppermute x6 -> x10, starting transfers between devices: 9.6 us -> 13.6 us  [exchange(): lax.ppermute(parts[k], 'dom', [(i, i ^ k * stride) for i in range(n)])]
    pallas_call x2 -> x5, Pallas kernels: 1.6 us -> 2.18 us  [the longest x1 1.47 us: logits_of(): pl.pallas_call(functools.partial(logits_kernel, order, slots), out_shape=...]
  transfers between devices with their start and end apart: 10 -> 14, of which waited for: 5 -> 9; matrix products, arithmetic and copies ran while one was open for 0% -> 0% of each run, Pallas kernels for 6% -> 5%
where the time goes in v9:
time: 51.1 us; the launch traced here: 51.4 us
  waiting for transfers between devices  24.8 us (49%)
  starting transfers between devices  14.6 us (29%)
  Pallas kernels  11.7 us (23%)
    ppermute x10, waiting for transfers between devices, exchange(): lax.ppermute(parts[k], 'dom', [(i, i ^ k * stride) for i in range(n)])  23.6 us
    ppermute x10, starting transfers between devices, exchange(): lax.ppermute(parts[k], 'dom', [(i, i ^ k * stride) for i in range(n)])  13.6 us
    pallas_call x1, Pallas kernels, neighbour_terms(): pl.pallas_call(functools.partial(tiles_kernel, chunk, per, n, radix, grou...  6.53 us
    pallas_call x1, Pallas kernels, plan(): pl.pallas_call(functools.partial(plan_kernel, chunks, per, n, radix, n_sr...  2.76 us
    pallas_call x1, Pallas kernels, logits_of(): pl.pallas_call(functools.partial(logits_kernel, order, slots), out_shape=...  1.47 us
    ppermute x1, waiting for transfers between devices, body(): other = lax.ppermute(own, 'feat', swap)  1.19 us
  transfers between devices with their start and end apart: 14, of which 9 were waited for; matrix products, arithmetic and copies ran while one was open for 0% of the time, Pallas kernels for 5%

profile of v9, /device:TPU:0, one launch (start us, length us, event | category | flops | bytes accessed | tf_op | source)
XLA Modules:
  0.0 51.4 jit_solution(6717508812538353459)
XLA Ops:
  0.0 0.5 collective-permute-start
  0.5 0.1 collective-permute-start.2
  0.5 0.5 collective-permute-start.1
  1.0 0.1 pad_add_fusion.ids
  1.0 2.8 %plan.1 = (s32[2,640]{1,0:T(2,128)S(1)}, bf16[512,16,128]{2,1,0:T(8,128)(2,1)S(1)}, bf16[128,128]{1,0:T(8,128)(2,1)S(1)}, bf16[1024,512]{1,0:T(8,128)(2,1)S(1)},...) custom-call(s32[2]{0:T(128)S(1)} %pad_add_fusion.ids, s32[1,128]{1,0:T(1,128)} %bitcast.13, ...), custom_call_target="tpu_custom_call" | custom-call | tf_op jit(solution)/shard_map/plan/pallas_call | solution.py:150
  3.8 0.0 collective-permute-done.2.sp
  3.8 0.0 collective-permute-done.1.wp
  3.8 0.0 collective-permute-done.xp
  3.8 0.0 copy-start
  3.8 0.0 copy-start.1
  3.9 0.0 copy-start.2
  3.9 6.5 %neighbour_terms.1 = (f32[256,256]{1,0:T(8,128)S(1)}, s16[272,256]{1,0:T(8,128)(2,1)S(1)}, s16[272,256]{1,0:T(8,128)(2,1)S(1)}, s16[272,256]{1,0:T(8,128)(2,1)S(1)}) custom-call(s32[2]{0:T(128)S(1)} %pad_add_fusion.ids, s32[2,640]{1,0:T(2,128)S(1)} %get-tuple-element.28.table, bf16[512,16,128]{2,1,0:T(8,128)(2,1)S(1)} %get-tuple-element.29.tbuf, ...), custom_call_target="tpu_custom_call" | custom-call | flops 3221225472 | bytes 8388608 | tf_op jit(solution)/shard_map/neighbour_terms/pallas_call | solution.py:250
  10.4 4.6 %collective-permute-start.3 = (s16[272,256]{1,0:T(8,128)(2,1)S(1)}, s16[272,256]{1,0:T(8,128)(2,1)S(1)}, u32[]{:S(2)}, u32[]{:S(2)}) collective-permute-start(s16[272,256]{1,0:T(8,128)(2,1)S(1)} %get-tuple-element.34), channel_id=1, source_target_pairs={{0,3},{1,2},{2,1},{3,0},{4,7},{5,6},{6,5},{7,4},{8,11},{9,10},{10,... | collective-permute-start | bytes 417800 | tf_op jit(solution)/shard_map/ppermute | solution.py:416
  15.0 0.0 collective-permute-start.4
  15.0 0.6 %collective-permute-start.5 = (s16[272,256]{1,0:T(8,128)(2,1)S(1)}, s16[272,256]{1,0:T(8,128)(2,1)S(1)}, u32[]{:S(2)}, u32[]{:S(2)}) collective-permute-start(s16[272,256]{1,0:T(8,128)(2,1)S(1)} %get-tuple-element.36), channel_id=1, source_target_pairs={{0,1},{1,0},{2,3},{3,2},{4,5},{5,4},{6,7},{7,6},{8,9},{9,8},{10,11... | collective-permute-start | bytes 417800 | tf_op jit(solution)/shard_map/ppermute | solution.py:416
  15.7 3.8 %collective-permute-done.3.refs_0_ = s16[272,256]{1,0:T(8,128)(2,1)S(1)} collective-permute-done((s16[272,256]{1,0:T(8,128)(2,1)S(1)}, s16[272,256]{1,0:T(8,128)(2,1)S(1)}, u32[]{:S(2)}, u32[]{:S(2)}) %collective-permute-start.3) | collective-permute-done | bytes 139296 | tf_op jit(solution)/shard_map/ppermute | solution.py:416
  19.5 2.7 %collective-permute-done.4.refs_1_ = s16[272,256]{1,0:T(8,128)(2,1)S(1)} collective-permute-done((s16[272,256]{1,0:T(8,128)(2,1)S(1)}, s16[272,256]{1,0:T(8,128)(2,1)S(1)}, u32[]{:S(2)}, u32[]{:S(2)}) %collective-permute-start.4) | collective-permute-done | bytes 139296 | tf_op jit(solution)/shard_map/ppermute | solution.py:416
  22.2 0.0 collective-permute-done.5.refs_2_
  22.2 0.2 combine.1
  22.4 3.8 %collective-permute-start.6 = (s16[80,256]{1,0:T(8,128)(2,1)S(1)}, s16[80,256]{1,0:T(8,128)(2,1)S(1)}, u32[]{:S(2)}, u32[]{:S(2)}) collective-permute-start(s16[80,256]{1,0:T(8,128)(2,1)S(1)} %get-tuple-element.38), channel_id=1, source_target_pairs={{0,12},{1,13},{2,14},{3,15},{4,8},{5,9},{6,10},{7,11},{8,4},{9,5},... | collective-permute-start | bytes 122888 | tf_op jit(solution)/shard_map/ppermute | solution.py:416
  26.2 0.0 collective-permute-start.7
  26.2 0.6 %collective-permute-start.8 = (s16[80,256]{1,0:T(8,128)(2,1)S(1)}, s16[80,256]{1,0:T(8,128)(2,1)S(1)}, u32[]{:S(2)}, u32[]{:S(2)}) collective-permute-start(s16[80,256]{1,0:T(8,128)(2,1)S(1)} %get-tuple-element.40), channel_id=1, source_target_pairs={{0,4},{1,5},{2,6},{3,7},{4,0},{5,1},{6,2},{7,3},{8,12},{9,13},{10,... | collective-permute-start | bytes 122888 | tf_op jit(solution)/shard_map/ppermute | solution.py:416
  26.8 1.5 %collective-permute-done.6.refs_1_ = s16[80,256]{1,0:T(8,128)(2,1)S(1)} collective-permute-done((s16[80,256]{1,0:T(8,128)(2,1)S(1)}, s16[80,256]{1,0:T(8,128)(2,1)S(1)}, u32[]{:S(2)}, u32[]{:S(2)}) %collective-permute-start.6) | collective-permute-done | bytes 40992 | tf_op jit(solution)/shard_map/ppermute | solution.py:416
  28.4 2.7 %collective-permute-done.7.refs_2_ = s16[80,256]{1,0:T(8,128)(2,1)S(1)} collective-permute-done((s16[80,256]{1,0:T(8,128)(2,1)S(1)}, s16[80,256]{1,0:T(8,128)(2,1)S(1)}, u32[]{:S(2)}, u32[]{:S(2)}) %collective-permute-start.7) | collective-permute-done | bytes 40992 | tf_op jit(solution)/shard_map/ppermute | solution.py:416
  31.1 0.0 collective-permute-done.8.refs_3_
  31.1 0.1 collective-permute-start.9
  31.2 1.2 %collective-permute-done.9.other = bf16[64,256]{1,0:T(8,128)(2,1)S(1)} collective-permute-done((bf16[64,256]{1,0:T(8,128)(2,1)S(1)}, bf16[64,256]{1,0:T(8,128)(2,1)S(1)}, u32[]{:S(2)}, u32[]{:S(2)}) %collective-permute-start.9) | collective-permute-done | bytes 32800 | tf_op jit(solution)/shard_map/ppermute | solution.py:464
  32.4 0.7 %rows_to_send.1 = (bf16[128,256]{1,0:T(8,128)(2,1)S(1)}, bf16[64,256]{1,0:T(8,128)(2,1)S(1)}, bf16[64,256]{1,0:T(8,128)(2,1)S(1)}) custom-call(s32[2]{0:T(128)S(1)} %pad_add_fusion.ids, bf16[64,256]{1,0:T(8,128)(2,1)S(1)} %hidden_rows.1.own, bf16[64,256]{1,0:T(8,128)(2,1)S(1)} %collective-permute-done.9.other, bf16[128,128]{1,0:T(8,128)(2,1)S(1)} %get-tuple-element.41.sel), custom_call_target="tpu_custom_call" | custom-call | tf_op jit(solution)/shard_map/rows_to_send/pallas_call | solution.py:342
  33.1 0.8 %collective-permute-start.10 = (bf16[64,256]{1,0:T(8,128)(2,1)S(1)}, bf16[64,256]{1,0:T(8,128)(2,1)S(1)}, u32[]{:S(2)}, u32[]{:S(2)}) collective-permute-start(bf16[64,256]{1,0:T(8,128)(2,1)S(1)} %get-tuple-element.44), channel_id=1, source_target_pairs={{0,1},{1,0},{2,3},{3,2},{4,5},{5,4},{6,7},{7,6},{8,9},{9,8},{10,11... | collective-permute-start | bytes 98312 | tf_op jit(solution)/shard_map/ppermute | solution.py:416
  33.9 3.1 %collective-permute-done.10.refs_1_ = bf16[64,256]{1,0:T(8,128)(2,1)S(1)} collective-permute-done((bf16[64,256]{1,0:T(8,128)(2,1)S(1)}, bf16[64,256]{1,0:T(8,128)(2,1)S(1)}, u32[]{:S(2)}, u32[]{:S(2)}) %collective-permute-start.10) | collective-permute-done | bytes 32800 | tf_op jit(solution)/shard_map/ppermute | solution.py:416
  37.1 0.7 %collective-permute-start.11 = (bf16[64,256]{1,0:T(8,128)(2,1)S(1)}, bf16[64,256]{1,0:T(8,128)(2,1)S(1)}, u32[]{:S(2)}, u32[]{:S(2)}) collective-permute-start(bf16[64,256]{1,0:T(8,128)(2,1)S(1)} %get-tuple-element.46), channel_id=1, source_target_pairs={{0,2},{1,3},{2,0},{3,1},{4,6},{5,7},{6,4},{7,5},{8,10},{9,11},{10,... | collective-permute-start | bytes 98312 | tf_op jit(solution)/shard_map/ppermute | solution.py:416
  37.7 3.3 %collective-permute-done.11.refs_1_ = bf16[64,256]{1,0:T(8,128)(2,1)S(1)} collective-permute-done((bf16[64,256]{1,0:T(8,128)(2,1)S(1)}, bf16[64,256]{1,0:T(8,128)(2,1)S(1)}, u32[]{:S(2)}, u32[]{:S(2)}) %collective-permute-start.11) | collective-permute-done | bytes 32800 | tf_op jit(solution)/shard_map/ppermute | solution.py:416
  41.0 0.3 collective-permute-start.12
  41.4 3.6 %collective-permute-done.12.refs_1_ = bf16[64,256]{1,0:T(8,128)(2,1)S(1)} collective-permute-done((bf16[64,256]{1,0:T(8,128)(2,1)S(1)}, bf16[64,256]{1,0:T(8,128)(2,1)S(1)}, u32[]{:S(2)}, u32[]{:S(2)}) %collective-permute-start.12) | collective-permute-done | bytes 32800 | tf_op jit(solution)/shard_map/ppermute | solution.py:416
  44.9 2.0 %collective-permute-start.13 = (bf16[64,256]{1,0:T(8,128)(2,1)S(1)}, bf16[64,256]{1,0:T(8,128)(2,1)S(1)}, u32[]{:S(2)}, u32[]{:S(2)}) collective-permute-start(bf16[64,256]{1,0:T(8,128)(2,1)S(1)} %get-tuple-element.50), channel_id=1, source_target_pairs={{0,8},{1,9},{2,10},{3,11},{4,12},{5,13},{6,14},{7,15},{8,0},{9,1},... | collective-permute-start | bytes 98312 | tf_op jit(solution)/shard_map/ppermute | solution.py:416
  47.0 2.9 %collective-permute-done.13.refs_1_ = bf16[64,256]{1,0:T(8,128)(2,1)S(1)} collective-permute-done((bf16[64,256]{1,0:T(8,128)(2,1)S(1)}, bf16[64,256]{1,0:T(8,128)(2,1)S(1)}, u32[]{:S(2)}, u32[]{:S(2)}) %collective-permute-start.13) | collective-permute-done | bytes 32800 | tf_op jit(solution)/shard_map/ppermute | solution.py:416
  49.9 0.0 copy-done
  49.9 0.0 copy-done.1
  49.9 0.0 copy-done.2
  49.9 1.5 %logits.1 = f32[64,172]{1,0:T(8,128)} custom-call(s32[2]{0:T(128)S(1)} %pad_add_fusion.ids, bf16[128,256]{1,0:T(8,128)(2,1)S(1)} %get-tuple-element.42.hidden, bf16[64,256]{1,0:T(8,128)(2,1)S(1)} %copy-done.2, bf16[172,256]{1,0:T(8,128)(2,1)S(1)} %bitcast.9, bf16[172,256]{1,0:T(8,128)(2,1)S(1)} %bitcast.10, bf16[64,256]{1,0:T(8,128)(2,1)S(1)} %get-tuple-element.49.refs_0_, ...), custom_call_target="tpu_custom_call" | custom-call | tf_op jit(solution)/shard_map/logits/pallas_call | solution.py:402
  (4 shorter events, 0.1 us)
Async XLA Ops:
  0.0 3.8 %collective-permute-start = (bf16[1024,512]{1,0:T(8,128)(2,1)}, bf16[1024,512]{1,0:T(8,128)(2,1)S(1)}, u32[]{:S(2)}, u32[]{:S(2)}) collective-permute-start(bf16[1024,512]{1,0:T(8,128)(2,1)} %xo.1), channel_id=1, source_target_pairs={{0,16},{16,0},{1,17},{17,1},{2,18},{18,2},{3,19},{19,3},{4,20},{20... | collective-permute-start | bytes 3145736 | tf_op jit(solution)/shard_map/ppermute | solution.py:443
  0.5 3.4 %collective-permute-start.2 = (bf16[512,256]{1,0:T(8,128)(2,1)}, bf16[512,256]{1,0:T(8,128)(2,1)S(1)}, u32[]{:S(2)}, u32[]{:S(2)}) collective-permute-start(bf16[512,256]{1,0:T(8,128)(2,1)} %so.1), channel_id=1, source_target_pairs={{0,16},{16,0},{1,17},{17,1},{2,18},{18,2},{3,19},{19,3},{4,20},{20... | collective-permute-start | bytes 786440 | tf_op jit(solution)/shard_map/ppermute | solution.py:445
  0.5 3.3 %collective-permute-start.1 = (bf16[512,256]{1,0:T(8,128)(2,1)}, bf16[512,256]{1,0:T(8,128)(2,1)S(1)}, u32[]{:S(2)}, u32[]{:S(2)}) collective-permute-start(bf16[512,256]{1,0:T(8,128)(2,1)} %wo.1), channel_id=1, source_target_pairs={{0,16},{16,0},{1,17},{17,1},{2,18},{18,2},{3,19},{19,3},{4,20},{20... | collective-permute-start | bytes 786440 | tf_op jit(solution)/shard_map/ppermute | solution.py:444
  3.8 46.0 %copy-start = (bf16[256,172]{0,1:T(8,128)(2,1)S(1)}, bf16[256,172]{0,1:T(8,128)(2,1)}, u32[]{:S(2)}) copy-start(bf16[256,172]{0,1:T(8,128)(2,1)} %param.22) | copy-start | bytes 264196
  3.8 46.0 %copy-start.1 = (bf16[256,172]{0,1:T(8,128)(2,1)S(1)}, bf16[256,172]{0,1:T(8,128)(2,1)}, u32[]{:S(2)}) copy-start(bf16[256,172]{0,1:T(8,128)(2,1)} %param.23) | copy-start | bytes 264196
  3.9 46.0 %copy-start.2 = (bf16[64,256]{1,0:T(8,128)(2,1)S(1)}, bf16[64,256]{1,0:T(8,128)(2,1)}, u32[]{:S(2)}) copy-start(bf16[64,256]{1,0:T(8,128)(2,1)} %adj.1) | copy-start | bytes 98308
  10.4 9.1 %collective-permute-start.3 = (s16[272,256]{1,0:T(8,128)(2,1)S(1)}, s16[272,256]{1,0:T(8,128)(2,1)S(1)}, u32[]{:S(2)}, u32[]{:S(2)}) collective-permute-start(s16[272,256]{1,0:T(8,128)(2,1)S(1)} %get-tuple-element.34), channel_id=1, source_target_pairs={{0,3},{1,2},{2,1},{3,0},{4,7},{5,6},{6,5},{7,4},{8,11},{9,10},{10,... | collective-permute-start | bytes 417800 | tf_op jit(solution)/shard_map/ppermute | solution.py:416
  15.0 7.1 %collective-permute-start.4 = (s16[272,256]{1,0:T(8,128)(2,1)S(1)}, s16[272,256]{1,0:T(8,128)(2,1)S(1)}, u32[]{:S(2)}, u32[]{:S(2)}) collective-permute-start(s16[272,256]{1,0:T(8,128)(2,1)S(1)} %get-tuple-element.35), channel_id=1, source_target_pairs={{0,2},{1,3},{2,0},{3,1},{4,6},{5,7},{6,4},{7,5},{8,10},{9,11},{10,... | collective-permute-start | bytes 417800 | tf_op jit(solution)/shard_map/ppermute | solution.py:416
  15.0 7.1 %collective-permute-start.5 = (s16[272,256]{1,0:T(8,128)(2,1)S(1)}, s16[272,256]{1,0:T(8,128)(2,1)S(1)}, u32[]{:S(2)}, u32[]{:S(2)}) collective-permute-start(s16[272,256]{1,0:T(8,128)(2,1)S(1)} %get-tuple-element.36), channel_id=1, source_target_pairs={{0,1},{1,0},{2,3},{3,2},{4,5},{5,4},{6,7},{7,6},{8,9},{9,8},{10,11... | collective-permute-start | bytes 417800 | tf_op jit(solution)/shard_map/ppermute | solution.py:416
  22.4 6.0 %collective-permute-start.6 = (s16[80,256]{1,0:T(8,128)(2,1)S(1)}, s16[80,256]{1,0:T(8,128)(2,1)S(1)}, u32[]{:S(2)}, u32[]{:S(2)}) collective-permute-start(s16[80,256]{1,0:T(8,128)(2,1)S(1)} %get-tuple-element.38), channel_id=1, source_target_pairs={{0,12},{1,13},{2,14},{3,15},{4,8},{5,9},{6,10},{7,11},{8,4},{9,5},... | collective-permute-start | bytes 122888 | tf_op jit(solution)/shard_map/ppermute | solution.py:416
  26.2 4.9 %collective-permute-start.7 = (s16[80,256]{1,0:T(8,128)(2,1)S(1)}, s16[80,256]{1,0:T(8,128)(2,1)S(1)}, u32[]{:S(2)}, u32[]{:S(2)}) collective-permute-start(s16[80,256]{1,0:T(8,128)(2,1)S(1)} %get-tuple-element.39), channel_id=1, source_target_pairs={{0,8},{1,9},{2,10},{3,11},{4,12},{5,13},{6,14},{7,15},{8,0},{9,1},... | collective-permute-start | bytes 122888 | tf_op jit(solution)/shard_map/ppermute | solution.py:416
  26.2 4.9 %collective-permute-start.8 = (s16[80,256]{1,0:T(8,128)(2,1)S(1)}, s16[80,256]{1,0:T(8,128)(2,1)S(1)}, u32[]{:S(2)}, u32[]{:S(2)}) collective-permute-start(s16[80,256]{1,0:T(8,128)(2,1)S(1)} %get-tuple-element.40), channel_id=1, source_target_pairs={{0,4},{1,5},{2,6},{3,7},{4,0},{5,1},{6,2},{7,3},{8,12},{9,13},{10,... | collective-permute-start | bytes 122888 | tf_op jit(solution)/shard_map/ppermute | solution.py:416
  31.1 1.3 %collective-permute-start.9 = (bf16[64,256]{1,0:T(8,128)(2,1)S(1)}, bf16[64,256]{1,0:T(8,128)(2,1)S(1)}, u32[]{:S(2)}, u32[]{:S(2)}) collective-permute-start(bf16[64,256]{1,0:T(8,128)(2,1)S(1)} %hidden_rows.1.own), channel_id=1, source_target_pairs={{0,16},{16,0},{1,17},{17,1},{2,18},{18,2},{3,19},{19,3},{4,20},{20... | collective-permute-start | bytes 98312 | tf_op jit(solution)/shard_map/ppermute | solution.py:464
  33.1 4.0 %collective-permute-start.10 = (bf16[64,256]{1,0:T(8,128)(2,1)S(1)}, bf16[64,256]{1,0:T(8,128)(2,1)S(1)}, u32[]{:S(2)}, u32[]{:S(2)}) collective-permute-start(bf16[64,256]{1,0:T(8,128)(2,1)S(1)} %get-tuple-element.44), channel_id=1, source_target_pairs={{0,1},{1,0},{2,3},{3,2},{4,5},{5,4},{6,7},{7,6},{8,9},{9,8},{10,11... | collective-permute-start | bytes 98312 | tf_op jit(solution)/shard_map/ppermute | solution.py:416
  37.1 3.9 %collective-permute-start.11 = (bf16[64,256]{1,0:T(8,128)(2,1)S(1)}, bf16[64,256]{1,0:T(8,128)(2,1)S(1)}, u32[]{:S(2)}, u32[]{:S(2)}) collective-permute-start(bf16[64,256]{1,0:T(8,128)(2,1)S(1)} %get-tuple-element.46), channel_id=1, source_target_pairs={{0,2},{1,3},{2,0},{3,1},{4,6},{5,7},{6,4},{7,5},{8,10},{9,11},{10,... | collective-permute-start | bytes 98312 | tf_op jit(solution)/shard_map/ppermute | solution.py:416
  41.0 3.9 %collective-permute-start.12 = (bf16[64,256]{1,0:T(8,128)(2,1)S(1)}, bf16[64,256]{1,0:T(8,128)(2,1)S(1)}, u32[]{:S(2)}, u32[]{:S(2)}) collective-permute-start(bf16[64,256]{1,0:T(8,128)(2,1)S(1)} %get-tuple-element.48), channel_id=1, source_target_pairs={{0,4},{1,5},{2,6},{3,7},{4,0},{5,1},{6,2},{7,3},{8,12},{9,13},{10,... | collective-permute-start | bytes 98312 | tf_op jit(solution)/shard_map/ppermute | solution.py:416
  44.9 4.9 %collective-permute-start.13 = (bf16[64,256]{1,0:T(8,128)(2,1)S(1)}, bf16[64,256]{1,0:T(8,128)(2,1)S(1)}, u32[]{:S(2)}, u32[]{:S(2)}) collective-permute-start(bf16[64,256]{1,0:T(8,128)(2,1)S(1)} %get-tuple-element.50), channel_id=1, source_target_pairs={{0,8},{1,9},{2,10},{3,11},{4,12},{5,13},{6,14},{7,15},{8,0},{9,1},... | collective-permute-start | bytes 98312 | tf_op jit(solution)/shard_map/ppermute | solution.py:416

commit v10 on v8

--- a/solution.py
+++ b/solution.py
@@ -127,8 +127,11 @@
         picked = jnp.where(k_n == k, mine[k:k + 1, :], picked)
     good = jnp.logical_and(lax.div(q_n, slots) == r_n, k_n < cnt)
     row = jnp.sum(jnp.where(good, picked + 1.0, 0.0), axis=1, keepdims=True) - 1.0
-    lane = lax.broadcasted_iota(jnp.int32, (1, sel.shape[1]), 1).astype(jnp.float32)
-    sel[...] = jnp.where(row == lane, 1.0, 0.0).astype(jnp.bfloat16)
+    lane = lax.broadcasted_iota(jnp.int32, (1, sel.shape[1]), 1)
+    name = jnp.zeros(lane.shape, jnp.int32)
+    for i, g in enumerate(gs + [group_of(1 - core, i, groups) for i in range(half)]):
+        name = jnp.where(lax.div(lane, UNIT) == i, g * UNIT + jnp.bitwise_and(lane, UNIT - 1), name)
+    sel[...] = jnp.where(row == name.astype(jnp.float32), 1.0, 0.0).astype(jnp.bfloat16)
 
     for c in copies[5:]:
         c.wait()
@@ -173,18 +176,20 @@
     ])
 
 
-def tiles_kernel(chunk, per, n, radix, groups, ids, table, tbuf, xo, xp, wo, wp, so, sp, *rest):
-    own, outs, rest = rest[0], rest[1:radix], rest[radix:]
-    masks, sums, tail, accs = rest[0], rest[1], rest[2], rest[3:]
+def tiles_kernel(table_v, tbuf, xo, xp, *rest):
+    parts = len(rest) - 3
+    accs, (masks, table, sem) = rest[:parts], rest[parts:]
     tile = tbuf.shape[2]
     width = xo.shape[1]
-    core = ids[0]
+    to_scalar = pltpu.make_async_copy(table_v, table, sem)
+    to_scalar.start()
     for acc in accs:
         acc[...] = jnp.zeros_like(acc)
     row_i = lax.broadcasted_iota(jnp.int32, (UNIT, tile), 0)
     for m in range(UNIT + 1):
         masks[m] = jnp.where(row_i < m, 1.0, 0.0).astype(jnp.bfloat16)
-    parts = [(x, w, h) for x, w in ((xo, wo), (xp, wp)) for h in range(0, width, PART)]
+    columns = [(x, h) for x in (xo, xp) for h in range(0, width, PART)]
+    to_scalar.wait()
 
     def step(i, carry):
         for m in range(STEP):
@@ -197,7 +202,7 @@
                 rows.append(tbuf[u] * masks[jnp.bitwise_and(word, 31)])
                 places.append(pl.multiple_of(lax.shift_right_logical(word, 14) * UNIT, UNIT))
             lhs = jnp.concatenate(rows, axis=0)
-            for acc, (x, _, h) in zip(accs, parts):
+            for acc, (x, h) in zip(accs, columns):
                 got = jnp.dot(lhs, x[pl.ds(base, tile), h:h + PART], preferred_element_type=jnp.float32)
                 got = got.astype(jnp.bfloat16).astype(jnp.float32)
                 for k in range(BLOCK):
@@ -207,59 +212,99 @@
     steps = lax.div(table[1, table.shape[1] - 1] + STEP - 1, STEP)
     lax.fori_loop(0, steps, step, 0)
 
-    slots, rows = n // radix, per * UNIT
-    size = min(256, slots * rows)
-    for k in range(radix):
-        out = own if k == 0 else sums
-
-        def weigh(r, carry):
-            at = pl.multiple_of(r * size, size)
-            got = jnp.zeros((size, out.shape[1]), jnp.float32)
-            for acc, (_, w, h) in zip(accs, parts):
-                value = acc[pl.ds(k * slots * rows + at, size), :]
-                high = value.astype(jnp.bfloat16)
-                low = (value - high.astype(jnp.float32)).astype(jnp.bfloat16)
-                got = got + jnp.dot(high, w[h:h + PART, :], preferred_element_type=jnp.float32)
-                got = got + jnp.dot(low, w[h:h + PART, :], preferred_element_type=jnp.float32)
-            out[pl.ds(at, size), :] = got
-            return carry
-
-        lax.fori_loop(0, slots * rows // size, weigh, 0)
-        if k == 0:
-            for j in range(per):
-                at = pl.multiple_of(group_of(core, chunk * per + j, groups) * UNIT, UNIT)
-                self = jnp.dot(xo[pl.ds(at, UNIT), :], so[...], preferred_element_type=jnp.float32)
-                self = self + jnp.dot(xp[pl.ds(at, UNIT), :], sp[...], preferred_element_type=jnp.float32)
-                out[j * UNIT:(j + 1) * UNIT, :] += self
-        else:
-            write_coded(outs[k - 1], tail, slots, rows, lambda s: sums[s * rows:(s + 1) * rows, :])
-
-
-def neighbour_terms(chunk, per, n, radix, groups, ids, table, tbuf, xo, xp, wo, wp, so, sp):
-    hidden = wo.shape[1]
+
+def gathered_sums(per, n, table, tbuf, xo, xp):
     width = xo.shape[1]
     tile = tbuf.shape[2]
-    smem = pl.BlockSpec(memory_space=pltpu.SMEM)
-    vmem = pl.BlockSpec(memory_space=pltpu.VMEM)
-    flops = 2 * tbuf.shape[0] * UNIT * tile * 2 * width + 4 * n * per * UNIT * 2 * width * hidden
-    slots, rows = n // radix, per * UNIT
-    held = (n * per + 1) * UNIT * 2 * width * 4
-    coded = jax.ShapeDtypeStruct((slots * rows + tail_rows(slots), hidden), jnp.int16)
-    return pl.pallas_call(
-        functools.partial(tiles_kernel, chunk, per, n, radix, groups),
-        out_shape=[jax.ShapeDtypeStruct((slots * rows, hidden), jnp.float32)] + [coded] * (radix - 1),
-        in_specs=[smem] * 2 + [vmem] * 7,
-        out_specs=[vmem] * radix,
+    vmem = pl.BlockSpec(memory_space=pltpu.VMEM)
+    flops = 2 * tbuf.shape[0] * UNIT * tile * 2 * width
+    parts = 2 * width // PART
+    sums = jax.ShapeDtypeStruct(((n * per + 1) * UNIT, PART), jnp.float32)
+    return pl.pallas_call(
+        tiles_kernel,
+        out_shape=[sums] * parts,
+        in_specs=[vmem] * 4,
+        out_specs=[vmem] * parts,
         scratch_shapes=[
             pltpu.VMEM((UNIT + 1, UNIT, tile), jnp.bfloat16),
+            pltpu.SMEM(table.shape, jnp.int32),
+            pltpu.SemaphoreType.DMA,
+        ],
+        compiler_params=pltpu.CompilerParams(vmem_limit_bytes=(12 << 20) + sums.size * 4 * parts),
+        cost_estimate=pl.CostEstimate(flops=flops, bytes_accessed=8 << 20, transcendentals=0),
+        name="gathered_sums",
+    )(table, tbuf, xo, xp)
+
+
+def weigh(accs, weights, first, count, out):
+    size = min(256, count)
+
+    def piece(r, carry):
+        at = pl.multiple_of(r * size, size)
+        got = jnp.zeros((size, out.shape[1]), jnp.float32)
+        for i, acc in enumerate(accs):
+            w, h = weights[i * PART // weights[0].shape[0]], i * PART % weights[0].shape[0]
+            value = acc[pl.ds(first + at, size), :]
+            high = value.astype(jnp.bfloat16)
+            low = (value - high.astype(jnp.float32)).astype(jnp.bfloat16)
+            got = got + jnp.dot(high, w[h:h + PART, :], preferred_element_type=jnp.float32)
+            got = got + jnp.dot(low, w[h:h + PART, :], preferred_element_type=jnp.float32)
+        out[pl.ds(at, size), :] = got
+        return carry
+
+    lax.fori_loop(0, count // size, piece, 0)
+
+
+def sent_kernel(k, slots, rows, parts, wo, wp, *refs):
+    accs, (out, sums, tail) = refs[:parts], refs[parts:]
+    weigh(accs, (wo, wp), k * slots * rows, slots * rows, sums)
+    write_coded(out, tail, slots, rows, lambda s: sums[s * rows:(s + 1) * rows, :])
+
+
+def sent_terms(k, slots, rows, accs, wo, wp):
+    hidden = wo.shape[1]
+    vmem = pl.BlockSpec(memory_space=pltpu.VMEM)
+    return pl.pallas_call(
+        functools.partial(sent_kernel, k, slots, rows, len(accs)),
+        out_shape=jax.ShapeDtypeStruct((slots * rows + tail_rows(slots), hidden), jnp.int16),
+        in_specs=[vmem] * (2 + len(accs)),
+        out_specs=vmem,
+        scratch_shapes=[
             pltpu.VMEM((slots * rows, hidden), jnp.float32),
             pltpu.VMEM((tail_rows(slots), hidden), jnp.float32),
-        ]
-        + [pltpu.VMEM(((n * per + 1) * UNIT, PART), jnp.float32)] * (2 * width // PART),
-        compiler_params=pltpu.CompilerParams(vmem_limit_bytes=(16 << 20) + held),
-        cost_estimate=pl.CostEstimate(flops=flops, bytes_accessed=8 << 20, transcendentals=0),
-        name="neighbour_terms",
-    )(ids, table, tbuf, xo, xp, wo, wp, so, sp)
+        ],
+        compiler_params=pltpu.CompilerParams(vmem_limit_bytes=(12 << 20) + accs[0].size * 4 * len(accs)),
+        cost_estimate=pl.CostEstimate(
+            flops=4 * slots * rows * PART * len(accs) * hidden, bytes_accessed=2 << 20, transcendentals=0),
+        name="sent_terms",
+    )(wo, wp, *accs)
+
+
+def own_kernel(chunk, per, groups, parts, ids, wo, wp, xo, xp, so, sp, *refs):
+    accs, out = refs[:parts], refs[parts]
+    weigh(accs, (wo, wp), 0, out.shape[0], out)
+    for j in range(per):
+        at = pl.multiple_of(group_of(ids[0], chunk * per + j, groups) * UNIT, UNIT)
+        self = jnp.dot(xo[pl.ds(at, UNIT), :], so[...], preferred_element_type=jnp.float32)
+        self = self + jnp.dot(xp[pl.ds(at, UNIT), :], sp[...], preferred_element_type=jnp.float32)
+        out[j * UNIT:(j + 1) * UNIT, :] += self
+
+
+def own_terms(chunk, per, groups, slots, ids, accs, wo, wp, xo, xp, so, sp):
+    hidden = wo.shape[1]
+    rows = per * UNIT
+    smem = pl.BlockSpec(memory_space=pltpu.SMEM)
+    vmem = pl.BlockSpec(memory_space=pltpu.VMEM)
+    return pl.pallas_call(
+        functools.partial(own_kernel, chunk, per, groups, len(accs)),
+        out_shape=jax.ShapeDtypeStruct((slots * rows, hidden), jnp.float32),
+        in_specs=[smem] + [vmem] * (6 + len(accs)),
+        out_specs=vmem,
+        compiler_params=pltpu.CompilerParams(vmem_limit_bytes=(12 << 20) + accs[0].size * 4 * len(accs)),
+        cost_estimate=pl.CostEstimate(
+            flops=4 * slots * rows * PART * len(accs) * hidden, bytes_accessed=2 << 20, transcendentals=0),
+        name="own_terms",
+    )(ids, wo, wp, xo, xp, so, sp, *accs)
 
 
 def combine_kernel(slots, rows, ways, own, *refs):
@@ -320,58 +365,77 @@
     )(*flat)
 
 
-def send_kernel(groups, ids, own, other, sel, hidden, send):
+def send_kernel(own, other, sel, send):
+    both = jnp.concatenate([own[...], other[...]], axis=0)
+    send[...] = jnp.dot(sel[...], both, preferred_element_type=jnp.float32).astype(jnp.bfloat16)
+
+
+def rows_to_send(own, other, sel):
+    vmem = pl.BlockSpec(memory_space=pltpu.VMEM)
+    return pl.pallas_call(
+        send_kernel,
+        out_shape=jax.ShapeDtypeStruct((sel.shape[0], own.shape[1]), jnp.bfloat16),
+        in_specs=[vmem] * 3,
+        out_specs=vmem,
+        compiler_params=pltpu.CompilerParams(vmem_limit_bytes=32 * 1024 * 1024),
+        name="rows_to_send",
+    )(own, other, sel)
+
+
+def local_kernel(groups, ids, own, other, adj, w_self, part, logits, hidden):
     core = ids[0]
     for i in range(groups // 2):
         mine = group_of(core, i, groups)
         theirs = group_of(1 - core, i, groups)
         hidden[pl.ds(pl.multiple_of(mine * UNIT, UNIT), UNIT), :] = own[i * UNIT:(i + 1) * UNIT, :]
         hidden[pl.ds(pl.multiple_of(theirs * UNIT, UNIT), UNIT), :] = other[i * UNIT:(i + 1) * UNIT, :]
-    send[...] = jnp.dot(sel[...], hidden[...], preferred_element_type=jnp.float32).astype(jnp.bfloat16)
-
-
-def rows_to_send(groups, ids, own, other, sel):
+    tile, rows = hidden.shape[0], adj.shape[0]
+    part[...] = jnp.dot(adj[:, :tile], hidden[...], preferred_element_type=jnp.float32)
+    dims = (((1,), (1,)), ((), ()))
+    logits[...] = lax.dot_general(hidden[:rows, :], w_self[...], dims, preferred_element_type=jnp.float32)
+
+
+def local_terms(groups, ids, own, other, adj, w_self):
     smem = pl.BlockSpec(memory_space=pltpu.SMEM)
     vmem = pl.BlockSpec(memory_space=pltpu.VMEM)
     width = own.shape[1]
     return pl.pallas_call(
-        functools.partial(send_kernel, groups),
+        functools.partial(local_kernel, groups),
         out_shape=[
-            jax.ShapeDtypeStruct((groups * UNIT, width), jnp.bfloat16),
-            jax.ShapeDtypeStruct((sel.shape[0], width), jnp.bfloat16),
+            jax.ShapeDtypeStruct((adj.shape[0], width), jnp.float32),
+            jax.ShapeDtypeStruct((adj.shape[0], w_self.shape[1]), jnp.float32),
         ],
-        in_specs=[smem] + [vmem] * 3,
+        in_specs=[smem] + [vmem] * 4,
         out_specs=[vmem] * 2,
+        scratch_shapes=[pltpu.VMEM((groups * UNIT, width), jnp.bfloat16)],
         compiler_params=pltpu.CompilerParams(vmem_limit_bytes=32 * 1024 * 1024),
-        name="rows_to_send",
-    )(ids, own, other, sel)
-
-
-def logits_kernel(hidden, received, adj, w_self, w_neigh, out):
-    tile, rows = hidden.shape[0], adj.shape[0]
-    mean = jnp.dot(adj[:, :tile], hidden[...], preferred_element_type=jnp.float32)
-    mean = mean + jnp.dot(adj[:, tile:], received[...], preferred_element_type=jnp.float32)
+        name="local_terms",
+    )(ids, own, other, adj, w_self.T)
+
+
+def logits_kernel(part, logits, received, adj, w_neigh, out):
+    tile = adj.shape[1] - received.shape[0]
+    mean = part[...] + jnp.dot(adj[:, tile:], received[...], preferred_element_type=jnp.float32)
     dims = (((1,), (1,)), ((), ()))
-    got = lax.dot_general(hidden[:rows, :], w_self[...], dims, preferred_element_type=jnp.float32)
-    got = got + lax.dot_general(mean.astype(jnp.bfloat16), w_neigh[...], dims, preferred_element_type=jnp.float32)
-    out[...] = got
-
-
-def logits_of(hidden, received, adj, w_self, w_neigh):
+    got = lax.dot_general(mean.astype(jnp.bfloat16), w_neigh[...], dims, preferred_element_type=jnp.float32)
+    out[...] = logits[...] + got
+
+
+def logits_of(part, logits, received, adj, w_neigh):
     vmem = pl.BlockSpec(memory_space=pltpu.VMEM)
     return pl.pallas_call(
         logits_kernel,
-        out_shape=jax.ShapeDtypeStruct((adj.shape[0], w_self.shape[1]), jnp.float32),
+        out_shape=jax.ShapeDtypeStruct(logits.shape, jnp.float32),
         in_specs=[vmem] * 5,
         out_specs=vmem,
         compiler_params=pltpu.CompilerParams(vmem_limit_bytes=32 * 1024 * 1024),
         name="logits",
-    )(hidden, received, adj, w_self.T, w_neigh.T)
-
-
-def exchange(parts, stride, n):
+    )(part, logits, received, adj, w_neigh.T)
+
+
+def exchange(parts, stride, n, places):
     got = [parts[0]]
-    for k in reversed(range(1, len(parts))):
+    for k in places:
         got.append(lax.ppermute(parts[k], "dom", [(i, i ^ (k * stride)) for i in range(n)]))
     return got
 
@@ -410,20 +474,24 @@
     tables, tbufs, (sel, xo, wo, so) = planned[:CHUNKS], planned[CHUNKS:2 * CHUNKS], planned[2 * CHUNKS:]
     done = []
     for chunk in range(CHUNKS):
-        parts = neighbour_terms(chunk, per, n, 4, groups, ids, tables[chunk], tbufs[chunk], xo, xp, wo, wp, so, sp)
-        got = exchange(parts, 1, n)
+        accs = gathered_sums(per, n, tables[chunk], tbufs[chunk], xo, xp)
+        slots, rows = n // 4, per * UNIT
+        parts = {k: sent_terms(k, slots, rows, accs, wo, wp) for k in (1, 2, 3)}
+        parts[0] = own_terms(chunk, per, groups, slots, ids, accs, wo, wp, xo, xp, so, sp)
+        got = exchange(parts, 1, n, (1, 2, 3))
         stride = 4
         for radix in radices[1:]:
             ways = 1 << radix
             parts = combine(n // stride, per * UNIT, ways, got[0], got[1:])
-            got = exchange(parts, stride, n)
+            got = exchange(parts, stride, n, range(ways - 1, 0, -1))
             stride *= ways
         done.append(got)
     own = hidden_rows(done, per * UNIT)
     other = lax.ppermute(own, "feat", swap)
-    hidden, send = rows_to_send(groups, ids, own, other, sel)
+    send = rows_to_send(own, other, sel)
     received = lax.all_to_all(send, "dom", 0, 0, tiled=True)
-    return logits_of(hidden, received, adj_two, w_self2, w_neigh2)
+    part, logits = local_terms(groups, ids, own, other, adj_two, w_self2)
+    return logits_of(part, logits, received, adj_two, w_neigh2)
 
 
 def solution(mesh):

time: 46 us -> 45.2 us (0.983); the launches traced: 45.8 us -> 44.5 us
  blocking collectives: 12 us -> 0 us
  waiting for transfers between devices: 11.8 us -> 16.8 us
  starting transfers between devices: 10.6 us -> 14.7 us
  Pallas kernels: 11.2 us -> 12.8 us
    all_to_all x1 -> x0, blocking collectives: 12 us -> none  [body(): received = lax.all_to_all(send, 'dom', 0, 0, tiled=True)]
    all_to_all x0 -> x1, waiting for transfers between devices: none -> 6.8 us  [body(): received = lax.all_to_all(send, 'dom', 0, 0, tiled=True)]
    all_to_all x0 -> x1, starting transfers between devices: none -> 4.68 us  [body(): received = lax.all_to_all(send, 'dom', 0, 0, tiled=True)]
    ppermute x6, waiting for transfers between devices: 10.6 us -> 8.8 us  [exchange(): lax.ppermute(parts[k], 'dom', [(i, i ^ k * stride) for i in range(n)])]
    pallas_call x3 -> x8, Pallas kernels: 8.17 us -> 9.83 us  [the longest x1 4.64 us: gathered_sums(): pl.pallas_call(tiles_kernel, out_shape=[sums] * parts, in_specs=[vmem] *...]
    ppermute x6, starting transfers between devices: 9.6 us -> 8.98 us  [exchange(): lax.ppermute(parts[k], 'dom', [(i, i ^ k * stride) for i in range(n)])]
  transfers between devices with their start and end apart: 10 -> 11, of which waited for: 5 -> 7; matrix products, arithmetic and copies ran while one was open for 0% -> 0% of each run, Pallas kernels for 6% -> 25%
where the time goes in v10:
time: 45.2 us; the launch traced here: 44.5 us
  waiting for transfers between devices  16.8 us (37%)
  starting transfers between devices  14.7 us (33%)
  Pallas kernels  12.8 us (28%)
    ppermute x6, starting transfers between devices, exchange(): lax.ppermute(parts[k], 'dom', [(i, i ^ k * stride) for i in range(n)])  8.98 us
    ppermute x6, waiting for transfers between devices, exchange(): lax.ppermute(parts[k], 'dom', [(i, i ^ k * stride) for i in range(n)])  8.8 us
    all_to_all x1, waiting for transfers between devices, body(): received = lax.all_to_all(send, 'dom', 0, 0, tiled=True)  6.8 us
    all_to_all x1, starting transfers between devices, body(): received = lax.all_to_all(send, 'dom', 0, 0, tiled=True)  4.68 us
    pallas_call x1, Pallas kernels, gathered_sums(): pl.pallas_call(tiles_kernel, out_shape=[sums] * parts, in_specs=[vmem] *...  4.64 us
    pallas_call x1, Pallas kernels, plan(): pl.pallas_call(functools.partial(plan_kernel, chunks, per, n, radix, n_sr...  2.76 us
    pallas_call x3, Pallas kernels, sent_terms(): pl.pallas_call(functools.partial(sent_kernel, k, slots, rows, len(accs)),...  1.56 us
    pallas_call x1, Pallas kernels, own_terms(): pl.pallas_call(functools.partial(own_kernel, chunk, per, groups, len(accs...  1.24 us
  transfers between devices with their start and end apart: 11, of which 7 were waited for; matrix products, arithmetic and copies ran while one was open for 0% of the time, Pallas kernels for 25%

profile of v10, /device:TPU:0, one launch (start us, length us, event | category | flops | bytes accessed | tf_op | source)
XLA Modules:
  0.0 44.5 jit_solution(13359027043460895136)
XLA Ops:
  0.0 0.5 %collective-permute-start.1 = (bf16[1024,512]{1,0:T(8,128)(2,1)}, bf16[1024,512]{1,0:T(8,128)(2,1)S(1)}, u32[]{:S(2)}, u32[]{:S(2)}) collective-permute-start(bf16[1024,512]{1,0:T(8,128)(2,1)} %xo.1), channel_id=1, source_target_pairs={{0,16},{16,0},{1,17},{17,1},{2,18},{18,2},{3,19},{19,3},{4,20},{20... | collective-permute-start | bytes 3145736 | tf_op jit(solution)/shard_map/ppermute | solution.py:466
  0.5 0.1 collective-permute-start
  0.5 0.5 %collective-permute-start.2 = (bf16[512,256]{1,0:T(8,128)(2,1)}, bf16[512,256]{1,0:T(8,128)(2,1)S(1)}, u32[]{:S(2)}, u32[]{:S(2)}) collective-permute-start(bf16[512,256]{1,0:T(8,128)(2,1)} %so.1), channel_id=1, source_target_pairs={{0,16},{16,0},{1,17},{17,1},{2,18},{18,2},{3,19},{19,3},{4,20},{20... | collective-permute-start | bytes 786440 | tf_op jit(solution)/shard_map/ppermute | solution.py:468
  1.0 0.1 pad_add_fusion.ids
  1.0 2.8 %plan.1 = (s32[2,640]{1,0:T(2,128)S(1)}, bf16[512,16,128]{2,1,0:T(8,128)(2,1)S(1)}, bf16[128,128]{1,0:T(8,128)(2,1)S(1)}, bf16[1024,512]{1,0:T(8,128)(2,1)S(1)},...) custom-call(s32[2]{0:T(128)S(1)} %pad_add_fusion.ids, s32[1,128]{1,0:T(1,128)} %bitcast.16, ...), custom_call_target="tpu_custom_call" | custom-call | tf_op jit(solution)/shard_map/plan/pallas_call | solution.py:151
  3.8 0.0 collective-permute-done.1.xp
  3.8 4.6 %gathered_sums.1 = (f32[1040,256]{1,0:T(8,128)S(1)}, f32[1040,256]{1,0:T(8,128)S(1)}, f32[1040,256]{1,0:T(8,128)S(1)}, f32[1040,256]{1,0:T(8,128)S(1)}) custom-call(s32[2,640]{1,0:T(2,128)S(1)} %get-tuple-element.24.table_v, bf16[512,16,128]{2,1,0:T(8,128)(2,1)S(1)} %get-tuple-element.25.tbuf, bf16[1024,512]{1,0:T(8,128)(2,1)S(1)} %get-tuple-element.22.xo, ...), custom_call_target="tpu_custom_call" | custom-call | flops 2147483648 | bytes 8388608 | tf_op jit(solution)/shard_map/gathered_sums/pallas_call | solution.py:223
  8.5 0.0 collective-permute-done.wp
  8.5 0.5 %sent_terms.5 = s16[272,256]{1,0:T(8,128)(2,1)S(1)} custom-call(bf16[512,256]{1,0:T(8,128)(2,1)S(1)} %get-tuple-element.21.wo, bf16[512,256]{1,0:T(8,128)(2,1)S(1)} %collective-permute-done.wp, f32[1040,256]{1,0:T(8,128)S(1)} %get-tuple-element.26.refs_0_, f32[1040,256]{1,0:T(8,128)S(1)} %get-tuple-element.27.refs_1_, ...), custom_call_target="tpu_custom_call" | custom-call | flops 268435456 | bytes 2097152 | tf_op jit(solution)/shard_map/sent_terms/pallas_call | solution.py:267
  9.0 3.5 %collective-permute-start.5 = (s16[272,256]{1,0:T(8,128)(2,1)S(1)}, s16[272,256]{1,0:T(8,128)(2,1)S(1)}, u32[]{:S(2)}, u32[]{:S(2)}) collective-permute-start(s16[272,256]{1,0:T(8,128)(2,1)S(1)} %sent_terms.5), channel_id=1, source_target_pairs={{0,3},{1,2},{2,1},{3,0},{4,7},{5,6},{6,5},{7,4},{8,11},{9,10},{10,... | collective-permute-start | bytes 417800 | tf_op jit(solution)/shard_map/ppermute | solution.py:439
  12.5 0.5 %sent_terms.4 = s16[272,256]{1,0:T(8,128)(2,1)S(1)} custom-call(bf16[512,256]{1,0:T(8,128)(2,1)S(1)} %get-tuple-element.21.wo, bf16[512,256]{1,0:T(8,128)(2,1)S(1)} %collective-permute-done.wp, f32[1040,256]{1,0:T(8,128)S(1)} %get-tuple-element.26.refs_0_, f32[1040,256]{1,0:T(8,128)S(1)} %get-tuple-element.27.refs_1_, ...), custom_call_target="tpu_custom_call" | custom-call | flops 268435456 | bytes 2097152 | tf_op jit(solution)/shard_map/sent_terms/pallas_call | solution.py:267
  13.0 0.6 %collective-permute-start.4 = (s16[272,256]{1,0:T(8,128)(2,1)S(1)}, s16[272,256]{1,0:T(8,128)(2,1)S(1)}, u32[]{:S(2)}, u32[]{:S(2)}) collective-permute-start(s16[272,256]{1,0:T(8,128)(2,1)S(1)} %sent_terms.4), channel_id=1, source_target_pairs={{0,2},{1,3},{2,0},{3,1},{4,6},{5,7},{6,4},{7,5},{8,10},{9,11},{10,... | collective-permute-start | bytes 417800 | tf_op jit(solution)/shard_map/ppermute | solution.py:439
  13.5 0.5 %sent_terms.3 = s16[272,256]{1,0:T(8,128)(2,1)S(1)} custom-call(bf16[512,256]{1,0:T(8,128)(2,1)S(1)} %get-tuple-element.21.wo, bf16[512,256]{1,0:T(8,128)(2,1)S(1)} %collective-permute-done.wp, f32[1040,256]{1,0:T(8,128)S(1)} %get-tuple-element.26.refs_0_, f32[1040,256]{1,0:T(8,128)S(1)} %get-tuple-element.27.refs_1_, ...), custom_call_target="tpu_custom_call" | custom-call | flops 268435456 | bytes 2097152 | tf_op jit(solution)/shard_map/sent_terms/pallas_call | solution.py:267
  14.1 0.1 collective-permute-start.3
  14.2 0.0 collective-permute-done.2.sp
  14.2 1.2 %own_terms.1.own = f32[256,256]{1,0:T(8,128)S(1)} custom-call(s32[2]{0:T(128)S(1)} %pad_add_fusion.ids, bf16[512,256]{1,0:T(8,128)(2,1)S(1)} %get-tuple-element.21.wo, bf16[512,256]{1,0:T(8,128)(2,1)S(1)} %collective-permute-done.wp, bf16[1024,512]{1,0:T(8,128)(2,1)S(1)} %get-tuple-element.22.xo, bf16[1024,512]{1,0:T(8,128)(2,1)S(1)} %collective-permute-done.1.xp, ...), custom_call_target="tpu_custom_call" | custom-call | flops 268435456 | bytes 2097152 | tf_op jit(solution)/shard_map/own_terms/pallas_call | solution.py:298
  15.5 0.0 copy-start
  15.5 0.0 copy-start.1
  15.5 0.0 copy-start.2
  15.5 1.4 %collective-permute-done.5.refs_2_ = s16[272,256]{1,0:T(8,128)(2,1)S(1)} collective-permute-done((s16[272,256]{1,0:T(8,128)(2,1)S(1)}, s16[272,256]{1,0:T(8,128)(2,1)S(1)}, u32[]{:S(2)}, u32[]{:S(2)}) %collective-permute-start.5) | collective-permute-done | bytes 139296 | tf_op jit(solution)/shard_map/ppermute | solution.py:439
  16.9 2.9 %collective-permute-done.4.refs_1_ = s16[272,256]{1,0:T(8,128)(2,1)S(1)} collective-permute-done((s16[272,256]{1,0:T(8,128)(2,1)S(1)}, s16[272,256]{1,0:T(8,128)(2,1)S(1)}, u32[]{:S(2)}, u32[]{:S(2)}) %collective-permute-start.4) | collective-permute-done | bytes 139296 | tf_op jit(solution)/shard_map/ppermute | solution.py:439
  19.8 0.3 collective-permute-done.3.refs_0_
  20.0 0.2 combine.1
  20.2 4.2 %collective-permute-start.6 = (s16[80,256]{1,0:T(8,128)(2,1)S(1)}, s16[80,256]{1,0:T(8,128)(2,1)S(1)}, u32[]{:S(2)}, u32[]{:S(2)}) collective-permute-start(s16[80,256]{1,0:T(8,128)(2,1)S(1)} %get-tuple-element.31), channel_id=1, source_target_pairs={{0,12},{1,13},{2,14},{3,15},{4,8},{5,9},{6,10},{7,11},{8,4},{9,5},... | collective-permute-start | bytes 122888 | tf_op jit(solution)/shard_map/ppermute | solution.py:439
  24.4 0.0 collective-permute-start.7
  24.4 0.6 %collective-permute-start.8 = (s16[80,256]{1,0:T(8,128)(2,1)S(1)}, s16[80,256]{1,0:T(8,128)(2,1)S(1)}, u32[]{:S(2)}, u32[]{:S(2)}) collective-permute-start(s16[80,256]{1,0:T(8,128)(2,1)S(1)} %get-tuple-element.33), channel_id=1, source_target_pairs={{0,4},{1,5},{2,6},{3,7},{4,0},{5,1},{6,2},{7,3},{8,12},{9,13},{10,... | collective-permute-start | bytes 122888 | tf_op jit(solution)/shard_map/ppermute | solution.py:439
  25.1 1.4 %collective-permute-done.6.refs_1_ = s16[80,256]{1,0:T(8,128)(2,1)S(1)} collective-permute-done((s16[80,256]{1,0:T(8,128)(2,1)S(1)}, s16[80,256]{1,0:T(8,128)(2,1)S(1)}, u32[]{:S(2)}, u32[]{:S(2)}) %collective-permute-start.6) | collective-permute-done | bytes 40992 | tf_op jit(solution)/shard_map/ppermute | solution.py:439
  26.4 2.9 %collective-permute-done.7.refs_2_ = s16[80,256]{1,0:T(8,128)(2,1)S(1)} collective-permute-done((s16[80,256]{1,0:T(8,128)(2,1)S(1)}, s16[80,256]{1,0:T(8,128)(2,1)S(1)}, u32[]{:S(2)}, u32[]{:S(2)}) %collective-permute-start.7) | collective-permute-done | bytes 40992 | tf_op jit(solution)/shard_map/ppermute | solution.py:439
  29.3 0.0 collective-permute-done.8.refs_3_
  29.4 0.1 collective-permute-start.9
  29.5 1.2 %collective-permute-done.9.other = bf16[64,256]{1,0:T(8,128)(2,1)S(1)} collective-permute-done((bf16[64,256]{1,0:T(8,128)(2,1)S(1)}, bf16[64,256]{1,0:T(8,128)(2,1)S(1)}, u32[]{:S(2)}, u32[]{:S(2)}) %collective-permute-start.9) | collective-permute-done | bytes 32800 | tf_op jit(solution)/shard_map/ppermute | solution.py:490
  30.6 0.8 %rows_to_send.1 = bf16[128,256]{1,0:T(8,128)(2,1)} custom-call(bf16[64,256]{1,0:T(8,128)(2,1)S(1)} %hidden_rows.1.own, bf16[64,256]{1,0:T(8,128)(2,1)S(1)} %collective-permute-done.9.other, bf16[128,128]{1,0:T(8,128)(2,1)S(1)} %get-tuple-element.36.sel), custom_call_target="tpu_custom_call" | custom-call | tf_op jit(solution)/shard_map/rows_to_send/pallas_call | solution.py:375
  31.4 4.7 %all-to-all-start = ((bf16[16,8,256]{2,1,0:T(8,128)(2,1)}), bf16[16,8,256]{2,1,0:T(8,128)(2,1)S(1)}, u32[]{:S(2)}, u32[]{:S(2)}) async-start(bf16[16,8,256]{2,1,0:T(8,128)(2,1)} %bitcast.8), calls=%async_computation | async-start | bytes 131072 | tf_op jit(solution)/shard_map/all_to_all | solution.py:492
  36.1 0.0 copy-done
  36.1 0.0 copy-done.1
  36.1 0.7 %local_terms.1 = (f32[64,256]{1,0:T(8,128)S(1)}, f32[64,172]{1,0:T(8,128)S(1)}) custom-call(s32[2]{0:T(128)S(1)} %pad_add_fusion.ids, bf16[64,256]{1,0:T(8,128)(2,1)S(1)} %hidden_rows.1.own, bf16[64,256]{1,0:T(8,128)(2,1)S(1)} %collective-permute-done.9.other, bf16[64,256]{1,0:T(8,128)(2,1)S(1)} %copy-done, bf16[172,256]{1,0:T(8,128)(2,1)S(1)} %bitcast.12), custom_call_target="tpu_custom_call" | custom-call | tf_op jit(solution)/shard_map/local_terms/pallas_call | solution.py:402
  36.9 6.8 %all-to-all-done = bf16[16,8,256]{2,1,0:T(8,128)(2,1)S(1)} async-done(((bf16[16,8,256]{2,1,0:T(8,128)(2,1)}), bf16[16,8,256]{2,1,0:T(8,128)(2,1)S(1)}, u32[]{:S(2)}, u32[]{:S(2)}) %all-to-all-start) | async-done | bytes 65568 | tf_op jit(solution)/shard_map/all_to_all | solution.py:492
  43.6 0.0 copy-done.2
  43.6 0.9 %logits.1 = f32[64,172]{1,0:T(8,128)} custom-call(f32[64,256]{1,0:T(8,128)S(1)} %get-tuple-element.34.part, f32[64,172]{1,0:T(8,128)S(1)} %get-tuple-element.35.logits, bf16[128,256]{1,0:T(8,128)(2,1)S(1)} %bitcast.11, bf16[64,256]{1,0:T(8,128)(2,1)S(1)} %copy-done, bf16[172,256]{1,0:T(8,128)(2,1)S(1)} %bitcast.13), custom_call_target="tpu_custom_call" | custom-call | tf_op jit(solution)/shard_map/logits/pallas_call | solution.py:426
  (1 shorter events, 0.0 us)
Async XLA Ops:
  0.0 3.8 %collective-permute-start.1 = (bf16[1024,512]{1,0:T(8,128)(2,1)}, bf16[1024,512]{1,0:T(8,128)(2,1)S(1)}, u32[]{:S(2)}, u32[]{:S(2)}) collective-permute-start(bf16[1024,512]{1,0:T(8,128)(2,1)} %xo.1), channel_id=1, source_target_pairs={{0,16},{16,0},{1,17},{17,1},{2,18},{18,2},{3,19},{19,3},{4,20},{20... | collective-permute-start | bytes 3145736 | tf_op jit(solution)/shard_map/ppermute | solution.py:466
  0.5 8.0 %collective-permute-start = (bf16[512,256]{1,0:T(8,128)(2,1)}, bf16[512,256]{1,0:T(8,128)(2,1)S(1)}, u32[]{:S(2)}, u32[]{:S(2)}) collective-permute-start(bf16[512,256]{1,0:T(8,128)(2,1)} %wo.1), channel_id=1, source_target_pairs={{0,16},{16,0},{1,17},{17,1},{2,18},{18,2},{3,19},{19,3},{4,20},{20... | collective-permute-start | bytes 786440 | tf_op jit(solution)/shard_map/ppermute | solution.py:467
  0.5 13.7 %collective-permute-start.2 = (bf16[512,256]{1,0:T(8,128)(2,1)}, bf16[512,256]{1,0:T(8,128)(2,1)S(1)}, u32[]{:S(2)}, u32[]{:S(2)}) collective-permute-start(bf16[512,256]{1,0:T(8,128)(2,1)} %so.1), channel_id=1, source_target_pairs={{0,16},{16,0},{1,17},{17,1},{2,18},{18,2},{3,19},{19,3},{4,20},{20... | collective-permute-start | bytes 786440 | tf_op jit(solution)/shard_map/ppermute | solution.py:468
  9.0 7.9 %collective-permute-start.5 = (s16[272,256]{1,0:T(8,128)(2,1)S(1)}, s16[272,256]{1,0:T(8,128)(2,1)S(1)}, u32[]{:S(2)}, u32[]{:S(2)}) collective-permute-start(s16[272,256]{1,0:T(8,128)(2,1)S(1)} %sent_terms.5), channel_id=1, source_target_pairs={{0,3},{1,2},{2,1},{3,0},{4,7},{5,6},{6,5},{7,4},{8,11},{9,10},{10,... | collective-permute-start | bytes 417800 | tf_op jit(solution)/shard_map/ppermute | solution.py:439
  13.0 6.8 %collective-permute-start.4 = (s16[272,256]{1,0:T(8,128)(2,1)S(1)}, s16[272,256]{1,0:T(8,128)(2,1)S(1)}, u32[]{:S(2)}, u32[]{:S(2)}) collective-permute-start(s16[272,256]{1,0:T(8,128)(2,1)S(1)} %sent_terms.4), channel_id=1, source_target_pairs={{0,2},{1,3},{2,0},{3,1},{4,6},{5,7},{6,4},{7,5},{8,10},{9,11},{10,... | collective-permute-start | bytes 417800 | tf_op jit(solution)/shard_map/ppermute | solution.py:439
  14.1 6.0 %collective-permute-start.3 = (s16[272,256]{1,0:T(8,128)(2,1)S(1)}, s16[272,256]{1,0:T(8,128)(2,1)S(1)}, u32[]{:S(2)}, u32[]{:S(2)}) collective-permute-start(s16[272,256]{1,0:T(8,128)(2,1)S(1)} %sent_terms.3), channel_id=1, source_target_pairs={{0,1},{1,0},{2,3},{3,2},{4,5},{5,4},{6,7},{7,6},{8,9},{9,8},{10,11... | collective-permute-start | bytes 417800 | tf_op jit(solution)/shard_map/ppermute | solution.py:439
  15.5 20.6 %copy-start = (bf16[64,256]{1,0:T(8,128)(2,1)S(1)}, bf16[64,256]{1,0:T(8,128)(2,1)}, u32[]{:S(2)}) copy-start(bf16[64,256]{1,0:T(8,128)(2,1)} %adj.3) | copy-start | bytes 98308
  15.5 20.6 %copy-start.1 = (bf16[256,172]{0,1:T(8,128)(2,1)S(1)}, bf16[256,172]{0,1:T(8,128)(2,1)}, u32[]{:S(2)}) copy-start(bf16[256,172]{0,1:T(8,128)(2,1)} %param.22) | copy-start | bytes 264196
  15.5 28.2 %copy-start.2 = (bf16[256,172]{0,1:T(8,128)(2,1)S(1)}, bf16[256,172]{0,1:T(8,128)(2,1)}, u32[]{:S(2)}) copy-start(bf16[256,172]{0,1:T(8,128)(2,1)} %param.23) | copy-start | bytes 264196
  20.2 6.2 %collective-permute-start.6 = (s16[80,256]{1,0:T(8,128)(2,1)S(1)}, s16[80,256]{1,0:T(8,128)(2,1)S(1)}, u32[]{:S(2)}, u32[]{:S(2)}) collective-permute-start(s16[80,256]{1,0:T(8,128)(2,1)S(1)} %get-tuple-element.31), channel_id=1, source_target_pairs={{0,12},{1,13},{2,14},{3,15},{4,8},{5,9},{6,10},{7,11},{8,4},{9,5},... | collective-permute-start | bytes 122888 | tf_op jit(solution)/shard_map/ppermute | solution.py:439
  24.4 4.9 %collective-permute-start.7 = (s16[80,256]{1,0:T(8,128)(2,1)S(1)}, s16[80,256]{1,0:T(8,128)(2,1)S(1)}, u32[]{:S(2)}, u32[]{:S(2)}) collective-permute-start(s16[80,256]{1,0:T(8,128)(2,1)S(1)} %get-tuple-element.32), channel_id=1, source_target_pairs={{0,8},{1,9},{2,10},{3,11},{4,12},{5,13},{6,14},{7,15},{8,0},{9,1},... | collective-permute-start | bytes 122888 | tf_op jit(solution)/shard_map/ppermute | solution.py:439
  24.4 4.9 %collective-permute-start.8 = (s16[80,256]{1,0:T(8,128)(2,1)S(1)}, s16[80,256]{1,0:T(8,128)(2,1)S(1)}, u32[]{:S(2)}, u32[]{:S(2)}) collective-permute-start(s16[80,256]{1,0:T(8,128)(2,1)S(1)} %get-tuple-element.33), channel_id=1, source_target_pairs={{0,4},{1,5},{2,6},{3,7},{4,0},{5,1},{6,2},{7,3},{8,12},{9,13},{10,... | collective-permute-start | bytes 122888 | tf_op jit(solution)/shard_map/ppermute | solution.py:439
  29.4 1.3 %collective-permute-start.9 = (bf16[64,256]{1,0:T(8,128)(2,1)S(1)}, bf16[64,256]{1,0:T(8,128)(2,1)S(1)}, u32[]{:S(2)}, u32[]{:S(2)}) collective-permute-start(bf16[64,256]{1,0:T(8,128)(2,1)S(1)} %hidden_rows.1.own), channel_id=1, source_target_pairs={{0,16},{16,0},{1,17},{17,1},{2,18},{18,2},{3,19},{19,3},{4,20},{20... | collective-permute-start | bytes 98312 | tf_op jit(solution)/shard_map/ppermute | solution.py:490
  31.4 12.2 %all-to-all-start = ((bf16[16,8,256]{2,1,0:T(8,128)(2,1)}), bf16[16,8,256]{2,1,0:T(8,128)(2,1)S(1)}, u32[]{:S(2)}, u32[]{:S(2)}) async-start(bf16[16,8,256]{2,1,0:T(8,128)(2,1)} %bitcast.8), calls=%async_computation | async-start | bytes 131072 | tf_op jit(solution)/shard_map/all_to_all | solution.py:492

commit v11 on v10

--- a/solution.py
+++ b/solution.py
@@ -125,7 +125,7 @@
     k_n = jnp.bitwise_and(q_n, slots - 1)
     for k in range(slots):
         picked = jnp.where(k_n == k, mine[k:k + 1, :], picked)
-    good = jnp.logical_and(lax.div(q_n, slots) == r_n, k_n < cnt)
+    good = jnp.logical_and(n - 1 - lax.div(q_n, slots) == r_n, k_n < cnt)
     row = jnp.sum(jnp.where(good, picked + 1.0, 0.0), axis=1, keepdims=True) - 1.0
     lane = lax.broadcasted_iota(jnp.int32, (1, sel.shape[1]), 1)
     name = jnp.zeros(lane.shape, jnp.int32)
@@ -413,18 +413,22 @@
     )(ids, own, other, adj, w_self.T)
 
 
-def logits_kernel(part, logits, received, adj, w_neigh, out):
-    tile = adj.shape[1] - received.shape[0]
-    mean = part[...] + jnp.dot(adj[:, tile:], received[...], preferred_element_type=jnp.float32)
+def logits_kernel(slots, part, logits, received, adj, w_neigh, out):
+    count = received.shape[0]
+    tile = adj.shape[1] - count
+    value = received[...].astype(jnp.float32)
+    rows = [value[at:at + slots, :] for at in range(count - slots, -1, -slots)]
+    rows = jnp.concatenate(rows, axis=0).astype(jnp.bfloat16)
+    mean = part[...] + jnp.dot(adj[:, tile:], rows, preferred_element_type=jnp.float32)
     dims = (((1,), (1,)), ((), ()))
     got = lax.dot_general(mean.astype(jnp.bfloat16), w_neigh[...], dims, preferred_element_type=jnp.float32)
     out[...] = logits[...] + got
 
 
-def logits_of(part, logits, received, adj, w_neigh):
-    vmem = pl.BlockSpec(memory_space=pltpu.VMEM)
-    return pl.pallas_call(
-        logits_kernel,
+def logits_of(slots, part, logits, received, adj, w_neigh):
+    vmem = pl.BlockSpec(memory_space=pltpu.VMEM)
+    return pl.pallas_call(
+        functools.partial(logits_kernel, slots),
         out_shape=jax.ShapeDtypeStruct(logits.shape, jnp.float32),
         in_specs=[vmem] * 5,
         out_specs=vmem,
@@ -489,9 +493,10 @@
     own = hidden_rows(done, per * UNIT)
     other = lax.ppermute(own, "feat", swap)
     send = rows_to_send(own, other, sel)
-    received = lax.all_to_all(send, "dom", 0, 0, tiled=True)
+    backwards = [list(range(n - 1, -1, -1))]
+    received = lax.all_to_all(send, "dom", 0, 0, axis_index_groups=backwards, tiled=True)
     part, logits = local_terms(groups, ids, own, other, adj_two, w_self2)
-    return logits_of(part, logits, received, adj_two, w_neigh2)
+    return logits_of(send_list.shape[2], part, logits, received, adj_two, w_neigh2)
 
 
 def solution(mesh):

time: 45.2 us -> 42.8 us (0.947)
  waiting for transfers between devices: 16.8 us -> 12.5 us
  starting transfers between devices: 14.7 us -> 17 us
    all_to_all x1, waiting for transfers between devices: 6.8 us -> 2.22 us  [body(): lax.all_to_all(send, 'dom', 0, 0, axis_index_groups=backwards, tiled=True)]
    all_to_all x1, starting transfers between devices: 4.68 us -> 6.92 us  [body(): lax.all_to_all(send, 'dom', 0, 0, axis_index_groups=backwards, tiled=True)]
  transfers between devices with their start and end apart: 11 -> 11, of which waited for: 7 -> 7; matrix products, arithmetic and copies ran while one was open for 0% -> 0% of each run, Pallas kernels for 25% -> 26%
where the time goes in v11:
time: 42.8 us; the launch traced here: 42.6 us
  starting transfers between devices  17 us (40%)
  Pallas kernels  12.8 us (30%)
  waiting for transfers between devices  12.5 us (29%)
    ppermute x6, starting transfers between devices, exchange(): lax.ppermute(parts[k], 'dom', [(i, i ^ k * stride) for i in range(n)])  9.09 us
    ppermute x6, waiting for transfers between devices, exchange(): lax.ppermute(parts[k], 'dom', [(i, i ^ k * stride) for i in range(n)])  9.08 us
    all_to_all x1, starting transfers between devices, body(): lax.all_to_all(send, 'dom', 0, 0, axis_index_groups=backwards, tiled=True)  6.92 us
    pallas_call x1, Pallas kernels, gathered_sums(): pl.pallas_call(tiles_kernel, out_shape=[sums] * parts, in_specs=[vmem] *...  4.63 us
    pallas_call x1, Pallas kernels, plan(): pl.pallas_call(functools.partial(plan_kernel, chunks, per, n, radix, n_sr...  2.76 us
    all_to_all x1, waiting for transfers between devices, body(): lax.all_to_all(send, 'dom', 0, 0, axis_index_groups=backwards, tiled=True)  2.22 us
    pallas_call x3, Pallas kernels, sent_terms(): pl.pallas_call(functools.partial(sent_kernel, k, slots, rows, len(accs)),...  1.53 us
    pallas_call x1, Pallas kernels, own_terms(): pl.pallas_call(functools.partial(own_kernel, chunk, per, groups, len(accs...  1.25 us
  transfers between devices with their start and end apart: 11, of which 7 were waited for; matrix products, arithmetic and copies ran while one was open for 0% of the time, Pallas kernels for 26%

profile of v11, /device:TPU:0, one launch (start us, length us, event | category | flops | bytes accessed | tf_op | source)
XLA Modules:
  0.0 42.6 jit_solution(14768826499093132388)
XLA Ops:
  0.0 0.5 %collective-permute-start.1 = (bf16[1024,512]{1,0:T(8,128)(2,1)}, bf16[1024,512]{1,0:T(8,128)(2,1)S(1)}, u32[]{:S(2)}, u32[]{:S(2)}) collective-permute-start(bf16[1024,512]{1,0:T(8,128)(2,1)} %xo.1), channel_id=1, source_target_pairs={{0,16},{16,0},{1,17},{17,1},{2,18},{18,2},{3,19},{19,3},{4,20},{20... | collective-permute-start | bytes 3145736 | tf_op jit(solution)/shard_map/ppermute | solution.py:470
  0.5 0.1 collective-permute-start
  0.5 0.5 %collective-permute-start.2 = (bf16[512,256]{1,0:T(8,128)(2,1)}, bf16[512,256]{1,0:T(8,128)(2,1)S(1)}, u32[]{:S(2)}, u32[]{:S(2)}) collective-permute-start(bf16[512,256]{1,0:T(8,128)(2,1)} %so.1), channel_id=1, source_target_pairs={{0,16},{16,0},{1,17},{17,1},{2,18},{18,2},{3,19},{19,3},{4,20},{20... | collective-permute-start | bytes 786440 | tf_op jit(solution)/shard_map/ppermute | solution.py:472
  1.0 0.1 pad_add_fusion.ids
  1.0 2.8 %plan.1 = (s32[2,640]{1,0:T(2,128)S(1)}, bf16[512,16,128]{2,1,0:T(8,128)(2,1)S(1)}, bf16[128,128]{1,0:T(8,128)(2,1)S(1)}, bf16[1024,512]{1,0:T(8,128)(2,1)S(1)},...) custom-call(s32[2]{0:T(128)S(1)} %pad_add_fusion.ids, s32[1,128]{1,0:T(1,128)} %bitcast.16, ...), custom_call_target="tpu_custom_call" | custom-call | tf_op jit(solution)/shard_map/plan/pallas_call | solution.py:151
  3.8 0.0 collective-permute-done.1.xp
  3.8 4.6 %gathered_sums.1 = (f32[1040,256]{1,0:T(8,128)S(1)}, f32[1040,256]{1,0:T(8,128)S(1)}, f32[1040,256]{1,0:T(8,128)S(1)}, f32[1040,256]{1,0:T(8,128)S(1)}) custom-call(s32[2,640]{1,0:T(2,128)S(1)} %get-tuple-element.24.table_v, bf16[512,16,128]{2,1,0:T(8,128)(2,1)S(1)} %get-tuple-element.25.tbuf, bf16[1024,512]{1,0:T(8,128)(2,1)S(1)} %get-tuple-element.22.xo, ...), custom_call_target="tpu_custom_call" | custom-call | flops 2147483648 | bytes 8388608 | tf_op jit(solution)/shard_map/gathered_sums/pallas_call | solution.py:223
  8.5 0.0 collective-permute-done.wp
  8.5 0.5 %sent_terms.5 = s16[272,256]{1,0:T(8,128)(2,1)S(1)} custom-call(bf16[512,256]{1,0:T(8,128)(2,1)S(1)} %get-tuple-element.21.wo, bf16[512,256]{1,0:T(8,128)(2,1)S(1)} %collective-permute-done.wp, f32[1040,256]{1,0:T(8,128)S(1)} %get-tuple-element.26.refs_0_, f32[1040,256]{1,0:T(8,128)S(1)} %get-tuple-element.27.refs_1_, ...), custom_call_target="tpu_custom_call" | custom-call | flops 268435456 | bytes 2097152 | tf_op jit(solution)/shard_map/sent_terms/pallas_call | solution.py:267
  9.0 3.4 %collective-permute-start.5 = (s16[272,256]{1,0:T(8,128)(2,1)S(1)}, s16[272,256]{1,0:T(8,128)(2,1)S(1)}, u32[]{:S(2)}, u32[]{:S(2)}) collective-permute-start(s16[272,256]{1,0:T(8,128)(2,1)S(1)} %sent_terms.5), channel_id=1, source_target_pairs={{0,3},{1,2},{2,1},{3,0},{4,7},{5,6},{6,5},{7,4},{8,11},{9,10},{10,... | collective-permute-start | bytes 417800 | tf_op jit(solution)/shard_map/ppermute | solution.py:443
  12.4 0.5 %sent_terms.4 = s16[272,256]{1,0:T(8,128)(2,1)S(1)} custom-call(bf16[512,256]{1,0:T(8,128)(2,1)S(1)} %get-tuple-element.21.wo, bf16[512,256]{1,0:T(8,128)(2,1)S(1)} %collective-permute-done.wp, f32[1040,256]{1,0:T(8,128)S(1)} %get-tuple-element.26.refs_0_, f32[1040,256]{1,0:T(8,128)S(1)} %get-tuple-element.27.refs_1_, ...), custom_call_target="tpu_custom_call" | custom-call | flops 268435456 | bytes 2097152 | tf_op jit(solution)/shard_map/sent_terms/pallas_call | solution.py:267
  12.9 0.7 %collective-permute-start.4 = (s16[272,256]{1,0:T(8,128)(2,1)S(1)}, s16[272,256]{1,0:T(8,128)(2,1)S(1)}, u32[]{:S(2)}, u32[]{:S(2)}) collective-permute-start(s16[272,256]{1,0:T(8,128)(2,1)S(1)} %sent_terms.4), channel_id=1, source_target_pairs={{0,2},{1,3},{2,0},{3,1},{4,6},{5,7},{6,4},{7,5},{8,10},{9,11},{10,... | collective-permute-start | bytes 417800 | tf_op jit(solution)/shard_map/ppermute | solution.py:443
  13.6 0.5 %sent_terms.3 = s16[272,256]{1,0:T(8,128)(2,1)S(1)} custom-call(bf16[512,256]{1,0:T(8,128)(2,1)S(1)} %get-tuple-element.21.wo, bf16[512,256]{1,0:T(8,128)(2,1)S(1)} %collective-permute-done.wp, f32[1040,256]{1,0:T(8,128)S(1)} %get-tuple-element.26.refs_0_, f32[1040,256]{1,0:T(8,128)S(1)} %get-tuple-element.27.refs_1_, ...), custom_call_target="tpu_custom_call" | custom-call | flops 268435456 | bytes 2097152 | tf_op jit(solution)/shard_map/sent_terms/pallas_call | solution.py:267
  14.1 0.1 collective-permute-start.3
  14.2 0.0 collective-permute-done.2.sp
  14.2 1.2 %own_terms.1.own = f32[256,256]{1,0:T(8,128)S(1)} custom-call(s32[2]{0:T(128)S(1)} %pad_add_fusion.ids, bf16[512,256]{1,0:T(8,128)(2,1)S(1)} %get-tuple-element.21.wo, bf16[512,256]{1,0:T(8,128)(2,1)S(1)} %collective-permute-done.wp, bf16[1024,512]{1,0:T(8,128)(2,1)S(1)} %get-tuple-element.22.xo, bf16[1024,512]{1,0:T(8,128)(2,1)S(1)} %collective-permute-done.1.xp, ...), custom_call_target="tpu_custom_call" | custom-call | flops 268435456 | bytes 2097152 | tf_op jit(solution)/shard_map/own_terms/pallas_call | solution.py:298
  15.5 0.0 copy-start
  15.5 0.0 copy-start.1
  15.5 0.0 copy-start.2
  15.5 0.7 %collective-permute-done.5.refs_2_ = s16[272,256]{1,0:T(8,128)(2,1)S(1)} collective-permute-done((s16[272,256]{1,0:T(8,128)(2,1)S(1)}, s16[272,256]{1,0:T(8,128)(2,1)S(1)}, u32[]{:S(2)}, u32[]{:S(2)}) %collective-permute-start.5) | collective-permute-done | bytes 139296 | tf_op jit(solution)/shard_map/ppermute | solution.py:443
  16.3 3.7 %collective-permute-done.4.refs_1_ = s16[272,256]{1,0:T(8,128)(2,1)S(1)} collective-permute-done((s16[272,256]{1,0:T(8,128)(2,1)S(1)}, s16[272,256]{1,0:T(8,128)(2,1)S(1)}, u32[]{:S(2)}, u32[]{:S(2)}) %collective-permute-start.4) | collective-permute-done | bytes 139296 | tf_op jit(solution)/shard_map/ppermute | solution.py:443
  19.9 0.4 collective-permute-done.3.refs_0_
  20.3 0.2 combine.1
  20.5 4.3 %collective-permute-start.6 = (s16[80,256]{1,0:T(8,128)(2,1)S(1)}, s16[80,256]{1,0:T(8,128)(2,1)S(1)}, u32[]{:S(2)}, u32[]{:S(2)}) collective-permute-start(s16[80,256]{1,0:T(8,128)(2,1)S(1)} %get-tuple-element.31), channel_id=1, source_target_pairs={{0,12},{1,13},{2,14},{3,15},{4,8},{5,9},{6,10},{7,11},{8,4},{9,5},... | collective-permute-start | bytes 122888 | tf_op jit(solution)/shard_map/ppermute | solution.py:443
  24.8 0.0 collective-permute-start.7
  24.8 0.6 %collective-permute-start.8 = (s16[80,256]{1,0:T(8,128)(2,1)S(1)}, s16[80,256]{1,0:T(8,128)(2,1)S(1)}, u32[]{:S(2)}, u32[]{:S(2)}) collective-permute-start(s16[80,256]{1,0:T(8,128)(2,1)S(1)} %get-tuple-element.33), channel_id=1, source_target_pairs={{0,4},{1,5},{2,6},{3,7},{4,0},{5,1},{6,2},{7,3},{8,12},{9,13},{10,... | collective-permute-start | bytes 122888 | tf_op jit(solution)/shard_map/ppermute | solution.py:443
  25.4 1.5 %collective-permute-done.6.refs_1_ = s16[80,256]{1,0:T(8,128)(2,1)S(1)} collective-permute-done((s16[80,256]{1,0:T(8,128)(2,1)S(1)}, s16[80,256]{1,0:T(8,128)(2,1)S(1)}, u32[]{:S(2)}, u32[]{:S(2)}) %collective-permute-start.6) | collective-permute-done | bytes 40992 | tf_op jit(solution)/shard_map/ppermute | solution.py:443
  27.0 2.7 %collective-permute-done.7.refs_2_ = s16[80,256]{1,0:T(8,128)(2,1)S(1)} collective-permute-done((s16[80,256]{1,0:T(8,128)(2,1)S(1)}, s16[80,256]{1,0:T(8,128)(2,1)S(1)}, u32[]{:S(2)}, u32[]{:S(2)}) %collective-permute-start.7) | collective-permute-done | bytes 40992 | tf_op jit(solution)/shard_map/ppermute | solution.py:443
  29.7 0.0 collective-permute-done.8.refs_3_
  29.7 0.1 collective-permute-start.9
  29.8 1.2 %collective-permute-done.9.other = bf16[64,256]{1,0:T(8,128)(2,1)S(1)} collective-permute-done((bf16[64,256]{1,0:T(8,128)(2,1)S(1)}, bf16[64,256]{1,0:T(8,128)(2,1)S(1)}, u32[]{:S(2)}, u32[]{:S(2)}) %collective-permute-start.9) | collective-permute-done | bytes 32800 | tf_op jit(solution)/shard_map/ppermute | solution.py:494
  31.0 0.8 %rows_to_send.1 = bf16[128,256]{1,0:T(8,128)(2,1)} custom-call(bf16[64,256]{1,0:T(8,128)(2,1)S(1)} %hidden_rows.1.own, bf16[64,256]{1,0:T(8,128)(2,1)S(1)} %collective-permute-done.9.other, bf16[128,128]{1,0:T(8,128)(2,1)S(1)} %get-tuple-element.36.sel), custom_call_target="tpu_custom_call" | custom-call | tf_op jit(solution)/shard_map/rows_to_send/pallas_call | solution.py:375
  31.8 6.9 %all-to-all-start = ((bf16[16,8,256]{2,1,0:T(8,128)(2,1)}), bf16[16,8,256]{2,1,0:T(8,128)(2,1)S(1)}, u32[]{:S(2)}, u32[]{:S(2)}) async-start(bf16[16,8,256]{2,1,0:T(8,128)(2,1)} %bitcast.8), calls=%async_computation | async-start | bytes 131072 | tf_op jit(solution)/shard_map/all_to_all | solution.py:497
  38.7 0.0 copy-done
  38.7 0.0 copy-done.1
  38.7 0.7 %local_terms.1 = (f32[64,256]{1,0:T(8,128)S(1)}, f32[64,172]{1,0:T(8,128)S(1)}) custom-call(s32[2]{0:T(128)S(1)} %pad_add_fusion.ids, bf16[64,256]{1,0:T(8,128)(2,1)S(1)} %hidden_rows.1.own, bf16[64,256]{1,0:T(8,128)(2,1)S(1)} %collective-permute-done.9.other, bf16[64,256]{1,0:T(8,128)(2,1)S(1)} %copy-done, bf16[172,256]{1,0:T(8,128)(2,1)S(1)} %bitcast.12), custom_call_target="tpu_custom_call" | custom-call | tf_op jit(solution)/shard_map/local_terms/pallas_call | solution.py:402
  39.4 2.2 %all-to-all-done = bf16[16,8,256]{2,1,0:T(8,128)(2,1)S(1)} async-done(((bf16[16,8,256]{2,1,0:T(8,128)(2,1)}), bf16[16,8,256]{2,1,0:T(8,128)(2,1)S(1)}, u32[]{:S(2)}, u32[]{:S(2)}) %all-to-all-start) | async-done | bytes 65568 | tf_op jit(solution)/shard_map/all_to_all | solution.py:497
  41.7 0.0 copy-done.2
  41.7 0.9 %logits.1 = f32[64,172]{1,0:T(8,128)} custom-call(f32[64,256]{1,0:T(8,128)S(1)} %get-tuple-element.34.part, f32[64,172]{1,0:T(8,128)S(1)} %get-tuple-element.35.logits, bf16[128,256]{1,0:T(8,128)(2,1)S(1)} %bitcast.11, bf16[64,256]{1,0:T(8,128)(2,1)S(1)} %copy-done, bf16[172,256]{1,0:T(8,128)(2,1)S(1)} %bitcast.13), custom_call_target="tpu_custom_call" | custom-call | tf_op jit(solution)/shard_map/logits/pallas_call | solution.py:430
  (1 shorter events, 0.0 us)
Async XLA Ops:
  0.0 3.8 %collective-permute-start.1 = (bf16[1024,512]{1,0:T(8,128)(2,1)}, bf16[1024,512]{1,0:T(8,128)(2,1)S(1)}, u32[]{:S(2)}, u32[]{:S(2)}) collective-permute-start(bf16[1024,512]{1,0:T(8,128)(2,1)} %xo.1), channel_id=1, source_target_pairs={{0,16},{16,0},{1,17},{17,1},{2,18},{18,2},{3,19},{19,3},{4,20},{20... | collective-permute-start | bytes 3145736 | tf_op jit(solution)/shard_map/ppermute | solution.py:470
  0.5 8.0 %collective-permute-start = (bf16[512,256]{1,0:T(8,128)(2,1)}, bf16[512,256]{1,0:T(8,128)(2,1)S(1)}, u32[]{:S(2)}, u32[]{:S(2)}) collective-permute-start(bf16[512,256]{1,0:T(8,128)(2,1)} %wo.1), channel_id=1, source_target_pairs={{0,16},{16,0},{1,17},{17,1},{2,18},{18,2},{3,19},{19,3},{4,20},{20... | collective-permute-start | bytes 786440 | tf_op jit(solution)/shard_map/ppermute | solution.py:471
  0.5 13.7 %collective-permute-start.2 = (bf16[512,256]{1,0:T(8,128)(2,1)}, bf16[512,256]{1,0:T(8,128)(2,1)S(1)}, u32[]{:S(2)}, u32[]{:S(2)}) collective-permute-start(bf16[512,256]{1,0:T(8,128)(2,1)} %so.1), channel_id=1, source_target_pairs={{0,16},{16,0},{1,17},{17,1},{2,18},{18,2},{3,19},{19,3},{4,20},{20... | collective-permute-start | bytes 786440 | tf_op jit(solution)/shard_map/ppermute | solution.py:472
  9.0 7.3 %collective-permute-start.5 = (s16[272,256]{1,0:T(8,128)(2,1)S(1)}, s16[272,256]{1,0:T(8,128)(2,1)S(1)}, u32[]{:S(2)}, u32[]{:S(2)}) collective-permute-start(s16[272,256]{1,0:T(8,128)(2,1)S(1)} %sent_terms.5), channel_id=1, source_target_pairs={{0,3},{1,2},{2,1},{3,0},{4,7},{5,6},{6,5},{7,4},{8,11},{9,10},{10,... | collective-permute-start | bytes 417800 | tf_op jit(solution)/shard_map/ppermute | solution.py:443
  12.9 7.0 %collective-permute-start.4 = (s16[272,256]{1,0:T(8,128)(2,1)S(1)}, s16[272,256]{1,0:T(8,128)(2,1)S(1)}, u32[]{:S(2)}, u32[]{:S(2)}) collective-permute-start(s16[272,256]{1,0:T(8,128)(2,1)S(1)} %sent_terms.4), channel_id=1, source_target_pairs={{0,2},{1,3},{2,0},{3,1},{4,6},{5,7},{6,4},{7,5},{8,10},{9,11},{10,... | collective-permute-start | bytes 417800 | tf_op jit(solution)/shard_map/ppermute | solution.py:443
  14.1 6.2 %collective-permute-start.3 = (s16[272,256]{1,0:T(8,128)(2,1)S(1)}, s16[272,256]{1,0:T(8,128)(2,1)S(1)}, u32[]{:S(2)}, u32[]{:S(2)}) collective-permute-start(s16[272,256]{1,0:T(8,128)(2,1)S(1)} %sent_terms.3), channel_id=1, source_target_pairs={{0,1},{1,0},{2,3},{3,2},{4,5},{5,4},{6,7},{7,6},{8,9},{9,8},{10,11... | collective-permute-start | bytes 417800 | tf_op jit(solution)/shard_map/ppermute | solution.py:443
  15.5 23.2 %copy-start = (bf16[64,256]{1,0:T(8,128)(2,1)S(1)}, bf16[64,256]{1,0:T(8,128)(2,1)}, u32[]{:S(2)}) copy-start(bf16[64,256]{1,0:T(8,128)(2,1)} %adj.3) | copy-start | bytes 98308
  15.5 23.2 %copy-start.1 = (bf16[256,172]{0,1:T(8,128)(2,1)S(1)}, bf16[256,172]{0,1:T(8,128)(2,1)}, u32[]{:S(2)}) copy-start(bf16[256,172]{0,1:T(8,128)(2,1)} %param.22) | copy-start | bytes 264196
  15.5 26.2 %copy-start.2 = (bf16[256,172]{0,1:T(8,128)(2,1)S(1)}, bf16[256,172]{0,1:T(8,128)(2,1)}, u32[]{:S(2)}) copy-start(bf16[256,172]{0,1:T(8,128)(2,1)} %param.23) | copy-start | bytes 264196
  20.5 6.4 %collective-permute-start.6 = (s16[80,256]{1,0:T(8,128)(2,1)S(1)}, s16[80,256]{1,0:T(8,128)(2,1)S(1)}, u32[]{:S(2)}, u32[]{:S(2)}) collective-permute-start(s16[80,256]{1,0:T(8,128)(2,1)S(1)} %get-tuple-element.31), channel_id=1, source_target_pairs={{0,12},{1,13},{2,14},{3,15},{4,8},{5,9},{6,10},{7,11},{8,4},{9,5},... | collective-permute-start | bytes 122888 | tf_op jit(solution)/shard_map/ppermute | solution.py:443
  24.8 4.9 %collective-permute-start.7 = (s16[80,256]{1,0:T(8,128)(2,1)S(1)}, s16[80,256]{1,0:T(8,128)(2,1)S(1)}, u32[]{:S(2)}, u32[]{:S(2)}) collective-permute-start(s16[80,256]{1,0:T(8,128)(2,1)S(1)} %get-tuple-element.32), channel_id=1, source_target_pairs={{0,8},{1,9},{2,10},{3,11},{4,12},{5,13},{6,14},{7,15},{8,0},{9,1},... | collective-permute-start | bytes 122888 | tf_op jit(solution)/shard_map/ppermute | solution.py:443
  24.8 4.9 %collective-permute-start.8 = (s16[80,256]{1,0:T(8,128)(2,1)S(1)}, s16[80,256]{1,0:T(8,128)(2,1)S(1)}, u32[]{:S(2)}, u32[]{:S(2)}) collective-permute-start(s16[80,256]{1,0:T(8,128)(2,1)S(1)} %get-tuple-element.33), channel_id=1, source_target_pairs={{0,4},{1,5},{2,6},{3,7},{4,0},{5,1},{6,2},{7,3},{8,12},{9,13},{10,... | collective-permute-start | bytes 122888 | tf_op jit(solution)/shard_map/ppermute | solution.py:443
  29.7 1.3 %collective-permute-start.9 = (bf16[64,256]{1,0:T(8,128)(2,1)S(1)}, bf16[64,256]{1,0:T(8,128)(2,1)S(1)}, u32[]{:S(2)}, u32[]{:S(2)}) collective-permute-start(bf16[64,256]{1,0:T(8,128)(2,1)S(1)} %hidden_rows.1.own), channel_id=1, source_target_pairs={{0,16},{16,0},{1,17},{17,1},{2,18},{18,2},{3,19},{19,3},{4,20},{20... | collective-permute-start | bytes 98312 | tf_op jit(solution)/shard_map/ppermute | solution.py:494
  31.8 9.9 %all-to-all-start = ((bf16[16,8,256]{2,1,0:T(8,128)(2,1)}), bf16[16,8,256]{2,1,0:T(8,128)(2,1)S(1)}, u32[]{:S(2)}, u32[]{:S(2)}) async-start(bf16[16,8,256]{2,1,0:T(8,128)(2,1)} %bitcast.8), calls=%async_computation | async-start | bytes 131072 | tf_op jit(solution)/shard_map/all_to_all | solution.py:497

commit v12 on v10

--- a/solution.py
+++ b/solution.py
@@ -15,8 +15,18 @@
 
 
 def group_of(core, place, groups):
-    pair = 2 * (place // 2) + core
-    return pair if place % 2 == 0 else groups - 1 - pair
+    return 2 * place + 1 - core
+
+
+def group_order(n):
+    first = n * 9 // 16
+    return [first] + [i for i in range(n - 1, -1, -1) if i != first]
+
+
+def ordered(block, n):
+    first = n * 9 // 16
+    down = n - block
+    return jnp.where(block == 0, first, jnp.where(down > first, down, down - 1))
 
 
 LN2 = 0.6931471805599453
@@ -55,11 +65,11 @@
     return value_of
 
 
-def plan_kernel(chunks, per, n, radix, n_src, ids, src_h, rows_h, dst_h, lists_h, counts_h, tw, xo, wo, so, *rest):
+def plan_kernel(chunks, per, n, radix, n_src, ids, src_h, rows_h, dst_h, tw, xo, wo, so, *rest):
     tables, rest = rest[:chunks], rest[chunks:]
     tbufs, rest = rest[:chunks], rest[chunks:]
-    sel, xo_out, wo_out, so_out = rest[:4]
-    src_v, rows_v, dst_v, lists, counts, sems = rest[4:]
+    xo_out, wo_out, so_out = rest[:3]
+    src_v, rows_v, dst_v, sems = rest[3:]
     core, me = ids[0], ids[1]
     tiles = src_v.shape[1]
     n_pos = tables[0].shape[1]
@@ -67,7 +77,7 @@
     groups = 2 * per * chunks
     half = groups // 2
     gs = [group_of(core, i, groups) for i in range(half)]
-    small = [(src_h, src_v), (rows_h, rows_v), (dst_h, dst_v), (lists_h, lists), (counts_h, counts)]
+    small = [(src_h, src_v), (rows_h, rows_v), (dst_h, dst_v)]
     large = [(tw.at[:, g], tbufs[i // per].at[pl.ds(i % per * tiles, tiles)]) for i, g in enumerate(gs)]
     large += [(xo, xo_out), (wo, wo_out), (so, so_out)]
     copies = [pltpu.make_async_copy(a, b, sems.at[i]) for i, (a, b) in enumerate(small + large)]
@@ -80,7 +90,7 @@
     pos_i = lax.broadcasted_iota(jnp.int32, (tiles, n_pos), 1).astype(jnp.float32)
     place_i = lax.broadcasted_iota(jnp.int32, (1, n_pos), 1)
     trash = float(n * per << 14)
-    for c in copies[:5]:
+    for c in copies[:3]:
         c.wait()
     src, rows = src_v[...], rows_v[...]
     slot = jnp.bitwise_xor(dst_v[...], me)
@@ -115,6 +125,47 @@
         tables[c][0:1, :] = word.astype(jnp.int32)
         tables[c][1:2, :] = owner.astype(jnp.int32)
 
+    for c in copies[3:]:
+        c.wait()
+
+
+def plan(chunks, per, n, radix, ids, src, rows, dst, tw, xo, wo, so):
+    tiles, _, _, tile = tw.shape
+    n_src = xo.shape[0] // tile
+    blocks = -(-(per * tiles // BLOCK + n_src) // STEP) * STEP
+    n_pos = -(-(blocks * BLOCK + 1) // 128) * 128
+    smem = pl.BlockSpec(memory_space=pltpu.SMEM)
+    vmem = pl.BlockSpec(memory_space=pltpu.VMEM)
+    hbm = pl.BlockSpec(memory_space=pltpu.HBM)
+    half = chunks * per
+    return pl.pallas_call(
+        functools.partial(plan_kernel, chunks, per, n, radix, n_src),
+        out_shape=[jax.ShapeDtypeStruct((2, n_pos), jnp.int32)] * chunks
+        + [jax.ShapeDtypeStruct((per * tiles, UNIT, tile), tw.dtype)] * chunks
+        + [
+            jax.ShapeDtypeStruct(xo.shape, xo.dtype),
+            jax.ShapeDtypeStruct(wo.shape, wo.dtype),
+            jax.ShapeDtypeStruct(so.shape, so.dtype),
+        ],
+        in_specs=[smem] + [hbm] * 7,
+        out_specs=[vmem] * (2 * chunks + 3),
+        scratch_shapes=[
+            pltpu.VMEM((1, tiles), jnp.int32),
+            pltpu.VMEM((1, tiles), jnp.int32),
+            pltpu.VMEM((1, tiles), jnp.int32),
+            pltpu.SemaphoreType.DMA((3 + half + 3,)),
+        ],
+        compiler_params=pltpu.CompilerParams(vmem_limit_bytes=32 * 1024 * 1024),
+        name="plan",
+    )(ids, *[
+        pltpu.with_memory_space_constraint(a, pltpu.HBM)
+        for a in (src.reshape(1, tiles), rows.reshape(1, tiles), dst.reshape(1, tiles), tw, xo, wo, so)
+    ])
+
+
+def select_kernel(groups, ids, lists, counts, sel):
+    core, me = ids[0], ids[1]
+    n = lists.shape[0]
     slots = lists.shape[1]
     total = n * slots
     q_n = lax.broadcasted_iota(jnp.int32, (total, n), 0)
@@ -125,55 +176,28 @@
     k_n = jnp.bitwise_and(q_n, slots - 1)
     for k in range(slots):
         picked = jnp.where(k_n == k, mine[k:k + 1, :], picked)
-    good = jnp.logical_and(lax.div(q_n, slots) == r_n, k_n < cnt)
+    good = jnp.logical_and(ordered(lax.div(q_n, slots), n) == r_n, k_n < cnt)
     row = jnp.sum(jnp.where(good, picked + 1.0, 0.0), axis=1, keepdims=True) - 1.0
     lane = lax.broadcasted_iota(jnp.int32, (1, sel.shape[1]), 1)
     name = jnp.zeros(lane.shape, jnp.int32)
-    for i, g in enumerate(gs + [group_of(1 - core, i, groups) for i in range(half)]):
+    names = [group_of(c, i, groups) for c in (core, 1 - core) for i in range(groups // 2)]
+    for i, g in enumerate(names):
         name = jnp.where(lax.div(lane, UNIT) == i, g * UNIT + jnp.bitwise_and(lane, UNIT - 1), name)
     sel[...] = jnp.where(row == name.astype(jnp.float32), 1.0, 0.0).astype(jnp.bfloat16)
 
-    for c in copies[5:]:
-        c.wait()
-
-
-def plan(chunks, per, n, radix, ids, src, rows, dst, send_list, send_count, tw, xo, wo, so):
-    tiles, _, _, tile = tw.shape
-    slots = send_list.shape[2]
-    n_src = xo.shape[0] // tile
-    blocks = -(-(per * tiles // BLOCK + n_src) // STEP) * STEP
-    n_pos = -(-(blocks * BLOCK + 1) // 128) * 128
+
+def selection(groups, ids, send_list, send_count):
+    n, _, slots = send_list.shape
     smem = pl.BlockSpec(memory_space=pltpu.SMEM)
     vmem = pl.BlockSpec(memory_space=pltpu.VMEM)
-    hbm = pl.BlockSpec(memory_space=pltpu.HBM)
-    lists = jnp.swapaxes(send_list, 1, 2)
-    half = chunks * per
-    return pl.pallas_call(
-        functools.partial(plan_kernel, chunks, per, n, radix, n_src),
-        out_shape=[jax.ShapeDtypeStruct((2, n_pos), jnp.int32)] * chunks
-        + [jax.ShapeDtypeStruct((per * tiles, UNIT, tile), tw.dtype)] * chunks
-        + [
-            jax.ShapeDtypeStruct((n * slots, 2 * half * UNIT), jnp.bfloat16),
-            jax.ShapeDtypeStruct(xo.shape, xo.dtype),
-            jax.ShapeDtypeStruct(wo.shape, wo.dtype),
-            jax.ShapeDtypeStruct(so.shape, so.dtype),
-        ],
-        in_specs=[smem] + [hbm] * 9,
-        out_specs=[vmem] * (2 * chunks + 4),
-        scratch_shapes=[
-            pltpu.VMEM((1, tiles), jnp.int32),
-            pltpu.VMEM((1, tiles), jnp.int32),
-            pltpu.VMEM((1, tiles), jnp.int32),
-            pltpu.VMEM(lists.shape, jnp.int32),
-            pltpu.VMEM(send_count.shape, jnp.int32),
-            pltpu.SemaphoreType.DMA((5 + half + 3,)),
-        ],
-        compiler_params=pltpu.CompilerParams(vmem_limit_bytes=32 * 1024 * 1024),
-        name="plan",
-    )(ids, *[
-        pltpu.with_memory_space_constraint(a, pltpu.HBM)
-        for a in (src.reshape(1, tiles), rows.reshape(1, tiles), dst.reshape(1, tiles), lists, send_count, tw, xo, wo, so)
-    ])
+    return pl.pallas_call(
+        functools.partial(select_kernel, groups),
+        out_shape=jax.ShapeDtypeStruct((n * slots, groups * UNIT), jnp.bfloat16),
+        in_specs=[smem, vmem, vmem],
+        out_specs=vmem,
+        compiler_params=pltpu.CompilerParams(vmem_limit_bytes=32 * 1024 * 1024),
+        name="selection",
+    )(ids, jnp.swapaxes(send_list, 1, 2), send_count)
 
 
 def tiles_kernel(table_v, tbuf, xo, xp, *rest):
@@ -374,7 +398,7 @@
     vmem = pl.BlockSpec(memory_space=pltpu.VMEM)
     return pl.pallas_call(
         send_kernel,
-        out_shape=jax.ShapeDtypeStruct((sel.shape[0], own.shape[1]), jnp.bfloat16),
+        out_shape=pltpu.VMEM((sel.shape[0], own.shape[1]), jnp.bfloat16),
         in_specs=[vmem] * 3,
         out_specs=vmem,
         compiler_params=pltpu.CompilerParams(vmem_limit_bytes=32 * 1024 * 1024),
@@ -382,7 +406,7 @@
     )(own, other, sel)
 
 
-def local_kernel(groups, ids, own, other, adj, w_self, part, logits, hidden):
+def local_kernel(n, groups, ids, own, other, adj, w_self, part, logits, adj_out, hidden):
     core = ids[0]
     for i in range(groups // 2):
         mine = group_of(core, i, groups)
@@ -393,20 +417,27 @@
     part[...] = jnp.dot(adj[:, :tile], hidden[...], preferred_element_type=jnp.float32)
     dims = (((1,), (1,)), ((), ()))
     logits[...] = lax.dot_general(hidden[:rows, :], w_self[...], dims, preferred_element_type=jnp.float32)
-
-
-def local_terms(groups, ids, own, other, adj, w_self):
+    count = adj.shape[1] - tile
+    slots = count // n
+    column = lax.broadcasted_iota(jnp.int32, (1, count), 1)
+    source = ordered(lax.div(column, slots), n) * slots + lax.rem(column, slots)
+    moved = jnp.where(lax.broadcasted_iota(jnp.int32, (count, count), 0) == source, 1.0, 0.0).astype(jnp.bfloat16)
+    adj_out[...] = jnp.dot(adj[:, tile:], moved, preferred_element_type=jnp.float32).astype(jnp.bfloat16)
+
+
+def local_terms(n, groups, ids, own, other, adj, w_self):
     smem = pl.BlockSpec(memory_space=pltpu.SMEM)
     vmem = pl.BlockSpec(memory_space=pltpu.VMEM)
     width = own.shape[1]
     return pl.pallas_call(
-        functools.partial(local_kernel, groups),
+        functools.partial(local_kernel, n, groups),
         out_shape=[
             jax.ShapeDtypeStruct((adj.shape[0], width), jnp.float32),
             jax.ShapeDtypeStruct((adj.shape[0], w_self.shape[1]), jnp.float32),
+            jax.ShapeDtypeStruct((adj.shape[0], adj.shape[1] - groups * UNIT), jnp.bfloat16),
         ],
         in_specs=[smem] + [vmem] * 4,
-        out_specs=[vmem] * 2,
+        out_specs=[vmem] * 3,
         scratch_shapes=[pltpu.VMEM((groups * UNIT, width), jnp.bfloat16)],
         compiler_params=pltpu.CompilerParams(vmem_limit_bytes=32 * 1024 * 1024),
         name="local_terms",
@@ -414,8 +445,7 @@
 
 
 def logits_kernel(part, logits, received, adj, w_neigh, out):
-    tile = adj.shape[1] - received.shape[0]
-    mean = part[...] + jnp.dot(adj[:, tile:], received[...], preferred_element_type=jnp.float32)
+    mean = part[...] + jnp.dot(adj[...], received[...], preferred_element_type=jnp.float32)
     dims = (((1,), (1,)), ((), ()))
     got = lax.dot_general(mean.astype(jnp.bfloat16), w_neigh[...], dims, preferred_element_type=jnp.float32)
     out[...] = logits[...] + got
@@ -468,10 +498,9 @@
     sp = lax.ppermute(w_self1, "feat", swap)
     tw = tile_weight.reshape(tile_weight.shape[0], groups, UNIT, tile)
     planned = plan(
-        CHUNKS, per, n, 4, ids, tile_src, tile_rows, tile_dst, send_list, send_count, tw, features,
-        neighbour_weight_first, w_self1,
+        CHUNKS, per, n, 4, ids, tile_src, tile_rows, tile_dst, tw, features, neighbour_weight_first, w_self1,
     )
-    tables, tbufs, (sel, xo, wo, so) = planned[:CHUNKS], planned[CHUNKS:2 * CHUNKS], planned[2 * CHUNKS:]
+    tables, tbufs, (xo, wo, so) = planned[:CHUNKS], planned[CHUNKS:2 * CHUNKS], planned[2 * CHUNKS:]
     done = []
     for chunk in range(CHUNKS):
         accs = gathered_sums(per, n, tables[chunk], tbufs[chunk], xo, xp)
@@ -486,12 +515,13 @@
             got = exchange(parts, stride, n, range(ways - 1, 0, -1))
             stride *= ways
         done.append(got)
+    sel = selection(groups, ids, send_list, send_count)
     own = hidden_rows(done, per * UNIT)
     other = lax.ppermute(own, "feat", swap)
     send = rows_to_send(own, other, sel)
-    received = lax.all_to_all(send, "dom", 0, 0, tiled=True)
-    part, logits = local_terms(groups, ids, own, other, adj_two, w_self2)
-    return logits_of(part, logits, received, adj_two, w_neigh2)
+    received = lax.all_to_all(send, "dom", 0, 0, axis_index_groups=[group_order(n)], tiled=True)
+    part, logits, adj = local_terms(n, groups, ids, own, other, adj_two, w_self2)
+    return logits_of(part, logits, received, adj, w_neigh2)
 
 
 def solution(mesh):

time: 45.2 us -> 43.5 us (0.962); the launches traced: 44.5 us -> 43.5 us
  waiting for transfers between devices: 16.8 us -> 13.6 us
  starting transfers between devices: 14.7 us -> 16.3 us
  Pallas kernels: 12.8 us -> 13.4 us
    all_to_all x1, waiting for transfers between devices: 6.8 us -> 3.8 us  [body(): lax.all_to_all(send, 'dom', 0, 0, axis_index_groups=[group_order(n)], til...]
    all_to_all x1, starting transfers between devices: 4.68 us -> 6.41 us  [body(): lax.all_to_all(send, 'dom', 0, 0, axis_index_groups=[group_order(n)], til...]
    ppermute x1, waiting for transfers between devices: 1.19 us -> 0.49 us  [body(): other = lax.ppermute(own, 'feat', swap)]
    pallas_call x2 -> x3, Pallas kernels: 1.49 us -> 2.18 us  [the longest x1 0.78 us: rows_to_send(): pl.pallas_call(send_kernel, out_shape=pltpu.VMEM((sel.shape[0], own.shape...]
    ppermute x6, waiting for transfers between devices: 8.8 us -> 9.26 us  [exchange(): lax.ppermute(parts[k], 'dom', [(i, i ^ k * stride) for i in range(n)])]
  transfers between devices with their start and end apart: 11 -> 11, of which waited for: 7 -> 7; matrix products, arithmetic and copies ran while one was open for 0% -> 0% of each run, Pallas kernels for 25% -> 26%
where the time goes in v12:
time: 43.5 us
  starting transfers between devices  16.3 us (37%)
  waiting for transfers between devices  13.6 us (31%)
  Pallas kernels  13.4 us (31%)
    ppermute x6, waiting for transfers between devices, exchange(): lax.ppermute(parts[k], 'dom', [(i, i ^ k * stride) for i in range(n)])  9.26 us
    ppermute x6, starting transfers between devices, exchange(): lax.ppermute(parts[k], 'dom', [(i, i ^ k * stride) for i in range(n)])  8.84 us
    all_to_all x1, starting transfers between devices, body(): lax.all_to_all(send, 'dom', 0, 0, axis_index_groups=[group_order(n)], til...  6.41 us
    pallas_call x1, Pallas kernels, gathered_sums(): pl.pallas_call(tiles_kernel, out_shape=[sums] * parts, in_specs=[vmem] *...  4.61 us
    all_to_all x1, waiting for transfers between devices, body(): lax.all_to_all(send, 'dom', 0, 0, axis_index_groups=[group_order(n)], til...  3.8 us
    pallas_call x1, Pallas kernels, plan(): pl.pallas_call(functools.partial(plan_kernel, chunks, per, n, radix, n_sr...  2.68 us
    pallas_call x3, Pallas kernels, sent_terms(): pl.pallas_call(functools.partial(sent_kernel, k, slots, rows, len(accs)),...  1.55 us
    pallas_call x1, Pallas kernels, own_terms(): pl.pallas_call(functools.partial(own_kernel, chunk, per, groups, len(accs...  1.24 us
  transfers between devices with their start and end apart: 11, of which 7 were waited for; matrix products, arithmetic and copies ran while one was open for 0% of the time, Pallas kernels for 26%

profile of v12, /device:TPU:0, one launch (start us, length us, event | category | flops | bytes accessed | tf_op | source)
XLA Modules:
  0.0 43.5 jit_solution(14461896001617871661)
XLA Ops:
  0.0 0.5 %collective-permute-start.1 = (bf16[1024,512]{1,0:T(8,128)(2,1)}, bf16[1024,512]{1,0:T(8,128)(2,1)S(1)}, u32[]{:S(2)}, u32[]{:S(2)}) collective-permute-start(bf16[1024,512]{1,0:T(8,128)(2,1)} %xo.1), channel_id=1, source_target_pairs={{0,16},{16,0},{1,17},{17,1},{2,18},{18,2},{3,19},{19,3},{4,20},{20... | collective-permute-start | bytes 3145736 | tf_op jit(solution)/shard_map/ppermute | solution.py:496
  0.5 0.1 collective-permute-start
  0.5 0.5 %collective-permute-start.2 = (bf16[512,256]{1,0:T(8,128)(2,1)}, bf16[512,256]{1,0:T(8,128)(2,1)S(1)}, u32[]{:S(2)}, u32[]{:S(2)}) collective-permute-start(bf16[512,256]{1,0:T(8,128)(2,1)} %so.1), channel_id=1, source_target_pairs={{0,16},{16,0},{1,17},{17,1},{2,18},{18,2},{3,19},{19,3},{4,20},{20... | collective-permute-start | bytes 786440 | tf_op jit(solution)/shard_map/ppermute | solution.py:498
  1.0 0.1 pad_add_fusion.ids
  1.0 2.7 %plan.1 = (s32[2,640]{1,0:T(2,128)S(1)}, bf16[512,16,128]{2,1,0:T(8,128)(2,1)S(1)}, bf16[1024,512]{1,0:T(8,128)(2,1)S(1)}, bf16[512,256]{1,0:T(8,128)(2,1)S(1)}, bf16[512,256]{1,0:T(8,128)(2,1)S(1)}) custom-call(s32[2]{0:T(128)S(1)} %pad_add_fusion.ids, s32[1,128]{1,0:T(1,128)} %bitcast.16, s32[1,128]{1,0:T(1,128)} %bitcast.17, s32[1,128]{1,0:T(1,128)} %bitcast.18, ...), custom_call_target="tpu_custom_call" | custom-call | tf_op jit(solution)/shard_map/plan/pallas_call | solution.py:141
  3.7 0.0 collective-permute-done.1.xp
  3.7 4.6 %gathered_sums.1 = (f32[1040,256]{1,0:T(8,128)S(1)}, f32[1040,256]{1,0:T(8,128)S(1)}, f32[1040,256]{1,0:T(8,128)S(1)}, f32[1040,256]{1,0:T(8,128)S(1)}) custom-call(s32[2,640]{1,0:T(2,128)S(1)} %get-tuple-element.24.table_v, bf16[512,16,128]{2,1,0:T(8,128)(2,1)S(1)} %get-tuple-element.25.tbuf, bf16[1024,512]{1,0:T(8,128)(2,1)S(1)} %get-tuple-element.22.xo, ...), custom_call_target="tpu_custom_call" | custom-call | flops 2147483648 | bytes 8388608 | tf_op jit(solution)/shard_map/gathered_sums/pallas_call | solution.py:247
  8.4 0.0 collective-permute-done.wp
  8.4 0.5 %sent_terms.5 = s16[272,256]{1,0:T(8,128)(2,1)S(1)} custom-call(bf16[512,256]{1,0:T(8,128)(2,1)S(1)} %get-tuple-element.21.wo, bf16[512,256]{1,0:T(8,128)(2,1)S(1)} %collective-permute-done.wp, f32[1040,256]{1,0:T(8,128)S(1)} %get-tuple-element.26.refs_0_, f32[1040,256]{1,0:T(8,128)S(1)} %get-tuple-element.27.refs_1_, ...), custom_call_target="tpu_custom_call" | custom-call | flops 268435456 | bytes 2097152 | tf_op jit(solution)/shard_map/sent_terms/pallas_call | solution.py:291
  8.9 3.6 %collective-permute-start.5 = (s16[272,256]{1,0:T(8,128)(2,1)S(1)}, s16[272,256]{1,0:T(8,128)(2,1)S(1)}, u32[]{:S(2)}, u32[]{:S(2)}) collective-permute-start(s16[272,256]{1,0:T(8,128)(2,1)S(1)} %sent_terms.5), channel_id=1, source_target_pairs={{0,3},{1,2},{2,1},{3,0},{4,7},{5,6},{6,5},{7,4},{8,11},{9,10},{10,... | collective-permute-start | bytes 417800 | tf_op jit(solution)/shard_map/ppermute | solution.py:469
  12.5 0.5 %sent_terms.4 = s16[272,256]{1,0:T(8,128)(2,1)S(1)} custom-call(bf16[512,256]{1,0:T(8,128)(2,1)S(1)} %get-tuple-element.21.wo, bf16[512,256]{1,0:T(8,128)(2,1)S(1)} %collective-permute-done.wp, f32[1040,256]{1,0:T(8,128)S(1)} %get-tuple-element.26.refs_0_, f32[1040,256]{1,0:T(8,128)S(1)} %get-tuple-element.27.refs_1_, ...), custom_call_target="tpu_custom_call" | custom-call | flops 268435456 | bytes 2097152 | tf_op jit(solution)/shard_map/sent_terms/pallas_call | solution.py:291
  13.0 0.6 %collective-permute-start.4 = (s16[272,256]{1,0:T(8,128)(2,1)S(1)}, s16[272,256]{1,0:T(8,128)(2,1)S(1)}, u32[]{:S(2)}, u32[]{:S(2)}) collective-permute-start(s16[272,256]{1,0:T(8,128)(2,1)S(1)} %sent_terms.4), channel_id=1, source_target_pairs={{0,2},{1,3},{2,0},{3,1},{4,6},{5,7},{6,4},{7,5},{8,10},{9,11},{10,... | collective-permute-start | bytes 417800 | tf_op jit(solution)/shard_map/ppermute | solution.py:469
  13.5 0.5 %sent_terms.3 = s16[272,256]{1,0:T(8,128)(2,1)S(1)} custom-call(bf16[512,256]{1,0:T(8,128)(2,1)S(1)} %get-tuple-element.21.wo, bf16[512,256]{1,0:T(8,128)(2,1)S(1)} %collective-permute-done.wp, f32[1040,256]{1,0:T(8,128)S(1)} %get-tuple-element.26.refs_0_, f32[1040,256]{1,0:T(8,128)S(1)} %get-tuple-element.27.refs_1_, ...), custom_call_target="tpu_custom_call" | custom-call | flops 268435456 | bytes 2097152 | tf_op jit(solution)/shard_map/sent_terms/pallas_call | solution.py:291
  14.1 0.2 collective-permute-start.3
  14.2 0.0 collective-permute-done.2.sp
  14.2 0.0 copy-start.2
  14.2 0.0 copy-start.4
  14.2 1.2 %own_terms.1.own = f32[256,256]{1,0:T(8,128)S(1)} custom-call(s32[2]{0:T(128)S(1)} %pad_add_fusion.ids, bf16[512,256]{1,0:T(8,128)(2,1)S(1)} %get-tuple-element.21.wo, bf16[512,256]{1,0:T(8,128)(2,1)S(1)} %collective-permute-done.wp, bf16[1024,512]{1,0:T(8,128)(2,1)S(1)} %get-tuple-element.22.xo, bf16[1024,512]{1,0:T(8,128)(2,1)S(1)} %collective-permute-done.1.xp, ...), custom_call_target="tpu_custom_call" | custom-call | flops 268435456 | bytes 2097152 | tf_op jit(solution)/shard_map/own_terms/pallas_call | solution.py:322
  15.5 0.0 copy-start
  15.5 0.0 copy-start.3
  15.5 0.0 copy-start.1
  15.5 0.9 %collective-permute-done.5.refs_2_ = s16[272,256]{1,0:T(8,128)(2,1)S(1)} collective-permute-done((s16[272,256]{1,0:T(8,128)(2,1)S(1)}, s16[272,256]{1,0:T(8,128)(2,1)S(1)}, u32[]{:S(2)}, u32[]{:S(2)}) %collective-permute-start.5) | collective-permute-done | bytes 139296 | tf_op jit(solution)/shard_map/ppermute | solution.py:469
  16.4 3.5 %collective-permute-done.4.refs_1_ = s16[272,256]{1,0:T(8,128)(2,1)S(1)} collective-permute-done((s16[272,256]{1,0:T(8,128)(2,1)S(1)}, s16[272,256]{1,0:T(8,128)(2,1)S(1)}, u32[]{:S(2)}, u32[]{:S(2)}) %collective-permute-start.4) | collective-permute-done | bytes 139296 | tf_op jit(solution)/shard_map/ppermute | solution.py:469
  20.0 0.6 %collective-permute-done.3.refs_0_ = s16[272,256]{1,0:T(8,128)(2,1)S(1)} collective-permute-done((s16[272,256]{1,0:T(8,128)(2,1)S(1)}, s16[272,256]{1,0:T(8,128)(2,1)S(1)}, u32[]{:S(2)}, u32[]{:S(2)}) %collective-permute-start.3) | collective-permute-done | bytes 139296 | tf_op jit(solution)/shard_map/ppermute | solution.py:469
  20.5 0.2 combine.1
  20.7 3.9 %collective-permute-start.6 = (s16[80,256]{1,0:T(8,128)(2,1)S(1)}, s16[80,256]{1,0:T(8,128)(2,1)S(1)}, u32[]{:S(2)}, u32[]{:S(2)}) collective-permute-start(s16[80,256]{1,0:T(8,128)(2,1)S(1)} %get-tuple-element.31), channel_id=1, source_target_pairs={{0,12},{1,13},{2,14},{3,15},{4,8},{5,9},{6,10},{7,11},{8,4},{9,5},... | collective-permute-start | bytes 122888 | tf_op jit(solution)/shard_map/ppermute | solution.py:469
  24.6 0.0 collective-permute-start.7
  24.6 0.6 %collective-permute-start.8 = (s16[80,256]{1,0:T(8,128)(2,1)S(1)}, s16[80,256]{1,0:T(8,128)(2,1)S(1)}, u32[]{:S(2)}, u32[]{:S(2)}) collective-permute-start(s16[80,256]{1,0:T(8,128)(2,1)S(1)} %get-tuple-element.33), channel_id=1, source_target_pairs={{0,4},{1,5},{2,6},{3,7},{4,0},{5,1},{6,2},{7,3},{8,12},{9,13},{10,... | collective-permute-start | bytes 122888 | tf_op jit(solution)/shard_map/ppermute | solution.py:469
  25.3 1.3 %collective-permute-done.6.refs_1_ = s16[80,256]{1,0:T(8,128)(2,1)S(1)} collective-permute-done((s16[80,256]{1,0:T(8,128)(2,1)S(1)}, s16[80,256]{1,0:T(8,128)(2,1)S(1)}, u32[]{:S(2)}, u32[]{:S(2)}) %collective-permute-start.6) | collective-permute-done | bytes 40992 | tf_op jit(solution)/shard_map/ppermute | solution.py:469
  26.6 2.9 %collective-permute-done.7.refs_2_ = s16[80,256]{1,0:T(8,128)(2,1)S(1)} collective-permute-done((s16[80,256]{1,0:T(8,128)(2,1)S(1)}, s16[80,256]{1,0:T(8,128)(2,1)S(1)}, u32[]{:S(2)}, u32[]{:S(2)}) %collective-permute-start.7) | collective-permute-done | bytes 40992 | tf_op jit(solution)/shard_map/ppermute | solution.py:469
  29.5 0.0 collective-permute-done.8.refs_3_
  29.6 0.1 collective-permute-start.9
  29.7 0.0 copy-done.2
  29.7 0.0 copy-done.4
  29.7 0.7 %selection.1.sel = bf16[128,128]{1,0:T(8,128)(2,1)S(1)} custom-call(s32[2]{0:T(128)S(1)} %pad_add_fusion.ids, s32[16,8,16]{2,1,0:T(8,128)S(1)} %bitcast.14, s32[16,16]{1,0:T(8,128)S(1)} %copy-done.4), custom_call_target="tpu_custom_call" | custom-call | tf_op jit(solution)/shard_map/selection/pallas_call | solution.py:193
  30.4 0.5 %collective-permute-done.9.other = bf16[64,256]{1,0:T(8,128)(2,1)S(1)} collective-permute-done((bf16[64,256]{1,0:T(8,128)(2,1)S(1)}, bf16[64,256]{1,0:T(8,128)(2,1)S(1)}, u32[]{:S(2)}, u32[]{:S(2)}) %collective-permute-start.9) | collective-permute-done | bytes 32800 | tf_op jit(solution)/shard_map/ppermute | solution.py:520
  30.9 0.8 %rows_to_send.1 = bf16[128,256]{1,0:T(8,128)(2,1)} custom-call(bf16[64,256]{1,0:T(8,128)(2,1)S(1)} %hidden_rows.1.own, bf16[64,256]{1,0:T(8,128)(2,1)S(1)} %collective-permute-done.9.other, bf16[128,128]{1,0:T(8,128)(2,1)S(1)} %selection.1.sel), custom_call_target="tpu_custom_call" | custom-call | tf_op jit(solution)/shard_map/rows_to_send/pallas_call | solution.py:399
  31.6 6.4 %all-to-all-start = ((bf16[16,8,256]{2,1,0:T(8,128)(2,1)}), bf16[16,8,256]{2,1,0:T(8,128)(2,1)S(1)}, u32[]{:S(2)}, u32[]{:S(2)}) async-start(bf16[16,8,256]{2,1,0:T(8,128)(2,1)} %bitcast.8), calls=%async_computation | async-start | bytes 131072 | tf_op jit(solution)/shard_map/all_to_all | solution.py:522
  38.1 0.0 copy-done
  38.1 0.0 copy-done.3
  38.1 0.7 %local_terms.1 = (f32[64,256]{1,0:T(8,128)S(1)}, f32[64,172]{1,0:T(8,128)S(1)}, bf16[64,128]{1,0:T(8,128)(2,1)S(1)}) custom-call(s32[2]{0:T(128)S(1)} %pad_add_fusion.ids, bf16[64,256]{1,0:T(8,128)(2,1)S(1)} %hidden_rows.1.own, bf16[64,256]{1,0:T(8,128)(2,1)S(1)} %collective-permute-done.9.other, bf16[64,256]{1,0:T(8,128)(2,1)S(1)} %copy-done.3, ...), custom_call_target="tpu_custom_call" | custom-call | tf_op jit(solution)/shard_map/local_terms/pallas_call | solution.py:432
  38.8 3.8 %all-to-all-done = bf16[16,8,256]{2,1,0:T(8,128)(2,1)S(1)} async-done(((bf16[16,8,256]{2,1,0:T(8,128)(2,1)}), bf16[16,8,256]{2,1,0:T(8,128)(2,1)S(1)}, u32[]{:S(2)}, u32[]{:S(2)}) %all-to-all-start) | async-done | bytes 65568 | tf_op jit(solution)/shard_map/all_to_all | solution.py:522
  42.6 0.0 copy-done.1
  42.6 0.9 %logits.1 = f32[64,172]{1,0:T(8,128)} custom-call(f32[64,256]{1,0:T(8,128)S(1)} %get-tuple-element.34.part, f32[64,172]{1,0:T(8,128)S(1)} %get-tuple-element.35.logits, bf16[128,256]{1,0:T(8,128)(2,1)S(1)} %bitcast.11, bf16[64,128]{1,0:T(8,128)(2,1)S(1)} %get-tuple-element.36.adj, bf16[172,256]{1,0:T(8,128)(2,1)S(1)} %bitcast.13), custom_call_target="tpu_custom_call" | custom-call | tf_op jit(solution)/shard_map/logits/pallas_call | solution.py:456
  (1 shorter events, 0.0 us)
Async XLA Ops:
  0.0 3.7 %collective-permute-start.1 = (bf16[1024,512]{1,0:T(8,128)(2,1)}, bf16[1024,512]{1,0:T(8,128)(2,1)S(1)}, u32[]{:S(2)}, u32[]{:S(2)}) collective-permute-start(bf16[1024,512]{1,0:T(8,128)(2,1)} %xo.1), channel_id=1, source_target_pairs={{0,16},{16,0},{1,17},{17,1},{2,18},{18,2},{3,19},{19,3},{4,20},{20... | collective-permute-start | bytes 3145736 | tf_op jit(solution)/shard_map/ppermute | solution.py:496
  0.5 7.9 %collective-permute-start = (bf16[512,256]{1,0:T(8,128)(2,1)}, bf16[512,256]{1,0:T(8,128)(2,1)S(1)}, u32[]{:S(2)}, u32[]{:S(2)}) collective-permute-start(bf16[512,256]{1,0:T(8,128)(2,1)} %wo.1), channel_id=1, source_target_pairs={{0,16},{16,0},{1,17},{17,1},{2,18},{18,2},{3,19},{19,3},{4,20},{20... | collective-permute-start | bytes 786440 | tf_op jit(solution)/shard_map/ppermute | solution.py:497
  0.5 13.7 %collective-permute-start.2 = (bf16[512,256]{1,0:T(8,128)(2,1)}, bf16[512,256]{1,0:T(8,128)(2,1)S(1)}, u32[]{:S(2)}, u32[]{:S(2)}) collective-permute-start(bf16[512,256]{1,0:T(8,128)(2,1)} %so.1), channel_id=1, source_target_pairs={{0,16},{16,0},{1,17},{17,1},{2,18},{18,2},{3,19},{19,3},{4,20},{20... | collective-permute-start | bytes 786440 | tf_op jit(solution)/shard_map/ppermute | solution.py:498
  8.9 7.5 %collective-permute-start.5 = (s16[272,256]{1,0:T(8,128)(2,1)S(1)}, s16[272,256]{1,0:T(8,128)(2,1)S(1)}, u32[]{:S(2)}, u32[]{:S(2)}) collective-permute-start(s16[272,256]{1,0:T(8,128)(2,1)S(1)} %sent_terms.5), channel_id=1, source_target_pairs={{0,3},{1,2},{2,1},{3,0},{4,7},{5,6},{6,5},{7,4},{8,11},{9,10},{10,... | collective-permute-start | bytes 417800 | tf_op jit(solution)/shard_map/ppermute | solution.py:469
  13.0 7.0 %collective-permute-start.4 = (s16[272,256]{1,0:T(8,128)(2,1)S(1)}, s16[272,256]{1,0:T(8,128)(2,1)S(1)}, u32[]{:S(2)}, u32[]{:S(2)}) collective-permute-start(s16[272,256]{1,0:T(8,128)(2,1)S(1)} %sent_terms.4), channel_id=1, source_target_pairs={{0,2},{1,3},{2,0},{3,1},{4,6},{5,7},{6,4},{7,5},{8,10},{9,11},{10,... | collective-permute-start | bytes 417800 | tf_op jit(solution)/shard_map/ppermute | solution.py:469
  14.1 6.4 %collective-permute-start.3 = (s16[272,256]{1,0:T(8,128)(2,1)S(1)}, s16[272,256]{1,0:T(8,128)(2,1)S(1)}, u32[]{:S(2)}, u32[]{:S(2)}) collective-permute-start(s16[272,256]{1,0:T(8,128)(2,1)S(1)} %sent_terms.3), channel_id=1, source_target_pairs={{0,1},{1,0},{2,3},{3,2},{4,5},{5,4},{6,7},{7,6},{8,9},{9,8},{10,11... | collective-permute-start | bytes 417800 | tf_op jit(solution)/shard_map/ppermute | solution.py:469
  14.2 15.4 %copy-start.2 = (s32[16,16,8]{1,2,0:T(8,128)S(1)}, s32[16,16,8]{1,2,0:T(8,128)}, u32[]{:S(2)}) copy-start(s32[16,16,8]{1,2,0:T(8,128)} %param.19) | copy-start | bytes 24580
  14.2 15.5 %copy-start.4 = (s32[16,16]{1,0:T(8,128)S(1)}, s32[16,16]{1,0:T(8,128)}, u32[]{:S(2)}) copy-start(s32[16,16]{1,0:T(8,128)} %counts.1) | copy-start | bytes 3076
  15.5 22.6 %copy-start = (bf16[256,172]{0,1:T(8,128)(2,1)S(1)}, bf16[256,172]{0,1:T(8,128)(2,1)}, u32[]{:S(2)}) copy-start(bf16[256,172]{0,1:T(8,128)(2,1)} %param.22) | copy-start | bytes 264196
  15.5 22.6 %copy-start.3 = (bf16[64,256]{1,0:T(8,128)(2,1)S(1)}, bf16[64,256]{1,0:T(8,128)(2,1)}, u32[]{:S(2)}) copy-start(bf16[64,256]{1,0:T(8,128)(2,1)} %adj.1) | copy-start | bytes 98308
  15.5 27.1 %copy-start.1 = (bf16[256,172]{0,1:T(8,128)(2,1)S(1)}, bf16[256,172]{0,1:T(8,128)(2,1)}, u32[]{:S(2)}) copy-start(bf16[256,172]{0,1:T(8,128)(2,1)} %param.23) | copy-start | bytes 264196
  20.7 5.9 %collective-permute-start.6 = (s16[80,256]{1,0:T(8,128)(2,1)S(1)}, s16[80,256]{1,0:T(8,128)(2,1)S(1)}, u32[]{:S(2)}, u32[]{:S(2)}) collective-permute-start(s16[80,256]{1,0:T(8,128)(2,1)S(1)} %get-tuple-element.31), channel_id=1, source_target_pairs={{0,12},{1,13},{2,14},{3,15},{4,8},{5,9},{6,10},{7,11},{8,4},{9,5},... | collective-permute-start | bytes 122888 | tf_op jit(solution)/shard_map/ppermute | solution.py:469
  24.6 4.9 %collective-permute-start.7 = (s16[80,256]{1,0:T(8,128)(2,1)S(1)}, s16[80,256]{1,0:T(8,128)(2,1)S(1)}, u32[]{:S(2)}, u32[]{:S(2)}) collective-permute-start(s16[80,256]{1,0:T(8,128)(2,1)S(1)} %get-tuple-element.32), channel_id=1, source_target_pairs={{0,8},{1,9},{2,10},{3,11},{4,12},{5,13},{6,14},{7,15},{8,0},{9,1},... | collective-permute-start | bytes 122888 | tf_op jit(solution)/shard_map/ppermute | solution.py:469
  24.6 4.9 %collective-permute-start.8 = (s16[80,256]{1,0:T(8,128)(2,1)S(1)}, s16[80,256]{1,0:T(8,128)(2,1)S(1)}, u32[]{:S(2)}, u32[]{:S(2)}) collective-permute-start(s16[80,256]{1,0:T(8,128)(2,1)S(1)} %get-tuple-element.33), channel_id=1, source_target_pairs={{0,4},{1,5},{2,6},{3,7},{4,0},{5,1},{6,2},{7,3},{8,12},{9,13},{10,... | collective-permute-start | bytes 122888 | tf_op jit(solution)/shard_map/ppermute | solution.py:469
  29.6 1.3 %collective-permute-start.9 = (bf16[64,256]{1,0:T(8,128)(2,1)S(1)}, bf16[64,256]{1,0:T(8,128)(2,1)S(1)}, u32[]{:S(2)}, u32[]{:S(2)}) collective-permute-start(bf16[64,256]{1,0:T(8,128)(2,1)S(1)} %hidden_rows.1.own), channel_id=1, source_target_pairs={{0,16},{16,0},{1,17},{17,1},{2,18},{18,2},{3,19},{19,3},{4,20},{20... | collective-permute-start | bytes 98312 | tf_op jit(solution)/shard_map/ppermute | solution.py:520
  31.6 10.9 %all-to-all-start = ((bf16[16,8,256]{2,1,0:T(8,128)(2,1)}), bf16[16,8,256]{2,1,0:T(8,128)(2,1)S(1)}, u32[]{:S(2)}, u32[]{:S(2)}) async-start(bf16[16,8,256]{2,1,0:T(8,128)(2,1)} %bitcast.8), calls=%async_computation | async-start | bytes 131072 | tf_op jit(solution)/shard_map/all_to_all | solution.py:522

commit v13 on v12

--- a/solution.py
+++ b/solution.py
@@ -15,18 +15,8 @@
 
 
 def group_of(core, place, groups):
-    return 2 * place + 1 - core
-
-
-def group_order(n):
-    first = n * 9 // 16
-    return [first] + [i for i in range(n - 1, -1, -1) if i != first]
-
-
-def ordered(block, n):
-    first = n * 9 // 16
-    down = n - block
-    return jnp.where(block == 0, first, jnp.where(down > first, down, down - 1))
+    pair = 2 * (place // 2) + core
+    return pair if place % 2 == 0 else groups - 1 - pair
 
 
 LN2 = 0.6931471805599453
@@ -176,12 +166,12 @@
     k_n = jnp.bitwise_and(q_n, slots - 1)
     for k in range(slots):
         picked = jnp.where(k_n == k, mine[k:k + 1, :], picked)
-    good = jnp.logical_and(ordered(lax.div(q_n, slots), n) == r_n, k_n < cnt)
+    good = jnp.logical_and(n - 1 - lax.div(q_n, slots) == r_n, k_n < cnt)
     row = jnp.sum(jnp.where(good, picked + 1.0, 0.0), axis=1, keepdims=True) - 1.0
     lane = lax.broadcasted_iota(jnp.int32, (1, sel.shape[1]), 1)
     name = jnp.zeros(lane.shape, jnp.int32)
-    names = [group_of(c, i, groups) for c in (core, 1 - core) for i in range(groups // 2)]
-    for i, g in enumerate(names):
+    for i in range(groups // 2):
+        g = group_of(core, i, groups)
         name = jnp.where(lax.div(lane, UNIT) == i, g * UNIT + jnp.bitwise_and(lane, UNIT - 1), name)
     sel[...] = jnp.where(row == name.astype(jnp.float32), 1.0, 0.0).astype(jnp.bfloat16)
 
@@ -192,7 +182,7 @@
     vmem = pl.BlockSpec(memory_space=pltpu.VMEM)
     return pl.pallas_call(
         functools.partial(select_kernel, groups),
-        out_shape=jax.ShapeDtypeStruct((n * slots, groups * UNIT), jnp.bfloat16),
+        out_shape=jax.ShapeDtypeStruct((n * slots, groups // 2 * UNIT), jnp.bfloat16),
         in_specs=[smem, vmem, vmem],
         out_specs=vmem,
         compiler_params=pltpu.CompilerParams(vmem_limit_bytes=32 * 1024 * 1024),
@@ -365,45 +355,35 @@
 
 
 def hidden_kernel(chunks, parts, rows, *refs):
-    out = refs[chunks * parts]
+    sel, own, send = refs[chunks * parts:]
     for c in range(chunks):
-        own, coded = refs[c * parts], refs[c * parts + 1:(c + 1) * parts]
-        total = own[:rows, :]
+        mine, coded = refs[c * parts], refs[c * parts + 1:(c + 1) * parts]
+        total = mine[:rows, :]
         for a in coded:
             total = total + read_coded(a, 1, rows)(0)
-        out[c * rows:(c + 1) * rows, :] = jnp.maximum(total, 0.0).astype(jnp.bfloat16)
-
-
-def hidden_rows(chunk_parts, rows):
+        own[c * rows:(c + 1) * rows, :] = jnp.maximum(total, 0.0).astype(jnp.bfloat16)
+    picked = jnp.dot(sel[...], own[...], preferred_element_type=jnp.float32).astype(jnp.bfloat16)
+    half = picked.shape[0]
+    send[:half, :] = picked
+    send[half:, :] = picked
+
+
+def hidden_rows(chunk_parts, rows, sel):
     chunks, parts = len(chunk_parts), len(chunk_parts[0])
     width = chunk_parts[0][0].shape[1]
     vmem = pl.BlockSpec(memory_space=pltpu.VMEM)
     flat = [a for part in chunk_parts for a in part]
     return pl.pallas_call(
         functools.partial(hidden_kernel, chunks, parts, rows),
-        out_shape=jax.ShapeDtypeStruct((chunks * rows, width), jnp.bfloat16),
-        in_specs=[vmem] * len(flat),
-        out_specs=vmem,
+        out_shape=[
+            jax.ShapeDtypeStruct((chunks * rows, width), jnp.bfloat16),
+            jax.ShapeDtypeStruct((2 * sel.shape[0], width), jnp.bfloat16),
+        ],
+        in_specs=[vmem] * (len(flat) + 1),
+        out_specs=[vmem] * 2,
         compiler_params=pltpu.CompilerParams(vmem_limit_bytes=32 * 1024 * 1024),
         name="hidden_rows",
-    )(*flat)
-
-
-def send_kernel(own, other, sel, send):
-    both = jnp.concatenate([own[...], other[...]], axis=0)
-    send[...] = jnp.dot(sel[...], both, preferred_element_type=jnp.float32).astype(jnp.bfloat16)
-
-
-def rows_to_send(own, other, sel):
-    vmem = pl.BlockSpec(memory_space=pltpu.VMEM)
-    return pl.pallas_call(
-        send_kernel,
-        out_shape=pltpu.VMEM((sel.shape[0], own.shape[1]), jnp.bfloat16),
-        in_specs=[vmem] * 3,
-        out_specs=vmem,
-        compiler_params=pltpu.CompilerParams(vmem_limit_bytes=32 * 1024 * 1024),
-        name="rows_to_send",
-    )(own, other, sel)
+    )(*flat, sel)
 
 
 def local_kernel(n, groups, ids, own, other, adj, w_self, part, logits, adj_out, hidden):
@@ -420,7 +400,7 @@
     count = adj.shape[1] - tile
     slots = count // n
     column = lax.broadcasted_iota(jnp.int32, (1, count), 1)
-    source = ordered(lax.div(column, slots), n) * slots + lax.rem(column, slots)
+    source = (n - 1 - lax.div(column, slots)) * slots + lax.rem(column, slots)
     moved = jnp.where(lax.broadcasted_iota(jnp.int32, (count, count), 0) == source, 1.0, 0.0).astype(jnp.bfloat16)
     adj_out[...] = jnp.dot(adj[:, tile:], moved, preferred_element_type=jnp.float32).astype(jnp.bfloat16)
 
@@ -445,7 +425,9 @@
 
 
 def logits_kernel(part, logits, received, adj, w_neigh, out):
-    mean = part[...] + jnp.dot(adj[...], received[...], preferred_element_type=jnp.float32)
+    half = received.shape[0] // 2
+    rows = received[:half, :].astype(jnp.float32) + received[half:, :].astype(jnp.float32)
+    mean = part[...] + jnp.dot(adj[...], rows.astype(jnp.bfloat16), preferred_element_type=jnp.float32)
     dims = (((1,), (1,)), ((), ()))
     got = lax.dot_general(mean.astype(jnp.bfloat16), w_neigh[...], dims, preferred_element_type=jnp.float32)
     out[...] = logits[...] + got
@@ -516,10 +498,10 @@
             stride *= ways
         done.append(got)
     sel = selection(groups, ids, send_list, send_count)
-    own = hidden_rows(done, per * UNIT)
+    own, send = hidden_rows(done, per * UNIT, sel)
     other = lax.ppermute(own, "feat", swap)
-    send = rows_to_send(own, other, sel)
-    received = lax.all_to_all(send, "dom", 0, 0, axis_index_groups=[group_order(n)], tiled=True)
+    backwards = [list(range(2 * n - 1, -1, -1))]
+    received = lax.all_to_all(send, ("feat", "dom"), 0, 0, axis_index_groups=backwards, tiled=True)
     part, logits, adj = local_terms(n, groups, ids, own, other, adj_two, w_self2)
     return logits_of(part, logits, received, adj, w_neigh2)
 

time: 43.5 us -> 43.1 us (level)
  starting transfers between devices: 16.3 us -> 14.2 us
  waiting for transfers between devices: 13.6 us -> 15.1 us
    all_to_all x1, starting transfers between devices: 6.41 us -> 3.48 us  [body(): lax.all_to_all(send, ('feat', 'dom'), 0, 0, axis_index_groups=backwards,...]
    all_to_all x1, waiting for transfers between devices: 3.8 us -> 6.26 us  [body(): lax.all_to_all(send, ('feat', 'dom'), 0, 0, axis_index_groups=backwards,...]
    ppermute x6, waiting for transfers between devices: 9.26 us -> 7.89 us  [exchange(): lax.ppermute(parts[k], 'dom', [(i, i ^ k * stride) for i in range(n)])]
    pallas_call x1 -> x0, Pallas kernels: 0.78 us -> none  [rows_to_send(): pl.pallas_call(send_kernel, out_shape=pltpu.VMEM((sel.shape[0], own.shape...]
    pallas_call x1, Pallas kernels: 0.04 us -> 0.82 us  [hidden_rows(): pl.pallas_call(functools.partial(hidden_kernel, chunks, parts, rows), out...]
    ppermute x6, starting transfers between devices: 8.84 us -> 9.47 us  [exchange(): lax.ppermute(parts[k], 'dom', [(i, i ^ k * stride) for i in range(n)])]
    ppermute x1, waiting for transfers between devices: 0.49 us -> 0.96 us  [body(): other = lax.ppermute(own, 'feat', swap)]
  transfers between devices with their start and end apart: 11 -> 11, of which waited for: 7 -> 7; matrix products, arithmetic and copies ran while one was open for 0% -> 0% of each run, Pallas kernels for 26% -> 27%
where the time goes in v13:
time: 43.1 us; the launch traced here: 43 us
  waiting for transfers between devices  15.1 us (35%)
  starting transfers between devices  14.2 us (33%)
  Pallas kernels  13.4 us (31%)
    ppermute x6, starting transfers between devices, exchange(): lax.ppermute(parts[k], 'dom', [(i, i ^ k * stride) for i in range(n)])  9.47 us
    ppermute x6, waiting for transfers between devices, exchange(): lax.ppermute(parts[k], 'dom', [(i, i ^ k * stride) for i in range(n)])  7.89 us
    all_to_all x1, waiting for transfers between devices, body(): lax.all_to_all(send, ('feat', 'dom'), 0, 0, axis_index_groups=backwards,...  6.26 us
    pallas_call x1, Pallas kernels, gathered_sums(): pl.pallas_call(tiles_kernel, out_shape=[sums] * parts, in_specs=[vmem] *...  4.64 us
    all_to_all x1, starting transfers between devices, body(): lax.all_to_all(send, ('feat', 'dom'), 0, 0, axis_index_groups=backwards,...  3.48 us
    pallas_call x1, Pallas kernels, plan(): pl.pallas_call(functools.partial(plan_kernel, chunks, per, n, radix, n_sr...  2.68 us
    pallas_call x3, Pallas kernels, sent_terms(): pl.pallas_call(functools.partial(sent_kernel, k, slots, rows, len(accs)),...  1.55 us
    pallas_call x1, Pallas kernels, own_terms(): pl.pallas_call(functools.partial(own_kernel, chunk, per, groups, len(accs...  1.24 us
  transfers between devices with their start and end apart: 11, of which 7 were waited for; matrix products, arithmetic and copies ran while one was open for 0% of the time, Pallas kernels for 27%

profile of v13, /device:TPU:0, one launch (start us, length us, event | category | flops | bytes accessed | tf_op | source)
XLA Modules:
  0.0 43.0 jit_solution(4180428031662758906)
XLA Ops:
  0.0 0.5 %collective-permute-start.1 = (bf16[1024,512]{1,0:T(8,128)(2,1)}, bf16[1024,512]{1,0:T(8,128)(2,1)S(1)}, u32[]{:S(2)}, u32[]{:S(2)}) collective-permute-start(bf16[1024,512]{1,0:T(8,128)(2,1)} %xo.1), channel_id=1, source_target_pairs={{0,16},{16,0},{1,17},{17,1},{2,18},{18,2},{3,19},{19,3},{4,20},{20... | collective-permute-start | bytes 3145736 | tf_op jit(solution)/shard_map/ppermute | solution.py:478
  0.5 0.1 collective-permute-start
  0.5 0.5 %collective-permute-start.2 = (bf16[512,256]{1,0:T(8,128)(2,1)}, bf16[512,256]{1,0:T(8,128)(2,1)S(1)}, u32[]{:S(2)}, u32[]{:S(2)}) collective-permute-start(bf16[512,256]{1,0:T(8,128)(2,1)} %so.1), channel_id=1, source_target_pairs={{0,16},{16,0},{1,17},{17,1},{2,18},{18,2},{3,19},{19,3},{4,20},{20... | collective-permute-start | bytes 786440 | tf_op jit(solution)/shard_map/ppermute | solution.py:480
  1.0 0.1 pad_add_fusion.ids
  1.0 2.7 %plan.1 = (s32[2,640]{1,0:T(2,128)S(1)}, bf16[512,16,128]{2,1,0:T(8,128)(2,1)S(1)}, bf16[1024,512]{1,0:T(8,128)(2,1)S(1)}, bf16[512,256]{1,0:T(8,128)(2,1)S(1)}, bf16[512,256]{1,0:T(8,128)(2,1)S(1)}) custom-call(s32[2]{0:T(128)S(1)} %pad_add_fusion.ids, s32[1,128]{1,0:T(1,128)} %bitcast.16, s32[1,128]{1,0:T(1,128)} %bitcast.17, s32[1,128]{1,0:T(1,128)} %bitcast.18, ...), custom_call_target="tpu_custom_call" | custom-call | tf_op jit(solution)/shard_map/plan/pallas_call | solution.py:131
  3.7 0.0 collective-permute-done.1.xp
  3.7 4.6 %gathered_sums.1 = (f32[1040,256]{1,0:T(8,128)S(1)}, f32[1040,256]{1,0:T(8,128)S(1)}, f32[1040,256]{1,0:T(8,128)S(1)}, f32[1040,256]{1,0:T(8,128)S(1)}) custom-call(s32[2,640]{1,0:T(2,128)S(1)} %get-tuple-element.26.table_v, bf16[512,16,128]{2,1,0:T(8,128)(2,1)S(1)} %get-tuple-element.27.tbuf, bf16[1024,512]{1,0:T(8,128)(2,1)S(1)} %get-tuple-element.24.xo, ...), custom_call_target="tpu_custom_call" | custom-call | flops 2147483648 | bytes 8388608 | tf_op jit(solution)/shard_map/gathered_sums/pallas_call | solution.py:237
  8.4 0.0 collective-permute-done.wp
  8.4 0.5 %sent_terms.5 = s16[272,256]{1,0:T(8,128)(2,1)S(1)} custom-call(bf16[512,256]{1,0:T(8,128)(2,1)S(1)} %get-tuple-element.23.wo, bf16[512,256]{1,0:T(8,128)(2,1)S(1)} %collective-permute-done.wp, f32[1040,256]{1,0:T(8,128)S(1)} %get-tuple-element.28.refs_0_, f32[1040,256]{1,0:T(8,128)S(1)} %get-tuple-element.29.refs_1_, ...), custom_call_target="tpu_custom_call" | custom-call | flops 268435456 | bytes 2097152 | tf_op jit(solution)/shard_map/sent_terms/pallas_call | solution.py:281
  8.9 3.5 %collective-permute-start.5 = (s16[272,256]{1,0:T(8,128)(2,1)S(1)}, s16[272,256]{1,0:T(8,128)(2,1)S(1)}, u32[]{:S(2)}, u32[]{:S(2)}) collective-permute-start(s16[272,256]{1,0:T(8,128)(2,1)S(1)} %sent_terms.5), channel_id=1, source_target_pairs={{0,3},{1,2},{2,1},{3,0},{4,7},{5,6},{6,5},{7,4},{8,11},{9,10},{10,... | collective-permute-start | bytes 417800 | tf_op jit(solution)/shard_map/ppermute | solution.py:451
  12.4 0.5 %sent_terms.4 = s16[272,256]{1,0:T(8,128)(2,1)S(1)} custom-call(bf16[512,256]{1,0:T(8,128)(2,1)S(1)} %get-tuple-element.23.wo, bf16[512,256]{1,0:T(8,128)(2,1)S(1)} %collective-permute-done.wp, f32[1040,256]{1,0:T(8,128)S(1)} %get-tuple-element.28.refs_0_, f32[1040,256]{1,0:T(8,128)S(1)} %get-tuple-element.29.refs_1_, ...), custom_call_target="tpu_custom_call" | custom-call | flops 268435456 | bytes 2097152 | tf_op jit(solution)/shard_map/sent_terms/pallas_call | solution.py:281
  12.9 0.6 %collective-permute-start.4 = (s16[272,256]{1,0:T(8,128)(2,1)S(1)}, s16[272,256]{1,0:T(8,128)(2,1)S(1)}, u32[]{:S(2)}, u32[]{:S(2)}) collective-permute-start(s16[272,256]{1,0:T(8,128)(2,1)S(1)} %sent_terms.4), channel_id=1, source_target_pairs={{0,2},{1,3},{2,0},{3,1},{4,6},{5,7},{6,4},{7,5},{8,10},{9,11},{10,... | collective-permute-start | bytes 417800 | tf_op jit(solution)/shard_map/ppermute | solution.py:451
  13.5 0.5 %sent_terms.3 = s16[272,256]{1,0:T(8,128)(2,1)S(1)} custom-call(bf16[512,256]{1,0:T(8,128)(2,1)S(1)} %get-tuple-element.23.wo, bf16[512,256]{1,0:T(8,128)(2,1)S(1)} %collective-permute-done.wp, f32[1040,256]{1,0:T(8,128)S(1)} %get-tuple-element.28.refs_0_, f32[1040,256]{1,0:T(8,128)S(1)} %get-tuple-element.29.refs_1_, ...), custom_call_target="tpu_custom_call" | custom-call | flops 268435456 | bytes 2097152 | tf_op jit(solution)/shard_map/sent_terms/pallas_call | solution.py:281
  14.0 1.0 %collective-permute-start.3 = (s16[272,256]{1,0:T(8,128)(2,1)S(1)}, s16[272,256]{1,0:T(8,128)(2,1)S(1)}, u32[]{:S(2)}, u32[]{:S(2)}) collective-permute-start(s16[272,256]{1,0:T(8,128)(2,1)S(1)} %sent_terms.3), channel_id=1, source_target_pairs={{0,1},{1,0},{2,3},{3,2},{4,5},{5,4},{6,7},{7,6},{8,9},{9,8},{10,11... | collective-permute-start | bytes 417800 | tf_op jit(solution)/shard_map/ppermute | solution.py:451
  15.0 0.0 collective-permute-done.2.sp
  15.0 0.0 copy-start.2
  15.0 0.0 copy-start.4
  15.0 1.2 %own_terms.1.own = f32[256,256]{1,0:T(8,128)S(1)} custom-call(s32[2]{0:T(128)S(1)} %pad_add_fusion.ids, bf16[512,256]{1,0:T(8,128)(2,1)S(1)} %get-tuple-element.23.wo, bf16[512,256]{1,0:T(8,128)(2,1)S(1)} %collective-permute-done.wp, bf16[1024,512]{1,0:T(8,128)(2,1)S(1)} %get-tuple-element.24.xo, bf16[1024,512]{1,0:T(8,128)(2,1)S(1)} %collective-permute-done.1.xp, ...), custom_call_target="tpu_custom_call" | custom-call | flops 268435456 | bytes 2097152 | tf_op jit(solution)/shard_map/own_terms/pallas_call | solution.py:312
  16.2 0.0 copy-start
  16.3 0.0 copy-start.3
  16.3 0.0 copy-start.1
  16.3 0.5 %collective-permute-done.5.refs_2_ = s16[272,256]{1,0:T(8,128)(2,1)S(1)} collective-permute-done((s16[272,256]{1,0:T(8,128)(2,1)S(1)}, s16[272,256]{1,0:T(8,128)(2,1)S(1)}, u32[]{:S(2)}, u32[]{:S(2)}) %collective-permute-start.5) | collective-permute-done | bytes 139296 | tf_op jit(solution)/shard_map/ppermute | solution.py:451
  16.8 3.0 %collective-permute-done.4.refs_1_ = s16[272,256]{1,0:T(8,128)(2,1)S(1)} collective-permute-done((s16[272,256]{1,0:T(8,128)(2,1)S(1)}, s16[272,256]{1,0:T(8,128)(2,1)S(1)}, u32[]{:S(2)}, u32[]{:S(2)}) %collective-permute-start.4) | collective-permute-done | bytes 139296 | tf_op jit(solution)/shard_map/ppermute | solution.py:451
  19.8 1.1 %collective-permute-done.3.refs_0_ = s16[272,256]{1,0:T(8,128)(2,1)S(1)} collective-permute-done((s16[272,256]{1,0:T(8,128)(2,1)S(1)}, s16[272,256]{1,0:T(8,128)(2,1)S(1)}, u32[]{:S(2)}, u32[]{:S(2)}) %collective-permute-start.3) | collective-permute-done | bytes 139296 | tf_op jit(solution)/shard_map/ppermute | solution.py:451
  20.9 0.2 combine.1
  21.0 3.6 %collective-permute-start.6 = (s16[80,256]{1,0:T(8,128)(2,1)S(1)}, s16[80,256]{1,0:T(8,128)(2,1)S(1)}, u32[]{:S(2)}, u32[]{:S(2)}) collective-permute-start(s16[80,256]{1,0:T(8,128)(2,1)S(1)} %get-tuple-element.33), channel_id=1, source_target_pairs={{0,12},{1,13},{2,14},{3,15},{4,8},{5,9},{6,10},{7,11},{8,4},{9,5},... | collective-permute-start | bytes 122888 | tf_op jit(solution)/shard_map/ppermute | solution.py:451
  24.6 0.0 collective-permute-start.7
  24.6 0.9 %collective-permute-start.8 = (s16[80,256]{1,0:T(8,128)(2,1)S(1)}, s16[80,256]{1,0:T(8,128)(2,1)S(1)}, u32[]{:S(2)}, u32[]{:S(2)}) collective-permute-start(s16[80,256]{1,0:T(8,128)(2,1)S(1)} %get-tuple-element.35), channel_id=1, source_target_pairs={{0,4},{1,5},{2,6},{3,7},{4,0},{5,1},{6,2},{7,3},{8,12},{9,13},{10,... | collective-permute-start | bytes 122888 | tf_op jit(solution)/shard_map/ppermute | solution.py:451
  25.5 0.0 copy-done.2
  25.5 0.0 copy-done.4
  25.5 0.7 %selection.1.refs_4_ = bf16[128,64]{1,0:T(8,128)(2,1)S(1)} custom-call(s32[2]{0:T(128)S(1)} %pad_add_fusion.ids, s32[16,8,16]{2,1,0:T(8,128)S(1)} %bitcast.14, s32[16,16]{1,0:T(8,128)S(1)} %copy-done.4), custom_call_target="tpu_custom_call" | custom-call | tf_op jit(solution)/shard_map/selection/pallas_call | solution.py:183
  26.2 0.8 %collective-permute-done.6.refs_1_ = s16[80,256]{1,0:T(8,128)(2,1)S(1)} collective-permute-done((s16[80,256]{1,0:T(8,128)(2,1)S(1)}, s16[80,256]{1,0:T(8,128)(2,1)S(1)}, u32[]{:S(2)}, u32[]{:S(2)}) %collective-permute-start.6) | collective-permute-done | bytes 40992 | tf_op jit(solution)/shard_map/ppermute | solution.py:451
  27.0 2.5 %collective-permute-done.7.refs_2_ = s16[80,256]{1,0:T(8,128)(2,1)S(1)} collective-permute-done((s16[80,256]{1,0:T(8,128)(2,1)S(1)}, s16[80,256]{1,0:T(8,128)(2,1)S(1)}, u32[]{:S(2)}, u32[]{:S(2)}) %collective-permute-start.7) | collective-permute-done | bytes 40992 | tf_op jit(solution)/shard_map/ppermute | solution.py:451
  29.5 0.0 collective-permute-done.8.refs_3_
  29.5 0.8 %hidden_rows.1 = (bf16[64,256]{1,0:T(8,128)(2,1)S(1)}, bf16[256,256]{1,0:T(8,128)(2,1)}) custom-call(f32[64,256]{1,0:T(8,128)S(1)} %get-tuple-element.32.refs_0_, s16[80,256]{1,0:T(8,128)(2,1)S(1)} %collective-permute-done.6.refs_1_, s16[80,256]{1,0:T(8,128)(2,1)S(1)} %collective-permute-done.7.refs_2_, s16[80,256]{1,0:T(8,128)(2,1)S(1)} %collective-permute-done.8.refs_3_, ...), custom_call_target="tpu_custom_call" | custom-call | tf_op jit(solution)/shard_map/hidden_rows/pallas_call | solution.py:376
  30.3 3.5 %all-to-all-start = ((bf16[32,8,256]{2,1,0:T(8,128)(2,1)}), bf16[32,8,256]{2,1,0:T(8,128)(2,1)S(1)}, u32[]{:S(2)}, u32[]{:S(2)}) async-start(bf16[32,8,256]{2,1,0:T(8,128)(2,1)} %bitcast.8), calls=%async_computation | async-start | bytes 262144 | tf_op jit(solution)/shard_map/all_to_all | solution.py:504
  33.8 0.3 collective-permute-start.9
  34.1 1.0 %collective-permute-done.9.other = bf16[64,256]{1,0:T(8,128)(2,1)S(1)} collective-permute-done((bf16[64,256]{1,0:T(8,128)(2,1)S(1)}, bf16[64,256]{1,0:T(8,128)(2,1)S(1)}, u32[]{:S(2)}, u32[]{:S(2)}) %collective-permute-start.9) | collective-permute-done | bytes 32800 | tf_op jit(solution)/shard_map/ppermute | solution.py:502
  35.1 0.0 copy-done
  35.1 0.0 copy-done.3
  35.1 0.7 %local_terms.1 = (f32[64,256]{1,0:T(8,128)S(1)}, f32[64,172]{1,0:T(8,128)S(1)}, bf16[64,128]{1,0:T(8,128)(2,1)S(1)}) custom-call(s32[2]{0:T(128)S(1)} %pad_add_fusion.ids, bf16[64,256]{1,0:T(8,128)(2,1)S(1)} %get-tuple-element.36.own, bf16[64,256]{1,0:T(8,128)(2,1)S(1)} %collective-permute-done.9.other, bf16[64,256]{1,0:T(8,128)(2,1)S(1)} %copy-done.3, ...), custom_call_target="tpu_custom_call" | custom-call | tf_op jit(solution)/shard_map/local_terms/pallas_call | solution.py:412
  35.8 6.3 %all-to-all-done = bf16[32,8,256]{2,1,0:T(8,128)(2,1)S(1)} async-done(((bf16[32,8,256]{2,1,0:T(8,128)(2,1)}), bf16[32,8,256]{2,1,0:T(8,128)(2,1)S(1)}, u32[]{:S(2)}, u32[]{:S(2)}) %all-to-all-start) | async-done | bytes 131104 | tf_op jit(solution)/shard_map/all_to_all | solution.py:504
  42.1 0.0 copy-done.1
  42.1 0.9 %logits.1 = f32[64,172]{1,0:T(8,128)} custom-call(f32[64,256]{1,0:T(8,128)S(1)} %get-tuple-element.37.part, f32[64,172]{1,0:T(8,128)S(1)} %get-tuple-element.38.logits, bf16[256,256]{1,0:T(8,128)(2,1)S(1)} %bitcast.11, bf16[64,128]{1,0:T(8,128)(2,1)S(1)} %get-tuple-element.40.adj, bf16[172,256]{1,0:T(8,128)(2,1)S(1)} %bitcast.13), custom_call_target="tpu_custom_call" | custom-call | tf_op jit(solution)/shard_map/logits/pallas_call | solution.py:438
Async XLA Ops:
  0.0 3.7 %collective-permute-start.1 = (bf16[1024,512]{1,0:T(8,128)(2,1)}, bf16[1024,512]{1,0:T(8,128)(2,1)S(1)}, u32[]{:S(2)}, u32[]{:S(2)}) collective-permute-start(bf16[1024,512]{1,0:T(8,128)(2,1)} %xo.1), channel_id=1, source_target_pairs={{0,16},{16,0},{1,17},{17,1},{2,18},{18,2},{3,19},{19,3},{4,20},{20... | collective-permute-start | bytes 3145736 | tf_op jit(solution)/shard_map/ppermute | solution.py:478
  0.5 7.9 %collective-permute-start = (bf16[512,256]{1,0:T(8,128)(2,1)}, bf16[512,256]{1,0:T(8,128)(2,1)S(1)}, u32[]{:S(2)}, u32[]{:S(2)}) collective-permute-start(bf16[512,256]{1,0:T(8,128)(2,1)} %wo.1), channel_id=1, source_target_pairs={{0,16},{16,0},{1,17},{17,1},{2,18},{18,2},{3,19},{19,3},{4,20},{20... | collective-permute-start | bytes 786440 | tf_op jit(solution)/shard_map/ppermute | solution.py:479
  0.5 14.5 %collective-permute-start.2 = (bf16[512,256]{1,0:T(8,128)(2,1)}, bf16[512,256]{1,0:T(8,128)(2,1)S(1)}, u32[]{:S(2)}, u32[]{:S(2)}) collective-permute-start(bf16[512,256]{1,0:T(8,128)(2,1)} %so.1), channel_id=1, source_target_pairs={{0,16},{16,0},{1,17},{17,1},{2,18},{18,2},{3,19},{19,3},{4,20},{20... | collective-permute-start | bytes 786440 | tf_op jit(solution)/shard_map/ppermute | solution.py:480
  8.9 7.9 %collective-permute-start.5 = (s16[272,256]{1,0:T(8,128)(2,1)S(1)}, s16[272,256]{1,0:T(8,128)(2,1)S(1)}, u32[]{:S(2)}, u32[]{:S(2)}) collective-permute-start(s16[272,256]{1,0:T(8,128)(2,1)S(1)} %sent_terms.5), channel_id=1, source_target_pairs={{0,3},{1,2},{2,1},{3,0},{4,7},{5,6},{6,5},{7,4},{8,11},{9,10},{10,... | collective-permute-start | bytes 417800 | tf_op jit(solution)/shard_map/ppermute | solution.py:451
  12.9 6.9 %collective-permute-start.4 = (s16[272,256]{1,0:T(8,128)(2,1)S(1)}, s16[272,256]{1,0:T(8,128)(2,1)S(1)}, u32[]{:S(2)}, u32[]{:S(2)}) collective-permute-start(s16[272,256]{1,0:T(8,128)(2,1)S(1)} %sent_terms.4), channel_id=1, source_target_pairs={{0,2},{1,3},{2,0},{3,1},{4,6},{5,7},{6,4},{7,5},{8,10},{9,11},{10,... | collective-permute-start | bytes 417800 | tf_op jit(solution)/shard_map/ppermute | solution.py:451
  14.0 6.8 %collective-permute-start.3 = (s16[272,256]{1,0:T(8,128)(2,1)S(1)}, s16[272,256]{1,0:T(8,128)(2,1)S(1)}, u32[]{:S(2)}, u32[]{:S(2)}) collective-permute-start(s16[272,256]{1,0:T(8,128)(2,1)S(1)} %sent_terms.3), channel_id=1, source_target_pairs={{0,1},{1,0},{2,3},{3,2},{4,5},{5,4},{6,7},{7,6},{8,9},{9,8},{10,11... | collective-permute-start | bytes 417800 | tf_op jit(solution)/shard_map/ppermute | solution.py:451
  15.0 10.5 %copy-start.2 = (s32[16,16,8]{1,2,0:T(8,128)S(1)}, s32[16,16,8]{1,2,0:T(8,128)}, u32[]{:S(2)}) copy-start(s32[16,16,8]{1,2,0:T(8,128)} %param.19) | copy-start | bytes 24580
  15.0 10.5 %copy-start.4 = (s32[16,16]{1,0:T(8,128)S(1)}, s32[16,16]{1,0:T(8,128)}, u32[]{:S(2)}) copy-start(s32[16,16]{1,0:T(8,128)} %counts.1) | copy-start | bytes 3076
  16.2 18.8 %copy-start = (bf16[256,172]{0,1:T(8,128)(2,1)S(1)}, bf16[256,172]{0,1:T(8,128)(2,1)}, u32[]{:S(2)}) copy-start(bf16[256,172]{0,1:T(8,128)(2,1)} %param.22) | copy-start | bytes 264196
  16.3 18.8 %copy-start.3 = (bf16[64,256]{1,0:T(8,128)(2,1)S(1)}, bf16[64,256]{1,0:T(8,128)(2,1)}, u32[]{:S(2)}) copy-start(bf16[64,256]{1,0:T(8,128)(2,1)} %adj.1) | copy-start | bytes 98308
  16.3 25.8 %copy-start.1 = (bf16[256,172]{0,1:T(8,128)(2,1)S(1)}, bf16[256,172]{0,1:T(8,128)(2,1)}, u32[]{:S(2)}) copy-start(bf16[256,172]{0,1:T(8,128)(2,1)} %param.23) | copy-start | bytes 264196
  21.0 5.9 %collective-permute-start.6 = (s16[80,256]{1,0:T(8,128)(2,1)S(1)}, s16[80,256]{1,0:T(8,128)(2,1)S(1)}, u32[]{:S(2)}, u32[]{:S(2)}) collective-permute-start(s16[80,256]{1,0:T(8,128)(2,1)S(1)} %get-tuple-element.33), channel_id=1, source_target_pairs={{0,12},{1,13},{2,14},{3,15},{4,8},{5,9},{6,10},{7,11},{8,4},{9,5},... | collective-permute-start | bytes 122888 | tf_op jit(solution)/shard_map/ppermute | solution.py:451
  24.6 4.9 %collective-permute-start.7 = (s16[80,256]{1,0:T(8,128)(2,1)S(1)}, s16[80,256]{1,0:T(8,128)(2,1)S(1)}, u32[]{:S(2)}, u32[]{:S(2)}) collective-permute-start(s16[80,256]{1,0:T(8,128)(2,1)S(1)} %get-tuple-element.34), channel_id=1, source_target_pairs={{0,8},{1,9},{2,10},{3,11},{4,12},{5,13},{6,14},{7,15},{8,0},{9,1},... | collective-permute-start | bytes 122888 | tf_op jit(solution)/shard_map/ppermute | solution.py:451
  24.6 4.9 %collective-permute-start.8 = (s16[80,256]{1,0:T(8,128)(2,1)S(1)}, s16[80,256]{1,0:T(8,128)(2,1)S(1)}, u32[]{:S(2)}, u32[]{:S(2)}) collective-permute-start(s16[80,256]{1,0:T(8,128)(2,1)S(1)} %get-tuple-element.35), channel_id=1, source_target_pairs={{0,4},{1,5},{2,6},{3,7},{4,0},{5,1},{6,2},{7,3},{8,12},{9,13},{10,... | collective-permute-start | bytes 122888 | tf_op jit(solution)/shard_map/ppermute | solution.py:451
  30.3 11.8 %all-to-all-start = ((bf16[32,8,256]{2,1,0:T(8,128)(2,1)}), bf16[32,8,256]{2,1,0:T(8,128)(2,1)S(1)}, u32[]{:S(2)}, u32[]{:S(2)}) async-start(bf16[32,8,256]{2,1,0:T(8,128)(2,1)} %bitcast.8), calls=%async_computation | async-start | bytes 262144 | tf_op jit(solution)/shard_map/all_to_all | solution.py:504
  33.8 1.3 %collective-permute-start.9 = (bf16[64,256]{1,0:T(8,128)(2,1)S(1)}, bf16[64,256]{1,0:T(8,128)(2,1)S(1)}, u32[]{:S(2)}, u32[]{:S(2)}) collective-permute-start(bf16[64,256]{1,0:T(8,128)(2,1)S(1)} %get-tuple-element.36.own), channel_id=1, source_target_pairs={{0,16},{16,0},{1,17},{17,1},{2,18},{18,2},{3,19},{19,3},{4,20},{20... | collective-permute-start | bytes 98312 | tf_op jit(solution)/shard_map/ppermute | solution.py:502

commit v14 on v12

--- a/solution.py
+++ b/solution.py
@@ -15,18 +15,18 @@
 
 
 def group_of(core, place, groups):
-    return 2 * place + 1 - core
+    pair = 2 * (place // 2) + core
+    return pair if place % 2 == 0 else groups - 1 - pair
 
 
 def group_order(n):
     first = n * 9 // 16
-    return [first] + [i for i in range(n - 1, -1, -1) if i != first]
+    return [first] + [i for i in range(n) if i != first]
 
 
 def ordered(block, n):
     first = n * 9 // 16
-    down = n - block
-    return jnp.where(block == 0, first, jnp.where(down > first, down, down - 1))
+    return jnp.where(block == 0, first, jnp.where(block <= first, block - 1, block))
 
 
 LN2 = 0.6931471805599453
@@ -163,7 +163,7 @@
     ])
 
 
-def select_kernel(groups, ids, lists, counts, sel):
+def select_kernel(groups, ids, lists, counts, adj, sel, adj_out):
     core, me = ids[0], ids[1]
     n = lists.shape[0]
     slots = lists.shape[1]
@@ -184,20 +184,27 @@
     for i, g in enumerate(names):
         name = jnp.where(lax.div(lane, UNIT) == i, g * UNIT + jnp.bitwise_and(lane, UNIT - 1), name)
     sel[...] = jnp.where(row == name.astype(jnp.float32), 1.0, 0.0).astype(jnp.bfloat16)
-
-
-def selection(groups, ids, send_list, send_count):
+    column = lax.broadcasted_iota(jnp.int32, (1, total), 1)
+    source = ordered(lax.div(column, slots), n) * slots + lax.rem(column, slots)
+    moved = jnp.where(lax.broadcasted_iota(jnp.int32, (total, total), 0) == source, 1.0, 0.0).astype(jnp.bfloat16)
+    adj_out[...] = jnp.dot(adj[:, groups * UNIT:], moved, preferred_element_type=jnp.float32).astype(jnp.bfloat16)
+
+
+def selection(groups, ids, send_list, send_count, adj):
     n, _, slots = send_list.shape
     smem = pl.BlockSpec(memory_space=pltpu.SMEM)
     vmem = pl.BlockSpec(memory_space=pltpu.VMEM)
     return pl.pallas_call(
         functools.partial(select_kernel, groups),
-        out_shape=jax.ShapeDtypeStruct((n * slots, groups * UNIT), jnp.bfloat16),
-        in_specs=[smem, vmem, vmem],
-        out_specs=vmem,
+        out_shape=[
+            jax.ShapeDtypeStruct((n * slots, groups * UNIT), jnp.bfloat16),
+            jax.ShapeDtypeStruct((adj.shape[0], n * slots), jnp.bfloat16),
+        ],
+        in_specs=[smem, vmem, vmem, vmem],
+        out_specs=[vmem] * 2,
         compiler_params=pltpu.CompilerParams(vmem_limit_bytes=32 * 1024 * 1024),
         name="selection",
-    )(ids, jnp.swapaxes(send_list, 1, 2), send_count)
+    )(ids, jnp.swapaxes(send_list, 1, 2), send_count, adj)
 
 
 def tiles_kernel(table_v, tbuf, xo, xp, *rest):
@@ -398,7 +405,7 @@
     vmem = pl.BlockSpec(memory_space=pltpu.VMEM)
     return pl.pallas_call(
         send_kernel,
-        out_shape=pltpu.VMEM((sel.shape[0], own.shape[1]), jnp.bfloat16),
+        out_shape=jax.ShapeDtypeStruct((sel.shape[0], own.shape[1]), jnp.bfloat16),
         in_specs=[vmem] * 3,
         out_specs=vmem,
         compiler_params=pltpu.CompilerParams(vmem_limit_bytes=32 * 1024 * 1024),
@@ -406,7 +413,7 @@
     )(own, other, sel)
 
 
-def local_kernel(n, groups, ids, own, other, adj, w_self, part, logits, adj_out, hidden):
+def logits_kernel(groups, ids, own, other, received, adj, adj_received, w_self, w_neigh, out, hidden):
     core = ids[0]
     for i in range(groups // 2):
         mine = group_of(core, i, groups)
@@ -414,53 +421,26 @@
         hidden[pl.ds(pl.multiple_of(mine * UNIT, UNIT), UNIT), :] = own[i * UNIT:(i + 1) * UNIT, :]
         hidden[pl.ds(pl.multiple_of(theirs * UNIT, UNIT), UNIT), :] = other[i * UNIT:(i + 1) * UNIT, :]
     tile, rows = hidden.shape[0], adj.shape[0]
-    part[...] = jnp.dot(adj[:, :tile], hidden[...], preferred_element_type=jnp.float32)
+    mean = jnp.dot(adj_received[...], received[...], preferred_element_type=jnp.float32)
+    mean = mean + jnp.dot(adj[:, :tile], hidden[...], preferred_element_type=jnp.float32)
     dims = (((1,), (1,)), ((), ()))
-    logits[...] = lax.dot_general(hidden[:rows, :], w_self[...], dims, preferred_element_type=jnp.float32)
-    count = adj.shape[1] - tile
-    slots = count // n
-    column = lax.broadcasted_iota(jnp.int32, (1, count), 1)
-    source = ordered(lax.div(column, slots), n) * slots + lax.rem(column, slots)
-    moved = jnp.where(lax.broadcasted_iota(jnp.int32, (count, count), 0) == source, 1.0, 0.0).astype(jnp.bfloat16)
-    adj_out[...] = jnp.dot(adj[:, tile:], moved, preferred_element_type=jnp.float32).astype(jnp.bfloat16)
-
-
-def local_terms(n, groups, ids, own, other, adj, w_self):
+    got = lax.dot_general(hidden[:rows, :], w_self[...], dims, preferred_element_type=jnp.float32)
+    got = got + lax.dot_general(mean.astype(jnp.bfloat16), w_neigh[...], dims, preferred_element_type=jnp.float32)
+    out[...] = got
+
+
+def logits_of(groups, ids, own, other, received, adj, adj_received, w_self, w_neigh):
     smem = pl.BlockSpec(memory_space=pltpu.SMEM)
     vmem = pl.BlockSpec(memory_space=pltpu.VMEM)
-    width = own.shape[1]
-    return pl.pallas_call(
-        functools.partial(local_kernel, n, groups),
-        out_shape=[
-            jax.ShapeDtypeStruct((adj.shape[0], width), jnp.float32),
-            jax.ShapeDtypeStruct((adj.shape[0], w_self.shape[1]), jnp.float32),
-            jax.ShapeDtypeStruct((adj.shape[0], adj.shape[1] - groups * UNIT), jnp.bfloat16),
-        ],
-        in_specs=[smem] + [vmem] * 4,
-        out_specs=[vmem] * 3,
-        scratch_shapes=[pltpu.VMEM((groups * UNIT, width), jnp.bfloat16)],
-        compiler_params=pltpu.CompilerParams(vmem_limit_bytes=32 * 1024 * 1024),
-        name="local_terms",
-    )(ids, own, other, adj, w_self.T)
-
-
-def logits_kernel(part, logits, received, adj, w_neigh, out):
-    mean = part[...] + jnp.dot(adj[...], received[...], preferred_element_type=jnp.float32)
-    dims = (((1,), (1,)), ((), ()))
-    got = lax.dot_general(mean.astype(jnp.bfloat16), w_neigh[...], dims, preferred_element_type=jnp.float32)
-    out[...] = logits[...] + got
-
-
-def logits_of(part, logits, received, adj, w_neigh):
-    vmem = pl.BlockSpec(memory_space=pltpu.VMEM)
-    return pl.pallas_call(
-        logits_kernel,
-        out_shape=jax.ShapeDtypeStruct(logits.shape, jnp.float32),
-        in_specs=[vmem] * 5,
+    return pl.pallas_call(
+        functools.partial(logits_kernel, groups),
+        out_shape=jax.ShapeDtypeStruct((adj.shape[0], w_self.shape[1]), jnp.float32),
+        in_specs=[smem] + [vmem] * 7,
         out_specs=vmem,
+        scratch_shapes=[pltpu.VMEM((groups * UNIT, own.shape[1]), jnp.bfloat16)],
         compiler_params=pltpu.CompilerParams(vmem_limit_bytes=32 * 1024 * 1024),
         name="logits",
-    )(part, logits, received, adj, w_neigh.T)
+    )(ids, own, other, received, adj, adj_received, w_self.T, w_neigh.T)
 
 
 def exchange(parts, stride, n, places):
@@ -512,16 +492,15 @@
         for radix in radices[1:]:
             ways = 1 << radix
             parts = combine(n // stride, per * UNIT, ways, got[0], got[1:])
-            got = exchange(parts, stride, n, range(ways - 1, 0, -1))
+            got = exchange(parts, stride, n, (2, 3, 1) if ways == 4 else (1,))
             stride *= ways
         done.append(got)
-    sel = selection(groups, ids, send_list, send_count)
+    sel, adj_received = selection(groups, ids, send_list, send_count, adj_two)
     own = hidden_rows(done, per * UNIT)
     other = lax.ppermute(own, "feat", swap)
     send = rows_to_send(own, other, sel)
     received = lax.all_to_all(send, "dom", 0, 0, axis_index_groups=[group_order(n)], tiled=True)
-    part, logits, adj = local_terms(n, groups, ids, own, other, adj_two, w_self2)
-    return logits_of(part, logits, received, adj, w_neigh2)
+    return logits_of(groups, ids, own, other, received, adj_two, adj_received, w_self2, w_neigh2)
 
 
 def solution(mesh):

time: 43.5 us -> 42.7 us (0.982)
  blocking collectives: 0 us -> 10.5 us
  starting transfers between devices: 16.3 us -> 10.4 us
  waiting for transfers between devices: 13.6 us -> 8.79 us
  Pallas kernels: 13.4 us -> 12.6 us
    all_to_all x0 -> x1, blocking collectives: none -> 10.5 us  [body(): lax.all_to_all(send, 'dom', 0, 0, axis_index_groups=[group_order(n)], til...]
    all_to_all x1 -> x0, starting transfers between devices: 6.41 us -> none  [body(): lax.all_to_all(send, 'dom', 0, 0, axis_index_groups=[group_order(n)], til...]
    all_to_all x1 -> x0, waiting for transfers between devices: 3.8 us -> none  [body(): lax.all_to_all(send, 'dom', 0, 0, axis_index_groups=[group_order(n)], til...]
    ppermute x6, waiting for transfers between devices: 9.26 us -> 8.3 us  [exchange(): lax.ppermute(parts[k], 'dom', [(i, i ^ k * stride) for i in range(n)])]
    pallas_call x4 -> x3, Pallas kernels: 3.07 us -> 2.28 us  [the longest x1 1.46 us: logits_of(): pl.pallas_call(functools.partial(logits_kernel, groups), out_shape=jax.Sh...]
    ppermute x6, starting transfers between devices: 8.84 us -> 9.39 us  [exchange(): lax.ppermute(parts[k], 'dom', [(i, i ^ k * stride) for i in range(n)])]
  transfers between devices with their start and end apart: 11 -> 10, of which waited for: 7 -> 6; matrix products, arithmetic and copies ran while one was open for 0% -> 0% of each run, Pallas kernels for 26% -> 25%
where the time goes in v14:
time: 42.7 us; the launch traced here: 42.5 us
  Pallas kernels  12.6 us (30%)
  blocking collectives  10.5 us (25%)
  starting transfers between devices  10.4 us (24%)
  waiting for transfers between devices  8.79 us (21%)
    all_to_all x1, blocking collectives, body(): lax.all_to_all(send, 'dom', 0, 0, axis_index_groups=[group_order(n)], til...  10.5 us
    ppermute x6, starting transfers between devices, exchange(): lax.ppermute(parts[k], 'dom', [(i, i ^ k * stride) for i in range(n)])  9.39 us
    ppermute x6, waiting for transfers between devices, exchange(): lax.ppermute(parts[k], 'dom', [(i, i ^ k * stride) for i in range(n)])  8.3 us
    pallas_call x1, Pallas kernels, gathered_sums(): pl.pallas_call(tiles_kernel, out_shape=[sums] * parts, in_specs=[vmem] *...  4.57 us
    pallas_call x1, Pallas kernels, plan(): pl.pallas_call(functools.partial(plan_kernel, chunks, per, n, radix, n_sr...  2.68 us
    pallas_call x3, Pallas kernels, sent_terms(): pl.pallas_call(functools.partial(sent_kernel, k, slots, rows, len(accs)),...  1.55 us
    pallas_call x1, Pallas kernels, logits_of(): pl.pallas_call(functools.partial(logits_kernel, groups), out_shape=jax.Sh...  1.46 us
    pallas_call x1, Pallas kernels, own_terms(): pl.pallas_call(functools.partial(own_kernel, chunk, per, groups, len(accs...  1.25 us
  transfers between devices with their start and end apart: 10, of which 6 were waited for; matrix products, arithmetic and copies ran while one was open for 0% of the time, Pallas kernels for 25%

profile of v14, /device:TPU:0, one launch (start us, length us, event | category | flops | bytes accessed | tf_op | source)
XLA Modules:
  0.0 42.5 jit_solution(17064037171548757582)
XLA Ops:
  0.0 0.5 %collective-permute-start.1 = (bf16[1024,512]{1,0:T(8,128)(2,1)}, bf16[1024,512]{1,0:T(8,128)(2,1)S(1)}, u32[]{:S(2)}, u32[]{:S(2)}) collective-permute-start(bf16[1024,512]{1,0:T(8,128)(2,1)} %xo.1), channel_id=1, source_target_pairs={{0,16},{16,0},{1,17},{17,1},{2,18},{18,2},{3,19},{19,3},{4,20},{20... | collective-permute-start | bytes 3145736 | tf_op jit(solution)/shard_map/ppermute | solution.py:476
  0.5 0.1 collective-permute-start
  0.5 0.5 %collective-permute-start.2 = (bf16[512,256]{1,0:T(8,128)(2,1)}, bf16[512,256]{1,0:T(8,128)(2,1)S(1)}, u32[]{:S(2)}, u32[]{:S(2)}) collective-permute-start(bf16[512,256]{1,0:T(8,128)(2,1)} %so.1), channel_id=1, source_target_pairs={{0,16},{16,0},{1,17},{17,1},{2,18},{18,2},{3,19},{19,3},{4,20},{20... | collective-permute-start | bytes 786440 | tf_op jit(solution)/shard_map/ppermute | solution.py:478
  1.0 0.1 pad_add_fusion.ids
  1.0 2.7 %plan.1 = (s32[2,640]{1,0:T(2,128)S(1)}, bf16[512,16,128]{2,1,0:T(8,128)(2,1)S(1)}, bf16[1024,512]{1,0:T(8,128)(2,1)S(1)}, bf16[512,256]{1,0:T(8,128)(2,1)S(1)}, bf16[512,256]{1,0:T(8,128)(2,1)S(1)}) custom-call(s32[2]{0:T(128)S(1)} %pad_add_fusion.ids, s32[1,128]{1,0:T(1,128)} %bitcast.17, s32[1,128]{1,0:T(1,128)} %bitcast.18, s32[1,128]{1,0:T(1,128)} %bitcast.19, ...), custom_call_target="tpu_custom_call" | custom-call | tf_op jit(solution)/shard_map/plan/pallas_call | solution.py:141
  3.7 0.0 collective-permute-done.1.xp
  3.7 4.6 %gathered_sums.1 = (f32[1040,256]{1,0:T(8,128)S(1)}, f32[1040,256]{1,0:T(8,128)S(1)}, f32[1040,256]{1,0:T(8,128)S(1)}, f32[1040,256]{1,0:T(8,128)S(1)}) custom-call(s32[2,640]{1,0:T(2,128)S(1)} %get-tuple-element.23.table_v, bf16[512,16,128]{2,1,0:T(8,128)(2,1)S(1)} %get-tuple-element.24.tbuf, bf16[1024,512]{1,0:T(8,128)(2,1)S(1)} %get-tuple-element.21.xo, ...), custom_call_target="tpu_custom_call" | custom-call | flops 2147483648 | bytes 8388608 | tf_op jit(solution)/shard_map/gathered_sums/pallas_call | solution.py:254
  8.3 0.0 collective-permute-done.wp
  8.3 0.5 %sent_terms.5 = s16[272,256]{1,0:T(8,128)(2,1)S(1)} custom-call(bf16[512,256]{1,0:T(8,128)(2,1)S(1)} %get-tuple-element.20.wo, bf16[512,256]{1,0:T(8,128)(2,1)S(1)} %collective-permute-done.wp, f32[1040,256]{1,0:T(8,128)S(1)} %get-tuple-element.25.refs_0_, f32[1040,256]{1,0:T(8,128)S(1)} %get-tuple-element.26.refs_1_, ...), custom_call_target="tpu_custom_call" | custom-call | flops 268435456 | bytes 2097152 | tf_op jit(solution)/shard_map/sent_terms/pallas_call | solution.py:298
  8.9 4.4 %collective-permute-start.5 = (s16[272,256]{1,0:T(8,128)(2,1)S(1)}, s16[272,256]{1,0:T(8,128)(2,1)S(1)}, u32[]{:S(2)}, u32[]{:S(2)}) collective-permute-start(s16[272,256]{1,0:T(8,128)(2,1)S(1)} %sent_terms.5), channel_id=1, source_target_pairs={{0,3},{1,2},{2,1},{3,0},{4,7},{5,6},{6,5},{7,4},{8,11},{9,10},{10,... | collective-permute-start | bytes 417800 | tf_op jit(solution)/shard_map/ppermute | solution.py:449
  13.2 0.5 %sent_terms.4 = s16[272,256]{1,0:T(8,128)(2,1)S(1)} custom-call(bf16[512,256]{1,0:T(8,128)(2,1)S(1)} %get-tuple-element.20.wo, bf16[512,256]{1,0:T(8,128)(2,1)S(1)} %collective-permute-done.wp, f32[1040,256]{1,0:T(8,128)S(1)} %get-tuple-element.25.refs_0_, f32[1040,256]{1,0:T(8,128)S(1)} %get-tuple-element.26.refs_1_, ...), custom_call_target="tpu_custom_call" | custom-call | flops 268435456 | bytes 2097152 | tf_op jit(solution)/shard_map/sent_terms/pallas_call | solution.py:298
  13.7 0.6 %collective-permute-start.4 = (s16[272,256]{1,0:T(8,128)(2,1)S(1)}, s16[272,256]{1,0:T(8,128)(2,1)S(1)}, u32[]{:S(2)}, u32[]{:S(2)}) collective-permute-start(s16[272,256]{1,0:T(8,128)(2,1)S(1)} %sent_terms.4), channel_id=1, source_target_pairs={{0,2},{1,3},{2,0},{3,1},{4,6},{5,7},{6,4},{7,5},{8,10},{9,11},{10,... | collective-permute-start | bytes 417800 | tf_op jit(solution)/shard_map/ppermute | solution.py:449
  14.3 0.5 %sent_terms.3 = s16[272,256]{1,0:T(8,128)(2,1)S(1)} custom-call(bf16[512,256]{1,0:T(8,128)(2,1)S(1)} %get-tuple-element.20.wo, bf16[512,256]{1,0:T(8,128)(2,1)S(1)} %collective-permute-done.wp, f32[1040,256]{1,0:T(8,128)S(1)} %get-tuple-element.25.refs_0_, f32[1040,256]{1,0:T(8,128)S(1)} %get-tuple-element.26.refs_1_, ...), custom_call_target="tpu_custom_call" | custom-call | flops 268435456 | bytes 2097152 | tf_op jit(solution)/shard_map/sent_terms/pallas_call | solution.py:298
  14.9 0.1 collective-permute-start.3
  15.0 0.0 collective-permute-done.2.sp
  15.0 0.0 copy-start
  15.0 0.0 copy-start.3
  15.0 0.0 copy-start.4
  15.0 1.2 %own_terms.1.own = f32[256,256]{1,0:T(8,128)S(1)} custom-call(s32[2]{0:T(128)S(1)} %pad_add_fusion.ids, bf16[512,256]{1,0:T(8,128)(2,1)S(1)} %get-tuple-element.20.wo, bf16[512,256]{1,0:T(8,128)(2,1)S(1)} %collective-permute-done.wp, bf16[1024,512]{1,0:T(8,128)(2,1)S(1)} %get-tuple-element.21.xo, bf16[1024,512]{1,0:T(8,128)(2,1)S(1)} %collective-permute-done.1.xp, ...), custom_call_target="tpu_custom_call" | custom-call | flops 268435456 | bytes 2097152 | tf_op jit(solution)/shard_map/own_terms/pallas_call | solution.py:329
  16.2 0.0 copy-start.1
  16.3 0.0 copy-start.2
  16.3 1.4 %collective-permute-done.5.refs_2_ = s16[272,256]{1,0:T(8,128)(2,1)S(1)} collective-permute-done((s16[272,256]{1,0:T(8,128)(2,1)S(1)}, s16[272,256]{1,0:T(8,128)(2,1)S(1)}, u32[]{:S(2)}, u32[]{:S(2)}) %collective-permute-start.5) | collective-permute-done | bytes 139296 | tf_op jit(solution)/shard_map/ppermute | solution.py:449
  17.7 2.9 %collective-permute-done.4.refs_1_ = s16[272,256]{1,0:T(8,128)(2,1)S(1)} collective-permute-done((s16[272,256]{1,0:T(8,128)(2,1)S(1)}, s16[272,256]{1,0:T(8,128)(2,1)S(1)}, u32[]{:S(2)}, u32[]{:S(2)}) %collective-permute-start.4) | collective-permute-done | bytes 139296 | tf_op jit(solution)/shard_map/ppermute | solution.py:449
  20.6 0.0 collective-permute-done.3.refs_0_
  20.6 0.2 combine.1
  20.8 2.1 %collective-permute-start.6 = (s16[80,256]{1,0:T(8,128)(2,1)S(1)}, s16[80,256]{1,0:T(8,128)(2,1)S(1)}, u32[]{:S(2)}, u32[]{:S(2)}) collective-permute-start(s16[80,256]{1,0:T(8,128)(2,1)S(1)} %get-tuple-element.30), channel_id=1, source_target_pairs={{0,8},{1,9},{2,10},{3,11},{4,12},{5,13},{6,14},{7,15},{8,0},{9,1},... | collective-permute-start | bytes 122888 | tf_op jit(solution)/shard_map/ppermute | solution.py:449
  22.8 2.3 %collective-permute-start.7 = (s16[80,256]{1,0:T(8,128)(2,1)S(1)}, s16[80,256]{1,0:T(8,128)(2,1)S(1)}, u32[]{:S(2)}, u32[]{:S(2)}) collective-permute-start(s16[80,256]{1,0:T(8,128)(2,1)S(1)} %get-tuple-element.31), channel_id=1, source_target_pairs={{0,12},{1,13},{2,14},{3,15},{4,8},{5,9},{6,10},{7,11},{8,4},{9,5},... | collective-permute-start | bytes 122888 | tf_op jit(solution)/shard_map/ppermute | solution.py:449
  25.1 0.0 collective-permute-start.8
  25.1 1.1 %collective-permute-done.6.refs_1_ = s16[80,256]{1,0:T(8,128)(2,1)S(1)} collective-permute-done((s16[80,256]{1,0:T(8,128)(2,1)S(1)}, s16[80,256]{1,0:T(8,128)(2,1)S(1)}, u32[]{:S(2)}, u32[]{:S(2)}) %collective-permute-start.6) | collective-permute-done | bytes 40992 | tf_op jit(solution)/shard_map/ppermute | solution.py:449
  26.2 2.5 %collective-permute-done.7.refs_2_ = s16[80,256]{1,0:T(8,128)(2,1)S(1)} collective-permute-done((s16[80,256]{1,0:T(8,128)(2,1)S(1)}, s16[80,256]{1,0:T(8,128)(2,1)S(1)}, u32[]{:S(2)}, u32[]{:S(2)}) %collective-permute-start.7) | collective-permute-done | bytes 40992 | tf_op jit(solution)/shard_map/ppermute | solution.py:449
  28.6 0.5 %collective-permute-done.8.refs_3_ = s16[80,256]{1,0:T(8,128)(2,1)S(1)} collective-permute-done((s16[80,256]{1,0:T(8,128)(2,1)S(1)}, s16[80,256]{1,0:T(8,128)(2,1)S(1)}, u32[]{:S(2)}, u32[]{:S(2)}) %collective-permute-start.8) | collective-permute-done | bytes 40992 | tf_op jit(solution)/shard_map/ppermute | solution.py:449
  29.1 0.1 collective-permute-start.9
  29.2 0.0 copy-done
  29.2 0.0 copy-done.3
  29.2 0.0 copy-done.4
  29.2 0.7 %selection.1 = (bf16[128,128]{1,0:T(8,128)(2,1)S(1)}, bf16[64,128]{1,0:T(8,128)(2,1)S(1)}) custom-call(s32[2]{0:T(128)S(1)} %pad_add_fusion.ids, s32[16,8,16]{2,1,0:T(8,128)S(1)} %bitcast.15, s32[16,16]{1,0:T(8,128)S(1)} %copy-done.4, bf16[64,256]{1,0:T(8,128)(2,1)S(1)} %copy-done), custom_call_target="tpu_custom_call" | custom-call | tf_op jit(solution)/shard_map/selection/pallas_call | solution.py:197
  29.9 0.5 %collective-permute-done.9.other = bf16[64,256]{1,0:T(8,128)(2,1)S(1)} collective-permute-done((bf16[64,256]{1,0:T(8,128)(2,1)S(1)}, bf16[64,256]{1,0:T(8,128)(2,1)S(1)}, u32[]{:S(2)}, u32[]{:S(2)}) %collective-permute-start.9) | collective-permute-done | bytes 32800 | tf_op jit(solution)/shard_map/ppermute | solution.py:500
  30.4 0.1 rows_to_send.1
  30.6 10.5 %all_to_all.11 = bf16[16,8,256]{2,1,0:T(8,128)(2,1)S(1)} all-to-all(bf16[16,8,256]{2,1,0:T(8,128)(2,1)S(1)} %bitcast.11), channel_id=1, replica_groups={{9,0,1,2,3,4,5,6,7,8,10,11,12,13,14,15},{25,16,17,18,19,20,21,22,23,24,..., dimensions={0} | all-to-all | bytes 131072 | tf_op jit(solution)/shard_map/all_to_all | solution.py:502
  41.1 0.0 copy-done.1
  41.1 0.0 copy-done.2
  41.1 1.5 %logits.1 = f32[64,172]{1,0:T(8,128)} custom-call(s32[2]{0:T(128)S(1)} %pad_add_fusion.ids, bf16[64,256]{1,0:T(8,128)(2,1)S(1)} %hidden_rows.1.own, bf16[64,256]{1,0:T(8,128)(2,1)S(1)} %collective-permute-done.9.other, bf16[128,256]{1,0:T(8,128)(2,1)S(1)} %bitcast.12, bf16[64,256]{1,0:T(8,128)(2,1)S(1)} %copy-done, ...), custom_call_target="tpu_custom_call" | custom-call | tf_op jit(solution)/shard_map/logits/pallas_call | solution.py:435
  (1 shorter events, 0.0 us)
Async XLA Ops:
  0.0 3.7 %collective-permute-start.1 = (bf16[1024,512]{1,0:T(8,128)(2,1)}, bf16[1024,512]{1,0:T(8,128)(2,1)S(1)}, u32[]{:S(2)}, u32[]{:S(2)}) collective-permute-start(bf16[1024,512]{1,0:T(8,128)(2,1)} %xo.1), channel_id=1, source_target_pairs={{0,16},{16,0},{1,17},{17,1},{2,18},{18,2},{3,19},{19,3},{4,20},{20... | collective-permute-start | bytes 3145736 | tf_op jit(solution)/shard_map/ppermute | solution.py:476
  0.5 7.9 %collective-permute-start = (bf16[512,256]{1,0:T(8,128)(2,1)}, bf16[512,256]{1,0:T(8,128)(2,1)S(1)}, u32[]{:S(2)}, u32[]{:S(2)}) collective-permute-start(bf16[512,256]{1,0:T(8,128)(2,1)} %wo.1), channel_id=1, source_target_pairs={{0,16},{16,0},{1,17},{17,1},{2,18},{18,2},{3,19},{19,3},{4,20},{20... | collective-permute-start | bytes 786440 | tf_op jit(solution)/shard_map/ppermute | solution.py:477
  0.5 14.5 %collective-permute-start.2 = (bf16[512,256]{1,0:T(8,128)(2,1)}, bf16[512,256]{1,0:T(8,128)(2,1)S(1)}, u32[]{:S(2)}, u32[]{:S(2)}) collective-permute-start(bf16[512,256]{1,0:T(8,128)(2,1)} %so.1), channel_id=1, source_target_pairs={{0,16},{16,0},{1,17},{17,1},{2,18},{18,2},{3,19},{19,3},{4,20},{20... | collective-permute-start | bytes 786440 | tf_op jit(solution)/shard_map/ppermute | solution.py:478
  8.9 8.8 %collective-permute-start.5 = (s16[272,256]{1,0:T(8,128)(2,1)S(1)}, s16[272,256]{1,0:T(8,128)(2,1)S(1)}, u32[]{:S(2)}, u32[]{:S(2)}) collective-permute-start(s16[272,256]{1,0:T(8,128)(2,1)S(1)} %sent_terms.5), channel_id=1, source_target_pairs={{0,3},{1,2},{2,1},{3,0},{4,7},{5,6},{6,5},{7,4},{8,11},{9,10},{10,... | collective-permute-start | bytes 417800 | tf_op jit(solution)/shard_map/ppermute | solution.py:449
  13.7 6.8 %collective-permute-start.4 = (s16[272,256]{1,0:T(8,128)(2,1)S(1)}, s16[272,256]{1,0:T(8,128)(2,1)S(1)}, u32[]{:S(2)}, u32[]{:S(2)}) collective-permute-start(s16[272,256]{1,0:T(8,128)(2,1)S(1)} %sent_terms.4), channel_id=1, source_target_pairs={{0,2},{1,3},{2,0},{3,1},{4,6},{5,7},{6,4},{7,5},{8,10},{9,11},{10,... | collective-permute-start | bytes 417800 | tf_op jit(solution)/shard_map/ppermute | solution.py:449
  14.9 5.7 %collective-permute-start.3 = (s16[272,256]{1,0:T(8,128)(2,1)S(1)}, s16[272,256]{1,0:T(8,128)(2,1)S(1)}, u32[]{:S(2)}, u32[]{:S(2)}) collective-permute-start(s16[272,256]{1,0:T(8,128)(2,1)S(1)} %sent_terms.3), channel_id=1, source_target_pairs={{0,1},{1,0},{2,3},{3,2},{4,5},{5,4},{6,7},{7,6},{8,9},{9,8},{10,11... | collective-permute-start | bytes 417800 | tf_op jit(solution)/shard_map/ppermute | solution.py:449
  15.0 14.2 %copy-start = (bf16[64,256]{1,0:T(8,128)(2,1)S(1)}, bf16[64,256]{1,0:T(8,128)(2,1)}, u32[]{:S(2)}) copy-start(bf16[64,256]{1,0:T(8,128)(2,1)} %adj.3) | copy-start | bytes 98308
  15.0 14.3 %copy-start.3 = (s32[16,16,8]{1,2,0:T(8,128)S(1)}, s32[16,16,8]{1,2,0:T(8,128)}, u32[]{:S(2)}) copy-start(s32[16,16,8]{1,2,0:T(8,128)} %param.19) | copy-start | bytes 24580
  15.0 14.3 %copy-start.4 = (s32[16,16]{1,0:T(8,128)S(1)}, s32[16,16]{1,0:T(8,128)}, u32[]{:S(2)}) copy-start(s32[16,16]{1,0:T(8,128)} %counts.1) | copy-start | bytes 3076
  16.2 24.8 %copy-start.1 = (bf16[256,172]{0,1:T(8,128)(2,1)S(1)}, bf16[256,172]{0,1:T(8,128)(2,1)}, u32[]{:S(2)}) copy-start(bf16[256,172]{0,1:T(8,128)(2,1)} %param.22) | copy-start | bytes 264196
  16.3 24.8 %copy-start.2 = (bf16[256,172]{0,1:T(8,128)(2,1)S(1)}, bf16[256,172]{0,1:T(8,128)(2,1)}, u32[]{:S(2)}) copy-start(bf16[256,172]{0,1:T(8,128)(2,1)} %param.23) | copy-start | bytes 264196
  20.8 5.4 %collective-permute-start.6 = (s16[80,256]{1,0:T(8,128)(2,1)S(1)}, s16[80,256]{1,0:T(8,128)(2,1)S(1)}, u32[]{:S(2)}, u32[]{:S(2)}) collective-permute-start(s16[80,256]{1,0:T(8,128)(2,1)S(1)} %get-tuple-element.30), channel_id=1, source_target_pairs={{0,8},{1,9},{2,10},{3,11},{4,12},{5,13},{6,14},{7,15},{8,0},{9,1},... | collective-permute-start | bytes 122888 | tf_op jit(solution)/shard_map/ppermute | solution.py:449
  22.8 5.8 %collective-permute-start.7 = (s16[80,256]{1,0:T(8,128)(2,1)S(1)}, s16[80,256]{1,0:T(8,128)(2,1)S(1)}, u32[]{:S(2)}, u32[]{:S(2)}) collective-permute-start(s16[80,256]{1,0:T(8,128)(2,1)S(1)} %get-tuple-element.31), channel_id=1, source_target_pairs={{0,12},{1,13},{2,14},{3,15},{4,8},{5,9},{6,10},{7,11},{8,4},{9,5},... | collective-permute-start | bytes 122888 | tf_op jit(solution)/shard_map/ppermute | solution.py:449
  25.1 4.0 %collective-permute-start.8 = (s16[80,256]{1,0:T(8,128)(2,1)S(1)}, s16[80,256]{1,0:T(8,128)(2,1)S(1)}, u32[]{:S(2)}, u32[]{:S(2)}) collective-permute-start(s16[80,256]{1,0:T(8,128)(2,1)S(1)} %get-tuple-element.32), channel_id=1, source_target_pairs={{0,4},{1,5},{2,6},{3,7},{4,0},{5,1},{6,2},{7,3},{8,12},{9,13},{10,... | collective-permute-start | bytes 122888 | tf_op jit(solution)/shard_map/ppermute | solution.py:449
  29.1 1.3 %collective-permute-start.9 = (bf16[64,256]{1,0:T(8,128)(2,1)S(1)}, bf16[64,256]{1,0:T(8,128)(2,1)S(1)}, u32[]{:S(2)}, u32[]{:S(2)}) collective-permute-start(bf16[64,256]{1,0:T(8,128)(2,1)S(1)} %hidden_rows.1.own), channel_id=1, source_target_pairs={{0,16},{16,0},{1,17},{17,1},{2,18},{18,2},{3,19},{19,3},{4,20},{20... | collective-permute-start | bytes 98312 | tf_op jit(solution)/shard_map/ppermute | solution.py:500

commit v15 on v14

--- a/solution.py
+++ b/solution.py
@@ -20,13 +20,7 @@
 
 
 def group_order(n):
-    first = n * 9 // 16
-    return [first] + [i for i in range(n) if i != first]
-
-
-def ordered(block, n):
-    first = n * 9 // 16
-    return jnp.where(block == 0, first, jnp.where(block <= first, block - 1, block))
+    return list(range(n - 1, -1, -1))
 
 
 LN2 = 0.6931471805599453
@@ -163,7 +157,7 @@
     ])
 
 
-def select_kernel(groups, ids, lists, counts, adj, sel, adj_out):
+def select_kernel(groups, ids, lists, counts, adj, sel, front, adj_out):
     core, me = ids[0], ids[1]
     n = lists.shape[0]
     slots = lists.shape[1]
@@ -176,7 +170,7 @@
     k_n = jnp.bitwise_and(q_n, slots - 1)
     for k in range(slots):
         picked = jnp.where(k_n == k, mine[k:k + 1, :], picked)
-    good = jnp.logical_and(ordered(lax.div(q_n, slots), n) == r_n, k_n < cnt)
+    good = jnp.logical_and(n - 1 - lax.div(q_n, slots) == r_n, k_n < cnt)
     row = jnp.sum(jnp.where(good, picked + 1.0, 0.0), axis=1, keepdims=True) - 1.0
     lane = lax.broadcasted_iota(jnp.int32, (1, sel.shape[1]), 1)
     name = jnp.zeros(lane.shape, jnp.int32)
@@ -184,8 +178,12 @@
     for i, g in enumerate(names):
         name = jnp.where(lax.div(lane, UNIT) == i, g * UNIT + jnp.bitwise_and(lane, UNIT - 1), name)
     sel[...] = jnp.where(row == name.astype(jnp.float32), 1.0, 0.0).astype(jnp.bfloat16)
+    tile, out_rows = groups * UNIT, adj.shape[0]
+    placed = jnp.where(lax.broadcasted_iota(jnp.int32, (tile, tile), 0) == name, 1.0, 0.0).astype(jnp.bfloat16)
+    front[:out_rows, :] = jnp.dot(adj[:, :tile], placed, preferred_element_type=jnp.float32).astype(jnp.bfloat16)
+    front[out_rows:, :] = placed[:out_rows, :]
     column = lax.broadcasted_iota(jnp.int32, (1, total), 1)
-    source = ordered(lax.div(column, slots), n) * slots + lax.rem(column, slots)
+    source = (n - 1 - lax.div(column, slots)) * slots + lax.rem(column, slots)
     moved = jnp.where(lax.broadcasted_iota(jnp.int32, (total, total), 0) == source, 1.0, 0.0).astype(jnp.bfloat16)
     adj_out[...] = jnp.dot(adj[:, groups * UNIT:], moved, preferred_element_type=jnp.float32).astype(jnp.bfloat16)
 
@@ -198,10 +196,11 @@
         functools.partial(select_kernel, groups),
         out_shape=[
             jax.ShapeDtypeStruct((n * slots, groups * UNIT), jnp.bfloat16),
+            jax.ShapeDtypeStruct((2 * adj.shape[0], groups * UNIT), jnp.bfloat16),
             jax.ShapeDtypeStruct((adj.shape[0], n * slots), jnp.bfloat16),
         ],
         in_specs=[smem, vmem, vmem, vmem],
-        out_specs=[vmem] * 2,
+        out_specs=[vmem] * 3,
         compiler_params=pltpu.CompilerParams(vmem_limit_bytes=32 * 1024 * 1024),
         name="selection",
     )(ids, jnp.swapaxes(send_list, 1, 2), send_count, adj)
@@ -311,31 +310,37 @@
     )(wo, wp, *accs)
 
 
-def own_kernel(chunk, per, groups, parts, ids, wo, wp, xo, xp, so, sp, *refs):
-    accs, out = refs[:parts], refs[parts]
+def own_kernel(chunk, per, groups, parts, ids, wo, wp, xo, so, *refs):
+    accs, (out, theirs, terms) = refs[:parts], refs[parts:]
     weigh(accs, (wo, wp), 0, out.shape[0], out)
+    terms[...] = jnp.dot(xo[:groups * UNIT, :], so[...], preferred_element_type=jnp.float32)
     for j in range(per):
+        here = slice(j * UNIT, (j + 1) * UNIT)
         at = pl.multiple_of(group_of(ids[0], chunk * per + j, groups) * UNIT, UNIT)
-        self = jnp.dot(xo[pl.ds(at, UNIT), :], so[...], preferred_element_type=jnp.float32)
-        self = self + jnp.dot(xp[pl.ds(at, UNIT), :], sp[...], preferred_element_type=jnp.float32)
-        out[j * UNIT:(j + 1) * UNIT, :] += self
-
-
-def own_terms(chunk, per, groups, slots, ids, accs, wo, wp, xo, xp, so, sp):
+        out[here, :] += terms[pl.ds(at, UNIT), :]
+        at = pl.multiple_of(group_of(1 - ids[0], chunk * per + j, groups) * UNIT, UNIT)
+        theirs[here, :] = terms[pl.ds(at, UNIT), :]
+
+
+def own_terms(chunk, per, groups, slots, ids, accs, wo, wp, xo, so):
     hidden = wo.shape[1]
     rows = per * UNIT
     smem = pl.BlockSpec(memory_space=pltpu.SMEM)
     vmem = pl.BlockSpec(memory_space=pltpu.VMEM)
     return pl.pallas_call(
         functools.partial(own_kernel, chunk, per, groups, len(accs)),
-        out_shape=jax.ShapeDtypeStruct((slots * rows, hidden), jnp.float32),
-        in_specs=[smem] + [vmem] * (6 + len(accs)),
-        out_specs=vmem,
+        out_shape=[
+            jax.ShapeDtypeStruct((slots * rows, hidden), jnp.float32),
+            jax.ShapeDtypeStruct((rows, hidden), jnp.float32),
+        ],
+        in_specs=[smem] + [vmem] * (4 + len(accs)),
+        out_specs=[vmem] * 2,
+        scratch_shapes=[pltpu.VMEM((groups * UNIT, hidden), jnp.float32)],
         compiler_params=pltpu.CompilerParams(vmem_limit_bytes=(12 << 20) + accs[0].size * 4 * len(accs)),
         cost_estimate=pl.CostEstimate(
             flops=4 * slots * rows * PART * len(accs) * hidden, bytes_accessed=2 << 20, transcendentals=0),
         name="own_terms",
-    )(ids, wo, wp, xo, xp, so, sp, *accs)
+    )(ids, wo, wp, xo, so, *accs)
 
 
 def combine_kernel(slots, rows, ways, own, *refs):
@@ -372,16 +377,16 @@
 
 
 def hidden_kernel(chunks, parts, rows, *refs):
-    out = refs[chunks * parts]
+    out = refs[chunks * parts + 1]
     for c in range(chunks):
-        own, coded = refs[c * parts], refs[c * parts + 1:(c + 1) * parts]
-        total = own[:rows, :]
+        own, self, coded = refs[c * parts], refs[c * parts + 1], refs[c * parts + 2:(c + 1) * parts]
+        total = own[:rows, :] + self[...]
         for a in coded:
             total = total + read_coded(a, 1, rows)(0)
         out[c * rows:(c + 1) * rows, :] = jnp.maximum(total, 0.0).astype(jnp.bfloat16)
 
 
-def hidden_rows(chunk_parts, rows):
+def hidden_rows(chunk_parts, rows, sel):
     chunks, parts = len(chunk_parts), len(chunk_parts[0])
     width = chunk_parts[0][0].shape[1]
     vmem = pl.BlockSpec(memory_space=pltpu.VMEM)
@@ -389,11 +394,11 @@
     return pl.pallas_call(
         functools.partial(hidden_kernel, chunks, parts, rows),
         out_shape=jax.ShapeDtypeStruct((chunks * rows, width), jnp.bfloat16),
-        in_specs=[vmem] * len(flat),
+        in_specs=[vmem] * (len(flat) + 1),
         out_specs=vmem,
         compiler_params=pltpu.CompilerParams(vmem_limit_bytes=32 * 1024 * 1024),
         name="hidden_rows",
-    )(*flat)
+    )(*flat, sel)
 
 
 def send_kernel(own, other, sel, send):
@@ -413,34 +418,27 @@
     )(own, other, sel)
 
 
-def logits_kernel(groups, ids, own, other, received, adj, adj_received, w_self, w_neigh, out, hidden):
-    core = ids[0]
-    for i in range(groups // 2):
-        mine = group_of(core, i, groups)
-        theirs = group_of(1 - core, i, groups)
-        hidden[pl.ds(pl.multiple_of(mine * UNIT, UNIT), UNIT), :] = own[i * UNIT:(i + 1) * UNIT, :]
-        hidden[pl.ds(pl.multiple_of(theirs * UNIT, UNIT), UNIT), :] = other[i * UNIT:(i + 1) * UNIT, :]
-    tile, rows = hidden.shape[0], adj.shape[0]
-    mean = jnp.dot(adj_received[...], received[...], preferred_element_type=jnp.float32)
-    mean = mean + jnp.dot(adj[:, :tile], hidden[...], preferred_element_type=jnp.float32)
+def logits_kernel(own, other, received, front, adj_received, w_self, w_neigh, out):
+    rows = out.shape[0]
+    both = jnp.concatenate([own[...], other[...]], axis=0)
+    local = jnp.dot(front[...], both, preferred_element_type=jnp.float32)
+    mean = local[:rows, :] + jnp.dot(adj_received[...], received[...], preferred_element_type=jnp.float32)
     dims = (((1,), (1,)), ((), ()))
-    got = lax.dot_general(hidden[:rows, :], w_self[...], dims, preferred_element_type=jnp.float32)
+    got = lax.dot_general(local[rows:, :].astype(jnp.bfloat16), w_self[...], dims, preferred_element_type=jnp.float32)
     got = got + lax.dot_general(mean.astype(jnp.bfloat16), w_neigh[...], dims, preferred_element_type=jnp.float32)
     out[...] = got
 
 
-def logits_of(groups, ids, own, other, received, adj, adj_received, w_self, w_neigh):
-    smem = pl.BlockSpec(memory_space=pltpu.SMEM)
-    vmem = pl.BlockSpec(memory_space=pltpu.VMEM)
-    return pl.pallas_call(
-        functools.partial(logits_kernel, groups),
-        out_shape=jax.ShapeDtypeStruct((adj.shape[0], w_self.shape[1]), jnp.float32),
-        in_specs=[smem] + [vmem] * 7,
+def logits_of(own, other, received, front, adj_received, w_self, w_neigh):
+    vmem = pl.BlockSpec(memory_space=pltpu.VMEM)
+    return pl.pallas_call(
+        logits_kernel,
+        out_shape=jax.ShapeDtypeStruct((adj_received.shape[0], w_self.shape[1]), jnp.float32),
+        in_specs=[vmem] * 7,
         out_specs=vmem,
-        scratch_shapes=[pltpu.VMEM((groups * UNIT, own.shape[1]), jnp.bfloat16)],
         compiler_params=pltpu.CompilerParams(vmem_limit_bytes=32 * 1024 * 1024),
         name="logits",
-    )(ids, own, other, received, adj, adj_received, w_self.T, w_neigh.T)
+    )(own, other, received, front, adj_received, w_self.T, w_neigh.T)
 
 
 def exchange(parts, stride, n, places):
@@ -475,7 +473,6 @@
     swap = [(0, 1), (1, 0)]
     xp = lax.ppermute(features, "feat", swap)
     wp = lax.ppermute(neighbour_weight_first, "feat", swap)
-    sp = lax.ppermute(w_self1, "feat", swap)
     tw = tile_weight.reshape(tile_weight.shape[0], groups, UNIT, tile)
     planned = plan(
         CHUNKS, per, n, 4, ids, tile_src, tile_rows, tile_dst, tw, features, neighbour_weight_first, w_self1,
@@ -486,7 +483,8 @@
         accs = gathered_sums(per, n, tables[chunk], tbufs[chunk], xo, xp)
         slots, rows = n // 4, per * UNIT
         parts = {k: sent_terms(k, slots, rows, accs, wo, wp) for k in (1, 2, 3)}
-        parts[0] = own_terms(chunk, per, groups, slots, ids, accs, wo, wp, xo, xp, so, sp)
+        parts[0], theirs = own_terms(chunk, per, groups, slots, ids, accs, wo, wp, xo, so)
+        self = lax.ppermute(theirs, "feat", swap)
         got = exchange(parts, 1, n, (1, 2, 3))
         stride = 4
         for radix in radices[1:]:
@@ -494,13 +492,13 @@
             parts = combine(n // stride, per * UNIT, ways, got[0], got[1:])
             got = exchange(parts, stride, n, (2, 3, 1) if ways == 4 else (1,))
             stride *= ways
-        done.append(got)
-    sel, adj_received = selection(groups, ids, send_list, send_count, adj_two)
-    own = hidden_rows(done, per * UNIT)
+        done.append([got[0], self] + got[1:])
+    sel, front, adj_received = selection(groups, ids, send_list, send_count, adj_two)
+    own = hidden_rows(done, per * UNIT, sel)
     other = lax.ppermute(own, "feat", swap)
     send = rows_to_send(own, other, sel)
     received = lax.all_to_all(send, "dom", 0, 0, axis_index_groups=[group_order(n)], tiled=True)
-    return logits_of(groups, ids, own, other, received, adj_two, adj_received, w_self2, w_neigh2)
+    return logits_of(own, other, received, front, adj_received, w_self2, w_neigh2)
 
 
 def solution(mesh):

time: 42.7 us -> 41.3 us (0.967)
  blocking collectives: 10.5 us -> 9.8 us
  Pallas kernels: 12.6 us -> 12 us
    ppermute x6, waiting for transfers between devices: 8.3 us -> 7.55 us  [exchange(): lax.ppermute(parts[k], 'dom', [(i, i ^ k * stride) for i in range(n)])]
    all_to_all x1, blocking collectives: 10.5 us -> 9.8 us  [body(): lax.all_to_all(send, 'dom', 0, 0, axis_index_groups=[group_order(n)], til...]
    ppermute x1, waiting for transfers between devices: 0.48 us -> 1.19 us  [body(): other = lax.ppermute(own, 'feat', swap)]
    pallas_call x1, Pallas kernels: 1.46 us -> 0.98 us  [logits_of(): pl.pallas_call(logits_kernel, out_shape=jax.ShapeDtypeStruct((adj_receive...]
  transfers between devices with their start and end apart: 10 -> 10, of which waited for: 6 -> 7; matrix products, arithmetic and copies ran while one was open for 0% -> 0% of each run, Pallas kernels for 25% -> 25%
where the time goes in v15:
time: 41.3 us; the launch traced here: 41.2 us
  Pallas kernels  12 us (29%)
  starting transfers between devices  10.4 us (25%)
  blocking collectives  9.8 us (24%)
  waiting for transfers between devices  8.75 us (21%)
    all_to_all x1, blocking collectives, body(): lax.all_to_all(send, 'dom', 0, 0, axis_index_groups=[group_order(n)], til...  9.8 us
    ppermute x6, starting transfers between devices, exchange(): lax.ppermute(parts[k], 'dom', [(i, i ^ k * stride) for i in range(n)])  9.7 us
    ppermute x6, waiting for transfers between devices, exchange(): lax.ppermute(parts[k], 'dom', [(i, i ^ k * stride) for i in range(n)])  7.55 us
    pallas_call x1, Pallas kernels, gathered_sums(): pl.pallas_call(tiles_kernel, out_shape=[sums] * parts, in_specs=[vmem] *...  4.67 us
    pallas_call x1, Pallas kernels, plan(): pl.pallas_call(functools.partial(plan_kernel, chunks, per, n, radix, n_sr...  2.68 us
    pallas_call x3, Pallas kernels, sent_terms(): pl.pallas_call(functools.partial(sent_kernel, k, slots, rows, len(accs)),...  1.58 us
    ppermute x1, waiting for transfers between devices, body(): other = lax.ppermute(own, 'feat', swap)  1.19 us
    pallas_call x1, Pallas kernels, own_terms(): pl.pallas_call(functools.partial(own_kernel, chunk, per, groups, len(accs...  1.05 us
  transfers between devices with their start and end apart: 10, of which 7 were waited for; matrix products, arithmetic and copies ran while one was open for 0% of the time, Pallas kernels for 25%

profile of v15, /device:TPU:0, one launch (start us, length us, event | category | flops | bytes accessed | tf_op | source)
XLA Modules:
  0.0 41.2 jit_solution(3690908022670922759)
XLA Ops:
  0.0 0.5 %collective-permute-start.1 = (bf16[1024,512]{1,0:T(8,128)(2,1)}, bf16[1024,512]{1,0:T(8,128)(2,1)S(1)}, u32[]{:S(2)}, u32[]{:S(2)}) collective-permute-start(bf16[1024,512]{1,0:T(8,128)(2,1)} %xo.1), channel_id=1, source_target_pairs={{0,16},{16,0},{1,17},{17,1},{2,18},{18,2},{3,19},{19,3},{4,20},{20... | collective-permute-start | bytes 3145736 | tf_op jit(solution)/shard_map/ppermute | solution.py:474
  0.5 0.1 collective-permute-start
  0.5 0.1 pad_add_fusion.ids
  0.6 2.7 %plan.1 = (s32[2,640]{1,0:T(2,128)S(1)}, bf16[512,16,128]{2,1,0:T(8,128)(2,1)S(1)}, bf16[1024,512]{1,0:T(8,128)(2,1)S(1)}, bf16[512,256]{1,0:T(8,128)(2,1)S(1)}, bf16[512,256]{1,0:T(8,128)(2,1)S(1)}) custom-call(s32[2]{0:T(128)S(1)} %pad_add_fusion.ids, s32[1,128]{1,0:T(1,128)} %bitcast.17, s32[1,128]{1,0:T(1,128)} %bitcast.18, s32[1,128]{1,0:T(1,128)} %bitcast.19, ...), custom_call_target="tpu_custom_call" | custom-call | tf_op jit(solution)/shard_map/plan/pallas_call | solution.py:135
  3.3 0.0 collective-permute-done.1.xp
  3.3 4.7 %gathered_sums.1 = (f32[1040,256]{1,0:T(8,128)S(1)}, f32[1040,256]{1,0:T(8,128)S(1)}, f32[1040,256]{1,0:T(8,128)S(1)}, f32[1040,256]{1,0:T(8,128)S(1)}) custom-call(s32[2,640]{1,0:T(2,128)S(1)} %get-tuple-element.26.table_v, bf16[512,16,128]{2,1,0:T(8,128)(2,1)S(1)} %get-tuple-element.27.tbuf, bf16[1024,512]{1,0:T(8,128)(2,1)S(1)} %get-tuple-element.24.xo, ...), custom_call_target="tpu_custom_call" | custom-call | flops 2147483648 | bytes 8388608 | tf_op jit(solution)/shard_map/gathered_sums/pallas_call | solution.py:253
  8.0 0.0 collective-permute-done.wp
  8.0 0.5 %sent_terms.5 = s16[272,256]{1,0:T(8,128)(2,1)S(1)} custom-call(bf16[512,256]{1,0:T(8,128)(2,1)S(1)} %get-tuple-element.23.wo, bf16[512,256]{1,0:T(8,128)(2,1)S(1)} %collective-permute-done.wp, f32[1040,256]{1,0:T(8,128)S(1)} %get-tuple-element.28.refs_0_, f32[1040,256]{1,0:T(8,128)S(1)} %get-tuple-element.29.refs_1_, ...), custom_call_target="tpu_custom_call" | custom-call | flops 268435456 | bytes 2097152 | tf_op jit(solution)/shard_map/sent_terms/pallas_call | solution.py:297
  8.5 3.9 %collective-permute-start.4 = (s16[272,256]{1,0:T(8,128)(2,1)S(1)}, s16[272,256]{1,0:T(8,128)(2,1)S(1)}, u32[]{:S(2)}, u32[]{:S(2)}) collective-permute-start(s16[272,256]{1,0:T(8,128)(2,1)S(1)} %sent_terms.5), channel_id=1, source_target_pairs={{0,3},{1,2},{2,1},{3,0},{4,7},{5,6},{6,5},{7,4},{8,11},{9,10},{10,... | collective-permute-start | bytes 417800 | tf_op jit(solution)/shard_map/ppermute | solution.py:447
  12.4 0.5 %sent_terms.4 = s16[272,256]{1,0:T(8,128)(2,1)S(1)} custom-call(bf16[512,256]{1,0:T(8,128)(2,1)S(1)} %get-tuple-element.23.wo, bf16[512,256]{1,0:T(8,128)(2,1)S(1)} %collective-permute-done.wp, f32[1040,256]{1,0:T(8,128)S(1)} %get-tuple-element.28.refs_0_, f32[1040,256]{1,0:T(8,128)S(1)} %get-tuple-element.29.refs_1_, ...), custom_call_target="tpu_custom_call" | custom-call | flops 268435456 | bytes 2097152 | tf_op jit(solution)/shard_map/sent_terms/pallas_call | solution.py:297
  12.9 1.5 %collective-permute-start.3 = (s16[272,256]{1,0:T(8,128)(2,1)S(1)}, s16[272,256]{1,0:T(8,128)(2,1)S(1)}, u32[]{:S(2)}, u32[]{:S(2)}) collective-permute-start(s16[272,256]{1,0:T(8,128)(2,1)S(1)} %sent_terms.4), channel_id=1, source_target_pairs={{0,2},{1,3},{2,0},{3,1},{4,6},{5,7},{6,4},{7,5},{8,10},{9,11},{10,... | collective-permute-start | bytes 417800 | tf_op jit(solution)/shard_map/ppermute | solution.py:447
  14.4 0.5 %sent_terms.3 = s16[272,256]{1,0:T(8,128)(2,1)S(1)} custom-call(bf16[512,256]{1,0:T(8,128)(2,1)S(1)} %get-tuple-element.23.wo, bf16[512,256]{1,0:T(8,128)(2,1)S(1)} %collective-permute-done.wp, f32[1040,256]{1,0:T(8,128)S(1)} %get-tuple-element.28.refs_0_, f32[1040,256]{1,0:T(8,128)S(1)} %get-tuple-element.29.refs_1_, ...), custom_call_target="tpu_custom_call" | custom-call | flops 268435456 | bytes 2097152 | tf_op jit(solution)/shard_map/sent_terms/pallas_call | solution.py:297
  15.0 0.1 collective-permute-start.2
  15.0 0.0 copy-start.2
  15.0 0.0 copy-start.3
  15.1 0.0 copy-start.4
  15.1 1.0 %own_terms.1 = (f32[256,256]{1,0:T(8,128)S(1)}, f32[64,256]{1,0:T(8,128)S(1)}) custom-call(s32[2]{0:T(128)S(1)} %pad_add_fusion.ids, bf16[512,256]{1,0:T(8,128)(2,1)S(1)} %get-tuple-element.23.wo, bf16[512,256]{1,0:T(8,128)(2,1)S(1)} %collective-permute-done.wp, bf16[1024,512]{1,0:T(8,128)(2,1)S(1)} %get-tuple-element.24.xo, ...), custom_call_target="tpu_custom_call" | custom-call | flops 268435456 | bytes 2097152 | tf_op jit(solution)/shard_map/own_terms/pallas_call | solution.py:330
  16.1 0.0 copy-start
  16.1 0.0 copy-start.1
  16.2 0.1 collective-permute-start.5
  16.2 0.2 collective-permute-done.4.refs_2_
  16.5 2.9 %collective-permute-done.3.refs_1_ = s16[272,256]{1,0:T(8,128)(2,1)S(1)} collective-permute-done((s16[272,256]{1,0:T(8,128)(2,1)S(1)}, s16[272,256]{1,0:T(8,128)(2,1)S(1)}, u32[]{:S(2)}, u32[]{:S(2)}) %collective-permute-start.3) | collective-permute-done | bytes 139296 | tf_op jit(solution)/shard_map/ppermute | solution.py:447
  19.4 0.7 %collective-permute-done.2.refs_0_ = s16[272,256]{1,0:T(8,128)(2,1)S(1)} collective-permute-done((s16[272,256]{1,0:T(8,128)(2,1)S(1)}, s16[272,256]{1,0:T(8,128)(2,1)S(1)}, u32[]{:S(2)}, u32[]{:S(2)}) %collective-permute-start.2) | collective-permute-done | bytes 139296 | tf_op jit(solution)/shard_map/ppermute | solution.py:447
  20.1 0.2 combine.1
  20.3 2.7 %collective-permute-start.6 = (s16[80,256]{1,0:T(8,128)(2,1)S(1)}, s16[80,256]{1,0:T(8,128)(2,1)S(1)}, u32[]{:S(2)}, u32[]{:S(2)}) collective-permute-start(s16[80,256]{1,0:T(8,128)(2,1)S(1)} %get-tuple-element.35), channel_id=1, source_target_pairs={{0,8},{1,9},{2,10},{3,11},{4,12},{5,13},{6,14},{7,15},{8,0},{9,1},... | collective-permute-start | bytes 122888 | tf_op jit(solution)/shard_map/ppermute | solution.py:447
  22.9 1.6 %collective-permute-start.7 = (s16[80,256]{1,0:T(8,128)(2,1)S(1)}, s16[80,256]{1,0:T(8,128)(2,1)S(1)}, u32[]{:S(2)}, u32[]{:S(2)}) collective-permute-start(s16[80,256]{1,0:T(8,128)(2,1)S(1)} %get-tuple-element.36), channel_id=1, source_target_pairs={{0,12},{1,13},{2,14},{3,15},{4,8},{5,9},{6,10},{7,11},{8,4},{9,5},... | collective-permute-start | bytes 122888 | tf_op jit(solution)/shard_map/ppermute | solution.py:447
  24.5 0.0 collective-permute-start.8
  24.5 0.0 copy-done.2
  24.5 0.0 copy-done.3
  24.5 0.0 copy-done.4
  24.5 0.7 %selection.1 = (bf16[128,128]{1,0:T(8,128)(2,1)S(1)}, bf16[128,128]{1,0:T(8,128)(2,1)S(1)}, bf16[64,128]{1,0:T(8,128)(2,1)S(1)}) custom-call(s32[2]{0:T(128)S(1)} %pad_add_fusion.ids, s32[16,8,16]{2,1,0:T(8,128)S(1)} %bitcast.15, s32[16,16]{1,0:T(8,128)S(1)} %copy-done.4, bf16[64,256]{1,0:T(8,128)(2,1)S(1)} %copy-done.3), custom_call_target="tpu_custom_call" | custom-call | tf_op jit(solution)/shard_map/selection/pallas_call | solution.py:195
  25.2 0.0 collective-permute-done.5.refs_1_
  25.2 0.5 %collective-permute-done.6.refs_2_ = s16[80,256]{1,0:T(8,128)(2,1)S(1)} collective-permute-done((s16[80,256]{1,0:T(8,128)(2,1)S(1)}, s16[80,256]{1,0:T(8,128)(2,1)S(1)}, u32[]{:S(2)}, u32[]{:S(2)}) %collective-permute-start.6) | collective-permute-done | bytes 40992 | tf_op jit(solution)/shard_map/ppermute | solution.py:447
  25.8 3.1 %collective-permute-done.7.refs_3_ = s16[80,256]{1,0:T(8,128)(2,1)S(1)} collective-permute-done((s16[80,256]{1,0:T(8,128)(2,1)S(1)}, s16[80,256]{1,0:T(8,128)(2,1)S(1)}, u32[]{:S(2)}, u32[]{:S(2)}) %collective-permute-start.7) | collective-permute-done | bytes 40992 | tf_op jit(solution)/shard_map/ppermute | solution.py:447
  28.8 0.1 collective-permute-done.8.refs_4_
  29.0 0.1 collective-permute-start.9
  29.1 1.2 %collective-permute-done.9.other = bf16[64,256]{1,0:T(8,128)(2,1)S(1)} collective-permute-done((bf16[64,256]{1,0:T(8,128)(2,1)S(1)}, bf16[64,256]{1,0:T(8,128)(2,1)S(1)}, u32[]{:S(2)}, u32[]{:S(2)}) %collective-permute-start.9) | collective-permute-done | bytes 32800 | tf_op jit(solution)/shard_map/ppermute | solution.py:498
  30.3 0.1 rows_to_send.1
  30.4 9.8 %all_to_all.11 = bf16[16,8,256]{2,1,0:T(8,128)(2,1)S(1)} all-to-all(bf16[16,8,256]{2,1,0:T(8,128)(2,1)S(1)} %bitcast.11), channel_id=1, replica_groups={{15,14,13,12,11,10,9,8,7,6,5,4,3,2,1,0},{31,30,29,28,27,26,25,24,23,22,..., dimensions={0} | all-to-all | bytes 131072 | tf_op jit(solution)/shard_map/all_to_all | solution.py:500
  40.2 0.0 copy-done
  40.2 0.0 copy-done.1
  40.2 1.0 %logits.1 = f32[64,172]{1,0:T(8,128)} custom-call(bf16[64,256]{1,0:T(8,128)(2,1)S(1)} %hidden_rows.1.own, bf16[64,256]{1,0:T(8,128)(2,1)S(1)} %collective-permute-done.9.other, bf16[128,256]{1,0:T(8,128)(2,1)S(1)} %bitcast.12, bf16[128,128]{1,0:T(8,128)(2,1)S(1)} %get-tuple-element.39.front, bf16[64,128]{1,0:T(8,128)(2,1)S(1)} %get-tuple-element.40.adj_received, ...), custom_call_target="tpu_custom_call" | custom-call | tf_op jit(solution)/shard_map/logits/pallas_call | solution.py:434
  (1 shorter events, 0.0 us)
Async XLA Ops:
  0.0 3.3 %collective-permute-start.1 = (bf16[1024,512]{1,0:T(8,128)(2,1)}, bf16[1024,512]{1,0:T(8,128)(2,1)S(1)}, u32[]{:S(2)}, u32[]{:S(2)}) collective-permute-start(bf16[1024,512]{1,0:T(8,128)(2,1)} %xo.1), channel_id=1, source_target_pairs={{0,16},{16,0},{1,17},{17,1},{2,18},{18,2},{3,19},{19,3},{4,20},{20... | collective-permute-start | bytes 3145736 | tf_op jit(solution)/shard_map/ppermute | solution.py:474
  0.5 7.5 %collective-permute-start = (bf16[512,256]{1,0:T(8,128)(2,1)}, bf16[512,256]{1,0:T(8,128)(2,1)S(1)}, u32[]{:S(2)}, u32[]{:S(2)}) collective-permute-start(bf16[512,256]{1,0:T(8,128)(2,1)} %wo.1), channel_id=1, source_target_pairs={{0,16},{16,0},{1,17},{17,1},{2,18},{18,2},{3,19},{19,3},{4,20},{20... | collective-permute-start | bytes 786440 | tf_op jit(solution)/shard_map/ppermute | solution.py:475
  8.5 8.0 %collective-permute-start.4 = (s16[272,256]{1,0:T(8,128)(2,1)S(1)}, s16[272,256]{1,0:T(8,128)(2,1)S(1)}, u32[]{:S(2)}, u32[]{:S(2)}) collective-permute-start(s16[272,256]{1,0:T(8,128)(2,1)S(1)} %sent_terms.5), channel_id=1, source_target_pairs={{0,3},{1,2},{2,1},{3,0},{4,7},{5,6},{6,5},{7,4},{8,11},{9,10},{10,... | collective-permute-start | bytes 417800 | tf_op jit(solution)/shard_map/ppermute | solution.py:447
  12.9 6.4 %collective-permute-start.3 = (s16[272,256]{1,0:T(8,128)(2,1)S(1)}, s16[272,256]{1,0:T(8,128)(2,1)S(1)}, u32[]{:S(2)}, u32[]{:S(2)}) collective-permute-start(s16[272,256]{1,0:T(8,128)(2,1)S(1)} %sent_terms.4), channel_id=1, source_target_pairs={{0,2},{1,3},{2,0},{3,1},{4,6},{5,7},{6,4},{7,5},{8,10},{9,11},{10,... | collective-permute-start | bytes 417800 | tf_op jit(solution)/shard_map/ppermute | solution.py:447
  15.0 5.1 %collective-permute-start.2 = (s16[272,256]{1,0:T(8,128)(2,1)S(1)}, s16[272,256]{1,0:T(8,128)(2,1)S(1)}, u32[]{:S(2)}, u32[]{:S(2)}) collective-permute-start(s16[272,256]{1,0:T(8,128)(2,1)S(1)} %sent_terms.3), channel_id=1, source_target_pairs={{0,1},{1,0},{2,3},{3,2},{4,5},{5,4},{6,7},{7,6},{8,9},{9,8},{10,11... | collective-permute-start | bytes 417800 | tf_op jit(solution)/shard_map/ppermute | solution.py:447
  15.0 9.5 %copy-start.2 = (s32[16,16,8]{1,2,0:T(8,128)S(1)}, s32[16,16,8]{1,2,0:T(8,128)}, u32[]{:S(2)}) copy-start(s32[16,16,8]{1,2,0:T(8,128)} %param.19) | copy-start | bytes 24580
  15.0 9.5 %copy-start.3 = (bf16[64,256]{1,0:T(8,128)(2,1)S(1)}, bf16[64,256]{1,0:T(8,128)(2,1)}, u32[]{:S(2)}) copy-start(bf16[64,256]{1,0:T(8,128)(2,1)} %adj.1) | copy-start | bytes 98308
  15.1 9.5 %copy-start.4 = (s32[16,16]{1,0:T(8,128)S(1)}, s32[16,16]{1,0:T(8,128)}, u32[]{:S(2)}) copy-start(s32[16,16]{1,0:T(8,128)} %counts.1) | copy-start | bytes 3076
  16.1 24.1 %copy-start = (bf16[256,172]{0,1:T(8,128)(2,1)S(1)}, bf16[256,172]{0,1:T(8,128)(2,1)}, u32[]{:S(2)}) copy-start(bf16[256,172]{0,1:T(8,128)(2,1)} %param.22) | copy-start | bytes 264196
  16.1 24.1 %copy-start.1 = (bf16[256,172]{0,1:T(8,128)(2,1)S(1)}, bf16[256,172]{0,1:T(8,128)(2,1)}, u32[]{:S(2)}) copy-start(bf16[256,172]{0,1:T(8,128)(2,1)} %param.23) | copy-start | bytes 264196
  16.2 9.1 %collective-permute-start.5 = (f32[64,256]{1,0:T(8,128)S(1)}, f32[64,256]{1,0:T(8,128)S(1)}, u32[]{:S(2)}, u32[]{:S(2)}) collective-permute-start(f32[64,256]{1,0:T(8,128)S(1)} %get-tuple-element.34), channel_id=1, source_target_pairs={{0,16},{16,0},{1,17},{17,1},{2,18},{18,2},{3,19},{19,3},{4,20},{20... | collective-permute-start | bytes 196616 | tf_op jit(solution)/shard_map/ppermute | solution.py:487
  20.3 5.5 %collective-permute-start.6 = (s16[80,256]{1,0:T(8,128)(2,1)S(1)}, s16[80,256]{1,0:T(8,128)(2,1)S(1)}, u32[]{:S(2)}, u32[]{:S(2)}) collective-permute-start(s16[80,256]{1,0:T(8,128)(2,1)S(1)} %get-tuple-element.35), channel_id=1, source_target_pairs={{0,8},{1,9},{2,10},{3,11},{4,12},{5,13},{6,14},{7,15},{8,0},{9,1},... | collective-permute-start | bytes 122888 | tf_op jit(solution)/shard_map/ppermute | solution.py:447
  22.9 5.9 %collective-permute-start.7 = (s16[80,256]{1,0:T(8,128)(2,1)S(1)}, s16[80,256]{1,0:T(8,128)(2,1)S(1)}, u32[]{:S(2)}, u32[]{:S(2)}) collective-permute-start(s16[80,256]{1,0:T(8,128)(2,1)S(1)} %get-tuple-element.36), channel_id=1, source_target_pairs={{0,12},{1,13},{2,14},{3,15},{4,8},{5,9},{6,10},{7,11},{8,4},{9,5},... | collective-permute-start | bytes 122888 | tf_op jit(solution)/shard_map/ppermute | solution.py:447
  24.5 4.4 %collective-permute-start.8 = (s16[80,256]{1,0:T(8,128)(2,1)S(1)}, s16[80,256]{1,0:T(8,128)(2,1)S(1)}, u32[]{:S(2)}, u32[]{:S(2)}) collective-permute-start(s16[80,256]{1,0:T(8,128)(2,1)S(1)} %get-tuple-element.37), channel_id=1, source_target_pairs={{0,4},{1,5},{2,6},{3,7},{4,0},{5,1},{6,2},{7,3},{8,12},{9,13},{10,... | collective-permute-start | bytes 122888 | tf_op jit(solution)/shard_map/ppermute | solution.py:447
  29.0 1.3 %collective-permute-start.9 = (bf16[64,256]{1,0:T(8,128)(2,1)S(1)}, bf16[64,256]{1,0:T(8,128)(2,1)S(1)}, u32[]{:S(2)}, u32[]{:S(2)}) collective-permute-start(bf16[64,256]{1,0:T(8,128)(2,1)S(1)} %hidden_rows.1.own), channel_id=1, source_target_pairs={{0,16},{16,0},{1,17},{17,1},{2,18},{18,2},{3,19},{19,3},{4,20},{20... | collective-permute-start | bytes 98312 | tf_op jit(solution)/shard_map/ppermute | solution.py:498

commit v16 on v15

--- a/solution.py
+++ b/solution.py
@@ -27,7 +27,7 @@
 
 
 def tail_rows(slots):
-    return -(-slots // 16) * 16
+    return -(-slots // 8) * 8
 
 
 def encode(x):
@@ -223,20 +223,26 @@
 
     def step(i, carry):
         for m in range(STEP):
-            b = i * STEP + m
-            base = pl.multiple_of(table[1, b] * tile, tile)
+            at = i * STEP + m
+            base = pl.multiple_of(table[1, at] * tile, tile)
             rows, places = [], []
             for k in range(BLOCK):
-                word = table[0, b * BLOCK + k]
+                word = table[0, at * BLOCK + k]
                 u = jnp.bitwise_and(lax.shift_right_logical(word, 5), 511)
                 rows.append(tbuf[u] * masks[jnp.bitwise_and(word, 31)])
                 places.append(pl.multiple_of(lax.shift_right_logical(word, 14) * UNIT, UNIT))
             lhs = jnp.concatenate(rows, axis=0)
+            alike = [jnp.where(places[k] == places[k + 1], 1.0, 0.0) for k in range(0, BLOCK, 2)]
             for acc, (x, h) in zip(accs, columns):
                 got = jnp.dot(lhs, x[pl.ds(base, tile), h:h + PART], preferred_element_type=jnp.float32)
                 got = got.astype(jnp.bfloat16).astype(jnp.float32)
-                for k in range(BLOCK):
-                    acc[pl.ds(places[k], UNIT), :] += got[k * UNIT:(k + 1) * UNIT, :]
+                for k in range(0, BLOCK, 2):
+                    first, second = pl.ds(places[k], UNIT), pl.ds(places[k + 1], UNIT)
+                    a, b = got[k * UNIT:(k + 1) * UNIT, :], got[(k + 1) * UNIT:(k + 2) * UNIT, :]
+                    b = b + a * alike[k // 2]
+                    a, b = acc[first, :] + a, acc[second, :] + b
+                    acc[first, :] = a
+                    acc[second, :] = b
         return carry
 
     steps = lax.div(table[1, table.shape[1] - 1] + STEP - 1, STEP)

time: 41.3 us -> 41 us (level)
  Pallas kernels: 12 us -> 12.7 us
  starting transfers between devices: 10.4 us -> 9.88 us
  waiting for transfers between devices: 8.75 us -> 8.3 us
    pallas_call x1, Pallas kernels: 4.67 us -> 5.34 us  [gathered_sums(): pl.pallas_call(tiles_kernel, out_shape=[sums] * parts, in_specs=[vmem] *...]
    ppermute x6, starting transfers between devices: 9.7 us -> 9.23 us  [exchange(): lax.ppermute(parts[k], 'dom', [(i, i ^ k * stride) for i in range(n)])]
    ppermute x6, waiting for transfers between devices: 7.55 us -> 7.1 us  [exchange(): lax.ppermute(parts[k], 'dom', [(i, i ^ k * stride) for i in range(n)])]
  transfers between devices with their start and end apart: 10 -> 10, of which waited for: 7 -> 4; matrix products, arithmetic and copies ran while one was open for 0% -> 0% of each run, Pallas kernels for 25% -> 27%
where the time goes in v16:
time: 41 us; the launch traced here: 40.8 us
  Pallas kernels  12.7 us (31%)
  starting transfers between devices  9.88 us (24%)
  blocking collectives  9.67 us (24%)
  waiting for transfers between devices  8.3 us (20%)
    all_to_all x1, blocking collectives, body(): lax.all_to_all(send, 'dom', 0, 0, axis_index_groups=[group_order(n)], til...  9.67 us
    ppermute x6, starting transfers between devices, exchange(): lax.ppermute(parts[k], 'dom', [(i, i ^ k * stride) for i in range(n)])  9.23 us
    ppermute x6, waiting for transfers between devices, exchange(): lax.ppermute(parts[k], 'dom', [(i, i ^ k * stride) for i in range(n)])  7.1 us
    pallas_call x1, Pallas kernels, gathered_sums(): pl.pallas_call(tiles_kernel, out_shape=[sums] * parts, in_specs=[vmem] *...  5.34 us
    pallas_call x1, Pallas kernels, plan(): pl.pallas_call(functools.partial(plan_kernel, chunks, per, n, radix, n_sr...  2.68 us
    pallas_call x3, Pallas kernels, sent_terms(): pl.pallas_call(functools.partial(sent_kernel, k, slots, rows, len(accs)),...  1.55 us
    ppermute x1, waiting for transfers between devices, body(): other = lax.ppermute(own, 'feat', swap)  1.19 us
    pallas_call x1, Pallas kernels, own_terms(): pl.pallas_call(functools.partial(own_kernel, chunk, per, groups, len(accs...  1.04 us
  transfers between devices with their start and end apart: 10, of which 4 were waited for; matrix products, arithmetic and copies ran while one was open for 0% of the time, Pallas kernels for 27%

profile of v16, /device:TPU:0, one launch (start us, length us, event | category | flops | bytes accessed | tf_op | source)
XLA Modules:
  0.0 40.8 jit_solution(16193185549134357437)
XLA Ops:
  0.0 0.5 %collective-permute-start.1 = (bf16[1024,512]{1,0:T(8,128)(2,1)}, bf16[1024,512]{1,0:T(8,128)(2,1)S(1)}, u32[]{:S(2)}, u32[]{:S(2)}) collective-permute-start(bf16[1024,512]{1,0:T(8,128)(2,1)} %xo.1), channel_id=1, source_target_pairs={{0,16},{16,0},{1,17},{17,1},{2,18},{18,2},{3,19},{19,3},{4,20},{20... | collective-permute-start | bytes 3145736 | tf_op jit(solution)/shard_map/ppermute | solution.py:480
  0.5 0.1 collective-permute-start
  0.5 0.1 pad_add_fusion.ids
  0.6 2.7 %plan.1 = (s32[2,640]{1,0:T(2,128)S(1)}, bf16[512,16,128]{2,1,0:T(8,128)(2,1)S(1)}, bf16[1024,512]{1,0:T(8,128)(2,1)S(1)}, bf16[512,256]{1,0:T(8,128)(2,1)S(1)}, bf16[512,256]{1,0:T(8,128)(2,1)S(1)}) custom-call(s32[2]{0:T(128)S(1)} %pad_add_fusion.ids, s32[1,128]{1,0:T(1,128)} %bitcast.17, s32[1,128]{1,0:T(1,128)} %bitcast.18, s32[1,128]{1,0:T(1,128)} %bitcast.19, ...), custom_call_target="tpu_custom_call" | custom-call | tf_op jit(solution)/shard_map/plan/pallas_call | solution.py:135
  3.3 0.0 collective-permute-done.1.xp
  3.3 5.3 %gathered_sums.1 = (f32[1040,256]{1,0:T(8,128)S(1)}, f32[1040,256]{1,0:T(8,128)S(1)}, f32[1040,256]{1,0:T(8,128)S(1)}, f32[1040,256]{1,0:T(8,128)S(1)}) custom-call(s32[2,640]{1,0:T(2,128)S(1)} %get-tuple-element.26.table_v, bf16[512,16,128]{2,1,0:T(8,128)(2,1)S(1)} %get-tuple-element.27.tbuf, bf16[1024,512]{1,0:T(8,128)(2,1)S(1)} %get-tuple-element.24.xo, ...), custom_call_target="tpu_custom_call" | custom-call | flops 2147483648 | bytes 8388608 | tf_op jit(solution)/shard_map/gathered_sums/pallas_call | solution.py:259
  8.6 0.0 collective-permute-done.wp
  8.6 0.5 %sent_terms.5 = s16[264,256]{1,0:T(8,128)(2,1)S(1)} custom-call(bf16[512,256]{1,0:T(8,128)(2,1)S(1)} %get-tuple-element.23.wo, bf16[512,256]{1,0:T(8,128)(2,1)S(1)} %collective-permute-done.wp, f32[1040,256]{1,0:T(8,128)S(1)} %get-tuple-element.28.refs_0_, f32[1040,256]{1,0:T(8,128)S(1)} %get-tuple-element.29.refs_1_, ...), custom_call_target="tpu_custom_call" | custom-call | flops 268435456 | bytes 2097152 | tf_op jit(solution)/shard_map/sent_terms/pallas_call | solution.py:303
  9.2 3.9 %collective-permute-start.4 = (s16[264,256]{1,0:T(8,128)(2,1)S(1)}, s16[264,256]{1,0:T(8,128)(2,1)S(1)}, u32[]{:S(2)}, u32[]{:S(2)}) collective-permute-start(s16[264,256]{1,0:T(8,128)(2,1)S(1)} %sent_terms.5), channel_id=1, source_target_pairs={{0,3},{1,2},{2,1},{3,0},{4,7},{5,6},{6,5},{7,4},{8,11},{9,10},{10,... | collective-permute-start | bytes 405512 | tf_op jit(solution)/shard_map/ppermute | solution.py:453
  13.1 0.5 %sent_terms.4 = s16[264,256]{1,0:T(8,128)(2,1)S(1)} custom-call(bf16[512,256]{1,0:T(8,128)(2,1)S(1)} %get-tuple-element.23.wo, bf16[512,256]{1,0:T(8,128)(2,1)S(1)} %collective-permute-done.wp, f32[1040,256]{1,0:T(8,128)S(1)} %get-tuple-element.28.refs_0_, f32[1040,256]{1,0:T(8,128)S(1)} %get-tuple-element.29.refs_1_, ...), custom_call_target="tpu_custom_call" | custom-call | flops 268435456 | bytes 2097152 | tf_op jit(solution)/shard_map/sent_terms/pallas_call | solution.py:303
  13.6 0.1 collective-permute-start.3
  13.7 0.5 %sent_terms.3 = s16[264,256]{1,0:T(8,128)(2,1)S(1)} custom-call(bf16[512,256]{1,0:T(8,128)(2,1)S(1)} %get-tuple-element.23.wo, bf16[512,256]{1,0:T(8,128)(2,1)S(1)} %collective-permute-done.wp, f32[1040,256]{1,0:T(8,128)S(1)} %get-tuple-element.28.refs_0_, f32[1040,256]{1,0:T(8,128)S(1)} %get-tuple-element.29.refs_1_, ...), custom_call_target="tpu_custom_call" | custom-call | flops 268435456 | bytes 2097152 | tf_op jit(solution)/shard_map/sent_terms/pallas_call | solution.py:303
  14.2 0.6 %collective-permute-start.2 = (s16[264,256]{1,0:T(8,128)(2,1)S(1)}, s16[264,256]{1,0:T(8,128)(2,1)S(1)}, u32[]{:S(2)}, u32[]{:S(2)}) collective-permute-start(s16[264,256]{1,0:T(8,128)(2,1)S(1)} %sent_terms.3), channel_id=1, source_target_pairs={{0,1},{1,0},{2,3},{3,2},{4,5},{5,4},{6,7},{7,6},{8,9},{9,8},{10,11... | collective-permute-start | bytes 405512 | tf_op jit(solution)/shard_map/ppermute | solution.py:453
  14.9 0.0 copy-start.2
  14.9 0.0 copy-start.3
  14.9 0.0 copy-start.4
  14.9 1.0 %own_terms.1 = (f32[256,256]{1,0:T(8,128)S(1)}, f32[64,256]{1,0:T(8,128)S(1)}) custom-call(s32[2]{0:T(128)S(1)} %pad_add_fusion.ids, bf16[512,256]{1,0:T(8,128)(2,1)S(1)} %get-tuple-element.23.wo, bf16[512,256]{1,0:T(8,128)(2,1)S(1)} %collective-permute-done.wp, bf16[1024,512]{1,0:T(8,128)(2,1)S(1)} %get-tuple-element.24.xo, ...), custom_call_target="tpu_custom_call" | custom-call | flops 268435456 | bytes 2097152 | tf_op jit(solution)/shard_map/own_terms/pallas_call | solution.py:336
  15.9 0.0 copy-start
  15.9 0.0 copy-start.1
  15.9 0.1 collective-permute-start.5
  16.0 1.1 %collective-permute-done.4.refs_2_ = s16[264,256]{1,0:T(8,128)(2,1)S(1)} collective-permute-done((s16[264,256]{1,0:T(8,128)(2,1)S(1)}, s16[264,256]{1,0:T(8,128)(2,1)S(1)}, u32[]{:S(2)}, u32[]{:S(2)}) %collective-permute-start.4) | collective-permute-done | bytes 135200 | tf_op jit(solution)/shard_map/ppermute | solution.py:453
  17.1 2.6 %collective-permute-done.3.refs_1_ = s16[264,256]{1,0:T(8,128)(2,1)S(1)} collective-permute-done((s16[264,256]{1,0:T(8,128)(2,1)S(1)}, s16[264,256]{1,0:T(8,128)(2,1)S(1)}, u32[]{:S(2)}, u32[]{:S(2)}) %collective-permute-start.3) | collective-permute-done | bytes 135200 | tf_op jit(solution)/shard_map/ppermute | solution.py:453
  19.8 0.0 collective-permute-done.2.refs_0_
  19.8 0.2 combine.1
  20.0 2.9 %collective-permute-start.6 = (s16[72,256]{1,0:T(8,128)(2,1)S(1)}, s16[72,256]{1,0:T(8,128)(2,1)S(1)}, u32[]{:S(2)}, u32[]{:S(2)}) collective-permute-start(s16[72,256]{1,0:T(8,128)(2,1)S(1)} %get-tuple-element.35), channel_id=1, source_target_pairs={{0,8},{1,9},{2,10},{3,11},{4,12},{5,13},{6,14},{7,15},{8,0},{9,1},... | collective-permute-start | bytes 110600 | tf_op jit(solution)/shard_map/ppermute | solution.py:453
  22.9 1.4 %collective-permute-start.7 = (s16[72,256]{1,0:T(8,128)(2,1)S(1)}, s16[72,256]{1,0:T(8,128)(2,1)S(1)}, u32[]{:S(2)}, u32[]{:S(2)}) collective-permute-start(s16[72,256]{1,0:T(8,128)(2,1)S(1)} %get-tuple-element.36), channel_id=1, source_target_pairs={{0,12},{1,13},{2,14},{3,15},{4,8},{5,9},{6,10},{7,11},{8,4},{9,5},... | collective-permute-start | bytes 110600 | tf_op jit(solution)/shard_map/ppermute | solution.py:453
  24.3 0.3 collective-permute-start.8
  24.6 0.0 copy-done.2
  24.6 0.0 copy-done.3
  24.6 0.0 copy-done.4
  24.6 0.7 %selection.1 = (bf16[128,128]{1,0:T(8,128)(2,1)S(1)}, bf16[128,128]{1,0:T(8,128)(2,1)S(1)}, bf16[64,128]{1,0:T(8,128)(2,1)S(1)}) custom-call(s32[2]{0:T(128)S(1)} %pad_add_fusion.ids, s32[16,8,16]{2,1,0:T(8,128)S(1)} %bitcast.15, s32[16,16]{1,0:T(8,128)S(1)} %copy-done.4, bf16[64,256]{1,0:T(8,128)(2,1)S(1)} %copy-done.3), custom_call_target="tpu_custom_call" | custom-call | tf_op jit(solution)/shard_map/selection/pallas_call | solution.py:195
  25.3 0.0 collective-permute-done.5.refs_1_
  25.3 0.0 collective-permute-done.6.refs_2_
  25.3 3.4 %collective-permute-done.7.refs_3_ = s16[72,256]{1,0:T(8,128)(2,1)S(1)} collective-permute-done((s16[72,256]{1,0:T(8,128)(2,1)S(1)}, s16[72,256]{1,0:T(8,128)(2,1)S(1)}, u32[]{:S(2)}, u32[]{:S(2)}) %collective-permute-start.7) | collective-permute-done | bytes 36896 | tf_op jit(solution)/shard_map/ppermute | solution.py:453
  28.6 0.0 collective-permute-done.8.refs_4_
  28.7 0.1 collective-permute-start.9
  28.8 1.2 %collective-permute-done.9.other = bf16[64,256]{1,0:T(8,128)(2,1)S(1)} collective-permute-done((bf16[64,256]{1,0:T(8,128)(2,1)S(1)}, bf16[64,256]{1,0:T(8,128)(2,1)S(1)}, u32[]{:S(2)}, u32[]{:S(2)}) %collective-permute-start.9) | collective-permute-done | bytes 32800 | tf_op jit(solution)/shard_map/ppermute | solution.py:504
  30.0 0.1 rows_to_send.1
  30.1 9.7 %all_to_all.11 = bf16[16,8,256]{2,1,0:T(8,128)(2,1)S(1)} all-to-all(bf16[16,8,256]{2,1,0:T(8,128)(2,1)S(1)} %bitcast.11), channel_id=1, replica_groups={{15,14,13,12,11,10,9,8,7,6,5,4,3,2,1,0},{31,30,29,28,27,26,25,24,23,22,..., dimensions={0} | all-to-all | bytes 131072 | tf_op jit(solution)/shard_map/all_to_all | solution.py:506
  39.8 0.0 copy-done
  39.8 0.0 copy-done.1
  39.8 1.0 %logits.1 = f32[64,172]{1,0:T(8,128)} custom-call(bf16[64,256]{1,0:T(8,128)(2,1)S(1)} %hidden_rows.1.own, bf16[64,256]{1,0:T(8,128)(2,1)S(1)} %collective-permute-done.9.other, bf16[128,256]{1,0:T(8,128)(2,1)S(1)} %bitcast.12, bf16[128,128]{1,0:T(8,128)(2,1)S(1)} %get-tuple-element.39.front, bf16[64,128]{1,0:T(8,128)(2,1)S(1)} %get-tuple-element.40.adj_received, ...), custom_call_target="tpu_custom_call" | custom-call | tf_op jit(solution)/shard_map/logits/pallas_call | solution.py:440
  (1 shorter events, 0.0 us)
Async XLA Ops:
  0.0 3.3 %collective-permute-start.1 = (bf16[1024,512]{1,0:T(8,128)(2,1)}, bf16[1024,512]{1,0:T(8,128)(2,1)S(1)}, u32[]{:S(2)}, u32[]{:S(2)}) collective-permute-start(bf16[1024,512]{1,0:T(8,128)(2,1)} %xo.1), channel_id=1, source_target_pairs={{0,16},{16,0},{1,17},{17,1},{2,18},{18,2},{3,19},{19,3},{4,20},{20... | collective-permute-start | bytes 3145736 | tf_op jit(solution)/shard_map/ppermute | solution.py:480
  0.5 8.2 %collective-permute-start = (bf16[512,256]{1,0:T(8,128)(2,1)}, bf16[512,256]{1,0:T(8,128)(2,1)S(1)}, u32[]{:S(2)}, u32[]{:S(2)}) collective-permute-start(bf16[512,256]{1,0:T(8,128)(2,1)} %wo.1), channel_id=1, source_target_pairs={{0,16},{16,0},{1,17},{17,1},{2,18},{18,2},{3,19},{19,3},{4,20},{20... | collective-permute-start | bytes 786440 | tf_op jit(solution)/shard_map/ppermute | solution.py:481
  9.2 7.9 %collective-permute-start.4 = (s16[264,256]{1,0:T(8,128)(2,1)S(1)}, s16[264,256]{1,0:T(8,128)(2,1)S(1)}, u32[]{:S(2)}, u32[]{:S(2)}) collective-permute-start(s16[264,256]{1,0:T(8,128)(2,1)S(1)} %sent_terms.5), channel_id=1, source_target_pairs={{0,3},{1,2},{2,1},{3,0},{4,7},{5,6},{6,5},{7,4},{8,11},{9,10},{10,... | collective-permute-start | bytes 405512 | tf_op jit(solution)/shard_map/ppermute | solution.py:453
  13.6 6.1 %collective-permute-start.3 = (s16[264,256]{1,0:T(8,128)(2,1)S(1)}, s16[264,256]{1,0:T(8,128)(2,1)S(1)}, u32[]{:S(2)}, u32[]{:S(2)}) collective-permute-start(s16[264,256]{1,0:T(8,128)(2,1)S(1)} %sent_terms.4), channel_id=1, source_target_pairs={{0,2},{1,3},{2,0},{3,1},{4,6},{5,7},{6,4},{7,5},{8,10},{9,11},{10,... | collective-permute-start | bytes 405512 | tf_op jit(solution)/shard_map/ppermute | solution.py:453
  14.2 5.5 %collective-permute-start.2 = (s16[264,256]{1,0:T(8,128)(2,1)S(1)}, s16[264,256]{1,0:T(8,128)(2,1)S(1)}, u32[]{:S(2)}, u32[]{:S(2)}) collective-permute-start(s16[264,256]{1,0:T(8,128)(2,1)S(1)} %sent_terms.3), channel_id=1, source_target_pairs={{0,1},{1,0},{2,3},{3,2},{4,5},{5,4},{6,7},{7,6},{8,9},{9,8},{10,11... | collective-permute-start | bytes 405512 | tf_op jit(solution)/shard_map/ppermute | solution.py:453
  14.9 9.7 %copy-start.2 = (s32[16,16,8]{1,2,0:T(8,128)S(1)}, s32[16,16,8]{1,2,0:T(8,128)}, u32[]{:S(2)}) copy-start(s32[16,16,8]{1,2,0:T(8,128)} %param.19) | copy-start | bytes 24580
  14.9 9.7 %copy-start.3 = (bf16[64,256]{1,0:T(8,128)(2,1)S(1)}, bf16[64,256]{1,0:T(8,128)(2,1)}, u32[]{:S(2)}) copy-start(bf16[64,256]{1,0:T(8,128)(2,1)} %adj.1) | copy-start | bytes 98308
  14.9 9.7 %copy-start.4 = (s32[16,16]{1,0:T(8,128)S(1)}, s32[16,16]{1,0:T(8,128)}, u32[]{:S(2)}) copy-start(s32[16,16]{1,0:T(8,128)} %counts.1) | copy-start | bytes 3076
  15.9 23.9 %copy-start = (bf16[256,172]{0,1:T(8,128)(2,1)S(1)}, bf16[256,172]{0,1:T(8,128)(2,1)}, u32[]{:S(2)}) copy-start(bf16[256,172]{0,1:T(8,128)(2,1)} %param.22) | copy-start | bytes 264196
  15.9 23.9 %copy-start.1 = (bf16[256,172]{0,1:T(8,128)(2,1)S(1)}, bf16[256,172]{0,1:T(8,128)(2,1)}, u32[]{:S(2)}) copy-start(bf16[256,172]{0,1:T(8,128)(2,1)} %param.23) | copy-start | bytes 264196
  15.9 9.3 %collective-permute-start.5 = (f32[64,256]{1,0:T(8,128)S(1)}, f32[64,256]{1,0:T(8,128)S(1)}, u32[]{:S(2)}, u32[]{:S(2)}) collective-permute-start(f32[64,256]{1,0:T(8,128)S(1)} %get-tuple-element.34), channel_id=1, source_target_pairs={{0,16},{16,0},{1,17},{17,1},{2,18},{18,2},{3,19},{19,3},{4,20},{20... | collective-permute-start | bytes 196616 | tf_op jit(solution)/shard_map/ppermute | solution.py:493
  20.0 5.3 %collective-permute-start.6 = (s16[72,256]{1,0:T(8,128)(2,1)S(1)}, s16[72,256]{1,0:T(8,128)(2,1)S(1)}, u32[]{:S(2)}, u32[]{:S(2)}) collective-permute-start(s16[72,256]{1,0:T(8,128)(2,1)S(1)} %get-tuple-element.35), channel_id=1, source_target_pairs={{0,8},{1,9},{2,10},{3,11},{4,12},{5,13},{6,14},{7,15},{8,0},{9,1},... | collective-permute-start | bytes 110600 | tf_op jit(solution)/shard_map/ppermute | solution.py:453
  22.9 5.8 %collective-permute-start.7 = (s16[72,256]{1,0:T(8,128)(2,1)S(1)}, s16[72,256]{1,0:T(8,128)(2,1)S(1)}, u32[]{:S(2)}, u32[]{:S(2)}) collective-permute-start(s16[72,256]{1,0:T(8,128)(2,1)S(1)} %get-tuple-element.36), channel_id=1, source_target_pairs={{0,12},{1,13},{2,14},{3,15},{4,8},{5,9},{6,10},{7,11},{8,4},{9,5},... | collective-permute-start | bytes 110600 | tf_op jit(solution)/shard_map/ppermute | solution.py:453
  24.3 4.4 %collective-permute-start.8 = (s16[72,256]{1,0:T(8,128)(2,1)S(1)}, s16[72,256]{1,0:T(8,128)(2,1)S(1)}, u32[]{:S(2)}, u32[]{:S(2)}) collective-permute-start(s16[72,256]{1,0:T(8,128)(2,1)S(1)} %get-tuple-element.37), channel_id=1, source_target_pairs={{0,4},{1,5},{2,6},{3,7},{4,0},{5,1},{6,2},{7,3},{8,12},{9,13},{10,... | collective-permute-start | bytes 110600 | tf_op jit(solution)/shard_map/ppermute | solution.py:453
  28.7 1.3 %collective-permute-start.9 = (bf16[64,256]{1,0:T(8,128)(2,1)S(1)}, bf16[64,256]{1,0:T(8,128)(2,1)S(1)}, u32[]{:S(2)}, u32[]{:S(2)}) collective-permute-start(bf16[64,256]{1,0:T(8,128)(2,1)S(1)} %hidden_rows.1.own), channel_id=1, source_target_pairs={{0,16},{16,0},{1,17},{17,1},{2,18},{18,2},{3,19},{19,3},{4,20},{20... | collective-permute-start | bytes 98312 | tf_op jit(solution)/shard_map/ppermute | solution.py:504

commit v17 on v15

--- a/solution.py
+++ b/solution.py
@@ -8,8 +8,8 @@
 from jax.sharding import PartitionSpec as P
 
 UNIT = 16
-BLOCK = 8
-STEP = 8
+BLOCK = 16
+STEP = 4
 PART = 256
 CHUNKS = 1
 
@@ -27,7 +27,7 @@
 
 
 def tail_rows(slots):
-    return -(-slots // 16) * 16
+    return -(-slots // 8) * 8
 
 
 def encode(x):
@@ -223,11 +223,11 @@
 
     def step(i, carry):
         for m in range(STEP):
-            b = i * STEP + m
-            base = pl.multiple_of(table[1, b] * tile, tile)
+            at = i * STEP + m
+            base = pl.multiple_of(table[1, at] * tile, tile)
             rows, places = [], []
             for k in range(BLOCK):
-                word = table[0, b * BLOCK + k]
+                word = table[0, at * BLOCK + k]
                 u = jnp.bitwise_and(lax.shift_right_logical(word, 5), 511)
                 rows.append(tbuf[u] * masks[jnp.bitwise_and(word, 31)])
                 places.append(pl.multiple_of(lax.shift_right_logical(word, 14) * UNIT, UNIT))
@@ -277,8 +277,8 @@
             value = acc[pl.ds(first + at, size), :]
             high = value.astype(jnp.bfloat16)
             low = (value - high.astype(jnp.float32)).astype(jnp.bfloat16)
-            got = got + jnp.dot(high, w[h:h + PART, :], preferred_element_type=jnp.float32)
-            got = got + jnp.dot(low, w[h:h + PART, :], preferred_element_type=jnp.float32)
+            both = jnp.dot(jnp.concatenate([high, low], axis=0), w[h:h + PART, :], preferred_element_type=jnp.float32)
+            got = got + (both[:size, :] + both[size:, :])
         out[pl.ds(at, size), :] = got
         return carry
 

time: 41.3 us -> 41.4 us (level)
  Pallas kernels: 12 us -> 13.9 us
  starting transfers between devices: 10.4 us -> 8.56 us
    pallas_call x1, Pallas kernels: 4.67 us -> 6.58 us  [gathered_sums(): pl.pallas_call(tiles_kernel, out_shape=[sums] * parts, in_specs=[vmem] *...]
    ppermute x6, starting transfers between devices: 9.7 us -> 7.91 us  [exchange(): lax.ppermute(parts[k], 'dom', [(i, i ^ k * stride) for i in range(n)])]
  transfers between devices with their start and end apart: 10 -> 10, of which waited for: 7 -> 6; matrix products, arithmetic and copies ran while one was open for 0% -> 0% of each run, Pallas kernels for 25% -> 30%
where the time goes in v17:
time: 41.4 us; the launch traced here: 41.2 us
  Pallas kernels  13.9 us (34%)
  blocking collectives  9.86 us (24%)
  waiting for transfers between devices  8.65 us (21%)
  starting transfers between devices  8.56 us (21%)
    all_to_all x1, blocking collectives, body(): lax.all_to_all(send, 'dom', 0, 0, axis_index_groups=[group_order(n)], til...  9.86 us
    ppermute x6, starting transfers between devices, exchange(): lax.ppermute(parts[k], 'dom', [(i, i ^ k * stride) for i in range(n)])  7.91 us
    ppermute x6, waiting for transfers between devices, exchange(): lax.ppermute(parts[k], 'dom', [(i, i ^ k * stride) for i in range(n)])  7.45 us
    pallas_call x1, Pallas kernels, gathered_sums(): pl.pallas_call(tiles_kernel, out_shape=[sums] * parts, in_specs=[vmem] *...  6.58 us
    pallas_call x1, Pallas kernels, plan(): pl.pallas_call(functools.partial(plan_kernel, chunks, per, n, radix, n_sr...  2.68 us
    pallas_call x3, Pallas kernels, sent_terms(): pl.pallas_call(functools.partial(sent_kernel, k, slots, rows, len(accs)),...  1.54 us
    ppermute x1, waiting for transfers between devices, body(): other = lax.ppermute(own, 'feat', swap)  1.19 us
    pallas_call x1, Pallas kernels, own_terms(): pl.pallas_call(functools.partial(own_kernel, chunk, per, groups, len(accs...  1.05 us
  transfers between devices with their start and end apart: 10, of which 6 were waited for; matrix products, arithmetic and copies ran while one was open for 0% of the time, Pallas kernels for 30%

profile of v17, /device:TPU:0, one launch (start us, length us, event | category | flops | bytes accessed | tf_op | source)
XLA Modules:
  0.0 41.2 jit_solution(3107746352703909677)
XLA Ops:
  0.0 0.5 %collective-permute-start.1 = (bf16[1024,512]{1,0:T(8,128)(2,1)}, bf16[1024,512]{1,0:T(8,128)(2,1)S(1)}, u32[]{:S(2)}, u32[]{:S(2)}) collective-permute-start(bf16[1024,512]{1,0:T(8,128)(2,1)} %xo.1), channel_id=1, source_target_pairs={{0,16},{16,0},{1,17},{17,1},{2,18},{18,2},{3,19},{19,3},{4,20},{20... | collective-permute-start | bytes 3145736 | tf_op jit(solution)/shard_map/ppermute | solution.py:474
  0.5 0.1 collective-permute-start
  0.5 0.1 pad_add_fusion.ids
  0.6 2.7 %plan.1 = (s32[2,768]{1,0:T(2,128)S(1)}, bf16[512,16,128]{2,1,0:T(8,128)(2,1)S(1)}, bf16[1024,512]{1,0:T(8,128)(2,1)S(1)}, bf16[512,256]{1,0:T(8,128)(2,1)S(1)}, bf16[512,256]{1,0:T(8,128)(2,1)S(1)}) custom-call(s32[2]{0:T(128)S(1)} %pad_add_fusion.ids, s32[1,128]{1,0:T(1,128)} %bitcast.17, s32[1,128]{1,0:T(1,128)} %bitcast.18, s32[1,128]{1,0:T(1,128)} %bitcast.19, ...), custom_call_target="tpu_custom_call" | custom-call | tf_op jit(solution)/shard_map/plan/pallas_call | solution.py:135
  3.3 0.0 collective-permute-done.1.xp
  3.3 6.6 %gathered_sums.1 = (f32[1040,256]{1,0:T(8,128)S(1)}, f32[1040,256]{1,0:T(8,128)S(1)}, f32[1040,256]{1,0:T(8,128)S(1)}, f32[1040,256]{1,0:T(8,128)S(1)}) custom-call(s32[2,768]{1,0:T(2,128)S(1)} %get-tuple-element.26.table_v, bf16[512,16,128]{2,1,0:T(8,128)(2,1)S(1)} %get-tuple-element.27.tbuf, bf16[1024,512]{1,0:T(8,128)(2,1)S(1)} %get-tuple-element.24.xo, ...), custom_call_target="tpu_custom_call" | custom-call | flops 2147483648 | bytes 8388608 | tf_op jit(solution)/shard_map/gathered_sums/pallas_call | solution.py:253
  9.9 0.0 collective-permute-done.wp
  9.9 0.5 %sent_terms.5 = s16[264,256]{1,0:T(8,128)(2,1)S(1)} custom-call(bf16[512,256]{1,0:T(8,128)(2,1)S(1)} %get-tuple-element.23.wo, bf16[512,256]{1,0:T(8,128)(2,1)S(1)} %collective-permute-done.wp, f32[1040,256]{1,0:T(8,128)S(1)} %get-tuple-element.28.refs_0_, f32[1040,256]{1,0:T(8,128)S(1)} %get-tuple-element.29.refs_1_, ...), custom_call_target="tpu_custom_call" | custom-call | flops 268435456 | bytes 2097152 | tf_op jit(solution)/shard_map/sent_terms/pallas_call | solution.py:297
  10.4 3.1 %collective-permute-start.4 = (s16[264,256]{1,0:T(8,128)(2,1)S(1)}, s16[264,256]{1,0:T(8,128)(2,1)S(1)}, u32[]{:S(2)}, u32[]{:S(2)}) collective-permute-start(s16[264,256]{1,0:T(8,128)(2,1)S(1)} %sent_terms.5), channel_id=1, source_target_pairs={{0,3},{1,2},{2,1},{3,0},{4,7},{5,6},{6,5},{7,4},{8,11},{9,10},{10,... | collective-permute-start | bytes 405512 | tf_op jit(solution)/shard_map/ppermute | solution.py:447
  13.5 0.5 %sent_terms.4 = s16[264,256]{1,0:T(8,128)(2,1)S(1)} custom-call(bf16[512,256]{1,0:T(8,128)(2,1)S(1)} %get-tuple-element.23.wo, bf16[512,256]{1,0:T(8,128)(2,1)S(1)} %collective-permute-done.wp, f32[1040,256]{1,0:T(8,128)S(1)} %get-tuple-element.28.refs_0_, f32[1040,256]{1,0:T(8,128)S(1)} %get-tuple-element.29.refs_1_, ...), custom_call_target="tpu_custom_call" | custom-call | flops 268435456 | bytes 2097152 | tf_op jit(solution)/shard_map/sent_terms/pallas_call | solution.py:297
  14.0 0.6 %collective-permute-start.3 = (s16[264,256]{1,0:T(8,128)(2,1)S(1)}, s16[264,256]{1,0:T(8,128)(2,1)S(1)}, u32[]{:S(2)}, u32[]{:S(2)}) collective-permute-start(s16[264,256]{1,0:T(8,128)(2,1)S(1)} %sent_terms.4), channel_id=1, source_target_pairs={{0,2},{1,3},{2,0},{3,1},{4,6},{5,7},{6,4},{7,5},{8,10},{9,11},{10,... | collective-permute-start | bytes 405512 | tf_op jit(solution)/shard_map/ppermute | solution.py:447
  14.6 0.5 %sent_terms.3 = s16[264,256]{1,0:T(8,128)(2,1)S(1)} custom-call(bf16[512,256]{1,0:T(8,128)(2,1)S(1)} %get-tuple-element.23.wo, bf16[512,256]{1,0:T(8,128)(2,1)S(1)} %collective-permute-done.wp, f32[1040,256]{1,0:T(8,128)S(1)} %get-tuple-element.28.refs_0_, f32[1040,256]{1,0:T(8,128)S(1)} %get-tuple-element.29.refs_1_, ...), custom_call_target="tpu_custom_call" | custom-call | flops 268435456 | bytes 2097152 | tf_op jit(solution)/shard_map/sent_terms/pallas_call | solution.py:297
  15.1 0.1 collective-permute-start.2
  15.2 0.0 copy-start.2
  15.2 0.0 copy-start.3
  15.2 0.0 copy-start.4
  15.2 1.0 %own_terms.1 = (f32[256,256]{1,0:T(8,128)S(1)}, f32[64,256]{1,0:T(8,128)S(1)}) custom-call(s32[2]{0:T(128)S(1)} %pad_add_fusion.ids, bf16[512,256]{1,0:T(8,128)(2,1)S(1)} %get-tuple-element.23.wo, bf16[512,256]{1,0:T(8,128)(2,1)S(1)} %collective-permute-done.wp, bf16[1024,512]{1,0:T(8,128)(2,1)S(1)} %get-tuple-element.24.xo, ...), custom_call_target="tpu_custom_call" | custom-call | flops 268435456 | bytes 2097152 | tf_op jit(solution)/shard_map/own_terms/pallas_call | solution.py:330
  16.3 0.0 copy-start
  16.3 0.0 copy-start.1
  16.3 0.1 collective-permute-start.5
  16.4 1.1 %collective-permute-done.4.refs_2_ = s16[264,256]{1,0:T(8,128)(2,1)S(1)} collective-permute-done((s16[264,256]{1,0:T(8,128)(2,1)S(1)}, s16[264,256]{1,0:T(8,128)(2,1)S(1)}, u32[]{:S(2)}, u32[]{:S(2)}) %collective-permute-start.4) | collective-permute-done | bytes 135200 | tf_op jit(solution)/shard_map/ppermute | solution.py:447
  17.5 2.8 %collective-permute-done.3.refs_1_ = s16[264,256]{1,0:T(8,128)(2,1)S(1)} collective-permute-done((s16[264,256]{1,0:T(8,128)(2,1)S(1)}, s16[264,256]{1,0:T(8,128)(2,1)S(1)}, u32[]{:S(2)}, u32[]{:S(2)}) %collective-permute-start.3) | collective-permute-done | bytes 135200 | tf_op jit(solution)/shard_map/ppermute | solution.py:447
  20.3 0.1 collective-permute-done.2.refs_0_
  20.4 0.2 combine.1
  20.6 2.5 %collective-permute-start.6 = (s16[72,256]{1,0:T(8,128)(2,1)S(1)}, s16[72,256]{1,0:T(8,128)(2,1)S(1)}, u32[]{:S(2)}, u32[]{:S(2)}) collective-permute-start(s16[72,256]{1,0:T(8,128)(2,1)S(1)} %get-tuple-element.35), channel_id=1, source_target_pairs={{0,8},{1,9},{2,10},{3,11},{4,12},{5,13},{6,14},{7,15},{8,0},{9,1},... | collective-permute-start | bytes 110600 | tf_op jit(solution)/shard_map/ppermute | solution.py:447
  23.1 1.5 %collective-permute-start.7 = (s16[72,256]{1,0:T(8,128)(2,1)S(1)}, s16[72,256]{1,0:T(8,128)(2,1)S(1)}, u32[]{:S(2)}, u32[]{:S(2)}) collective-permute-start(s16[72,256]{1,0:T(8,128)(2,1)S(1)} %get-tuple-element.36), channel_id=1, source_target_pairs={{0,12},{1,13},{2,14},{3,15},{4,8},{5,9},{6,10},{7,11},{8,4},{9,5},... | collective-permute-start | bytes 110600 | tf_op jit(solution)/shard_map/ppermute | solution.py:447
  24.6 0.2 collective-permute-start.8
  24.8 0.0 copy-done.2
  24.8 0.0 copy-done.3
  24.8 0.0 copy-done.4
  24.8 0.7 %selection.1 = (bf16[128,128]{1,0:T(8,128)(2,1)S(1)}, bf16[128,128]{1,0:T(8,128)(2,1)S(1)}, bf16[64,128]{1,0:T(8,128)(2,1)S(1)}) custom-call(s32[2]{0:T(128)S(1)} %pad_add_fusion.ids, s32[16,8,16]{2,1,0:T(8,128)S(1)} %bitcast.15, s32[16,16]{1,0:T(8,128)S(1)} %copy-done.4, bf16[64,256]{1,0:T(8,128)(2,1)S(1)} %copy-done.3), custom_call_target="tpu_custom_call" | custom-call | tf_op jit(solution)/shard_map/selection/pallas_call | solution.py:195
  25.5 0.0 collective-permute-done.5.refs_1_
  25.5 0.4 collective-permute-done.6.refs_2_
  25.8 3.1 %collective-permute-done.7.refs_3_ = s16[72,256]{1,0:T(8,128)(2,1)S(1)} collective-permute-done((s16[72,256]{1,0:T(8,128)(2,1)S(1)}, s16[72,256]{1,0:T(8,128)(2,1)S(1)}, u32[]{:S(2)}, u32[]{:S(2)}) %collective-permute-start.7) | collective-permute-done | bytes 36896 | tf_op jit(solution)/shard_map/ppermute | solution.py:447
  28.9 0.0 collective-permute-done.8.refs_4_
  29.0 0.1 collective-permute-start.9
  29.0 1.2 %collective-permute-done.9.other = bf16[64,256]{1,0:T(8,128)(2,1)S(1)} collective-permute-done((bf16[64,256]{1,0:T(8,128)(2,1)S(1)}, bf16[64,256]{1,0:T(8,128)(2,1)S(1)}, u32[]{:S(2)}, u32[]{:S(2)}) %collective-permute-start.9) | collective-permute-done | bytes 32800 | tf_op jit(solution)/shard_map/ppermute | solution.py:498
  30.2 0.1 rows_to_send.1
  30.4 9.9 %all_to_all.11 = bf16[16,8,256]{2,1,0:T(8,128)(2,1)S(1)} all-to-all(bf16[16,8,256]{2,1,0:T(8,128)(2,1)S(1)} %bitcast.11), channel_id=1, replica_groups={{15,14,13,12,11,10,9,8,7,6,5,4,3,2,1,0},{31,30,29,28,27,26,25,24,23,22,..., dimensions={0} | all-to-all | bytes 131072 | tf_op jit(solution)/shard_map/all_to_all | solution.py:500
  40.2 0.0 copy-done
  40.2 0.0 copy-done.1
  40.2 1.0 %logits.1 = f32[64,172]{1,0:T(8,128)} custom-call(bf16[64,256]{1,0:T(8,128)(2,1)S(1)} %hidden_rows.1.own, bf16[64,256]{1,0:T(8,128)(2,1)S(1)} %collective-permute-done.9.other, bf16[128,256]{1,0:T(8,128)(2,1)S(1)} %bitcast.12, bf16[128,128]{1,0:T(8,128)(2,1)S(1)} %get-tuple-element.39.front, bf16[64,128]{1,0:T(8,128)(2,1)S(1)} %get-tuple-element.40.adj_received, ...), custom_call_target="tpu_custom_call" | custom-call | tf_op jit(solution)/shard_map/logits/pallas_call | solution.py:434
  (1 shorter events, 0.0 us)
Async XLA Ops:
  0.0 3.3 %collective-permute-start.1 = (bf16[1024,512]{1,0:T(8,128)(2,1)}, bf16[1024,512]{1,0:T(8,128)(2,1)S(1)}, u32[]{:S(2)}, u32[]{:S(2)}) collective-permute-start(bf16[1024,512]{1,0:T(8,128)(2,1)} %xo.1), channel_id=1, source_target_pairs={{0,16},{16,0},{1,17},{17,1},{2,18},{18,2},{3,19},{19,3},{4,20},{20... | collective-permute-start | bytes 3145736 | tf_op jit(solution)/shard_map/ppermute | solution.py:474
  0.5 9.4 %collective-permute-start = (bf16[512,256]{1,0:T(8,128)(2,1)}, bf16[512,256]{1,0:T(8,128)(2,1)S(1)}, u32[]{:S(2)}, u32[]{:S(2)}) collective-permute-start(bf16[512,256]{1,0:T(8,128)(2,1)} %wo.1), channel_id=1, source_target_pairs={{0,16},{16,0},{1,17},{17,1},{2,18},{18,2},{3,19},{19,3},{4,20},{20... | collective-permute-start | bytes 786440 | tf_op jit(solution)/shard_map/ppermute | solution.py:475
  10.4 7.1 %collective-permute-start.4 = (s16[264,256]{1,0:T(8,128)(2,1)S(1)}, s16[264,256]{1,0:T(8,128)(2,1)S(1)}, u32[]{:S(2)}, u32[]{:S(2)}) collective-permute-start(s16[264,256]{1,0:T(8,128)(2,1)S(1)} %sent_terms.5), channel_id=1, source_target_pairs={{0,3},{1,2},{2,1},{3,0},{4,7},{5,6},{6,5},{7,4},{8,11},{9,10},{10,... | collective-permute-start | bytes 405512 | tf_op jit(solution)/shard_map/ppermute | solution.py:447
  14.0 6.3 %collective-permute-start.3 = (s16[264,256]{1,0:T(8,128)(2,1)S(1)}, s16[264,256]{1,0:T(8,128)(2,1)S(1)}, u32[]{:S(2)}, u32[]{:S(2)}) collective-permute-start(s16[264,256]{1,0:T(8,128)(2,1)S(1)} %sent_terms.4), channel_id=1, source_target_pairs={{0,2},{1,3},{2,0},{3,1},{4,6},{5,7},{6,4},{7,5},{8,10},{9,11},{10,... | collective-permute-start | bytes 405512 | tf_op jit(solution)/shard_map/ppermute | solution.py:447
  15.1 5.3 %collective-permute-start.2 = (s16[264,256]{1,0:T(8,128)(2,1)S(1)}, s16[264,256]{1,0:T(8,128)(2,1)S(1)}, u32[]{:S(2)}, u32[]{:S(2)}) collective-permute-start(s16[264,256]{1,0:T(8,128)(2,1)S(1)} %sent_terms.3), channel_id=1, source_target_pairs={{0,1},{1,0},{2,3},{3,2},{4,5},{5,4},{6,7},{7,6},{8,9},{9,8},{10,11... | collective-permute-start | bytes 405512 | tf_op jit(solution)/shard_map/ppermute | solution.py:447
  15.2 9.5 %copy-start.2 = (s32[16,16,8]{1,2,0:T(8,128)S(1)}, s32[16,16,8]{1,2,0:T(8,128)}, u32[]{:S(2)}) copy-start(s32[16,16,8]{1,2,0:T(8,128)} %param.19) | copy-start | bytes 24580
  15.2 9.5 %copy-start.3 = (bf16[64,256]{1,0:T(8,128)(2,1)S(1)}, bf16[64,256]{1,0:T(8,128)(2,1)}, u32[]{:S(2)}) copy-start(bf16[64,256]{1,0:T(8,128)(2,1)} %adj.1) | copy-start | bytes 98308
  15.2 9.5 %copy-start.4 = (s32[16,16]{1,0:T(8,128)S(1)}, s32[16,16]{1,0:T(8,128)}, u32[]{:S(2)}) copy-start(s32[16,16]{1,0:T(8,128)} %counts.1) | copy-start | bytes 3076
  16.3 24.0 %copy-start = (bf16[256,172]{0,1:T(8,128)(2,1)S(1)}, bf16[256,172]{0,1:T(8,128)(2,1)}, u32[]{:S(2)}) copy-start(bf16[256,172]{0,1:T(8,128)(2,1)} %param.22) | copy-start | bytes 264196
  16.3 24.0 %copy-start.1 = (bf16[256,172]{0,1:T(8,128)(2,1)S(1)}, bf16[256,172]{0,1:T(8,128)(2,1)}, u32[]{:S(2)}) copy-start(bf16[256,172]{0,1:T(8,128)(2,1)} %param.23) | copy-start | bytes 264196
  16.3 9.2 %collective-permute-start.5 = (f32[64,256]{1,0:T(8,128)S(1)}, f32[64,256]{1,0:T(8,128)S(1)}, u32[]{:S(2)}, u32[]{:S(2)}) collective-permute-start(f32[64,256]{1,0:T(8,128)S(1)} %get-tuple-element.34), channel_id=1, source_target_pairs={{0,16},{16,0},{1,17},{17,1},{2,18},{18,2},{3,19},{19,3},{4,20},{20... | collective-permute-start | bytes 196616 | tf_op jit(solution)/shard_map/ppermute | solution.py:487
  20.6 5.2 %collective-permute-start.6 = (s16[72,256]{1,0:T(8,128)(2,1)S(1)}, s16[72,256]{1,0:T(8,128)(2,1)S(1)}, u32[]{:S(2)}, u32[]{:S(2)}) collective-permute-start(s16[72,256]{1,0:T(8,128)(2,1)S(1)} %get-tuple-element.35), channel_id=1, source_target_pairs={{0,8},{1,9},{2,10},{3,11},{4,12},{5,13},{6,14},{7,15},{8,0},{9,1},... | collective-permute-start | bytes 110600 | tf_op jit(solution)/shard_map/ppermute | solution.py:447
  23.1 5.8 %collective-permute-start.7 = (s16[72,256]{1,0:T(8,128)(2,1)S(1)}, s16[72,256]{1,0:T(8,128)(2,1)S(1)}, u32[]{:S(2)}, u32[]{:S(2)}) collective-permute-start(s16[72,256]{1,0:T(8,128)(2,1)S(1)} %get-tuple-element.36), channel_id=1, source_target_pairs={{0,12},{1,13},{2,14},{3,15},{4,8},{5,9},{6,10},{7,11},{8,4},{9,5},... | collective-permute-start | bytes 110600 | tf_op jit(solution)/shard_map/ppermute | solution.py:447
  24.6 4.4 %collective-permute-start.8 = (s16[72,256]{1,0:T(8,128)(2,1)S(1)}, s16[72,256]{1,0:T(8,128)(2,1)S(1)}, u32[]{:S(2)}, u32[]{:S(2)}) collective-permute-start(s16[72,256]{1,0:T(8,128)(2,1)S(1)} %get-tuple-element.37), channel_id=1, source_target_pairs={{0,4},{1,5},{2,6},{3,7},{4,0},{5,1},{6,2},{7,3},{8,12},{9,13},{10,... | collective-permute-start | bytes 110600 | tf_op jit(solution)/shard_map/ppermute | solution.py:447
  29.0 1.3 %collective-permute-start.9 = (bf16[64,256]{1,0:T(8,128)(2,1)S(1)}, bf16[64,256]{1,0:T(8,128)(2,1)S(1)}, u32[]{:S(2)}, u32[]{:S(2)}) collective-permute-start(bf16[64,256]{1,0:T(8,128)(2,1)S(1)} %hidden_rows.1.own), channel_id=1, source_target_pairs={{0,16},{16,0},{1,17},{17,1},{2,18},{18,2},{3,19},{19,3},{4,20},{20... | collective-permute-start | bytes 98312 | tf_op jit(solution)/shard_map/ppermute | solution.py:498

commit v18 on v15

--- a/solution.py
+++ b/solution.py
@@ -26,8 +26,13 @@
 LN2 = 0.6931471805599453
 
 
+def rounded(x):
+    spread = x * 65537.0
+    return spread - (spread - x)
+
+
 def tail_rows(slots):
-    return -(-slots // 16) * 16
+    return -(-slots // 8) * 8
 
 
 def encode(x):
@@ -234,7 +239,7 @@
             lhs = jnp.concatenate(rows, axis=0)
             for acc, (x, h) in zip(accs, columns):
                 got = jnp.dot(lhs, x[pl.ds(base, tile), h:h + PART], preferred_element_type=jnp.float32)
-                got = got.astype(jnp.bfloat16).astype(jnp.float32)
+                got = rounded(got)
                 for k in range(BLOCK):
                     acc[pl.ds(places[k], UNIT), :] += got[k * UNIT:(k + 1) * UNIT, :]
         return carry
@@ -275,10 +280,10 @@
         for i, acc in enumerate(accs):
             w, h = weights[i * PART // weights[0].shape[0]], i * PART % weights[0].shape[0]
             value = acc[pl.ds(first + at, size), :]
-            high = value.astype(jnp.bfloat16)
-            low = (value - high.astype(jnp.float32)).astype(jnp.bfloat16)
-            got = got + jnp.dot(high, w[h:h + PART, :], preferred_element_type=jnp.float32)
-            got = got + jnp.dot(low, w[h:h + PART, :], preferred_element_type=jnp.float32)
+            high = rounded(value)
+            both = jnp.concatenate([high.astype(jnp.bfloat16), (value - high).astype(jnp.bfloat16)], axis=0)
+            both = jnp.dot(both, w[h:h + PART, :], preferred_element_type=jnp.float32)
+            got = got + (both[:size, :] + both[size:, :])
         out[pl.ds(at, size), :] = got
         return carry
 

time: 41.3 us -> 41.8 us (1.012)
  Pallas kernels: 12 us -> 12.7 us
  waiting for transfers between devices: 8.75 us -> 8.28 us
    pallas_call x1, Pallas kernels: 4.67 us -> 5.25 us  [gathered_sums(): pl.pallas_call(tiles_kernel, out_shape=[sums] * parts, in_specs=[vmem] *...]
    ppermute x6, waiting for transfers between devices: 7.55 us -> 7.08 us  [exchange(): lax.ppermute(parts[k], 'dom', [(i, i ^ k * stride) for i in range(n)])]
  transfers between devices with their start and end apart: 10 -> 10, of which waited for: 7 -> 5; matrix products, arithmetic and copies ran while one was open for 0% -> 0% of each run, Pallas kernels for 25% -> 26%
where the time goes in v18:
time: 41.8 us; the launch traced here: 41.6 us
  Pallas kernels  12.7 us (30%)
  starting transfers between devices  10.2 us (24%)
  blocking collectives  10.2 us (24%)
  waiting for transfers between devices  8.28 us (20%)
    all_to_all x1, blocking collectives, body(): lax.all_to_all(send, 'dom', 0, 0, axis_index_groups=[group_order(n)], til...  10.2 us
    ppermute x6, starting transfers between devices, exchange(): lax.ppermute(parts[k], 'dom', [(i, i ^ k * stride) for i in range(n)])  9.54 us
    ppermute x6, waiting for transfers between devices, exchange(): lax.ppermute(parts[k], 'dom', [(i, i ^ k * stride) for i in range(n)])  7.08 us
    pallas_call x1, Pallas kernels, gathered_sums(): pl.pallas_call(tiles_kernel, out_shape=[sums] * parts, in_specs=[vmem] *...  5.25 us
    pallas_call x1, Pallas kernels, plan(): pl.pallas_call(functools.partial(plan_kernel, chunks, per, n, radix, n_sr...  2.68 us
    pallas_call x3, Pallas kernels, sent_terms(): pl.pallas_call(functools.partial(sent_kernel, k, slots, rows, len(accs)),...  1.63 us
    ppermute x1, waiting for transfers between devices, body(): other = lax.ppermute(own, 'feat', swap)  1.19 us
    pallas_call x1, Pallas kernels, own_terms(): pl.pallas_call(functools.partial(own_kernel, chunk, per, groups, len(accs...  1.09 us
  transfers between devices with their start and end apart: 10, of which 5 were waited for; matrix products, arithmetic and copies ran while one was open for 0% of the time, Pallas kernels for 26%

profile of v18, /device:TPU:0, one launch (start us, length us, event | category | flops | bytes accessed | tf_op | source)
XLA Modules:
  0.0 41.6 jit_solution(6824952647438280050)
XLA Ops:
  0.0 0.5 %collective-permute-start.1 = (bf16[1024,512]{1,0:T(8,128)(2,1)}, bf16[1024,512]{1,0:T(8,128)(2,1)S(1)}, u32[]{:S(2)}, u32[]{:S(2)}) collective-permute-start(bf16[1024,512]{1,0:T(8,128)(2,1)} %xo.1), channel_id=1, source_target_pairs={{0,16},{16,0},{1,17},{17,1},{2,18},{18,2},{3,19},{19,3},{4,20},{20... | collective-permute-start | bytes 3145736 | tf_op jit(solution)/shard_map/ppermute | solution.py:479
  0.5 0.1 collective-permute-start
  0.5 0.1 pad_add_fusion.ids
  0.6 2.7 %plan.1 = (s32[2,640]{1,0:T(2,128)S(1)}, bf16[512,16,128]{2,1,0:T(8,128)(2,1)S(1)}, bf16[1024,512]{1,0:T(8,128)(2,1)S(1)}, bf16[512,256]{1,0:T(8,128)(2,1)S(1)}, bf16[512,256]{1,0:T(8,128)(2,1)S(1)}) custom-call(s32[2]{0:T(128)S(1)} %pad_add_fusion.ids, s32[1,128]{1,0:T(1,128)} %bitcast.17, s32[1,128]{1,0:T(1,128)} %bitcast.18, s32[1,128]{1,0:T(1,128)} %bitcast.19, ...), custom_call_target="tpu_custom_call" | custom-call | tf_op jit(solution)/shard_map/plan/pallas_call | solution.py:140
  3.3 0.0 collective-permute-done.1.xp
  3.3 5.3 %gathered_sums.1 = (f32[1040,256]{1,0:T(8,128)S(1)}, f32[1040,256]{1,0:T(8,128)S(1)}, f32[1040,256]{1,0:T(8,128)S(1)}, f32[1040,256]{1,0:T(8,128)S(1)}) custom-call(s32[2,640]{1,0:T(2,128)S(1)} %get-tuple-element.26.table_v, bf16[512,16,128]{2,1,0:T(8,128)(2,1)S(1)} %get-tuple-element.27.tbuf, bf16[1024,512]{1,0:T(8,128)(2,1)S(1)} %get-tuple-element.24.xo, ...), custom_call_target="tpu_custom_call" | custom-call | flops 2147483648 | bytes 8388608 | tf_op jit(solution)/shard_map/gathered_sums/pallas_call | solution.py:258
  8.5 0.0 collective-permute-done.wp
  8.6 0.5 %sent_terms.5 = s16[264,256]{1,0:T(8,128)(2,1)S(1)} custom-call(bf16[512,256]{1,0:T(8,128)(2,1)S(1)} %get-tuple-element.23.wo, bf16[512,256]{1,0:T(8,128)(2,1)S(1)} %collective-permute-done.wp, f32[1040,256]{1,0:T(8,128)S(1)} %get-tuple-element.28.refs_0_, f32[1040,256]{1,0:T(8,128)S(1)} %get-tuple-element.29.refs_1_, ...), custom_call_target="tpu_custom_call" | custom-call | flops 268435456 | bytes 2097152 | tf_op jit(solution)/shard_map/sent_terms/pallas_call | solution.py:302
  9.1 4.0 %collective-permute-start.4 = (s16[264,256]{1,0:T(8,128)(2,1)S(1)}, s16[264,256]{1,0:T(8,128)(2,1)S(1)}, u32[]{:S(2)}, u32[]{:S(2)}) collective-permute-start(s16[264,256]{1,0:T(8,128)(2,1)S(1)} %sent_terms.5), channel_id=1, source_target_pairs={{0,3},{1,2},{2,1},{3,0},{4,7},{5,6},{6,5},{7,4},{8,11},{9,10},{10,... | collective-permute-start | bytes 405512 | tf_op jit(solution)/shard_map/ppermute | solution.py:452
  13.1 0.5 %sent_terms.4 = s16[264,256]{1,0:T(8,128)(2,1)S(1)} custom-call(bf16[512,256]{1,0:T(8,128)(2,1)S(1)} %get-tuple-element.23.wo, bf16[512,256]{1,0:T(8,128)(2,1)S(1)} %collective-permute-done.wp, f32[1040,256]{1,0:T(8,128)S(1)} %get-tuple-element.28.refs_0_, f32[1040,256]{1,0:T(8,128)S(1)} %get-tuple-element.29.refs_1_, ...), custom_call_target="tpu_custom_call" | custom-call | flops 268435456 | bytes 2097152 | tf_op jit(solution)/shard_map/sent_terms/pallas_call | solution.py:302
  13.6 1.5 %collective-permute-start.3 = (s16[264,256]{1,0:T(8,128)(2,1)S(1)}, s16[264,256]{1,0:T(8,128)(2,1)S(1)}, u32[]{:S(2)}, u32[]{:S(2)}) collective-permute-start(s16[264,256]{1,0:T(8,128)(2,1)S(1)} %sent_terms.4), channel_id=1, source_target_pairs={{0,2},{1,3},{2,0},{3,1},{4,6},{5,7},{6,4},{7,5},{8,10},{9,11},{10,... | collective-permute-start | bytes 405512 | tf_op jit(solution)/shard_map/ppermute | solution.py:452
  15.2 0.5 %sent_terms.3 = s16[264,256]{1,0:T(8,128)(2,1)S(1)} custom-call(bf16[512,256]{1,0:T(8,128)(2,1)S(1)} %get-tuple-element.23.wo, bf16[512,256]{1,0:T(8,128)(2,1)S(1)} %collective-permute-done.wp, f32[1040,256]{1,0:T(8,128)S(1)} %get-tuple-element.28.refs_0_, f32[1040,256]{1,0:T(8,128)S(1)} %get-tuple-element.29.refs_1_, ...), custom_call_target="tpu_custom_call" | custom-call | flops 268435456 | bytes 2097152 | tf_op jit(solution)/shard_map/sent_terms/pallas_call | solution.py:302
  15.7 0.1 collective-permute-start.2
  15.8 0.0 copy-start.2
  15.8 0.0 copy-start.3
  15.8 0.0 copy-start.4
  15.8 1.1 %own_terms.1 = (f32[256,256]{1,0:T(8,128)S(1)}, f32[64,256]{1,0:T(8,128)S(1)}) custom-call(s32[2]{0:T(128)S(1)} %pad_add_fusion.ids, bf16[512,256]{1,0:T(8,128)(2,1)S(1)} %get-tuple-element.23.wo, bf16[512,256]{1,0:T(8,128)(2,1)S(1)} %collective-permute-done.wp, bf16[1024,512]{1,0:T(8,128)(2,1)S(1)} %get-tuple-element.24.xo, ...), custom_call_target="tpu_custom_call" | custom-call | flops 268435456 | bytes 2097152 | tf_op jit(solution)/shard_map/own_terms/pallas_call | solution.py:335
  16.9 0.0 copy-start
  16.9 0.0 copy-start.1
  17.0 0.1 collective-permute-start.5
  17.0 0.0 collective-permute-done.4.refs_2_
  17.0 2.8 %collective-permute-done.3.refs_1_ = s16[264,256]{1,0:T(8,128)(2,1)S(1)} collective-permute-done((s16[264,256]{1,0:T(8,128)(2,1)S(1)}, s16[264,256]{1,0:T(8,128)(2,1)S(1)}, u32[]{:S(2)}, u32[]{:S(2)}) %collective-permute-start.3) | collective-permute-done | bytes 135200 | tf_op jit(solution)/shard_map/ppermute | solution.py:452
  19.8 1.2 %collective-permute-done.2.refs_0_ = s16[264,256]{1,0:T(8,128)(2,1)S(1)} collective-permute-done((s16[264,256]{1,0:T(8,128)(2,1)S(1)}, s16[264,256]{1,0:T(8,128)(2,1)S(1)}, u32[]{:S(2)}, u32[]{:S(2)}) %collective-permute-start.2) | collective-permute-done | bytes 135200 | tf_op jit(solution)/shard_map/ppermute | solution.py:452
  21.0 0.2 combine.1
  21.2 2.0 %collective-permute-start.6 = (s16[72,256]{1,0:T(8,128)(2,1)S(1)}, s16[72,256]{1,0:T(8,128)(2,1)S(1)}, u32[]{:S(2)}, u32[]{:S(2)}) collective-permute-start(s16[72,256]{1,0:T(8,128)(2,1)S(1)} %get-tuple-element.35), channel_id=1, source_target_pairs={{0,8},{1,9},{2,10},{3,11},{4,12},{5,13},{6,14},{7,15},{8,0},{9,1},... | collective-permute-start | bytes 110600 | tf_op jit(solution)/shard_map/ppermute | solution.py:452
  23.2 1.5 %collective-permute-start.7 = (s16[72,256]{1,0:T(8,128)(2,1)S(1)}, s16[72,256]{1,0:T(8,128)(2,1)S(1)}, u32[]{:S(2)}, u32[]{:S(2)}) collective-permute-start(s16[72,256]{1,0:T(8,128)(2,1)S(1)} %get-tuple-element.36), channel_id=1, source_target_pairs={{0,12},{1,13},{2,14},{3,15},{4,8},{5,9},{6,10},{7,11},{8,4},{9,5},... | collective-permute-start | bytes 110600 | tf_op jit(solution)/shard_map/ppermute | solution.py:452
  24.7 0.5 %collective-permute-start.8 = (s16[72,256]{1,0:T(8,128)(2,1)S(1)}, s16[72,256]{1,0:T(8,128)(2,1)S(1)}, u32[]{:S(2)}, u32[]{:S(2)}) collective-permute-start(s16[72,256]{1,0:T(8,128)(2,1)S(1)} %get-tuple-element.37), channel_id=1, source_target_pairs={{0,4},{1,5},{2,6},{3,7},{4,0},{5,1},{6,2},{7,3},{8,12},{9,13},{10,... | collective-permute-start | bytes 110600 | tf_op jit(solution)/shard_map/ppermute | solution.py:452
  25.1 0.0 copy-done.2
  25.2 0.0 copy-done.3
  25.2 0.0 copy-done.4
  25.2 0.7 %selection.1 = (bf16[128,128]{1,0:T(8,128)(2,1)S(1)}, bf16[128,128]{1,0:T(8,128)(2,1)S(1)}, bf16[64,128]{1,0:T(8,128)(2,1)S(1)}) custom-call(s32[2]{0:T(128)S(1)} %pad_add_fusion.ids, s32[16,8,16]{2,1,0:T(8,128)S(1)} %bitcast.15, s32[16,16]{1,0:T(8,128)S(1)} %copy-done.4, bf16[64,256]{1,0:T(8,128)(2,1)S(1)} %copy-done.3), custom_call_target="tpu_custom_call" | custom-call | tf_op jit(solution)/shard_map/selection/pallas_call | solution.py:200
  25.9 0.0 collective-permute-done.5.refs_1_
  25.9 1.3 %collective-permute-done.6.refs_2_ = s16[72,256]{1,0:T(8,128)(2,1)S(1)} collective-permute-done((s16[72,256]{1,0:T(8,128)(2,1)S(1)}, s16[72,256]{1,0:T(8,128)(2,1)S(1)}, u32[]{:S(2)}, u32[]{:S(2)}) %collective-permute-start.6) | collective-permute-done | bytes 36896 | tf_op jit(solution)/shard_map/ppermute | solution.py:452
  27.2 1.8 %collective-permute-done.7.refs_3_ = s16[72,256]{1,0:T(8,128)(2,1)S(1)} collective-permute-done((s16[72,256]{1,0:T(8,128)(2,1)S(1)}, s16[72,256]{1,0:T(8,128)(2,1)S(1)}, u32[]{:S(2)}, u32[]{:S(2)}) %collective-permute-start.7) | collective-permute-done | bytes 36896 | tf_op jit(solution)/shard_map/ppermute | solution.py:452
  29.0 0.0 collective-permute-done.8.refs_4_
  29.1 0.1 collective-permute-start.9
  29.1 1.2 %collective-permute-done.9.other = bf16[64,256]{1,0:T(8,128)(2,1)S(1)} collective-permute-done((bf16[64,256]{1,0:T(8,128)(2,1)S(1)}, bf16[64,256]{1,0:T(8,128)(2,1)S(1)}, u32[]{:S(2)}, u32[]{:S(2)}) %collective-permute-start.9) | collective-permute-done | bytes 32800 | tf_op jit(solution)/shard_map/ppermute | solution.py:503
  30.3 0.1 rows_to_send.1
  30.5 10.2 %all_to_all.11 = bf16[16,8,256]{2,1,0:T(8,128)(2,1)S(1)} all-to-all(bf16[16,8,256]{2,1,0:T(8,128)(2,1)S(1)} %bitcast.11), channel_id=1, replica_groups={{15,14,13,12,11,10,9,8,7,6,5,4,3,2,1,0},{31,30,29,28,27,26,25,24,23,22,..., dimensions={0} | all-to-all | bytes 131072 | tf_op jit(solution)/shard_map/all_to_all | solution.py:505
  40.6 0.0 copy-done
  40.6 0.0 copy-done.1
  40.7 1.0 %logits.1 = f32[64,172]{1,0:T(8,128)} custom-call(bf16[64,256]{1,0:T(8,128)(2,1)S(1)} %hidden_rows.1.own, bf16[64,256]{1,0:T(8,128)(2,1)S(1)} %collective-permute-done.9.other, bf16[128,256]{1,0:T(8,128)(2,1)S(1)} %bitcast.12, bf16[128,128]{1,0:T(8,128)(2,1)S(1)} %get-tuple-element.39.front, bf16[64,128]{1,0:T(8,128)(2,1)S(1)} %get-tuple-element.40.adj_received, ...), custom_call_target="tpu_custom_call" | custom-call | tf_op jit(solution)/shard_map/logits/pallas_call | solution.py:439
  (1 shorter events, 0.0 us)
Async XLA Ops:
  0.0 3.3 %collective-permute-start.1 = (bf16[1024,512]{1,0:T(8,128)(2,1)}, bf16[1024,512]{1,0:T(8,128)(2,1)S(1)}, u32[]{:S(2)}, u32[]{:S(2)}) collective-permute-start(bf16[1024,512]{1,0:T(8,128)(2,1)} %xo.1), channel_id=1, source_target_pairs={{0,16},{16,0},{1,17},{17,1},{2,18},{18,2},{3,19},{19,3},{4,20},{20... | collective-permute-start | bytes 3145736 | tf_op jit(solution)/shard_map/ppermute | solution.py:479
  0.5 8.1 %collective-permute-start = (bf16[512,256]{1,0:T(8,128)(2,1)}, bf16[512,256]{1,0:T(8,128)(2,1)S(1)}, u32[]{:S(2)}, u32[]{:S(2)}) collective-permute-start(bf16[512,256]{1,0:T(8,128)(2,1)} %wo.1), channel_id=1, source_target_pairs={{0,16},{16,0},{1,17},{17,1},{2,18},{18,2},{3,19},{19,3},{4,20},{20... | collective-permute-start | bytes 786440 | tf_op jit(solution)/shard_map/ppermute | solution.py:480
  9.1 7.9 %collective-permute-start.4 = (s16[264,256]{1,0:T(8,128)(2,1)S(1)}, s16[264,256]{1,0:T(8,128)(2,1)S(1)}, u32[]{:S(2)}, u32[]{:S(2)}) collective-permute-start(s16[264,256]{1,0:T(8,128)(2,1)S(1)} %sent_terms.5), channel_id=1, source_target_pairs={{0,3},{1,2},{2,1},{3,0},{4,7},{5,6},{6,5},{7,4},{8,11},{9,10},{10,... | collective-permute-start | bytes 405512 | tf_op jit(solution)/shard_map/ppermute | solution.py:452
  13.6 6.2 %collective-permute-start.3 = (s16[264,256]{1,0:T(8,128)(2,1)S(1)}, s16[264,256]{1,0:T(8,128)(2,1)S(1)}, u32[]{:S(2)}, u32[]{:S(2)}) collective-permute-start(s16[264,256]{1,0:T(8,128)(2,1)S(1)} %sent_terms.4), channel_id=1, source_target_pairs={{0,2},{1,3},{2,0},{3,1},{4,6},{5,7},{6,4},{7,5},{8,10},{9,11},{10,... | collective-permute-start | bytes 405512 | tf_op jit(solution)/shard_map/ppermute | solution.py:452
  15.7 5.3 %collective-permute-start.2 = (s16[264,256]{1,0:T(8,128)(2,1)S(1)}, s16[264,256]{1,0:T(8,128)(2,1)S(1)}, u32[]{:S(2)}, u32[]{:S(2)}) collective-permute-start(s16[264,256]{1,0:T(8,128)(2,1)S(1)} %sent_terms.3), channel_id=1, source_target_pairs={{0,1},{1,0},{2,3},{3,2},{4,5},{5,4},{6,7},{7,6},{8,9},{9,8},{10,11... | collective-permute-start | bytes 405512 | tf_op jit(solution)/shard_map/ppermute | solution.py:452
  15.8 9.3 %copy-start.2 = (s32[16,16,8]{1,2,0:T(8,128)S(1)}, s32[16,16,8]{1,2,0:T(8,128)}, u32[]{:S(2)}) copy-start(s32[16,16,8]{1,2,0:T(8,128)} %param.19) | copy-start | bytes 24580
  15.8 9.3 %copy-start.3 = (bf16[64,256]{1,0:T(8,128)(2,1)S(1)}, bf16[64,256]{1,0:T(8,128)(2,1)}, u32[]{:S(2)}) copy-start(bf16[64,256]{1,0:T(8,128)(2,1)} %adj.1) | copy-start | bytes 98308
  15.8 9.3 %copy-start.4 = (s32[16,16]{1,0:T(8,128)S(1)}, s32[16,16]{1,0:T(8,128)}, u32[]{:S(2)}) copy-start(s32[16,16]{1,0:T(8,128)} %counts.1) | copy-start | bytes 3076
  16.9 23.7 %copy-start = (bf16[256,172]{0,1:T(8,128)(2,1)S(1)}, bf16[256,172]{0,1:T(8,128)(2,1)}, u32[]{:S(2)}) copy-start(bf16[256,172]{0,1:T(8,128)(2,1)} %param.22) | copy-start | bytes 264196
  16.9 23.7 %copy-start.1 = (bf16[256,172]{0,1:T(8,128)(2,1)S(1)}, bf16[256,172]{0,1:T(8,128)(2,1)}, u32[]{:S(2)}) copy-start(bf16[256,172]{0,1:T(8,128)(2,1)} %param.23) | copy-start | bytes 264196
  17.0 8.9 %collective-permute-start.5 = (f32[64,256]{1,0:T(8,128)S(1)}, f32[64,256]{1,0:T(8,128)S(1)}, u32[]{:S(2)}, u32[]{:S(2)}) collective-permute-start(f32[64,256]{1,0:T(8,128)S(1)} %get-tuple-element.34), channel_id=1, source_target_pairs={{0,16},{16,0},{1,17},{17,1},{2,18},{18,2},{3,19},{19,3},{4,20},{20... | collective-permute-start | bytes 196616 | tf_op jit(solution)/shard_map/ppermute | solution.py:492
  21.2 6.0 %collective-permute-start.6 = (s16[72,256]{1,0:T(8,128)(2,1)S(1)}, s16[72,256]{1,0:T(8,128)(2,1)S(1)}, u32[]{:S(2)}, u32[]{:S(2)}) collective-permute-start(s16[72,256]{1,0:T(8,128)(2,1)S(1)} %get-tuple-element.35), channel_id=1, source_target_pairs={{0,8},{1,9},{2,10},{3,11},{4,12},{5,13},{6,14},{7,15},{8,0},{9,1},... | collective-permute-start | bytes 110600 | tf_op jit(solution)/shard_map/ppermute | solution.py:452
  23.2 5.8 %collective-permute-start.7 = (s16[72,256]{1,0:T(8,128)(2,1)S(1)}, s16[72,256]{1,0:T(8,128)(2,1)S(1)}, u32[]{:S(2)}, u32[]{:S(2)}) collective-permute-start(s16[72,256]{1,0:T(8,128)(2,1)S(1)} %get-tuple-element.36), channel_id=1, source_target_pairs={{0,12},{1,13},{2,14},{3,15},{4,8},{5,9},{6,10},{7,11},{8,4},{9,5},... | collective-permute-start | bytes 110600 | tf_op jit(solution)/shard_map/ppermute | solution.py:452
  24.7 4.4 %collective-permute-start.8 = (s16[72,256]{1,0:T(8,128)(2,1)S(1)}, s16[72,256]{1,0:T(8,128)(2,1)S(1)}, u32[]{:S(2)}, u32[]{:S(2)}) collective-permute-start(s16[72,256]{1,0:T(8,128)(2,1)S(1)} %get-tuple-element.37), channel_id=1, source_target_pairs={{0,4},{1,5},{2,6},{3,7},{4,0},{5,1},{6,2},{7,3},{8,12},{9,13},{10,... | collective-permute-start | bytes 110600 | tf_op jit(solution)/shard_map/ppermute | solution.py:452
  29.1 1.3 %collective-permute-start.9 = (bf16[64,256]{1,0:T(8,128)(2,1)S(1)}, bf16[64,256]{1,0:T(8,128)(2,1)S(1)}, u32[]{:S(2)}, u32[]{:S(2)}) collective-permute-start(bf16[64,256]{1,0:T(8,128)(2,1)S(1)} %hidden_rows.1.own), channel_id=1, source_target_pairs={{0,16},{16,0},{1,17},{17,1},{2,18},{18,2},{3,19},{19,3},{4,20},{20... | collective-permute-start | bytes 98312 | tf_op jit(solution)/shard_map/ppermute | solution.py:503

commit v19 on v15

--- a/solution.py
+++ b/solution.py
@@ -9,7 +9,7 @@
 
 UNIT = 16
 BLOCK = 8
-STEP = 8
+STEP = 4
 PART = 256
 CHUNKS = 1
 
@@ -27,7 +27,7 @@
 
 
 def tail_rows(slots):
-    return -(-slots // 16) * 16
+    return -(-slots // 8) * 8
 
 
 def encode(x):
@@ -59,11 +59,10 @@
     return value_of
 
 
-def plan_kernel(chunks, per, n, radix, n_src, ids, src_h, rows_h, dst_h, tw, xo, wo, so, *rest):
+def plan_kernel(chunks, per, n, radix, n_src, ids, src_h, rows_h, dst_h, tw, xo, *rest):
     tables, rest = rest[:chunks], rest[chunks:]
     tbufs, rest = rest[:chunks], rest[chunks:]
-    xo_out, wo_out, so_out = rest[:3]
-    src_v, rows_v, dst_v, sems = rest[3:]
+    xo_out, src_v, rows_v, dst_v, sems = rest
     core, me = ids[0], ids[1]
     tiles = src_v.shape[1]
     n_pos = tables[0].shape[1]
@@ -73,7 +72,7 @@
     gs = [group_of(core, i, groups) for i in range(half)]
     small = [(src_h, src_v), (rows_h, rows_v), (dst_h, dst_v)]
     large = [(tw.at[:, g], tbufs[i // per].at[pl.ds(i % per * tiles, tiles)]) for i, g in enumerate(gs)]
-    large += [(xo, xo_out), (wo, wo_out), (so, so_out)]
+    large += [(xo, xo_out)]
     copies = [pltpu.make_async_copy(a, b, sems.at[i]) for i, (a, b) in enumerate(small + large)]
     for c in copies:
         c.start()
@@ -123,7 +122,7 @@
         c.wait()
 
 
-def plan(chunks, per, n, radix, ids, src, rows, dst, tw, xo, wo, so):
+def plan(chunks, per, n, radix, ids, src, rows, dst, tw, xo):
     tiles, _, _, tile = tw.shape
     n_src = xo.shape[0] // tile
     blocks = -(-(per * tiles // BLOCK + n_src) // STEP) * STEP
@@ -136,24 +135,20 @@
         functools.partial(plan_kernel, chunks, per, n, radix, n_src),
         out_shape=[jax.ShapeDtypeStruct((2, n_pos), jnp.int32)] * chunks
         + [jax.ShapeDtypeStruct((per * tiles, UNIT, tile), tw.dtype)] * chunks
-        + [
-            jax.ShapeDtypeStruct(xo.shape, xo.dtype),
-            jax.ShapeDtypeStruct(wo.shape, wo.dtype),
-            jax.ShapeDtypeStruct(so.shape, so.dtype),
-        ],
-        in_specs=[smem] + [hbm] * 7,
-        out_specs=[vmem] * (2 * chunks + 3),
+        + [jax.ShapeDtypeStruct(xo.shape, xo.dtype)],
+        in_specs=[smem] + [hbm] * 5,
+        out_specs=[vmem] * (2 * chunks + 1),
         scratch_shapes=[
             pltpu.VMEM((1, tiles), jnp.int32),
             pltpu.VMEM((1, tiles), jnp.int32),
             pltpu.VMEM((1, tiles), jnp.int32),
-            pltpu.SemaphoreType.DMA((3 + half + 3,)),
+            pltpu.SemaphoreType.DMA((3 + half + 1,)),
         ],
         compiler_params=pltpu.CompilerParams(vmem_limit_bytes=32 * 1024 * 1024),
         name="plan",
     )(ids, *[
         pltpu.with_memory_space_constraint(a, pltpu.HBM)
-        for a in (src.reshape(1, tiles), rows.reshape(1, tiles), dst.reshape(1, tiles), tw, xo, wo, so)
+        for a in (src.reshape(1, tiles), rows.reshape(1, tiles), dst.reshape(1, tiles), tw, xo)
     ])
 
 
@@ -475,9 +470,10 @@
     wp = lax.ppermute(neighbour_weight_first, "feat", swap)
     tw = tile_weight.reshape(tile_weight.shape[0], groups, UNIT, tile)
     planned = plan(
-        CHUNKS, per, n, 4, ids, tile_src, tile_rows, tile_dst, tw, features, neighbour_weight_first, w_self1,
+        CHUNKS, per, n, 4, ids, tile_src, tile_rows, tile_dst, tw, features,
     )
-    tables, tbufs, (xo, wo, so) = planned[:CHUNKS], planned[CHUNKS:2 * CHUNKS], planned[2 * CHUNKS:]
+    tables, tbufs, xo = planned[:CHUNKS], planned[CHUNKS:2 * CHUNKS], planned[2 * CHUNKS]
+    wo, so = neighbour_weight_first, w_self1
     done = []
     for chunk in range(CHUNKS):
         accs = gathered_sums(per, n, tables[chunk], tbufs[chunk], xo, xp)

time: 41.3 us -> 41.6 us (level)
  Pallas kernels: 12 us -> 12.5 us
    pallas_call x1, Pallas kernels: 4.67 us -> 5.29 us  [gathered_sums(): pl.pallas_call(tiles_kernel, out_shape=[sums] * parts, in_specs=[vmem] *...]
  transfers between devices with their start and end apart: 10 -> 10, of which waited for: 7 -> 5; matrix products, arithmetic and copies ran while one was open for 0% -> 0% of each run, Pallas kernels for 25% -> 26%
where the time goes in v19:
time: 41.6 us; the launch traced here: 41.2 us
  Pallas kernels  12.5 us (30%)
  starting transfers between devices  10.4 us (25%)
  blocking collectives  9.67 us (23%)
  waiting for transfers between devices  8.34 us (20%)
    ppermute x6, starting transfers between devices, exchange(): lax.ppermute(parts[k], 'dom', [(i, i ^ k * stride) for i in range(n)])  9.74 us
    all_to_all x1, blocking collectives, body(): lax.all_to_all(send, 'dom', 0, 0, axis_index_groups=[group_order(n)], til...  9.67 us
    ppermute x6, waiting for transfers between devices, exchange(): lax.ppermute(parts[k], 'dom', [(i, i ^ k * stride) for i in range(n)])  7.14 us
    pallas_call x1, Pallas kernels, gathered_sums(): pl.pallas_call(tiles_kernel, out_shape=[sums] * parts, in_specs=[vmem] *...  5.29 us
    pallas_call x1, Pallas kernels, plan(): pl.pallas_call(functools.partial(plan_kernel, chunks, per, n, radix, n_sr...  2.55 us
    pallas_call x3, Pallas kernels, sent_terms(): pl.pallas_call(functools.partial(sent_kernel, k, slots, rows, len(accs)),...  1.54 us
    ppermute x1, waiting for transfers between devices, body(): other = lax.ppermute(own, 'feat', swap)  1.19 us
    pallas_call x1, Pallas kernels, own_terms(): pl.pallas_call(functools.partial(own_kernel, chunk, per, groups, len(accs...  1.04 us
  transfers between devices with their start and end apart: 10, of which 5 were waited for; matrix products, arithmetic and copies ran while one was open for 0% of the time, Pallas kernels for 26%

profile of v19, /device:TPU:0, one launch (start us, length us, event | category | flops | bytes accessed | tf_op | source)
XLA Modules:
  0.0 41.2 jit_solution(8442581035736050486)
XLA Ops:
  0.0 0.5 %collective-permute-start.1 = (bf16[1024,512]{1,0:T(8,128)(2,1)}, bf16[1024,512]{1,0:T(8,128)(2,1)S(1)}, u32[]{:S(2)}, u32[]{:S(2)}) collective-permute-start(bf16[1024,512]{1,0:T(8,128)(2,1)} %xo.1), channel_id=1, source_target_pairs={{0,16},{16,0},{1,17},{17,1},{2,18},{18,2},{3,19},{19,3},{4,20},{20... | collective-permute-start | bytes 3145736 | tf_op jit(solution)/shard_map/ppermute | solution.py:469
  0.5 0.1 collective-permute-start
  0.5 0.1 pad_add_fusion.ids
  0.6 2.5 %plan.1 = (s32[2,640]{1,0:T(2,128)S(1)}, bf16[512,16,128]{2,1,0:T(8,128)(2,1)S(1)}, bf16[1024,512]{1,0:T(8,128)(2,1)S(1)}) custom-call(s32[2]{0:T(128)S(1)} %pad_add_fusion.ids, s32[1,128]{1,0:T(1,128)} %bitcast.17, s32[1,128]{1,0:T(1,128)} %bitcast.18, s32[1,128]{1,0:T(1,128)} %bitcast.19, bf16[128,8,16,128]{3,2,1,0:T(8,128)(2,1)} %bitcast.16, ...), custom_call_target="tpu_custom_call" | custom-call | tf_op jit(solution)/shard_map/plan/pallas_call | solution.py:134
  3.1 0.0 collective-permute-done.1.xp
  3.2 0.0 copy-start
  3.2 5.3 %gathered_sums.1 = (f32[1040,256]{1,0:T(8,128)S(1)}, f32[1040,256]{1,0:T(8,128)S(1)}, f32[1040,256]{1,0:T(8,128)S(1)}, f32[1040,256]{1,0:T(8,128)S(1)}) custom-call(s32[2,640]{1,0:T(2,128)S(1)} %get-tuple-element.22.table_v, bf16[512,16,128]{2,1,0:T(8,128)(2,1)S(1)} %get-tuple-element.23.tbuf, bf16[1024,512]{1,0:T(8,128)(2,1)S(1)} %get-tuple-element.21.xo, ...), custom_call_target="tpu_custom_call" | custom-call | flops 2147483648 | bytes 8388608 | tf_op jit(solution)/shard_map/gathered_sums/pallas_call | solution.py:248
  8.5 0.0 collective-permute-done.wp
  8.5 0.0 copy-done
  8.5 0.5 %sent_terms.5 = s16[264,256]{1,0:T(8,128)(2,1)S(1)} custom-call(bf16[512,256]{1,0:T(8,128)(2,1)S(1)} %copy-done, bf16[512,256]{1,0:T(8,128)(2,1)S(1)} %collective-permute-done.wp, f32[1040,256]{1,0:T(8,128)S(1)} %get-tuple-element.24.refs_0_, f32[1040,256]{1,0:T(8,128)S(1)} %get-tuple-element.25.refs_1_, f32[1040,256]{1,0:T(8,128)S(1)} %get-tuple-element.26.refs_2_, ...), custom_call_target="tpu_custom_call" | custom-call | flops 268435456 | bytes 2097152 | tf_op jit(solution)/shard_map/sent_terms/pallas_call | solution.py:292
  9.0 3.5 %collective-permute-start.4 = (s16[264,256]{1,0:T(8,128)(2,1)S(1)}, s16[264,256]{1,0:T(8,128)(2,1)S(1)}, u32[]{:S(2)}, u32[]{:S(2)}) collective-permute-start(s16[264,256]{1,0:T(8,128)(2,1)S(1)} %sent_terms.5), channel_id=1, source_target_pairs={{0,3},{1,2},{2,1},{3,0},{4,7},{5,6},{6,5},{7,4},{8,11},{9,10},{10,... | collective-permute-start | bytes 405512 | tf_op jit(solution)/shard_map/ppermute | solution.py:442
  12.5 0.5 %sent_terms.4 = s16[264,256]{1,0:T(8,128)(2,1)S(1)} custom-call(bf16[512,256]{1,0:T(8,128)(2,1)S(1)} %copy-done, bf16[512,256]{1,0:T(8,128)(2,1)S(1)} %collective-permute-done.wp, f32[1040,256]{1,0:T(8,128)S(1)} %get-tuple-element.24.refs_0_, f32[1040,256]{1,0:T(8,128)S(1)} %get-tuple-element.25.refs_1_, f32[1040,256]{1,0:T(8,128)S(1)} %get-tuple-element.26.refs_2_, ...), custom_call_target="tpu_custom_call" | custom-call | flops 268435456 | bytes 2097152 | tf_op jit(solution)/shard_map/sent_terms/pallas_call | solution.py:292
  13.0 0.0 copy-start.1
  13.1 1.0 %collective-permute-start.3 = (s16[264,256]{1,0:T(8,128)(2,1)S(1)}, s16[264,256]{1,0:T(8,128)(2,1)S(1)}, u32[]{:S(2)}, u32[]{:S(2)}) collective-permute-start(s16[264,256]{1,0:T(8,128)(2,1)S(1)} %sent_terms.4), channel_id=1, source_target_pairs={{0,2},{1,3},{2,0},{3,1},{4,6},{5,7},{6,4},{7,5},{8,10},{9,11},{10,... | collective-permute-start | bytes 405512 | tf_op jit(solution)/shard_map/ppermute | solution.py:442
  14.0 0.5 %sent_terms.3 = s16[264,256]{1,0:T(8,128)(2,1)S(1)} custom-call(bf16[512,256]{1,0:T(8,128)(2,1)S(1)} %copy-done, bf16[512,256]{1,0:T(8,128)(2,1)S(1)} %collective-permute-done.wp, f32[1040,256]{1,0:T(8,128)S(1)} %get-tuple-element.24.refs_0_, f32[1040,256]{1,0:T(8,128)S(1)} %get-tuple-element.25.refs_1_, f32[1040,256]{1,0:T(8,128)S(1)} %get-tuple-element.26.refs_2_, ...), custom_call_target="tpu_custom_call" | custom-call | flops 268435456 | bytes 2097152 | tf_op jit(solution)/shard_map/sent_terms/pallas_call | solution.py:292
  14.6 0.0 copy-start.4
  14.6 0.0 copy-start.5
  14.6 0.0 copy-start.6
  14.6 0.2 collective-permute-start.2
  14.8 0.0 copy-done.1
  14.8 1.0 %own_terms.1 = (f32[256,256]{1,0:T(8,128)S(1)}, f32[64,256]{1,0:T(8,128)S(1)}) custom-call(s32[2]{0:T(128)S(1)} %pad_add_fusion.ids, bf16[512,256]{1,0:T(8,128)(2,1)S(1)} %copy-done, bf16[512,256]{1,0:T(8,128)(2,1)S(1)} %collective-permute-done.wp, bf16[1024,512]{1,0:T(8,128)(2,1)S(1)} %get-tuple-element.21.xo, bf16[512,256]{1,0:T(8,128)(2,1)S(1)} %copy-done.1, ...), custom_call_target="tpu_custom_call" | custom-call | flops 268435456 | bytes 2097152 | tf_op jit(solution)/shard_map/own_terms/pallas_call | solution.py:325
  15.8 0.0 copy-start.2
  15.8 0.0 copy-start.3
  15.9 0.1 collective-permute-start.5
  15.9 0.9 %collective-permute-done.4.refs_2_ = s16[264,256]{1,0:T(8,128)(2,1)S(1)} collective-permute-done((s16[264,256]{1,0:T(8,128)(2,1)S(1)}, s16[264,256]{1,0:T(8,128)(2,1)S(1)}, u32[]{:S(2)}, u32[]{:S(2)}) %collective-permute-start.4) | collective-permute-done | bytes 135200 | tf_op jit(solution)/shard_map/ppermute | solution.py:442
  16.9 2.8 %collective-permute-done.3.refs_1_ = s16[264,256]{1,0:T(8,128)(2,1)S(1)} collective-permute-done((s16[264,256]{1,0:T(8,128)(2,1)S(1)}, s16[264,256]{1,0:T(8,128)(2,1)S(1)}, u32[]{:S(2)}, u32[]{:S(2)}) %collective-permute-start.3) | collective-permute-done | bytes 135200 | tf_op jit(solution)/shard_map/ppermute | solution.py:442
  19.7 0.3 collective-permute-done.2.refs_0_
  19.9 0.2 combine.1
  20.1 3.2 %collective-permute-start.6 = (s16[72,256]{1,0:T(8,128)(2,1)S(1)}, s16[72,256]{1,0:T(8,128)(2,1)S(1)}, u32[]{:S(2)}, u32[]{:S(2)}) collective-permute-start(s16[72,256]{1,0:T(8,128)(2,1)S(1)} %get-tuple-element.31), channel_id=1, source_target_pairs={{0,8},{1,9},{2,10},{3,11},{4,12},{5,13},{6,14},{7,15},{8,0},{9,1},... | collective-permute-start | bytes 110600 | tf_op jit(solution)/shard_map/ppermute | solution.py:442
  23.3 1.4 %collective-permute-start.7 = (s16[72,256]{1,0:T(8,128)(2,1)S(1)}, s16[72,256]{1,0:T(8,128)(2,1)S(1)}, u32[]{:S(2)}, u32[]{:S(2)}) collective-permute-start(s16[72,256]{1,0:T(8,128)(2,1)S(1)} %get-tuple-element.32), channel_id=1, source_target_pairs={{0,12},{1,13},{2,14},{3,15},{4,8},{5,9},{6,10},{7,11},{8,4},{9,5},... | collective-permute-start | bytes 110600 | tf_op jit(solution)/shard_map/ppermute | solution.py:442
  24.7 0.5 %collective-permute-start.8 = (s16[72,256]{1,0:T(8,128)(2,1)S(1)}, s16[72,256]{1,0:T(8,128)(2,1)S(1)}, u32[]{:S(2)}, u32[]{:S(2)}) collective-permute-start(s16[72,256]{1,0:T(8,128)(2,1)S(1)} %get-tuple-element.33), channel_id=1, source_target_pairs={{0,4},{1,5},{2,6},{3,7},{4,0},{5,1},{6,2},{7,3},{8,12},{9,13},{10,... | collective-permute-start | bytes 110600 | tf_op jit(solution)/shard_map/ppermute | solution.py:442
  25.2 0.0 copy-done.4
  25.2 0.0 copy-done.5
  25.2 0.0 copy-done.6
  25.2 0.7 %selection.1 = (bf16[128,128]{1,0:T(8,128)(2,1)S(1)}, bf16[128,128]{1,0:T(8,128)(2,1)S(1)}, bf16[64,128]{1,0:T(8,128)(2,1)S(1)}) custom-call(s32[2]{0:T(128)S(1)} %pad_add_fusion.ids, s32[16,8,16]{2,1,0:T(8,128)S(1)} %bitcast.15, s32[16,16]{1,0:T(8,128)S(1)} %copy-done.6, bf16[64,256]{1,0:T(8,128)(2,1)S(1)} %copy-done.5), custom_call_target="tpu_custom_call" | custom-call | tf_op jit(solution)/shard_map/selection/pallas_call | solution.py:190
  25.9 0.0 collective-permute-done.5.refs_1_
  25.9 0.0 collective-permute-done.6.refs_2_
  25.9 3.1 %collective-permute-done.7.refs_3_ = s16[72,256]{1,0:T(8,128)(2,1)S(1)} collective-permute-done((s16[72,256]{1,0:T(8,128)(2,1)S(1)}, s16[72,256]{1,0:T(8,128)(2,1)S(1)}, u32[]{:S(2)}, u32[]{:S(2)}) %collective-permute-start.7) | collective-permute-done | bytes 36896 | tf_op jit(solution)/shard_map/ppermute | solution.py:442
  29.1 0.0 collective-permute-done.8.refs_4_
  29.1 0.1 collective-permute-start.9
  29.2 1.2 %collective-permute-done.9.other = bf16[64,256]{1,0:T(8,128)(2,1)S(1)} collective-permute-done((bf16[64,256]{1,0:T(8,128)(2,1)S(1)}, bf16[64,256]{1,0:T(8,128)(2,1)S(1)}, u32[]{:S(2)}, u32[]{:S(2)}) %collective-permute-start.9) | collective-permute-done | bytes 32800 | tf_op jit(solution)/shard_map/ppermute | solution.py:494
  30.4 0.1 rows_to_send.1
  30.5 9.7 %all_to_all.11 = bf16[16,8,256]{2,1,0:T(8,128)(2,1)S(1)} all-to-all(bf16[16,8,256]{2,1,0:T(8,128)(2,1)S(1)} %bitcast.11), channel_id=1, replica_groups={{15,14,13,12,11,10,9,8,7,6,5,4,3,2,1,0},{31,30,29,28,27,26,25,24,23,22,..., dimensions={0} | all-to-all | bytes 131072 | tf_op jit(solution)/shard_map/all_to_all | solution.py:496
  40.2 0.0 copy-done.2
  40.2 0.0 copy-done.3
  40.2 1.0 %logits.1 = f32[64,172]{1,0:T(8,128)} custom-call(bf16[64,256]{1,0:T(8,128)(2,1)S(1)} %hidden_rows.1.own, bf16[64,256]{1,0:T(8,128)(2,1)S(1)} %collective-permute-done.9.other, bf16[128,256]{1,0:T(8,128)(2,1)S(1)} %bitcast.12, bf16[128,128]{1,0:T(8,128)(2,1)S(1)} %get-tuple-element.35.front, bf16[64,128]{1,0:T(8,128)(2,1)S(1)} %get-tuple-element.36.adj_received, ...), custom_call_target="tpu_custom_call" | custom-call | tf_op jit(solution)/shard_map/logits/pallas_call | solution.py:429
  (1 shorter events, 0.0 us)
Async XLA Ops:
  0.0 3.1 %collective-permute-start.1 = (bf16[1024,512]{1,0:T(8,128)(2,1)}, bf16[1024,512]{1,0:T(8,128)(2,1)S(1)}, u32[]{:S(2)}, u32[]{:S(2)}) collective-permute-start(bf16[1024,512]{1,0:T(8,128)(2,1)} %xo.1), channel_id=1, source_target_pairs={{0,16},{16,0},{1,17},{17,1},{2,18},{18,2},{3,19},{19,3},{4,20},{20... | collective-permute-start | bytes 3145736 | tf_op jit(solution)/shard_map/ppermute | solution.py:469
  0.5 8.0 %collective-permute-start = (bf16[512,256]{1,0:T(8,128)(2,1)}, bf16[512,256]{1,0:T(8,128)(2,1)S(1)}, u32[]{:S(2)}, u32[]{:S(2)}) collective-permute-start(bf16[512,256]{1,0:T(8,128)(2,1)} %wo.7), channel_id=1, source_target_pairs={{0,16},{16,0},{1,17},{17,1},{2,18},{18,2},{3,19},{19,3},{4,20},{20... | collective-permute-start | bytes 786440 | tf_op jit(solution)/shard_map/ppermute | solution.py:470
  3.2 5.3 %copy-start = (bf16[512,256]{1,0:T(8,128)(2,1)S(1)}, bf16[512,256]{1,0:T(8,128)(2,1)}, u32[]{:S(2)}) copy-start(bf16[512,256]{1,0:T(8,128)(2,1)} %wo.7) | copy-start | bytes 786436
  9.0 7.8 %collective-permute-start.4 = (s16[264,256]{1,0:T(8,128)(2,1)S(1)}, s16[264,256]{1,0:T(8,128)(2,1)S(1)}, u32[]{:S(2)}, u32[]{:S(2)}) collective-permute-start(s16[264,256]{1,0:T(8,128)(2,1)S(1)} %sent_terms.5), channel_id=1, source_target_pairs={{0,3},{1,2},{2,1},{3,0},{4,7},{5,6},{6,5},{7,4},{8,11},{9,10},{10,... | collective-permute-start | bytes 405512 | tf_op jit(solution)/shard_map/ppermute | solution.py:442
  13.0 1.7 %copy-start.1 = (bf16[512,256]{1,0:T(8,128)(2,1)S(1)}, bf16[512,256]{1,0:T(8,128)(2,1)}, u32[]{:S(2)}) copy-start(bf16[512,256]{1,0:T(8,128)(2,1)} %so.1) | copy-start | bytes 786436
  13.1 6.6 %collective-permute-start.3 = (s16[264,256]{1,0:T(8,128)(2,1)S(1)}, s16[264,256]{1,0:T(8,128)(2,1)S(1)}, u32[]{:S(2)}, u32[]{:S(2)}) collective-permute-start(s16[264,256]{1,0:T(8,128)(2,1)S(1)} %sent_terms.4), channel_id=1, source_target_pairs={{0,2},{1,3},{2,0},{3,1},{4,6},{5,7},{6,4},{7,5},{8,10},{9,11},{10,... | collective-permute-start | bytes 405512 | tf_op jit(solution)/shard_map/ppermute | solution.py:442
  14.6 10.6 %copy-start.4 = (s32[16,16,8]{1,2,0:T(8,128)S(1)}, s32[16,16,8]{1,2,0:T(8,128)}, u32[]{:S(2)}) copy-start(s32[16,16,8]{1,2,0:T(8,128)} %param.19) | copy-start | bytes 24580
  14.6 10.6 %copy-start.5 = (bf16[64,256]{1,0:T(8,128)(2,1)S(1)}, bf16[64,256]{1,0:T(8,128)(2,1)}, u32[]{:S(2)}) copy-start(bf16[64,256]{1,0:T(8,128)(2,1)} %adj.1) | copy-start | bytes 98308
  14.6 10.6 %copy-start.6 = (s32[16,16]{1,0:T(8,128)S(1)}, s32[16,16]{1,0:T(8,128)}, u32[]{:S(2)}) copy-start(s32[16,16]{1,0:T(8,128)} %counts.1) | copy-start | bytes 3076
  14.6 5.3 %collective-permute-start.2 = (s16[264,256]{1,0:T(8,128)(2,1)S(1)}, s16[264,256]{1,0:T(8,128)(2,1)S(1)}, u32[]{:S(2)}, u32[]{:S(2)}) collective-permute-start(s16[264,256]{1,0:T(8,128)(2,1)S(1)} %sent_terms.3), channel_id=1, source_target_pairs={{0,1},{1,0},{2,3},{3,2},{4,5},{5,4},{6,7},{7,6},{8,9},{9,8},{10,11... | collective-permute-start | bytes 405512 | tf_op jit(solution)/shard_map/ppermute | solution.py:442
  15.8 24.4 %copy-start.2 = (bf16[256,172]{0,1:T(8,128)(2,1)S(1)}, bf16[256,172]{0,1:T(8,128)(2,1)}, u32[]{:S(2)}) copy-start(bf16[256,172]{0,1:T(8,128)(2,1)} %param.22) | copy-start | bytes 264196
  15.8 24.4 %copy-start.3 = (bf16[256,172]{0,1:T(8,128)(2,1)S(1)}, bf16[256,172]{0,1:T(8,128)(2,1)}, u32[]{:S(2)}) copy-start(bf16[256,172]{0,1:T(8,128)(2,1)} %param.23) | copy-start | bytes 264196
  15.9 10.0 %collective-permute-start.5 = (f32[64,256]{1,0:T(8,128)S(1)}, f32[64,256]{1,0:T(8,128)S(1)}, u32[]{:S(2)}, u32[]{:S(2)}) collective-permute-start(f32[64,256]{1,0:T(8,128)S(1)} %get-tuple-element.30), channel_id=1, source_target_pairs={{0,16},{16,0},{1,17},{17,1},{2,18},{18,2},{3,19},{19,3},{4,20},{20... | collective-permute-start | bytes 196616 | tf_op jit(solution)/shard_map/ppermute | solution.py:483
  20.1 5.8 %collective-permute-start.6 = (s16[72,256]{1,0:T(8,128)(2,1)S(1)}, s16[72,256]{1,0:T(8,128)(2,1)S(1)}, u32[]{:S(2)}, u32[]{:S(2)}) collective-permute-start(s16[72,256]{1,0:T(8,128)(2,1)S(1)} %get-tuple-element.31), channel_id=1, source_target_pairs={{0,8},{1,9},{2,10},{3,11},{4,12},{5,13},{6,14},{7,15},{8,0},{9,1},... | collective-permute-start | bytes 110600 | tf_op jit(solution)/shard_map/ppermute | solution.py:442
  23.3 5.8 %collective-permute-start.7 = (s16[72,256]{1,0:T(8,128)(2,1)S(1)}, s16[72,256]{1,0:T(8,128)(2,1)S(1)}, u32[]{:S(2)}, u32[]{:S(2)}) collective-permute-start(s16[72,256]{1,0:T(8,128)(2,1)S(1)} %get-tuple-element.32), channel_id=1, source_target_pairs={{0,12},{1,13},{2,14},{3,15},{4,8},{5,9},{6,10},{7,11},{8,4},{9,5},... | collective-permute-start | bytes 110600 | tf_op jit(solution)/shard_map/ppermute | solution.py:442
  24.7 4.4 %collective-permute-start.8 = (s16[72,256]{1,0:T(8,128)(2,1)S(1)}, s16[72,256]{1,0:T(8,128)(2,1)S(1)}, u32[]{:S(2)}, u32[]{:S(2)}) collective-permute-start(s16[72,256]{1,0:T(8,128)(2,1)S(1)} %get-tuple-element.33), channel_id=1, source_target_pairs={{0,4},{1,5},{2,6},{3,7},{4,0},{5,1},{6,2},{7,3},{8,12},{9,13},{10,... | collective-permute-start | bytes 110600 | tf_op jit(solution)/shard_map/ppermute | solution.py:442
  29.1 1.3 %collective-permute-start.9 = (bf16[64,256]{1,0:T(8,128)(2,1)S(1)}, bf16[64,256]{1,0:T(8,128)(2,1)S(1)}, u32[]{:S(2)}, u32[]{:S(2)}) collective-permute-start(bf16[64,256]{1,0:T(8,128)(2,1)S(1)} %hidden_rows.1.own), channel_id=1, source_target_pairs={{0,16},{16,0},{1,17},{17,1},{2,18},{18,2},{3,19},{19,3},{4,20},{20... | collective-permute-start | bytes 98312 | tf_op jit(solution)/shard_map/ppermute | solution.py:494

commit v20 on v19

--- a/solution.py
+++ b/solution.py
@@ -9,7 +9,7 @@
 
 UNIT = 16
 BLOCK = 8
-STEP = 4
+STEP = 8
 PART = 256
 CHUNKS = 1
 
@@ -99,13 +99,14 @@
         hot = jnp.concatenate(hot, axis=1)
         earlier = jnp.dot(hot.astype(jnp.bfloat16), before, preferred_element_type=jnp.float32)
         blocks = jnp.floor((jnp.sum(hot, axis=1, keepdims=True) + (BLOCK - 1)) * (1.0 / BLOCK))
-        run = jnp.zeros((1, 1), jnp.float32)
-        pos = jnp.zeros((1, units), jnp.float32)
-        owner = jnp.zeros((1, n_pos), jnp.float32)
-        for s in range(n_src):
-            pos = pos + hot[s:s + 1, :] * (earlier[s:s + 1, :] + run * BLOCK)
-            run = run + blocks[s:s + 1, :]
-            owner = owner + jnp.where(place_i.astype(jnp.float32) >= run, 1.0, 0.0)
+        ahead = jnp.zeros(blocks.shape, jnp.float32)
+        source_i = lax.broadcasted_iota(jnp.int32, blocks.shape, 0)
+        for s in range(n_src - 1):
+            ahead = ahead + jnp.where(source_i > s, blocks[s:s + 1, :], 0.0)
+        pos = jnp.sum(hot * (earlier + ahead * BLOCK), axis=0, keepdims=True)
+        behind = jnp.where(place_i.astype(jnp.float32) >= ahead + blocks, 1.0, 0.0)
+        owner = jnp.sum(behind, axis=0, keepdims=True)
+        run = ahead[n_src - 1:, :] + blocks[n_src - 1:, :]
         stack = [jnp.where(valid[j], pos[:, j * tiles:(j + 1) * tiles], -1.0) for j in range(per)]
         stack += [w.astype(jnp.float32) - trash for w in words]
         stack += [jnp.zeros((1, tiles), jnp.float32)] * (-len(stack) % 8)
@@ -216,13 +217,13 @@
     columns = [(x, h) for x in (xo, xp) for h in range(0, width, PART)]
     to_scalar.wait()
 
-    def step(i, carry):
-        for m in range(STEP):
-            b = i * STEP + m
-            base = pl.multiple_of(table[1, b] * tile, tile)
+    def blocks(first, count):
+        for m in range(count):
+            at = first + m
+            base = pl.multiple_of(table[1, at] * tile, tile)
             rows, places = [], []
             for k in range(BLOCK):
-                word = table[0, b * BLOCK + k]
+                word = table[0, at * BLOCK + k]
                 u = jnp.bitwise_and(lax.shift_right_logical(word, 5), 511)
                 rows.append(tbuf[u] * masks[jnp.bitwise_and(word, 31)])
                 places.append(pl.multiple_of(lax.shift_right_logical(word, 14) * UNIT, UNIT))
@@ -232,10 +233,21 @@
                 got = got.astype(jnp.bfloat16).astype(jnp.float32)
                 for k in range(BLOCK):
                     acc[pl.ds(places[k], UNIT), :] += got[k * UNIT:(k + 1) * UNIT, :]
+
+    half = STEP // 2
+    halves = lax.div(table[1, table.shape[1] - 1] + half - 1, half)
+    steps = lax.div(halves, 2)
+
+    def step(i, carry):
+        blocks(i * STEP, STEP)
         return carry
 
-    steps = lax.div(table[1, table.shape[1] - 1] + STEP - 1, STEP)
+    def last(i, carry):
+        blocks(steps * STEP, half)
+        return carry
+
     lax.fori_loop(0, steps, step, 0)
+    lax.fori_loop(0, lax.rem(halves, 2), last, 0)
 
 
 def gathered_sums(per, n, table, tbuf, xo, xp):

time: 41.6 us -> 40.6 us (0.976)
  starting transfers between devices: 10.4 us -> 9.78 us
    ppermute x6, starting transfers between devices: 9.74 us -> 9.13 us  [exchange(): lax.ppermute(parts[k], 'dom', [(i, i ^ k * stride) for i in range(n)])]
  transfers between devices with their start and end apart: 10 -> 10, of which waited for: 5 -> 6; matrix products, arithmetic and copies ran while one was open for 0% -> 0% of each run, Pallas kernels for 26% -> 26%
where the time goes in v20:
time: 40.6 us; the launch traced here: 40.5 us
  Pallas kernels  12.3 us (30%)
  starting transfers between devices  9.78 us (24%)
  blocking collectives  9.67 us (24%)
  waiting for transfers between devices  8.46 us (21%)
    all_to_all x1, blocking collectives, body(): lax.all_to_all(send, 'dom', 0, 0, axis_index_groups=[group_order(n)], til...  9.67 us
    ppermute x6, starting transfers between devices, exchange(): lax.ppermute(parts[k], 'dom', [(i, i ^ k * stride) for i in range(n)])  9.13 us
    ppermute x6, waiting for transfers between devices, exchange(): lax.ppermute(parts[k], 'dom', [(i, i ^ k * stride) for i in range(n)])  7.26 us
    pallas_call x1, Pallas kernels, gathered_sums(): pl.pallas_call(tiles_kernel, out_shape=[sums] * parts, in_specs=[vmem] *...  5.08 us
    pallas_call x1, Pallas kernels, plan(): pl.pallas_call(functools.partial(plan_kernel, chunks, per, n, radix, n_sr...  2.55 us
    pallas_call x3, Pallas kernels, sent_terms(): pl.pallas_call(functools.partial(sent_kernel, k, slots, rows, len(accs)),...  1.54 us
    ppermute x1, waiting for transfers between devices, body(): other = lax.ppermute(own, 'feat', swap)  1.19 us
    pallas_call x1, Pallas kernels, own_terms(): pl.pallas_call(functools.partial(own_kernel, chunk, per, groups, len(accs...  1.04 us
  transfers between devices with their start and end apart: 10, of which 6 were waited for; matrix products, arithmetic and copies ran while one was open for 0% of the time, Pallas kernels for 26%

profile of v20, /device:TPU:0, one launch (start us, length us, event | category | flops | bytes accessed | tf_op | source)
XLA Modules:
  0.0 40.5 jit_solution(7662522051232558060)
XLA Ops:
  0.0 0.5 %collective-permute-start.1 = (bf16[1024,512]{1,0:T(8,128)(2,1)}, bf16[1024,512]{1,0:T(8,128)(2,1)S(1)}, u32[]{:S(2)}, u32[]{:S(2)}) collective-permute-start(bf16[1024,512]{1,0:T(8,128)(2,1)} %xo.1), channel_id=1, source_target_pairs={{0,16},{16,0},{1,17},{17,1},{2,18},{18,2},{3,19},{19,3},{4,20},{20... | collective-permute-start | bytes 3145736 | tf_op jit(solution)/shard_map/ppermute | solution.py:481
  0.5 0.1 collective-permute-start
  0.5 0.1 pad_add_fusion.ids
  0.6 2.5 %plan.1 = (s32[2,640]{1,0:T(2,128)S(1)}, bf16[512,16,128]{2,1,0:T(8,128)(2,1)S(1)}, bf16[1024,512]{1,0:T(8,128)(2,1)S(1)}) custom-call(s32[2]{0:T(128)S(1)} %pad_add_fusion.ids, s32[1,128]{1,0:T(1,128)} %bitcast.17, s32[1,128]{1,0:T(1,128)} %bitcast.18, s32[1,128]{1,0:T(1,128)} %bitcast.19, bf16[128,8,16,128]{3,2,1,0:T(8,128)(2,1)} %bitcast.16, ...), custom_call_target="tpu_custom_call" | custom-call | tf_op jit(solution)/shard_map/plan/pallas_call | solution.py:135
  3.1 0.0 collective-permute-done.1.xp
  3.2 0.0 copy-start
  3.2 5.1 %gathered_sums.1 = (f32[1040,256]{1,0:T(8,128)S(1)}, f32[1040,256]{1,0:T(8,128)S(1)}, f32[1040,256]{1,0:T(8,128)S(1)}, f32[1040,256]{1,0:T(8,128)S(1)}) custom-call(s32[2,640]{1,0:T(2,128)S(1)} %get-tuple-element.22.table_v, bf16[512,16,128]{2,1,0:T(8,128)(2,1)S(1)} %get-tuple-element.23.tbuf, bf16[1024,512]{1,0:T(8,128)(2,1)S(1)} %get-tuple-element.21.xo, ...), custom_call_target="tpu_custom_call" | custom-call | flops 2147483648 | bytes 8388608 | tf_op jit(solution)/shard_map/gathered_sums/pallas_call | solution.py:260
  8.3 0.0 collective-permute-done.wp
  8.3 0.0 copy-done
  8.3 0.5 %sent_terms.5 = s16[264,256]{1,0:T(8,128)(2,1)S(1)} custom-call(bf16[512,256]{1,0:T(8,128)(2,1)S(1)} %copy-done, bf16[512,256]{1,0:T(8,128)(2,1)S(1)} %collective-permute-done.wp, f32[1040,256]{1,0:T(8,128)S(1)} %get-tuple-element.24.refs_0_, f32[1040,256]{1,0:T(8,128)S(1)} %get-tuple-element.25.refs_1_, f32[1040,256]{1,0:T(8,128)S(1)} %get-tuple-element.26.refs_2_, ...), custom_call_target="tpu_custom_call" | custom-call | flops 268435456 | bytes 2097152 | tf_op jit(solution)/shard_map/sent_terms/pallas_call | solution.py:304
  8.8 4.0 %collective-permute-start.4 = (s16[264,256]{1,0:T(8,128)(2,1)S(1)}, s16[264,256]{1,0:T(8,128)(2,1)S(1)}, u32[]{:S(2)}, u32[]{:S(2)}) collective-permute-start(s16[264,256]{1,0:T(8,128)(2,1)S(1)} %sent_terms.5), channel_id=1, source_target_pairs={{0,3},{1,2},{2,1},{3,0},{4,7},{5,6},{6,5},{7,4},{8,11},{9,10},{10,... | collective-permute-start | bytes 405512 | tf_op jit(solution)/shard_map/ppermute | solution.py:454
  12.8 0.5 %sent_terms.4 = s16[264,256]{1,0:T(8,128)(2,1)S(1)} custom-call(bf16[512,256]{1,0:T(8,128)(2,1)S(1)} %copy-done, bf16[512,256]{1,0:T(8,128)(2,1)S(1)} %collective-permute-done.wp, f32[1040,256]{1,0:T(8,128)S(1)} %get-tuple-element.24.refs_0_, f32[1040,256]{1,0:T(8,128)S(1)} %get-tuple-element.25.refs_1_, f32[1040,256]{1,0:T(8,128)S(1)} %get-tuple-element.26.refs_2_, ...), custom_call_target="tpu_custom_call" | custom-call | flops 268435456 | bytes 2097152 | tf_op jit(solution)/shard_map/sent_terms/pallas_call | solution.py:304
  13.3 0.0 copy-start.1
  13.3 0.1 collective-permute-start.3
  13.4 0.5 %sent_terms.3 = s16[264,256]{1,0:T(8,128)(2,1)S(1)} custom-call(bf16[512,256]{1,0:T(8,128)(2,1)S(1)} %copy-done, bf16[512,256]{1,0:T(8,128)(2,1)S(1)} %collective-permute-done.wp, f32[1040,256]{1,0:T(8,128)S(1)} %get-tuple-element.24.refs_0_, f32[1040,256]{1,0:T(8,128)S(1)} %get-tuple-element.25.refs_1_, f32[1040,256]{1,0:T(8,128)S(1)} %get-tuple-element.26.refs_2_, ...), custom_call_target="tpu_custom_call" | custom-call | flops 268435456 | bytes 2097152 | tf_op jit(solution)/shard_map/sent_terms/pallas_call | solution.py:304
  13.9 0.0 copy-start.4
  13.9 0.0 copy-start.5
  13.9 0.0 copy-start.6
  13.9 0.6 %collective-permute-start.2 = (s16[264,256]{1,0:T(8,128)(2,1)S(1)}, s16[264,256]{1,0:T(8,128)(2,1)S(1)}, u32[]{:S(2)}, u32[]{:S(2)}) collective-permute-start(s16[264,256]{1,0:T(8,128)(2,1)S(1)} %sent_terms.3), channel_id=1, source_target_pairs={{0,1},{1,0},{2,3},{3,2},{4,5},{5,4},{6,7},{7,6},{8,9},{9,8},{10,11... | collective-permute-start | bytes 405512 | tf_op jit(solution)/shard_map/ppermute | solution.py:454
  14.6 0.0 copy-done.1
  14.6 1.0 %own_terms.1 = (f32[256,256]{1,0:T(8,128)S(1)}, f32[64,256]{1,0:T(8,128)S(1)}) custom-call(s32[2]{0:T(128)S(1)} %pad_add_fusion.ids, bf16[512,256]{1,0:T(8,128)(2,1)S(1)} %copy-done, bf16[512,256]{1,0:T(8,128)(2,1)S(1)} %collective-permute-done.wp, bf16[1024,512]{1,0:T(8,128)(2,1)S(1)} %get-tuple-element.21.xo, bf16[512,256]{1,0:T(8,128)(2,1)S(1)} %copy-done.1, ...), custom_call_target="tpu_custom_call" | custom-call | flops 268435456 | bytes 2097152 | tf_op jit(solution)/shard_map/own_terms/pallas_call | solution.py:337
  15.6 0.0 copy-start.2
  15.6 0.0 copy-start.3
  15.6 0.1 collective-permute-start.5
  15.7 1.0 %collective-permute-done.4.refs_2_ = s16[264,256]{1,0:T(8,128)(2,1)S(1)} collective-permute-done((s16[264,256]{1,0:T(8,128)(2,1)S(1)}, s16[264,256]{1,0:T(8,128)(2,1)S(1)}, u32[]{:S(2)}, u32[]{:S(2)}) %collective-permute-start.4) | collective-permute-done | bytes 135200 | tf_op jit(solution)/shard_map/ppermute | solution.py:454
  16.7 2.2 %collective-permute-done.3.refs_1_ = s16[264,256]{1,0:T(8,128)(2,1)S(1)} collective-permute-done((s16[264,256]{1,0:T(8,128)(2,1)S(1)}, s16[264,256]{1,0:T(8,128)(2,1)S(1)}, u32[]{:S(2)}, u32[]{:S(2)}) %collective-permute-start.3) | collective-permute-done | bytes 135200 | tf_op jit(solution)/shard_map/ppermute | solution.py:454
  18.9 0.3 collective-permute-done.2.refs_0_
  19.3 0.2 combine.1
  19.5 3.2 %collective-permute-start.6 = (s16[72,256]{1,0:T(8,128)(2,1)S(1)}, s16[72,256]{1,0:T(8,128)(2,1)S(1)}, u32[]{:S(2)}, u32[]{:S(2)}) collective-permute-start(s16[72,256]{1,0:T(8,128)(2,1)S(1)} %get-tuple-element.31), channel_id=1, source_target_pairs={{0,8},{1,9},{2,10},{3,11},{4,12},{5,13},{6,14},{7,15},{8,0},{9,1},... | collective-permute-start | bytes 110600 | tf_op jit(solution)/shard_map/ppermute | solution.py:454
  22.6 1.3 %collective-permute-start.7 = (s16[72,256]{1,0:T(8,128)(2,1)S(1)}, s16[72,256]{1,0:T(8,128)(2,1)S(1)}, u32[]{:S(2)}, u32[]{:S(2)}) collective-permute-start(s16[72,256]{1,0:T(8,128)(2,1)S(1)} %get-tuple-element.32), channel_id=1, source_target_pairs={{0,12},{1,13},{2,14},{3,15},{4,8},{5,9},{6,10},{7,11},{8,4},{9,5},... | collective-permute-start | bytes 110600 | tf_op jit(solution)/shard_map/ppermute | solution.py:454
  23.9 0.0 collective-permute-start.8
  23.9 0.0 copy-done.4
  23.9 0.0 copy-done.5
  23.9 0.0 copy-done.6
  23.9 0.7 %selection.1 = (bf16[128,128]{1,0:T(8,128)(2,1)S(1)}, bf16[128,128]{1,0:T(8,128)(2,1)S(1)}, bf16[64,128]{1,0:T(8,128)(2,1)S(1)}) custom-call(s32[2]{0:T(128)S(1)} %pad_add_fusion.ids, s32[16,8,16]{2,1,0:T(8,128)S(1)} %bitcast.15, s32[16,16]{1,0:T(8,128)S(1)} %copy-done.6, bf16[64,256]{1,0:T(8,128)(2,1)S(1)} %copy-done.5), custom_call_target="tpu_custom_call" | custom-call | tf_op jit(solution)/shard_map/selection/pallas_call | solution.py:191
  24.6 0.0 collective-permute-done.5.refs_1_
  24.7 0.3 collective-permute-done.6.refs_2_
  25.0 3.4 %collective-permute-done.7.refs_3_ = s16[72,256]{1,0:T(8,128)(2,1)S(1)} collective-permute-done((s16[72,256]{1,0:T(8,128)(2,1)S(1)}, s16[72,256]{1,0:T(8,128)(2,1)S(1)}, u32[]{:S(2)}, u32[]{:S(2)}) %collective-permute-start.7) | collective-permute-done | bytes 36896 | tf_op jit(solution)/shard_map/ppermute | solution.py:454
  28.4 0.0 collective-permute-done.8.refs_4_
  28.4 0.1 collective-permute-start.9
  28.5 1.2 %collective-permute-done.9.other = bf16[64,256]{1,0:T(8,128)(2,1)S(1)} collective-permute-done((bf16[64,256]{1,0:T(8,128)(2,1)S(1)}, bf16[64,256]{1,0:T(8,128)(2,1)S(1)}, u32[]{:S(2)}, u32[]{:S(2)}) %collective-permute-start.9) | collective-permute-done | bytes 32800 | tf_op jit(solution)/shard_map/ppermute | solution.py:506
  29.7 0.1 rows_to_send.1
  29.9 9.7 %all_to_all.11 = bf16[16,8,256]{2,1,0:T(8,128)(2,1)S(1)} all-to-all(bf16[16,8,256]{2,1,0:T(8,128)(2,1)S(1)} %bitcast.11), channel_id=1, replica_groups={{15,14,13,12,11,10,9,8,7,6,5,4,3,2,1,0},{31,30,29,28,27,26,25,24,23,22,..., dimensions={0} | all-to-all | bytes 131072 | tf_op jit(solution)/shard_map/all_to_all | solution.py:508
  39.5 0.0 copy-done.2
  39.5 0.0 copy-done.3
  39.5 1.0 %logits.1 = f32[64,172]{1,0:T(8,128)} custom-call(bf16[64,256]{1,0:T(8,128)(2,1)S(1)} %hidden_rows.1.own, bf16[64,256]{1,0:T(8,128)(2,1)S(1)} %collective-permute-done.9.other, bf16[128,256]{1,0:T(8,128)(2,1)S(1)} %bitcast.12, bf16[128,128]{1,0:T(8,128)(2,1)S(1)} %get-tuple-element.35.front, bf16[64,128]{1,0:T(8,128)(2,1)S(1)} %get-tuple-element.36.adj_received, ...), custom_call_target="tpu_custom_call" | custom-call | tf_op jit(solution)/shard_map/logits/pallas_call | solution.py:441
  (1 shorter events, 0.0 us)
Async XLA Ops:
  0.0 3.1 %collective-permute-start.1 = (bf16[1024,512]{1,0:T(8,128)(2,1)}, bf16[1024,512]{1,0:T(8,128)(2,1)S(1)}, u32[]{:S(2)}, u32[]{:S(2)}) collective-permute-start(bf16[1024,512]{1,0:T(8,128)(2,1)} %xo.1), channel_id=1, source_target_pairs={{0,16},{16,0},{1,17},{17,1},{2,18},{18,2},{3,19},{19,3},{4,20},{20... | collective-permute-start | bytes 3145736 | tf_op jit(solution)/shard_map/ppermute | solution.py:481
  0.5 7.8 %collective-permute-start = (bf16[512,256]{1,0:T(8,128)(2,1)}, bf16[512,256]{1,0:T(8,128)(2,1)S(1)}, u32[]{:S(2)}, u32[]{:S(2)}) collective-permute-start(bf16[512,256]{1,0:T(8,128)(2,1)} %wo.7), channel_id=1, source_target_pairs={{0,16},{16,0},{1,17},{17,1},{2,18},{18,2},{3,19},{19,3},{4,20},{20... | collective-permute-start | bytes 786440 | tf_op jit(solution)/shard_map/ppermute | solution.py:482
  3.2 5.1 %copy-start = (bf16[512,256]{1,0:T(8,128)(2,1)S(1)}, bf16[512,256]{1,0:T(8,128)(2,1)}, u32[]{:S(2)}) copy-start(bf16[512,256]{1,0:T(8,128)(2,1)} %wo.7) | copy-start | bytes 786436
  8.8 7.9 %collective-permute-start.4 = (s16[264,256]{1,0:T(8,128)(2,1)S(1)}, s16[264,256]{1,0:T(8,128)(2,1)S(1)}, u32[]{:S(2)}, u32[]{:S(2)}) collective-permute-start(s16[264,256]{1,0:T(8,128)(2,1)S(1)} %sent_terms.5), channel_id=1, source_target_pairs={{0,3},{1,2},{2,1},{3,0},{4,7},{5,6},{6,5},{7,4},{8,11},{9,10},{10,... | collective-permute-start | bytes 405512 | tf_op jit(solution)/shard_map/ppermute | solution.py:454
  13.3 1.3 %copy-start.1 = (bf16[512,256]{1,0:T(8,128)(2,1)S(1)}, bf16[512,256]{1,0:T(8,128)(2,1)}, u32[]{:S(2)}) copy-start(bf16[512,256]{1,0:T(8,128)(2,1)} %so.1) | copy-start | bytes 786436
  13.3 5.6 %collective-permute-start.3 = (s16[264,256]{1,0:T(8,128)(2,1)S(1)}, s16[264,256]{1,0:T(8,128)(2,1)S(1)}, u32[]{:S(2)}, u32[]{:S(2)}) collective-permute-start(s16[264,256]{1,0:T(8,128)(2,1)S(1)} %sent_terms.4), channel_id=1, source_target_pairs={{0,2},{1,3},{2,0},{3,1},{4,6},{5,7},{6,4},{7,5},{8,10},{9,11},{10,... | collective-permute-start | bytes 405512 | tf_op jit(solution)/shard_map/ppermute | solution.py:454
  13.9 10.0 %copy-start.4 = (s32[16,16,8]{1,2,0:T(8,128)S(1)}, s32[16,16,8]{1,2,0:T(8,128)}, u32[]{:S(2)}) copy-start(s32[16,16,8]{1,2,0:T(8,128)} %param.19) | copy-start | bytes 24580
  13.9 10.0 %copy-start.5 = (bf16[64,256]{1,0:T(8,128)(2,1)S(1)}, bf16[64,256]{1,0:T(8,128)(2,1)}, u32[]{:S(2)}) copy-start(bf16[64,256]{1,0:T(8,128)(2,1)} %adj.1) | copy-start | bytes 98308
  13.9 10.0 %copy-start.6 = (s32[16,16]{1,0:T(8,128)S(1)}, s32[16,16]{1,0:T(8,128)}, u32[]{:S(2)}) copy-start(s32[16,16]{1,0:T(8,128)} %counts.1) | copy-start | bytes 3076
  13.9 5.3 %collective-permute-start.2 = (s16[264,256]{1,0:T(8,128)(2,1)S(1)}, s16[264,256]{1,0:T(8,128)(2,1)S(1)}, u32[]{:S(2)}, u32[]{:S(2)}) collective-permute-start(s16[264,256]{1,0:T(8,128)(2,1)S(1)} %sent_terms.3), channel_id=1, source_target_pairs={{0,1},{1,0},{2,3},{3,2},{4,5},{5,4},{6,7},{7,6},{8,9},{9,8},{10,11... | collective-permute-start | bytes 405512 | tf_op jit(solution)/shard_map/ppermute | solution.py:454
  15.6 23.9 %copy-start.2 = (bf16[256,172]{0,1:T(8,128)(2,1)S(1)}, bf16[256,172]{0,1:T(8,128)(2,1)}, u32[]{:S(2)}) copy-start(bf16[256,172]{0,1:T(8,128)(2,1)} %param.22) | copy-start | bytes 264196
  15.6 23.9 %copy-start.3 = (bf16[256,172]{0,1:T(8,128)(2,1)S(1)}, bf16[256,172]{0,1:T(8,128)(2,1)}, u32[]{:S(2)}) copy-start(bf16[256,172]{0,1:T(8,128)(2,1)} %param.23) | copy-start | bytes 264196
  15.6 9.0 %collective-permute-start.5 = (f32[64,256]{1,0:T(8,128)S(1)}, f32[64,256]{1,0:T(8,128)S(1)}, u32[]{:S(2)}, u32[]{:S(2)}) collective-permute-start(f32[64,256]{1,0:T(8,128)S(1)} %get-tuple-element.30), channel_id=1, source_target_pairs={{0,16},{16,0},{1,17},{17,1},{2,18},{18,2},{3,19},{19,3},{4,20},{20... | collective-permute-start | bytes 196616 | tf_op jit(solution)/shard_map/ppermute | solution.py:495
  19.5 5.5 %collective-permute-start.6 = (s16[72,256]{1,0:T(8,128)(2,1)S(1)}, s16[72,256]{1,0:T(8,128)(2,1)S(1)}, u32[]{:S(2)}, u32[]{:S(2)}) collective-permute-start(s16[72,256]{1,0:T(8,128)(2,1)S(1)} %get-tuple-element.31), channel_id=1, source_target_pairs={{0,8},{1,9},{2,10},{3,11},{4,12},{5,13},{6,14},{7,15},{8,0},{9,1},... | collective-permute-start | bytes 110600 | tf_op jit(solution)/shard_map/ppermute | solution.py:454
  22.6 5.8 %collective-permute-start.7 = (s16[72,256]{1,0:T(8,128)(2,1)S(1)}, s16[72,256]{1,0:T(8,128)(2,1)S(1)}, u32[]{:S(2)}, u32[]{:S(2)}) collective-permute-start(s16[72,256]{1,0:T(8,128)(2,1)S(1)} %get-tuple-element.32), channel_id=1, source_target_pairs={{0,12},{1,13},{2,14},{3,15},{4,8},{5,9},{6,10},{7,11},{8,4},{9,5},... | collective-permute-start | bytes 110600 | tf_op jit(solution)/shard_map/ppermute | solution.py:454
  23.9 4.5 %collective-permute-start.8 = (s16[72,256]{1,0:T(8,128)(2,1)S(1)}, s16[72,256]{1,0:T(8,128)(2,1)S(1)}, u32[]{:S(2)}, u32[]{:S(2)}) collective-permute-start(s16[72,256]{1,0:T(8,128)(2,1)S(1)} %get-tuple-element.33), channel_id=1, source_target_pairs={{0,4},{1,5},{2,6},{3,7},{4,0},{5,1},{6,2},{7,3},{8,12},{9,13},{10,... | collective-permute-start | bytes 110600 | tf_op jit(solution)/shard_map/ppermute | solution.py:454
  28.4 1.3 %collective-permute-start.9 = (bf16[64,256]{1,0:T(8,128)(2,1)S(1)}, bf16[64,256]{1,0:T(8,128)(2,1)S(1)}, u32[]{:S(2)}, u32[]{:S(2)}) collective-permute-start(bf16[64,256]{1,0:T(8,128)(2,1)S(1)} %hidden_rows.1.own), channel_id=1, source_target_pairs={{0,16},{16,0},{1,17},{17,1},{2,18},{18,2},{3,19},{19,3},{4,20},{20... | collective-permute-start | bytes 98312 | tf_op jit(solution)/shard_map/ppermute | solution.py:506

commit v21 on v20

--- a/solution.py
+++ b/solution.py
@@ -276,8 +276,7 @@
 def weigh(accs, weights, first, count, out):
     size = min(256, count)
 
-    def piece(r, carry):
-        at = pl.multiple_of(r * size, size)
+    def piece(at):
         got = jnp.zeros((size, out.shape[1]), jnp.float32)
         for i, acc in enumerate(accs):
             w, h = weights[i * PART // weights[0].shape[0]], i * PART % weights[0].shape[0]
@@ -287,32 +286,37 @@
             got = got + jnp.dot(high, w[h:h + PART, :], preferred_element_type=jnp.float32)
             got = got + jnp.dot(low, w[h:h + PART, :], preferred_element_type=jnp.float32)
         out[pl.ds(at, size), :] = got
-        return carry
-
-    lax.fori_loop(0, count // size, piece, 0)
-
-
-def sent_kernel(k, slots, rows, parts, wo, wp, *refs):
-    accs, (out, sums, tail) = refs[:parts], refs[parts:]
-    weigh(accs, (wo, wp), k * slots * rows, slots * rows, sums)
-    write_coded(out, tail, slots, rows, lambda s: sums[s * rows:(s + 1) * rows, :])
-
-
-def sent_terms(k, slots, rows, accs, wo, wp):
+
+    if count == size:
+        piece(0)
+    else:
+        lax.fori_loop(0, count // size, lambda r, carry: (piece(pl.multiple_of(r * size, size)), carry)[1], 0)
+
+
+def sent_kernel(slots, rows, ways, parts, wo, wp, *refs):
+    accs, outs, scratch = refs[:parts], refs[parts:parts + ways - 1], refs[parts + ways - 1:]
+    for k in range(ways - 1, 0, -1):
+        sums, tail = scratch[2 * k - 2:2 * k]
+        weigh(accs, (wo, wp), k * slots * rows, slots * rows, sums)
+        write_coded(outs[k - 1], tail, slots, rows, lambda s: sums[s * rows:(s + 1) * rows, :])
+
+
+def sent_terms(ways, slots, rows, accs, wo, wp):
     hidden = wo.shape[1]
     vmem = pl.BlockSpec(memory_space=pltpu.VMEM)
-    return pl.pallas_call(
-        functools.partial(sent_kernel, k, slots, rows, len(accs)),
-        out_shape=jax.ShapeDtypeStruct((slots * rows + tail_rows(slots), hidden), jnp.int16),
+    coded = jax.ShapeDtypeStruct((slots * rows + tail_rows(slots), hidden), jnp.int16)
+    return pl.pallas_call(
+        functools.partial(sent_kernel, slots, rows, ways, len(accs)),
+        out_shape=[coded] * (ways - 1),
         in_specs=[vmem] * (2 + len(accs)),
-        out_specs=vmem,
+        out_specs=[vmem] * (ways - 1),
         scratch_shapes=[
             pltpu.VMEM((slots * rows, hidden), jnp.float32),
             pltpu.VMEM((tail_rows(slots), hidden), jnp.float32),
-        ],
-        compiler_params=pltpu.CompilerParams(vmem_limit_bytes=(12 << 20) + accs[0].size * 4 * len(accs)),
+        ] * (ways - 1),
+        compiler_params=pltpu.CompilerParams(vmem_limit_bytes=(20 << 20) + accs[0].size * 4 * len(accs)),
         cost_estimate=pl.CostEstimate(
-            flops=4 * slots * rows * PART * len(accs) * hidden, bytes_accessed=2 << 20, transcendentals=0),
+            flops=4 * (ways - 1) * slots * rows * PART * len(accs) * hidden, bytes_accessed=6 << 20, transcendentals=0),
         name="sent_terms",
     )(wo, wp, *accs)
 
@@ -490,10 +494,10 @@
     for chunk in range(CHUNKS):
         accs = gathered_sums(per, n, tables[chunk], tbufs[chunk], xo, xp)
         slots, rows = n // 4, per * UNIT
-        parts = {k: sent_terms(k, slots, rows, accs, wo, wp) for k in (1, 2, 3)}
+        parts = dict(enumerate(sent_terms(4, slots, rows, accs, wo, wp), 1))
         parts[0], theirs = own_terms(chunk, per, groups, slots, ids, accs, wo, wp, xo, so)
         self = lax.ppermute(theirs, "feat", swap)
-        got = exchange(parts, 1, n, (1, 2, 3))
+        got = exchange(parts, 1, n, (3, 2, 1))
         stride = 4
         for radix in radices[1:]:
             ways = 1 << radix

time: 40.6 us -> 41.1 us (1.012)
  Pallas kernels: 12.3 us -> 11.5 us
  waiting for transfers between devices: 8.46 us -> 9.24 us
  starting transfers between devices: 9.78 us -> 10.2 us
    ppermute x6, waiting for transfers between devices: 7.26 us -> 8.03 us  [exchange(): lax.ppermute(parts[k], 'dom', [(i, i ^ k * stride) for i in range(n)])]
    pallas_call x3 -> x1, Pallas kernels: 1.54 us -> 1.13 us  [sent_terms(): pl.pallas_call(functools.partial(sent_kernel, slots, rows, ways, len(accs...]
  transfers between devices with their start and end apart: 10 -> 10, of which waited for: 6 -> 6; matrix products, arithmetic and copies ran while one was open for 0% -> 0% of each run, Pallas kernels for 26% -> 22%
where the time goes in v21:
time: 41.1 us; the launch traced here: 41 us
  Pallas kernels  11.5 us (28%)
  starting transfers between devices  10.2 us (25%)
  blocking collectives  9.86 us (24%)
  waiting for transfers between devices  9.24 us (22%)
    all_to_all x1, blocking collectives, body(): lax.all_to_all(send, 'dom', 0, 0, axis_index_groups=[group_order(n)], til...  9.86 us
    ppermute x6, starting transfers between devices, exchange(): lax.ppermute(parts[k], 'dom', [(i, i ^ k * stride) for i in range(n)])  9.5 us
    ppermute x6, waiting for transfers between devices, exchange(): lax.ppermute(parts[k], 'dom', [(i, i ^ k * stride) for i in range(n)])  8.03 us
    pallas_call x1, Pallas kernels, gathered_sums(): pl.pallas_call(tiles_kernel, out_shape=[sums] * parts, in_specs=[vmem] *...  4.69 us
    pallas_call x1, Pallas kernels, plan(): pl.pallas_call(functools.partial(plan_kernel, chunks, per, n, radix, n_sr...  2.55 us
    ppermute x1, waiting for transfers between devices, body(): other = lax.ppermute(own, 'feat', swap)  1.19 us
    pallas_call x1, Pallas kernels, sent_terms(): pl.pallas_call(functools.partial(sent_kernel, slots, rows, ways, len(accs...  1.13 us
    pallas_call x1, Pallas kernels, own_terms(): pl.pallas_call(functools.partial(own_kernel, chunk, per, groups, len(accs...  1.04 us
  transfers between devices with their start and end apart: 10, of which 6 were waited for; matrix products, arithmetic and copies ran while one was open for 0% of the time, Pallas kernels for 22%

profile of v21, /device:TPU:0, one launch (start us, length us, event | category | flops | bytes accessed | tf_op | source)
XLA Modules:
  0.0 41.0 jit_solution(13672626377561651149)
XLA Ops:
  0.0 0.5 %collective-permute-start.1 = (bf16[1024,512]{1,0:T(8,128)(2,1)}, bf16[1024,512]{1,0:T(8,128)(2,1)S(1)}, u32[]{:S(2)}, u32[]{:S(2)}) collective-permute-start(bf16[1024,512]{1,0:T(8,128)(2,1)} %xo.1), channel_id=1, source_target_pairs={{0,16},{16,0},{1,17},{17,1},{2,18},{18,2},{3,19},{19,3},{4,20},{20... | collective-permute-start | bytes 3145736 | tf_op jit(solution)/shard_map/ppermute | solution.py:485
  0.5 0.1 collective-permute-start
  0.5 0.1 pad_add_fusion.ids
  0.6 2.5 %plan.1 = (s32[2,640]{1,0:T(2,128)S(1)}, bf16[512,16,128]{2,1,0:T(8,128)(2,1)S(1)}, bf16[1024,512]{1,0:T(8,128)(2,1)S(1)}) custom-call(s32[2]{0:T(128)S(1)} %pad_add_fusion.ids, s32[1,128]{1,0:T(1,128)} %bitcast.17, s32[1,128]{1,0:T(1,128)} %bitcast.18, s32[1,128]{1,0:T(1,128)} %bitcast.19, bf16[128,8,16,128]{3,2,1,0:T(8,128)(2,1)} %bitcast.16, ...), custom_call_target="tpu_custom_call" | custom-call | tf_op jit(solution)/shard_map/plan/pallas_call | solution.py:135
  3.1 0.0 collective-permute-done.1.xp
  3.2 0.0 copy-start
  3.2 4.7 %gathered_sums.1 = (f32[1040,256]{1,0:T(8,128)S(1)}, f32[1040,256]{1,0:T(8,128)S(1)}, f32[1040,256]{1,0:T(8,128)S(1)}, f32[1040,256]{1,0:T(8,128)S(1)}) custom-call(s32[2,640]{1,0:T(2,128)S(1)} %get-tuple-element.25.table_v, bf16[512,16,128]{2,1,0:T(8,128)(2,1)S(1)} %get-tuple-element.26.tbuf, bf16[1024,512]{1,0:T(8,128)(2,1)S(1)} %get-tuple-element.24.xo, ...), custom_call_target="tpu_custom_call" | custom-call | flops 2147483648 | bytes 8388608 | tf_op jit(solution)/shard_map/gathered_sums/pallas_call | solution.py:260
  7.9 0.0 collective-permute-done.wp
  7.9 0.0 copy-done
  7.9 0.0 copy-start.1
  7.9 1.1 %sent_terms.1 = (s16[264,256]{1,0:T(8,128)(2,1)S(1)}, s16[264,256]{1,0:T(8,128)(2,1)S(1)}, s16[264,256]{1,0:T(8,128)(2,1)S(1)}) custom-call(bf16[512,256]{1,0:T(8,128)(2,1)S(1)} %copy-done, bf16[512,256]{1,0:T(8,128)(2,1)S(1)} %collective-permute-done.wp, f32[1040,256]{1,0:T(8,128)S(1)} %get-tuple-element.27.refs_0_, ...), custom_call_target="tpu_custom_call" | custom-call | flops 805306368 | bytes 6291456 | tf_op jit(solution)/shard_map/sent_terms/pallas_call | solution.py:308
  9.0 3.9 %collective-permute-start.2 = (s16[264,256]{1,0:T(8,128)(2,1)S(1)}, s16[264,256]{1,0:T(8,128)(2,1)S(1)}, u32[]{:S(2)}, u32[]{:S(2)}) collective-permute-start(s16[264,256]{1,0:T(8,128)(2,1)S(1)} %get-tuple-element.32), channel_id=1, source_target_pairs={{0,3},{1,2},{2,1},{3,0},{4,7},{5,6},{6,5},{7,4},{8,11},{9,10},{10,... | collective-permute-start | bytes 405512 | tf_op jit(solution)/shard_map/ppermute | solution.py:458
  12.9 1.0 %collective-permute-start.3 = (s16[264,256]{1,0:T(8,128)(2,1)S(1)}, s16[264,256]{1,0:T(8,128)(2,1)S(1)}, u32[]{:S(2)}, u32[]{:S(2)}) collective-permute-start(s16[264,256]{1,0:T(8,128)(2,1)S(1)} %get-tuple-element.33), channel_id=1, source_target_pairs={{0,2},{1,3},{2,0},{3,1},{4,6},{5,7},{6,4},{7,5},{8,10},{9,11},{10,... | collective-permute-start | bytes 405512 | tf_op jit(solution)/shard_map/ppermute | solution.py:458
  13.9 0.0 copy-start.4
  13.9 0.0 copy-start.5
  13.9 0.0 copy-start.6
  13.9 0.0 collective-permute-start.4
  13.9 0.0 copy-done.1
  14.0 1.0 %own_terms.1 = (f32[256,256]{1,0:T(8,128)S(1)}, f32[64,256]{1,0:T(8,128)S(1)}) custom-call(s32[2]{0:T(128)S(1)} %pad_add_fusion.ids, bf16[512,256]{1,0:T(8,128)(2,1)S(1)} %copy-done, bf16[512,256]{1,0:T(8,128)(2,1)S(1)} %collective-permute-done.wp, bf16[1024,512]{1,0:T(8,128)(2,1)S(1)} %get-tuple-element.24.xo, bf16[512,256]{1,0:T(8,128)(2,1)S(1)} %copy-done.1, ...), custom_call_target="tpu_custom_call" | custom-call | flops 268435456 | bytes 2097152 | tf_op jit(solution)/shard_map/own_terms/pallas_call | solution.py:341
  15.0 0.0 copy-start.2
  15.0 0.0 copy-start.3
  15.0 0.1 collective-permute-start.5
  15.1 1.9 %collective-permute-done.2.refs_0_ = s16[264,256]{1,0:T(8,128)(2,1)S(1)} collective-permute-done((s16[264,256]{1,0:T(8,128)(2,1)S(1)}, s16[264,256]{1,0:T(8,128)(2,1)S(1)}, u32[]{:S(2)}, u32[]{:S(2)}) %collective-permute-start.2) | collective-permute-done | bytes 135200 | tf_op jit(solution)/shard_map/ppermute | solution.py:458
  17.0 2.3 %collective-permute-done.3.refs_1_ = s16[264,256]{1,0:T(8,128)(2,1)S(1)} collective-permute-done((s16[264,256]{1,0:T(8,128)(2,1)S(1)}, s16[264,256]{1,0:T(8,128)(2,1)S(1)}, u32[]{:S(2)}, u32[]{:S(2)}) %collective-permute-start.3) | collective-permute-done | bytes 135200 | tf_op jit(solution)/shard_map/ppermute | solution.py:458
  19.2 0.3 collective-permute-done.4.refs_2_
  19.5 0.2 combine.1
  19.7 3.0 %collective-permute-start.6 = (s16[72,256]{1,0:T(8,128)(2,1)S(1)}, s16[72,256]{1,0:T(8,128)(2,1)S(1)}, u32[]{:S(2)}, u32[]{:S(2)}) collective-permute-start(s16[72,256]{1,0:T(8,128)(2,1)S(1)} %get-tuple-element.37), channel_id=1, source_target_pairs={{0,8},{1,9},{2,10},{3,11},{4,12},{5,13},{6,14},{7,15},{8,0},{9,1},... | collective-permute-start | bytes 110600 | tf_op jit(solution)/shard_map/ppermute | solution.py:458
  22.7 1.6 %collective-permute-start.7 = (s16[72,256]{1,0:T(8,128)(2,1)S(1)}, s16[72,256]{1,0:T(8,128)(2,1)S(1)}, u32[]{:S(2)}, u32[]{:S(2)}) collective-permute-start(s16[72,256]{1,0:T(8,128)(2,1)S(1)} %get-tuple-element.38), channel_id=1, source_target_pairs={{0,12},{1,13},{2,14},{3,15},{4,8},{5,9},{6,10},{7,11},{8,4},{9,5},... | collective-permute-start | bytes 110600 | tf_op jit(solution)/shard_map/ppermute | solution.py:458
  24.3 0.0 collective-permute-start.8
  24.3 0.0 copy-done.4
  24.3 0.0 copy-done.5
  24.4 0.0 copy-done.6
  24.4 0.7 %selection.1 = (bf16[128,128]{1,0:T(8,128)(2,1)S(1)}, bf16[128,128]{1,0:T(8,128)(2,1)S(1)}, bf16[64,128]{1,0:T(8,128)(2,1)S(1)}) custom-call(s32[2]{0:T(128)S(1)} %pad_add_fusion.ids, s32[16,8,16]{2,1,0:T(8,128)S(1)} %bitcast.15, s32[16,16]{1,0:T(8,128)S(1)} %copy-done.6, bf16[64,256]{1,0:T(8,128)(2,1)S(1)} %copy-done.5), custom_call_target="tpu_custom_call" | custom-call | tf_op jit(solution)/shard_map/selection/pallas_call | solution.py:191
  25.1 0.0 collective-permute-done.5.refs_1_
  25.1 0.0 collective-permute-done.6.refs_2_
  25.1 3.5 %collective-permute-done.7.refs_3_ = s16[72,256]{1,0:T(8,128)(2,1)S(1)} collective-permute-done((s16[72,256]{1,0:T(8,128)(2,1)S(1)}, s16[72,256]{1,0:T(8,128)(2,1)S(1)}, u32[]{:S(2)}, u32[]{:S(2)}) %collective-permute-start.7) | collective-permute-done | bytes 36896 | tf_op jit(solution)/shard_map/ppermute | solution.py:458
  28.6 0.1 collective-permute-done.8.refs_4_
  28.7 0.1 collective-permute-start.9
  28.8 1.2 %collective-permute-done.9.other = bf16[64,256]{1,0:T(8,128)(2,1)S(1)} collective-permute-done((bf16[64,256]{1,0:T(8,128)(2,1)S(1)}, bf16[64,256]{1,0:T(8,128)(2,1)S(1)}, u32[]{:S(2)}, u32[]{:S(2)}) %collective-permute-start.9) | collective-permute-done | bytes 32800 | tf_op jit(solution)/shard_map/ppermute | solution.py:510
  30.0 0.1 rows_to_send.1
  30.2 9.9 %all_to_all.11 = bf16[16,8,256]{2,1,0:T(8,128)(2,1)S(1)} all-to-all(bf16[16,8,256]{2,1,0:T(8,128)(2,1)S(1)} %bitcast.11), channel_id=1, replica_groups={{15,14,13,12,11,10,9,8,7,6,5,4,3,2,1,0},{31,30,29,28,27,26,25,24,23,22,..., dimensions={0} | all-to-all | bytes 131072 | tf_op jit(solution)/shard_map/all_to_all | solution.py:512
  40.0 0.0 copy-done.2
  40.0 0.0 copy-done.3
  40.0 1.0 %logits.1 = f32[64,172]{1,0:T(8,128)} custom-call(bf16[64,256]{1,0:T(8,128)(2,1)S(1)} %hidden_rows.1.own, bf16[64,256]{1,0:T(8,128)(2,1)S(1)} %collective-permute-done.9.other, bf16[128,256]{1,0:T(8,128)(2,1)S(1)} %bitcast.12, bf16[128,128]{1,0:T(8,128)(2,1)S(1)} %get-tuple-element.41.front, bf16[64,128]{1,0:T(8,128)(2,1)S(1)} %get-tuple-element.42.adj_received, ...), custom_call_target="tpu_custom_call" | custom-call | tf_op jit(solution)/shard_map/logits/pallas_call | solution.py:445
  (1 shorter events, 0.0 us)
Async XLA Ops:
  0.0 3.1 %collective-permute-start.1 = (bf16[1024,512]{1,0:T(8,128)(2,1)}, bf16[1024,512]{1,0:T(8,128)(2,1)S(1)}, u32[]{:S(2)}, u32[]{:S(2)}) collective-permute-start(bf16[1024,512]{1,0:T(8,128)(2,1)} %xo.1), channel_id=1, source_target_pairs={{0,16},{16,0},{1,17},{17,1},{2,18},{18,2},{3,19},{19,3},{4,20},{20... | collective-permute-start | bytes 3145736 | tf_op jit(solution)/shard_map/ppermute | solution.py:485
  0.5 7.4 %collective-permute-start = (bf16[512,256]{1,0:T(8,128)(2,1)}, bf16[512,256]{1,0:T(8,128)(2,1)S(1)}, u32[]{:S(2)}, u32[]{:S(2)}) collective-permute-start(bf16[512,256]{1,0:T(8,128)(2,1)} %wo.3), channel_id=1, source_target_pairs={{0,16},{16,0},{1,17},{17,1},{2,18},{18,2},{3,19},{19,3},{4,20},{20... | collective-permute-start | bytes 786440 | tf_op jit(solution)/shard_map/ppermute | solution.py:486
  3.2 4.7 %copy-start = (bf16[512,256]{1,0:T(8,128)(2,1)S(1)}, bf16[512,256]{1,0:T(8,128)(2,1)}, u32[]{:S(2)}) copy-start(bf16[512,256]{1,0:T(8,128)(2,1)} %wo.3) | copy-start | bytes 786436
  7.9 6.1 %copy-start.1 = (bf16[512,256]{1,0:T(8,128)(2,1)S(1)}, bf16[512,256]{1,0:T(8,128)(2,1)}, u32[]{:S(2)}) copy-start(bf16[512,256]{1,0:T(8,128)(2,1)} %so.1) | copy-start | bytes 786436
  9.0 7.9 %collective-permute-start.2 = (s16[264,256]{1,0:T(8,128)(2,1)S(1)}, s16[264,256]{1,0:T(8,128)(2,1)S(1)}, u32[]{:S(2)}, u32[]{:S(2)}) collective-permute-start(s16[264,256]{1,0:T(8,128)(2,1)S(1)} %get-tuple-element.32), channel_id=1, source_target_pairs={{0,3},{1,2},{2,1},{3,0},{4,7},{5,6},{6,5},{7,4},{8,11},{9,10},{10,... | collective-permute-start | bytes 405512 | tf_op jit(solution)/shard_map/ppermute | solution.py:458
  12.9 6.3 %collective-permute-start.3 = (s16[264,256]{1,0:T(8,128)(2,1)S(1)}, s16[264,256]{1,0:T(8,128)(2,1)S(1)}, u32[]{:S(2)}, u32[]{:S(2)}) collective-permute-start(s16[264,256]{1,0:T(8,128)(2,1)S(1)} %get-tuple-element.33), channel_id=1, source_target_pairs={{0,2},{1,3},{2,0},{3,1},{4,6},{5,7},{6,4},{7,5},{8,10},{9,11},{10,... | collective-permute-start | bytes 405512 | tf_op jit(solution)/shard_map/ppermute | solution.py:458
  13.9 10.4 %copy-start.4 = (s32[16,16,8]{1,2,0:T(8,128)S(1)}, s32[16,16,8]{1,2,0:T(8,128)}, u32[]{:S(2)}) copy-start(s32[16,16,8]{1,2,0:T(8,128)} %param.19) | copy-start | bytes 24580
  13.9 10.4 %copy-start.5 = (bf16[64,256]{1,0:T(8,128)(2,1)S(1)}, bf16[64,256]{1,0:T(8,128)(2,1)}, u32[]{:S(2)}) copy-start(bf16[64,256]{1,0:T(8,128)(2,1)} %adj.1) | copy-start | bytes 98308
  13.9 10.4 %copy-start.6 = (s32[16,16]{1,0:T(8,128)S(1)}, s32[16,16]{1,0:T(8,128)}, u32[]{:S(2)}) copy-start(s32[16,16]{1,0:T(8,128)} %counts.1) | copy-start | bytes 3076
  13.9 5.6 %collective-permute-start.4 = (s16[264,256]{1,0:T(8,128)(2,1)S(1)}, s16[264,256]{1,0:T(8,128)(2,1)S(1)}, u32[]{:S(2)}, u32[]{:S(2)}) collective-permute-start(s16[264,256]{1,0:T(8,128)(2,1)S(1)} %get-tuple-element.34), channel_id=1, source_target_pairs={{0,1},{1,0},{2,3},{3,2},{4,5},{5,4},{6,7},{7,6},{8,9},{9,8},{10,11... | collective-permute-start | bytes 405512 | tf_op jit(solution)/shard_map/ppermute | solution.py:458
  15.0 25.0 %copy-start.2 = (bf16[256,172]{0,1:T(8,128)(2,1)S(1)}, bf16[256,172]{0,1:T(8,128)(2,1)}, u32[]{:S(2)}) copy-start(bf16[256,172]{0,1:T(8,128)(2,1)} %param.22) | copy-start | bytes 264196
  15.0 25.0 %copy-start.3 = (bf16[256,172]{0,1:T(8,128)(2,1)S(1)}, bf16[256,172]{0,1:T(8,128)(2,1)}, u32[]{:S(2)}) copy-start(bf16[256,172]{0,1:T(8,128)(2,1)} %param.23) | copy-start | bytes 264196
  15.0 10.0 %collective-permute-start.5 = (f32[64,256]{1,0:T(8,128)S(1)}, f32[64,256]{1,0:T(8,128)S(1)}, u32[]{:S(2)}, u32[]{:S(2)}) collective-permute-start(f32[64,256]{1,0:T(8,128)S(1)} %get-tuple-element.36), channel_id=1, source_target_pairs={{0,16},{16,0},{1,17},{17,1},{2,18},{18,2},{3,19},{19,3},{4,20},{20... | collective-permute-start | bytes 196616 | tf_op jit(solution)/shard_map/ppermute | solution.py:499
  19.7 5.3 %collective-permute-start.6 = (s16[72,256]{1,0:T(8,128)(2,1)S(1)}, s16[72,256]{1,0:T(8,128)(2,1)S(1)}, u32[]{:S(2)}, u32[]{:S(2)}) collective-permute-start(s16[72,256]{1,0:T(8,128)(2,1)S(1)} %get-tuple-element.37), channel_id=1, source_target_pairs={{0,8},{1,9},{2,10},{3,11},{4,12},{5,13},{6,14},{7,15},{8,0},{9,1},... | collective-permute-start | bytes 110600 | tf_op jit(solution)/shard_map/ppermute | solution.py:458
  22.7 5.9 %collective-permute-start.7 = (s16[72,256]{1,0:T(8,128)(2,1)S(1)}, s16[72,256]{1,0:T(8,128)(2,1)S(1)}, u32[]{:S(2)}, u32[]{:S(2)}) collective-permute-start(s16[72,256]{1,0:T(8,128)(2,1)S(1)} %get-tuple-element.38), channel_id=1, source_target_pairs={{0,12},{1,13},{2,14},{3,15},{4,8},{5,9},{6,10},{7,11},{8,4},{9,5},... | collective-permute-start | bytes 110600 | tf_op jit(solution)/shard_map/ppermute | solution.py:458
  24.3 4.4 %collective-permute-start.8 = (s16[72,256]{1,0:T(8,128)(2,1)S(1)}, s16[72,256]{1,0:T(8,128)(2,1)S(1)}, u32[]{:S(2)}, u32[]{:S(2)}) collective-permute-start(s16[72,256]{1,0:T(8,128)(2,1)S(1)} %get-tuple-element.39), channel_id=1, source_target_pairs={{0,4},{1,5},{2,6},{3,7},{4,0},{5,1},{6,2},{7,3},{8,12},{9,13},{10,... | collective-permute-start | bytes 110600 | tf_op jit(solution)/shard_map/ppermute | solution.py:458
  28.7 1.3 %collective-permute-start.9 = (bf16[64,256]{1,0:T(8,128)(2,1)S(1)}, bf16[64,256]{1,0:T(8,128)(2,1)S(1)}, u32[]{:S(2)}, u32[]{:S(2)}) collective-permute-start(bf16[64,256]{1,0:T(8,128)(2,1)S(1)} %hidden_rows.1.own), channel_id=1, source_target_pairs={{0,16},{16,0},{1,17},{17,1},{2,18},{18,2},{3,19},{19,3},{4,20},{20... | collective-permute-start | bytes 98312 | tf_op jit(solution)/shard_map/ppermute | solution.py:510

commit v22 on v20

--- a/solution.py
+++ b/solution.py
@@ -15,8 +15,7 @@
 
 
 def group_of(core, place, groups):
-    pair = 2 * (place // 2) + core
-    return pair if place % 2 == 0 else groups - 1 - pair
+    return 2 * place + 1 - core
 
 
 def group_order(n):

time: 40.6 us -> 40.9 us (level)
  Pallas kernels: 12.3 us -> 11.8 us
  waiting for transfers between devices: 8.46 us -> 8.96 us
    ppermute x6, waiting for transfers between devices: 7.26 us -> 7.76 us  [exchange(): lax.ppermute(parts[k], 'dom', [(i, i ^ k * stride) for i in range(n)])]
    pallas_call x1, Pallas kernels: 5.08 us -> 4.63 us  [gathered_sums(): pl.pallas_call(tiles_kernel, out_shape=[sums] * parts, in_specs=[vmem] *...]
  transfers between devices with their start and end apart: 10 -> 10, of which waited for: 6 -> 5; matrix products, arithmetic and copies ran while one was open for 0% -> 0% of each run, Pallas kernels for 26% -> 25%
where the time goes in v22:
time: 40.9 us; the launch traced here: 40.8 us
  Pallas kernels  11.8 us (29%)
  starting transfers between devices  10.1 us (25%)
  blocking collectives  9.69 us (24%)
  waiting for transfers between devices  8.96 us (22%)
    all_to_all x1, blocking collectives, body(): lax.all_to_all(send, 'dom', 0, 0, axis_index_groups=[group_order(n)], til...  9.69 us
    ppermute x6, starting transfers between devices, exchange(): lax.ppermute(parts[k], 'dom', [(i, i ^ k * stride) for i in range(n)])  9.23 us
    ppermute x6, waiting for transfers between devices, exchange(): lax.ppermute(parts[k], 'dom', [(i, i ^ k * stride) for i in range(n)])  7.76 us
    pallas_call x1, Pallas kernels, gathered_sums(): pl.pallas_call(tiles_kernel, out_shape=[sums] * parts, in_specs=[vmem] *...  4.63 us
    pallas_call x1, Pallas kernels, plan(): pl.pallas_call(functools.partial(plan_kernel, chunks, per, n, radix, n_sr...  2.55 us
    pallas_call x3, Pallas kernels, sent_terms(): pl.pallas_call(functools.partial(sent_kernel, k, slots, rows, len(accs)),...  1.54 us
    ppermute x1, waiting for transfers between devices, body(): other = lax.ppermute(own, 'feat', swap)  1.19 us
    pallas_call x1, Pallas kernels, own_terms(): pl.pallas_call(functools.partial(own_kernel, chunk, per, groups, len(accs...  1.04 us
  transfers between devices with their start and end apart: 10, of which 5 were waited for; matrix products, arithmetic and copies ran while one was open for 0% of the time, Pallas kernels for 25%

profile of v22, /device:TPU:0, one launch (start us, length us, event | category | flops | bytes accessed | tf_op | source)
XLA Modules:
  0.0 40.8 jit_solution(11711576790344158063)
XLA Ops:
  0.0 0.5 %collective-permute-start.1 = (bf16[1024,512]{1,0:T(8,128)(2,1)}, bf16[1024,512]{1,0:T(8,128)(2,1)S(1)}, u32[]{:S(2)}, u32[]{:S(2)}) collective-permute-start(bf16[1024,512]{1,0:T(8,128)(2,1)} %xo.1), channel_id=1, source_target_pairs={{0,16},{16,0},{1,17},{17,1},{2,18},{18,2},{3,19},{19,3},{4,20},{20... | collective-permute-start | bytes 3145736 | tf_op jit(solution)/shard_map/ppermute | solution.py:480
  0.5 0.1 collective-permute-start
  0.5 0.1 pad_add_fusion.ids
  0.6 2.5 %plan.1 = (s32[2,640]{1,0:T(2,128)S(1)}, bf16[512,16,128]{2,1,0:T(8,128)(2,1)S(1)}, bf16[1024,512]{1,0:T(8,128)(2,1)S(1)}) custom-call(s32[2]{0:T(128)S(1)} %pad_add_fusion.ids, s32[1,128]{1,0:T(1,128)} %bitcast.17, s32[1,128]{1,0:T(1,128)} %bitcast.18, s32[1,128]{1,0:T(1,128)} %bitcast.19, bf16[128,8,16,128]{3,2,1,0:T(8,128)(2,1)} %bitcast.16, ...), custom_call_target="tpu_custom_call" | custom-call | tf_op jit(solution)/shard_map/plan/pallas_call | solution.py:134
  3.1 0.0 collective-permute-done.1.xp
  3.2 0.0 copy-start
  3.2 4.6 %gathered_sums.1 = (f32[1040,256]{1,0:T(8,128)S(1)}, f32[1040,256]{1,0:T(8,128)S(1)}, f32[1040,256]{1,0:T(8,128)S(1)}, f32[1040,256]{1,0:T(8,128)S(1)}) custom-call(s32[2,640]{1,0:T(2,128)S(1)} %get-tuple-element.22.table_v, bf16[512,16,128]{2,1,0:T(8,128)(2,1)S(1)} %get-tuple-element.23.tbuf, bf16[1024,512]{1,0:T(8,128)(2,1)S(1)} %get-tuple-element.21.xo, ...), custom_call_target="tpu_custom_call" | custom-call | flops 2147483648 | bytes 8388608 | tf_op jit(solution)/shard_map/gathered_sums/pallas_call | solution.py:259
  7.8 0.0 collective-permute-done.wp
  7.8 0.0 copy-done
  7.8 0.5 %sent_terms.5 = s16[264,256]{1,0:T(8,128)(2,1)S(1)} custom-call(bf16[512,256]{1,0:T(8,128)(2,1)S(1)} %copy-done, bf16[512,256]{1,0:T(8,128)(2,1)S(1)} %collective-permute-done.wp, f32[1040,256]{1,0:T(8,128)S(1)} %get-tuple-element.24.refs_0_, f32[1040,256]{1,0:T(8,128)S(1)} %get-tuple-element.25.refs_1_, f32[1040,256]{1,0:T(8,128)S(1)} %get-tuple-element.26.refs_2_, ...), custom_call_target="tpu_custom_call" | custom-call | flops 268435456 | bytes 2097152 | tf_op jit(solution)/shard_map/sent_terms/pallas_call | solution.py:303
  8.3 3.6 %collective-permute-start.4 = (s16[264,256]{1,0:T(8,128)(2,1)S(1)}, s16[264,256]{1,0:T(8,128)(2,1)S(1)}, u32[]{:S(2)}, u32[]{:S(2)}) collective-permute-start(s16[264,256]{1,0:T(8,128)(2,1)S(1)} %sent_terms.5), channel_id=1, source_target_pairs={{0,3},{1,2},{2,1},{3,0},{4,7},{5,6},{6,5},{7,4},{8,11},{9,10},{10,... | collective-permute-start | bytes 405512 | tf_op jit(solution)/shard_map/ppermute | solution.py:453
  12.0 0.5 %sent_terms.4 = s16[264,256]{1,0:T(8,128)(2,1)S(1)} custom-call(bf16[512,256]{1,0:T(8,128)(2,1)S(1)} %copy-done, bf16[512,256]{1,0:T(8,128)(2,1)S(1)} %collective-permute-done.wp, f32[1040,256]{1,0:T(8,128)S(1)} %get-tuple-element.24.refs_0_, f32[1040,256]{1,0:T(8,128)S(1)} %get-tuple-element.25.refs_1_, f32[1040,256]{1,0:T(8,128)S(1)} %get-tuple-element.26.refs_2_, ...), custom_call_target="tpu_custom_call" | custom-call | flops 268435456 | bytes 2097152 | tf_op jit(solution)/shard_map/sent_terms/pallas_call | solution.py:303
  12.5 0.0 copy-start.1
  12.5 0.5 %collective-permute-start.3 = (s16[264,256]{1,0:T(8,128)(2,1)S(1)}, s16[264,256]{1,0:T(8,128)(2,1)S(1)}, u32[]{:S(2)}, u32[]{:S(2)}) collective-permute-start(s16[264,256]{1,0:T(8,128)(2,1)S(1)} %sent_terms.4), channel_id=1, source_target_pairs={{0,2},{1,3},{2,0},{3,1},{4,6},{5,7},{6,4},{7,5},{8,10},{9,11},{10,... | collective-permute-start | bytes 405512 | tf_op jit(solution)/shard_map/ppermute | solution.py:453
  13.1 0.5 %sent_terms.3 = s16[264,256]{1,0:T(8,128)(2,1)S(1)} custom-call(bf16[512,256]{1,0:T(8,128)(2,1)S(1)} %copy-done, bf16[512,256]{1,0:T(8,128)(2,1)S(1)} %collective-permute-done.wp, f32[1040,256]{1,0:T(8,128)S(1)} %get-tuple-element.24.refs_0_, f32[1040,256]{1,0:T(8,128)S(1)} %get-tuple-element.25.refs_1_, f32[1040,256]{1,0:T(8,128)S(1)} %get-tuple-element.26.refs_2_, ...), custom_call_target="tpu_custom_call" | custom-call | flops 268435456 | bytes 2097152 | tf_op jit(solution)/shard_map/sent_terms/pallas_call | solution.py:303
  13.6 0.0 copy-start.4
  13.6 0.0 copy-start.5
  13.6 0.0 copy-start.6
  13.6 0.2 collective-permute-start.2
  13.8 0.0 copy-done.1
  13.8 1.0 %own_terms.1 = (f32[256,256]{1,0:T(8,128)S(1)}, f32[64,256]{1,0:T(8,128)S(1)}) custom-call(s32[2]{0:T(128)S(1)} %pad_add_fusion.ids, bf16[512,256]{1,0:T(8,128)(2,1)S(1)} %copy-done, bf16[512,256]{1,0:T(8,128)(2,1)S(1)} %collective-permute-done.wp, bf16[1024,512]{1,0:T(8,128)(2,1)S(1)} %get-tuple-element.21.xo, bf16[512,256]{1,0:T(8,128)(2,1)S(1)} %copy-done.1, ...), custom_call_target="tpu_custom_call" | custom-call | flops 268435456 | bytes 2097152 | tf_op jit(solution)/shard_map/own_terms/pallas_call | solution.py:336
  14.8 0.0 copy-start.2
  14.8 0.0 copy-start.3
  14.9 0.3 collective-permute-start.5
  15.1 1.3 %collective-permute-done.4.refs_2_ = s16[264,256]{1,0:T(8,128)(2,1)S(1)} collective-permute-done((s16[264,256]{1,0:T(8,128)(2,1)S(1)}, s16[264,256]{1,0:T(8,128)(2,1)S(1)}, u32[]{:S(2)}, u32[]{:S(2)}) %collective-permute-start.4) | collective-permute-done | bytes 135200 | tf_op jit(solution)/shard_map/ppermute | solution.py:453
  16.4 2.9 %collective-permute-done.3.refs_1_ = s16[264,256]{1,0:T(8,128)(2,1)S(1)} collective-permute-done((s16[264,256]{1,0:T(8,128)(2,1)S(1)}, s16[264,256]{1,0:T(8,128)(2,1)S(1)}, u32[]{:S(2)}, u32[]{:S(2)}) %collective-permute-start.3) | collective-permute-done | bytes 135200 | tf_op jit(solution)/shard_map/ppermute | solution.py:453
  19.3 0.1 collective-permute-done.2.refs_0_
  19.4 0.2 combine.1
  19.6 3.3 %collective-permute-start.6 = (s16[72,256]{1,0:T(8,128)(2,1)S(1)}, s16[72,256]{1,0:T(8,128)(2,1)S(1)}, u32[]{:S(2)}, u32[]{:S(2)}) collective-permute-start(s16[72,256]{1,0:T(8,128)(2,1)S(1)} %get-tuple-element.31), channel_id=1, source_target_pairs={{0,8},{1,9},{2,10},{3,11},{4,12},{5,13},{6,14},{7,15},{8,0},{9,1},... | collective-permute-start | bytes 110600 | tf_op jit(solution)/shard_map/ppermute | solution.py:453
  22.9 1.1 %collective-permute-start.7 = (s16[72,256]{1,0:T(8,128)(2,1)S(1)}, s16[72,256]{1,0:T(8,128)(2,1)S(1)}, u32[]{:S(2)}, u32[]{:S(2)}) collective-permute-start(s16[72,256]{1,0:T(8,128)(2,1)S(1)} %get-tuple-element.32), channel_id=1, source_target_pairs={{0,12},{1,13},{2,14},{3,15},{4,8},{5,9},{6,10},{7,11},{8,4},{9,5},... | collective-permute-start | bytes 110600 | tf_op jit(solution)/shard_map/ppermute | solution.py:453
  24.0 0.5 %collective-permute-start.8 = (s16[72,256]{1,0:T(8,128)(2,1)S(1)}, s16[72,256]{1,0:T(8,128)(2,1)S(1)}, u32[]{:S(2)}, u32[]{:S(2)}) collective-permute-start(s16[72,256]{1,0:T(8,128)(2,1)S(1)} %get-tuple-element.33), channel_id=1, source_target_pairs={{0,4},{1,5},{2,6},{3,7},{4,0},{5,1},{6,2},{7,3},{8,12},{9,13},{10,... | collective-permute-start | bytes 110600 | tf_op jit(solution)/shard_map/ppermute | solution.py:453
  24.5 0.0 copy-done.4
  24.5 0.0 copy-done.5
  24.5 0.0 copy-done.6
  24.5 0.7 %selection.1 = (bf16[128,128]{1,0:T(8,128)(2,1)S(1)}, bf16[128,128]{1,0:T(8,128)(2,1)S(1)}, bf16[64,128]{1,0:T(8,128)(2,1)S(1)}) custom-call(s32[2]{0:T(128)S(1)} %pad_add_fusion.ids, s32[16,8,16]{2,1,0:T(8,128)S(1)} %bitcast.15, s32[16,16]{1,0:T(8,128)S(1)} %copy-done.6, bf16[64,256]{1,0:T(8,128)(2,1)S(1)} %copy-done.5), custom_call_target="tpu_custom_call" | custom-call | tf_op jit(solution)/shard_map/selection/pallas_call | solution.py:190
  25.2 0.0 collective-permute-done.5.refs_1_
  25.2 0.0 collective-permute-done.6.refs_2_
  25.3 3.4 %collective-permute-done.7.refs_3_ = s16[72,256]{1,0:T(8,128)(2,1)S(1)} collective-permute-done((s16[72,256]{1,0:T(8,128)(2,1)S(1)}, s16[72,256]{1,0:T(8,128)(2,1)S(1)}, u32[]{:S(2)}, u32[]{:S(2)}) %collective-permute-start.7) | collective-permute-done | bytes 36896 | tf_op jit(solution)/shard_map/ppermute | solution.py:453
  28.7 0.0 collective-permute-done.8.refs_4_
  28.7 0.1 collective-permute-start.9
  28.8 1.2 %collective-permute-done.9.other = bf16[64,256]{1,0:T(8,128)(2,1)S(1)} collective-permute-done((bf16[64,256]{1,0:T(8,128)(2,1)S(1)}, bf16[64,256]{1,0:T(8,128)(2,1)S(1)}, u32[]{:S(2)}, u32[]{:S(2)}) %collective-permute-start.9) | collective-permute-done | bytes 32800 | tf_op jit(solution)/shard_map/ppermute | solution.py:505
  30.0 0.1 rows_to_send.1
  30.1 9.7 %all_to_all.11 = bf16[16,8,256]{2,1,0:T(8,128)(2,1)S(1)} all-to-all(bf16[16,8,256]{2,1,0:T(8,128)(2,1)S(1)} %bitcast.11), channel_id=1, replica_groups={{15,14,13,12,11,10,9,8,7,6,5,4,3,2,1,0},{31,30,29,28,27,26,25,24,23,22,..., dimensions={0} | all-to-all | bytes 131072 | tf_op jit(solution)/shard_map/all_to_all | solution.py:507
  39.8 0.0 copy-done.2
  39.8 0.0 copy-done.3
  39.8 1.0 %logits.1 = f32[64,172]{1,0:T(8,128)} custom-call(bf16[64,256]{1,0:T(8,128)(2,1)S(1)} %hidden_rows.1.own, bf16[64,256]{1,0:T(8,128)(2,1)S(1)} %collective-permute-done.9.other, bf16[128,256]{1,0:T(8,128)(2,1)S(1)} %bitcast.12, bf16[128,128]{1,0:T(8,128)(2,1)S(1)} %get-tuple-element.35.front, bf16[64,128]{1,0:T(8,128)(2,1)S(1)} %get-tuple-element.36.adj_received, ...), custom_call_target="tpu_custom_call" | custom-call | tf_op jit(solution)/shard_map/logits/pallas_call | solution.py:440
  (1 shorter events, 0.0 us)
Async XLA Ops:
  0.0 3.1 %collective-permute-start.1 = (bf16[1024,512]{1,0:T(8,128)(2,1)}, bf16[1024,512]{1,0:T(8,128)(2,1)S(1)}, u32[]{:S(2)}, u32[]{:S(2)}) collective-permute-start(bf16[1024,512]{1,0:T(8,128)(2,1)} %xo.1), channel_id=1, source_target_pairs={{0,16},{16,0},{1,17},{17,1},{2,18},{18,2},{3,19},{19,3},{4,20},{20... | collective-permute-start | bytes 3145736 | tf_op jit(solution)/shard_map/ppermute | solution.py:480
  0.5 7.4 %collective-permute-start = (bf16[512,256]{1,0:T(8,128)(2,1)}, bf16[512,256]{1,0:T(8,128)(2,1)S(1)}, u32[]{:S(2)}, u32[]{:S(2)}) collective-permute-start(bf16[512,256]{1,0:T(8,128)(2,1)} %wo.7), channel_id=1, source_target_pairs={{0,16},{16,0},{1,17},{17,1},{2,18},{18,2},{3,19},{19,3},{4,20},{20... | collective-permute-start | bytes 786440 | tf_op jit(solution)/shard_map/ppermute | solution.py:481
  3.2 4.7 %copy-start = (bf16[512,256]{1,0:T(8,128)(2,1)S(1)}, bf16[512,256]{1,0:T(8,128)(2,1)}, u32[]{:S(2)}) copy-start(bf16[512,256]{1,0:T(8,128)(2,1)} %wo.7) | copy-start | bytes 786436
  8.3 8.1 %collective-permute-start.4 = (s16[264,256]{1,0:T(8,128)(2,1)S(1)}, s16[264,256]{1,0:T(8,128)(2,1)S(1)}, u32[]{:S(2)}, u32[]{:S(2)}) collective-permute-start(s16[264,256]{1,0:T(8,128)(2,1)S(1)} %sent_terms.5), channel_id=1, source_target_pairs={{0,3},{1,2},{2,1},{3,0},{4,7},{5,6},{6,5},{7,4},{8,11},{9,10},{10,... | collective-permute-start | bytes 405512 | tf_op jit(solution)/shard_map/ppermute | solution.py:453
  12.5 1.3 %copy-start.1 = (bf16[512,256]{1,0:T(8,128)(2,1)S(1)}, bf16[512,256]{1,0:T(8,128)(2,1)}, u32[]{:S(2)}) copy-start(bf16[512,256]{1,0:T(8,128)(2,1)} %so.1) | copy-start | bytes 786436
  12.5 6.8 %collective-permute-start.3 = (s16[264,256]{1,0:T(8,128)(2,1)S(1)}, s16[264,256]{1,0:T(8,128)(2,1)S(1)}, u32[]{:S(2)}, u32[]{:S(2)}) collective-permute-start(s16[264,256]{1,0:T(8,128)(2,1)S(1)} %sent_terms.4), channel_id=1, source_target_pairs={{0,2},{1,3},{2,0},{3,1},{4,6},{5,7},{6,4},{7,5},{8,10},{9,11},{10,... | collective-permute-start | bytes 405512 | tf_op jit(solution)/shard_map/ppermute | solution.py:453
  13.6 11.0 %copy-start.4 = (s32[16,16,8]{1,2,0:T(8,128)S(1)}, s32[16,16,8]{1,2,0:T(8,128)}, u32[]{:S(2)}) copy-start(s32[16,16,8]{1,2,0:T(8,128)} %param.19) | copy-start | bytes 24580
  13.6 10.9 %copy-start.5 = (bf16[64,256]{1,0:T(8,128)(2,1)S(1)}, bf16[64,256]{1,0:T(8,128)(2,1)}, u32[]{:S(2)}) copy-start(bf16[64,256]{1,0:T(8,128)(2,1)} %adj.1) | copy-start | bytes 98308
  13.6 10.9 %copy-start.6 = (s32[16,16]{1,0:T(8,128)S(1)}, s32[16,16]{1,0:T(8,128)}, u32[]{:S(2)}) copy-start(s32[16,16]{1,0:T(8,128)} %counts.1) | copy-start | bytes 3076
  13.6 5.8 %collective-permute-start.2 = (s16[264,256]{1,0:T(8,128)(2,1)S(1)}, s16[264,256]{1,0:T(8,128)(2,1)S(1)}, u32[]{:S(2)}, u32[]{:S(2)}) collective-permute-start(s16[264,256]{1,0:T(8,128)(2,1)S(1)} %sent_terms.3), channel_id=1, source_target_pairs={{0,1},{1,0},{2,3},{3,2},{4,5},{5,4},{6,7},{7,6},{8,9},{9,8},{10,11... | collective-permute-start | bytes 405512 | tf_op jit(solution)/shard_map/ppermute | solution.py:453
  14.8 25.0 %copy-start.2 = (bf16[256,172]{0,1:T(8,128)(2,1)S(1)}, bf16[256,172]{0,1:T(8,128)(2,1)}, u32[]{:S(2)}) copy-start(bf16[256,172]{0,1:T(8,128)(2,1)} %param.22) | copy-start | bytes 264196
  14.8 25.0 %copy-start.3 = (bf16[256,172]{0,1:T(8,128)(2,1)S(1)}, bf16[256,172]{0,1:T(8,128)(2,1)}, u32[]{:S(2)}) copy-start(bf16[256,172]{0,1:T(8,128)(2,1)} %param.23) | copy-start | bytes 264196
  14.9 10.4 %collective-permute-start.5 = (f32[64,256]{1,0:T(8,128)S(1)}, f32[64,256]{1,0:T(8,128)S(1)}, u32[]{:S(2)}, u32[]{:S(2)}) collective-permute-start(f32[64,256]{1,0:T(8,128)S(1)} %get-tuple-element.30), channel_id=1, source_target_pairs={{0,16},{16,0},{1,17},{17,1},{2,18},{18,2},{3,19},{19,3},{4,20},{20... | collective-permute-start | bytes 196616 | tf_op jit(solution)/shard_map/ppermute | solution.py:494
  19.6 5.6 %collective-permute-start.6 = (s16[72,256]{1,0:T(8,128)(2,1)S(1)}, s16[72,256]{1,0:T(8,128)(2,1)S(1)}, u32[]{:S(2)}, u32[]{:S(2)}) collective-permute-start(s16[72,256]{1,0:T(8,128)(2,1)S(1)} %get-tuple-element.31), channel_id=1, source_target_pairs={{0,8},{1,9},{2,10},{3,11},{4,12},{5,13},{6,14},{7,15},{8,0},{9,1},... | collective-permute-start | bytes 110600 | tf_op jit(solution)/shard_map/ppermute | solution.py:453
  22.9 5.8 %collective-permute-start.7 = (s16[72,256]{1,0:T(8,128)(2,1)S(1)}, s16[72,256]{1,0:T(8,128)(2,1)S(1)}, u32[]{:S(2)}, u32[]{:S(2)}) collective-permute-start(s16[72,256]{1,0:T(8,128)(2,1)S(1)} %get-tuple-element.32), channel_id=1, source_target_pairs={{0,12},{1,13},{2,14},{3,15},{4,8},{5,9},{6,10},{7,11},{8,4},{9,5},... | collective-permute-start | bytes 110600 | tf_op jit(solution)/shard_map/ppermute | solution.py:453
  24.0 4.6 %collective-permute-start.8 = (s16[72,256]{1,0:T(8,128)(2,1)S(1)}, s16[72,256]{1,0:T(8,128)(2,1)S(1)}, u32[]{:S(2)}, u32[]{:S(2)}) collective-permute-start(s16[72,256]{1,0:T(8,128)(2,1)S(1)} %get-tuple-element.33), channel_id=1, source_target_pairs={{0,4},{1,5},{2,6},{3,7},{4,0},{5,1},{6,2},{7,3},{8,12},{9,13},{10,... | collective-permute-start | bytes 110600 | tf_op jit(solution)/shard_map/ppermute | solution.py:453
  28.7 1.3 %collective-permute-start.9 = (bf16[64,256]{1,0:T(8,128)(2,1)S(1)}, bf16[64,256]{1,0:T(8,128)(2,1)S(1)}, u32[]{:S(2)}, u32[]{:S(2)}) collective-permute-start(bf16[64,256]{1,0:T(8,128)(2,1)S(1)} %hidden_rows.1.own), channel_id=1, source_target_pairs={{0,16},{16,0},{1,17},{17,1},{2,18},{18,2},{3,19},{19,3},{4,20},{20... | collective-permute-start | bytes 98312 | tf_op jit(solution)/shard_map/ppermute | solution.py:505

commit v23 on v20

--- a/solution.py
+++ b/solution.py
@@ -23,6 +23,7 @@
     return list(range(n - 1, -1, -1))
 
 
+KINDS = 3
 LN2 = 0.6931471805599453
 
 
@@ -57,6 +58,10 @@
         return whole * jnp.exp(powers[s:s + 1, :] * LN2)
 
     return value_of
+
+
+def trash_of(n, per, radix):
+    return (radix - 2) * (n // radix) * per
 
 
 def plan_kernel(chunks, per, n, radix, n_src, ids, src_h, rows_h, dst_h, tw, xo, *rest):
@@ -77,17 +82,21 @@
     for c in copies:
         c.start()
     lane = lax.broadcasted_iota(jnp.int32, (1, tiles), 1)
-    block_i = lax.broadcasted_iota(jnp.int32, (n_src, tiles), 0)
+    block_i = lax.broadcasted_iota(jnp.int32, (KINDS * n_src, tiles), 0)
     before = lax.broadcasted_iota(jnp.int32, (units, units), 0) < lax.broadcasted_iota(jnp.int32, (units, units), 1)
     before = jnp.where(before, 1.0, 0.0).astype(jnp.bfloat16)
     pos_i = lax.broadcasted_iota(jnp.int32, (tiles, n_pos), 1).astype(jnp.float32)
     place_i = lax.broadcasted_iota(jnp.int32, (1, n_pos), 1)
-    trash = float(n * per << 14)
+    trash = float(trash_of(n, per, radix) << 14)
     for c in copies[:3]:
         c.wait()
     src, rows = src_v[...], rows_v[...]
     slot = jnp.bitwise_xor(dst_v[...], me)
-    slot = jnp.bitwise_and(slot, radix - 1) * (n // radix) + lax.div(slot, radix)
+    partner = jnp.bitwise_and(slot, radix - 1)
+    kind = jnp.where(partner == radix - 1, 0, jnp.where(partner > 0, 1, 2))
+    slot = lax.div(slot, radix) + jnp.where(kind == 1, partner - 1, 0) * (n // radix)
+    cell = kind * n_src + src
+    cells = KINDS * n_src
     for c in range(chunks):
         hot, words, valid = [], [], []
         for j in range(per):
@@ -95,18 +104,28 @@
             ok = limit > 0
             valid.append(ok)
             words.append(((slot * per + j) * 512 + (j * tiles + lane)) * 32 + limit)
-            hot.append(jnp.where(jnp.logical_and(block_i == src, ok), 1.0, 0.0))
+            hot.append(jnp.where(jnp.logical_and(block_i == cell, ok), 1.0, 0.0))
         hot = jnp.concatenate(hot, axis=1)
         earlier = jnp.dot(hot.astype(jnp.bfloat16), before, preferred_element_type=jnp.float32)
         blocks = jnp.floor((jnp.sum(hot, axis=1, keepdims=True) + (BLOCK - 1)) * (1.0 / BLOCK))
+        half_step = STEP // 2
         ahead = jnp.zeros(blocks.shape, jnp.float32)
-        source_i = lax.broadcasted_iota(jnp.int32, blocks.shape, 0)
-        for s in range(n_src - 1):
-            ahead = ahead + jnp.where(source_i > s, blocks[s:s + 1, :], 0.0)
+        cell_i = lax.broadcasted_iota(jnp.int32, blocks.shape, 0)
+        starts = [jnp.zeros((1, 1), jnp.float32)]
+        for k in range(KINDS):
+            count = jnp.zeros((1, 1), jnp.float32)
+            for s in range(k * n_src, (k + 1) * n_src):
+                here = blocks[s:s + 1, :]
+                ahead = ahead + jnp.where(jnp.logical_and(cell_i > s, cell_i < (k + 1) * n_src), here, 0.0)
+                count = count + here
+            ahead = ahead + jnp.where(lax.div(cell_i, n_src) == k, starts[k], 0.0)
+            starts.append(starts[k] + jnp.floor((count + (half_step - 1)) * (1.0 / half_step)) * half_step)
         pos = jnp.sum(hot * (earlier + ahead * BLOCK), axis=0, keepdims=True)
         behind = jnp.where(place_i.astype(jnp.float32) >= ahead + blocks, 1.0, 0.0)
-        owner = jnp.sum(behind, axis=0, keepdims=True)
-        run = ahead[n_src - 1:, :] + blocks[n_src - 1:, :]
+        owner = jnp.minimum(jnp.sum(behind, axis=0, keepdims=True), cells - 1.0)
+        owner = owner - n_src * jnp.floor(owner * (1.0 / n_src))
+        for k in range(KINDS + 1):
+            owner = jnp.where(place_i == n_pos - 1 - k, starts[k], owner)
         stack = [jnp.where(valid[j], pos[:, j * tiles:(j + 1) * tiles], -1.0) for j in range(per)]
         stack += [w.astype(jnp.float32) - trash for w in words]
         stack += [jnp.zeros((1, tiles), jnp.float32)] * (-len(stack) % 8)
@@ -115,7 +134,6 @@
         for j in range(per):
             found = found + jnp.where(cols[:, j:j + 1] == pos_i, cols[:, per + j:per + j + 1], 0.0)
         word = jnp.sum(found, axis=0, keepdims=True) + trash
-        owner = jnp.where(place_i == n_pos - 1, run, jnp.minimum(owner, n_src - 1.0))
         tables[c][0:1, :] = word.astype(jnp.int32)
         tables[c][1:2, :] = owner.astype(jnp.int32)
 
@@ -126,8 +144,9 @@
 def plan(chunks, per, n, radix, ids, src, rows, dst, tw, xo):
     tiles, _, _, tile = tw.shape
     n_src = xo.shape[0] // tile
-    blocks = -(-(per * tiles // BLOCK + n_src) // STEP) * STEP
-    n_pos = -(-(blocks * BLOCK + 1) // 128) * 128
+    half_step = STEP // 2
+    blocks = per * tiles // BLOCK + KINDS * n_src + KINDS * half_step
+    n_pos = -(-(blocks * BLOCK) // 128) * 128
     smem = pl.BlockSpec(memory_space=pltpu.SMEM)
     vmem = pl.BlockSpec(memory_space=pltpu.VMEM)
     hbm = pl.BlockSpec(memory_space=pltpu.HBM)
@@ -202,7 +221,7 @@
     )(ids, jnp.swapaxes(send_list, 1, 2), send_count, adj)
 
 
-def tiles_kernel(table_v, tbuf, xo, xp, *rest):
+def tiles_kernel(kind, used, table_v, tbuf, xo, xp, *rest):
     parts = len(rest) - 3
     accs, (masks, table, sem) = rest[:parts], rest[parts:]
     tile = tbuf.shape[2]
@@ -210,7 +229,7 @@
     to_scalar = pltpu.make_async_copy(table_v, table, sem)
     to_scalar.start()
     for acc in accs:
-        acc[...] = jnp.zeros_like(acc)
+        acc[:used, :] = jnp.zeros((used, acc.shape[1]), jnp.float32)
     row_i = lax.broadcasted_iota(jnp.int32, (UNIT, tile), 0)
     for m in range(UNIT + 1):
         masks[m] = jnp.where(row_i < m, 1.0, 0.0).astype(jnp.bfloat16)
@@ -235,30 +254,31 @@
                     acc[pl.ds(places[k], UNIT), :] += got[k * UNIT:(k + 1) * UNIT, :]
 
     half = STEP // 2
-    halves = lax.div(table[1, table.shape[1] - 1] + half - 1, half)
+    begin = table[1, table.shape[1] - 1 - kind]
+    halves = lax.div(table[1, table.shape[1] - 2 - kind] - begin, half)
     steps = lax.div(halves, 2)
 
     def step(i, carry):
-        blocks(i * STEP, STEP)
+        blocks(begin + i * STEP, STEP)
         return carry
 
     def last(i, carry):
-        blocks(steps * STEP, half)
+        blocks(begin + steps * STEP, half)
         return carry
 
     lax.fori_loop(0, steps, step, 0)
     lax.fori_loop(0, lax.rem(halves, 2), last, 0)
 
 
-def gathered_sums(per, n, table, tbuf, xo, xp):
+def gathered_sums(kind, used, per, n, radix, table, tbuf, xo, xp):
     width = xo.shape[1]
     tile = tbuf.shape[2]
     vmem = pl.BlockSpec(memory_space=pltpu.VMEM)
-    flops = 2 * tbuf.shape[0] * UNIT * tile * 2 * width
+    flops = 2 * tbuf.shape[0] * UNIT * tile * 2 * width // 3
     parts = 2 * width // PART
-    sums = jax.ShapeDtypeStruct(((n * per + 1) * UNIT, PART), jnp.float32)
-    return pl.pallas_call(
-        tiles_kernel,
+    sums = jax.ShapeDtypeStruct(((trash_of(n, per, radix) + 1) * UNIT, PART), jnp.float32)
+    return pl.pallas_call(
+        functools.partial(tiles_kernel, kind, used),
         out_shape=[sums] * parts,
         in_specs=[vmem] * 4,
         out_specs=[vmem] * parts,
@@ -268,7 +288,7 @@
             pltpu.SemaphoreType.DMA,
         ],
         compiler_params=pltpu.CompilerParams(vmem_limit_bytes=(12 << 20) + sums.size * 4 * parts),
-        cost_estimate=pl.CostEstimate(flops=flops, bytes_accessed=8 << 20, transcendentals=0),
+        cost_estimate=pl.CostEstimate(flops=flops, bytes_accessed=4 << 20, transcendentals=0),
         name="gathered_sums",
     )(table, tbuf, xo, xp)
 
@@ -292,17 +312,17 @@
     lax.fori_loop(0, count // size, piece, 0)
 
 
-def sent_kernel(k, slots, rows, parts, wo, wp, *refs):
+def sent_kernel(first, slots, rows, parts, wo, wp, *refs):
     accs, (out, sums, tail) = refs[:parts], refs[parts:]
-    weigh(accs, (wo, wp), k * slots * rows, slots * rows, sums)
+    weigh(accs, (wo, wp), first, slots * rows, sums)
     write_coded(out, tail, slots, rows, lambda s: sums[s * rows:(s + 1) * rows, :])
 
 
-def sent_terms(k, slots, rows, accs, wo, wp):
+def sent_terms(first, slots, rows, accs, wo, wp):
     hidden = wo.shape[1]
     vmem = pl.BlockSpec(memory_space=pltpu.VMEM)
     return pl.pallas_call(
-        functools.partial(sent_kernel, k, slots, rows, len(accs)),
+        functools.partial(sent_kernel, first, slots, rows, len(accs)),
         out_shape=jax.ShapeDtypeStruct((slots * rows + tail_rows(slots), hidden), jnp.int16),
         in_specs=[vmem] * (2 + len(accs)),
         out_specs=vmem,
@@ -488,10 +508,18 @@
     wo, so = neighbour_weight_first, w_self1
     done = []
     for chunk in range(CHUNKS):
-        accs = gathered_sums(per, n, tables[chunk], tbufs[chunk], xo, xp)
         slots, rows = n // 4, per * UNIT
-        parts = {k: sent_terms(k, slots, rows, accs, wo, wp) for k in (1, 2, 3)}
-        parts[0], theirs = own_terms(chunk, per, groups, slots, ids, accs, wo, wp, xo, so)
+        size = slots * rows
+        far, near, mine = (
+            gathered_sums(kind, used, per, n, 4, tables[chunk], tbufs[chunk], xo, xp)
+            for kind, used in enumerate((size, 2 * size, size))
+        )
+        parts = {
+            1: sent_terms(0, slots, rows, near, wo, wp),
+            2: sent_terms(size, slots, rows, near, wo, wp),
+            3: sent_terms(0, slots, rows, far, wo, wp),
+        }
+        parts[0], theirs = own_terms(chunk, per, groups, slots, ids, mine, wo, wp, xo, so)
         self = lax.ppermute(theirs, "feat", swap)
         got = exchange(parts, 1, n, (1, 2, 3))
         stride = 4

time: 40.6 us -> 41.4 us (1.020)
  Pallas kernels: 12.3 us -> 14.9 us
  waiting for transfers between devices: 8.46 us -> 6.95 us
    pallas_call x4 -> x6, Pallas kernels: 6.62 us -> 9.25 us  [the longest x3 7.69 us: gathered_sums(): pl.pallas_call(functools.partial(tiles_kernel, kind, used), out_shape=[su...]
    ppermute x6, waiting for transfers between devices: 7.26 us -> 5.75 us  [exchange(): lax.ppermute(parts[k], 'dom', [(i, i ^ k * stride) for i in range(n)])]
  transfers between devices with their start and end apart: 10 -> 10, of which waited for: 6 -> 5; matrix products, arithmetic and copies ran while one was open for 0% -> 0% of each run, Pallas kernels for 26% -> 32%
where the time goes in v23:
time: 41.4 us; the launch traced here: 41.2 us
  Pallas kernels  14.9 us (36%)
  blocking collectives  9.67 us (23%)
  starting transfers between devices  9.4 us (23%)
  waiting for transfers between devices  6.95 us (17%)
    all_to_all x1, blocking collectives, body(): lax.all_to_all(send, 'dom', 0, 0, axis_index_groups=[group_order(n)], til...  9.67 us
    ppermute x6, starting transfers between devices, exchange(): lax.ppermute(parts[k], 'dom', [(i, i ^ k * stride) for i in range(n)])  8.75 us
    pallas_call x3, Pallas kernels, gathered_sums(): pl.pallas_call(functools.partial(tiles_kernel, kind, used), out_shape=[su...  7.69 us
    ppermute x6, waiting for transfers between devices, exchange(): lax.ppermute(parts[k], 'dom', [(i, i ^ k * stride) for i in range(n)])  5.75 us
    pallas_call x1, Pallas kernels, plan(): pl.pallas_call(functools.partial(plan_kernel, chunks, per, n, radix, n_sr...  2.55 us
    pallas_call x3, Pallas kernels, sent_terms(): pl.pallas_call(functools.partial(sent_kernel, first, slots, rows, len(acc...  1.56 us
    ppermute x1, waiting for transfers between devices, body(): other = lax.ppermute(own, 'feat', swap)  1.19 us
    pallas_call x1, Pallas kernels, own_terms(): pl.pallas_call(functools.partial(own_kernel, chunk, per, groups, len(accs...  1.04 us
  transfers between devices with their start and end apart: 10, of which 5 were waited for; matrix products, arithmetic and copies ran while one was open for 0% of the time, Pallas kernels for 32%

profile of v23, /device:TPU:0, one launch (start us, length us, event | category | flops | bytes accessed | tf_op | source)
XLA Modules:
  0.0 41.2 jit_solution(11500053780760724273)
XLA Ops:
  0.0 0.5 %collective-permute-start.1 = (bf16[1024,512]{1,0:T(8,128)(2,1)}, bf16[1024,512]{1,0:T(8,128)(2,1)S(1)}, u32[]{:S(2)}, u32[]{:S(2)}) collective-permute-start(bf16[1024,512]{1,0:T(8,128)(2,1)} %xo.1), channel_id=1, source_target_pairs={{0,16},{16,0},{1,17},{17,1},{2,18},{18,2},{3,19},{19,3},{4,20},{20... | collective-permute-start | bytes 3145736 | tf_op jit(solution)/shard_map/ppermute | solution.py:501
  0.5 0.1 collective-permute-start
  0.5 0.1 pad_add_fusion.ids
  0.6 0.0 copy-start
  0.6 2.5 %plan.1 = (s32[2,896]{1,0:T(2,128)S(1)}, bf16[512,16,128]{2,1,0:T(8,128)(2,1)S(1)}, bf16[1024,512]{1,0:T(8,128)(2,1)S(1)}) custom-call(s32[2]{0:T(128)S(1)} %pad_add_fusion.ids, s32[1,128]{1,0:T(1,128)} %bitcast.17, s32[1,128]{1,0:T(1,128)} %bitcast.18, s32[1,128]{1,0:T(1,128)} %bitcast.19, bf16[128,8,16,128]{3,2,1,0:T(8,128)(2,1)} %bitcast.16, ...), custom_call_target="tpu_custom_call" | custom-call | tf_op jit(solution)/shard_map/plan/pallas_call | solution.py:154
  3.1 0.0 collective-permute-done.1.xp
  3.2 2.0 %gathered_sums.5 = (f32[528,256]{1,0:T(8,128)S(1)}, f32[528,256]{1,0:T(8,128)S(1)}, f32[528,256]{1,0:T(8,128)S(1)}, f32[528,256]{1,0:T(8,128)S(1)}) custom-call(s32[2,896]{1,0:T(2,128)S(1)} %get-tuple-element.30.table_v, bf16[512,16,128]{2,1,0:T(8,128)(2,1)S(1)} %get-tuple-element.31.tbuf, bf16[1024,512]{1,0:T(8,128)(2,1)S(1)} %get-tuple-element.29.xo, ...), custom_call_target="tpu_custom_call" | custom-call | flops 715827904 | bytes 4194304 | tf_op jit(solution)/shard_map/gathered_sums/pallas_call | solution.py:280
  5.2 0.0 collective-permute-done.wp
  5.2 0.0 copy-done
  5.2 0.5 %sent_terms.5 = s16[264,256]{1,0:T(8,128)(2,1)S(1)} custom-call(bf16[512,256]{1,0:T(8,128)(2,1)S(1)} %copy-done, bf16[512,256]{1,0:T(8,128)(2,1)S(1)} %collective-permute-done.wp, f32[528,256]{1,0:T(8,128)S(1)} %get-tuple-element.41.refs_0_, f32[528,256]{1,0:T(8,128)S(1)} %get-tuple-element.42.refs_1_, f32[528,256]{1,0:T(8,128)S(1)} %get-tuple-element.43.refs_2_, ...), custom_call_target="tpu_custom_call" | custom-call | flops 268435456 | bytes 2097152 | tf_op jit(solution)/shard_map/sent_terms/pallas_call | solution.py:324
  5.7 4.0 %collective-permute-start.4 = (s16[264,256]{1,0:T(8,128)(2,1)S(1)}, s16[264,256]{1,0:T(8,128)(2,1)S(1)}, u32[]{:S(2)}, u32[]{:S(2)}) collective-permute-start(s16[264,256]{1,0:T(8,128)(2,1)S(1)} %sent_terms.5), channel_id=1, source_target_pairs={{0,3},{1,2},{2,1},{3,0},{4,7},{5,6},{6,5},{7,4},{8,11},{9,10},{10,... | collective-permute-start | bytes 405512 | tf_op jit(solution)/shard_map/ppermute | solution.py:474
  9.7 3.6 %gathered_sums.4 = (f32[528,256]{1,0:T(8,128)S(1)}, f32[528,256]{1,0:T(8,128)S(1)}, f32[528,256]{1,0:T(8,128)S(1)}, f32[528,256]{1,0:T(8,128)S(1)}) custom-call(s32[2,896]{1,0:T(2,128)S(1)} %get-tuple-element.30.table_v, bf16[512,16,128]{2,1,0:T(8,128)(2,1)S(1)} %get-tuple-element.31.tbuf, bf16[1024,512]{1,0:T(8,128)(2,1)S(1)} %get-tuple-element.29.xo, ...), custom_call_target="tpu_custom_call" | custom-call | flops 715827904 | bytes 4194304 | tf_op jit(solution)/shard_map/gathered_sums/pallas_call | solution.py:280
  13.3 0.5 %sent_terms.4 = s16[264,256]{1,0:T(8,128)(2,1)S(1)} custom-call(bf16[512,256]{1,0:T(8,128)(2,1)S(1)} %copy-done, bf16[512,256]{1,0:T(8,128)(2,1)S(1)} %collective-permute-done.wp, f32[528,256]{1,0:T(8,128)S(1)} %get-tuple-element.37.refs_0_, f32[528,256]{1,0:T(8,128)S(1)} %get-tuple-element.38.refs_1_, f32[528,256]{1,0:T(8,128)S(1)} %get-tuple-element.39.refs_2_, ...), custom_call_target="tpu_custom_call" | custom-call | flops 268435456 | bytes 2097152 | tf_op jit(solution)/shard_map/sent_terms/pallas_call | solution.py:324
  13.9 0.0 copy-start.1
  13.9 0.1 collective-permute-start.3
  14.0 0.5 %sent_terms.3 = s16[264,256]{1,0:T(8,128)(2,1)S(1)} custom-call(bf16[512,256]{1,0:T(8,128)(2,1)S(1)} %copy-done, bf16[512,256]{1,0:T(8,128)(2,1)S(1)} %collective-permute-done.wp, f32[528,256]{1,0:T(8,128)S(1)} %get-tuple-element.37.refs_0_, f32[528,256]{1,0:T(8,128)S(1)} %get-tuple-element.38.refs_1_, f32[528,256]{1,0:T(8,128)S(1)} %get-tuple-element.39.refs_2_, ...), custom_call_target="tpu_custom_call" | custom-call | flops 268435456 | bytes 2097152 | tf_op jit(solution)/shard_map/sent_terms/pallas_call | solution.py:324
  14.5 0.0 copy-start.4
  14.5 0.0 copy-start.5
  14.5 0.0 copy-start.6
  14.5 0.0 copy-start.2
  14.6 0.0 copy-start.3
  14.6 0.6 %collective-permute-start.2 = (s16[264,256]{1,0:T(8,128)(2,1)S(1)}, s16[264,256]{1,0:T(8,128)(2,1)S(1)}, u32[]{:S(2)}, u32[]{:S(2)}) collective-permute-start(s16[264,256]{1,0:T(8,128)(2,1)S(1)} %sent_terms.3), channel_id=1, source_target_pairs={{0,1},{1,0},{2,3},{3,2},{4,5},{5,4},{6,7},{7,6},{8,9},{9,8},{10,11... | collective-permute-start | bytes 405512 | tf_op jit(solution)/shard_map/ppermute | solution.py:474
  15.2 2.1 %gathered_sums.3 = (f32[528,256]{1,0:T(8,128)S(1)}, f32[528,256]{1,0:T(8,128)S(1)}, f32[528,256]{1,0:T(8,128)S(1)}, f32[528,256]{1,0:T(8,128)S(1)}) custom-call(s32[2,896]{1,0:T(2,128)S(1)} %get-tuple-element.30.table_v, bf16[512,16,128]{2,1,0:T(8,128)(2,1)S(1)} %get-tuple-element.31.tbuf, bf16[1024,512]{1,0:T(8,128)(2,1)S(1)} %get-tuple-element.29.xo, ...), custom_call_target="tpu_custom_call" | custom-call | flops 715827904 | bytes 4194304 | tf_op jit(solution)/shard_map/gathered_sums/pallas_call | solution.py:280
  17.2 0.0 copy-done.1
  17.2 1.0 %own_terms.1 = (f32[256,256]{1,0:T(8,128)S(1)}, f32[64,256]{1,0:T(8,128)S(1)}) custom-call(s32[2]{0:T(128)S(1)} %pad_add_fusion.ids, bf16[512,256]{1,0:T(8,128)(2,1)S(1)} %copy-done, bf16[512,256]{1,0:T(8,128)(2,1)S(1)} %collective-permute-done.wp, bf16[1024,512]{1,0:T(8,128)(2,1)S(1)} %get-tuple-element.29.xo, bf16[512,256]{1,0:T(8,128)(2,1)S(1)} %copy-done.1, ...), custom_call_target="tpu_custom_call" | custom-call | flops 268435456 | bytes 2097152 | tf_op jit(solution)/shard_map/own_terms/pallas_call | solution.py:357
  18.3 0.1 collective-permute-start.5
  18.4 0.0 collective-permute-done.4.refs_2_
  18.4 0.8 %collective-permute-done.3.refs_1_ = s16[264,256]{1,0:T(8,128)(2,1)S(1)} collective-permute-done((s16[264,256]{1,0:T(8,128)(2,1)S(1)}, s16[264,256]{1,0:T(8,128)(2,1)S(1)}, u32[]{:S(2)}, u32[]{:S(2)}) %collective-permute-start.3) | collective-permute-done | bytes 135200 | tf_op jit(solution)/shard_map/ppermute | solution.py:474
  19.2 0.9 %collective-permute-done.2.refs_0_ = s16[264,256]{1,0:T(8,128)(2,1)S(1)} collective-permute-done((s16[264,256]{1,0:T(8,128)(2,1)S(1)}, s16[264,256]{1,0:T(8,128)(2,1)S(1)}, u32[]{:S(2)}, u32[]{:S(2)}) %collective-permute-start.2) | collective-permute-done | bytes 135200 | tf_op jit(solution)/shard_map/ppermute | solution.py:474
  20.1 0.2 combine.1
  20.3 3.1 %collective-permute-start.6 = (s16[72,256]{1,0:T(8,128)(2,1)S(1)}, s16[72,256]{1,0:T(8,128)(2,1)S(1)}, u32[]{:S(2)}, u32[]{:S(2)}) collective-permute-start(s16[72,256]{1,0:T(8,128)(2,1)S(1)} %get-tuple-element.47), channel_id=1, source_target_pairs={{0,8},{1,9},{2,10},{3,11},{4,12},{5,13},{6,14},{7,15},{8,0},{9,1},... | collective-permute-start | bytes 110600 | tf_op jit(solution)/shard_map/ppermute | solution.py:474
  23.4 0.8 %collective-permute-start.7 = (s16[72,256]{1,0:T(8,128)(2,1)S(1)}, s16[72,256]{1,0:T(8,128)(2,1)S(1)}, u32[]{:S(2)}, u32[]{:S(2)}) collective-permute-start(s16[72,256]{1,0:T(8,128)(2,1)S(1)} %get-tuple-element.48), channel_id=1, source_target_pairs={{0,12},{1,13},{2,14},{3,15},{4,8},{5,9},{6,10},{7,11},{8,4},{9,5},... | collective-permute-start | bytes 110600 | tf_op jit(solution)/shard_map/ppermute | solution.py:474
  24.1 0.2 collective-permute-start.8
  24.3 0.0 copy-done.4
  24.3 0.0 copy-done.5
  24.3 0.0 copy-done.6
  24.3 0.7 %selection.1 = (bf16[128,128]{1,0:T(8,128)(2,1)S(1)}, bf16[128,128]{1,0:T(8,128)(2,1)S(1)}, bf16[64,128]{1,0:T(8,128)(2,1)S(1)}) custom-call(s32[2]{0:T(128)S(1)} %pad_add_fusion.ids, s32[16,8,16]{2,1,0:T(8,128)S(1)} %bitcast.15, s32[16,16]{1,0:T(8,128)S(1)} %copy-done.6, bf16[64,256]{1,0:T(8,128)(2,1)S(1)} %copy-done.5), custom_call_target="tpu_custom_call" | custom-call | tf_op jit(solution)/shard_map/selection/pallas_call | solution.py:210
  25.0 0.0 collective-permute-done.5.refs_1_
  25.0 0.2 collective-permute-done.6.refs_2_
  25.3 3.8 %collective-permute-done.7.refs_3_ = s16[72,256]{1,0:T(8,128)(2,1)S(1)} collective-permute-done((s16[72,256]{1,0:T(8,128)(2,1)S(1)}, s16[72,256]{1,0:T(8,128)(2,1)S(1)}, u32[]{:S(2)}, u32[]{:S(2)}) %collective-permute-start.7) | collective-permute-done | bytes 36896 | tf_op jit(solution)/shard_map/ppermute | solution.py:474
  29.1 0.0 collective-permute-done.8.refs_4_
  29.2 0.1 collective-permute-start.9
  29.2 1.2 %collective-permute-done.9.other = bf16[64,256]{1,0:T(8,128)(2,1)S(1)} collective-permute-done((bf16[64,256]{1,0:T(8,128)(2,1)S(1)}, bf16[64,256]{1,0:T(8,128)(2,1)S(1)}, u32[]{:S(2)}, u32[]{:S(2)}) %collective-permute-start.9) | collective-permute-done | bytes 32800 | tf_op jit(solution)/shard_map/ppermute | solution.py:534
  30.4 0.1 rows_to_send.1
  30.6 9.7 %all_to_all.11 = bf16[16,8,256]{2,1,0:T(8,128)(2,1)S(1)} all-to-all(bf16[16,8,256]{2,1,0:T(8,128)(2,1)S(1)} %bitcast.11), channel_id=1, replica_groups={{15,14,13,12,11,10,9,8,7,6,5,4,3,2,1,0},{31,30,29,28,27,26,25,24,23,22,..., dimensions={0} | all-to-all | bytes 131072 | tf_op jit(solution)/shard_map/all_to_all | solution.py:536
  40.3 0.0 copy-done.2
  40.3 0.0 copy-done.3
  40.3 1.0 %logits.1 = f32[64,172]{1,0:T(8,128)} custom-call(bf16[64,256]{1,0:T(8,128)(2,1)S(1)} %hidden_rows.1.own, bf16[64,256]{1,0:T(8,128)(2,1)S(1)} %collective-permute-done.9.other, bf16[128,256]{1,0:T(8,128)(2,1)S(1)} %bitcast.12, bf16[128,128]{1,0:T(8,128)(2,1)S(1)} %get-tuple-element.51.front, bf16[64,128]{1,0:T(8,128)(2,1)S(1)} %get-tuple-element.52.adj_received, ...), custom_call_target="tpu_custom_call" | custom-call | tf_op jit(solution)/shard_map/logits/pallas_call | solution.py:461
  (1 shorter events, 0.0 us)
Async XLA Ops:
  0.0 3.1 %collective-permute-start.1 = (bf16[1024,512]{1,0:T(8,128)(2,1)}, bf16[1024,512]{1,0:T(8,128)(2,1)S(1)}, u32[]{:S(2)}, u32[]{:S(2)}) collective-permute-start(bf16[1024,512]{1,0:T(8,128)(2,1)} %xo.1), channel_id=1, source_target_pairs={{0,16},{16,0},{1,17},{17,1},{2,18},{18,2},{3,19},{19,3},{4,20},{20... | collective-permute-start | bytes 3145736 | tf_op jit(solution)/shard_map/ppermute | solution.py:501
  0.5 4.7 %collective-permute-start = (bf16[512,256]{1,0:T(8,128)(2,1)}, bf16[512,256]{1,0:T(8,128)(2,1)S(1)}, u32[]{:S(2)}, u32[]{:S(2)}) collective-permute-start(bf16[512,256]{1,0:T(8,128)(2,1)} %wo.7), channel_id=1, source_target_pairs={{0,16},{16,0},{1,17},{17,1},{2,18},{18,2},{3,19},{19,3},{4,20},{20... | collective-permute-start | bytes 786440 | tf_op jit(solution)/shard_map/ppermute | solution.py:502
  0.6 4.6 %copy-start = (bf16[512,256]{1,0:T(8,128)(2,1)S(1)}, bf16[512,256]{1,0:T(8,128)(2,1)}, u32[]{:S(2)}) copy-start(bf16[512,256]{1,0:T(8,128)(2,1)} %wo.7) | copy-start | bytes 786436
  5.7 12.7 %collective-permute-start.4 = (s16[264,256]{1,0:T(8,128)(2,1)S(1)}, s16[264,256]{1,0:T(8,128)(2,1)S(1)}, u32[]{:S(2)}, u32[]{:S(2)}) collective-permute-start(s16[264,256]{1,0:T(8,128)(2,1)S(1)} %sent_terms.5), channel_id=1, source_target_pairs={{0,3},{1,2},{2,1},{3,0},{4,7},{5,6},{6,5},{7,4},{8,11},{9,10},{10,... | collective-permute-start | bytes 405512 | tf_op jit(solution)/shard_map/ppermute | solution.py:474
  13.9 3.4 %copy-start.1 = (bf16[512,256]{1,0:T(8,128)(2,1)S(1)}, bf16[512,256]{1,0:T(8,128)(2,1)}, u32[]{:S(2)}) copy-start(bf16[512,256]{1,0:T(8,128)(2,1)} %so.1) | copy-start | bytes 786436
  13.9 5.3 %collective-permute-start.3 = (s16[264,256]{1,0:T(8,128)(2,1)S(1)}, s16[264,256]{1,0:T(8,128)(2,1)S(1)}, u32[]{:S(2)}, u32[]{:S(2)}) collective-permute-start(s16[264,256]{1,0:T(8,128)(2,1)S(1)} %sent_terms.4), channel_id=1, source_target_pairs={{0,2},{1,3},{2,0},{3,1},{4,6},{5,7},{6,4},{7,5},{8,10},{9,11},{10,... | collective-permute-start | bytes 405512 | tf_op jit(solution)/shard_map/ppermute | solution.py:474
  14.5 9.8 %copy-start.4 = (s32[16,16,8]{1,2,0:T(8,128)S(1)}, s32[16,16,8]{1,2,0:T(8,128)}, u32[]{:S(2)}) copy-start(s32[16,16,8]{1,2,0:T(8,128)} %param.19) | copy-start | bytes 24580
  14.5 9.8 %copy-start.5 = (bf16[64,256]{1,0:T(8,128)(2,1)S(1)}, bf16[64,256]{1,0:T(8,128)(2,1)}, u32[]{:S(2)}) copy-start(bf16[64,256]{1,0:T(8,128)(2,1)} %adj.1) | copy-start | bytes 98308
  14.5 9.8 %copy-start.6 = (s32[16,16]{1,0:T(8,128)S(1)}, s32[16,16]{1,0:T(8,128)}, u32[]{:S(2)}) copy-start(s32[16,16]{1,0:T(8,128)} %counts.1) | copy-start | bytes 3076
  14.5 25.7 %copy-start.2 = (bf16[256,172]{0,1:T(8,128)(2,1)S(1)}, bf16[256,172]{0,1:T(8,128)(2,1)}, u32[]{:S(2)}) copy-start(bf16[256,172]{0,1:T(8,128)(2,1)} %param.22) | copy-start | bytes 264196
  14.6 25.7 %copy-start.3 = (bf16[256,172]{0,1:T(8,128)(2,1)S(1)}, bf16[256,172]{0,1:T(8,128)(2,1)}, u32[]{:S(2)}) copy-start(bf16[256,172]{0,1:T(8,128)(2,1)} %param.23) | copy-start | bytes 264196
  14.6 5.5 %collective-permute-start.2 = (s16[264,256]{1,0:T(8,128)(2,1)S(1)}, s16[264,256]{1,0:T(8,128)(2,1)S(1)}, u32[]{:S(2)}, u32[]{:S(2)}) collective-permute-start(s16[264,256]{1,0:T(8,128)(2,1)S(1)} %sent_terms.3), channel_id=1, source_target_pairs={{0,1},{1,0},{2,3},{3,2},{4,5},{5,4},{6,7},{7,6},{8,9},{9,8},{10,11... | collective-permute-start | bytes 405512 | tf_op jit(solution)/shard_map/ppermute | solution.py:474
  18.3 6.8 %collective-permute-start.5 = (f32[64,256]{1,0:T(8,128)S(1)}, f32[64,256]{1,0:T(8,128)S(1)}, u32[]{:S(2)}, u32[]{:S(2)}) collective-permute-start(f32[64,256]{1,0:T(8,128)S(1)} %get-tuple-element.46), channel_id=1, source_target_pairs={{0,16},{16,0},{1,17},{17,1},{2,18},{18,2},{3,19},{19,3},{4,20},{20... | collective-permute-start | bytes 196616 | tf_op jit(solution)/shard_map/ppermute | solution.py:523
  20.3 5.0 %collective-permute-start.6 = (s16[72,256]{1,0:T(8,128)(2,1)S(1)}, s16[72,256]{1,0:T(8,128)(2,1)S(1)}, u32[]{:S(2)}, u32[]{:S(2)}) collective-permute-start(s16[72,256]{1,0:T(8,128)(2,1)S(1)} %get-tuple-element.47), channel_id=1, source_target_pairs={{0,8},{1,9},{2,10},{3,11},{4,12},{5,13},{6,14},{7,15},{8,0},{9,1},... | collective-permute-start | bytes 110600 | tf_op jit(solution)/shard_map/ppermute | solution.py:474
  23.4 5.8 %collective-permute-start.7 = (s16[72,256]{1,0:T(8,128)(2,1)S(1)}, s16[72,256]{1,0:T(8,128)(2,1)S(1)}, u32[]{:S(2)}, u32[]{:S(2)}) collective-permute-start(s16[72,256]{1,0:T(8,128)(2,1)S(1)} %get-tuple-element.48), channel_id=1, source_target_pairs={{0,12},{1,13},{2,14},{3,15},{4,8},{5,9},{6,10},{7,11},{8,4},{9,5},... | collective-permute-start | bytes 110600 | tf_op jit(solution)/shard_map/ppermute | solution.py:474
  24.1 5.0 %collective-permute-start.8 = (s16[72,256]{1,0:T(8,128)(2,1)S(1)}, s16[72,256]{1,0:T(8,128)(2,1)S(1)}, u32[]{:S(2)}, u32[]{:S(2)}) collective-permute-start(s16[72,256]{1,0:T(8,128)(2,1)S(1)} %get-tuple-element.49), channel_id=1, source_target_pairs={{0,4},{1,5},{2,6},{3,7},{4,0},{5,1},{6,2},{7,3},{8,12},{9,13},{10,... | collective-permute-start | bytes 110600 | tf_op jit(solution)/shard_map/ppermute | solution.py:474
  29.2 1.3 %collective-permute-start.9 = (bf16[64,256]{1,0:T(8,128)(2,1)S(1)}, bf16[64,256]{1,0:T(8,128)(2,1)S(1)}, u32[]{:S(2)}, u32[]{:S(2)}) collective-permute-start(bf16[64,256]{1,0:T(8,128)(2,1)S(1)} %hidden_rows.1.own), channel_id=1, source_target_pairs={{0,16},{16,0},{1,17},{17,1},{2,18},{18,2},{3,19},{19,3},{4,20},{20... | collective-permute-start | bytes 98312 | tf_op jit(solution)/shard_map/ppermute | solution.py:534

commit v24 on v23

--- a/solution.py
+++ b/solution.py
@@ -8,8 +8,8 @@
 from jax.sharding import PartitionSpec as P
 
 UNIT = 16
-BLOCK = 8
-STEP = 8
+BLOCK = 4
+STEP = 16
 PART = 256
 CHUNKS = 1
 
@@ -337,37 +337,49 @@
     )(wo, wp, *accs)
 
 
-def own_kernel(chunk, per, groups, parts, ids, wo, wp, xo, so, *refs):
-    accs, (out, theirs, terms) = refs[:parts], refs[parts:]
+def own_kernel(parts, wo, wp, *refs):
+    accs, out = refs[:parts], refs[parts]
     weigh(accs, (wo, wp), 0, out.shape[0], out)
+
+
+def own_terms(count, accs, wo, wp):
+    hidden = wo.shape[1]
+    vmem = pl.BlockSpec(memory_space=pltpu.VMEM)
+    return pl.pallas_call(
+        functools.partial(own_kernel, len(accs)),
+        out_shape=jax.ShapeDtypeStruct((count, hidden), jnp.float32),
+        in_specs=[vmem] * (2 + len(accs)),
+        out_specs=vmem,
+        compiler_params=pltpu.CompilerParams(vmem_limit_bytes=(12 << 20) + accs[0].size * 4 * len(accs)),
+        cost_estimate=pl.CostEstimate(
+            flops=4 * count * PART * len(accs) * hidden, bytes_accessed=2 << 20, transcendentals=0),
+        name="own_terms",
+    )(wo, wp, *accs)
+
+
+def self_kernel(chunk, per, groups, ids, xo, so, unused, mine, theirs, terms):
     terms[...] = jnp.dot(xo[:groups * UNIT, :], so[...], preferred_element_type=jnp.float32)
     for j in range(per):
         here = slice(j * UNIT, (j + 1) * UNIT)
         at = pl.multiple_of(group_of(ids[0], chunk * per + j, groups) * UNIT, UNIT)
-        out[here, :] += terms[pl.ds(at, UNIT), :]
+        mine[here, :] = terms[pl.ds(at, UNIT), :]
         at = pl.multiple_of(group_of(1 - ids[0], chunk * per + j, groups) * UNIT, UNIT)
         theirs[here, :] = terms[pl.ds(at, UNIT), :]
 
 
-def own_terms(chunk, per, groups, slots, ids, accs, wo, wp, xo, so):
-    hidden = wo.shape[1]
-    rows = per * UNIT
+def self_terms(chunk, per, groups, ids, xo, so, after):
+    rows, hidden = per * UNIT, so.shape[1]
     smem = pl.BlockSpec(memory_space=pltpu.SMEM)
     vmem = pl.BlockSpec(memory_space=pltpu.VMEM)
     return pl.pallas_call(
-        functools.partial(own_kernel, chunk, per, groups, len(accs)),
-        out_shape=[
-            jax.ShapeDtypeStruct((slots * rows, hidden), jnp.float32),
-            jax.ShapeDtypeStruct((rows, hidden), jnp.float32),
-        ],
-        in_specs=[smem] + [vmem] * (4 + len(accs)),
+        functools.partial(self_kernel, chunk, per, groups),
+        out_shape=[jax.ShapeDtypeStruct((rows, hidden), jnp.float32)] * 2,
+        in_specs=[smem, vmem, vmem, vmem],
         out_specs=[vmem] * 2,
         scratch_shapes=[pltpu.VMEM((groups * UNIT, hidden), jnp.float32)],
-        compiler_params=pltpu.CompilerParams(vmem_limit_bytes=(12 << 20) + accs[0].size * 4 * len(accs)),
-        cost_estimate=pl.CostEstimate(
-            flops=4 * slots * rows * PART * len(accs) * hidden, bytes_accessed=2 << 20, transcendentals=0),
-        name="own_terms",
-    )(ids, wo, wp, xo, so, *accs)
+        compiler_params=pltpu.CompilerParams(vmem_limit_bytes=32 * 1024 * 1024),
+        name="self_terms",
+    )(ids, xo, so, after)
 
 
 def combine_kernel(slots, rows, ways, own, *refs):
@@ -406,8 +418,8 @@
 def hidden_kernel(chunks, parts, rows, *refs):
     out = refs[chunks * parts + 1]
     for c in range(chunks):
-        own, self, coded = refs[c * parts], refs[c * parts + 1], refs[c * parts + 2:(c + 1) * parts]
-        total = own[:rows, :] + self[...]
+        own, mine, theirs, coded = *refs[c * parts:c * parts + 3], refs[c * parts + 3:(c + 1) * parts]
+        total = own[:rows, :] + (mine[...] + theirs[...])
         for a in coded:
             total = total + read_coded(a, 1, rows)(0)
         out[c * rows:(c + 1) * rows, :] = jnp.maximum(total, 0.0).astype(jnp.bfloat16)
@@ -519,8 +531,7 @@
             2: sent_terms(size, slots, rows, near, wo, wp),
             3: sent_terms(0, slots, rows, far, wo, wp),
         }
-        parts[0], theirs = own_terms(chunk, per, groups, slots, ids, mine, wo, wp, xo, so)
-        self = lax.ppermute(theirs, "feat", swap)
+        parts[0] = own_terms(size, mine, wo, wp)
         got = exchange(parts, 1, n, (1, 2, 3))
         stride = 4
         for radix in radices[1:]:
@@ -528,7 +539,9 @@
             parts = combine(n // stride, per * UNIT, ways, got[0], got[1:])
             got = exchange(parts, stride, n, (2, 3, 1) if ways == 4 else (1,))
             stride *= ways
-        done.append([got[0], self] + got[1:])
+        self_here, self_there = self_terms(chunk, per, groups, ids, xo, so, parts[0])
+        self_other = lax.ppermute(self_there, "feat", swap)
+        done.append([got[0], self_here, self_other] + got[1:])
     sel, front, adj_received = selection(groups, ids, send_list, send_count, adj_two)
     own = hidden_rows(done, per * UNIT, sel)
     other = lax.ppermute(own, "feat", swap)

time: 41.4 us -> 41.7 us (level)
    pallas_call x1 -> x2, Pallas kernels: 1.04 us -> 1.19 us  [the longest x1 0.74 us: self_terms(): pl.pallas_call(functools.partial(self_kernel, chunk, per, groups), out_sh...]
  transfers between devices with their start and end apart: 10 -> 10, of which waited for: 5 -> 4; matrix products, arithmetic and copies ran while one was open for 0% -> 0% of each run, Pallas kernels for 32% -> 29%
where the time goes in v24:
time: 41.7 us
  Pallas kernels  14.7 us (35%)
  starting transfers between devices  9.72 us (23%)
  blocking collectives  9.67 us (23%)
  waiting for transfers between devices  7.31 us (18%)
    all_to_all x1, blocking collectives, body(): lax.all_to_all(send, 'dom', 0, 0, axis_index_groups=[group_order(n)], til...  9.67 us
    ppermute x6, starting transfers between devices, exchange(): lax.ppermute(parts[k], 'dom', [(i, i ^ k * stride) for i in range(n)])  9.07 us
    pallas_call x3, Pallas kernels, gathered_sums(): pl.pallas_call(functools.partial(tiles_kernel, kind, used), out_shape=[su...  7.31 us
    ppermute x6, waiting for transfers between devices, exchange(): lax.ppermute(parts[k], 'dom', [(i, i ^ k * stride) for i in range(n)])  6.11 us
    pallas_call x1, Pallas kernels, plan(): pl.pallas_call(functools.partial(plan_kernel, chunks, per, n, radix, n_sr...  2.55 us
    pallas_call x3, Pallas kernels, sent_terms(): pl.pallas_call(functools.partial(sent_kernel, first, slots, rows, len(acc...  1.56 us
    ppermute x1, waiting for transfers between devices, body(): other = lax.ppermute(own, 'feat', swap)  1.19 us
    pallas_call x1, Pallas kernels, logits_of(): pl.pallas_call(logits_kernel, out_shape=jax.ShapeDtypeStruct((adj_receive...  0.98 us
  transfers between devices with their start and end apart: 10, of which 4 were waited for; matrix products, arithmetic and copies ran while one was open for 0% of the time, Pallas kernels for 29%

profile of v24, /device:TPU:0, one launch (start us, length us, event | category | flops | bytes accessed | tf_op | source)
XLA Modules:
  0.0 41.7 jit_solution(10672739672180435499)
XLA Ops:
  0.0 0.5 %collective-permute-start.1 = (bf16[1024,512]{1,0:T(8,128)(2,1)}, bf16[1024,512]{1,0:T(8,128)(2,1)S(1)}, u32[]{:S(2)}, u32[]{:S(2)}) collective-permute-start(bf16[1024,512]{1,0:T(8,128)(2,1)} %xo.1), channel_id=1, source_target_pairs={{0,16},{16,0},{1,17},{17,1},{2,18},{18,2},{3,19},{19,3},{4,20},{20... | collective-permute-start | bytes 3145736 | tf_op jit(solution)/shard_map/ppermute | solution.py:513
  0.5 0.1 collective-permute-start
  0.5 0.1 pad_add_fusion.ids
  0.6 0.0 copy-start
  0.6 2.5 %plan.1 = (s32[2,768]{1,0:T(2,128)S(1)}, bf16[512,16,128]{2,1,0:T(8,128)(2,1)S(1)}, bf16[1024,512]{1,0:T(8,128)(2,1)S(1)}) custom-call(s32[2]{0:T(128)S(1)} %pad_add_fusion.ids, s32[1,128]{1,0:T(1,128)} %bitcast.17, s32[1,128]{1,0:T(1,128)} %bitcast.18, s32[1,128]{1,0:T(1,128)} %bitcast.19, bf16[128,8,16,128]{3,2,1,0:T(8,128)(2,1)} %bitcast.16, ...), custom_call_target="tpu_custom_call" | custom-call | tf_op jit(solution)/shard_map/plan/pallas_call | solution.py:154
  3.1 0.0 collective-permute-done.1.xp
  3.2 2.4 %gathered_sums.5 = (f32[528,256]{1,0:T(8,128)S(1)}, f32[528,256]{1,0:T(8,128)S(1)}, f32[528,256]{1,0:T(8,128)S(1)}, f32[528,256]{1,0:T(8,128)S(1)}) custom-call(s32[2,768]{1,0:T(2,128)S(1)} %get-tuple-element.29.table_v, bf16[512,16,128]{2,1,0:T(8,128)(2,1)S(1)} %get-tuple-element.30.tbuf, bf16[1024,512]{1,0:T(8,128)(2,1)S(1)} %get-tuple-element.31.xo, ...), custom_call_target="tpu_custom_call" | custom-call | flops 715827904 | bytes 4194304 | tf_op jit(solution)/shard_map/gathered_sums/pallas_call | solution.py:280
  5.5 0.0 collective-permute-done.wp
  5.5 0.0 copy-done
  5.5 0.5 %sent_terms.5 = s16[264,256]{1,0:T(8,128)(2,1)S(1)} custom-call(bf16[512,256]{1,0:T(8,128)(2,1)S(1)} %copy-done, bf16[512,256]{1,0:T(8,128)(2,1)S(1)} %collective-permute-done.wp, f32[528,256]{1,0:T(8,128)S(1)} %get-tuple-element.40.refs_0_, f32[528,256]{1,0:T(8,128)S(1)} %get-tuple-element.41.refs_1_, f32[528,256]{1,0:T(8,128)S(1)} %get-tuple-element.42.refs_2_, ...), custom_call_target="tpu_custom_call" | custom-call | flops 268435456 | bytes 2097152 | tf_op jit(solution)/shard_map/sent_terms/pallas_call | solution.py:324
  6.1 3.6 %collective-permute-start.4 = (s16[264,256]{1,0:T(8,128)(2,1)S(1)}, s16[264,256]{1,0:T(8,128)(2,1)S(1)}, u32[]{:S(2)}, u32[]{:S(2)}) collective-permute-start(s16[264,256]{1,0:T(8,128)(2,1)S(1)} %sent_terms.5), channel_id=1, source_target_pairs={{0,3},{1,2},{2,1},{3,0},{4,7},{5,6},{6,5},{7,4},{8,11},{9,10},{10,... | collective-permute-start | bytes 405512 | tf_op jit(solution)/shard_map/ppermute | solution.py:486
  9.7 2.9 %gathered_sums.4 = (f32[528,256]{1,0:T(8,128)S(1)}, f32[528,256]{1,0:T(8,128)S(1)}, f32[528,256]{1,0:T(8,128)S(1)}, f32[528,256]{1,0:T(8,128)S(1)}) custom-call(s32[2,768]{1,0:T(2,128)S(1)} %get-tuple-element.29.table_v, bf16[512,16,128]{2,1,0:T(8,128)(2,1)S(1)} %get-tuple-element.30.tbuf, bf16[1024,512]{1,0:T(8,128)(2,1)S(1)} %get-tuple-element.31.xo, ...), custom_call_target="tpu_custom_call" | custom-call | flops 715827904 | bytes 4194304 | tf_op jit(solution)/shard_map/gathered_sums/pallas_call | solution.py:280
  12.6 0.5 %sent_terms.4 = s16[264,256]{1,0:T(8,128)(2,1)S(1)} custom-call(bf16[512,256]{1,0:T(8,128)(2,1)S(1)} %copy-done, bf16[512,256]{1,0:T(8,128)(2,1)S(1)} %collective-permute-done.wp, f32[528,256]{1,0:T(8,128)S(1)} %get-tuple-element.36.refs_0_, f32[528,256]{1,0:T(8,128)S(1)} %get-tuple-element.37.refs_1_, f32[528,256]{1,0:T(8,128)S(1)} %get-tuple-element.38.refs_2_, ...), custom_call_target="tpu_custom_call" | custom-call | flops 268435456 | bytes 2097152 | tf_op jit(solution)/shard_map/sent_terms/pallas_call | solution.py:324
  13.2 0.9 %collective-permute-start.3 = (s16[264,256]{1,0:T(8,128)(2,1)S(1)}, s16[264,256]{1,0:T(8,128)(2,1)S(1)}, u32[]{:S(2)}, u32[]{:S(2)}) collective-permute-start(s16[264,256]{1,0:T(8,128)(2,1)S(1)} %sent_terms.4), channel_id=1, source_target_pairs={{0,2},{1,3},{2,0},{3,1},{4,6},{5,7},{6,4},{7,5},{8,10},{9,11},{10,... | collective-permute-start | bytes 405512 | tf_op jit(solution)/shard_map/ppermute | solution.py:486
  14.1 0.5 %sent_terms.3 = s16[264,256]{1,0:T(8,128)(2,1)S(1)} custom-call(bf16[512,256]{1,0:T(8,128)(2,1)S(1)} %copy-done, bf16[512,256]{1,0:T(8,128)(2,1)S(1)} %collective-permute-done.wp, f32[528,256]{1,0:T(8,128)S(1)} %get-tuple-element.36.refs_0_, f32[528,256]{1,0:T(8,128)S(1)} %get-tuple-element.37.refs_1_, f32[528,256]{1,0:T(8,128)S(1)} %get-tuple-element.38.refs_2_, ...), custom_call_target="tpu_custom_call" | custom-call | flops 268435456 | bytes 2097152 | tf_op jit(solution)/shard_map/sent_terms/pallas_call | solution.py:324
  14.6 0.0 copy-start.1
  14.6 0.0 copy-start.4
  14.6 0.0 copy-start.5
  14.6 0.0 copy-start.6
  14.6 0.0 copy-start.2
  14.7 0.0 copy-start.3
  14.7 0.1 collective-permute-start.2
  14.7 2.0 %gathered_sums.3 = (f32[528,256]{1,0:T(8,128)S(1)}, f32[528,256]{1,0:T(8,128)S(1)}, f32[528,256]{1,0:T(8,128)S(1)}, f32[528,256]{1,0:T(8,128)S(1)}) custom-call(s32[2,768]{1,0:T(2,128)S(1)} %get-tuple-element.29.table_v, bf16[512,16,128]{2,1,0:T(8,128)(2,1)S(1)} %get-tuple-element.30.tbuf, bf16[1024,512]{1,0:T(8,128)(2,1)S(1)} %get-tuple-element.31.xo, ...), custom_call_target="tpu_custom_call" | custom-call | flops 715827904 | bytes 4194304 | tf_op jit(solution)/shard_map/gathered_sums/pallas_call | solution.py:280
  16.8 0.5 %own_terms.1.own = f32[256,256]{1,0:T(8,128)S(1)} custom-call(bf16[512,256]{1,0:T(8,128)(2,1)S(1)} %copy-done, bf16[512,256]{1,0:T(8,128)(2,1)S(1)} %collective-permute-done.wp, f32[528,256]{1,0:T(8,128)S(1)} %get-tuple-element.32.refs_0_, f32[528,256]{1,0:T(8,128)S(1)} %get-tuple-element.33.refs_1_, f32[528,256]{1,0:T(8,128)S(1)} %get-tuple-element.34.refs_2_, ...), custom_call_target="tpu_custom_call" | custom-call | flops 268435456 | bytes 2097152 | tf_op jit(solution)/shard_map/own_terms/pallas_call | solution.py:348
  17.2 0.0 collective-permute-done.4.refs_2_
  17.3 1.1 %collective-permute-done.3.refs_1_ = s16[264,256]{1,0:T(8,128)(2,1)S(1)} collective-permute-done((s16[264,256]{1,0:T(8,128)(2,1)S(1)}, s16[264,256]{1,0:T(8,128)(2,1)S(1)}, u32[]{:S(2)}, u32[]{:S(2)}) %collective-permute-start.3) | collective-permute-done | bytes 135200 | tf_op jit(solution)/shard_map/ppermute | solution.py:486
  18.4 1.4 %collective-permute-done.2.refs_0_ = s16[264,256]{1,0:T(8,128)(2,1)S(1)} collective-permute-done((s16[264,256]{1,0:T(8,128)(2,1)S(1)}, s16[264,256]{1,0:T(8,128)(2,1)S(1)}, u32[]{:S(2)}, u32[]{:S(2)}) %collective-permute-start.2) | collective-permute-done | bytes 135200 | tf_op jit(solution)/shard_map/ppermute | solution.py:486
  19.7 0.2 combine.1
  19.9 0.0 copy-done.1
  20.0 0.7 %self_terms.1 = (f32[64,256]{1,0:T(8,128)S(1)}, f32[64,256]{1,0:T(8,128)S(1)}) custom-call(s32[2]{0:T(128)S(1)} %pad_add_fusion.ids, bf16[1024,512]{1,0:T(8,128)(2,1)S(1)} %get-tuple-element.31.xo, bf16[512,256]{1,0:T(8,128)(2,1)S(1)} %copy-done.1, f32[64,256]{1,0:T(8,128)S(1)} %get-tuple-element.44.unused.refs_0_), custom_call_target="tpu_custom_call" | custom-call | tf_op jit(solution)/shard_map/self_terms/pallas_call | solution.py:374
  20.7 0.1 collective-permute-start.5
  20.8 3.0 %collective-permute-start.6 = (s16[72,256]{1,0:T(8,128)(2,1)S(1)}, s16[72,256]{1,0:T(8,128)(2,1)S(1)}, u32[]{:S(2)}, u32[]{:S(2)}) collective-permute-start(s16[72,256]{1,0:T(8,128)(2,1)S(1)} %get-tuple-element.47), channel_id=1, source_target_pairs={{0,8},{1,9},{2,10},{3,11},{4,12},{5,13},{6,14},{7,15},{8,0},{9,1},... | collective-permute-start | bytes 110600 | tf_op jit(solution)/shard_map/ppermute | solution.py:486
  23.8 1.4 %collective-permute-start.7 = (s16[72,256]{1,0:T(8,128)(2,1)S(1)}, s16[72,256]{1,0:T(8,128)(2,1)S(1)}, u32[]{:S(2)}, u32[]{:S(2)}) collective-permute-start(s16[72,256]{1,0:T(8,128)(2,1)S(1)} %get-tuple-element.48), channel_id=1, source_target_pairs={{0,12},{1,13},{2,14},{3,15},{4,8},{5,9},{6,10},{7,11},{8,4},{9,5},... | collective-permute-start | bytes 110600 | tf_op jit(solution)/shard_map/ppermute | solution.py:486
  25.2 0.0 collective-permute-start.8
  25.2 0.0 copy-done.4
  25.2 0.0 copy-done.5
  25.2 0.0 copy-done.6
  25.3 0.7 %selection.1 = (bf16[128,128]{1,0:T(8,128)(2,1)S(1)}, bf16[128,128]{1,0:T(8,128)(2,1)S(1)}, bf16[64,128]{1,0:T(8,128)(2,1)S(1)}) custom-call(s32[2]{0:T(128)S(1)} %pad_add_fusion.ids, s32[16,8,16]{2,1,0:T(8,128)S(1)} %bitcast.15, s32[16,16]{1,0:T(8,128)S(1)} %copy-done.6, bf16[64,256]{1,0:T(8,128)(2,1)S(1)} %copy-done.5), custom_call_target="tpu_custom_call" | custom-call | tf_op jit(solution)/shard_map/selection/pallas_call | solution.py:210
  26.0 0.0 collective-permute-done.6.refs_3_
  26.0 3.6 %collective-permute-done.7.refs_4_ = s16[72,256]{1,0:T(8,128)(2,1)S(1)} collective-permute-done((s16[72,256]{1,0:T(8,128)(2,1)S(1)}, s16[72,256]{1,0:T(8,128)(2,1)S(1)}, u32[]{:S(2)}, u32[]{:S(2)}) %collective-permute-start.7) | collective-permute-done | bytes 36896 | tf_op jit(solution)/shard_map/ppermute | solution.py:486
  29.6 0.0 collective-permute-done.8.refs_5_
  29.6 0.0 collective-permute-done.5.refs_2_
  29.6 0.1 hidden_rows.1.own
  29.6 0.1 collective-permute-start.9
  29.7 1.2 %collective-permute-done.9.other = bf16[64,256]{1,0:T(8,128)(2,1)S(1)} collective-permute-done((bf16[64,256]{1,0:T(8,128)(2,1)S(1)}, bf16[64,256]{1,0:T(8,128)(2,1)S(1)}, u32[]{:S(2)}, u32[]{:S(2)}) %collective-permute-start.9) | collective-permute-done | bytes 32800 | tf_op jit(solution)/shard_map/ppermute | solution.py:547
  30.9 0.1 rows_to_send.1
  31.1 9.7 %all_to_all.11 = bf16[16,8,256]{2,1,0:T(8,128)(2,1)S(1)} all-to-all(bf16[16,8,256]{2,1,0:T(8,128)(2,1)S(1)} %bitcast.11), channel_id=1, replica_groups={{15,14,13,12,11,10,9,8,7,6,5,4,3,2,1,0},{31,30,29,28,27,26,25,24,23,22,..., dimensions={0} | all-to-all | bytes 131072 | tf_op jit(solution)/shard_map/all_to_all | solution.py:549
  40.7 0.0 copy-done.2
  40.7 0.0 copy-done.3
  40.7 1.0 %logits.1 = f32[64,172]{1,0:T(8,128)} custom-call(bf16[64,256]{1,0:T(8,128)(2,1)S(1)} %hidden_rows.1.own, bf16[64,256]{1,0:T(8,128)(2,1)S(1)} %collective-permute-done.9.other, bf16[128,256]{1,0:T(8,128)(2,1)S(1)} %bitcast.12, bf16[128,128]{1,0:T(8,128)(2,1)S(1)} %get-tuple-element.51.front, bf16[64,128]{1,0:T(8,128)(2,1)S(1)} %get-tuple-element.52.adj_received, ...), custom_call_target="tpu_custom_call" | custom-call | tf_op jit(solution)/shard_map/logits/pallas_call | solution.py:473
Async XLA Ops:
  0.0 3.1 %collective-permute-start.1 = (bf16[1024,512]{1,0:T(8,128)(2,1)}, bf16[1024,512]{1,0:T(8,128)(2,1)S(1)}, u32[]{:S(2)}, u32[]{:S(2)}) collective-permute-start(bf16[1024,512]{1,0:T(8,128)(2,1)} %xo.1), channel_id=1, source_target_pairs={{0,16},{16,0},{1,17},{17,1},{2,18},{18,2},{3,19},{19,3},{4,20},{20... | collective-permute-start | bytes 3145736 | tf_op jit(solution)/shard_map/ppermute | solution.py:513
  0.5 5.1 %collective-permute-start = (bf16[512,256]{1,0:T(8,128)(2,1)}, bf16[512,256]{1,0:T(8,128)(2,1)S(1)}, u32[]{:S(2)}, u32[]{:S(2)}) collective-permute-start(bf16[512,256]{1,0:T(8,128)(2,1)} %wo.7), channel_id=1, source_target_pairs={{0,16},{16,0},{1,17},{17,1},{2,18},{18,2},{3,19},{19,3},{4,20},{20... | collective-permute-start | bytes 786440 | tf_op jit(solution)/shard_map/ppermute | solution.py:514
  0.6 5.0 %copy-start = (bf16[512,256]{1,0:T(8,128)(2,1)S(1)}, bf16[512,256]{1,0:T(8,128)(2,1)}, u32[]{:S(2)}) copy-start(bf16[512,256]{1,0:T(8,128)(2,1)} %wo.7) | copy-start | bytes 786436
  6.1 11.2 %collective-permute-start.4 = (s16[264,256]{1,0:T(8,128)(2,1)S(1)}, s16[264,256]{1,0:T(8,128)(2,1)S(1)}, u32[]{:S(2)}, u32[]{:S(2)}) collective-permute-start(s16[264,256]{1,0:T(8,128)(2,1)S(1)} %sent_terms.5), channel_id=1, source_target_pairs={{0,3},{1,2},{2,1},{3,0},{4,7},{5,6},{6,5},{7,4},{8,11},{9,10},{10,... | collective-permute-start | bytes 405512 | tf_op jit(solution)/shard_map/ppermute | solution.py:486
  13.2 5.2 %collective-permute-start.3 = (s16[264,256]{1,0:T(8,128)(2,1)S(1)}, s16[264,256]{1,0:T(8,128)(2,1)S(1)}, u32[]{:S(2)}, u32[]{:S(2)}) collective-permute-start(s16[264,256]{1,0:T(8,128)(2,1)S(1)} %sent_terms.4), channel_id=1, source_target_pairs={{0,2},{1,3},{2,0},{3,1},{4,6},{5,7},{6,4},{7,5},{8,10},{9,11},{10,... | collective-permute-start | bytes 405512 | tf_op jit(solution)/shard_map/ppermute | solution.py:486
  14.6 5.4 %copy-start.1 = (bf16[512,256]{1,0:T(8,128)(2,1)S(1)}, bf16[512,256]{1,0:T(8,128)(2,1)}, u32[]{:S(2)}) copy-start(bf16[512,256]{1,0:T(8,128)(2,1)} %so.1) | copy-start | bytes 786436
  14.6 10.6 %copy-start.4 = (s32[16,16,8]{1,2,0:T(8,128)S(1)}, s32[16,16,8]{1,2,0:T(8,128)}, u32[]{:S(2)}) copy-start(s32[16,16,8]{1,2,0:T(8,128)} %param.19) | copy-start | bytes 24580
  14.6 10.6 %copy-start.5 = (bf16[64,256]{1,0:T(8,128)(2,1)S(1)}, bf16[64,256]{1,0:T(8,128)(2,1)}, u32[]{:S(2)}) copy-start(bf16[64,256]{1,0:T(8,128)(2,1)} %adj.1) | copy-start | bytes 98308
  14.6 10.6 %copy-start.6 = (s32[16,16]{1,0:T(8,128)S(1)}, s32[16,16]{1,0:T(8,128)}, u32[]{:S(2)}) copy-start(s32[16,16]{1,0:T(8,128)} %counts.1) | copy-start | bytes 3076
  14.6 26.1 %copy-start.2 = (bf16[256,172]{0,1:T(8,128)(2,1)S(1)}, bf16[256,172]{0,1:T(8,128)(2,1)}, u32[]{:S(2)}) copy-start(bf16[256,172]{0,1:T(8,128)(2,1)} %param.22) | copy-start | bytes 264196
  14.7 26.1 %copy-start.3 = (bf16[256,172]{0,1:T(8,128)(2,1)S(1)}, bf16[256,172]{0,1:T(8,128)(2,1)}, u32[]{:S(2)}) copy-start(bf16[256,172]{0,1:T(8,128)(2,1)} %param.23) | copy-start | bytes 264196
  14.7 5.1 %collective-permute-start.2 = (s16[264,256]{1,0:T(8,128)(2,1)S(1)}, s16[264,256]{1,0:T(8,128)(2,1)S(1)}, u32[]{:S(2)}, u32[]{:S(2)}) collective-permute-start(s16[264,256]{1,0:T(8,128)(2,1)S(1)} %sent_terms.3), channel_id=1, source_target_pairs={{0,1},{1,0},{2,3},{3,2},{4,5},{5,4},{6,7},{7,6},{8,9},{9,8},{10,11... | collective-permute-start | bytes 405512 | tf_op jit(solution)/shard_map/ppermute | solution.py:486
  20.7 8.9 %collective-permute-start.5 = (f32[64,256]{1,0:T(8,128)S(1)}, f32[64,256]{1,0:T(8,128)S(1)}, u32[]{:S(2)}, u32[]{:S(2)}) collective-permute-start(f32[64,256]{1,0:T(8,128)S(1)} %get-tuple-element.46), channel_id=1, source_target_pairs={{0,16},{16,0},{1,17},{17,1},{2,18},{18,2},{3,19},{19,3},{4,20},{20... | collective-permute-start | bytes 196616 | tf_op jit(solution)/shard_map/ppermute | solution.py:543
  20.8 5.2 %collective-permute-start.6 = (s16[72,256]{1,0:T(8,128)(2,1)S(1)}, s16[72,256]{1,0:T(8,128)(2,1)S(1)}, u32[]{:S(2)}, u32[]{:S(2)}) collective-permute-start(s16[72,256]{1,0:T(8,128)(2,1)S(1)} %get-tuple-element.47), channel_id=1, source_target_pairs={{0,8},{1,9},{2,10},{3,11},{4,12},{5,13},{6,14},{7,15},{8,0},{9,1},... | collective-permute-start | bytes 110600 | tf_op jit(solution)/shard_map/ppermute | solution.py:486
  23.8 5.8 %collective-permute-start.7 = (s16[72,256]{1,0:T(8,128)(2,1)S(1)}, s16[72,256]{1,0:T(8,128)(2,1)S(1)}, u32[]{:S(2)}, u32[]{:S(2)}) collective-permute-start(s16[72,256]{1,0:T(8,128)(2,1)S(1)} %get-tuple-element.48), channel_id=1, source_target_pairs={{0,12},{1,13},{2,14},{3,15},{4,8},{5,9},{6,10},{7,11},{8,4},{9,5},... | collective-permute-start | bytes 110600 | tf_op jit(solution)/shard_map/ppermute | solution.py:486
  25.2 4.4 %collective-permute-start.8 = (s16[72,256]{1,0:T(8,128)(2,1)S(1)}, s16[72,256]{1,0:T(8,128)(2,1)S(1)}, u32[]{:S(2)}, u32[]{:S(2)}) collective-permute-start(s16[72,256]{1,0:T(8,128)(2,1)S(1)} %get-tuple-element.49), channel_id=1, source_target_pairs={{0,4},{1,5},{2,6},{3,7},{4,0},{5,1},{6,2},{7,3},{8,12},{9,13},{10,... | collective-permute-start | bytes 110600 | tf_op jit(solution)/shard_map/ppermute | solution.py:486
  29.6 1.3 %collective-permute-start.9 = (bf16[64,256]{1,0:T(8,128)(2,1)S(1)}, bf16[64,256]{1,0:T(8,128)(2,1)S(1)}, u32[]{:S(2)}, u32[]{:S(2)}) collective-permute-start(bf16[64,256]{1,0:T(8,128)(2,1)S(1)} %hidden_rows.1.own), channel_id=1, source_target_pairs={{0,16},{16,0},{1,17},{17,1},{2,18},{18,2},{3,19},{19,3},{4,20},{20... | collective-permute-start | bytes 98312 | tf_op jit(solution)/shard_map/ppermute | solution.py:547

commit v25 on v21

--- a/solution.py
+++ b/solution.py
@@ -8,8 +8,8 @@
 from jax.sharding import PartitionSpec as P
 
 UNIT = 16
-BLOCK = 8
-STEP = 8
+BLOCK = 4
+STEP = 16
 PART = 256
 CHUNKS = 1
 
@@ -276,7 +276,8 @@
 def weigh(accs, weights, first, count, out):
     size = min(256, count)
 
-    def piece(at):
+    def piece(r, carry):
+        at = r * size if isinstance(r, int) else pl.multiple_of(r * size, size)
         got = jnp.zeros((size, out.shape[1]), jnp.float32)
         for i, acc in enumerate(accs):
             w, h = weights[i * PART // weights[0].shape[0]], i * PART % weights[0].shape[0]
@@ -286,37 +287,38 @@
             got = got + jnp.dot(high, w[h:h + PART, :], preferred_element_type=jnp.float32)
             got = got + jnp.dot(low, w[h:h + PART, :], preferred_element_type=jnp.float32)
         out[pl.ds(at, size), :] = got
+        return carry
 
     if count == size:
-        piece(0)
+        piece(0, 0)
     else:
-        lax.fori_loop(0, count // size, lambda r, carry: (piece(pl.multiple_of(r * size, size)), carry)[1], 0)
-
-
-def sent_kernel(slots, rows, ways, parts, wo, wp, *refs):
-    accs, outs, scratch = refs[:parts], refs[parts:parts + ways - 1], refs[parts + ways - 1:]
-    for k in range(ways - 1, 0, -1):
-        sums, tail = scratch[2 * k - 2:2 * k]
+        lax.fori_loop(0, count // size, piece, 0)
+
+
+def sent_kernel(ks, slots, rows, parts, wo, wp, *refs):
+    accs, outs, scratch = refs[:parts], refs[parts:parts + len(ks)], refs[parts + len(ks):]
+    for i, k in enumerate(ks):
+        sums, tail = scratch[2 * i:2 * i + 2]
         weigh(accs, (wo, wp), k * slots * rows, slots * rows, sums)
-        write_coded(outs[k - 1], tail, slots, rows, lambda s: sums[s * rows:(s + 1) * rows, :])
-
-
-def sent_terms(ways, slots, rows, accs, wo, wp):
+        write_coded(outs[i], tail, slots, rows, lambda s: sums[s * rows:(s + 1) * rows, :])
+
+
+def sent_terms(ks, slots, rows, accs, wo, wp):
     hidden = wo.shape[1]
     vmem = pl.BlockSpec(memory_space=pltpu.VMEM)
     coded = jax.ShapeDtypeStruct((slots * rows + tail_rows(slots), hidden), jnp.int16)
     return pl.pallas_call(
-        functools.partial(sent_kernel, slots, rows, ways, len(accs)),
-        out_shape=[coded] * (ways - 1),
+        functools.partial(sent_kernel, ks, slots, rows, len(accs)),
+        out_shape=[coded] * len(ks),
         in_specs=[vmem] * (2 + len(accs)),
-        out_specs=[vmem] * (ways - 1),
+        out_specs=[vmem] * len(ks),
         scratch_shapes=[
             pltpu.VMEM((slots * rows, hidden), jnp.float32),
             pltpu.VMEM((tail_rows(slots), hidden), jnp.float32),
-        ] * (ways - 1),
+        ] * len(ks),
         compiler_params=pltpu.CompilerParams(vmem_limit_bytes=(20 << 20) + accs[0].size * 4 * len(accs)),
         cost_estimate=pl.CostEstimate(
-            flops=4 * (ways - 1) * slots * rows * PART * len(accs) * hidden, bytes_accessed=6 << 20, transcendentals=0),
+            flops=4 * len(ks) * slots * rows * PART * len(accs) * hidden, bytes_accessed=2 << 20, transcendentals=0),
         name="sent_terms",
     )(wo, wp, *accs)
 
@@ -494,10 +496,12 @@
     for chunk in range(CHUNKS):
         accs = gathered_sums(per, n, tables[chunk], tbufs[chunk], xo, xp)
         slots, rows = n // 4, per * UNIT
-        parts = dict(enumerate(sent_terms(4, slots, rows, accs, wo, wp), 1))
+        parts = {}
+        (parts[3],) = sent_terms((3,), slots, rows, accs, wo, wp)
+        parts[2], parts[1] = sent_terms((2, 1), slots, rows, accs, wo, wp)
         parts[0], theirs = own_terms(chunk, per, groups, slots, ids, accs, wo, wp, xo, so)
         self = lax.ppermute(theirs, "feat", swap)
-        got = exchange(parts, 1, n, (3, 2, 1))
+        got = exchange(parts, 1, n, (1, 2, 3))
         stride = 4
         for radix in radices[1:]:
             ways = 1 << radix

time: 41.1 us -> 40.6 us (0.988)
    pallas_call x1 -> x2, Pallas kernels: 1.13 us -> 1.37 us  [sent_terms(): pl.pallas_call(functools.partial(sent_kernel, ks, slots, rows, len(accs))...]
  transfers between devices with their start and end apart: 10 -> 10, of which waited for: 6 -> 5; matrix products, arithmetic and copies ran while one was open for 0% -> 0% of each run, Pallas kernels for 22% -> 24%
where the time goes in v25:
time: 40.6 us; the launch traced here: 40.5 us
  Pallas kernels  11.4 us (28%)
  starting transfers between devices  10.3 us (25%)
  blocking collectives  9.67 us (24%)
  waiting for transfers between devices  8.89 us (22%)
    all_to_all x1, blocking collectives, body(): lax.all_to_all(send, 'dom', 0, 0, axis_index_groups=[group_order(n)], til...  9.67 us
    ppermute x6, starting transfers between devices, exchange(): lax.ppermute(parts[k], 'dom', [(i, i ^ k * stride) for i in range(n)])  9.62 us
    ppermute x6, waiting for transfers between devices, exchange(): lax.ppermute(parts[k], 'dom', [(i, i ^ k * stride) for i in range(n)])  7.69 us
    pallas_call x1, Pallas kernels, gathered_sums(): pl.pallas_call(tiles_kernel, out_shape=[sums] * parts, in_specs=[vmem] *...  4.43 us
    pallas_call x1, Pallas kernels, plan(): pl.pallas_call(functools.partial(plan_kernel, chunks, per, n, radix, n_sr...  2.55 us
    pallas_call x2, Pallas kernels, sent_terms(): pl.pallas_call(functools.partial(sent_kernel, ks, slots, rows, len(accs))...  1.37 us
    ppermute x1, waiting for transfers between devices, body(): other = lax.ppermute(own, 'feat', swap)  1.19 us
    pallas_call x1, Pallas kernels, own_terms(): pl.pallas_call(functools.partial(own_kernel, chunk, per, groups, len(accs...  1.04 us
  transfers between devices with their start and end apart: 10, of which 5 were waited for; matrix products, arithmetic and copies ran while one was open for 0% of the time, Pallas kernels for 24%

profile of v25, /device:TPU:0, one launch (start us, length us, event | category | flops | bytes accessed | tf_op | source)
XLA Modules:
  0.0 40.5 jit_solution(13355360518579010546)
XLA Ops:
  0.0 0.5 %collective-permute-start.1 = (bf16[1024,512]{1,0:T(8,128)(2,1)}, bf16[1024,512]{1,0:T(8,128)(2,1)S(1)}, u32[]{:S(2)}, u32[]{:S(2)}) collective-permute-start(bf16[1024,512]{1,0:T(8,128)(2,1)} %xo.1), channel_id=1, source_target_pairs={{0,16},{16,0},{1,17},{17,1},{2,18},{18,2},{3,19},{19,3},{4,20},{20... | collective-permute-start | bytes 3145736 | tf_op jit(solution)/shard_map/ppermute | solution.py:487
  0.5 0.1 collective-permute-start
  0.5 0.1 pad_add_fusion.ids
  0.6 2.5 %plan.1 = (s32[2,640]{1,0:T(2,128)S(1)}, bf16[512,16,128]{2,1,0:T(8,128)(2,1)S(1)}, bf16[1024,512]{1,0:T(8,128)(2,1)S(1)}) custom-call(s32[2]{0:T(128)S(1)} %pad_add_fusion.ids, s32[1,128]{1,0:T(1,128)} %bitcast.17, s32[1,128]{1,0:T(1,128)} %bitcast.18, s32[1,128]{1,0:T(1,128)} %bitcast.19, bf16[128,8,16,128]{3,2,1,0:T(8,128)(2,1)} %bitcast.16, ...), custom_call_target="tpu_custom_call" | custom-call | tf_op jit(solution)/shard_map/plan/pallas_call | solution.py:135
  3.1 0.0 collective-permute-done.1.xp
  3.2 0.0 copy-start
  3.2 4.4 %gathered_sums.1 = (f32[1040,256]{1,0:T(8,128)S(1)}, f32[1040,256]{1,0:T(8,128)S(1)}, f32[1040,256]{1,0:T(8,128)S(1)}, f32[1040,256]{1,0:T(8,128)S(1)}) custom-call(s32[2,640]{1,0:T(2,128)S(1)} %get-tuple-element.24.table_v, bf16[512,16,128]{2,1,0:T(8,128)(2,1)S(1)} %get-tuple-element.25.tbuf, bf16[1024,512]{1,0:T(8,128)(2,1)S(1)} %get-tuple-element.23.xo, ...), custom_call_target="tpu_custom_call" | custom-call | flops 2147483648 | bytes 8388608 | tf_op jit(solution)/shard_map/gathered_sums/pallas_call | solution.py:260
  7.6 0.0 collective-permute-done.wp
  7.6 0.0 copy-done
  7.6 0.5 %sent_terms.3 = s16[264,256]{1,0:T(8,128)(2,1)S(1)} custom-call(bf16[512,256]{1,0:T(8,128)(2,1)S(1)} %copy-done, bf16[512,256]{1,0:T(8,128)(2,1)S(1)} %collective-permute-done.wp, f32[1040,256]{1,0:T(8,128)S(1)} %get-tuple-element.26.refs_0_, f32[1040,256]{1,0:T(8,128)S(1)} %get-tuple-element.27.refs_1_, f32[1040,256]{1,0:T(8,128)S(1)} %get-tuple-element.28.refs_2_, ...), custom_call_target="tpu_custom_call" | custom-call | flops 268435456 | bytes 2097152 | tf_op jit(solution)/shard_map/sent_terms/pallas_call | solution.py:310
  8.2 0.0 copy-start.1
  8.2 4.3 %collective-permute-start.4 = (s16[264,256]{1,0:T(8,128)(2,1)S(1)}, s16[264,256]{1,0:T(8,128)(2,1)S(1)}, u32[]{:S(2)}, u32[]{:S(2)}) collective-permute-start(s16[264,256]{1,0:T(8,128)(2,1)S(1)} %sent_terms.3), channel_id=1, source_target_pairs={{0,3},{1,2},{2,1},{3,0},{4,7},{5,6},{6,5},{7,4},{8,11},{9,10},{10,... | collective-permute-start | bytes 405512 | tf_op jit(solution)/shard_map/ppermute | solution.py:460
  12.5 0.8 %sent_terms.2 = (s16[264,256]{1,0:T(8,128)(2,1)S(1)}, s16[264,256]{1,0:T(8,128)(2,1)S(1)}) custom-call(bf16[512,256]{1,0:T(8,128)(2,1)S(1)} %copy-done, bf16[512,256]{1,0:T(8,128)(2,1)S(1)} %collective-permute-done.wp, f32[1040,256]{1,0:T(8,128)S(1)} %get-tuple-element.26.refs_0_, f32[1040,256]{1,0:T(8,128)S(1)} %get-tuple-element.27.refs_1_, ...), custom_call_target="tpu_custom_call" | custom-call | flops 536870912 | bytes 2097152 | tf_op jit(solution)/shard_map/sent_terms/pallas_call | solution.py:310
  13.3 0.6 %collective-permute-start.2 = (s16[264,256]{1,0:T(8,128)(2,1)S(1)}, s16[264,256]{1,0:T(8,128)(2,1)S(1)}, u32[]{:S(2)}, u32[]{:S(2)}) collective-permute-start(s16[264,256]{1,0:T(8,128)(2,1)S(1)} %get-tuple-element.31), channel_id=1, source_target_pairs={{0,1},{1,0},{2,3},{3,2},{4,5},{5,4},{6,7},{7,6},{8,9},{9,8},{10,11... | collective-permute-start | bytes 405512 | tf_op jit(solution)/shard_map/ppermute | solution.py:460
  13.9 0.0 copy-start.4
  13.9 0.0 copy-start.5
  13.9 0.0 copy-start.6
  13.9 0.1 collective-permute-start.3
  14.0 0.0 copy-done.1
  14.0 1.0 %own_terms.1 = (f32[256,256]{1,0:T(8,128)S(1)}, f32[64,256]{1,0:T(8,128)S(1)}) custom-call(s32[2]{0:T(128)S(1)} %pad_add_fusion.ids, bf16[512,256]{1,0:T(8,128)(2,1)S(1)} %copy-done, bf16[512,256]{1,0:T(8,128)(2,1)S(1)} %collective-permute-done.wp, bf16[1024,512]{1,0:T(8,128)(2,1)S(1)} %get-tuple-element.23.xo, bf16[512,256]{1,0:T(8,128)(2,1)S(1)} %copy-done.1, ...), custom_call_target="tpu_custom_call" | custom-call | flops 268435456 | bytes 2097152 | tf_op jit(solution)/shard_map/own_terms/pallas_call | solution.py:343
  15.1 0.0 copy-start.2
  15.1 0.0 copy-start.3
  15.1 0.1 collective-permute-start.5
  15.2 1.5 %collective-permute-done.4.refs_2_ = s16[264,256]{1,0:T(8,128)(2,1)S(1)} collective-permute-done((s16[264,256]{1,0:T(8,128)(2,1)S(1)}, s16[264,256]{1,0:T(8,128)(2,1)S(1)}, u32[]{:S(2)}, u32[]{:S(2)}) %collective-permute-start.4) | collective-permute-done | bytes 135200 | tf_op jit(solution)/shard_map/ppermute | solution.py:460
  16.6 2.4 %collective-permute-done.2.refs_0_ = s16[264,256]{1,0:T(8,128)(2,1)S(1)} collective-permute-done((s16[264,256]{1,0:T(8,128)(2,1)S(1)}, s16[264,256]{1,0:T(8,128)(2,1)S(1)}, u32[]{:S(2)}, u32[]{:S(2)}) %collective-permute-start.2) | collective-permute-done | bytes 135200 | tf_op jit(solution)/shard_map/ppermute | solution.py:460
  19.0 0.1 collective-permute-done.3.refs_1_
  19.1 0.2 combine.1
  19.3 3.3 %collective-permute-start.6 = (s16[72,256]{1,0:T(8,128)(2,1)S(1)}, s16[72,256]{1,0:T(8,128)(2,1)S(1)}, u32[]{:S(2)}, u32[]{:S(2)}) collective-permute-start(s16[72,256]{1,0:T(8,128)(2,1)S(1)} %get-tuple-element.35), channel_id=1, source_target_pairs={{0,8},{1,9},{2,10},{3,11},{4,12},{5,13},{6,14},{7,15},{8,0},{9,1},... | collective-permute-start | bytes 110600 | tf_op jit(solution)/shard_map/ppermute | solution.py:460
  22.7 1.0 %collective-permute-start.7 = (s16[72,256]{1,0:T(8,128)(2,1)S(1)}, s16[72,256]{1,0:T(8,128)(2,1)S(1)}, u32[]{:S(2)}, u32[]{:S(2)}) collective-permute-start(s16[72,256]{1,0:T(8,128)(2,1)S(1)} %get-tuple-element.36), channel_id=1, source_target_pairs={{0,12},{1,13},{2,14},{3,15},{4,8},{5,9},{6,10},{7,11},{8,4},{9,5},... | collective-permute-start | bytes 110600 | tf_op jit(solution)/shard_map/ppermute | solution.py:460
  23.6 0.3 collective-permute-start.8
  23.9 0.0 copy-done.4
  23.9 0.0 copy-done.5
  23.9 0.0 copy-done.6
  23.9 0.7 %selection.1 = (bf16[128,128]{1,0:T(8,128)(2,1)S(1)}, bf16[128,128]{1,0:T(8,128)(2,1)S(1)}, bf16[64,128]{1,0:T(8,128)(2,1)S(1)}) custom-call(s32[2]{0:T(128)S(1)} %pad_add_fusion.ids, s32[16,8,16]{2,1,0:T(8,128)S(1)} %bitcast.15, s32[16,16]{1,0:T(8,128)S(1)} %copy-done.6, bf16[64,256]{1,0:T(8,128)(2,1)S(1)} %copy-done.5), custom_call_target="tpu_custom_call" | custom-call | tf_op jit(solution)/shard_map/selection/pallas_call | solution.py:191
  24.6 0.0 collective-permute-done.5.refs_1_
  24.7 0.0 collective-permute-done.6.refs_2_
  24.7 3.8 %collective-permute-done.7.refs_3_ = s16[72,256]{1,0:T(8,128)(2,1)S(1)} collective-permute-done((s16[72,256]{1,0:T(8,128)(2,1)S(1)}, s16[72,256]{1,0:T(8,128)(2,1)S(1)}, u32[]{:S(2)}, u32[]{:S(2)}) %collective-permute-start.7) | collective-permute-done | bytes 36896 | tf_op jit(solution)/shard_map/ppermute | solution.py:460
  28.4 0.0 collective-permute-done.8.refs_4_
  28.5 0.1 collective-permute-start.9
  28.5 1.2 %collective-permute-done.9.other = bf16[64,256]{1,0:T(8,128)(2,1)S(1)} collective-permute-done((bf16[64,256]{1,0:T(8,128)(2,1)S(1)}, bf16[64,256]{1,0:T(8,128)(2,1)S(1)}, u32[]{:S(2)}, u32[]{:S(2)}) %collective-permute-start.9) | collective-permute-done | bytes 32800 | tf_op jit(solution)/shard_map/ppermute | solution.py:514
  29.7 0.1 rows_to_send.1
  29.9 9.7 %all_to_all.11 = bf16[16,8,256]{2,1,0:T(8,128)(2,1)S(1)} all-to-all(bf16[16,8,256]{2,1,0:T(8,128)(2,1)S(1)} %bitcast.11), channel_id=1, replica_groups={{15,14,13,12,11,10,9,8,7,6,5,4,3,2,1,0},{31,30,29,28,27,26,25,24,23,22,..., dimensions={0} | all-to-all | bytes 131072 | tf_op jit(solution)/shard_map/all_to_all | solution.py:516
  39.6 0.0 copy-done.2
  39.6 0.0 copy-done.3
  39.6 1.0 %logits.1 = f32[64,172]{1,0:T(8,128)} custom-call(bf16[64,256]{1,0:T(8,128)(2,1)S(1)} %hidden_rows.1.own, bf16[64,256]{1,0:T(8,128)(2,1)S(1)} %collective-permute-done.9.other, bf16[128,256]{1,0:T(8,128)(2,1)S(1)} %bitcast.12, bf16[128,128]{1,0:T(8,128)(2,1)S(1)} %get-tuple-element.39.front, bf16[64,128]{1,0:T(8,128)(2,1)S(1)} %get-tuple-element.40.adj_received, ...), custom_call_target="tpu_custom_call" | custom-call | tf_op jit(solution)/shard_map/logits/pallas_call | solution.py:447
  (1 shorter events, 0.0 us)
Async XLA Ops:
  0.0 3.1 %collective-permute-start.1 = (bf16[1024,512]{1,0:T(8,128)(2,1)}, bf16[1024,512]{1,0:T(8,128)(2,1)S(1)}, u32[]{:S(2)}, u32[]{:S(2)}) collective-permute-start(bf16[1024,512]{1,0:T(8,128)(2,1)} %xo.1), channel_id=1, source_target_pairs={{0,16},{16,0},{1,17},{17,1},{2,18},{18,2},{3,19},{19,3},{4,20},{20... | collective-permute-start | bytes 3145736 | tf_op jit(solution)/shard_map/ppermute | solution.py:487
  0.5 7.2 %collective-permute-start = (bf16[512,256]{1,0:T(8,128)(2,1)}, bf16[512,256]{1,0:T(8,128)(2,1)S(1)}, u32[]{:S(2)}, u32[]{:S(2)}) collective-permute-start(bf16[512,256]{1,0:T(8,128)(2,1)} %wo.5), channel_id=1, source_target_pairs={{0,16},{16,0},{1,17},{17,1},{2,18},{18,2},{3,19},{19,3},{4,20},{20... | collective-permute-start | bytes 786440 | tf_op jit(solution)/shard_map/ppermute | solution.py:488
  3.2 4.5 %copy-start = (bf16[512,256]{1,0:T(8,128)(2,1)S(1)}, bf16[512,256]{1,0:T(8,128)(2,1)}, u32[]{:S(2)}) copy-start(bf16[512,256]{1,0:T(8,128)(2,1)} %wo.5) | copy-start | bytes 786436
  8.2 5.9 %copy-start.1 = (bf16[512,256]{1,0:T(8,128)(2,1)S(1)}, bf16[512,256]{1,0:T(8,128)(2,1)}, u32[]{:S(2)}) copy-start(bf16[512,256]{1,0:T(8,128)(2,1)} %so.1) | copy-start | bytes 786436
  8.2 8.5 %collective-permute-start.4 = (s16[264,256]{1,0:T(8,128)(2,1)S(1)}, s16[264,256]{1,0:T(8,128)(2,1)S(1)}, u32[]{:S(2)}, u32[]{:S(2)}) collective-permute-start(s16[264,256]{1,0:T(8,128)(2,1)S(1)} %sent_terms.3), channel_id=1, source_target_pairs={{0,3},{1,2},{2,1},{3,0},{4,7},{5,6},{6,5},{7,4},{8,11},{9,10},{10,... | collective-permute-start | bytes 405512 | tf_op jit(solution)/shard_map/ppermute | solution.py:460
  13.3 5.7 %collective-permute-start.2 = (s16[264,256]{1,0:T(8,128)(2,1)S(1)}, s16[264,256]{1,0:T(8,128)(2,1)S(1)}, u32[]{:S(2)}, u32[]{:S(2)}) collective-permute-start(s16[264,256]{1,0:T(8,128)(2,1)S(1)} %get-tuple-element.31), channel_id=1, source_target_pairs={{0,1},{1,0},{2,3},{3,2},{4,5},{5,4},{6,7},{7,6},{8,9},{9,8},{10,11... | collective-permute-start | bytes 405512 | tf_op jit(solution)/shard_map/ppermute | solution.py:460
  13.9 10.0 %copy-start.4 = (s32[16,16,8]{1,2,0:T(8,128)S(1)}, s32[16,16,8]{1,2,0:T(8,128)}, u32[]{:S(2)}) copy-start(s32[16,16,8]{1,2,0:T(8,128)} %param.19) | copy-start | bytes 24580
  13.9 10.0 %copy-start.5 = (bf16[64,256]{1,0:T(8,128)(2,1)S(1)}, bf16[64,256]{1,0:T(8,128)(2,1)}, u32[]{:S(2)}) copy-start(bf16[64,256]{1,0:T(8,128)(2,1)} %adj.1) | copy-start | bytes 98308
  13.9 10.0 %copy-start.6 = (s32[16,16]{1,0:T(8,128)S(1)}, s32[16,16]{1,0:T(8,128)}, u32[]{:S(2)}) copy-start(s32[16,16]{1,0:T(8,128)} %counts.1) | copy-start | bytes 3076
  13.9 5.2 %collective-permute-start.3 = (s16[264,256]{1,0:T(8,128)(2,1)S(1)}, s16[264,256]{1,0:T(8,128)(2,1)S(1)}, u32[]{:S(2)}, u32[]{:S(2)}) collective-permute-start(s16[264,256]{1,0:T(8,128)(2,1)S(1)} %get-tuple-element.32), channel_id=1, source_target_pairs={{0,2},{1,3},{2,0},{3,1},{4,6},{5,7},{6,4},{7,5},{8,10},{9,11},{10,... | collective-permute-start | bytes 405512 | tf_op jit(solution)/shard_map/ppermute | solution.py:460
  15.1 24.5 %copy-start.2 = (bf16[256,172]{0,1:T(8,128)(2,1)S(1)}, bf16[256,172]{0,1:T(8,128)(2,1)}, u32[]{:S(2)}) copy-start(bf16[256,172]{0,1:T(8,128)(2,1)} %param.22) | copy-start | bytes 264196
  15.1 24.5 %copy-start.3 = (bf16[256,172]{0,1:T(8,128)(2,1)S(1)}, bf16[256,172]{0,1:T(8,128)(2,1)}, u32[]{:S(2)}) copy-start(bf16[256,172]{0,1:T(8,128)(2,1)} %param.23) | copy-start | bytes 264196
  15.1 9.5 %collective-permute-start.5 = (f32[64,256]{1,0:T(8,128)S(1)}, f32[64,256]{1,0:T(8,128)S(1)}, u32[]{:S(2)}, u32[]{:S(2)}) collective-permute-start(f32[64,256]{1,0:T(8,128)S(1)} %get-tuple-element.34), channel_id=1, source_target_pairs={{0,16},{16,0},{1,17},{17,1},{2,18},{18,2},{3,19},{19,3},{4,20},{20... | collective-permute-start | bytes 196616 | tf_op jit(solution)/shard_map/ppermute | solution.py:503
  19.3 5.3 %collective-permute-start.6 = (s16[72,256]{1,0:T(8,128)(2,1)S(1)}, s16[72,256]{1,0:T(8,128)(2,1)S(1)}, u32[]{:S(2)}, u32[]{:S(2)}) collective-permute-start(s16[72,256]{1,0:T(8,128)(2,1)S(1)} %get-tuple-element.35), channel_id=1, source_target_pairs={{0,8},{1,9},{2,10},{3,11},{4,12},{5,13},{6,14},{7,15},{8,0},{9,1},... | collective-permute-start | bytes 110600 | tf_op jit(solution)/shard_map/ppermute | solution.py:460
  22.7 5.8 %collective-permute-start.7 = (s16[72,256]{1,0:T(8,128)(2,1)S(1)}, s16[72,256]{1,0:T(8,128)(2,1)S(1)}, u32[]{:S(2)}, u32[]{:S(2)}) collective-permute-start(s16[72,256]{1,0:T(8,128)(2,1)S(1)} %get-tuple-element.36), channel_id=1, source_target_pairs={{0,12},{1,13},{2,14},{3,15},{4,8},{5,9},{6,10},{7,11},{8,4},{9,5},... | collective-permute-start | bytes 110600 | tf_op jit(solution)/shard_map/ppermute | solution.py:460
  23.6 4.8 %collective-permute-start.8 = (s16[72,256]{1,0:T(8,128)(2,1)S(1)}, s16[72,256]{1,0:T(8,128)(2,1)S(1)}, u32[]{:S(2)}, u32[]{:S(2)}) collective-permute-start(s16[72,256]{1,0:T(8,128)(2,1)S(1)} %get-tuple-element.37), channel_id=1, source_target_pairs={{0,4},{1,5},{2,6},{3,7},{4,0},{5,1},{6,2},{7,3},{8,12},{9,13},{10,... | collective-permute-start | bytes 110600 | tf_op jit(solution)/shard_map/ppermute | solution.py:460
  28.5 1.3 %collective-permute-start.9 = (bf16[64,256]{1,0:T(8,128)(2,1)S(1)}, bf16[64,256]{1,0:T(8,128)(2,1)S(1)}, u32[]{:S(2)}, u32[]{:S(2)}) collective-permute-start(bf16[64,256]{1,0:T(8,128)(2,1)S(1)} %hidden_rows.1.own), channel_id=1, source_target_pairs={{0,16},{16,0},{1,17},{17,1},{2,18},{18,2},{3,19},{19,3},{4,20},{20... | collective-permute-start | bytes 98312 | tf_op jit(solution)/shard_map/ppermute | solution.py:514

commit v26 on v25

--- a/solution.py
+++ b/solution.py
@@ -10,6 +10,7 @@
 UNIT = 16
 BLOCK = 4
 STEP = 16
+PIECES = 4
 PART = 256
 CHUNKS = 1
 
@@ -71,8 +72,13 @@
     half = groups // 2
     gs = [group_of(core, i, groups) for i in range(half)]
     small = [(src_h, src_v), (rows_h, rows_v), (dst_h, dst_v)]
-    large = [(tw.at[:, g], tbufs[i // per].at[pl.ds(i % per * tiles, tiles)]) for i, g in enumerate(gs)]
-    large += [(xo, xo_out)]
+    some, rows = tiles // PIECES, xo.shape[0] // PIECES
+    large = [
+        (tw.at[pl.ds(q * some, some), g], tbufs[i // per].at[pl.ds(i % per * tiles + q * some, some)])
+        for i, g in enumerate(gs)
+        for q in range(PIECES)
+    ]
+    large += [(xo.at[pl.ds(q * rows, rows)], xo_out.at[pl.ds(q * rows, rows)]) for q in range(PIECES)]
     copies = [pltpu.make_async_copy(a, b, sems.at[i]) for i, (a, b) in enumerate(small + large)]
     for c in copies:
         c.start()
@@ -143,7 +149,7 @@
             pltpu.VMEM((1, tiles), jnp.int32),
             pltpu.VMEM((1, tiles), jnp.int32),
             pltpu.VMEM((1, tiles), jnp.int32),
-            pltpu.SemaphoreType.DMA((3 + half + 1,)),
+            pltpu.SemaphoreType.DMA((3 + (half + 1) * PIECES,)),
         ],
         compiler_params=pltpu.CompilerParams(vmem_limit_bytes=32 * 1024 * 1024),
         name="plan",

time: 40.6 us -> 40.9 us (level)
  Pallas kernels: 11.4 us -> 11.9 us
  starting transfers between devices: 10.3 us -> 9.8 us
    ppermute x6, starting transfers between devices: 9.62 us -> 9.14 us  [exchange(): lax.ppermute(parts[k], 'dom', [(i, i ^ k * stride) for i in range(n)])]
  transfers between devices with their start and end apart: 10 -> 10, of which waited for: 5 -> 5; matrix products, arithmetic and copies ran while one was open for 0% -> 0% of each run, Pallas kernels for 24% -> 25%
where the time goes in v26:
time: 40.9 us; the launch traced here: 40.8 us
  Pallas kernels  11.9 us (29%)
  starting transfers between devices  9.8 us (24%)
  blocking collectives  9.67 us (24%)
  waiting for transfers between devices  9.09 us (22%)
    all_to_all x1, blocking collectives, body(): lax.all_to_all(send, 'dom', 0, 0, axis_index_groups=[group_order(n)], til...  9.67 us
    ppermute x6, starting transfers between devices, exchange(): lax.ppermute(parts[k], 'dom', [(i, i ^ k * stride) for i in range(n)])  9.14 us
    ppermute x6, waiting for transfers between devices, exchange(): lax.ppermute(parts[k], 'dom', [(i, i ^ k * stride) for i in range(n)])  7.89 us
    pallas_call x1, Pallas kernels, gathered_sums(): pl.pallas_call(tiles_kernel, out_shape=[sums] * parts, in_specs=[vmem] *...  4.74 us
    pallas_call x1, Pallas kernels, plan(): pl.pallas_call(functools.partial(plan_kernel, chunks, per, n, radix, n_sr...  2.73 us
    pallas_call x2, Pallas kernels, sent_terms(): pl.pallas_call(functools.partial(sent_kernel, ks, slots, rows, len(accs))...  1.36 us
    ppermute x1, waiting for transfers between devices, body(): other = lax.ppermute(own, 'feat', swap)  1.19 us
    pallas_call x1, Pallas kernels, own_terms(): pl.pallas_call(functools.partial(own_kernel, chunk, per, groups, len(accs...  1.04 us
  transfers between devices with their start and end apart: 10, of which 5 were waited for; matrix products, arithmetic and copies ran while one was open for 0% of the time, Pallas kernels for 25%

profile of v26, /device:TPU:0, one launch (start us, length us, event | category | flops | bytes accessed | tf_op | source)
XLA Modules:
  0.0 40.8 jit_solution(11351117505005644424)
XLA Ops:
  0.0 0.5 %collective-permute-start.1 = (bf16[1024,512]{1,0:T(8,128)(2,1)}, bf16[1024,512]{1,0:T(8,128)(2,1)S(1)}, u32[]{:S(2)}, u32[]{:S(2)}) collective-permute-start(bf16[1024,512]{1,0:T(8,128)(2,1)} %xo.1), channel_id=1, source_target_pairs={{0,16},{16,0},{1,17},{17,1},{2,18},{18,2},{3,19},{19,3},{4,20},{20... | collective-permute-start | bytes 3145736 | tf_op jit(solution)/shard_map/ppermute | solution.py:493
  0.5 0.1 collective-permute-start
  0.5 0.1 pad_add_fusion.ids
  0.6 2.7 %plan.1 = (s32[2,640]{1,0:T(2,128)S(1)}, bf16[512,16,128]{2,1,0:T(8,128)(2,1)S(1)}, bf16[1024,512]{1,0:T(8,128)(2,1)S(1)}) custom-call(s32[2]{0:T(128)S(1)} %pad_add_fusion.ids, s32[1,128]{1,0:T(1,128)} %bitcast.17, s32[1,128]{1,0:T(1,128)} %bitcast.18, s32[1,128]{1,0:T(1,128)} %bitcast.19, bf16[128,8,16,128]{3,2,1,0:T(8,128)(2,1)} %bitcast.16, ...), custom_call_target="tpu_custom_call" | custom-call | tf_op jit(solution)/shard_map/plan/pallas_call | solution.py:141
  3.3 0.0 collective-permute-done.1.xp
  3.3 0.0 copy-start
  3.3 4.7 %gathered_sums.1 = (f32[1040,256]{1,0:T(8,128)S(1)}, f32[1040,256]{1,0:T(8,128)S(1)}, f32[1040,256]{1,0:T(8,128)S(1)}, f32[1040,256]{1,0:T(8,128)S(1)}) custom-call(s32[2,640]{1,0:T(2,128)S(1)} %get-tuple-element.24.table_v, bf16[512,16,128]{2,1,0:T(8,128)(2,1)S(1)} %get-tuple-element.25.tbuf, bf16[1024,512]{1,0:T(8,128)(2,1)S(1)} %get-tuple-element.23.xo, ...), custom_call_target="tpu_custom_call" | custom-call | flops 2147483648 | bytes 8388608 | tf_op jit(solution)/shard_map/gathered_sums/pallas_call | solution.py:266
  8.1 0.0 collective-permute-done.wp
  8.1 0.0 copy-done
  8.1 0.5 %sent_terms.3 = s16[264,256]{1,0:T(8,128)(2,1)S(1)} custom-call(bf16[512,256]{1,0:T(8,128)(2,1)S(1)} %copy-done, bf16[512,256]{1,0:T(8,128)(2,1)S(1)} %collective-permute-done.wp, f32[1040,256]{1,0:T(8,128)S(1)} %get-tuple-element.26.refs_0_, f32[1040,256]{1,0:T(8,128)S(1)} %get-tuple-element.27.refs_1_, f32[1040,256]{1,0:T(8,128)S(1)} %get-tuple-element.28.refs_2_, ...), custom_call_target="tpu_custom_call" | custom-call | flops 268435456 | bytes 2097152 | tf_op jit(solution)/shard_map/sent_terms/pallas_call | solution.py:316
  8.6 0.0 copy-start.1
  8.7 4.0 %collective-permute-start.4 = (s16[264,256]{1,0:T(8,128)(2,1)S(1)}, s16[264,256]{1,0:T(8,128)(2,1)S(1)}, u32[]{:S(2)}, u32[]{:S(2)}) collective-permute-start(s16[264,256]{1,0:T(8,128)(2,1)S(1)} %sent_terms.3), channel_id=1, source_target_pairs={{0,3},{1,2},{2,1},{3,0},{4,7},{5,6},{6,5},{7,4},{8,11},{9,10},{10,... | collective-permute-start | bytes 405512 | tf_op jit(solution)/shard_map/ppermute | solution.py:466
  12.6 0.8 %sent_terms.2 = (s16[264,256]{1,0:T(8,128)(2,1)S(1)}, s16[264,256]{1,0:T(8,128)(2,1)S(1)}) custom-call(bf16[512,256]{1,0:T(8,128)(2,1)S(1)} %copy-done, bf16[512,256]{1,0:T(8,128)(2,1)S(1)} %collective-permute-done.wp, f32[1040,256]{1,0:T(8,128)S(1)} %get-tuple-element.26.refs_0_, f32[1040,256]{1,0:T(8,128)S(1)} %get-tuple-element.27.refs_1_, ...), custom_call_target="tpu_custom_call" | custom-call | flops 536870912 | bytes 2097152 | tf_op jit(solution)/shard_map/sent_terms/pallas_call | solution.py:316
  13.5 0.6 %collective-permute-start.2 = (s16[264,256]{1,0:T(8,128)(2,1)S(1)}, s16[264,256]{1,0:T(8,128)(2,1)S(1)}, u32[]{:S(2)}, u32[]{:S(2)}) collective-permute-start(s16[264,256]{1,0:T(8,128)(2,1)S(1)} %get-tuple-element.31), channel_id=1, source_target_pairs={{0,1},{1,0},{2,3},{3,2},{4,5},{5,4},{6,7},{7,6},{8,9},{9,8},{10,11... | collective-permute-start | bytes 405512 | tf_op jit(solution)/shard_map/ppermute | solution.py:466
  14.1 0.0 copy-start.4
  14.1 0.0 copy-start.5
  14.1 0.0 copy-start.6
  14.1 0.1 collective-permute-start.3
  14.2 0.0 copy-done.1
  14.2 1.0 %own_terms.1 = (f32[256,256]{1,0:T(8,128)S(1)}, f32[64,256]{1,0:T(8,128)S(1)}) custom-call(s32[2]{0:T(128)S(1)} %pad_add_fusion.ids, bf16[512,256]{1,0:T(8,128)(2,1)S(1)} %copy-done, bf16[512,256]{1,0:T(8,128)(2,1)S(1)} %collective-permute-done.wp, bf16[1024,512]{1,0:T(8,128)(2,1)S(1)} %get-tuple-element.23.xo, bf16[512,256]{1,0:T(8,128)(2,1)S(1)} %copy-done.1, ...), custom_call_target="tpu_custom_call" | custom-call | flops 268435456 | bytes 2097152 | tf_op jit(solution)/shard_map/own_terms/pallas_call | solution.py:349
  15.2 0.0 copy-start.2
  15.2 0.0 copy-start.3
  15.3 0.1 collective-permute-start.5
  15.3 1.5 %collective-permute-done.4.refs_2_ = s16[264,256]{1,0:T(8,128)(2,1)S(1)} collective-permute-done((s16[264,256]{1,0:T(8,128)(2,1)S(1)}, s16[264,256]{1,0:T(8,128)(2,1)S(1)}, u32[]{:S(2)}, u32[]{:S(2)}) %collective-permute-start.4) | collective-permute-done | bytes 135200 | tf_op jit(solution)/shard_map/ppermute | solution.py:466
  16.9 2.6 %collective-permute-done.2.refs_0_ = s16[264,256]{1,0:T(8,128)(2,1)S(1)} collective-permute-done((s16[264,256]{1,0:T(8,128)(2,1)S(1)}, s16[264,256]{1,0:T(8,128)(2,1)S(1)}, u32[]{:S(2)}, u32[]{:S(2)}) %collective-permute-start.2) | collective-permute-done | bytes 135200 | tf_op jit(solution)/shard_map/ppermute | solution.py:466
  19.5 0.0 collective-permute-done.3.refs_1_
  19.5 0.2 combine.1
  19.7 3.2 %collective-permute-start.6 = (s16[72,256]{1,0:T(8,128)(2,1)S(1)}, s16[72,256]{1,0:T(8,128)(2,1)S(1)}, u32[]{:S(2)}, u32[]{:S(2)}) collective-permute-start(s16[72,256]{1,0:T(8,128)(2,1)S(1)} %get-tuple-element.35), channel_id=1, source_target_pairs={{0,8},{1,9},{2,10},{3,11},{4,12},{5,13},{6,14},{7,15},{8,0},{9,1},... | collective-permute-start | bytes 110600 | tf_op jit(solution)/shard_map/ppermute | solution.py:466
  22.9 1.3 %collective-permute-start.7 = (s16[72,256]{1,0:T(8,128)(2,1)S(1)}, s16[72,256]{1,0:T(8,128)(2,1)S(1)}, u32[]{:S(2)}, u32[]{:S(2)}) collective-permute-start(s16[72,256]{1,0:T(8,128)(2,1)S(1)} %get-tuple-element.36), channel_id=1, source_target_pairs={{0,12},{1,13},{2,14},{3,15},{4,8},{5,9},{6,10},{7,11},{8,4},{9,5},... | collective-permute-start | bytes 110600 | tf_op jit(solution)/shard_map/ppermute | solution.py:466
  24.2 0.0 collective-permute-start.8
  24.2 0.0 copy-done.4
  24.2 0.0 copy-done.5
  24.2 0.0 copy-done.6
  24.2 0.7 %selection.1 = (bf16[128,128]{1,0:T(8,128)(2,1)S(1)}, bf16[128,128]{1,0:T(8,128)(2,1)S(1)}, bf16[64,128]{1,0:T(8,128)(2,1)S(1)}) custom-call(s32[2]{0:T(128)S(1)} %pad_add_fusion.ids, s32[16,8,16]{2,1,0:T(8,128)S(1)} %bitcast.15, s32[16,16]{1,0:T(8,128)S(1)} %copy-done.6, bf16[64,256]{1,0:T(8,128)(2,1)S(1)} %copy-done.5), custom_call_target="tpu_custom_call" | custom-call | tf_op jit(solution)/shard_map/selection/pallas_call | solution.py:197
  24.9 0.0 collective-permute-done.5.refs_1_
  24.9 0.1 collective-permute-done.6.refs_2_
  25.0 3.6 %collective-permute-done.7.refs_3_ = s16[72,256]{1,0:T(8,128)(2,1)S(1)} collective-permute-done((s16[72,256]{1,0:T(8,128)(2,1)S(1)}, s16[72,256]{1,0:T(8,128)(2,1)S(1)}, u32[]{:S(2)}, u32[]{:S(2)}) %collective-permute-start.7) | collective-permute-done | bytes 36896 | tf_op jit(solution)/shard_map/ppermute | solution.py:466
  28.6 0.0 collective-permute-done.8.refs_4_
  28.7 0.1 collective-permute-start.9
  28.8 1.2 %collective-permute-done.9.other = bf16[64,256]{1,0:T(8,128)(2,1)S(1)} collective-permute-done((bf16[64,256]{1,0:T(8,128)(2,1)S(1)}, bf16[64,256]{1,0:T(8,128)(2,1)S(1)}, u32[]{:S(2)}, u32[]{:S(2)}) %collective-permute-start.9) | collective-permute-done | bytes 32800 | tf_op jit(solution)/shard_map/ppermute | solution.py:520
  30.0 0.1 rows_to_send.1
  30.1 9.7 %all_to_all.11 = bf16[16,8,256]{2,1,0:T(8,128)(2,1)S(1)} all-to-all(bf16[16,8,256]{2,1,0:T(8,128)(2,1)S(1)} %bitcast.11), channel_id=1, replica_groups={{15,14,13,12,11,10,9,8,7,6,5,4,3,2,1,0},{31,30,29,28,27,26,25,24,23,22,..., dimensions={0} | all-to-all | bytes 131072 | tf_op jit(solution)/shard_map/all_to_all | solution.py:522
  39.8 0.0 copy-done.2
  39.8 0.0 copy-done.3
  39.8 1.0 %logits.1 = f32[64,172]{1,0:T(8,128)} custom-call(bf16[64,256]{1,0:T(8,128)(2,1)S(1)} %hidden_rows.1.own, bf16[64,256]{1,0:T(8,128)(2,1)S(1)} %collective-permute-done.9.other, bf16[128,256]{1,0:T(8,128)(2,1)S(1)} %bitcast.12, bf16[128,128]{1,0:T(8,128)(2,1)S(1)} %get-tuple-element.39.front, bf16[64,128]{1,0:T(8,128)(2,1)S(1)} %get-tuple-element.40.adj_received, ...), custom_call_target="tpu_custom_call" | custom-call | tf_op jit(solution)/shard_map/logits/pallas_call | solution.py:453
  (1 shorter events, 0.0 us)
Async XLA Ops:
  0.0 3.3 %collective-permute-start.1 = (bf16[1024,512]{1,0:T(8,128)(2,1)}, bf16[1024,512]{1,0:T(8,128)(2,1)S(1)}, u32[]{:S(2)}, u32[]{:S(2)}) collective-permute-start(bf16[1024,512]{1,0:T(8,128)(2,1)} %xo.1), channel_id=1, source_target_pairs={{0,16},{16,0},{1,17},{17,1},{2,18},{18,2},{3,19},{19,3},{4,20},{20... | collective-permute-start | bytes 3145736 | tf_op jit(solution)/shard_map/ppermute | solution.py:493
  0.5 7.6 %collective-permute-start = (bf16[512,256]{1,0:T(8,128)(2,1)}, bf16[512,256]{1,0:T(8,128)(2,1)S(1)}, u32[]{:S(2)}, u32[]{:S(2)}) collective-permute-start(bf16[512,256]{1,0:T(8,128)(2,1)} %wo.5), channel_id=1, source_target_pairs={{0,16},{16,0},{1,17},{17,1},{2,18},{18,2},{3,19},{19,3},{4,20},{20... | collective-permute-start | bytes 786440 | tf_op jit(solution)/shard_map/ppermute | solution.py:494
  3.3 4.8 %copy-start = (bf16[512,256]{1,0:T(8,128)(2,1)S(1)}, bf16[512,256]{1,0:T(8,128)(2,1)}, u32[]{:S(2)}) copy-start(bf16[512,256]{1,0:T(8,128)(2,1)} %wo.5) | copy-start | bytes 786436
  8.6 5.6 %copy-start.1 = (bf16[512,256]{1,0:T(8,128)(2,1)S(1)}, bf16[512,256]{1,0:T(8,128)(2,1)}, u32[]{:S(2)}) copy-start(bf16[512,256]{1,0:T(8,128)(2,1)} %so.1) | copy-start | bytes 786436
  8.7 8.2 %collective-permute-start.4 = (s16[264,256]{1,0:T(8,128)(2,1)S(1)}, s16[264,256]{1,0:T(8,128)(2,1)S(1)}, u32[]{:S(2)}, u32[]{:S(2)}) collective-permute-start(s16[264,256]{1,0:T(8,128)(2,1)S(1)} %sent_terms.3), channel_id=1, source_target_pairs={{0,3},{1,2},{2,1},{3,0},{4,7},{5,6},{6,5},{7,4},{8,11},{9,10},{10,... | collective-permute-start | bytes 405512 | tf_op jit(solution)/shard_map/ppermute | solution.py:466
  13.5 6.0 %collective-permute-start.2 = (s16[264,256]{1,0:T(8,128)(2,1)S(1)}, s16[264,256]{1,0:T(8,128)(2,1)S(1)}, u32[]{:S(2)}, u32[]{:S(2)}) collective-permute-start(s16[264,256]{1,0:T(8,128)(2,1)S(1)} %get-tuple-element.31), channel_id=1, source_target_pairs={{0,1},{1,0},{2,3},{3,2},{4,5},{5,4},{6,7},{7,6},{8,9},{9,8},{10,11... | collective-permute-start | bytes 405512 | tf_op jit(solution)/shard_map/ppermute | solution.py:466
  14.1 10.1 %copy-start.4 = (s32[16,16,8]{1,2,0:T(8,128)S(1)}, s32[16,16,8]{1,2,0:T(8,128)}, u32[]{:S(2)}) copy-start(s32[16,16,8]{1,2,0:T(8,128)} %param.19) | copy-start | bytes 24580
  14.1 10.1 %copy-start.5 = (bf16[64,256]{1,0:T(8,128)(2,1)S(1)}, bf16[64,256]{1,0:T(8,128)(2,1)}, u32[]{:S(2)}) copy-start(bf16[64,256]{1,0:T(8,128)(2,1)} %adj.1) | copy-start | bytes 98308
  14.1 10.1 %copy-start.6 = (s32[16,16]{1,0:T(8,128)S(1)}, s32[16,16]{1,0:T(8,128)}, u32[]{:S(2)}) copy-start(s32[16,16]{1,0:T(8,128)} %counts.1) | copy-start | bytes 3076
  14.1 5.4 %collective-permute-start.3 = (s16[264,256]{1,0:T(8,128)(2,1)S(1)}, s16[264,256]{1,0:T(8,128)(2,1)S(1)}, u32[]{:S(2)}, u32[]{:S(2)}) collective-permute-start(s16[264,256]{1,0:T(8,128)(2,1)S(1)} %get-tuple-element.32), channel_id=1, source_target_pairs={{0,2},{1,3},{2,0},{3,1},{4,6},{5,7},{6,4},{7,5},{8,10},{9,11},{10,... | collective-permute-start | bytes 405512 | tf_op jit(solution)/shard_map/ppermute | solution.py:466
  15.2 24.5 %copy-start.2 = (bf16[256,172]{0,1:T(8,128)(2,1)S(1)}, bf16[256,172]{0,1:T(8,128)(2,1)}, u32[]{:S(2)}) copy-start(bf16[256,172]{0,1:T(8,128)(2,1)} %param.22) | copy-start | bytes 264196
  15.2 24.5 %copy-start.3 = (bf16[256,172]{0,1:T(8,128)(2,1)S(1)}, bf16[256,172]{0,1:T(8,128)(2,1)}, u32[]{:S(2)}) copy-start(bf16[256,172]{0,1:T(8,128)(2,1)} %param.23) | copy-start | bytes 264196
  15.3 9.7 %collective-permute-start.5 = (f32[64,256]{1,0:T(8,128)S(1)}, f32[64,256]{1,0:T(8,128)S(1)}, u32[]{:S(2)}, u32[]{:S(2)}) collective-permute-start(f32[64,256]{1,0:T(8,128)S(1)} %get-tuple-element.34), channel_id=1, source_target_pairs={{0,16},{16,0},{1,17},{17,1},{2,18},{18,2},{3,19},{19,3},{4,20},{20... | collective-permute-start | bytes 196616 | tf_op jit(solution)/shard_map/ppermute | solution.py:509
  19.7 5.3 %collective-permute-start.6 = (s16[72,256]{1,0:T(8,128)(2,1)S(1)}, s16[72,256]{1,0:T(8,128)(2,1)S(1)}, u32[]{:S(2)}, u32[]{:S(2)}) collective-permute-start(s16[72,256]{1,0:T(8,128)(2,1)S(1)} %get-tuple-element.35), channel_id=1, source_target_pairs={{0,8},{1,9},{2,10},{3,11},{4,12},{5,13},{6,14},{7,15},{8,0},{9,1},... | collective-permute-start | bytes 110600 | tf_op jit(solution)/shard_map/ppermute | solution.py:466
  22.9 5.8 %collective-permute-start.7 = (s16[72,256]{1,0:T(8,128)(2,1)S(1)}, s16[72,256]{1,0:T(8,128)(2,1)S(1)}, u32[]{:S(2)}, u32[]{:S(2)}) collective-permute-start(s16[72,256]{1,0:T(8,128)(2,1)S(1)} %get-tuple-element.36), channel_id=1, source_target_pairs={{0,12},{1,13},{2,14},{3,15},{4,8},{5,9},{6,10},{7,11},{8,4},{9,5},... | collective-permute-start | bytes 110600 | tf_op jit(solution)/shard_map/ppermute | solution.py:466
  24.2 4.5 %collective-permute-start.8 = (s16[72,256]{1,0:T(8,128)(2,1)S(1)}, s16[72,256]{1,0:T(8,128)(2,1)S(1)}, u32[]{:S(2)}, u32[]{:S(2)}) collective-permute-start(s16[72,256]{1,0:T(8,128)(2,1)S(1)} %get-tuple-element.37), channel_id=1, source_target_pairs={{0,4},{1,5},{2,6},{3,7},{4,0},{5,1},{6,2},{7,3},{8,12},{9,13},{10,... | collective-permute-start | bytes 110600 | tf_op jit(solution)/shard_map/ppermute | solution.py:466
  28.7 1.3 %collective-permute-start.9 = (bf16[64,256]{1,0:T(8,128)(2,1)S(1)}, bf16[64,256]{1,0:T(8,128)(2,1)S(1)}, u32[]{:S(2)}, u32[]{:S(2)}) collective-permute-start(bf16[64,256]{1,0:T(8,128)(2,1)S(1)} %hidden_rows.1.own), channel_id=1, source_target_pairs={{0,16},{16,0},{1,17},{17,1},{2,18},{18,2},{3,19},{19,3},{4,20},{20... | collective-permute-start | bytes 98312 | tf_op jit(solution)/shard_map/ppermute | solution.py:520

commit v27 on v25

--- a/solution.py
+++ b/solution.py
@@ -78,7 +78,7 @@
         c.start()
     lane = lax.broadcasted_iota(jnp.int32, (1, tiles), 1)
     block_i = lax.broadcasted_iota(jnp.int32, (n_src, tiles), 0)
-    before = lax.broadcasted_iota(jnp.int32, (units, units), 0) < lax.broadcasted_iota(jnp.int32, (units, units), 1)
+    before = lax.broadcasted_iota(jnp.int32, (tiles, tiles), 0) < lax.broadcasted_iota(jnp.int32, (tiles, tiles), 1)
     before = jnp.where(before, 1.0, 0.0).astype(jnp.bfloat16)
     pos_i = lax.broadcasted_iota(jnp.int32, (tiles, n_pos), 1).astype(jnp.float32)
     place_i = lax.broadcasted_iota(jnp.int32, (1, n_pos), 1)
@@ -96,18 +96,24 @@
             valid.append(ok)
             words.append(((slot * per + j) * 512 + (j * tiles + lane)) * 32 + limit)
             hot.append(jnp.where(jnp.logical_and(block_i == src, ok), 1.0, 0.0))
-        hot = jnp.concatenate(hot, axis=1)
-        earlier = jnp.dot(hot.astype(jnp.bfloat16), before, preferred_element_type=jnp.float32)
-        blocks = jnp.floor((jnp.sum(hot, axis=1, keepdims=True) + (BLOCK - 1)) * (1.0 / BLOCK))
+        stacked = jnp.concatenate(hot, axis=0)
+        earlier = jnp.dot(stacked.astype(jnp.bfloat16), before, preferred_element_type=jnp.float32)
+        counts = jnp.sum(stacked, axis=1, keepdims=True)
+        counts = [counts[j * n_src:(j + 1) * n_src, :] for j in range(per)]
+        blocks = jnp.floor((sum(counts) + (BLOCK - 1)) * (1.0 / BLOCK))
         ahead = jnp.zeros(blocks.shape, jnp.float32)
         source_i = lax.broadcasted_iota(jnp.int32, blocks.shape, 0)
         for s in range(n_src - 1):
             ahead = ahead + jnp.where(source_i > s, blocks[s:s + 1, :], 0.0)
-        pos = jnp.sum(hot * (earlier + ahead * BLOCK), axis=0, keepdims=True)
+        first, pos = ahead * BLOCK, []
+        for j in range(per):
+            place = hot[j] * (earlier[j * n_src:(j + 1) * n_src, :] + first)
+            pos.append(jnp.sum(place, axis=0, keepdims=True))
+            first = first + counts[j]
         behind = jnp.where(place_i.astype(jnp.float32) >= ahead + blocks, 1.0, 0.0)
         owner = jnp.sum(behind, axis=0, keepdims=True)
         run = ahead[n_src - 1:, :] + blocks[n_src - 1:, :]
-        stack = [jnp.where(valid[j], pos[:, j * tiles:(j + 1) * tiles], -1.0) for j in range(per)]
+        stack = [jnp.where(valid[j], pos[j], -1.0) for j in range(per)]
         stack += [w.astype(jnp.float32) - trash for w in words]
         stack += [jnp.zeros((1, tiles), jnp.float32)] * (-len(stack) % 8)
         cols = jnp.concatenate(stack, axis=0).T

time: 40.6 us -> 40.6 us (level)
  starting transfers between devices: 10.3 us -> 9.82 us
    ppermute x6, starting transfers between devices: 9.62 us -> 9.16 us  [exchange(): lax.ppermute(parts[k], 'dom', [(i, i ^ k * stride) for i in range(n)])]
where the time goes in v27:
time: 40.6 us; the launch traced here: 40.3 us
  Pallas kernels  11.4 us (28%)
  blocking collectives  9.89 us (24%)
  starting transfers between devices  9.82 us (24%)
  waiting for transfers between devices  8.99 us (22%)
    all_to_all x1, blocking collectives, body(): lax.all_to_all(send, 'dom', 0, 0, axis_index_groups=[group_order(n)], til...  9.89 us
    ppermute x6, starting transfers between devices, exchange(): lax.ppermute(parts[k], 'dom', [(i, i ^ k * stride) for i in range(n)])  9.16 us
    ppermute x6, waiting for transfers between devices, exchange(): lax.ppermute(parts[k], 'dom', [(i, i ^ k * stride) for i in range(n)])  7.79 us
    pallas_call x1, Pallas kernels, gathered_sums(): pl.pallas_call(tiles_kernel, out_shape=[sums] * parts, in_specs=[vmem] *...  4.38 us
    pallas_call x1, Pallas kernels, plan(): pl.pallas_call(functools.partial(plan_kernel, chunks, per, n, radix, n_sr...  2.55 us
    pallas_call x2, Pallas kernels, sent_terms(): pl.pallas_call(functools.partial(sent_kernel, ks, slots, rows, len(accs))...  1.36 us
    ppermute x1, waiting for transfers between devices, body(): other = lax.ppermute(own, 'feat', swap)  1.19 us
    pallas_call x1, Pallas kernels, own_terms(): pl.pallas_call(functools.partial(own_kernel, chunk, per, groups, len(accs...  1.04 us
  transfers between devices with their start and end apart: 10, of which 5 were waited for; matrix products, arithmetic and copies ran while one was open for 0% of the time, Pallas kernels for 24%

profile of v27, /device:TPU:0, one launch (start us, length us, event | category | flops | bytes accessed | tf_op | source)
XLA Modules:
  0.0 40.3 jit_solution(10983318152438747983)
XLA Ops:
  0.0 0.5 %collective-permute-start.1 = (bf16[1024,512]{1,0:T(8,128)(2,1)}, bf16[1024,512]{1,0:T(8,128)(2,1)S(1)}, u32[]{:S(2)}, u32[]{:S(2)}) collective-permute-start(bf16[1024,512]{1,0:T(8,128)(2,1)} %xo.1), channel_id=1, source_target_pairs={{0,16},{16,0},{1,17},{17,1},{2,18},{18,2},{3,19},{19,3},{4,20},{20... | collective-permute-start | bytes 3145736 | tf_op jit(solution)/shard_map/ppermute | solution.py:493
  0.5 0.1 collective-permute-start
  0.5 0.1 pad_add_fusion.ids
  0.6 2.5 %plan.1 = (s32[2,640]{1,0:T(2,128)S(1)}, bf16[512,16,128]{2,1,0:T(8,128)(2,1)S(1)}, bf16[1024,512]{1,0:T(8,128)(2,1)S(1)}) custom-call(s32[2]{0:T(128)S(1)} %pad_add_fusion.ids, s32[1,128]{1,0:T(1,128)} %bitcast.17, s32[1,128]{1,0:T(1,128)} %bitcast.18, s32[1,128]{1,0:T(1,128)} %bitcast.19, bf16[128,8,16,128]{3,2,1,0:T(8,128)(2,1)} %bitcast.16, ...), custom_call_target="tpu_custom_call" | custom-call | tf_op jit(solution)/shard_map/plan/pallas_call | solution.py:141
  3.1 0.0 collective-permute-done.1.xp
  3.2 0.0 copy-start
  3.2 4.4 %gathered_sums.1 = (f32[1040,256]{1,0:T(8,128)S(1)}, f32[1040,256]{1,0:T(8,128)S(1)}, f32[1040,256]{1,0:T(8,128)S(1)}, f32[1040,256]{1,0:T(8,128)S(1)}) custom-call(s32[2,640]{1,0:T(2,128)S(1)} %get-tuple-element.24.table_v, bf16[512,16,128]{2,1,0:T(8,128)(2,1)S(1)} %get-tuple-element.25.tbuf, bf16[1024,512]{1,0:T(8,128)(2,1)S(1)} %get-tuple-element.23.xo, ...), custom_call_target="tpu_custom_call" | custom-call | flops 2147483648 | bytes 8388608 | tf_op jit(solution)/shard_map/gathered_sums/pallas_call | solution.py:266
  7.5 0.0 collective-permute-done.wp
  7.6 0.0 copy-done
  7.6 0.5 %sent_terms.3 = s16[264,256]{1,0:T(8,128)(2,1)S(1)} custom-call(bf16[512,256]{1,0:T(8,128)(2,1)S(1)} %copy-done, bf16[512,256]{1,0:T(8,128)(2,1)S(1)} %collective-permute-done.wp, f32[1040,256]{1,0:T(8,128)S(1)} %get-tuple-element.26.refs_0_, f32[1040,256]{1,0:T(8,128)S(1)} %get-tuple-element.27.refs_1_, f32[1040,256]{1,0:T(8,128)S(1)} %get-tuple-element.28.refs_2_, ...), custom_call_target="tpu_custom_call" | custom-call | flops 268435456 | bytes 2097152 | tf_op jit(solution)/shard_map/sent_terms/pallas_call | solution.py:316
  8.1 0.0 copy-start.1
  8.1 4.3 %collective-permute-start.4 = (s16[264,256]{1,0:T(8,128)(2,1)S(1)}, s16[264,256]{1,0:T(8,128)(2,1)S(1)}, u32[]{:S(2)}, u32[]{:S(2)}) collective-permute-start(s16[264,256]{1,0:T(8,128)(2,1)S(1)} %sent_terms.3), channel_id=1, source_target_pairs={{0,3},{1,2},{2,1},{3,0},{4,7},{5,6},{6,5},{7,4},{8,11},{9,10},{10,... | collective-permute-start | bytes 405512 | tf_op jit(solution)/shard_map/ppermute | solution.py:466
  12.4 0.8 %sent_terms.2 = (s16[264,256]{1,0:T(8,128)(2,1)S(1)}, s16[264,256]{1,0:T(8,128)(2,1)S(1)}) custom-call(bf16[512,256]{1,0:T(8,128)(2,1)S(1)} %copy-done, bf16[512,256]{1,0:T(8,128)(2,1)S(1)} %collective-permute-done.wp, f32[1040,256]{1,0:T(8,128)S(1)} %get-tuple-element.26.refs_0_, f32[1040,256]{1,0:T(8,128)S(1)} %get-tuple-element.27.refs_1_, ...), custom_call_target="tpu_custom_call" | custom-call | flops 536870912 | bytes 2097152 | tf_op jit(solution)/shard_map/sent_terms/pallas_call | solution.py:316
  13.3 0.7 %collective-permute-start.2 = (s16[264,256]{1,0:T(8,128)(2,1)S(1)}, s16[264,256]{1,0:T(8,128)(2,1)S(1)}, u32[]{:S(2)}, u32[]{:S(2)}) collective-permute-start(s16[264,256]{1,0:T(8,128)(2,1)S(1)} %get-tuple-element.31), channel_id=1, source_target_pairs={{0,1},{1,0},{2,3},{3,2},{4,5},{5,4},{6,7},{7,6},{8,9},{9,8},{10,11... | collective-permute-start | bytes 405512 | tf_op jit(solution)/shard_map/ppermute | solution.py:466
  13.9 0.0 copy-start.4
  13.9 0.0 copy-start.5
  13.9 0.0 copy-start.6
  13.9 0.0 collective-permute-start.3
  14.0 0.0 copy-done.1
  14.0 1.0 %own_terms.1 = (f32[256,256]{1,0:T(8,128)S(1)}, f32[64,256]{1,0:T(8,128)S(1)}) custom-call(s32[2]{0:T(128)S(1)} %pad_add_fusion.ids, bf16[512,256]{1,0:T(8,128)(2,1)S(1)} %copy-done, bf16[512,256]{1,0:T(8,128)(2,1)S(1)} %collective-permute-done.wp, bf16[1024,512]{1,0:T(8,128)(2,1)S(1)} %get-tuple-element.23.xo, bf16[512,256]{1,0:T(8,128)(2,1)S(1)} %copy-done.1, ...), custom_call_target="tpu_custom_call" | custom-call | flops 268435456 | bytes 2097152 | tf_op jit(solution)/shard_map/own_terms/pallas_call | solution.py:349
  15.0 0.0 copy-start.2
  15.0 0.0 copy-start.3
  15.1 0.1 collective-permute-start.5
  15.1 1.5 %collective-permute-done.4.refs_2_ = s16[264,256]{1,0:T(8,128)(2,1)S(1)} collective-permute-done((s16[264,256]{1,0:T(8,128)(2,1)S(1)}, s16[264,256]{1,0:T(8,128)(2,1)S(1)}, u32[]{:S(2)}, u32[]{:S(2)}) %collective-permute-start.4) | collective-permute-done | bytes 135200 | tf_op jit(solution)/shard_map/ppermute | solution.py:466
  16.6 2.7 %collective-permute-done.2.refs_0_ = s16[264,256]{1,0:T(8,128)(2,1)S(1)} collective-permute-done((s16[264,256]{1,0:T(8,128)(2,1)S(1)}, s16[264,256]{1,0:T(8,128)(2,1)S(1)}, u32[]{:S(2)}, u32[]{:S(2)}) %collective-permute-start.2) | collective-permute-done | bytes 135200 | tf_op jit(solution)/shard_map/ppermute | solution.py:466
  19.4 0.0 collective-permute-done.3.refs_1_
  19.4 0.2 combine.1
  19.6 2.6 %collective-permute-start.6 = (s16[72,256]{1,0:T(8,128)(2,1)S(1)}, s16[72,256]{1,0:T(8,128)(2,1)S(1)}, u32[]{:S(2)}, u32[]{:S(2)}) collective-permute-start(s16[72,256]{1,0:T(8,128)(2,1)S(1)} %get-tuple-element.35), channel_id=1, source_target_pairs={{0,8},{1,9},{2,10},{3,11},{4,12},{5,13},{6,14},{7,15},{8,0},{9,1},... | collective-permute-start | bytes 110600 | tf_op jit(solution)/shard_map/ppermute | solution.py:466
  22.2 1.4 %collective-permute-start.7 = (s16[72,256]{1,0:T(8,128)(2,1)S(1)}, s16[72,256]{1,0:T(8,128)(2,1)S(1)}, u32[]{:S(2)}, u32[]{:S(2)}) collective-permute-start(s16[72,256]{1,0:T(8,128)(2,1)S(1)} %get-tuple-element.36), channel_id=1, source_target_pairs={{0,12},{1,13},{2,14},{3,15},{4,8},{5,9},{6,10},{7,11},{8,4},{9,5},... | collective-permute-start | bytes 110600 | tf_op jit(solution)/shard_map/ppermute | solution.py:466
  23.6 0.1 collective-permute-start.8
  23.7 0.0 copy-done.4
  23.7 0.0 copy-done.5
  23.7 0.0 copy-done.6
  23.7 0.7 %selection.1 = (bf16[128,128]{1,0:T(8,128)(2,1)S(1)}, bf16[128,128]{1,0:T(8,128)(2,1)S(1)}, bf16[64,128]{1,0:T(8,128)(2,1)S(1)}) custom-call(s32[2]{0:T(128)S(1)} %pad_add_fusion.ids, s32[16,8,16]{2,1,0:T(8,128)S(1)} %bitcast.15, s32[16,16]{1,0:T(8,128)S(1)} %copy-done.6, bf16[64,256]{1,0:T(8,128)(2,1)S(1)} %copy-done.5), custom_call_target="tpu_custom_call" | custom-call | tf_op jit(solution)/shard_map/selection/pallas_call | solution.py:197
  24.4 0.0 collective-permute-done.5.refs_1_
  24.5 0.1 collective-permute-done.6.refs_2_
  24.5 3.5 %collective-permute-done.7.refs_3_ = s16[72,256]{1,0:T(8,128)(2,1)S(1)} collective-permute-done((s16[72,256]{1,0:T(8,128)(2,1)S(1)}, s16[72,256]{1,0:T(8,128)(2,1)S(1)}, u32[]{:S(2)}, u32[]{:S(2)}) %collective-permute-start.7) | collective-permute-done | bytes 36896 | tf_op jit(solution)/shard_map/ppermute | solution.py:466
  28.0 0.0 collective-permute-done.8.refs_4_
  28.0 0.1 collective-permute-start.9
  28.1 1.2 %collective-permute-done.9.other = bf16[64,256]{1,0:T(8,128)(2,1)S(1)} collective-permute-done((bf16[64,256]{1,0:T(8,128)(2,1)S(1)}, bf16[64,256]{1,0:T(8,128)(2,1)S(1)}, u32[]{:S(2)}, u32[]{:S(2)}) %collective-permute-start.9) | collective-permute-done | bytes 32800 | tf_op jit(solution)/shard_map/ppermute | solution.py:520
  29.3 0.1 rows_to_send.1
  29.5 9.9 %all_to_all.11 = bf16[16,8,256]{2,1,0:T(8,128)(2,1)S(1)} all-to-all(bf16[16,8,256]{2,1,0:T(8,128)(2,1)S(1)} %bitcast.11), channel_id=1, replica_groups={{15,14,13,12,11,10,9,8,7,6,5,4,3,2,1,0},{31,30,29,28,27,26,25,24,23,22,..., dimensions={0} | all-to-all | bytes 131072 | tf_op jit(solution)/shard_map/all_to_all | solution.py:522
  39.4 0.0 copy-done.2
  39.4 0.0 copy-done.3
  39.4 1.0 %logits.1 = f32[64,172]{1,0:T(8,128)} custom-call(bf16[64,256]{1,0:T(8,128)(2,1)S(1)} %hidden_rows.1.own, bf16[64,256]{1,0:T(8,128)(2,1)S(1)} %collective-permute-done.9.other, bf16[128,256]{1,0:T(8,128)(2,1)S(1)} %bitcast.12, bf16[128,128]{1,0:T(8,128)(2,1)S(1)} %get-tuple-element.39.front, bf16[64,128]{1,0:T(8,128)(2,1)S(1)} %get-tuple-element.40.adj_received, ...), custom_call_target="tpu_custom_call" | custom-call | tf_op jit(solution)/shard_map/logits/pallas_call | solution.py:453
  (1 shorter events, 0.0 us)
Async XLA Ops:
  0.0 3.1 %collective-permute-start.1 = (bf16[1024,512]{1,0:T(8,128)(2,1)}, bf16[1024,512]{1,0:T(8,128)(2,1)S(1)}, u32[]{:S(2)}, u32[]{:S(2)}) collective-permute-start(bf16[1024,512]{1,0:T(8,128)(2,1)} %xo.1), channel_id=1, source_target_pairs={{0,16},{16,0},{1,17},{17,1},{2,18},{18,2},{3,19},{19,3},{4,20},{20... | collective-permute-start | bytes 3145736 | tf_op jit(solution)/shard_map/ppermute | solution.py:493
  0.5 7.1 %collective-permute-start = (bf16[512,256]{1,0:T(8,128)(2,1)}, bf16[512,256]{1,0:T(8,128)(2,1)S(1)}, u32[]{:S(2)}, u32[]{:S(2)}) collective-permute-start(bf16[512,256]{1,0:T(8,128)(2,1)} %wo.5), channel_id=1, source_target_pairs={{0,16},{16,0},{1,17},{17,1},{2,18},{18,2},{3,19},{19,3},{4,20},{20... | collective-permute-start | bytes 786440 | tf_op jit(solution)/shard_map/ppermute | solution.py:494
  3.2 4.4 %copy-start = (bf16[512,256]{1,0:T(8,128)(2,1)S(1)}, bf16[512,256]{1,0:T(8,128)(2,1)}, u32[]{:S(2)}) copy-start(bf16[512,256]{1,0:T(8,128)(2,1)} %wo.5) | copy-start | bytes 786436
  8.1 5.9 %copy-start.1 = (bf16[512,256]{1,0:T(8,128)(2,1)S(1)}, bf16[512,256]{1,0:T(8,128)(2,1)}, u32[]{:S(2)}) copy-start(bf16[512,256]{1,0:T(8,128)(2,1)} %so.1) | copy-start | bytes 786436
  8.1 8.5 %collective-permute-start.4 = (s16[264,256]{1,0:T(8,128)(2,1)S(1)}, s16[264,256]{1,0:T(8,128)(2,1)S(1)}, u32[]{:S(2)}, u32[]{:S(2)}) collective-permute-start(s16[264,256]{1,0:T(8,128)(2,1)S(1)} %sent_terms.3), channel_id=1, source_target_pairs={{0,3},{1,2},{2,1},{3,0},{4,7},{5,6},{6,5},{7,4},{8,11},{9,10},{10,... | collective-permute-start | bytes 405512 | tf_op jit(solution)/shard_map/ppermute | solution.py:466
  13.3 6.1 %collective-permute-start.2 = (s16[264,256]{1,0:T(8,128)(2,1)S(1)}, s16[264,256]{1,0:T(8,128)(2,1)S(1)}, u32[]{:S(2)}, u32[]{:S(2)}) collective-permute-start(s16[264,256]{1,0:T(8,128)(2,1)S(1)} %get-tuple-element.31), channel_id=1, source_target_pairs={{0,1},{1,0},{2,3},{3,2},{4,5},{5,4},{6,7},{7,6},{8,9},{9,8},{10,11... | collective-permute-start | bytes 405512 | tf_op jit(solution)/shard_map/ppermute | solution.py:466
  13.9 9.8 %copy-start.4 = (s32[16,16,8]{1,2,0:T(8,128)S(1)}, s32[16,16,8]{1,2,0:T(8,128)}, u32[]{:S(2)}) copy-start(s32[16,16,8]{1,2,0:T(8,128)} %param.19) | copy-start | bytes 24580
  13.9 9.8 %copy-start.5 = (bf16[64,256]{1,0:T(8,128)(2,1)S(1)}, bf16[64,256]{1,0:T(8,128)(2,1)}, u32[]{:S(2)}) copy-start(bf16[64,256]{1,0:T(8,128)(2,1)} %adj.1) | copy-start | bytes 98308
  13.9 9.8 %copy-start.6 = (s32[16,16]{1,0:T(8,128)S(1)}, s32[16,16]{1,0:T(8,128)}, u32[]{:S(2)}) copy-start(s32[16,16]{1,0:T(8,128)} %counts.1) | copy-start | bytes 3076
  13.9 5.4 %collective-permute-start.3 = (s16[264,256]{1,0:T(8,128)(2,1)S(1)}, s16[264,256]{1,0:T(8,128)(2,1)S(1)}, u32[]{:S(2)}, u32[]{:S(2)}) collective-permute-start(s16[264,256]{1,0:T(8,128)(2,1)S(1)} %get-tuple-element.32), channel_id=1, source_target_pairs={{0,2},{1,3},{2,0},{3,1},{4,6},{5,7},{6,4},{7,5},{8,10},{9,11},{10,... | collective-permute-start | bytes 405512 | tf_op jit(solution)/shard_map/ppermute | solution.py:466
  15.0 24.3 %copy-start.2 = (bf16[256,172]{0,1:T(8,128)(2,1)S(1)}, bf16[256,172]{0,1:T(8,128)(2,1)}, u32[]{:S(2)}) copy-start(bf16[256,172]{0,1:T(8,128)(2,1)} %param.22) | copy-start | bytes 264196
  15.0 24.3 %copy-start.3 = (bf16[256,172]{0,1:T(8,128)(2,1)S(1)}, bf16[256,172]{0,1:T(8,128)(2,1)}, u32[]{:S(2)}) copy-start(bf16[256,172]{0,1:T(8,128)(2,1)} %param.23) | copy-start | bytes 264196
  15.1 9.4 %collective-permute-start.5 = (f32[64,256]{1,0:T(8,128)S(1)}, f32[64,256]{1,0:T(8,128)S(1)}, u32[]{:S(2)}, u32[]{:S(2)}) collective-permute-start(f32[64,256]{1,0:T(8,128)S(1)} %get-tuple-element.34), channel_id=1, source_target_pairs={{0,16},{16,0},{1,17},{17,1},{2,18},{18,2},{3,19},{19,3},{4,20},{20... | collective-permute-start | bytes 196616 | tf_op jit(solution)/shard_map/ppermute | solution.py:509
  19.6 4.9 %collective-permute-start.6 = (s16[72,256]{1,0:T(8,128)(2,1)S(1)}, s16[72,256]{1,0:T(8,128)(2,1)S(1)}, u32[]{:S(2)}, u32[]{:S(2)}) collective-permute-start(s16[72,256]{1,0:T(8,128)(2,1)S(1)} %get-tuple-element.35), channel_id=1, source_target_pairs={{0,8},{1,9},{2,10},{3,11},{4,12},{5,13},{6,14},{7,15},{8,0},{9,1},... | collective-permute-start | bytes 110600 | tf_op jit(solution)/shard_map/ppermute | solution.py:466
  22.2 5.8 %collective-permute-start.7 = (s16[72,256]{1,0:T(8,128)(2,1)S(1)}, s16[72,256]{1,0:T(8,128)(2,1)S(1)}, u32[]{:S(2)}, u32[]{:S(2)}) collective-permute-start(s16[72,256]{1,0:T(8,128)(2,1)S(1)} %get-tuple-element.36), channel_id=1, source_target_pairs={{0,12},{1,13},{2,14},{3,15},{4,8},{5,9},{6,10},{7,11},{8,4},{9,5},... | collective-permute-start | bytes 110600 | tf_op jit(solution)/shard_map/ppermute | solution.py:466
  23.6 4.4 %collective-permute-start.8 = (s16[72,256]{1,0:T(8,128)(2,1)S(1)}, s16[72,256]{1,0:T(8,128)(2,1)S(1)}, u32[]{:S(2)}, u32[]{:S(2)}) collective-permute-start(s16[72,256]{1,0:T(8,128)(2,1)S(1)} %get-tuple-element.37), channel_id=1, source_target_pairs={{0,4},{1,5},{2,6},{3,7},{4,0},{5,1},{6,2},{7,3},{8,12},{9,13},{10,... | collective-permute-start | bytes 110600 | tf_op jit(solution)/shard_map/ppermute | solution.py:466
  28.0 1.3 %collective-permute-start.9 = (bf16[64,256]{1,0:T(8,128)(2,1)S(1)}, bf16[64,256]{1,0:T(8,128)(2,1)S(1)}, u32[]{:S(2)}, u32[]{:S(2)}) collective-permute-start(bf16[64,256]{1,0:T(8,128)(2,1)S(1)} %hidden_rows.1.own), channel_id=1, source_target_pairs={{0,16},{16,0},{1,17},{17,1},{2,18},{18,2},{3,19},{19,3},{4,20},{20... | collective-permute-start | bytes 98312 | tf_op jit(solution)/shard_map/ppermute | solution.py:520

commit v28 on v27

--- a/solution.py
+++ b/solution.py
@@ -60,9 +60,7 @@
 
 
 def plan_kernel(chunks, per, n, radix, n_src, ids, src_h, rows_h, dst_h, tw, xo, *rest):
-    tables, rest = rest[:chunks], rest[chunks:]
-    tbufs, rest = rest[:chunks], rest[chunks:]
-    xo_out, src_v, rows_v, dst_v, sems = rest
+    tables, (tbuf, xo_out, src_v, rows_v, dst_v, sems) = rest[:chunks], rest[chunks:]
     core, me = ids[0], ids[1]
     tiles = src_v.shape[1]
     n_pos = tables[0].shape[1]
@@ -71,8 +69,7 @@
     half = groups // 2
     gs = [group_of(core, i, groups) for i in range(half)]
     small = [(src_h, src_v), (rows_h, rows_v), (dst_h, dst_v)]
-    large = [(tw.at[:, g], tbufs[i // per].at[pl.ds(i % per * tiles, tiles)]) for i, g in enumerate(gs)]
-    large += [(xo, xo_out)]
+    large = [(tw, tbuf), (xo, xo_out)]
     copies = [pltpu.make_async_copy(a, b, sems.at[i]) for i, (a, b) in enumerate(small + large)]
     for c in copies:
         c.start()
@@ -137,19 +134,17 @@
     smem = pl.BlockSpec(memory_space=pltpu.SMEM)
     vmem = pl.BlockSpec(memory_space=pltpu.VMEM)
     hbm = pl.BlockSpec(memory_space=pltpu.HBM)
-    half = chunks * per
     return pl.pallas_call(
         functools.partial(plan_kernel, chunks, per, n, radix, n_src),
         out_shape=[jax.ShapeDtypeStruct((2, n_pos), jnp.int32)] * chunks
-        + [jax.ShapeDtypeStruct((per * tiles, UNIT, tile), tw.dtype)] * chunks
-        + [jax.ShapeDtypeStruct(xo.shape, xo.dtype)],
+        + [jax.ShapeDtypeStruct(tw.shape, tw.dtype), jax.ShapeDtypeStruct(xo.shape, xo.dtype)],
         in_specs=[smem] + [hbm] * 5,
-        out_specs=[vmem] * (2 * chunks + 1),
+        out_specs=[vmem] * (chunks + 2),
         scratch_shapes=[
             pltpu.VMEM((1, tiles), jnp.int32),
             pltpu.VMEM((1, tiles), jnp.int32),
             pltpu.VMEM((1, tiles), jnp.int32),
-            pltpu.SemaphoreType.DMA((3 + half + 1,)),
+            pltpu.SemaphoreType.DMA((3 + 2,)),
         ],
         compiler_params=pltpu.CompilerParams(vmem_limit_bytes=32 * 1024 * 1024),
         name="plan",
@@ -208,11 +203,12 @@
     )(ids, jnp.swapaxes(send_list, 1, 2), send_count, adj)
 
 
-def tiles_kernel(table_v, tbuf, xo, xp, *rest):
+def tiles_kernel(chunk, per, ids, table_v, tbuf, xo, xp, *rest):
     parts = len(rest) - 3
     accs, (masks, table, sem) = rest[:parts], rest[parts:]
-    tile = tbuf.shape[2]
+    tiles, groups, _, tile = tbuf.shape
     width = xo.shape[1]
+    core = ids[0]
     to_scalar = pltpu.make_async_copy(table_v, table, sem)
     to_scalar.start()
     for acc in accs:
@@ -231,7 +227,10 @@
             for k in range(BLOCK):
                 word = table[0, at * BLOCK + k]
                 u = jnp.bitwise_and(lax.shift_right_logical(word, 5), 511)
-                rows.append(tbuf[u] * masks[jnp.bitwise_and(word, 31)])
+                place = lax.div(u, tiles) + chunk * per
+                odd = jnp.bitwise_and(place, 1)
+                row = odd * groups + (1 - 2 * odd) * (place + core)
+                rows.append(tbuf[lax.rem(u, tiles), row] * masks[jnp.bitwise_and(word, 31)])
                 places.append(pl.multiple_of(lax.shift_right_logical(word, 14) * UNIT, UNIT))
             lhs = jnp.concatenate(rows, axis=0)
             for acc, (x, h) in zip(accs, columns):
@@ -256,17 +255,18 @@
     lax.fori_loop(0, lax.rem(halves, 2), last, 0)
 
 
-def gathered_sums(per, n, table, tbuf, xo, xp):
+def gathered_sums(chunk, per, n, ids, table, tbuf, xo, xp):
     width = xo.shape[1]
-    tile = tbuf.shape[2]
-    vmem = pl.BlockSpec(memory_space=pltpu.VMEM)
-    flops = 2 * tbuf.shape[0] * UNIT * tile * 2 * width
+    tile = tbuf.shape[3]
+    smem = pl.BlockSpec(memory_space=pltpu.SMEM)
+    vmem = pl.BlockSpec(memory_space=pltpu.VMEM)
+    flops = 2 * tbuf.shape[0] * per * UNIT * tile * 2 * width
     parts = 2 * width // PART
     sums = jax.ShapeDtypeStruct(((n * per + 1) * UNIT, PART), jnp.float32)
     return pl.pallas_call(
-        tiles_kernel,
+        functools.partial(tiles_kernel, chunk, per),
         out_shape=[sums] * parts,
-        in_specs=[vmem] * 4,
+        in_specs=[smem] + [vmem] * 4,
         out_specs=[vmem] * parts,
         scratch_shapes=[
             pltpu.VMEM((UNIT + 1, UNIT, tile), jnp.bfloat16),
@@ -276,7 +276,7 @@
         compiler_params=pltpu.CompilerParams(vmem_limit_bytes=(12 << 20) + sums.size * 4 * parts),
         cost_estimate=pl.CostEstimate(flops=flops, bytes_accessed=8 << 20, transcendentals=0),
         name="gathered_sums",
-    )(table, tbuf, xo, xp)
+    )(ids, table, tbuf, xo, xp)
 
 
 def weigh(accs, weights, first, count, out):
@@ -496,11 +496,11 @@
     planned = plan(
         CHUNKS, per, n, 4, ids, tile_src, tile_rows, tile_dst, tw, features,
     )
-    tables, tbufs, xo = planned[:CHUNKS], planned[CHUNKS:2 * CHUNKS], planned[2 * CHUNKS]
+    tables, (tbuf, xo) = planned[:CHUNKS], planned[CHUNKS:]
     wo, so = neighbour_weight_first, w_self1
     done = []
     for chunk in range(CHUNKS):
-        accs = gathered_sums(per, n, tables[chunk], tbufs[chunk], xo, xp)
+        accs = gathered_sums(chunk, per, n, ids, tables[chunk], tbuf, xo, xp)
         slots, rows = n // 4, per * UNIT
         parts = {}
         (parts[3],) = sent_terms((3,), slots, rows, accs, wo, wp)

time: 40.6 us -> 43.2 us (1.064)
  Pallas kernels: 11.4 us -> 14.1 us
    pallas_call x1, Pallas kernels: 4.38 us -> 6.55 us  [gathered_sums(): pl.pallas_call(functools.partial(tiles_kernel, chunk, per), out_shape=[su...]
    pallas_call x1, Pallas kernels: 2.55 us -> 3.12 us  [plan(): pl.pallas_call(functools.partial(plan_kernel, chunks, per, n, radix, n_sr...]
  transfers between devices with their start and end apart: 10 -> 10, of which waited for: 5 -> 5; matrix products, arithmetic and copies ran while one was open for 0% -> 0% of each run, Pallas kernels for 24% -> 29%
where the time goes in v28:
time: 43.2 us; the launch traced here: 42.9 us
  Pallas kernels  14.1 us (33%)
  starting transfers between devices  10.2 us (24%)
  blocking collectives  9.67 us (22%)
  waiting for transfers between devices  8.66 us (20%)
    all_to_all x1, blocking collectives, body(): lax.all_to_all(send, 'dom', 0, 0, axis_index_groups=[group_order(n)], til...  9.67 us
    ppermute x6, starting transfers between devices, exchange(): lax.ppermute(parts[k], 'dom', [(i, i ^ k * stride) for i in range(n)])  9.55 us
    ppermute x6, waiting for transfers between devices, exchange(): lax.ppermute(parts[k], 'dom', [(i, i ^ k * stride) for i in range(n)])  7.46 us
    pallas_call x1, Pallas kernels, gathered_sums(): pl.pallas_call(functools.partial(tiles_kernel, chunk, per), out_shape=[su...  6.55 us
    pallas_call x1, Pallas kernels, plan(): pl.pallas_call(functools.partial(plan_kernel, chunks, per, n, radix, n_sr...  3.12 us
    pallas_call x2, Pallas kernels, sent_terms(): pl.pallas_call(functools.partial(sent_kernel, ks, slots, rows, len(accs))...  1.38 us
    ppermute x1, waiting for transfers between devices, body(): other = lax.ppermute(own, 'feat', swap)  1.19 us
    pallas_call x1, Pallas kernels, own_terms(): pl.pallas_call(functools.partial(own_kernel, chunk, per, groups, len(accs...  1.03 us
  transfers between devices with their start and end apart: 10, of which 5 were waited for; matrix products, arithmetic and copies ran while one was open for 0% of the time, Pallas kernels for 29%

profile of v28, /device:TPU:0, one launch (start us, length us, event | category | flops | bytes accessed | tf_op | source)
XLA Modules:
  0.0 42.9 jit_solution(6286175033344976548)
XLA Ops:
  0.0 0.5 %collective-permute-start.1 = (bf16[1024,512]{1,0:T(8,128)(2,1)}, bf16[1024,512]{1,0:T(8,128)(2,1)S(1)}, u32[]{:S(2)}, u32[]{:S(2)}) collective-permute-start(bf16[1024,512]{1,0:T(8,128)(2,1)} %xo.1), channel_id=1, source_target_pairs={{0,16},{16,0},{1,17},{17,1},{2,18},{18,2},{3,19},{19,3},{4,20},{20... | collective-permute-start | bytes 3145736 | tf_op jit(solution)/shard_map/ppermute | solution.py:493
  0.5 0.1 collective-permute-start
  0.5 0.1 pad_add_fusion.ids
  0.6 3.1 %plan.1 = (s32[2,640]{1,0:T(2,128)S(1)}, bf16[128,8,16,128]{3,2,1,0:T(8,128)(2,1)S(1)}, bf16[1024,512]{1,0:T(8,128)(2,1)S(1)}) custom-call(s32[2]{0:T(128)S(1)} %pad_add_fusion.ids, s32[1,128]{1,0:T(1,128)} %bitcast.17, s32[1,128]{1,0:T(1,128)} %bitcast.18, s32[1,128]{1,0:T(1,128)} %bitcast.19, bf16[128,8,16,128]{3,2,1,0:T(8,128)(2,1)} %bitcast.16, ...), custom_call_target="tpu_custom_call" | custom-call | tf_op jit(solution)/shard_map/plan/pallas_call | solution.py:137
  3.7 0.0 collective-permute-done.1.xp
  3.7 0.0 copy-start
  3.7 6.6 %gathered_sums.1 = (f32[1040,256]{1,0:T(8,128)S(1)}, f32[1040,256]{1,0:T(8,128)S(1)}, f32[1040,256]{1,0:T(8,128)S(1)}, f32[1040,256]{1,0:T(8,128)S(1)}) custom-call(s32[2]{0:T(128)S(1)} %pad_add_fusion.ids, s32[2,640]{1,0:T(2,128)S(1)} %get-tuple-element.24.table_v, bf16[128,8,16,128]{3,2,1,0:T(8,128)(2,1)S(1)} %get-tuple-element.25.tbuf, ...), custom_call_target="tpu_custom_call" | custom-call | flops 2147483648 | bytes 8388608 | tf_op jit(solution)/shard_map/gathered_sums/pallas_call | solution.py:266
  10.3 0.0 collective-permute-done.wp
  10.3 0.0 copy-done
  10.3 0.5 %sent_terms.3 = s16[264,256]{1,0:T(8,128)(2,1)S(1)} custom-call(bf16[512,256]{1,0:T(8,128)(2,1)S(1)} %copy-done, bf16[512,256]{1,0:T(8,128)(2,1)S(1)} %collective-permute-done.wp, f32[1040,256]{1,0:T(8,128)S(1)} %get-tuple-element.26.refs_0_, f32[1040,256]{1,0:T(8,128)S(1)} %get-tuple-element.27.refs_1_, f32[1040,256]{1,0:T(8,128)S(1)} %get-tuple-element.28.refs_2_, ...), custom_call_target="tpu_custom_call" | custom-call | flops 268435456 | bytes 2097152 | tf_op jit(solution)/shard_map/sent_terms/pallas_call | solution.py:316
  10.9 0.0 copy-start.1
  10.9 3.9 %collective-permute-start.4 = (s16[264,256]{1,0:T(8,128)(2,1)S(1)}, s16[264,256]{1,0:T(8,128)(2,1)S(1)}, u32[]{:S(2)}, u32[]{:S(2)}) collective-permute-start(s16[264,256]{1,0:T(8,128)(2,1)S(1)} %sent_terms.3), channel_id=1, source_target_pairs={{0,3},{1,2},{2,1},{3,0},{4,7},{5,6},{6,5},{7,4},{8,11},{9,10},{10,... | collective-permute-start | bytes 405512 | tf_op jit(solution)/shard_map/ppermute | solution.py:466
  14.8 0.8 %sent_terms.2 = (s16[264,256]{1,0:T(8,128)(2,1)S(1)}, s16[264,256]{1,0:T(8,128)(2,1)S(1)}) custom-call(bf16[512,256]{1,0:T(8,128)(2,1)S(1)} %copy-done, bf16[512,256]{1,0:T(8,128)(2,1)S(1)} %collective-permute-done.wp, f32[1040,256]{1,0:T(8,128)S(1)} %get-tuple-element.26.refs_0_, f32[1040,256]{1,0:T(8,128)S(1)} %get-tuple-element.27.refs_1_, ...), custom_call_target="tpu_custom_call" | custom-call | flops 536870912 | bytes 2097152 | tf_op jit(solution)/shard_map/sent_terms/pallas_call | solution.py:316
  15.7 0.6 %collective-permute-start.2 = (s16[264,256]{1,0:T(8,128)(2,1)S(1)}, s16[264,256]{1,0:T(8,128)(2,1)S(1)}, u32[]{:S(2)}, u32[]{:S(2)}) collective-permute-start(s16[264,256]{1,0:T(8,128)(2,1)S(1)} %get-tuple-element.31), channel_id=1, source_target_pairs={{0,1},{1,0},{2,3},{3,2},{4,5},{5,4},{6,7},{7,6},{8,9},{9,8},{10,11... | collective-permute-start | bytes 405512 | tf_op jit(solution)/shard_map/ppermute | solution.py:466
  16.3 0.0 copy-start.4
  16.3 0.0 copy-start.5
  16.3 0.0 copy-start.6
  16.3 0.1 collective-permute-start.3
  16.4 0.0 copy-done.1
  16.4 1.0 %own_terms.1 = (f32[256,256]{1,0:T(8,128)S(1)}, f32[64,256]{1,0:T(8,128)S(1)}) custom-call(s32[2]{0:T(128)S(1)} %pad_add_fusion.ids, bf16[512,256]{1,0:T(8,128)(2,1)S(1)} %copy-done, bf16[512,256]{1,0:T(8,128)(2,1)S(1)} %collective-permute-done.wp, bf16[1024,512]{1,0:T(8,128)(2,1)S(1)} %get-tuple-element.23.xo, bf16[512,256]{1,0:T(8,128)(2,1)S(1)} %copy-done.1, ...), custom_call_target="tpu_custom_call" | custom-call | flops 268435456 | bytes 2097152 | tf_op jit(solution)/shard_map/own_terms/pallas_call | solution.py:349
  17.4 0.0 copy-start.2
  17.4 0.0 copy-start.3
  17.4 0.1 collective-permute-start.5
  17.5 1.5 %collective-permute-done.4.refs_2_ = s16[264,256]{1,0:T(8,128)(2,1)S(1)} collective-permute-done((s16[264,256]{1,0:T(8,128)(2,1)S(1)}, s16[264,256]{1,0:T(8,128)(2,1)S(1)}, u32[]{:S(2)}, u32[]{:S(2)}) %collective-permute-start.4) | collective-permute-done | bytes 135200 | tf_op jit(solution)/shard_map/ppermute | solution.py:466
  19.0 2.7 %collective-permute-done.2.refs_0_ = s16[264,256]{1,0:T(8,128)(2,1)S(1)} collective-permute-done((s16[264,256]{1,0:T(8,128)(2,1)S(1)}, s16[264,256]{1,0:T(8,128)(2,1)S(1)}, u32[]{:S(2)}, u32[]{:S(2)}) %collective-permute-start.2) | collective-permute-done | bytes 135200 | tf_op jit(solution)/shard_map/ppermute | solution.py:466
  21.7 0.0 collective-permute-done.3.refs_1_
  21.7 0.2 combine.1
  21.9 2.7 %collective-permute-start.6 = (s16[72,256]{1,0:T(8,128)(2,1)S(1)}, s16[72,256]{1,0:T(8,128)(2,1)S(1)}, u32[]{:S(2)}, u32[]{:S(2)}) collective-permute-start(s16[72,256]{1,0:T(8,128)(2,1)S(1)} %get-tuple-element.35), channel_id=1, source_target_pairs={{0,8},{1,9},{2,10},{3,11},{4,12},{5,13},{6,14},{7,15},{8,0},{9,1},... | collective-permute-start | bytes 110600 | tf_op jit(solution)/shard_map/ppermute | solution.py:466
  24.7 1.8 %collective-permute-start.7 = (s16[72,256]{1,0:T(8,128)(2,1)S(1)}, s16[72,256]{1,0:T(8,128)(2,1)S(1)}, u32[]{:S(2)}, u32[]{:S(2)}) collective-permute-start(s16[72,256]{1,0:T(8,128)(2,1)S(1)} %get-tuple-element.36), channel_id=1, source_target_pairs={{0,12},{1,13},{2,14},{3,15},{4,8},{5,9},{6,10},{7,11},{8,4},{9,5},... | collective-permute-start | bytes 110600 | tf_op jit(solution)/shard_map/ppermute | solution.py:466
  26.5 0.4 collective-permute-start.8
  26.8 0.0 copy-done.4
  26.8 0.0 copy-done.5
  26.8 0.0 copy-done.6
  26.8 0.7 %selection.1 = (bf16[128,128]{1,0:T(8,128)(2,1)S(1)}, bf16[128,128]{1,0:T(8,128)(2,1)S(1)}, bf16[64,128]{1,0:T(8,128)(2,1)S(1)}) custom-call(s32[2]{0:T(128)S(1)} %pad_add_fusion.ids, s32[16,8,16]{2,1,0:T(8,128)S(1)} %bitcast.15, s32[16,16]{1,0:T(8,128)S(1)} %copy-done.6, bf16[64,256]{1,0:T(8,128)(2,1)S(1)} %copy-done.5), custom_call_target="tpu_custom_call" | custom-call | tf_op jit(solution)/shard_map/selection/pallas_call | solution.py:192
  27.5 0.0 collective-permute-done.5.refs_1_
  27.6 0.0 collective-permute-done.6.refs_2_
  27.6 3.1 %collective-permute-done.7.refs_3_ = s16[72,256]{1,0:T(8,128)(2,1)S(1)} collective-permute-done((s16[72,256]{1,0:T(8,128)(2,1)S(1)}, s16[72,256]{1,0:T(8,128)(2,1)S(1)}, u32[]{:S(2)}, u32[]{:S(2)}) %collective-permute-start.7) | collective-permute-done | bytes 36896 | tf_op jit(solution)/shard_map/ppermute | solution.py:466
  30.6 0.2 collective-permute-done.8.refs_4_
  30.9 0.1 collective-permute-start.9
  31.0 1.2 %collective-permute-done.9.other = bf16[64,256]{1,0:T(8,128)(2,1)S(1)} collective-permute-done((bf16[64,256]{1,0:T(8,128)(2,1)S(1)}, bf16[64,256]{1,0:T(8,128)(2,1)S(1)}, u32[]{:S(2)}, u32[]{:S(2)}) %collective-permute-start.9) | collective-permute-done | bytes 32800 | tf_op jit(solution)/shard_map/ppermute | solution.py:520
  32.1 0.1 rows_to_send.1
  32.3 9.7 %all_to_all.11 = bf16[16,8,256]{2,1,0:T(8,128)(2,1)S(1)} all-to-all(bf16[16,8,256]{2,1,0:T(8,128)(2,1)S(1)} %bitcast.11), channel_id=1, replica_groups={{15,14,13,12,11,10,9,8,7,6,5,4,3,2,1,0},{31,30,29,28,27,26,25,24,23,22,..., dimensions={0} | all-to-all | bytes 131072 | tf_op jit(solution)/shard_map/all_to_all | solution.py:522
  42.0 0.0 copy-done.2
  42.0 0.0 copy-done.3
  42.0 1.0 %logits.1 = f32[64,172]{1,0:T(8,128)} custom-call(bf16[64,256]{1,0:T(8,128)(2,1)S(1)} %hidden_rows.1.own, bf16[64,256]{1,0:T(8,128)(2,1)S(1)} %collective-permute-done.9.other, bf16[128,256]{1,0:T(8,128)(2,1)S(1)} %bitcast.12, bf16[128,128]{1,0:T(8,128)(2,1)S(1)} %get-tuple-element.39.front, bf16[64,128]{1,0:T(8,128)(2,1)S(1)} %get-tuple-element.40.adj_received, ...), custom_call_target="tpu_custom_call" | custom-call | tf_op jit(solution)/shard_map/logits/pallas_call | solution.py:453
  (1 shorter events, 0.0 us)
Async XLA Ops:
  0.0 3.7 %collective-permute-start.1 = (bf16[1024,512]{1,0:T(8,128)(2,1)}, bf16[1024,512]{1,0:T(8,128)(2,1)S(1)}, u32[]{:S(2)}, u32[]{:S(2)}) collective-permute-start(bf16[1024,512]{1,0:T(8,128)(2,1)} %xo.1), channel_id=1, source_target_pairs={{0,16},{16,0},{1,17},{17,1},{2,18},{18,2},{3,19},{19,3},{4,20},{20... | collective-permute-start | bytes 3145736 | tf_op jit(solution)/shard_map/ppermute | solution.py:493
  0.5 9.8 %collective-permute-start = (bf16[512,256]{1,0:T(8,128)(2,1)}, bf16[512,256]{1,0:T(8,128)(2,1)S(1)}, u32[]{:S(2)}, u32[]{:S(2)}) collective-permute-start(bf16[512,256]{1,0:T(8,128)(2,1)} %wo.5), channel_id=1, source_target_pairs={{0,16},{16,0},{1,17},{17,1},{2,18},{18,2},{3,19},{19,3},{4,20},{20... | collective-permute-start | bytes 786440 | tf_op jit(solution)/shard_map/ppermute | solution.py:494
  3.7 6.6 %copy-start = (bf16[512,256]{1,0:T(8,128)(2,1)S(1)}, bf16[512,256]{1,0:T(8,128)(2,1)}, u32[]{:S(2)}) copy-start(bf16[512,256]{1,0:T(8,128)(2,1)} %wo.5) | copy-start | bytes 786436
  10.9 5.5 %copy-start.1 = (bf16[512,256]{1,0:T(8,128)(2,1)S(1)}, bf16[512,256]{1,0:T(8,128)(2,1)}, u32[]{:S(2)}) copy-start(bf16[512,256]{1,0:T(8,128)(2,1)} %so.1) | copy-start | bytes 786436
  10.9 8.1 %collective-permute-start.4 = (s16[264,256]{1,0:T(8,128)(2,1)S(1)}, s16[264,256]{1,0:T(8,128)(2,1)S(1)}, u32[]{:S(2)}, u32[]{:S(2)}) collective-permute-start(s16[264,256]{1,0:T(8,128)(2,1)S(1)} %sent_terms.3), channel_id=1, source_target_pairs={{0,3},{1,2},{2,1},{3,0},{4,7},{5,6},{6,5},{7,4},{8,11},{9,10},{10,... | collective-permute-start | bytes 405512 | tf_op jit(solution)/shard_map/ppermute | solution.py:466
  15.7 6.1 %collective-permute-start.2 = (s16[264,256]{1,0:T(8,128)(2,1)S(1)}, s16[264,256]{1,0:T(8,128)(2,1)S(1)}, u32[]{:S(2)}, u32[]{:S(2)}) collective-permute-start(s16[264,256]{1,0:T(8,128)(2,1)S(1)} %get-tuple-element.31), channel_id=1, source_target_pairs={{0,1},{1,0},{2,3},{3,2},{4,5},{5,4},{6,7},{7,6},{8,9},{9,8},{10,11... | collective-permute-start | bytes 405512 | tf_op jit(solution)/shard_map/ppermute | solution.py:466
  16.3 10.6 %copy-start.4 = (s32[16,16,8]{1,2,0:T(8,128)S(1)}, s32[16,16,8]{1,2,0:T(8,128)}, u32[]{:S(2)}) copy-start(s32[16,16,8]{1,2,0:T(8,128)} %param.19) | copy-start | bytes 24580
  16.3 10.6 %copy-start.5 = (bf16[64,256]{1,0:T(8,128)(2,1)S(1)}, bf16[64,256]{1,0:T(8,128)(2,1)}, u32[]{:S(2)}) copy-start(bf16[64,256]{1,0:T(8,128)(2,1)} %adj.1) | copy-start | bytes 98308
  16.3 10.6 %copy-start.6 = (s32[16,16]{1,0:T(8,128)S(1)}, s32[16,16]{1,0:T(8,128)}, u32[]{:S(2)}) copy-start(s32[16,16]{1,0:T(8,128)} %counts.1) | copy-start | bytes 3076
  16.3 5.5 %collective-permute-start.3 = (s16[264,256]{1,0:T(8,128)(2,1)S(1)}, s16[264,256]{1,0:T(8,128)(2,1)S(1)}, u32[]{:S(2)}, u32[]{:S(2)}) collective-permute-start(s16[264,256]{1,0:T(8,128)(2,1)S(1)} %get-tuple-element.32), channel_id=1, source_target_pairs={{0,2},{1,3},{2,0},{3,1},{4,6},{5,7},{6,4},{7,5},{8,10},{9,11},{10,... | collective-permute-start | bytes 405512 | tf_op jit(solution)/shard_map/ppermute | solution.py:466
  17.4 24.5 %copy-start.2 = (bf16[256,172]{0,1:T(8,128)(2,1)S(1)}, bf16[256,172]{0,1:T(8,128)(2,1)}, u32[]{:S(2)}) copy-start(bf16[256,172]{0,1:T(8,128)(2,1)} %param.22) | copy-start | bytes 264196
  17.4 24.5 %copy-start.3 = (bf16[256,172]{0,1:T(8,128)(2,1)S(1)}, bf16[256,172]{0,1:T(8,128)(2,1)}, u32[]{:S(2)}) copy-start(bf16[256,172]{0,1:T(8,128)(2,1)} %param.23) | copy-start | bytes 264196
  17.4 10.1 %collective-permute-start.5 = (f32[64,256]{1,0:T(8,128)S(1)}, f32[64,256]{1,0:T(8,128)S(1)}, u32[]{:S(2)}, u32[]{:S(2)}) collective-permute-start(f32[64,256]{1,0:T(8,128)S(1)} %get-tuple-element.34), channel_id=1, source_target_pairs={{0,16},{16,0},{1,17},{17,1},{2,18},{18,2},{3,19},{19,3},{4,20},{20... | collective-permute-start | bytes 196616 | tf_op jit(solution)/shard_map/ppermute | solution.py:509
  21.9 5.6 %collective-permute-start.6 = (s16[72,256]{1,0:T(8,128)(2,1)S(1)}, s16[72,256]{1,0:T(8,128)(2,1)S(1)}, u32[]{:S(2)}, u32[]{:S(2)}) collective-permute-start(s16[72,256]{1,0:T(8,128)(2,1)S(1)} %get-tuple-element.35), channel_id=1, source_target_pairs={{0,8},{1,9},{2,10},{3,11},{4,12},{5,13},{6,14},{7,15},{8,0},{9,1},... | collective-permute-start | bytes 110600 | tf_op jit(solution)/shard_map/ppermute | solution.py:466
  24.7 6.0 %collective-permute-start.7 = (s16[72,256]{1,0:T(8,128)(2,1)S(1)}, s16[72,256]{1,0:T(8,128)(2,1)S(1)}, u32[]{:S(2)}, u32[]{:S(2)}) collective-permute-start(s16[72,256]{1,0:T(8,128)(2,1)S(1)} %get-tuple-element.36), channel_id=1, source_target_pairs={{0,12},{1,13},{2,14},{3,15},{4,8},{5,9},{6,10},{7,11},{8,4},{9,5},... | collective-permute-start | bytes 110600 | tf_op jit(solution)/shard_map/ppermute | solution.py:466
  26.5 4.3 %collective-permute-start.8 = (s16[72,256]{1,0:T(8,128)(2,1)S(1)}, s16[72,256]{1,0:T(8,128)(2,1)S(1)}, u32[]{:S(2)}, u32[]{:S(2)}) collective-permute-start(s16[72,256]{1,0:T(8,128)(2,1)S(1)} %get-tuple-element.37), channel_id=1, source_target_pairs={{0,4},{1,5},{2,6},{3,7},{4,0},{5,1},{6,2},{7,3},{8,12},{9,13},{10,... | collective-permute-start | bytes 110600 | tf_op jit(solution)/shard_map/ppermute | solution.py:466
  30.9 1.3 %collective-permute-start.9 = (bf16[64,256]{1,0:T(8,128)(2,1)S(1)}, bf16[64,256]{1,0:T(8,128)(2,1)S(1)}, u32[]{:S(2)}, u32[]{:S(2)}) collective-permute-start(bf16[64,256]{1,0:T(8,128)(2,1)S(1)} %hidden_rows.1.own), channel_id=1, source_target_pairs={{0,16},{16,0},{1,17},{17,1},{2,18},{18,2},{3,19},{19,3},{4,20},{20... | collective-permute-start | bytes 98312 | tf_op jit(solution)/shard_map/ppermute | solution.py:520

commit v29 on v27

--- a/solution.py
+++ b/solution.py
@@ -122,8 +122,11 @@
             found = found + jnp.where(cols[:, j:j + 1] == pos_i, cols[:, per + j:per + j + 1], 0.0)
         word = jnp.sum(found, axis=0, keepdims=True) + trash
         owner = jnp.where(place_i == n_pos - 1, run, jnp.minimum(owner, n_src - 1.0))
-        tables[c][0:1, :] = word.astype(jnp.int32)
+        word = word.astype(jnp.int32)
+        tables[c][0:1, :] = jnp.bitwise_and(lax.shift_right_logical(word, 5), 511)
         tables[c][1:2, :] = owner.astype(jnp.int32)
+        tables[c][2:3, :] = lax.shift_right_logical(word, 14)
+        tables[c][3:4, :] = jnp.bitwise_and(word, 31)
 
     for c in copies[3:]:
         c.wait()
@@ -140,7 +143,7 @@
     half = chunks * per
     return pl.pallas_call(
         functools.partial(plan_kernel, chunks, per, n, radix, n_src),
-        out_shape=[jax.ShapeDtypeStruct((2, n_pos), jnp.int32)] * chunks
+        out_shape=[jax.ShapeDtypeStruct((4, n_pos), jnp.int32)] * chunks
         + [jax.ShapeDtypeStruct((per * tiles, UNIT, tile), tw.dtype)] * chunks
         + [jax.ShapeDtypeStruct(xo.shape, xo.dtype)],
         in_specs=[smem] + [hbm] * 5,
@@ -229,16 +232,14 @@
             base = pl.multiple_of(table[1, at] * tile, tile)
             rows, places = [], []
             for k in range(BLOCK):
-                word = table[0, at * BLOCK + k]
-                u = jnp.bitwise_and(lax.shift_right_logical(word, 5), 511)
-                rows.append(tbuf[u] * masks[jnp.bitwise_and(word, 31)])
-                places.append(pl.multiple_of(lax.shift_right_logical(word, 14) * UNIT, UNIT))
+                rows.append(tbuf[table[0, at * BLOCK + k]] * masks[table[3, at * BLOCK + k]])
+                places.append(table[2, at * BLOCK + k])
             lhs = jnp.concatenate(rows, axis=0)
             for acc, (x, h) in zip(accs, columns):
                 got = jnp.dot(lhs, x[pl.ds(base, tile), h:h + PART], preferred_element_type=jnp.float32)
                 got = got.astype(jnp.bfloat16).astype(jnp.float32)
                 for k in range(BLOCK):
-                    acc[pl.ds(places[k], UNIT), :] += got[k * UNIT:(k + 1) * UNIT, :]
+                    acc[places[k]] += got[k * UNIT:(k + 1) * UNIT, :]
 
     half = STEP // 2
     halves = lax.div(table[1, table.shape[1] - 1] + half - 1, half)
@@ -262,7 +263,7 @@
     vmem = pl.BlockSpec(memory_space=pltpu.VMEM)
     flops = 2 * tbuf.shape[0] * UNIT * tile * 2 * width
     parts = 2 * width // PART
-    sums = jax.ShapeDtypeStruct(((n * per + 1) * UNIT, PART), jnp.float32)
+    sums = jax.ShapeDtypeStruct((n * per + 1, UNIT, PART), jnp.float32)
     return pl.pallas_call(
         tiles_kernel,
         out_shape=[sums] * parts,
@@ -287,7 +288,7 @@
         got = jnp.zeros((size, out.shape[1]), jnp.float32)
         for i, acc in enumerate(accs):
             w, h = weights[i * PART // weights[0].shape[0]], i * PART % weights[0].shape[0]
-            value = acc[pl.ds(first + at, size), :]
+            value = acc[pl.ds(first // UNIT + r * (size // UNIT), size // UNIT)].reshape(size, PART)
             high = value.astype(jnp.bfloat16)
             low = (value - high.astype(jnp.float32)).astype(jnp.bfloat16)
             got = got + jnp.dot(high, w[h:h + PART, :], preferred_element_type=jnp.float32)

time: 40.6 us -> 40.7 us (level)
  Pallas kernels: 11.4 us -> 11.9 us
    pallas_call x1, Pallas kernels: 4.38 us -> 4.88 us  [gathered_sums(): pl.pallas_call(tiles_kernel, out_shape=[sums] * parts, in_specs=[vmem] *...]
  transfers between devices with their start and end apart: 10 -> 10, of which waited for: 5 -> 4; matrix products, arithmetic and copies ran while one was open for 0% -> 0% of each run, Pallas kernels for 24% -> 25%
where the time goes in v29:
time: 40.7 us; the launch traced here: 40.4 us
  Pallas kernels  11.9 us (29%)
  blocking collectives  9.91 us (24%)
  starting transfers between devices  9.55 us (23%)
  waiting for transfers between devices  8.77 us (22%)
    all_to_all x1, blocking collectives, body(): lax.all_to_all(send, 'dom', 0, 0, axis_index_groups=[group_order(n)], til...  9.91 us
    ppermute x6, starting transfers between devices, exchange(): lax.ppermute(parts[k], 'dom', [(i, i ^ k * stride) for i in range(n)])  8.9 us
    ppermute x6, waiting for transfers between devices, exchange(): lax.ppermute(parts[k], 'dom', [(i, i ^ k * stride) for i in range(n)])  7.57 us
    pallas_call x1, Pallas kernels, gathered_sums(): pl.pallas_call(tiles_kernel, out_shape=[sums] * parts, in_specs=[vmem] *...  4.88 us
    pallas_call x1, Pallas kernels, plan(): pl.pallas_call(functools.partial(plan_kernel, chunks, per, n, radix, n_sr...  2.55 us
    pallas_call x2, Pallas kernels, sent_terms(): pl.pallas_call(functools.partial(sent_kernel, ks, slots, rows, len(accs))...  1.38 us
    ppermute x1, waiting for transfers between devices, body(): other = lax.ppermute(own, 'feat', swap)  1.19 us
    pallas_call x1, Pallas kernels, own_terms(): pl.pallas_call(functools.partial(own_kernel, chunk, per, groups, len(accs...  1.03 us
  transfers between devices with their start and end apart: 10, of which 4 were waited for; matrix products, arithmetic and copies ran while one was open for 0% of the time, Pallas kernels for 25%

profile of v29, /device:TPU:0, one launch (start us, length us, event | category | flops | bytes accessed | tf_op | source)
XLA Modules:
  0.0 40.4 jit_solution(8100928503413183116)
XLA Ops:
  0.0 0.5 %collective-permute-start.1 = (bf16[1024,512]{1,0:T(8,128)(2,1)}, bf16[1024,512]{1,0:T(8,128)(2,1)S(1)}, u32[]{:S(2)}, u32[]{:S(2)}) collective-permute-start(bf16[1024,512]{1,0:T(8,128)(2,1)} %xo.1), channel_id=1, source_target_pairs={{0,16},{16,0},{1,17},{17,1},{2,18},{18,2},{3,19},{19,3},{4,20},{20... | collective-permute-start | bytes 3145736 | tf_op jit(solution)/shard_map/ppermute | solution.py:494
  0.5 0.1 collective-permute-start
  0.5 0.1 pad_add_fusion.ids
  0.6 2.5 %plan.1 = (s32[4,640]{1,0:T(4,128)S(1)}, bf16[512,16,128]{2,1,0:T(8,128)(2,1)S(1)}, bf16[1024,512]{1,0:T(8,128)(2,1)S(1)}) custom-call(s32[2]{0:T(128)S(1)} %pad_add_fusion.ids, s32[1,128]{1,0:T(1,128)} %bitcast.17, s32[1,128]{1,0:T(1,128)} %bitcast.18, s32[1,128]{1,0:T(1,128)} %bitcast.19, bf16[128,8,16,128]{3,2,1,0:T(8,128)(2,1)} %bitcast.16, ...), custom_call_target="tpu_custom_call" | custom-call | tf_op jit(solution)/shard_map/plan/pallas_call | solution.py:144
  3.1 0.0 collective-permute-done.1.xp
  3.2 0.0 copy-start
  3.2 4.9 %gathered_sums.1 = (f32[65,16,256]{2,1,0:T(8,128)S(1)}, f32[65,16,256]{2,1,0:T(8,128)S(1)}, f32[65,16,256]{2,1,0:T(8,128)S(1)}, f32[65,16,256]{2,1,0:T(8,128)S(1)}) custom-call(s32[4,640]{1,0:T(4,128)S(1)} %get-tuple-element.24.table_v, bf16[512,16,128]{2,1,0:T(8,128)(2,1)S(1)} %get-tuple-element.25.tbuf, bf16[1024,512]{1,0:T(8,128)(2,1)S(1)} %get-tuple-element.23.xo, ...), custom_call_target="tpu_custom_call" | custom-call | flops 2147483648 | bytes 8388608 | tf_op jit(solution)/shard_map/gathered_sums/pallas_call | solution.py:267
  8.0 0.0 collective-permute-done.wp
  8.1 0.0 copy-done
  8.1 0.5 %sent_terms.3 = s16[264,256]{1,0:T(8,128)(2,1)S(1)} custom-call(bf16[512,256]{1,0:T(8,128)(2,1)S(1)} %copy-done, bf16[512,256]{1,0:T(8,128)(2,1)S(1)} %collective-permute-done.wp, f32[65,16,256]{2,1,0:T(8,128)S(1)} %get-tuple-element.26.refs_0_, f32[65,16,256]{2,1,0:T(8,128)S(1)} %get-tuple-element.27.refs_1_, f32[65,16,256]{2,1,0:T(8,128)S(1)} %get-tuple-element.28.refs_2_, ...), custom_call_target="tpu_custom_call" | custom-call | flops 268435456 | bytes 2097152 | tf_op jit(solution)/shard_map/sent_terms/pallas_call | solution.py:317
  8.6 0.0 copy-start.1
  8.6 4.0 %collective-permute-start.4 = (s16[264,256]{1,0:T(8,128)(2,1)S(1)}, s16[264,256]{1,0:T(8,128)(2,1)S(1)}, u32[]{:S(2)}, u32[]{:S(2)}) collective-permute-start(s16[264,256]{1,0:T(8,128)(2,1)S(1)} %sent_terms.3), channel_id=1, source_target_pairs={{0,3},{1,2},{2,1},{3,0},{4,7},{5,6},{6,5},{7,4},{8,11},{9,10},{10,... | collective-permute-start | bytes 405512 | tf_op jit(solution)/shard_map/ppermute | solution.py:467
  12.6 0.9 %sent_terms.2 = (s16[264,256]{1,0:T(8,128)(2,1)S(1)}, s16[264,256]{1,0:T(8,128)(2,1)S(1)}) custom-call(bf16[512,256]{1,0:T(8,128)(2,1)S(1)} %copy-done, bf16[512,256]{1,0:T(8,128)(2,1)S(1)} %collective-permute-done.wp, f32[65,16,256]{2,1,0:T(8,128)S(1)} %get-tuple-element.26.refs_0_, f32[65,16,256]{2,1,0:T(8,128)S(1)} %get-tuple-element.27.refs_1_, ...), custom_call_target="tpu_custom_call" | custom-call | flops 536870912 | bytes 2097152 | tf_op jit(solution)/shard_map/sent_terms/pallas_call | solution.py:317
  13.4 0.6 %collective-permute-start.2 = (s16[264,256]{1,0:T(8,128)(2,1)S(1)}, s16[264,256]{1,0:T(8,128)(2,1)S(1)}, u32[]{:S(2)}, u32[]{:S(2)}) collective-permute-start(s16[264,256]{1,0:T(8,128)(2,1)S(1)} %get-tuple-element.31), channel_id=1, source_target_pairs={{0,1},{1,0},{2,3},{3,2},{4,5},{5,4},{6,7},{7,6},{8,9},{9,8},{10,11... | collective-permute-start | bytes 405512 | tf_op jit(solution)/shard_map/ppermute | solution.py:467
  14.0 0.0 copy-start.4
  14.0 0.0 copy-start.5
  14.0 0.0 copy-start.6
  14.0 0.1 collective-permute-start.3
  14.1 0.0 copy-done.1
  14.1 1.0 %own_terms.1 = (f32[256,256]{1,0:T(8,128)S(1)}, f32[64,256]{1,0:T(8,128)S(1)}) custom-call(s32[2]{0:T(128)S(1)} %pad_add_fusion.ids, bf16[512,256]{1,0:T(8,128)(2,1)S(1)} %copy-done, bf16[512,256]{1,0:T(8,128)(2,1)S(1)} %collective-permute-done.wp, bf16[1024,512]{1,0:T(8,128)(2,1)S(1)} %get-tuple-element.23.xo, bf16[512,256]{1,0:T(8,128)(2,1)S(1)} %copy-done.1, ...), custom_call_target="tpu_custom_call" | custom-call | flops 268435456 | bytes 2097152 | tf_op jit(solution)/shard_map/own_terms/pallas_call | solution.py:350
  15.1 0.0 copy-start.2
  15.2 0.0 copy-start.3
  15.2 0.1 collective-permute-start.5
  15.2 1.5 %collective-permute-done.4.refs_2_ = s16[264,256]{1,0:T(8,128)(2,1)S(1)} collective-permute-done((s16[264,256]{1,0:T(8,128)(2,1)S(1)}, s16[264,256]{1,0:T(8,128)(2,1)S(1)}, u32[]{:S(2)}, u32[]{:S(2)}) %collective-permute-start.4) | collective-permute-done | bytes 135200 | tf_op jit(solution)/shard_map/ppermute | solution.py:467
  16.7 2.8 %collective-permute-done.2.refs_0_ = s16[264,256]{1,0:T(8,128)(2,1)S(1)} collective-permute-done((s16[264,256]{1,0:T(8,128)(2,1)S(1)}, s16[264,256]{1,0:T(8,128)(2,1)S(1)}, u32[]{:S(2)}, u32[]{:S(2)}) %collective-permute-start.2) | collective-permute-done | bytes 135200 | tf_op jit(solution)/shard_map/ppermute | solution.py:467
  19.5 0.0 collective-permute-done.3.refs_1_
  19.5 0.2 combine.1
  19.7 2.6 %collective-permute-start.6 = (s16[72,256]{1,0:T(8,128)(2,1)S(1)}, s16[72,256]{1,0:T(8,128)(2,1)S(1)}, u32[]{:S(2)}, u32[]{:S(2)}) collective-permute-start(s16[72,256]{1,0:T(8,128)(2,1)S(1)} %get-tuple-element.35), channel_id=1, source_target_pairs={{0,8},{1,9},{2,10},{3,11},{4,12},{5,13},{6,14},{7,15},{8,0},{9,1},... | collective-permute-start | bytes 110600 | tf_op jit(solution)/shard_map/ppermute | solution.py:467
  22.3 1.4 %collective-permute-start.7 = (s16[72,256]{1,0:T(8,128)(2,1)S(1)}, s16[72,256]{1,0:T(8,128)(2,1)S(1)}, u32[]{:S(2)}, u32[]{:S(2)}) collective-permute-start(s16[72,256]{1,0:T(8,128)(2,1)S(1)} %get-tuple-element.36), channel_id=1, source_target_pairs={{0,12},{1,13},{2,14},{3,15},{4,8},{5,9},{6,10},{7,11},{8,4},{9,5},... | collective-permute-start | bytes 110600 | tf_op jit(solution)/shard_map/ppermute | solution.py:467
  23.6 0.3 collective-permute-start.8
  24.0 0.0 copy-done.4
  24.0 0.0 copy-done.5
  24.0 0.0 copy-done.6
  24.0 0.7 %selection.1 = (bf16[128,128]{1,0:T(8,128)(2,1)S(1)}, bf16[128,128]{1,0:T(8,128)(2,1)S(1)}, bf16[64,128]{1,0:T(8,128)(2,1)S(1)}) custom-call(s32[2]{0:T(128)S(1)} %pad_add_fusion.ids, s32[16,8,16]{2,1,0:T(8,128)S(1)} %bitcast.15, s32[16,16]{1,0:T(8,128)S(1)} %copy-done.6, bf16[64,256]{1,0:T(8,128)(2,1)S(1)} %copy-done.5), custom_call_target="tpu_custom_call" | custom-call | tf_op jit(solution)/shard_map/selection/pallas_call | solution.py:200
  24.7 0.0 collective-permute-done.5.refs_1_
  24.7 0.0 collective-permute-done.6.refs_2_
  24.7 3.3 %collective-permute-done.7.refs_3_ = s16[72,256]{1,0:T(8,128)(2,1)S(1)} collective-permute-done((s16[72,256]{1,0:T(8,128)(2,1)S(1)}, s16[72,256]{1,0:T(8,128)(2,1)S(1)}, u32[]{:S(2)}, u32[]{:S(2)}) %collective-permute-start.7) | collective-permute-done | bytes 36896 | tf_op jit(solution)/shard_map/ppermute | solution.py:467
  28.0 0.0 collective-permute-done.8.refs_4_
  28.1 0.1 collective-permute-start.9
  28.2 1.2 %collective-permute-done.9.other = bf16[64,256]{1,0:T(8,128)(2,1)S(1)} collective-permute-done((bf16[64,256]{1,0:T(8,128)(2,1)S(1)}, bf16[64,256]{1,0:T(8,128)(2,1)S(1)}, u32[]{:S(2)}, u32[]{:S(2)}) %collective-permute-start.9) | collective-permute-done | bytes 32800 | tf_op jit(solution)/shard_map/ppermute | solution.py:521
  29.4 0.1 rows_to_send.1
  29.5 9.9 %all_to_all.11 = bf16[16,8,256]{2,1,0:T(8,128)(2,1)S(1)} all-to-all(bf16[16,8,256]{2,1,0:T(8,128)(2,1)S(1)} %bitcast.11), channel_id=1, replica_groups={{15,14,13,12,11,10,9,8,7,6,5,4,3,2,1,0},{31,30,29,28,27,26,25,24,23,22,..., dimensions={0} | all-to-all | bytes 131072 | tf_op jit(solution)/shard_map/all_to_all | solution.py:523
  39.4 0.0 copy-done.2
  39.4 0.0 copy-done.3
  39.4 1.0 %logits.1 = f32[64,172]{1,0:T(8,128)} custom-call(bf16[64,256]{1,0:T(8,128)(2,1)S(1)} %hidden_rows.1.own, bf16[64,256]{1,0:T(8,128)(2,1)S(1)} %collective-permute-done.9.other, bf16[128,256]{1,0:T(8,128)(2,1)S(1)} %bitcast.12, bf16[128,128]{1,0:T(8,128)(2,1)S(1)} %get-tuple-element.39.front, bf16[64,128]{1,0:T(8,128)(2,1)S(1)} %get-tuple-element.40.adj_received, ...), custom_call_target="tpu_custom_call" | custom-call | tf_op jit(solution)/shard_map/logits/pallas_call | solution.py:454
  (1 shorter events, 0.0 us)
Async XLA Ops:
  0.0 3.1 %collective-permute-start.1 = (bf16[1024,512]{1,0:T(8,128)(2,1)}, bf16[1024,512]{1,0:T(8,128)(2,1)S(1)}, u32[]{:S(2)}, u32[]{:S(2)}) collective-permute-start(bf16[1024,512]{1,0:T(8,128)(2,1)} %xo.1), channel_id=1, source_target_pairs={{0,16},{16,0},{1,17},{17,1},{2,18},{18,2},{3,19},{19,3},{4,20},{20... | collective-permute-start | bytes 3145736 | tf_op jit(solution)/shard_map/ppermute | solution.py:494
  0.5 7.6 %collective-permute-start = (bf16[512,256]{1,0:T(8,128)(2,1)}, bf16[512,256]{1,0:T(8,128)(2,1)S(1)}, u32[]{:S(2)}, u32[]{:S(2)}) collective-permute-start(bf16[512,256]{1,0:T(8,128)(2,1)} %wo.5), channel_id=1, source_target_pairs={{0,16},{16,0},{1,17},{17,1},{2,18},{18,2},{3,19},{19,3},{4,20},{20... | collective-permute-start | bytes 786440 | tf_op jit(solution)/shard_map/ppermute | solution.py:495
  3.2 4.9 %copy-start = (bf16[512,256]{1,0:T(8,128)(2,1)S(1)}, bf16[512,256]{1,0:T(8,128)(2,1)}, u32[]{:S(2)}) copy-start(bf16[512,256]{1,0:T(8,128)(2,1)} %wo.5) | copy-start | bytes 786436
  8.6 5.5 %copy-start.1 = (bf16[512,256]{1,0:T(8,128)(2,1)S(1)}, bf16[512,256]{1,0:T(8,128)(2,1)}, u32[]{:S(2)}) copy-start(bf16[512,256]{1,0:T(8,128)(2,1)} %so.1) | copy-start | bytes 786436
  8.6 8.1 %collective-permute-start.4 = (s16[264,256]{1,0:T(8,128)(2,1)S(1)}, s16[264,256]{1,0:T(8,128)(2,1)S(1)}, u32[]{:S(2)}, u32[]{:S(2)}) collective-permute-start(s16[264,256]{1,0:T(8,128)(2,1)S(1)} %sent_terms.3), channel_id=1, source_target_pairs={{0,3},{1,2},{2,1},{3,0},{4,7},{5,6},{6,5},{7,4},{8,11},{9,10},{10,... | collective-permute-start | bytes 405512 | tf_op jit(solution)/shard_map/ppermute | solution.py:467
  13.4 6.1 %collective-permute-start.2 = (s16[264,256]{1,0:T(8,128)(2,1)S(1)}, s16[264,256]{1,0:T(8,128)(2,1)S(1)}, u32[]{:S(2)}, u32[]{:S(2)}) collective-permute-start(s16[264,256]{1,0:T(8,128)(2,1)S(1)} %get-tuple-element.31), channel_id=1, source_target_pairs={{0,1},{1,0},{2,3},{3,2},{4,5},{5,4},{6,7},{7,6},{8,9},{9,8},{10,11... | collective-permute-start | bytes 405512 | tf_op jit(solution)/shard_map/ppermute | solution.py:467
  14.0 9.9 %copy-start.4 = (s32[16,16,8]{1,2,0:T(8,128)S(1)}, s32[16,16,8]{1,2,0:T(8,128)}, u32[]{:S(2)}) copy-start(s32[16,16,8]{1,2,0:T(8,128)} %param.19) | copy-start | bytes 24580
  14.0 10.0 %copy-start.5 = (bf16[64,256]{1,0:T(8,128)(2,1)S(1)}, bf16[64,256]{1,0:T(8,128)(2,1)}, u32[]{:S(2)}) copy-start(bf16[64,256]{1,0:T(8,128)(2,1)} %adj.1) | copy-start | bytes 98308
  14.0 10.0 %copy-start.6 = (s32[16,16]{1,0:T(8,128)S(1)}, s32[16,16]{1,0:T(8,128)}, u32[]{:S(2)}) copy-start(s32[16,16]{1,0:T(8,128)} %counts.1) | copy-start | bytes 3076
  14.0 5.5 %collective-permute-start.3 = (s16[264,256]{1,0:T(8,128)(2,1)S(1)}, s16[264,256]{1,0:T(8,128)(2,1)S(1)}, u32[]{:S(2)}, u32[]{:S(2)}) collective-permute-start(s16[264,256]{1,0:T(8,128)(2,1)S(1)} %get-tuple-element.32), channel_id=1, source_target_pairs={{0,2},{1,3},{2,0},{3,1},{4,6},{5,7},{6,4},{7,5},{8,10},{9,11},{10,... | collective-permute-start | bytes 405512 | tf_op jit(solution)/shard_map/ppermute | solution.py:467
  15.1 24.3 %copy-start.2 = (bf16[256,172]{0,1:T(8,128)(2,1)S(1)}, bf16[256,172]{0,1:T(8,128)(2,1)}, u32[]{:S(2)}) copy-start(bf16[256,172]{0,1:T(8,128)(2,1)} %param.22) | copy-start | bytes 264196
  15.2 24.3 %copy-start.3 = (bf16[256,172]{0,1:T(8,128)(2,1)S(1)}, bf16[256,172]{0,1:T(8,128)(2,1)}, u32[]{:S(2)}) copy-start(bf16[256,172]{0,1:T(8,128)(2,1)} %param.23) | copy-start | bytes 264196
  15.2 9.5 %collective-permute-start.5 = (f32[64,256]{1,0:T(8,128)S(1)}, f32[64,256]{1,0:T(8,128)S(1)}, u32[]{:S(2)}, u32[]{:S(2)}) collective-permute-start(f32[64,256]{1,0:T(8,128)S(1)} %get-tuple-element.34), channel_id=1, source_target_pairs={{0,16},{16,0},{1,17},{17,1},{2,18},{18,2},{3,19},{19,3},{4,20},{20... | collective-permute-start | bytes 196616 | tf_op jit(solution)/shard_map/ppermute | solution.py:510
  19.7 5.0 %collective-permute-start.6 = (s16[72,256]{1,0:T(8,128)(2,1)S(1)}, s16[72,256]{1,0:T(8,128)(2,1)S(1)}, u32[]{:S(2)}, u32[]{:S(2)}) collective-permute-start(s16[72,256]{1,0:T(8,128)(2,1)S(1)} %get-tuple-element.35), channel_id=1, source_target_pairs={{0,8},{1,9},{2,10},{3,11},{4,12},{5,13},{6,14},{7,15},{8,0},{9,1},... | collective-permute-start | bytes 110600 | tf_op jit(solution)/shard_map/ppermute | solution.py:467
  22.3 5.8 %collective-permute-start.7 = (s16[72,256]{1,0:T(8,128)(2,1)S(1)}, s16[72,256]{1,0:T(8,128)(2,1)S(1)}, u32[]{:S(2)}, u32[]{:S(2)}) collective-permute-start(s16[72,256]{1,0:T(8,128)(2,1)S(1)} %get-tuple-element.36), channel_id=1, source_target_pairs={{0,12},{1,13},{2,14},{3,15},{4,8},{5,9},{6,10},{7,11},{8,4},{9,5},... | collective-permute-start | bytes 110600 | tf_op jit(solution)/shard_map/ppermute | solution.py:467
  23.6 4.4 %collective-permute-start.8 = (s16[72,256]{1,0:T(8,128)(2,1)S(1)}, s16[72,256]{1,0:T(8,128)(2,1)S(1)}, u32[]{:S(2)}, u32[]{:S(2)}) collective-permute-start(s16[72,256]{1,0:T(8,128)(2,1)S(1)} %get-tuple-element.37), channel_id=1, source_target_pairs={{0,4},{1,5},{2,6},{3,7},{4,0},{5,1},{6,2},{7,3},{8,12},{9,13},{10,... | collective-permute-start | bytes 110600 | tf_op jit(solution)/shard_map/ppermute | solution.py:467
  28.1 1.3 %collective-permute-start.9 = (bf16[64,256]{1,0:T(8,128)(2,1)S(1)}, bf16[64,256]{1,0:T(8,128)(2,1)S(1)}, u32[]{:S(2)}, u32[]{:S(2)}) collective-permute-start(bf16[64,256]{1,0:T(8,128)(2,1)S(1)} %hidden_rows.1.own), channel_id=1, source_target_pairs={{0,16},{16,0},{1,17},{17,1},{2,18},{18,2},{3,19},{19,3},{4,20},{20... | collective-permute-start | bytes 98312 | tf_op jit(solution)/shard_map/ppermute | solution.py:521

commit v30 on v29

--- a/solution.py
+++ b/solution.py
@@ -8,8 +8,8 @@
 from jax.sharding import PartitionSpec as P
 
 UNIT = 16
-BLOCK = 4
-STEP = 16
+BLOCK = 8
+STEP = 8
 PART = 256
 CHUNKS = 1
 

time: 40.7 us -> 40.7 us (level)
  starting transfers between devices: 9.55 us -> 10.7 us
  waiting for transfers between devices: 8.77 us -> 8.3 us
    ppermute x6, starting transfers between devices: 8.9 us -> 10 us  [exchange(): lax.ppermute(parts[k], 'dom', [(i, i ^ k * stride) for i in range(n)])]
    ppermute x6, waiting for transfers between devices: 7.57 us -> 7.1 us  [exchange(): lax.ppermute(parts[k], 'dom', [(i, i ^ k * stride) for i in range(n)])]
  transfers between devices with their start and end apart: 10 -> 10, of which waited for: 4 -> 5; matrix products, arithmetic and copies ran while one was open for 0% -> 0% of each run, Pallas kernels for 25% -> 25%
where the time goes in v30:
time: 40.7 us; the launch traced here: 40.5 us
  Pallas kernels  11.6 us (29%)
  starting transfers between devices  10.7 us (26%)
  blocking collectives  9.67 us (24%)
  waiting for transfers between devices  8.3 us (20%)
    ppermute x6, starting transfers between devices, exchange(): lax.ppermute(parts[k], 'dom', [(i, i ^ k * stride) for i in range(n)])  10 us
    all_to_all x1, blocking collectives, body(): lax.all_to_all(send, 'dom', 0, 0, axis_index_groups=[group_order(n)], til...  9.67 us
    ppermute x6, waiting for transfers between devices, exchange(): lax.ppermute(parts[k], 'dom', [(i, i ^ k * stride) for i in range(n)])  7.1 us
    pallas_call x1, Pallas kernels, gathered_sums(): pl.pallas_call(tiles_kernel, out_shape=[sums] * parts, in_specs=[vmem] *...  4.61 us
    pallas_call x1, Pallas kernels, plan(): pl.pallas_call(functools.partial(plan_kernel, chunks, per, n, radix, n_sr...  2.55 us
    pallas_call x2, Pallas kernels, sent_terms(): pl.pallas_call(functools.partial(sent_kernel, ks, slots, rows, len(accs))...  1.38 us
    ppermute x1, waiting for transfers between devices, body(): other = lax.ppermute(own, 'feat', swap)  1.19 us
    pallas_call x1, Pallas kernels, own_terms(): pl.pallas_call(functools.partial(own_kernel, chunk, per, groups, len(accs...  1.03 us
  transfers between devices with their start and end apart: 10, of which 5 were waited for; matrix products, arithmetic and copies ran while one was open for 0% of the time, Pallas kernels for 25%

profile of v30, /device:TPU:0, one launch (start us, length us, event | category | flops | bytes accessed | tf_op | source)
XLA Modules:
  0.0 40.5 jit_solution(4671644971279715636)
XLA Ops:
  0.0 0.5 %collective-permute-start.1 = (bf16[1024,512]{1,0:T(8,128)(2,1)}, bf16[1024,512]{1,0:T(8,128)(2,1)S(1)}, u32[]{:S(2)}, u32[]{:S(2)}) collective-permute-start(bf16[1024,512]{1,0:T(8,128)(2,1)} %xo.1), channel_id=1, source_target_pairs={{0,16},{16,0},{1,17},{17,1},{2,18},{18,2},{3,19},{19,3},{4,20},{20... | collective-permute-start | bytes 3145736 | tf_op jit(solution)/shard_map/ppermute | solution.py:494
  0.5 0.1 collective-permute-start
  0.5 0.1 pad_add_fusion.ids
  0.6 2.5 %plan.1 = (s32[4,640]{1,0:T(4,128)S(1)}, bf16[512,16,128]{2,1,0:T(8,128)(2,1)S(1)}, bf16[1024,512]{1,0:T(8,128)(2,1)S(1)}) custom-call(s32[2]{0:T(128)S(1)} %pad_add_fusion.ids, s32[1,128]{1,0:T(1,128)} %bitcast.17, s32[1,128]{1,0:T(1,128)} %bitcast.18, s32[1,128]{1,0:T(1,128)} %bitcast.19, bf16[128,8,16,128]{3,2,1,0:T(8,128)(2,1)} %bitcast.16, ...), custom_call_target="tpu_custom_call" | custom-call | tf_op jit(solution)/shard_map/plan/pallas_call | solution.py:144
  3.1 0.0 collective-permute-done.1.xp
  3.2 0.0 copy-start
  3.2 4.6 %gathered_sums.1 = (f32[65,16,256]{2,1,0:T(8,128)S(1)}, f32[65,16,256]{2,1,0:T(8,128)S(1)}, f32[65,16,256]{2,1,0:T(8,128)S(1)}, f32[65,16,256]{2,1,0:T(8,128)S(1)}) custom-call(s32[4,640]{1,0:T(4,128)S(1)} %get-tuple-element.24.table_v, bf16[512,16,128]{2,1,0:T(8,128)(2,1)S(1)} %get-tuple-element.25.tbuf, bf16[1024,512]{1,0:T(8,128)(2,1)S(1)} %get-tuple-element.23.xo, ...), custom_call_target="tpu_custom_call" | custom-call | flops 2147483648 | bytes 8388608 | tf_op jit(solution)/shard_map/gathered_sums/pallas_call | solution.py:267
  7.8 0.0 collective-permute-done.wp
  7.8 0.0 copy-done
  7.8 0.5 %sent_terms.3 = s16[264,256]{1,0:T(8,128)(2,1)S(1)} custom-call(bf16[512,256]{1,0:T(8,128)(2,1)S(1)} %copy-done, bf16[512,256]{1,0:T(8,128)(2,1)S(1)} %collective-permute-done.wp, f32[65,16,256]{2,1,0:T(8,128)S(1)} %get-tuple-element.26.refs_0_, f32[65,16,256]{2,1,0:T(8,128)S(1)} %get-tuple-element.27.refs_1_, f32[65,16,256]{2,1,0:T(8,128)S(1)} %get-tuple-element.28.refs_2_, ...), custom_call_target="tpu_custom_call" | custom-call | flops 268435456 | bytes 2097152 | tf_op jit(solution)/shard_map/sent_terms/pallas_call | solution.py:317
  8.3 0.0 copy-start.1
  8.3 4.0 %collective-permute-start.4 = (s16[264,256]{1,0:T(8,128)(2,1)S(1)}, s16[264,256]{1,0:T(8,128)(2,1)S(1)}, u32[]{:S(2)}, u32[]{:S(2)}) collective-permute-start(s16[264,256]{1,0:T(8,128)(2,1)S(1)} %sent_terms.3), channel_id=1, source_target_pairs={{0,3},{1,2},{2,1},{3,0},{4,7},{5,6},{6,5},{7,4},{8,11},{9,10},{10,... | collective-permute-start | bytes 405512 | tf_op jit(solution)/shard_map/ppermute | solution.py:467
  12.3 0.9 %sent_terms.2 = (s16[264,256]{1,0:T(8,128)(2,1)S(1)}, s16[264,256]{1,0:T(8,128)(2,1)S(1)}) custom-call(bf16[512,256]{1,0:T(8,128)(2,1)S(1)} %copy-done, bf16[512,256]{1,0:T(8,128)(2,1)S(1)} %collective-permute-done.wp, f32[65,16,256]{2,1,0:T(8,128)S(1)} %get-tuple-element.26.refs_0_, f32[65,16,256]{2,1,0:T(8,128)S(1)} %get-tuple-element.27.refs_1_, ...), custom_call_target="tpu_custom_call" | custom-call | flops 536870912 | bytes 2097152 | tf_op jit(solution)/shard_map/sent_terms/pallas_call | solution.py:317
  13.2 0.2 collective-permute-start.2
  13.5 0.0 copy-start.4
  13.5 0.0 copy-start.5
  13.5 0.0 copy-start.6
  13.5 0.9 %collective-permute-start.3 = (s16[264,256]{1,0:T(8,128)(2,1)S(1)}, s16[264,256]{1,0:T(8,128)(2,1)S(1)}, u32[]{:S(2)}, u32[]{:S(2)}) collective-permute-start(s16[264,256]{1,0:T(8,128)(2,1)S(1)} %get-tuple-element.32), channel_id=1, source_target_pairs={{0,2},{1,3},{2,0},{3,1},{4,6},{5,7},{6,4},{7,5},{8,10},{9,11},{10,... | collective-permute-start | bytes 405512 | tf_op jit(solution)/shard_map/ppermute | solution.py:467
  14.4 0.0 copy-done.1
  14.4 1.0 %own_terms.1 = (f32[256,256]{1,0:T(8,128)S(1)}, f32[64,256]{1,0:T(8,128)S(1)}) custom-call(s32[2]{0:T(128)S(1)} %pad_add_fusion.ids, bf16[512,256]{1,0:T(8,128)(2,1)S(1)} %copy-done, bf16[512,256]{1,0:T(8,128)(2,1)S(1)} %collective-permute-done.wp, bf16[1024,512]{1,0:T(8,128)(2,1)S(1)} %get-tuple-element.23.xo, bf16[512,256]{1,0:T(8,128)(2,1)S(1)} %copy-done.1, ...), custom_call_target="tpu_custom_call" | custom-call | flops 268435456 | bytes 2097152 | tf_op jit(solution)/shard_map/own_terms/pallas_call | solution.py:350
  15.4 0.0 copy-start.2
  15.4 0.0 copy-start.3
  15.4 0.1 collective-permute-start.5
  15.5 0.8 %collective-permute-done.4.refs_2_ = s16[264,256]{1,0:T(8,128)(2,1)S(1)} collective-permute-done((s16[264,256]{1,0:T(8,128)(2,1)S(1)}, s16[264,256]{1,0:T(8,128)(2,1)S(1)}, u32[]{:S(2)}, u32[]{:S(2)}) %collective-permute-start.4) | collective-permute-done | bytes 135200 | tf_op jit(solution)/shard_map/ppermute | solution.py:467
  16.3 2.6 %collective-permute-done.2.refs_0_ = s16[264,256]{1,0:T(8,128)(2,1)S(1)} collective-permute-done((s16[264,256]{1,0:T(8,128)(2,1)S(1)}, s16[264,256]{1,0:T(8,128)(2,1)S(1)}, u32[]{:S(2)}, u32[]{:S(2)}) %collective-permute-start.2) | collective-permute-done | bytes 135200 | tf_op jit(solution)/shard_map/ppermute | solution.py:467
  18.9 0.1 collective-permute-done.3.refs_1_
  19.0 0.2 combine.1
  19.2 3.5 %collective-permute-start.6 = (s16[72,256]{1,0:T(8,128)(2,1)S(1)}, s16[72,256]{1,0:T(8,128)(2,1)S(1)}, u32[]{:S(2)}, u32[]{:S(2)}) collective-permute-start(s16[72,256]{1,0:T(8,128)(2,1)S(1)} %get-tuple-element.35), channel_id=1, source_target_pairs={{0,8},{1,9},{2,10},{3,11},{4,12},{5,13},{6,14},{7,15},{8,0},{9,1},... | collective-permute-start | bytes 110600 | tf_op jit(solution)/shard_map/ppermute | solution.py:467
  22.6 0.9 %collective-permute-start.7 = (s16[72,256]{1,0:T(8,128)(2,1)S(1)}, s16[72,256]{1,0:T(8,128)(2,1)S(1)}, u32[]{:S(2)}, u32[]{:S(2)}) collective-permute-start(s16[72,256]{1,0:T(8,128)(2,1)S(1)} %get-tuple-element.36), channel_id=1, source_target_pairs={{0,12},{1,13},{2,14},{3,15},{4,8},{5,9},{6,10},{7,11},{8,4},{9,5},... | collective-permute-start | bytes 110600 | tf_op jit(solution)/shard_map/ppermute | solution.py:467
  23.6 0.5 %collective-permute-start.8 = (s16[72,256]{1,0:T(8,128)(2,1)S(1)}, s16[72,256]{1,0:T(8,128)(2,1)S(1)}, u32[]{:S(2)}, u32[]{:S(2)}) collective-permute-start(s16[72,256]{1,0:T(8,128)(2,1)S(1)} %get-tuple-element.37), channel_id=1, source_target_pairs={{0,4},{1,5},{2,6},{3,7},{4,0},{5,1},{6,2},{7,3},{8,12},{9,13},{10,... | collective-permute-start | bytes 110600 | tf_op jit(solution)/shard_map/ppermute | solution.py:467
  24.1 0.0 copy-done.4
  24.1 0.0 copy-done.5
  24.1 0.0 copy-done.6
  24.1 0.7 %selection.1 = (bf16[128,128]{1,0:T(8,128)(2,1)S(1)}, bf16[128,128]{1,0:T(8,128)(2,1)S(1)}, bf16[64,128]{1,0:T(8,128)(2,1)S(1)}) custom-call(s32[2]{0:T(128)S(1)} %pad_add_fusion.ids, s32[16,8,16]{2,1,0:T(8,128)S(1)} %bitcast.15, s32[16,16]{1,0:T(8,128)S(1)} %copy-done.6, bf16[64,256]{1,0:T(8,128)(2,1)S(1)} %copy-done.5), custom_call_target="tpu_custom_call" | custom-call | tf_op jit(solution)/shard_map/selection/pallas_call | solution.py:200
  24.8 0.0 collective-permute-done.5.refs_1_
  24.8 0.0 collective-permute-done.6.refs_2_
  24.8 3.6 %collective-permute-done.7.refs_3_ = s16[72,256]{1,0:T(8,128)(2,1)S(1)} collective-permute-done((s16[72,256]{1,0:T(8,128)(2,1)S(1)}, s16[72,256]{1,0:T(8,128)(2,1)S(1)}, u32[]{:S(2)}, u32[]{:S(2)}) %collective-permute-start.7) | collective-permute-done | bytes 36896 | tf_op jit(solution)/shard_map/ppermute | solution.py:467
  28.4 0.0 collective-permute-done.8.refs_4_
  28.4 0.1 collective-permute-start.9
  28.5 1.2 %collective-permute-done.9.other = bf16[64,256]{1,0:T(8,128)(2,1)S(1)} collective-permute-done((bf16[64,256]{1,0:T(8,128)(2,1)S(1)}, bf16[64,256]{1,0:T(8,128)(2,1)S(1)}, u32[]{:S(2)}, u32[]{:S(2)}) %collective-permute-start.9) | collective-permute-done | bytes 32800 | tf_op jit(solution)/shard_map/ppermute | solution.py:521
  29.7 0.1 rows_to_send.1
  29.9 9.7 %all_to_all.11 = bf16[16,8,256]{2,1,0:T(8,128)(2,1)S(1)} all-to-all(bf16[16,8,256]{2,1,0:T(8,128)(2,1)S(1)} %bitcast.11), channel_id=1, replica_groups={{15,14,13,12,11,10,9,8,7,6,5,4,3,2,1,0},{31,30,29,28,27,26,25,24,23,22,..., dimensions={0} | all-to-all | bytes 131072 | tf_op jit(solution)/shard_map/all_to_all | solution.py:523
  39.5 0.0 copy-done.2
  39.5 0.0 copy-done.3
  39.5 1.0 %logits.1 = f32[64,172]{1,0:T(8,128)} custom-call(bf16[64,256]{1,0:T(8,128)(2,1)S(1)} %hidden_rows.1.own, bf16[64,256]{1,0:T(8,128)(2,1)S(1)} %collective-permute-done.9.other, bf16[128,256]{1,0:T(8,128)(2,1)S(1)} %bitcast.12, bf16[128,128]{1,0:T(8,128)(2,1)S(1)} %get-tuple-element.39.front, bf16[64,128]{1,0:T(8,128)(2,1)S(1)} %get-tuple-element.40.adj_received, ...), custom_call_target="tpu_custom_call" | custom-call | tf_op jit(solution)/shard_map/logits/pallas_call | solution.py:454
  (1 shorter events, 0.0 us)
Async XLA Ops:
  0.0 3.1 %collective-permute-start.1 = (bf16[1024,512]{1,0:T(8,128)(2,1)}, bf16[1024,512]{1,0:T(8,128)(2,1)S(1)}, u32[]{:S(2)}, u32[]{:S(2)}) collective-permute-start(bf16[1024,512]{1,0:T(8,128)(2,1)} %xo.1), channel_id=1, source_target_pairs={{0,16},{16,0},{1,17},{17,1},{2,18},{18,2},{3,19},{19,3},{4,20},{20... | collective-permute-start | bytes 3145736 | tf_op jit(solution)/shard_map/ppermute | solution.py:494
  0.5 7.3 %collective-permute-start = (bf16[512,256]{1,0:T(8,128)(2,1)}, bf16[512,256]{1,0:T(8,128)(2,1)S(1)}, u32[]{:S(2)}, u32[]{:S(2)}) collective-permute-start(bf16[512,256]{1,0:T(8,128)(2,1)} %wo.5), channel_id=1, source_target_pairs={{0,16},{16,0},{1,17},{17,1},{2,18},{18,2},{3,19},{19,3},{4,20},{20... | collective-permute-start | bytes 786440 | tf_op jit(solution)/shard_map/ppermute | solution.py:495
  3.2 4.6 %copy-start = (bf16[512,256]{1,0:T(8,128)(2,1)S(1)}, bf16[512,256]{1,0:T(8,128)(2,1)}, u32[]{:S(2)}) copy-start(bf16[512,256]{1,0:T(8,128)(2,1)} %wo.5) | copy-start | bytes 786436
  8.3 6.0 %copy-start.1 = (bf16[512,256]{1,0:T(8,128)(2,1)S(1)}, bf16[512,256]{1,0:T(8,128)(2,1)}, u32[]{:S(2)}) copy-start(bf16[512,256]{1,0:T(8,128)(2,1)} %so.1) | copy-start | bytes 786436
  8.3 8.0 %collective-permute-start.4 = (s16[264,256]{1,0:T(8,128)(2,1)S(1)}, s16[264,256]{1,0:T(8,128)(2,1)S(1)}, u32[]{:S(2)}, u32[]{:S(2)}) collective-permute-start(s16[264,256]{1,0:T(8,128)(2,1)S(1)} %sent_terms.3), channel_id=1, source_target_pairs={{0,3},{1,2},{2,1},{3,0},{4,7},{5,6},{6,5},{7,4},{8,11},{9,10},{10,... | collective-permute-start | bytes 405512 | tf_op jit(solution)/shard_map/ppermute | solution.py:467
  13.2 5.7 %collective-permute-start.2 = (s16[264,256]{1,0:T(8,128)(2,1)S(1)}, s16[264,256]{1,0:T(8,128)(2,1)S(1)}, u32[]{:S(2)}, u32[]{:S(2)}) collective-permute-start(s16[264,256]{1,0:T(8,128)(2,1)S(1)} %get-tuple-element.31), channel_id=1, source_target_pairs={{0,1},{1,0},{2,3},{3,2},{4,5},{5,4},{6,7},{7,6},{8,9},{9,8},{10,11... | collective-permute-start | bytes 405512 | tf_op jit(solution)/shard_map/ppermute | solution.py:467
  13.5 10.6 %copy-start.4 = (s32[16,16,8]{1,2,0:T(8,128)S(1)}, s32[16,16,8]{1,2,0:T(8,128)}, u32[]{:S(2)}) copy-start(s32[16,16,8]{1,2,0:T(8,128)} %param.19) | copy-start | bytes 24580
  13.5 10.6 %copy-start.5 = (bf16[64,256]{1,0:T(8,128)(2,1)S(1)}, bf16[64,256]{1,0:T(8,128)(2,1)}, u32[]{:S(2)}) copy-start(bf16[64,256]{1,0:T(8,128)(2,1)} %adj.1) | copy-start | bytes 98308
  13.5 10.6 %copy-start.6 = (s32[16,16]{1,0:T(8,128)S(1)}, s32[16,16]{1,0:T(8,128)}, u32[]{:S(2)}) copy-start(s32[16,16]{1,0:T(8,128)} %counts.1) | copy-start | bytes 3076
  13.5 5.5 %collective-permute-start.3 = (s16[264,256]{1,0:T(8,128)(2,1)S(1)}, s16[264,256]{1,0:T(8,128)(2,1)S(1)}, u32[]{:S(2)}, u32[]{:S(2)}) collective-permute-start(s16[264,256]{1,0:T(8,128)(2,1)S(1)} %get-tuple-element.32), channel_id=1, source_target_pairs={{0,2},{1,3},{2,0},{3,1},{4,6},{5,7},{6,4},{7,5},{8,10},{9,11},{10,... | collective-permute-start | bytes 405512 | tf_op jit(solution)/shard_map/ppermute | solution.py:467
  15.4 24.1 %copy-start.2 = (bf16[256,172]{0,1:T(8,128)(2,1)S(1)}, bf16[256,172]{0,1:T(8,128)(2,1)}, u32[]{:S(2)}) copy-start(bf16[256,172]{0,1:T(8,128)(2,1)} %param.22) | copy-start | bytes 264196
  15.4 24.1 %copy-start.3 = (bf16[256,172]{0,1:T(8,128)(2,1)S(1)}, bf16[256,172]{0,1:T(8,128)(2,1)}, u32[]{:S(2)}) copy-start(bf16[256,172]{0,1:T(8,128)(2,1)} %param.23) | copy-start | bytes 264196
  15.4 9.3 %collective-permute-start.5 = (f32[64,256]{1,0:T(8,128)S(1)}, f32[64,256]{1,0:T(8,128)S(1)}, u32[]{:S(2)}, u32[]{:S(2)}) collective-permute-start(f32[64,256]{1,0:T(8,128)S(1)} %get-tuple-element.34), channel_id=1, source_target_pairs={{0,16},{16,0},{1,17},{17,1},{2,18},{18,2},{3,19},{19,3},{4,20},{20... | collective-permute-start | bytes 196616 | tf_op jit(solution)/shard_map/ppermute | solution.py:510
  19.2 5.6 %collective-permute-start.6 = (s16[72,256]{1,0:T(8,128)(2,1)S(1)}, s16[72,256]{1,0:T(8,128)(2,1)S(1)}, u32[]{:S(2)}, u32[]{:S(2)}) collective-permute-start(s16[72,256]{1,0:T(8,128)(2,1)S(1)} %get-tuple-element.35), channel_id=1, source_target_pairs={{0,8},{1,9},{2,10},{3,11},{4,12},{5,13},{6,14},{7,15},{8,0},{9,1},... | collective-permute-start | bytes 110600 | tf_op jit(solution)/shard_map/ppermute | solution.py:467
  22.6 5.8 %collective-permute-start.7 = (s16[72,256]{1,0:T(8,128)(2,1)S(1)}, s16[72,256]{1,0:T(8,128)(2,1)S(1)}, u32[]{:S(2)}, u32[]{:S(2)}) collective-permute-start(s16[72,256]{1,0:T(8,128)(2,1)S(1)} %get-tuple-element.36), channel_id=1, source_target_pairs={{0,12},{1,13},{2,14},{3,15},{4,8},{5,9},{6,10},{7,11},{8,4},{9,5},... | collective-permute-start | bytes 110600 | tf_op jit(solution)/shard_map/ppermute | solution.py:467
  23.6 4.8 %collective-permute-start.8 = (s16[72,256]{1,0:T(8,128)(2,1)S(1)}, s16[72,256]{1,0:T(8,128)(2,1)S(1)}, u32[]{:S(2)}, u32[]{:S(2)}) collective-permute-start(s16[72,256]{1,0:T(8,128)(2,1)S(1)} %get-tuple-element.37), channel_id=1, source_target_pairs={{0,4},{1,5},{2,6},{3,7},{4,0},{5,1},{6,2},{7,3},{8,12},{9,13},{10,... | collective-permute-start | bytes 110600 | tf_op jit(solution)/shard_map/ppermute | solution.py:467
  28.4 1.3 %collective-permute-start.9 = (bf16[64,256]{1,0:T(8,128)(2,1)S(1)}, bf16[64,256]{1,0:T(8,128)(2,1)S(1)}, u32[]{:S(2)}, u32[]{:S(2)}) collective-permute-start(bf16[64,256]{1,0:T(8,128)(2,1)S(1)} %hidden_rows.1.own), channel_id=1, source_target_pairs={{0,16},{16,0},{1,17},{17,1},{2,18},{18,2},{3,19},{19,3},{4,20},{20... | collective-permute-start | bytes 98312 | tf_op jit(solution)/shard_map/ppermute | solution.py:521

commit v31 on v30

--- a/solution.py
+++ b/solution.py
@@ -9,7 +9,7 @@
 
 UNIT = 16
 BLOCK = 8
-STEP = 8
+STEP = 12
 PART = 256
 CHUNKS = 1
 

time: 40.7 us -> 40.5 us (level)
  starting transfers between devices: 10.7 us -> 9.63 us
  waiting for transfers between devices: 8.3 us -> 9.26 us
    ppermute x6, starting transfers between devices: 10 us -> 8.98 us  [exchange(): lax.ppermute(parts[k], 'dom', [(i, i ^ k * stride) for i in range(n)])]
    ppermute x6, waiting for transfers between devices: 7.1 us -> 8.06 us  [exchange(): lax.ppermute(parts[k], 'dom', [(i, i ^ k * stride) for i in range(n)])]
  transfers between devices with their start and end apart: 10 -> 10, of which waited for: 5 -> 4; matrix products, arithmetic and copies ran while one was open for 0% -> 0% of each run, Pallas kernels for 25% -> 25%
where the time goes in v31:
time: 40.5 us
  Pallas kernels  11.6 us (29%)
  blocking collectives  9.67 us (24%)
  starting transfers between devices  9.63 us (24%)
  waiting for transfers between devices  9.26 us (23%)
    all_to_all x1, blocking collectives, body(): lax.all_to_all(send, 'dom', 0, 0, axis_index_groups=[group_order(n)], til...  9.67 us
    ppermute x6, starting transfers between devices, exchange(): lax.ppermute(parts[k], 'dom', [(i, i ^ k * stride) for i in range(n)])  8.98 us
    ppermute x6, waiting for transfers between devices, exchange(): lax.ppermute(parts[k], 'dom', [(i, i ^ k * stride) for i in range(n)])  8.06 us
    pallas_call x1, Pallas kernels, gathered_sums(): pl.pallas_call(tiles_kernel, out_shape=[sums] * parts, in_specs=[vmem] *...  4.62 us
    pallas_call x1, Pallas kernels, plan(): pl.pallas_call(functools.partial(plan_kernel, chunks, per, n, radix, n_sr...  2.55 us
    pallas_call x2, Pallas kernels, sent_terms(): pl.pallas_call(functools.partial(sent_kernel, ks, slots, rows, len(accs))...  1.38 us
    ppermute x1, waiting for transfers between devices, body(): other = lax.ppermute(own, 'feat', swap)  1.19 us
    pallas_call x1, Pallas kernels, own_terms(): pl.pallas_call(functools.partial(own_kernel, chunk, per, groups, len(accs...  1.03 us
  transfers between devices with their start and end apart: 10, of which 4 were waited for; matrix products, arithmetic and copies ran while one was open for 0% of the time, Pallas kernels for 25%

profile of v31, /device:TPU:0, one launch (start us, length us, event | category | flops | bytes accessed | tf_op | source)
XLA Modules:
  0.0 40.5 jit_solution(5576733667612543401)
XLA Ops:
  0.0 0.5 %collective-permute-start.1 = (bf16[1024,512]{1,0:T(8,128)(2,1)}, bf16[1024,512]{1,0:T(8,128)(2,1)S(1)}, u32[]{:S(2)}, u32[]{:S(2)}) collective-permute-start(bf16[1024,512]{1,0:T(8,128)(2,1)} %xo.1), channel_id=1, source_target_pairs={{0,16},{16,0},{1,17},{17,1},{2,18},{18,2},{3,19},{19,3},{4,20},{20... | collective-permute-start | bytes 3145736 | tf_op jit(solution)/shard_map/ppermute | solution.py:494
  0.5 0.1 collective-permute-start
  0.5 0.1 pad_add_fusion.ids
  0.6 2.5 %plan.1 = (s32[4,640]{1,0:T(4,128)S(1)}, bf16[512,16,128]{2,1,0:T(8,128)(2,1)S(1)}, bf16[1024,512]{1,0:T(8,128)(2,1)S(1)}) custom-call(s32[2]{0:T(128)S(1)} %pad_add_fusion.ids, s32[1,128]{1,0:T(1,128)} %bitcast.17, s32[1,128]{1,0:T(1,128)} %bitcast.18, s32[1,128]{1,0:T(1,128)} %bitcast.19, bf16[128,8,16,128]{3,2,1,0:T(8,128)(2,1)} %bitcast.16, ...), custom_call_target="tpu_custom_call" | custom-call | tf_op jit(solution)/shard_map/plan/pallas_call | solution.py:144
  3.1 0.0 collective-permute-done.1.xp
  3.2 0.0 copy-start
  3.2 4.6 %gathered_sums.1 = (f32[65,16,256]{2,1,0:T(8,128)S(1)}, f32[65,16,256]{2,1,0:T(8,128)S(1)}, f32[65,16,256]{2,1,0:T(8,128)S(1)}, f32[65,16,256]{2,1,0:T(8,128)S(1)}) custom-call(s32[4,640]{1,0:T(4,128)S(1)} %get-tuple-element.24.table_v, bf16[512,16,128]{2,1,0:T(8,128)(2,1)S(1)} %get-tuple-element.25.tbuf, bf16[1024,512]{1,0:T(8,128)(2,1)S(1)} %get-tuple-element.23.xo, ...), custom_call_target="tpu_custom_call" | custom-call | flops 2147483648 | bytes 8388608 | tf_op jit(solution)/shard_map/gathered_sums/pallas_call | solution.py:267
  7.8 0.0 collective-permute-done.wp
  7.8 0.0 copy-done
  7.8 0.5 %sent_terms.3 = s16[264,256]{1,0:T(8,128)(2,1)S(1)} custom-call(bf16[512,256]{1,0:T(8,128)(2,1)S(1)} %copy-done, bf16[512,256]{1,0:T(8,128)(2,1)S(1)} %collective-permute-done.wp, f32[65,16,256]{2,1,0:T(8,128)S(1)} %get-tuple-element.26.refs_0_, f32[65,16,256]{2,1,0:T(8,128)S(1)} %get-tuple-element.27.refs_1_, f32[65,16,256]{2,1,0:T(8,128)S(1)} %get-tuple-element.28.refs_2_, ...), custom_call_target="tpu_custom_call" | custom-call | flops 268435456 | bytes 2097152 | tf_op jit(solution)/shard_map/sent_terms/pallas_call | solution.py:317
  8.4 0.0 copy-start.1
  8.4 3.9 %collective-permute-start.4 = (s16[264,256]{1,0:T(8,128)(2,1)S(1)}, s16[264,256]{1,0:T(8,128)(2,1)S(1)}, u32[]{:S(2)}, u32[]{:S(2)}) collective-permute-start(s16[264,256]{1,0:T(8,128)(2,1)S(1)} %sent_terms.3), channel_id=1, source_target_pairs={{0,3},{1,2},{2,1},{3,0},{4,7},{5,6},{6,5},{7,4},{8,11},{9,10},{10,... | collective-permute-start | bytes 405512 | tf_op jit(solution)/shard_map/ppermute | solution.py:467
  12.3 0.9 %sent_terms.2 = (s16[264,256]{1,0:T(8,128)(2,1)S(1)}, s16[264,256]{1,0:T(8,128)(2,1)S(1)}) custom-call(bf16[512,256]{1,0:T(8,128)(2,1)S(1)} %copy-done, bf16[512,256]{1,0:T(8,128)(2,1)S(1)} %collective-permute-done.wp, f32[65,16,256]{2,1,0:T(8,128)S(1)} %get-tuple-element.26.refs_0_, f32[65,16,256]{2,1,0:T(8,128)S(1)} %get-tuple-element.27.refs_1_, ...), custom_call_target="tpu_custom_call" | custom-call | flops 536870912 | bytes 2097152 | tf_op jit(solution)/shard_map/sent_terms/pallas_call | solution.py:317
  13.2 0.7 %collective-permute-start.2 = (s16[264,256]{1,0:T(8,128)(2,1)S(1)}, s16[264,256]{1,0:T(8,128)(2,1)S(1)}, u32[]{:S(2)}, u32[]{:S(2)}) collective-permute-start(s16[264,256]{1,0:T(8,128)(2,1)S(1)} %get-tuple-element.31), channel_id=1, source_target_pairs={{0,1},{1,0},{2,3},{3,2},{4,5},{5,4},{6,7},{7,6},{8,9},{9,8},{10,11... | collective-permute-start | bytes 405512 | tf_op jit(solution)/shard_map/ppermute | solution.py:467
  13.8 0.0 copy-start.4
  13.8 0.0 copy-start.5
  13.8 0.0 copy-start.6
  13.8 0.1 collective-permute-start.3
  13.9 0.0 copy-done.1
  13.9 1.0 %own_terms.1 = (f32[256,256]{1,0:T(8,128)S(1)}, f32[64,256]{1,0:T(8,128)S(1)}) custom-call(s32[2]{0:T(128)S(1)} %pad_add_fusion.ids, bf16[512,256]{1,0:T(8,128)(2,1)S(1)} %copy-done, bf16[512,256]{1,0:T(8,128)(2,1)S(1)} %collective-permute-done.wp, bf16[1024,512]{1,0:T(8,128)(2,1)S(1)} %get-tuple-element.23.xo, bf16[512,256]{1,0:T(8,128)(2,1)S(1)} %copy-done.1, ...), custom_call_target="tpu_custom_call" | custom-call | flops 268435456 | bytes 2097152 | tf_op jit(solution)/shard_map/own_terms/pallas_call | solution.py:350
  15.0 0.0 copy-start.2
  15.0 0.0 copy-start.3
  15.0 0.1 collective-permute-start.5
  15.1 1.5 %collective-permute-done.4.refs_2_ = s16[264,256]{1,0:T(8,128)(2,1)S(1)} collective-permute-done((s16[264,256]{1,0:T(8,128)(2,1)S(1)}, s16[264,256]{1,0:T(8,128)(2,1)S(1)}, u32[]{:S(2)}, u32[]{:S(2)}) %collective-permute-start.4) | collective-permute-done | bytes 135200 | tf_op jit(solution)/shard_map/ppermute | solution.py:467
  16.6 2.7 %collective-permute-done.2.refs_0_ = s16[264,256]{1,0:T(8,128)(2,1)S(1)} collective-permute-done((s16[264,256]{1,0:T(8,128)(2,1)S(1)}, s16[264,256]{1,0:T(8,128)(2,1)S(1)}, u32[]{:S(2)}, u32[]{:S(2)}) %collective-permute-start.2) | collective-permute-done | bytes 135200 | tf_op jit(solution)/shard_map/ppermute | solution.py:467
  19.3 0.0 collective-permute-done.3.refs_1_
  19.3 0.2 combine.1
  19.5 3.1 %collective-permute-start.6 = (s16[72,256]{1,0:T(8,128)(2,1)S(1)}, s16[72,256]{1,0:T(8,128)(2,1)S(1)}, u32[]{:S(2)}, u32[]{:S(2)}) collective-permute-start(s16[72,256]{1,0:T(8,128)(2,1)S(1)} %get-tuple-element.35), channel_id=1, source_target_pairs={{0,8},{1,9},{2,10},{3,11},{4,12},{5,13},{6,14},{7,15},{8,0},{9,1},... | collective-permute-start | bytes 110600 | tf_op jit(solution)/shard_map/ppermute | solution.py:467
  22.6 1.0 %collective-permute-start.7 = (s16[72,256]{1,0:T(8,128)(2,1)S(1)}, s16[72,256]{1,0:T(8,128)(2,1)S(1)}, u32[]{:S(2)}, u32[]{:S(2)}) collective-permute-start(s16[72,256]{1,0:T(8,128)(2,1)S(1)} %get-tuple-element.36), channel_id=1, source_target_pairs={{0,12},{1,13},{2,14},{3,15},{4,8},{5,9},{6,10},{7,11},{8,4},{9,5},... | collective-permute-start | bytes 110600 | tf_op jit(solution)/shard_map/ppermute | solution.py:467
  23.6 0.2 collective-permute-start.8
  23.8 0.0 copy-done.4
  23.8 0.0 copy-done.5
  23.8 0.0 copy-done.6
  23.8 0.7 %selection.1 = (bf16[128,128]{1,0:T(8,128)(2,1)S(1)}, bf16[128,128]{1,0:T(8,128)(2,1)S(1)}, bf16[64,128]{1,0:T(8,128)(2,1)S(1)}) custom-call(s32[2]{0:T(128)S(1)} %pad_add_fusion.ids, s32[16,8,16]{2,1,0:T(8,128)S(1)} %bitcast.15, s32[16,16]{1,0:T(8,128)S(1)} %copy-done.6, bf16[64,256]{1,0:T(8,128)(2,1)S(1)} %copy-done.5), custom_call_target="tpu_custom_call" | custom-call | tf_op jit(solution)/shard_map/selection/pallas_call | solution.py:200
  24.5 0.0 collective-permute-done.5.refs_1_
  24.5 0.0 collective-permute-done.6.refs_2_
  24.5 3.8 %collective-permute-done.7.refs_3_ = s16[72,256]{1,0:T(8,128)(2,1)S(1)} collective-permute-done((s16[72,256]{1,0:T(8,128)(2,1)S(1)}, s16[72,256]{1,0:T(8,128)(2,1)S(1)}, u32[]{:S(2)}, u32[]{:S(2)}) %collective-permute-start.7) | collective-permute-done | bytes 36896 | tf_op jit(solution)/shard_map/ppermute | solution.py:467
  28.3 0.0 collective-permute-done.8.refs_4_
  28.4 0.1 collective-permute-start.9
  28.5 1.2 %collective-permute-done.9.other = bf16[64,256]{1,0:T(8,128)(2,1)S(1)} collective-permute-done((bf16[64,256]{1,0:T(8,128)(2,1)S(1)}, bf16[64,256]{1,0:T(8,128)(2,1)S(1)}, u32[]{:S(2)}, u32[]{:S(2)}) %collective-permute-start.9) | collective-permute-done | bytes 32800 | tf_op jit(solution)/shard_map/ppermute | solution.py:521
  29.7 0.1 rows_to_send.1
  29.8 9.7 %all_to_all.11 = bf16[16,8,256]{2,1,0:T(8,128)(2,1)S(1)} all-to-all(bf16[16,8,256]{2,1,0:T(8,128)(2,1)S(1)} %bitcast.11), channel_id=1, replica_groups={{15,14,13,12,11,10,9,8,7,6,5,4,3,2,1,0},{31,30,29,28,27,26,25,24,23,22,..., dimensions={0} | all-to-all | bytes 131072 | tf_op jit(solution)/shard_map/all_to_all | solution.py:523
  39.5 0.0 copy-done.2
  39.5 0.0 copy-done.3
  39.5 1.0 %logits.1 = f32[64,172]{1,0:T(8,128)} custom-call(bf16[64,256]{1,0:T(8,128)(2,1)S(1)} %hidden_rows.1.own, bf16[64,256]{1,0:T(8,128)(2,1)S(1)} %collective-permute-done.9.other, bf16[128,256]{1,0:T(8,128)(2,1)S(1)} %bitcast.12, bf16[128,128]{1,0:T(8,128)(2,1)S(1)} %get-tuple-element.39.front, bf16[64,128]{1,0:T(8,128)(2,1)S(1)} %get-tuple-element.40.adj_received, ...), custom_call_target="tpu_custom_call" | custom-call | tf_op jit(solution)/shard_map/logits/pallas_call | solution.py:454
  (1 shorter events, 0.0 us)
Async XLA Ops:
  0.0 3.1 %collective-permute-start.1 = (bf16[1024,512]{1,0:T(8,128)(2,1)}, bf16[1024,512]{1,0:T(8,128)(2,1)S(1)}, u32[]{:S(2)}, u32[]{:S(2)}) collective-permute-start(bf16[1024,512]{1,0:T(8,128)(2,1)} %xo.1), channel_id=1, source_target_pairs={{0,16},{16,0},{1,17},{17,1},{2,18},{18,2},{3,19},{19,3},{4,20},{20... | collective-permute-start | bytes 3145736 | tf_op jit(solution)/shard_map/ppermute | solution.py:494
  0.5 7.3 %collective-permute-start = (bf16[512,256]{1,0:T(8,128)(2,1)}, bf16[512,256]{1,0:T(8,128)(2,1)S(1)}, u32[]{:S(2)}, u32[]{:S(2)}) collective-permute-start(bf16[512,256]{1,0:T(8,128)(2,1)} %wo.5), channel_id=1, source_target_pairs={{0,16},{16,0},{1,17},{17,1},{2,18},{18,2},{3,19},{19,3},{4,20},{20... | collective-permute-start | bytes 786440 | tf_op jit(solution)/shard_map/ppermute | solution.py:495
  3.2 4.7 %copy-start = (bf16[512,256]{1,0:T(8,128)(2,1)S(1)}, bf16[512,256]{1,0:T(8,128)(2,1)}, u32[]{:S(2)}) copy-start(bf16[512,256]{1,0:T(8,128)(2,1)} %wo.5) | copy-start | bytes 786436
  8.4 5.6 %copy-start.1 = (bf16[512,256]{1,0:T(8,128)(2,1)S(1)}, bf16[512,256]{1,0:T(8,128)(2,1)}, u32[]{:S(2)}) copy-start(bf16[512,256]{1,0:T(8,128)(2,1)} %so.1) | copy-start | bytes 786436
  8.4 8.2 %collective-permute-start.4 = (s16[264,256]{1,0:T(8,128)(2,1)S(1)}, s16[264,256]{1,0:T(8,128)(2,1)S(1)}, u32[]{:S(2)}, u32[]{:S(2)}) collective-permute-start(s16[264,256]{1,0:T(8,128)(2,1)S(1)} %sent_terms.3), channel_id=1, source_target_pairs={{0,3},{1,2},{2,1},{3,0},{4,7},{5,6},{6,5},{7,4},{8,11},{9,10},{10,... | collective-permute-start | bytes 405512 | tf_op jit(solution)/shard_map/ppermute | solution.py:467
  13.2 6.1 %collective-permute-start.2 = (s16[264,256]{1,0:T(8,128)(2,1)S(1)}, s16[264,256]{1,0:T(8,128)(2,1)S(1)}, u32[]{:S(2)}, u32[]{:S(2)}) collective-permute-start(s16[264,256]{1,0:T(8,128)(2,1)S(1)} %get-tuple-element.31), channel_id=1, source_target_pairs={{0,1},{1,0},{2,3},{3,2},{4,5},{5,4},{6,7},{7,6},{8,9},{9,8},{10,11... | collective-permute-start | bytes 405512 | tf_op jit(solution)/shard_map/ppermute | solution.py:467
  13.8 9.9 %copy-start.4 = (s32[16,16,8]{1,2,0:T(8,128)S(1)}, s32[16,16,8]{1,2,0:T(8,128)}, u32[]{:S(2)}) copy-start(s32[16,16,8]{1,2,0:T(8,128)} %param.19) | copy-start | bytes 24580
  13.8 9.9 %copy-start.5 = (bf16[64,256]{1,0:T(8,128)(2,1)S(1)}, bf16[64,256]{1,0:T(8,128)(2,1)}, u32[]{:S(2)}) copy-start(bf16[64,256]{1,0:T(8,128)(2,1)} %adj.1) | copy-start | bytes 98308
  13.8 9.9 %copy-start.6 = (s32[16,16]{1,0:T(8,128)S(1)}, s32[16,16]{1,0:T(8,128)}, u32[]{:S(2)}) copy-start(s32[16,16]{1,0:T(8,128)} %counts.1) | copy-start | bytes 3076
  13.8 5.4 %collective-permute-start.3 = (s16[264,256]{1,0:T(8,128)(2,1)S(1)}, s16[264,256]{1,0:T(8,128)(2,1)S(1)}, u32[]{:S(2)}, u32[]{:S(2)}) collective-permute-start(s16[264,256]{1,0:T(8,128)(2,1)S(1)} %get-tuple-element.32), channel_id=1, source_target_pairs={{0,2},{1,3},{2,0},{3,1},{4,6},{5,7},{6,4},{7,5},{8,10},{9,11},{10,... | collective-permute-start | bytes 405512 | tf_op jit(solution)/shard_map/ppermute | solution.py:467
  15.0 24.5 %copy-start.2 = (bf16[256,172]{0,1:T(8,128)(2,1)S(1)}, bf16[256,172]{0,1:T(8,128)(2,1)}, u32[]{:S(2)}) copy-start(bf16[256,172]{0,1:T(8,128)(2,1)} %param.22) | copy-start | bytes 264196
  15.0 24.5 %copy-start.3 = (bf16[256,172]{0,1:T(8,128)(2,1)S(1)}, bf16[256,172]{0,1:T(8,128)(2,1)}, u32[]{:S(2)}) copy-start(bf16[256,172]{0,1:T(8,128)(2,1)} %param.23) | copy-start | bytes 264196
  15.0 9.5 %collective-permute-start.5 = (f32[64,256]{1,0:T(8,128)S(1)}, f32[64,256]{1,0:T(8,128)S(1)}, u32[]{:S(2)}, u32[]{:S(2)}) collective-permute-start(f32[64,256]{1,0:T(8,128)S(1)} %get-tuple-element.34), channel_id=1, source_target_pairs={{0,16},{16,0},{1,17},{17,1},{2,18},{18,2},{3,19},{19,3},{4,20},{20... | collective-permute-start | bytes 196616 | tf_op jit(solution)/shard_map/ppermute | solution.py:510
  19.5 5.0 %collective-permute-start.6 = (s16[72,256]{1,0:T(8,128)(2,1)S(1)}, s16[72,256]{1,0:T(8,128)(2,1)S(1)}, u32[]{:S(2)}, u32[]{:S(2)}) collective-permute-start(s16[72,256]{1,0:T(8,128)(2,1)S(1)} %get-tuple-element.35), channel_id=1, source_target_pairs={{0,8},{1,9},{2,10},{3,11},{4,12},{5,13},{6,14},{7,15},{8,0},{9,1},... | collective-permute-start | bytes 110600 | tf_op jit(solution)/shard_map/ppermute | solution.py:467
  22.6 5.8 %collective-permute-start.7 = (s16[72,256]{1,0:T(8,128)(2,1)S(1)}, s16[72,256]{1,0:T(8,128)(2,1)S(1)}, u32[]{:S(2)}, u32[]{:S(2)}) collective-permute-start(s16[72,256]{1,0:T(8,128)(2,1)S(1)} %get-tuple-element.36), channel_id=1, source_target_pairs={{0,12},{1,13},{2,14},{3,15},{4,8},{5,9},{6,10},{7,11},{8,4},{9,5},... | collective-permute-start | bytes 110600 | tf_op jit(solution)/shard_map/ppermute | solution.py:467
  23.6 4.8 %collective-permute-start.8 = (s16[72,256]{1,0:T(8,128)(2,1)S(1)}, s16[72,256]{1,0:T(8,128)(2,1)S(1)}, u32[]{:S(2)}, u32[]{:S(2)}) collective-permute-start(s16[72,256]{1,0:T(8,128)(2,1)S(1)} %get-tuple-element.37), channel_id=1, source_target_pairs={{0,4},{1,5},{2,6},{3,7},{4,0},{5,1},{6,2},{7,3},{8,12},{9,13},{10,... | collective-permute-start | bytes 110600 | tf_op jit(solution)/shard_map/ppermute | solution.py:467
  28.4 1.3 %collective-permute-start.9 = (bf16[64,256]{1,0:T(8,128)(2,1)S(1)}, bf16[64,256]{1,0:T(8,128)(2,1)S(1)}, u32[]{:S(2)}, u32[]{:S(2)}) collective-permute-start(bf16[64,256]{1,0:T(8,128)(2,1)S(1)} %hidden_rows.1.own), channel_id=1, source_target_pairs={{0,16},{16,0},{1,17},{17,1},{2,18},{18,2},{3,19},{19,3},{4,20},{20... | collective-permute-start | bytes 98312 | tf_op jit(solution)/shard_map/ppermute | solution.py:521
